TPU v7x, 32 devices: a whole 2x2x4 slice. The times are simulated.
32 devices in a mesh: energy: 8 (over y, x, core), slab: 4 (over z).
Axes of the slice: x: 2, y: 2, z: 4, core: 2. Of those that a mesh axis runs over, the one named last changes fastest.
Arguments:
- potential_old: float32 [64, 32, 128], P('slab', 'energy'), may hold values from -6 to 6
- charge: float32 [64, 32, 128], P('slab', 'energy'), may hold values from -6 to 6
- permittivity: float32 [64, 32, 128], P('slab', 'energy'), may hold values from 1 to 12
- owner_cell: int32 [16, 256], P('slab'), may hold values from 0 to 16383
- green_free: float32 [8, 16, 2, 256, 256], P('energy', 'slab')
- coupling: float32 [16, 2, 256, 256], P('slab'), may hold values from -0.25 to 0.25
- shifts: int32 [4], replicated, may hold values from 1 to 2, as said below
- occupation: float32 [4], replicated, may hold values from 0.1 to 3
- mode_tiles: float32 [4, 256, 256], replicated, may hold values from -6 to 6
Outputs:
- potential_new: float32 [64, 32, 128], P('slab', 'energy')
- self_energy: float32 [8, 16, 2, 256, 256], P('energy', 'slab')
Inputs may be any that keep to these rules, and one draw needn't show every extreme that they name: `shifts`: every whole number from 1 to 2 is the shift of some mode.
All inputs are finite; a program needn't handle non-finite values.
Results may differ from a plain program's by a relative error of at most 0.00023.
Values sent between devices are 32-bit elements; how exact they have to be, the bound alone decides.
No kernel may reach another device: no remote copies, remote signals or barrier semaphores. Data moves between devices by JAX's collectives and lax.ppermute only.
A program may use at most 128 MiB of HBM per device.

v0:
```python
import functools
import jax
import jax.numpy as jnp
from jax import lax
from jax.experimental import pallas as pl
from jax.experimental.pallas import tpu as pltpu
from jax.sharding import PartitionSpec as P

SHIFT_MOST = 2
VMEM_LIMIT = 56 * 1024 * 1024


def halves(value):
    high = value.astype(jnp.bfloat16)
    low = (value - high.astype(jnp.float32)).astype(jnp.bfloat16)
    return high, low


def left_form(block):
    forms = []
    for real, imag in zip(halves(block[0]), halves(block[1])):
        upper = jnp.concatenate([real, -imag], axis=1)
        lower = jnp.concatenate([imag, real], axis=1)
        forms.append(jnp.concatenate([upper, lower], axis=0))
    return forms


def right_form(block):
    return [
        jnp.concatenate([real, imag], axis=0)
        for real, imag in zip(halves(block[0]), halves(block[1]))
    ]


def right_form_flipped(block):
    return [
        jnp.concatenate([real, imag], axis=1)
        for real, imag in zip(halves(block[0]), halves(block[1]))
    ]


def three_passes(left, right, flipped):
    dims = (((1,), (1 if flipped else 0,)), ((), ()))
    dot = functools.partial(
        lax.dot_general, dimension_numbers=dims, preferred_element_type=jnp.float32
    )
    out = dot(left[0], right[0]) + (dot(left[0], right[1]) + dot(left[1], right[0]))
    width = out.shape[0] // 2
    return out[:width], out[width:]


def product(former, latter):
    return three_passes(left_form(former), right_form(latter), False)


def sandwich(link, inner):
    half_way = product(link, inner)
    return three_passes(left_form(half_way), right_form_flipped(link), True)


def added(first, second):
    return first[0] + second[0], first[1] + second[1]


def pair_of(ref, *where):
    return ref[(*where, 0)], ref[(*where, 1)]


def put(ref, value, *where):
    ref[(*where, 0)] = value[0]
    ref[(*where, 1)] = value[1]


def call(kernel, out_shapes, *operands, **more):
    return pl.pallas_call(
        kernel,
        out_shape=out_shapes,
        compiler_params=pltpu.CompilerParams(vmem_limit_bytes=VMEM_LIMIT),
        **more,
    )(*operands)


def shape(*dims):
    return jax.ShapeDtypeStruct(dims, jnp.float32)


def linkage_kernel(free, coupling, link, whole_map):
    count = free.shape[0]
    total = None
    for slab in range(count):
        now = product(pair_of(free, slab), pair_of(coupling, slab))
        put(link, now, slab)
        total = now if total is None else product(now, total)
    put(whole_map, total)


def source_of(free, potential, slab):
    block = pair_of(free, slab)
    row = potential[slab : slab + 1, :]
    scaled = (block[0] * row, block[1] * row)
    return added(block, product(scaled, block))


def source_kernel(free, link, potential, source, whole_source):
    count = free.shape[0]
    state = None
    for slab in range(count):
        now = source_of(free, potential, slab)
        put(source, now, slab)
        state = now if state is None else added(sandwich(pair_of(link, slab), state), now)
    put(whole_source, state)


def hop_kernel(whole_map, whole_source, carried, out):
    put(out, added(sandwich(pair_of(whole_map), pair_of(carried)), pair_of(whole_source)))


def neighbour_kernel(free_near, free_far, coupling, potential, link, source):
    potential_row = potential[0]
    for which, free in enumerate((free_near, free_far)):
        block = pair_of(free, 0)
        put(link, product(block, pair_of(coupling, 0)), which, 0)
        scaled = (block[0] * potential_row, block[1] * potential_row)
        put(source, added(block, product(scaled, block)), which, 0)


def own_greens_kernel(link, source, carried, greens, state):
    @pl.when(pl.program_id(0) == 0)
    def _():
        state[...] = carried[...]

    now = added(sandwich(pair_of(link, 0), pair_of(state)), pair_of(source, 0))
    put(state, now)
    put(greens, now, 0)


def mixing_kernel(link, source, near, far, own, weights, here, there, state):
    @pl.when(pl.program_id(0) == 0)
    def _():
        state[0] = near[...]
        state[1] = far[...]

    near_now = added(sandwich(pair_of(link, 0, 0), pair_of(state, 0)), pair_of(source, 0, 0))
    far_now = added(sandwich(pair_of(link, 1, 0), pair_of(state, 1)), pair_of(source, 1, 0))
    put(state, near_now, 0)
    put(state, far_now, 1)
    by_one, by_two = weights[0], weights[1]
    for part in range(2):
        here[0, part] = by_one * near_now[part] + by_two * far_now[part]
        there[0, part] = by_one * own[0, part] + by_two * near_now[part]


def relaxed(field, perm, charge, halos):
    numerator = charge
    denominator = jnp.zeros_like(charge)
    for dim in range(3):
        length = charge.shape[dim]
        before, after = halos[dim]
        for side in range(2):
            sides = []
            for which, array in enumerate((field, perm)):
                if side == 0:
                    kept = lax.slice_in_dim(array, 1, length, axis=dim)
                    parts = [kept, after[which]]
                else:
                    kept = lax.slice_in_dim(array, 0, length - 1, axis=dim)
                    parts = [before[which], kept]
                sides.append(jnp.concatenate(parts, axis=dim))
            face = 0.5 * (perm + sides[1])
            numerator = numerator + face * sides[0]
            denominator = denominator + face
    return numerator / denominator


def halo_planes(stacked, axis, dim):
    peers, length = lax.axis_size(axis), stacked.shape[dim]
    up = [(i, i + 1) for i in range(peers - 1)]
    down = [(j, i) for i, j in up]
    last = lax.slice_in_dim(stacked, length - 1, length, axis=dim)
    first = lax.slice_in_dim(stacked, 0, 1, axis=dim)
    return lax.ppermute(last, axis, up), lax.ppermute(first, axis, down)


def orbital_values(potential_new, owner_cell):
    slab_count, _ = owner_cell.shape
    cells, rows, depth = potential_new.shape
    cells = cells // slab_count
    cross = rows * lax.axis_size("energy")
    first = owner_cell // (cross * depth)
    second = (owner_cell // depth) % cross - lax.axis_index("energy") * rows
    third = owner_cell % depth
    mine = (second >= 0) & (second < rows)
    row = jnp.where(mine, first * rows + second, -1)
    table = potential_new.reshape(slab_count, 1, cells * rows, depth)
    row_ids = lax.broadcasted_iota(jnp.int32, (1, 1, cells * rows, 1), 2)
    lane_ids = lax.broadcasted_iota(jnp.int32, (1, 1, 1, depth), 3)
    hit = (row[:, :, None, None] == row_ids) & (third[:, :, None, None] == lane_ids)
    values = jnp.sum(jnp.where(hit, table, 0.0), axis=(2, 3))
    return lax.psum(values, "energy")


def per_device(
    potential_old,
    charge,
    permittivity,
    owner_cell,
    green_free,
    coupling,
    shifts,
    occupation,
    mode_tiles,
):
    energies, peers = lax.axis_size("energy"), lax.axis_size("slab")
    free = green_free[0]
    count, _, width, _ = free.shape

    near_pairs = [(e, e + 1 if e % 2 else e - 1) for e in range(energies)]
    far_pairs = [(e, e - 2 if e % 2 else e + 2) for e in range(energies)]
    near_pairs = [(a, b) for a, b in near_pairs if 0 <= b < energies]
    far_pairs = [(a, b) for a, b in far_pairs if 0 <= b < energies]
    twin_pairs = [(e, e ^ 1) for e in range(energies)]

    stacked = jnp.stack([potential_old, permittivity])
    slab_halo = halo_planes(stacked, "slab", 1)
    energy_halo = halo_planes(stacked, "energy", 2)
    edge = jnp.zeros((2, *charge.shape[:2], 1), jnp.float32)
    potential_new = relaxed(
        potential_old, permittivity, charge, (slab_halo, energy_halo, (edge, edge))
    )
    orbital_potential = orbital_values(potential_new, owner_cell)

    free_near = lax.ppermute(free, "energy", near_pairs)
    free_far = lax.ppermute(free, "energy", far_pairs)

    link, whole_map = call(
        linkage_kernel, (shape(count, 2, width, width), shape(2, width, width)), free, coupling
    )
    source, whole_source = call(
        source_kernel,
        (shape(count, 2, width, width), shape(2, width, width)),
        free,
        link,
        orbital_potential,
    )

    onward = [(i, i + 1) for i in range(peers - 1)]
    leaving = whole_source
    for _ in range(peers - 2):
        carried = lax.ppermute(leaving, "slab", onward)
        leaving = call(hop_kernel, shape(2, width, width), whole_map, whole_source, carried)

    def both(pairs):
        return [(a * peers + i, b * peers + j) for a, b in pairs for i, j in onward]

    carried = lax.ppermute(leaving, "slab", onward)
    carried_near = lax.ppermute(leaving, ("energy", "slab"), both(near_pairs))
    carried_far = lax.ppermute(leaving, ("energy", "slab"), both(far_pairs))

    block = pl.BlockSpec((1, 2, width, width), lambda s: (s, 0, 0, 0))
    two_blocks = pl.BlockSpec((2, 1, 2, width, width), lambda s: (0, s, 0, 0, 0))
    one_state = pl.BlockSpec((2, width, width), lambda s: (0, 0, 0))
    greens = call(
        own_greens_kernel,
        shape(count, 2, width, width),
        link,
        source,
        carried,
        grid=(count,),
        in_specs=[block, block, one_state],
        out_specs=block,
        scratch_shapes=[pltpu.VMEM((2, width, width), jnp.float32)],
    )
    link_beside, source_beside = call(
        neighbour_kernel,
        (shape(2, count, 2, width, width), shape(2, count, 2, width, width)),
        free_near,
        free_far,
        coupling,
        orbital_potential.reshape(count, 1, width),
        grid=(count,),
        in_specs=[block, block, block, pl.BlockSpec((1, 1, width), lambda s: (s, 0, 0))],
        out_specs=(two_blocks, two_blocks),
    )

    levels = jnp.arange(1, SHIFT_MOST + 1, dtype=jnp.int32)
    matches = (shifts[None, :] == levels[:, None]).astype(jnp.float32)
    lowered = (1 - lax.axis_index("energy") % 2).astype(jnp.float32)
    factors = matches * (occupation + lowered)[None, :]
    weights = jnp.sum(factors[:, :, None, None] * mode_tiles[None], axis=1)

    here, there = call(
        mixing_kernel,
        (shape(count, 2, width, width), shape(count, 2, width, width)),
        link_beside,
        source_beside,
        carried_near,
        carried_far,
        greens,
        weights,
        grid=(count,),
        in_specs=[two_blocks, two_blocks, one_state, one_state, block, one_state],
        out_specs=(block, block),
        scratch_shapes=[pltpu.VMEM((2, 2, width, width), jnp.float32)],
    )
    self_energy = here + lax.ppermute(there, "energy", twin_pairs)
    return potential_new, self_energy[None]


def solution(mesh):
    in_specs = (
        P("slab", "energy", None),
        P("slab", "energy", None),
        P("slab", "energy", None),
        P("slab", None),
        P("energy", "slab", None, None, None),
        P("slab", None, None, None),
        P(),
        P(),
        P(),
    )
    out_specs = (P("slab", "energy", None), P("energy", "slab", None, None, None))
    return jax.shard_map(
        per_device, mesh=mesh, in_specs=in_specs, out_specs=out_specs, check_vma=False
    )
```

profile of v0, /device:TPU:13, one launch (start us, length us, event | category | flops | bytes accessed | tf_op | source)
XLA Modules:
  0.0 254.8 jit_solution(3360640651024651526)
XLA Ops:
  0.6 3.7 %collective-permute-start.4 = (f32[4,2,256,256]{3,2,1,0:T(8,128)}, f32[4,2,256,256]{3,2,1,0:T(8,128)S(1)}, u32[]{:S(2)}, u32[]{:S(2)}) collective-permute-start(f32[4,2,256,256]{3,2,1,0:T(8,128)} %bitcast.23), channel_id=1, source_target_pairs={{4,8},{8,4},{12,16},{16,12},{20,24},{24,20},{5,9},{9,5},{13,17},{1... | collective-permute-start | bytes 6291464 | tf_op jit(solution)/shard_map/ppermute | solution.py:232
  4.3 3.1 %collective-permute-start.5 = (f32[4,2,256,256]{3,2,1,0:T(8,128)}, f32[4,2,256,256]{3,2,1,0:T(8,128)}, u32[]{:S(2)}, u32[]{:S(2)}) collective-permute-start(f32[4,2,256,256]{3,2,1,0:T(8,128)} %bitcast.24), channel_id=1, source_target_pairs={{0,8},{8,16},{12,4},{16,24},{20,12},{28,20},{1,9},{9,17},{13,5},{1... | collective-permute-start | bytes 6291464 | tf_op jit(solution)/shard_map/ppermute | solution.py:233
  8.2 2.1 collective-permute-start
  10.3 3.2 %collective-permute-start.1 = (f32[2,1,4,128]{3,1,2,0:T(1,128)S(1)}, f32[2,1,4,128]{3,1,2,0:T(1,128)S(1)}, u32[]{:S(2)}, u32[]{:S(2)}) collective-permute-start(f32[2,1,4,128]{3,1,2,0:T(1,128)S(1)} %get-tuple-element.20), channel_id=1, source_target_pairs={{0,1},{1,2},{2,3},{4,5},{5,6},{6,7},{8,9},{9,10},{10,11},{12,13},{... | collective-permute-start | bytes 12296 | tf_op jit(solution)/shard_map/ppermute | solution.py:181
  13.5 1.9 collective-permute-start.2
  16.3 0.9 fusion.20
  17.1 0.9 fusion.17
  19.2 7.0 %shard_map.105 = (f32[4,2,256,256]{3,2,1,0:T(8,128)}, f32[2,256,256]{2,1,0:T(8,128)}) custom-call(f32[4,2,256,256]{3,2,1,0:T(8,128)} %bitcast.25, f32[4,2,256,256]{3,2,1,0:T(8,128)} %coupling.3), custom_call_target="tpu_custom_call" | custom-call | tf_op jit(solution)/shard_map/pallas_call | solution.py:75
  26.2 3.6 %collective-permute-start.3 = (f32[2,16,1,128]{3,1,2,0:T(8,128)S(1)}, f32[2,16,1,128]{3,1,2,0:T(8,128)S(1)}, u32[]{:S(2)}, u32[]{:S(2)}) collective-permute-start(f32[2,16,1,128]{3,1,2,0:T(8,128)S(1)} %get-tuple-element.18), channel_id=1, source_target_pairs={{0,4},{4,8},{8,12},{12,16},{16,20},{20,24},{24,28},{1,5},{5,9},{9,... | collective-permute-start | bytes 49160 | tf_op jit(solution)/shard_map/ppermute | solution.py:181
  29.9 18.3 %collective-permute-done.2 = f32[2,16,1,128]{3,1,2,0:T(8,128)S(1)} collective-permute-done((f32[2,16,1,128]{3,1,2,0:T(8,128)S(1)}, f32[2,16,1,128]{3,1,2,0:T(8,128)S(1)}, u32[]{:S(2)}, u32[]{:S(2)}) %collective-permute-start.2) | collective-permute-done | bytes 16416 | tf_op jit(solution)/shard_map/ppermute | solution.py:181
  48.2 47.0 %collective-permute-done.3 = f32[2,16,1,128]{3,1,2,0:T(8,128)S(1)} collective-permute-done((f32[2,16,1,128]{3,1,2,0:T(8,128)S(1)}, f32[2,16,1,128]{3,1,2,0:T(8,128)S(1)}, u32[]{:S(2)}, u32[]{:S(2)}) %collective-permute-start.3) | collective-permute-done | bytes 16416 | tf_op jit(solution)/shard_map/ppermute | solution.py:181
  95.4 16.3 %select_reduce_fusion = f32[4,256]{1,0:T(4,128)S(1)} fusion(f32[4,16,128]{2,1,0:T(8,128)S(1)} %bitcast.27, pred[4,256,128]{2,1,0:T(8,128)(4,1)S(1)} %iota_compare_fusion, pred[4,256,16]{2,1,0:T(8,128)(4,1)S(1)} %iota_compare_fusion.1), kind=kLoop, calls=%fused_computation | loop fusion | flops 6290432 | bytes 184320 | tf_op jit(solution)/shard_map/reduce_sum | solution.py:198
  111.8 13.1 %psum.7.potential = f32[4,256]{1,0:T(4,128)} all-reduce(f32[4,256]{1,0:T(4,128)S(1)} %select_reduce_fusion), channel_id=1, replica_groups=mesh['energy'=8,'slab'=4] {'energy'}, use_global_device_ids=true, to_apply=%region_1.2 | all-reduce | flops 1024 | bytes 8192 | tf_op jit(solution)/shard_map/psum | solution.py:199
  124.9 9.0 %shard_map.106 = (f32[4,2,256,256]{3,2,1,0:T(8,128)}, f32[2,256,256]{2,1,0:T(8,128)}) custom-call(f32[4,2,256,256]{3,2,1,0:T(8,128)} %bitcast.26, f32[4,2,256,256]{3,2,1,0:T(8,128)} %get-tuple-element.13.link, f32[4,256]{1,0:T(4,128)} %psum.7.potential), custom_call_target="tpu_custom_call" | custom-call | tf_op jit(solution)/shard_map/pallas_call | solution.py:75
  133.9 3.2 %collective-permute-start.6 = (f32[2,256,256]{2,1,0:T(8,128)}, f32[2,256,256]{2,1,0:T(8,128)S(1)}, u32[]{:S(2)}, u32[]{:S(2)}) collective-permute-start(f32[2,256,256]{2,1,0:T(8,128)} %get-tuple-element.14.whole_source), channel_id=1, source_target_pairs={{0,1},{1,2},{2,3},{4,5},{5,6},{6,7},{8,9},{9,10},{10,11},{12,13},{... | collective-permute-start | bytes 1572872 | tf_op jit(solution)/shard_map/ppermute | solution.py:249
  137.1 9.9 %collective-permute-done.6.carried = f32[2,256,256]{2,1,0:T(8,128)S(1)} collective-permute-done((f32[2,256,256]{2,1,0:T(8,128)}, f32[2,256,256]{2,1,0:T(8,128)S(1)}, u32[]{:S(2)}, u32[]{:S(2)}) %collective-permute-start.6) | collective-permute-done | bytes 524320 | tf_op jit(solution)/shard_map/ppermute | solution.py:249
  147.8 4.0 %shard_map.107 = f32[2,256,256]{2,1,0:T(8,128)} custom-call(f32[2,256,256]{2,1,0:T(8,128)} %get-tuple-element.12.whole_map, f32[2,256,256]{2,1,0:T(8,128)} %get-tuple-element.14.whole_source, f32[2,256,256]{2,1,0:T(8,128)} %copy-done.5), custom_call_target="tpu_custom_call" | custom-call | tf_op jit(solution)/shard_map/pallas_call | solution.py:75
  151.8 3.3 %collective-permute-start.7 = (f32[2,256,256]{2,1,0:T(8,128)}, f32[2,256,256]{2,1,0:T(8,128)}, u32[]{:S(2)}, u32[]{:S(2)}) collective-permute-start(f32[2,256,256]{2,1,0:T(8,128)} %shard_map.107), channel_id=1, source_target_pairs={{0,1},{1,2},{2,3},{4,5},{5,6},{6,7},{8,9},{9,10},{10,11},{12,13},{... | collective-permute-start | bytes 1572872 | tf_op jit(solution)/shard_map/ppermute | solution.py:249
  155.1 9.1 %collective-permute-done.7.carried = f32[2,256,256]{2,1,0:T(8,128)} collective-permute-done((f32[2,256,256]{2,1,0:T(8,128)}, f32[2,256,256]{2,1,0:T(8,128)}, u32[]{:S(2)}, u32[]{:S(2)}) %collective-permute-start.7) | collective-permute-done | bytes 524320 | tf_op jit(solution)/shard_map/ppermute | solution.py:249
  164.2 4.0 %shard_map.108 = f32[2,256,256]{2,1,0:T(8,128)} custom-call(f32[2,256,256]{2,1,0:T(8,128)} %get-tuple-element.12.whole_map, f32[2,256,256]{2,1,0:T(8,128)} %get-tuple-element.14.whole_source, f32[2,256,256]{2,1,0:T(8,128)} %collective-permute-done.7.carried), custom_call_target="tpu_custom_call" | custom-call | tf_op jit(solution)/shard_map/pallas_call | solution.py:75
  168.2 7.2 %collective-permute-start.8 = (f32[2,256,256]{2,1,0:T(8,128)}, f32[2,256,256]{2,1,0:T(8,128)S(1)}, u32[]{:S(2)}, u32[]{:S(2)}) collective-permute-start(f32[2,256,256]{2,1,0:T(8,128)} %shard_map.108), channel_id=1, source_target_pairs={{4,9},{5,10},{6,11},{8,5},{9,6},{10,7},{12,17},{13,18},{14,19},{16... | collective-permute-start | bytes 1572872 | tf_op jit(solution)/shard_map/ppermute | solution.py:256
  175.4 5.1 %collective-permute-start.9 = (f32[2,256,256]{2,1,0:T(8,128)}, f32[2,256,256]{2,1,0:T(8,128)S(1)}, u32[]{:S(2)}, u32[]{:S(2)}) collective-permute-start(f32[2,256,256]{2,1,0:T(8,128)} %shard_map.108), channel_id=1, source_target_pairs={{0,9},{1,10},{2,11},{8,17},{9,18},{10,19},{12,5},{13,6},{14,7},{16... | collective-permute-start | bytes 1572872 | tf_op jit(solution)/shard_map/ppermute | solution.py:257
  180.5 2.6 %collective-permute-start.10 = (f32[2,256,256]{2,1,0:T(8,128)}, f32[2,256,256]{2,1,0:T(8,128)S(1)}, u32[]{:S(2)}, u32[]{:S(2)}) collective-permute-start(f32[2,256,256]{2,1,0:T(8,128)} %shard_map.108), channel_id=1, source_target_pairs={{0,1},{1,2},{2,3},{4,5},{5,6},{6,7},{8,9},{9,10},{10,11},{12,13},{... | collective-permute-start | bytes 1572872 | tf_op jit(solution)/shard_map/ppermute | solution.py:255
  183.3 1.0 multiply_reduce_fusion.weights
  184.9 22.1 %collective-permute-done.10.carried = f32[2,256,256]{2,1,0:T(8,128)S(1)} collective-permute-done((f32[2,256,256]{2,1,0:T(8,128)}, f32[2,256,256]{2,1,0:T(8,128)S(1)}, u32[]{:S(2)}, u32[]{:S(2)}) %collective-permute-start.10) | collective-permute-done | bytes 524320 | tf_op jit(solution)/shard_map/ppermute | solution.py:255
  207.8 9.3 %shard_map.109.own = f32[4,2,256,256]{3,2,1,0:T(8,128)} custom-call(f32[4,2,256,256]{3,2,1,0:T(8,128)} %get-tuple-element.13.link, f32[4,2,256,256]{3,2,1,0:T(8,128)} %get-tuple-element.15.source, f32[2,256,256]{2,1,0:T(8,128)} %copy-done.6), custom_call_target="tpu_custom_call" | custom-call | tf_op jit(solution)/shard_map/pallas_call | solution.py:75
  217.2 1.3 copy-done
  218.5 10.4 %shard_map.104 = (f32[2,4,2,256,256]{4,3,2,1,0:T(8,128)}, f32[2,4,2,256,256]{4,3,2,1,0:T(8,128)}) custom-call(f32[4,2,256,256]{3,2,1,0:T(8,128)} %copy-done, f32[4,2,256,256]{3,2,1,0:T(8,128)} %collective-permute-done.5.free_far, f32[4,2,256,256]{3,2,1,0:T(8,128)} %coupling.3, f32[4,1,256]{2,1,0:T(1,128)} %copy.22.potential), custom_call_target="tpu_custom_call" | custom-call | tf_op jit(solution)/shard_map/pallas_call | solution.py:75
  230.0 13.5 %shard_map.110 = (f32[4,2,256,256]{3,2,1,0:T(8,128)}, f32[4,2,256,256]{3,2,1,0:T(8,128)}) custom-call(f32[2,4,2,256,256]{4,3,2,1,0:T(8,128)} %get-tuple-element.10.link, f32[2,4,2,256,256]{4,3,2,1,0:T(8,128)} %get-tuple-element.11.source, f32[2,256,256]{2,1,0:T(8,128)} %copy-done.3, f32[2,256,256]{2,1,0:T(8,128)} %copy-done.4, ...), custom_call_target="tpu_custom_call" | custom-call | tf_op jit(solution)/shard_map/pallas_call | solution.py:75
  243.5 4.1 %collective-permute-start.11 = (f32[4,2,256,256]{3,2,1,0:T(8,128)}, f32[4,2,256,256]{3,2,1,0:T(8,128)S(1)}, u32[]{:S(2)}, u32[]{:S(2)}) collective-permute-start(f32[4,2,256,256]{3,2,1,0:T(8,128)} %get-tuple-element.17), channel_id=1, source_target_pairs={{0,4},{4,0},{8,12},{12,8},{16,20},{20,16},{24,28},{28,24},{1,5},{5... | collective-permute-start | bytes 6291464 | tf_op jit(solution)/shard_map/ppermute | solution.py:305
  247.6 4.0 %collective-permute-done.11 = f32[4,2,256,256]{3,2,1,0:T(8,128)S(1)} collective-permute-done((f32[4,2,256,256]{3,2,1,0:T(8,128)}, f32[4,2,256,256]{3,2,1,0:T(8,128)S(1)}, u32[]{:S(2)}, u32[]{:S(2)}) %collective-permute-start.11) | collective-permute-done | bytes 2097184 | tf_op jit(solution)/shard_map/ppermute | solution.py:305
  251.6 3.2 %add_bitcast_fusion = f32[1,4,2,256,256]{4,3,2,1,0:T(8,128)} fusion(f32[4,2,256,256]{3,2,1,0:T(8,128)} %get-tuple-element.16, f32[4,2,256,256]{3,2,1,0:T(8,128)S(1)} %collective-permute-done.11), kind=kLoop, calls=%fused_computation.1 | loop fusion | flops 524288 | bytes 6291456 | tf_op jit(solution)/shard_map/broadcast_in_dim | solution.py:306
  (45 shorter events, 6.3 us)
Async XLA Ops:
  0.6 216.5 %collective-permute-start.4 = (f32[4,2,256,256]{3,2,1,0:T(8,128)}, f32[4,2,256,256]{3,2,1,0:T(8,128)S(1)}, u32[]{:S(2)}, u32[]{:S(2)}) collective-permute-start(f32[4,2,256,256]{3,2,1,0:T(8,128)} %bitcast.23), channel_id=1, source_target_pairs={{4,8},{8,4},{12,16},{16,12},{20,24},{24,20},{5,9},{9,5},{13,17},{1... | collective-permute-start | bytes 6291464 | tf_op jit(solution)/shard_map/ppermute | solution.py:232
  4.3 212.9 %collective-permute-start.5 = (f32[4,2,256,256]{3,2,1,0:T(8,128)}, f32[4,2,256,256]{3,2,1,0:T(8,128)}, u32[]{:S(2)}, u32[]{:S(2)}) collective-permute-start(f32[4,2,256,256]{3,2,1,0:T(8,128)} %bitcast.24), channel_id=1, source_target_pairs={{0,8},{8,16},{12,4},{16,24},{20,12},{28,20},{1,9},{9,17},{13,5},{1... | collective-permute-start | bytes 6291464 | tf_op jit(solution)/shard_map/ppermute | solution.py:233
  8.2 18.1 %collective-permute-start = (f32[2,1,4,128]{3,1,2,0:T(1,128)S(1)}, f32[2,1,4,128]{3,1,2,0:T(1,128)S(1)}, u32[]{:S(2)}, u32[]{:S(2)}) collective-permute-start(f32[2,1,4,128]{3,1,2,0:T(1,128)S(1)} %get-tuple-element.21), channel_id=1, source_target_pairs={{1,0},{2,1},{3,2},{5,4},{6,5},{7,6},{9,8},{10,9},{11,10},{13,12},{... | collective-permute-start | bytes 12296 | tf_op jit(solution)/shard_map/ppermute | solution.py:181
  10.3 19.6 %collective-permute-start.1 = (f32[2,1,4,128]{3,1,2,0:T(1,128)S(1)}, f32[2,1,4,128]{3,1,2,0:T(1,128)S(1)}, u32[]{:S(2)}, u32[]{:S(2)}) collective-permute-start(f32[2,1,4,128]{3,1,2,0:T(1,128)S(1)} %get-tuple-element.20), channel_id=1, source_target_pairs={{0,1},{1,2},{2,3},{4,5},{5,6},{6,7},{8,9},{9,10},{10,11},{12,13},{... | collective-permute-start | bytes 12296 | tf_op jit(solution)/shard_map/ppermute | solution.py:181
  13.5 34.7 %collective-permute-start.2 = (f32[2,16,1,128]{3,1,2,0:T(8,128)S(1)}, f32[2,16,1,128]{3,1,2,0:T(8,128)S(1)}, u32[]{:S(2)}, u32[]{:S(2)}) collective-permute-start(f32[2,16,1,128]{3,1,2,0:T(8,128)S(1)} %get-tuple-element.19), channel_id=1, source_target_pairs={{4,0},{8,4},{12,8},{16,12},{20,16},{24,20},{28,24},{5,1},{9,5},{13... | collective-permute-start | bytes 49160 | tf_op jit(solution)/shard_map/ppermute | solution.py:181
  19.2 76.0 %copy-start.1 = (f32[16,4,128]{2,1,0:T(4,128)S(1)}, f32[16,4,128]{2,1,0:T(4,128)}, u32[]{:S(2)}) copy-start(f32[16,4,128]{2,1,0:T(4,128)} %param.11) | copy-start | bytes 98308
  19.2 76.0 %copy-start.9 = (f32[16,4,128]{2,1,0:T(4,128)S(1)}, f32[16,4,128]{2,1,0:T(4,128)}, u32[]{:S(2)}) copy-start(f32[16,4,128]{2,1,0:T(4,128)} %param.10) | copy-start | bytes 98308
  26.2 69.0 %collective-permute-start.3 = (f32[2,16,1,128]{3,1,2,0:T(8,128)S(1)}, f32[2,16,1,128]{3,1,2,0:T(8,128)S(1)}, u32[]{:S(2)}, u32[]{:S(2)}) collective-permute-start(f32[2,16,1,128]{3,1,2,0:T(8,128)S(1)} %get-tuple-element.18), channel_id=1, source_target_pairs={{0,4},{4,8},{8,12},{12,16},{16,20},{20,24},{24,28},{1,5},{5,9},{9,... | collective-permute-start | bytes 49160 | tf_op jit(solution)/shard_map/ppermute | solution.py:181
  95.4 38.4 %copy-start.7 = (f32[16,4,128]{2,1,0:T(4,128)}, f32[16,4,128]{2,1,0:T(4,128)S(1)}, u32[]{:S(2)}) copy-start(f32[16,4,128]{2,1,0:T(4,128)S(1)} %fusion.7) | copy-start | bytes 98308
  133.9 13.1 %collective-permute-start.6 = (f32[2,256,256]{2,1,0:T(8,128)}, f32[2,256,256]{2,1,0:T(8,128)S(1)}, u32[]{:S(2)}, u32[]{:S(2)}) collective-permute-start(f32[2,256,256]{2,1,0:T(8,128)} %get-tuple-element.14.whole_source), channel_id=1, source_target_pairs={{0,1},{1,2},{2,3},{4,5},{5,6},{6,7},{8,9},{9,10},{10,11},{12,13},{... | collective-permute-start | bytes 1572872 | tf_op jit(solution)/shard_map/ppermute | solution.py:249
  147.0 0.8 copy-start.5
  147.8 35.4 %copy-start.11 = (f32[4]{0:T(128)S(1)}, f32[4]{0:T(128)}, u32[]{:S(2)}) copy-start(f32[4]{0:T(128)} %param.16) | copy-start | bytes 52
  147.8 35.5 %copy-start.10 = (s32[4]{0:T(128)S(1)}, s32[4]{0:T(128)}, u32[]{:S(2)}) copy-start(s32[4]{0:T(128)} %param.15) | copy-start | bytes 52
  147.8 35.5 %copy-start.2 = (f32[4,256,256]{2,1,0:T(8,128)S(1)}, f32[4,256,256]{2,1,0:T(8,128)}, u32[]{:S(2)}) copy-start(f32[4,256,256]{2,1,0:T(8,128)} %param.17) | copy-start | bytes 3145732
  151.8 32.5 %copy-start.8 = (f32[4,256]{1,0:T(4,128)S(1)}, f32[4,256]{1,0:T(4,128)}, u32[]{:S(2)}) copy-start(f32[4,256]{1,0:T(4,128)} %psum.7.potential) | copy-start | bytes 12292
  151.8 12.4 %collective-permute-start.7 = (f32[2,256,256]{2,1,0:T(8,128)}, f32[2,256,256]{2,1,0:T(8,128)}, u32[]{:S(2)}, u32[]{:S(2)}) collective-permute-start(f32[2,256,256]{2,1,0:T(8,128)} %shard_map.107), channel_id=1, source_target_pairs={{0,1},{1,2},{2,3},{4,5},{5,6},{6,7},{8,9},{9,10},{10,11},{12,13},{... | collective-permute-start | bytes 1572872 | tf_op jit(solution)/shard_map/ppermute | solution.py:249
  168.2 60.7 %collective-permute-start.8 = (f32[2,256,256]{2,1,0:T(8,128)}, f32[2,256,256]{2,1,0:T(8,128)S(1)}, u32[]{:S(2)}, u32[]{:S(2)}) collective-permute-start(f32[2,256,256]{2,1,0:T(8,128)} %shard_map.108), channel_id=1, source_target_pairs={{4,9},{5,10},{6,11},{8,5},{9,6},{10,7},{12,17},{13,18},{14,19},{16... | collective-permute-start | bytes 1572872 | tf_op jit(solution)/shard_map/ppermute | solution.py:256
  175.4 53.5 %collective-permute-start.9 = (f32[2,256,256]{2,1,0:T(8,128)}, f32[2,256,256]{2,1,0:T(8,128)S(1)}, u32[]{:S(2)}, u32[]{:S(2)}) collective-permute-start(f32[2,256,256]{2,1,0:T(8,128)} %shard_map.108), channel_id=1, source_target_pairs={{0,9},{1,10},{2,11},{8,17},{9,18},{10,19},{12,5},{13,6},{14,7},{16... | collective-permute-start | bytes 1572872 | tf_op jit(solution)/shard_map/ppermute | solution.py:257
  180.5 26.5 %collective-permute-start.10 = (f32[2,256,256]{2,1,0:T(8,128)}, f32[2,256,256]{2,1,0:T(8,128)S(1)}, u32[]{:S(2)}, u32[]{:S(2)}) collective-permute-start(f32[2,256,256]{2,1,0:T(8,128)} %shard_map.108), channel_id=1, source_target_pairs={{0,1},{1,2},{2,3},{4,5},{5,6},{6,7},{8,9},{9,10},{10,11},{12,13},{... | collective-permute-start | bytes 1572872 | tf_op jit(solution)/shard_map/ppermute | solution.py:255
  207.0 0.8 copy-start.6
  217.2 1.3 copy-start
  228.9 0.8 copy-start.3
  228.9 1.0 copy-start.4
  243.5 8.1 %collective-permute-start.11 = (f32[4,2,256,256]{3,2,1,0:T(8,128)}, f32[4,2,256,256]{3,2,1,0:T(8,128)S(1)}, u32[]{:S(2)}, u32[]{:S(2)}) collective-permute-start(f32[4,2,256,256]{3,2,1,0:T(8,128)} %get-tuple-element.17), channel_id=1, source_target_pairs={{0,4},{4,0},{8,12},{12,8},{16,20},{20,16},{24,28},{28,24},{1,5},{5... | collective-permute-start | bytes 6291464 | tf_op jit(solution)/shard_map/ppermute | solution.py:305
where the time goes:
time: 257 us; the launch traced here: 255 us
  waiting for transfers between devices  110 us (43%)
  Pallas kernels  57.3 us (22%)
  starting transfers between devices  43.2 us (17%)
  other arithmetic  21.9 us (9%)
  blocking collectives  13.1 us (5%)
  local copies, waits for them, and re-layouts  7.99 us (3%)
    ppermute x4, waiting for transfers between devices, halo_planes(): return (lax.ppermute(last, axis, up), lax.ppermute(first, axis, down))  65.3 us
    pallas_call x7, Pallas kernels, call(): pl.pallas_call(kernel, out_shape=out_shapes, compiler_params=pltpu.Compil...  57.3 us
    ppermute x3, waiting for transfers between devices, per_device(): carried = lax.ppermute(leaving, 'slab', onward)  41.1 us
    reduce_sum x1, other arithmetic, orbital_values(): values = jnp.sum(jnp.where(hit, table, 0.0), axis=(2, 3))  16.3 us
    psum x1, blocking collectives, orbital_values(): return lax.psum(values, 'energy')  13.1 us
    ppermute x4, starting transfers between devices, halo_planes(): return (lax.ppermute(last, axis, up), lax.ppermute(first, axis, down))  10.8 us
    ppermute x3, starting transfers between devices, per_device(): carried = lax.ppermute(leaving, 'slab', onward)  9.16 us
    ppermute x1, starting transfers between devices, per_device(): carried_near = lax.ppermute(leaving, ('energy', 'slab'), both(near_pairs))  7.19 us
  transfers between devices with their start and end apart: 12, of which 6 were waited for; matrix products, arithmetic and copies ran while one was open for 9% of the time, Pallas kernels for 17%

commit v1 on v0

v1 whole, which is shorter than its diff:
```python
import functools
import jax
import jax.numpy as jnp
from jax import lax
from jax.experimental import pallas as pl
from jax.experimental.pallas import tpu as pltpu
from jax.sharding import PartitionSpec as P

VMEM_LIMIT = 56 * 1024 * 1024


def halves(value):
    high = value.astype(jnp.bfloat16)
    low = (value - high.astype(jnp.float32)).astype(jnp.bfloat16)
    return high, low


def left_form(block):
    forms = []
    for real, imag in zip(halves(block[0]), halves(block[1])):
        upper = jnp.concatenate([real, -imag], axis=1)
        lower = jnp.concatenate([imag, real], axis=1)
        forms.append(jnp.concatenate([upper, lower], axis=0))
    return forms


def right_form(block, axis=0):
    return [
        jnp.concatenate([real, imag], axis=axis)
        for real, imag in zip(halves(block[0]), halves(block[1]))
    ]


def three_passes(left, right, flipped):
    dims = (((1,), (1 if flipped else 0,)), ((), ()))
    dot = functools.partial(
        lax.dot_general, dimension_numbers=dims, preferred_element_type=jnp.float32
    )
    out = dot(left[0], right[0]) + (dot(left[0], right[1]) + dot(left[1], right[0]))
    width = out.shape[0] // 2
    return out[:width], out[width:]


def row_blocks(block, count=2):
    rows = block[0].shape[0] // count
    return [
        (block[0][i * rows : (i + 1) * rows], block[1][i * rows : (i + 1) * rows])
        for i in range(count)
    ]


def stacked_rows(blocks):
    return tuple(jnp.concatenate([b[part] for b in blocks], axis=0) for part in range(2))


def product(former, latter):
    right = right_form(latter)
    return stacked_rows(
        [three_passes(left_form(rows), right, False) for rows in row_blocks(former)]
    )


def sandwich(link, inner):
    right, outer = right_form(inner), right_form(link, 1)
    half_way = [three_passes(left_form(rows), right, False) for rows in row_blocks(link)]
    return stacked_rows([three_passes(left_form(rows), outer, True) for rows in half_way])


def added(first, second):
    return first[0] + second[0], first[1] + second[1]


def pair_of(ref, *where):
    return ref[(*where, 0)], ref[(*where, 1)]


def put(ref, value, *where):
    ref[(*where, 0)] = value[0]
    ref[(*where, 1)] = value[1]


def call(kernel, out_shapes, *operands, **more):
    return pl.pallas_call(
        kernel,
        out_shape=out_shapes,
        compiler_params=pltpu.CompilerParams(vmem_limit_bytes=VMEM_LIMIT),
        **more,
    )(*operands)


def shape(*dims):
    return jax.ShapeDtypeStruct(dims, jnp.float32)


def gather_kernel(rows, field, perm, charge, before, after, key, lane, out):
    total, depth = charge.shape
    count = key.shape[0]
    height = total // count
    row_ids = lax.broadcasted_iota(jnp.int32, (total, depth), 0) % rows
    lane_ids = lax.broadcasted_iota(jnp.int32, (total, depth), 1)

    def neighbours(inner, first, last):
        down = jnp.concatenate([first, inner[:-rows]], axis=0)
        up = jnp.concatenate([inner[rows:], last], axis=0)
        left = jnp.where(lane_ids == 0, 0.0, pltpu.roll(inner, 1, axis=1))
        right = jnp.where(lane_ids == depth - 1, 0.0, pltpu.roll(inner, depth - 1, axis=1))
        low = jnp.where(row_ids == 0, 0.0, pltpu.roll(inner, 1, axis=0))
        high = jnp.where(row_ids == rows - 1, 0.0, pltpu.roll(inner, total - 1, axis=0))
        return (down + up) + (left + right) + (low + high)

    first, last = (before[0], before[1]), (after[0], after[1])
    field_now, perm_now = field[...], perm[...]
    both = perm_now * field_now
    own = [
        charge[...],
        perm_now,
        neighbours(field_now, first[0], last[0]),
        neighbours(both, first[0] * first[1], last[0] * last[1]),
        neighbours(perm_now, first[1], last[1]),
    ]
    beside = [jnp.zeros_like(both), jnp.zeros_like(both), field_now, both, perm_now]
    kinds = len(own)
    places = lax.broadcasted_iota(jnp.int32, (2 * height, key.shape[2]), 0)
    for slab in range(count):
        cut = slice(slab * height, (slab + 1) * height)
        table = jnp.concatenate(
            [
                jnp.concatenate([t[cut] for t in own], axis=1),
                jnp.concatenate([t[cut] for t in beside], axis=1),
            ],
            axis=0,
        ).T
        high, rest = halves(table)
        middle = rest.astype(jnp.float32)
        lowest = ((table - high.astype(jnp.float32)) - middle).astype(jnp.bfloat16)
        hit = jnp.where(places == key[slab], 1.0, 0.0).astype(jnp.bfloat16)
        found = jnp.dot(
            jnp.concatenate([high, rest, lowest], axis=1),
            jnp.concatenate([hit, hit, hit], axis=0),
            preferred_element_type=jnp.float32,
        )
        depths = lax.broadcasted_iota(jnp.int32, (depth, key.shape[2]), 0)
        here = depths == lane[slab]
        for kind in range(kinds):
            part = found[kind * depth : (kind + 1) * depth]
            out[kind, slab : slab + 1, :] = jnp.sum(
                jnp.where(here, part, 0.0), axis=0, keepdims=True
            )


def potential_of(sums, slab):
    charge, perm, fields, both, perms = (sums[k, slab : slab + 1, :] for k in range(5))
    return (charge + 0.5 * (perm * fields + both)) / (3.0 * perm + 0.5 * perms)


def source_of(block, potential):
    scaled = (block[0] * potential, block[1] * potential)
    return added(block, product(scaled, block))


def linkage_kernel(free, coupling, link, whole_map):
    count = free.shape[0]
    links = []
    for slab in range(count):
        links.append(product(pair_of(free, slab), pair_of(coupling, slab)))
        put(link, links[-1], slab)
    while len(links) > 1:
        paired = [product(b, a) for a, b in zip(links[0::2], links[1::2])]
        links = paired + links[len(paired) * 2 :]
    put(whole_map, links[0])


def source_kernel(free, link, sums, source, whole_source):
    count = free.shape[0]
    state = None
    for slab in range(count):
        now = source_of(pair_of(free, slab), potential_of(sums, slab))
        put(source, now, slab)
        state = now if state is None else added(sandwich(pair_of(link, slab), state), now)
    put(whole_source, state)


def hop_kernel(whole_map, whole_source, carried, out):
    put(out, added(sandwich(pair_of(whole_map), pair_of(carried)), pair_of(whole_source)))


def beside_kernel(free, coupling, sums, link, source):
    for slab in range(free.shape[0]):
        block = pair_of(free, slab)
        put(link, product(block, pair_of(coupling, slab)), slab)
        put(source, source_of(block, potential_of(sums, slab)), slab)


def greens_kernel(link, source, carried, greens, state):
    @pl.when(pl.program_id(0) == 0)
    def _():
        state[...] = carried[...]

    now = added(sandwich(pair_of(link, 0), pair_of(state)), pair_of(source, 0))
    put(state, now)
    put(greens, now, 0)


def mixing_kernel(pick, link, source, carried, own, first, weights, here, there, state):
    @pl.when(pl.program_id(0) == 0)
    def _():
        state[...] = carried[...]

    second = added(sandwich(pair_of(link, 0), pair_of(state)), pair_of(source, 0))
    put(state, second)
    for part in range(2):
        first_now = first[0, part]
        here[0, part] = weights[0] * first_now + weights[1] * second[part]
        picked = jnp.where(pick[0] == 0, first_now, second[part])
        there[0, part] = weights[2] * own[0, part] + weights[3] * picked


def relaxed(field, perm, charge, halos):
    numerator = charge
    denominator = jnp.zeros_like(charge)
    for dim in range(3):
        length = charge.shape[dim]
        before, after = halos[dim]
        for side in range(2):
            sides = []
            for which, array in enumerate((field, perm)):
                if side == 0:
                    kept = lax.slice_in_dim(array, 1, length, axis=dim)
                    parts = [kept, after[which]]
                else:
                    kept = lax.slice_in_dim(array, 0, length - 1, axis=dim)
                    parts = [before[which], kept]
                sides.append(jnp.concatenate(parts, axis=dim))
            face = 0.5 * (perm + sides[1])
            numerator = numerator + face * sides[0]
            denominator = denominator + face
    return numerator / denominator


def halo_planes(stacked, axis, dim):
    peers, length = lax.axis_size(axis), stacked.shape[dim]
    up = [(i, i + 1) for i in range(peers - 1)]
    down = [(j, i) for i, j in up]
    last = lax.slice_in_dim(stacked, length - 1, length, axis=dim)
    first = lax.slice_in_dim(stacked, 0, 1, axis=dim)
    return lax.ppermute(last, axis, up), lax.ppermute(first, axis, down)


def orbital_sums(potential_old, permittivity, charge, slab_halo, owner_cell):
    slab_count, orbitals = owner_cell.shape
    cells, rows, depth = charge.shape
    cells = cells // slab_count
    cross = rows * lax.axis_size("energy")
    first = owner_cell // (cross * depth)
    second = (owner_cell // depth) % cross - lax.axis_index("energy") * rows
    third = owner_cell % depth
    mine = first * rows + second
    low = cells * rows + first * rows
    high = low + rows - 1
    key = jnp.where(second == -1, low, jnp.where(second == rows, high, -1))
    key = jnp.where((second >= 0) & (second < rows), mine, key)
    flat = [array.reshape(-1, depth) for array in (potential_old, permittivity, charge)]
    planes = [plane.reshape(2, rows, depth) for plane in slab_halo]
    sums = call(
        functools.partial(gather_kernel, rows),
        shape(5, slab_count, orbitals),
        *flat,
        *planes,
        key.reshape(slab_count, 1, orbitals),
        third.reshape(slab_count, 1, orbitals),
    )
    return lax.psum(sums, "energy")


def per_device(
    potential_old,
    charge,
    permittivity,
    owner_cell,
    green_free,
    coupling,
    shifts,
    occupation,
    mode_tiles,
):
    energies, peers = lax.axis_size("energy"), lax.axis_size("slab")
    mine = lax.axis_index("energy")
    free = green_free[0]
    count, _, width, _ = free.shape
    whole = shape(2, width, width)
    blocks = shape(count, 2, width, width)

    everyone = range(energies)
    relayed = energies == 8
    if relayed:
        first_pairs = [(e, e ^ 2) for e in everyone]
        second_pairs = [(2, 4), (3, 5), (4, 2), (5, 3)]
        relay_pairs = [(0, 4), (1, 5), (6, 2), (7, 3)]
        turned = (mine // 2) % 2
    else:
        first_pairs = [(e, e - 2) for e in everyone if e >= 2]
        second_pairs = [(e, e + 2) for e in everyone if e + 2 < energies]
        relay_pairs = None
        turned = jnp.zeros_like(mine)
    twin_pairs = [(e, e ^ 1) for e in everyone]

    stacked = jnp.stack([potential_old, permittivity])
    slab_halo = halo_planes(stacked, "slab", 1)
    sums = orbital_sums(potential_old, permittivity, charge, slab_halo, owner_cell)
    link, whole_map = call(linkage_kernel, (blocks, whole), free, coupling)

    stacked, free_out, sums = lax.optimization_barrier((stacked, free, sums))
    source, whole_source = call(source_kernel, (blocks, whole), free, link, sums)
    energy_halo = halo_planes(stacked, "energy", 2)
    edge = jnp.zeros((2, *charge.shape[:2], 1), jnp.float32)
    potential_new = relaxed(
        potential_old, permittivity, charge, (slab_halo, energy_halo, (edge, edge))
    )
    cuts = [free_out[: count // 2], free_out[count // 2 :]]
    free_first = [lax.ppermute(cut, "energy", first_pairs) for cut in cuts]
    if relayed:
        free_second = [lax.ppermute(cut, "energy", relay_pairs) for cut in free_first]
    else:
        free_second = [lax.ppermute(cut, "energy", second_pairs) for cut in cuts]

    onward = [(i, i + 1) for i in range(peers - 1)]
    leaving = whole_source
    for _ in range(peers - 2):
        carried = lax.ppermute(leaving, "slab", onward)
        leaving = call(hop_kernel, whole, whole_map, whole_source, carried)

    def both(pairs):
        return [(a * peers + i, b * peers + j) for a, b in pairs for i, j in onward]

    carried = lax.ppermute(leaving, "slab", onward)
    carried_first = lax.ppermute(leaving, ("energy", "slab"), both(first_pairs))
    carried_second = lax.ppermute(leaving, ("energy", "slab"), both(second_pairs))

    def beside(parts):
        made = []
        for index, part in enumerate(parts):
            cut = slice(index * count // 2, (index + 1) * count // 2)
            half = shape(count // 2, 2, width, width)
            made.append(call(beside_kernel, (half, half), part, coupling[cut], sums[:, cut]))
        return made

    beside_first, beside_second = beside(free_first), beside(free_second)

    block = pl.BlockSpec((1, 2, width, width), lambda s: (s, 0, 0, 0))
    one_state = pl.BlockSpec((2, width, width), lambda s: (0, 0, 0))
    state = pltpu.VMEM((2, width, width), jnp.float32)

    def greens_of(link, source, carried):
        return call(
            greens_kernel,
            shape(*link.shape),
            link,
            source,
            carried,
            grid=(link.shape[0],),
            in_specs=[block, block, one_state],
            out_specs=block,
            scratch_shapes=[state],
        )

    greens = greens_of(link, source, carried)
    greens_first = []
    for part in beside_first:
        greens_first.append(greens_of(*part, carried_first))
        carried_first = greens_first[-1][-1]

    odd = mine % 2
    distance = jnp.array([2, 2, 1, 1], jnp.int32)
    lowered = jnp.stack([turned, 1 - turned, 1 - odd, odd]).astype(jnp.float32)
    factors = (shifts[None, :] == distance[:, None]) * (occupation[None, :] + lowered[:, None])
    weights = jnp.sum(factors[:, :, None, None] * mode_tiles[None], axis=1)
    pick = jnp.reshape(turned ^ odd, (1,)).astype(jnp.int32)

    outputs = []
    half = count // 2
    own_block = [
        pl.BlockSpec((1, 2, width, width), lambda s, first=i * half: (first + s, 0, 0, 0))
        for i in range(2)
    ]
    for index, part in enumerate(beside_second):
        here, there, carried_second = call(
            mixing_kernel,
            (shape(half, 2, width, width), shape(half, 2, width, width), whole),
            pick,
            *part,
            carried_second,
            greens,
            greens_first[index],
            weights,
            grid=(half,),
            in_specs=[
                pl.BlockSpec(memory_space=pltpu.SMEM),
                block,
                block,
                one_state,
                own_block[index],
                block,
                pl.BlockSpec((4, width, width), lambda s: (0, 0, 0)),
            ],
            out_specs=(block, block, one_state),
        )
        outputs.append(here + lax.ppermute(there, "energy", twin_pairs))
    return potential_new, jnp.concatenate(outputs, axis=0)[None]


def solution(mesh):
    in_specs = (
        P("slab", "energy", None),
        P("slab", "energy", None),
        P("slab", "energy", None),
        P("slab", None),
        P("energy", "slab", None, None, None),
        P("slab", None, None, None),
        P(),
        P(),
        P(),
    )
    out_specs = (P("slab", "energy", None), P("energy", "slab", None, None, None))
    return jax.shard_map(
        per_device, mesh=mesh, in_specs=in_specs, out_specs=out_specs, check_vma=False
    )
```

time: 257 us -> 172 us (0.67)
  the two profiles are of different devices: /device:TPU:13 before, /device:TPU:0 now
where the time goes in v1:
time: 172 us; the launch traced here: 171 us
  Pallas kernels  67.9 us (39%)
  starting transfers between devices  43.1 us (25%)
  blocking collectives  25 us (15%)
  waiting for transfers between devices  17.2 us (10%)
  local copies, waits for them, and re-layouts  10.2 us (6%)
  other arithmetic  6.3 us (4%)
    pallas_call x14, Pallas kernels, call(): pl.pallas_call(kernel, out_shape=out_shapes, compiler_params=pltpu.Compil...  67.9 us
    psum x1, blocking collectives, orbital_sums(): return lax.psum(sums, 'energy')  25 us
    ppermute x3, starting transfers between devices, per_device(): carried = lax.ppermute(leaving, 'slab', onward)  11.6 us
    ppermute x4, starting transfers between devices, halo_planes(): return (lax.ppermute(last, axis, up), lax.ppermute(first, axis, down))  10.5 us
    ppermute x3, waiting for transfers between devices, per_device(): carried = lax.ppermute(leaving, 'slab', onward)  8.14 us
    ppermute x2, starting transfers between devices, per_device(): lax.ppermute(cut, 'energy', relay_pairs)  7.92 us
    ppermute x2, waiting for transfers between devices, per_device(): free_first = [lax.ppermute(cut, 'energy', first_pairs) for cut in cuts]  7.29 us
    ppermute x2, starting transfers between devices, per_device(): outputs.append(here + lax.ppermute(there, 'energy', twin_pairs))  6.09 us
  transfers between devices with their start and end apart: 15, of which 3 were waited for; matrix products, arithmetic and copies ran while one was open for 6% of the time, Pallas kernels for 38%

profile of v1, /device:TPU:0, one launch (start us, length us, event | category | flops | bytes accessed | tf_op | source)
XLA Modules:
  0.0 170.8 jit_solution(1997402529919421335)
XLA Ops:
  1.4 4.9 %collective-permute-start.1 = (f32[2,1,4,128]{3,2,0,1:T(4,128)S(1)}, f32[2,1,4,128]{3,2,0,1:T(4,128)S(1)}, u32[]{:S(2)}, u32[]{:S(2)}) collective-permute-start(f32[2,1,4,128]{3,2,0,1:T(4,128)S(1)} %get-tuple-element.48), channel_id=1, source_target_pairs={{0,1},{1,2},{2,3},{4,5},{5,6},{6,7},{8,9},{9,10},{10,11},{12,13},{... | collective-permute-start | bytes 12296 | tf_op jit(solution)/shard_map/ppermute | solution.py:246
  10.3 6.3 %shard_map.115 = (f32[4,2,256,256]{3,2,1,0:T(8,128)}, f32[2,256,256]{2,1,0:T(8,128)}) custom-call(f32[4,2,256,256]{3,2,1,0:T(8,128)} %bitcast.43, f32[4,2,256,256]{3,2,1,0:T(8,128)} %coupling.1), custom_call_target="tpu_custom_call" | custom-call | tf_op jit(solution)/shard_map/pallas_call | solution.py:83
  17.2 2.5 %shard_map.113 = f32[5,4,256]{2,1,0:T(4,128)} custom-call(f32[64,128]{1,0:T(8,128)} %bitcast.51, f32[64,128]{1,0:T(8,128)} %bitcast.48, f32[64,128]{1,0:T(8,128)} %bitcast.52, f32[2,4,128]{2,1,0:T(4,128)} %bitcast.53, f32[2,4,128]{2,1,0:T(4,128)} %bitcast.54, s32[4,1,256]{2,1,0:T(1,128)} %copy.17.key, s32[4,1,256]{2,1,0:T(1,128)} %reshape.122.lane), custom_call_target="tpu_custom_call" | custom-call | tf_op jit(solution)/shard_map/pallas_call | solution.py:83
  19.8 25.0 %psum.7.sums = f32[5,4,256]{2,1,0:T(4,128)} all-reduce(f32[5,4,256]{2,1,0:T(4,128)} %shard_map.113), channel_id=1, replica_groups=mesh['energy'=8,'slab'=4] {'energy'}, use_global_device_ids=true, to_apply=%region_0.1 | all-reduce | flops 5120 | bytes 40960 | tf_op jit(solution)/shard_map/psum | solution.py:272
  45.1 2.0 %collective-permute-start.12 = (f32[2,2,256,256]{3,2,1,0:T(8,128)S(1)}, f32[2,2,256,256]{3,2,1,0:T(8,128)S(1)}, u32[]{:S(2)}, u32[]{:S(2)}) collective-permute-start(f32[2,2,256,256]{3,2,1,0:T(8,128)S(1)} %get-tuple-element.45), channel_id=1, source_target_pairs={{0,8},{4,12},{8,0},{12,4},{16,24},{20,28},{24,16},{28,20},{1,9},{5... | collective-permute-start | bytes 3145736 | tf_op jit(solution)/shard_map/ppermute | solution.py:320
  47.8 7.6 %shard_map.116 = (f32[4,2,256,256]{3,2,1,0:T(8,128)}, f32[2,256,256]{2,1,0:T(8,128)}) custom-call(f32[4,2,256,256]{3,2,1,0:T(8,128)} %bitcast.44, f32[4,2,256,256]{3,2,1,0:T(8,128)} %get-tuple-element.28.link, f32[5,4,256]{2,1,0:T(4,128)} %psum.7.sums), custom_call_target="tpu_custom_call" | custom-call | tf_op jit(solution)/shard_map/pallas_call | solution.py:83
  55.3 4.4 %collective-permute-start.6 = (f32[2,256,256]{2,1,0:T(8,128)}, f32[2,256,256]{2,1,0:T(8,128)S(1)}, u32[]{:S(2)}, u32[]{:S(2)}) collective-permute-start(f32[2,256,256]{2,1,0:T(8,128)} %get-tuple-element.29.whole_source), channel_id=1, source_target_pairs={{0,1},{1,2},{2,3},{4,5},{5,6},{6,7},{8,9},{9,10},{10,11},{12,13},{... | collective-permute-start | bytes 1572872 | tf_op jit(solution)/shard_map/ppermute | solution.py:329
  60.0 8.1 %collective-permute-done.6.carried = f32[2,256,256]{2,1,0:T(8,128)S(1)} collective-permute-done((f32[2,256,256]{2,1,0:T(8,128)}, f32[2,256,256]{2,1,0:T(8,128)S(1)}, u32[]{:S(2)}, u32[]{:S(2)}) %collective-permute-start.6) | collective-permute-done | bytes 524320 | tf_op jit(solution)/shard_map/ppermute | solution.py:329
  68.9 3.2 %shard_map.117 = f32[2,256,256]{2,1,0:T(8,128)} custom-call(f32[2,256,256]{2,1,0:T(8,128)} %get-tuple-element.27.whole_map, f32[2,256,256]{2,1,0:T(8,128)} %get-tuple-element.29.whole_source, f32[2,256,256]{2,1,0:T(8,128)} %copy-done.11), custom_call_target="tpu_custom_call" | custom-call | tf_op jit(solution)/shard_map/pallas_call | solution.py:83
  72.1 4.4 %collective-permute-start.7 = (f32[2,256,256]{2,1,0:T(8,128)}, f32[2,256,256]{2,1,0:T(8,128)S(1)}, u32[]{:S(2)}, u32[]{:S(2)}) collective-permute-start(f32[2,256,256]{2,1,0:T(8,128)} %shard_map.117), channel_id=1, source_target_pairs={{0,1},{1,2},{2,3},{4,5},{5,6},{6,7},{8,9},{9,10},{10,11},{12,13},{... | collective-permute-start | bytes 1572872 | tf_op jit(solution)/shard_map/ppermute | solution.py:329
  76.6 1.5 fusion.17
  78.1 4.6 %collective-permute-start.5 = (f32[2,2,256,256]{3,2,1,0:T(8,128)S(1)}, f32[2,2,256,256]{3,2,1,0:T(8,128)}, u32[]{:S(2)}, u32[]{:S(2)}) collective-permute-start(f32[2,2,256,256]{3,2,1,0:T(8,128)S(1)} %collective-permute-done.4.free), channel_id=1, source_target_pairs={{0,16},{4,20},{24,8},{28,12},{1,17},{5,21},{25,9},{29,13},{2,18},{... | collective-permute-start | bytes 3145736 | tf_op jit(solution)/shard_map/ppermute | solution.py:322
  82.6 7.3 %collective-permute-done.12.free = f32[2,2,256,256]{3,2,1,0:T(8,128)S(1)} collective-permute-done((f32[2,2,256,256]{3,2,1,0:T(8,128)S(1)}, f32[2,2,256,256]{3,2,1,0:T(8,128)S(1)}, u32[]{:S(2)}, u32[]{:S(2)}) %collective-permute-start.12) | collective-permute-done | bytes 1048608 | tf_op jit(solution)/shard_map/ppermute | solution.py:320
  89.9 3.4 %collective-permute-start.13 = (f32[2,2,256,256]{3,2,1,0:T(8,128)S(1)}, f32[2,2,256,256]{3,2,1,0:T(8,128)S(1)}, u32[]{:S(2)}, u32[]{:S(2)}) collective-permute-start(f32[2,2,256,256]{3,2,1,0:T(8,128)S(1)} %collective-permute-done.12.free), channel_id=1, source_target_pairs={{0,16},{4,20},{24,8},{28,12},{1,17},{5,21},{25,9},{29,13},{2,18},{... | collective-permute-start | bytes 3145736 | tf_op jit(solution)/shard_map/ppermute | solution.py:322
  94.2 3.2 %shard_map.118 = f32[2,256,256]{2,1,0:T(8,128)} custom-call(f32[2,256,256]{2,1,0:T(8,128)} %get-tuple-element.27.whole_map, f32[2,256,256]{2,1,0:T(8,128)} %get-tuple-element.29.whole_source, f32[2,256,256]{2,1,0:T(8,128)} %copy-done.10), custom_call_target="tpu_custom_call" | custom-call | tf_op jit(solution)/shard_map/pallas_call | solution.py:83
  97.4 4.1 %collective-permute-start.10 = (f32[2,256,256]{2,1,0:T(8,128)}, f32[2,256,256]{2,1,0:T(8,128)}, u32[]{:S(2)}, u32[]{:S(2)}) collective-permute-start(f32[2,256,256]{2,1,0:T(8,128)} %shard_map.118), channel_id=1, source_target_pairs={{0,9},{1,10},{2,11},{4,13},{5,14},{6,15},{8,1},{9,2},{10,3},{12,5}... | collective-permute-start | bytes 1572872 | tf_op jit(solution)/shard_map/ppermute | solution.py:336
  101.5 1.4 multiply_reduce_fusion.weights
  102.9 2.7 %collective-permute-start.9 = (f32[2,256,256]{2,1,0:T(8,128)}, f32[2,256,256]{2,1,0:T(8,128)S(1)}, u32[]{:S(2)}, u32[]{:S(2)}) collective-permute-start(f32[2,256,256]{2,1,0:T(8,128)} %shard_map.118), channel_id=1, source_target_pairs={{0,1},{1,2},{2,3},{4,5},{5,6},{6,7},{8,9},{9,10},{10,11},{12,13},{... | collective-permute-start | bytes 1572872 | tf_op jit(solution)/shard_map/ppermute | solution.py:335
  107.1 4.4 %shard_map.120 = (f32[2,2,256,256]{3,2,1,0:T(8,128)}, f32[2,2,256,256]{3,2,1,0:T(8,128)}) custom-call(f32[2,2,256,256]{3,2,1,0:T(8,128)} %copy-done.8, f32[2,2,256,256]{3,2,1,0:T(8,128)} %get-tuple-element.42.coupling, f32[5,2,256]{2,1,0:T(2,128)} %get-tuple-element.62.sums), custom_call_target="tpu_custom_call" | custom-call | tf_op jit(solution)/shard_map/pallas_call | solution.py:83
  111.5 4.3 %shard_map.124 = (f32[2,2,256,256]{3,2,1,0:T(8,128)}, f32[2,2,256,256]{3,2,1,0:T(8,128)}) custom-call(f32[2,2,256,256]{3,2,1,0:T(8,128)} %copy-done.7, f32[2,2,256,256]{3,2,1,0:T(8,128)} %get-tuple-element.43.coupling, f32[5,2,256]{2,1,0:T(2,128)} %get-tuple-element.63.sums), custom_call_target="tpu_custom_call" | custom-call | tf_op jit(solution)/shard_map/pallas_call | solution.py:83
  117.1 4.4 %shard_map.121.first = f32[2,2,256,256]{3,2,1,0:T(8,128)} custom-call(f32[2,2,256,256]{3,2,1,0:T(8,128)} %get-tuple-element.31.link, f32[2,2,256,256]{3,2,1,0:T(8,128)} %get-tuple-element.32.source, f32[2,256,256]{2,1,0:T(8,128)} %collective-permute-done.10.carried), custom_call_target="tpu_custom_call" | custom-call | tf_op jit(solution)/shard_map/pallas_call | solution.py:83
  121.5 1.9 %slice_bitcast_fusion.carried = f32[2,256,256]{2,1,0:T(8,128)} fusion(f32[2,2,256,256]{3,2,1,0:T(8,128)} %shard_map.121.first), kind=kLoop, calls=%fused_computation.2 | loop fusion | bytes 1048576 | tf_op jit(solution)/shard_map/squeeze | solution.py:370
  123.4 4.4 %shard_map.125.first = f32[2,2,256,256]{3,2,1,0:T(8,128)} custom-call(f32[2,2,256,256]{3,2,1,0:T(8,128)} %get-tuple-element.38.link, f32[2,2,256,256]{3,2,1,0:T(8,128)} %get-tuple-element.39.source, f32[2,256,256]{2,1,0:T(8,128)} %slice_bitcast_fusion.carried), custom_call_target="tpu_custom_call" | custom-call | tf_op jit(solution)/shard_map/pallas_call | solution.py:83
  127.8 3.0 %collective-permute-start.3 = (f32[2,16,1,128]{3,2,0,1:T(1,128)S(1)}, f32[2,16,1,128]{3,2,0,1:T(1,128)S(1)}, u32[]{:S(2)}, u32[]{:S(2)}) collective-permute-start(f32[2,16,1,128]{3,2,0,1:T(1,128)S(1)} %get-tuple-element.46), channel_id=1, source_target_pairs={{0,4},{4,8},{8,12},{12,16},{16,20},{20,24},{24,28},{1,5},{5,9},{9,... | collective-permute-start | bytes 49160 | tf_op jit(solution)/shard_map/ppermute | solution.py:246
  130.8 7.0 %shard_map.119.own = f32[4,2,256,256]{3,2,1,0:T(8,128)} custom-call(f32[4,2,256,256]{3,2,1,0:T(8,128)} %get-tuple-element.28.link, f32[4,2,256,256]{3,2,1,0:T(8,128)} %get-tuple-element.30.source, f32[2,256,256]{2,1,0:T(8,128)} %copy-done.13), custom_call_target="tpu_custom_call" | custom-call | tf_op jit(solution)/shard_map/pallas_call | solution.py:83
  137.8 4.3 %shard_map.114 = (f32[2,2,256,256]{3,2,1,0:T(8,128)}, f32[2,2,256,256]{3,2,1,0:T(8,128)}) custom-call(f32[2,2,256,256]{3,2,1,0:T(8,128)} %collective-permute-done.5.free, f32[2,2,256,256]{3,2,1,0:T(8,128)} %get-tuple-element.42.coupling, f32[5,2,256]{2,1,0:T(2,128)} %get-tuple-element.62.sums), custom_call_target="tpu_custom_call" | custom-call | tf_op jit(solution)/shard_map/pallas_call | solution.py:83
  142.9 5.9 %shard_map.122 = (f32[2,2,256,256]{3,2,1,0:T(8,128)}, f32[2,2,256,256]{3,2,1,0:T(8,128)}, f32[2,256,256]{2,1,0:T(8,128)}) custom-call(s32[1]{0:T(128)} %bitcast.21.pick, f32[2,2,256,256]{3,2,1,0:T(8,128)} %get-tuple-element.25.link, f32[2,2,256,256]{3,2,1,0:T(8,128)} %get-tuple-element.26.source, f32[2,256,256]{2,1,0:T(8,128)} %copy-done.12, ...), custom_call_target="tpu_custom_call" | custom-call | tf_op jit(solution)/shard_map/pallas_call | solution.py:83
  148.8 6.0 %collective-permute-start.11 = (f32[2,2,256,256]{3,2,1,0:T(8,128)}, f32[2,2,256,256]{3,2,1,0:T(8,128)S(1)}, u32[]{:S(2)}, u32[]{:S(2)}) collective-permute-start(f32[2,2,256,256]{3,2,1,0:T(8,128)} %get-tuple-element.34), channel_id=1, source_target_pairs={{0,4},{4,0},{8,12},{12,8},{16,20},{20,16},{24,28},{28,24},{1,5},{5... | collective-permute-start | bytes 3145736 | tf_op jit(solution)/shard_map/ppermute | solution.py:407
  155.8 4.4 %shard_map.123 = (f32[2,2,256,256]{3,2,1,0:T(8,128)}, f32[2,2,256,256]{3,2,1,0:T(8,128)}) custom-call(f32[2,2,256,256]{3,2,1,0:T(8,128)} %copy-done.9, f32[2,2,256,256]{3,2,1,0:T(8,128)} %get-tuple-element.43.coupling, f32[5,2,256]{2,1,0:T(2,128)} %get-tuple-element.63.sums), custom_call_target="tpu_custom_call" | custom-call | tf_op jit(solution)/shard_map/pallas_call | solution.py:83
  160.2 6.0 %shard_map.126 = (f32[2,2,256,256]{3,2,1,0:T(8,128)}, f32[2,2,256,256]{3,2,1,0:T(8,128)}, f32[2,256,256]{2,1,0:T(8,128)}) custom-call(s32[1]{0:T(128)} %bitcast.21.pick, f32[2,2,256,256]{3,2,1,0:T(8,128)} %get-tuple-element.35.link, f32[2,2,256,256]{3,2,1,0:T(8,128)} %get-tuple-element.36.source, f32[2,256,256]{2,1,0:T(8,128)} %get-tuple-element.37.carried, ...), custom_call_target="tpu_custom_call" | custom-call | tf_op jit(solution)/shard_map/pallas_call | solution.py:83
  167.4 1.8 %collective-permute-done.14 = f32[2,2,256,256]{3,2,1,0:T(8,128)S(1)} collective-permute-done((f32[2,2,256,256]{3,2,1,0:T(8,128)}, f32[2,2,256,256]{3,2,1,0:T(8,128)S(1)}, u32[]{:S(2)}, u32[]{:S(2)}) %collective-permute-start.14) | collective-permute-done | bytes 1048608 | tf_op jit(solution)/shard_map/ppermute | solution.py:407
  169.3 1.5 maximum_bitcast_fusion
  (91 shorter events, 14.0 us)
Async XLA Ops:
  1.4 15.3 %collective-permute-start.1 = (f32[2,1,4,128]{3,2,0,1:T(4,128)S(1)}, f32[2,1,4,128]{3,2,0,1:T(4,128)S(1)}, u32[]{:S(2)}, u32[]{:S(2)}) collective-permute-start(f32[2,1,4,128]{3,2,0,1:T(4,128)S(1)} %get-tuple-element.48), channel_id=1, source_target_pairs={{0,1},{1,2},{2,3},{4,5},{5,6},{6,7},{8,9},{9,10},{10,11},{12,13},{... | collective-permute-start | bytes 12296 | tf_op jit(solution)/shard_map/ppermute | solution.py:246
  6.3 10.3 %collective-permute-start = (f32[2,1,4,128]{3,2,0,1:T(4,128)S(1)}, f32[2,1,4,128]{3,2,0,1:T(4,128)S(1)}, u32[]{:S(2)}, u32[]{:S(2)}) collective-permute-start(f32[2,1,4,128]{3,2,0,1:T(4,128)S(1)} %get-tuple-element.49), channel_id=1, source_target_pairs={{1,0},{2,1},{3,2},{5,4},{6,5},{7,6},{9,8},{10,9},{11,10},{13,12},{... | collective-permute-start | bytes 12296 | tf_op jit(solution)/shard_map/ppermute | solution.py:246
  10.3 34.5 %copy-start = (f32[1,4,2,256,256]{4,3,2,1,0:T(8,128)S(1)}, f32[1,4,2,256,256]{4,3,2,1,0:T(8,128)}, u32[]{:S(2)}) copy-start(f32[1,4,2,256,256]{4,3,2,1,0:T(8,128)} %param.14) | copy-start | bytes 6291460
  45.0 33.0 %collective-permute-start.4 = (f32[2,2,256,256]{3,2,1,0:T(8,128)S(1)}, f32[2,2,256,256]{3,2,1,0:T(8,128)S(1)}, u32[]{:S(2)}, u32[]{:S(2)}) collective-permute-start(f32[2,2,256,256]{3,2,1,0:T(8,128)S(1)} %get-tuple-element.44), channel_id=1, source_target_pairs={{0,8},{4,12},{8,0},{12,4},{16,24},{20,28},{24,16},{28,20},{1,9},{5... | collective-permute-start | bytes 3145736 | tf_op jit(solution)/shard_map/ppermute | solution.py:320
  45.1 44.8 %collective-permute-start.12 = (f32[2,2,256,256]{3,2,1,0:T(8,128)S(1)}, f32[2,2,256,256]{3,2,1,0:T(8,128)S(1)}, u32[]{:S(2)}, u32[]{:S(2)}) collective-permute-start(f32[2,2,256,256]{3,2,1,0:T(8,128)S(1)} %get-tuple-element.45), channel_id=1, source_target_pairs={{0,8},{4,12},{8,0},{12,4},{16,24},{20,28},{24,16},{28,20},{1,9},{5... | collective-permute-start | bytes 3145736 | tf_op jit(solution)/shard_map/ppermute | solution.py:320
  55.3 21.2 %copy-start.1 = (f32[4,2,256,256]{3,2,1,0:T(8,128)S(1)}, f32[4,2,256,256]{3,2,1,0:T(8,128)}, u32[]{:S(2)}) copy-start(f32[4,2,256,256]{3,2,1,0:T(8,128)} %coupling.1) | copy-start | bytes 6291460
  55.3 12.8 %collective-permute-start.6 = (f32[2,256,256]{2,1,0:T(8,128)}, f32[2,256,256]{2,1,0:T(8,128)S(1)}, u32[]{:S(2)}, u32[]{:S(2)}) collective-permute-start(f32[2,256,256]{2,1,0:T(8,128)} %get-tuple-element.29.whole_source), channel_id=1, source_target_pairs={{0,1},{1,2},{2,3},{4,5},{5,6},{6,7},{8,9},{9,10},{10,11},{12,13},{... | collective-permute-start | bytes 1572872 | tf_op jit(solution)/shard_map/ppermute | solution.py:329
  72.1 21.2 %copy-start.24 = (f32[4]{0:T(128)S(1)}, f32[4]{0:T(128)}, u32[]{:S(2)}) copy-start(f32[4]{0:T(128)} %param.17) | copy-start | bytes 52
  72.1 21.2 %copy-start.25 = (s32[4]{0:T(128)S(1)}, s32[4]{0:T(128)}, u32[]{:S(2)}) copy-start(s32[4]{0:T(128)} %param.16) | copy-start | bytes 52
  72.1 21.2 %copy-start.26 = (s32[4]{0:T(128)S(1)}, s32[4]{0:T(128)}, u32[]{:S(2)}) copy-start(s32[4]{0:T(128)} %constant.103.clone) | copy-start | bytes 52
  72.1 21.3 %collective-permute-start.7 = (f32[2,256,256]{2,1,0:T(8,128)}, f32[2,256,256]{2,1,0:T(8,128)S(1)}, u32[]{:S(2)}, u32[]{:S(2)}) collective-permute-start(f32[2,256,256]{2,1,0:T(8,128)} %shard_map.117), channel_id=1, source_target_pairs={{0,1},{1,2},{2,3},{4,5},{5,6},{6,7},{8,9},{9,10},{10,11},{12,13},{... | collective-permute-start | bytes 1572872 | tf_op jit(solution)/shard_map/ppermute | solution.py:329
  78.1 23.4 %copy-start.6 = (f32[4,256,256]{2,1,0:T(8,128)S(1)}, f32[4,256,256]{2,1,0:T(8,128)}, u32[]{:S(2)}) copy-start(f32[4,256,256]{2,1,0:T(8,128)} %param.18) | copy-start | bytes 3145732
  78.1 24.8 %copy-start.8 = (f32[2,2,256,256]{3,2,1,0:T(8,128)}, f32[2,2,256,256]{3,2,1,0:T(8,128)S(1)}, u32[]{:S(2)}) copy-start(f32[2,2,256,256]{3,2,1,0:T(8,128)S(1)} %collective-permute-done.4.free) | copy-start | bytes 3145732
  78.1 59.7 %collective-permute-start.5 = (f32[2,2,256,256]{3,2,1,0:T(8,128)S(1)}, f32[2,2,256,256]{3,2,1,0:T(8,128)}, u32[]{:S(2)}, u32[]{:S(2)}) collective-permute-start(f32[2,2,256,256]{3,2,1,0:T(8,128)S(1)} %collective-permute-done.4.free), channel_id=1, source_target_pairs={{0,16},{4,20},{24,8},{28,12},{1,17},{5,21},{25,9},{29,13},{2,18},{... | collective-permute-start | bytes 3145736 | tf_op jit(solution)/shard_map/ppermute | solution.py:322
  89.9 12.9 %copy-start.7 = (f32[2,2,256,256]{3,2,1,0:T(8,128)}, f32[2,2,256,256]{3,2,1,0:T(8,128)S(1)}, u32[]{:S(2)}) copy-start(f32[2,2,256,256]{3,2,1,0:T(8,128)S(1)} %collective-permute-done.12.free) | copy-start | bytes 3145732
  89.9 64.9 %collective-permute-start.13 = (f32[2,2,256,256]{3,2,1,0:T(8,128)S(1)}, f32[2,2,256,256]{3,2,1,0:T(8,128)S(1)}, u32[]{:S(2)}, u32[]{:S(2)}) collective-permute-start(f32[2,2,256,256]{3,2,1,0:T(8,128)S(1)} %collective-permute-done.12.free), channel_id=1, source_target_pairs={{0,16},{4,20},{24,8},{28,12},{1,17},{5,21},{25,9},{29,13},{2,18},{... | collective-permute-start | bytes 3145736 | tf_op jit(solution)/shard_map/ppermute | solution.py:322
  93.4 13.1 %copy-start.14 = (f32[5,4,256]{2,1,0:T(4,128)S(1)}, f32[5,4,256]{2,1,0:T(4,128)}, u32[]{:S(2)}) copy-start(f32[5,4,256]{2,1,0:T(4,128)} %psum.7.sums) | copy-start | bytes 61444
  97.4 18.4 %collective-permute-start.10 = (f32[2,256,256]{2,1,0:T(8,128)}, f32[2,256,256]{2,1,0:T(8,128)}, u32[]{:S(2)}, u32[]{:S(2)}) collective-permute-start(f32[2,256,256]{2,1,0:T(8,128)} %shard_map.118), channel_id=1, source_target_pairs={{0,9},{1,10},{2,11},{4,13},{5,14},{6,15},{8,1},{9,2},{10,3},{12,5}... | collective-permute-start | bytes 1572872 | tf_op jit(solution)/shard_map/ppermute | solution.py:336
  102.9 24.9 %collective-permute-start.9 = (f32[2,256,256]{2,1,0:T(8,128)}, f32[2,256,256]{2,1,0:T(8,128)S(1)}, u32[]{:S(2)}, u32[]{:S(2)}) collective-permute-start(f32[2,256,256]{2,1,0:T(8,128)} %shard_map.118), channel_id=1, source_target_pairs={{0,1},{1,2},{2,3},{4,5},{5,6},{6,7},{8,9},{9,10},{10,11},{12,13},{... | collective-permute-start | bytes 1572872 | tf_op jit(solution)/shard_map/ppermute | solution.py:335
  105.6 36.5 %collective-permute-start.8 = (f32[2,256,256]{2,1,0:T(8,128)}, f32[2,256,256]{2,1,0:T(8,128)S(1)}, u32[]{:S(2)}, u32[]{:S(2)}) collective-permute-start(f32[2,256,256]{2,1,0:T(8,128)} %shard_map.118), channel_id=1, source_target_pairs={{8,17},{9,18},{10,19},{12,21},{13,22},{14,23},{16,9},{17,10},{18,1... | collective-permute-start | bytes 1572872 | tf_op jit(solution)/shard_map/ppermute | solution.py:337
  115.8 50.5 %collective-permute-start.2 = (f32[2,16,1,128]{3,2,0,1:T(1,128)S(1)}, f32[2,16,1,128]{3,2,0,1:T(1,128)S(1)}, u32[]{:S(2)}, u32[]{:S(2)}) collective-permute-start(f32[2,16,1,128]{3,2,0,1:T(1,128)S(1)} %get-tuple-element.47), channel_id=1, source_target_pairs={{4,0},{8,4},{12,8},{16,12},{20,16},{24,20},{28,24},{5,1},{9,5},{13... | collective-permute-start | bytes 49160 | tf_op jit(solution)/shard_map/ppermute | solution.py:246
  127.8 38.6 %collective-permute-start.3 = (f32[2,16,1,128]{3,2,0,1:T(1,128)S(1)}, f32[2,16,1,128]{3,2,0,1:T(1,128)S(1)}, u32[]{:S(2)}, u32[]{:S(2)}) collective-permute-start(f32[2,16,1,128]{3,2,0,1:T(1,128)S(1)} %get-tuple-element.46), channel_id=1, source_target_pairs={{0,4},{4,8},{8,12},{12,16},{16,20},{20,24},{24,28},{1,5},{5,9},{9,... | collective-permute-start | bytes 49160 | tf_op jit(solution)/shard_map/ppermute | solution.py:246
  148.8 18.5 %collective-permute-start.11 = (f32[2,2,256,256]{3,2,1,0:T(8,128)}, f32[2,2,256,256]{3,2,1,0:T(8,128)S(1)}, u32[]{:S(2)}, u32[]{:S(2)}) collective-permute-start(f32[2,2,256,256]{3,2,1,0:T(8,128)} %get-tuple-element.34), channel_id=1, source_target_pairs={{0,4},{4,0},{8,12},{12,8},{16,20},{20,16},{24,28},{28,24},{1,5},{5... | collective-permute-start | bytes 3145736 | tf_op jit(solution)/shard_map/ppermute | solution.py:407
  160.2 6.2 %copy-start.23 = (f32[2,1,4,128]{3,2,0,1:T(4,128)S(1)}, f32[2,1,4,128]{3,2,0,1:T(4,128)}, u32[]{:S(2)}) copy-start(f32[2,1,4,128]{3,2,0,1:T(4,128)} %copy-done.22) | copy-start | bytes 12292
  160.2 6.2 %copy-start.21 = (f32[2,1,4,128]{3,2,0,1:T(4,128)S(1)}, f32[2,1,4,128]{3,2,0,1:T(4,128)}, u32[]{:S(2)}) copy-start(f32[2,1,4,128]{3,2,0,1:T(4,128)} %copy-done.20) | copy-start | bytes 12292
  160.2 6.3 %copy-start.15 = (f32[16,4,128]{2,1,0:T(4,128)S(1)}, f32[16,4,128]{2,1,0:T(4,128)}, u32[]{:S(2)}) copy-start(f32[16,4,128]{2,1,0:T(4,128)} %param.11) | copy-start | bytes 98308
  160.2 6.3 %copy-start.16 = (f32[15,4,128]{2,1,0:T(4,128)S(1)}, f32[15,4,128]{2,1,0:T(4,128)}, u32[]{:S(2)}) copy-start(f32[15,4,128]{2,1,0:T(4,128)} %get-tuple-element.54) | copy-start | bytes 92164
  160.2 6.3 %copy-start.17 = (f32[15,4,128]{2,1,0:T(4,128)S(1)}, f32[15,4,128]{2,1,0:T(4,128)}, u32[]{:S(2)}) copy-start(f32[15,4,128]{2,1,0:T(4,128)} %get-tuple-element.55) | copy-start | bytes 92164
  160.2 6.3 %copy-start.18 = (f32[15,4,128]{2,1,0:T(4,128)S(1)}, f32[15,4,128]{2,1,0:T(4,128)}, u32[]{:S(2)}) copy-start(f32[15,4,128]{2,1,0:T(4,128)} %get-tuple-element.76) | copy-start | bytes 92164
  160.2 6.3 %copy-start.19 = (f32[15,4,128]{2,1,0:T(4,128)S(1)}, f32[15,4,128]{2,1,0:T(4,128)}, u32[]{:S(2)}) copy-start(f32[15,4,128]{2,1,0:T(4,128)} %get-tuple-element.77) | copy-start | bytes 92164
  160.2 7.1 %copy-start.4 = (f32[2,2,256,256]{3,2,1,0:T(8,128)S(1)}, f32[2,2,256,256]{3,2,1,0:T(8,128)}, u32[]{:S(2)}) copy-start(f32[2,2,256,256]{3,2,1,0:T(8,128)} %get-tuple-element.33) | copy-start | bytes 3145732
  166.3 2.9 %collective-permute-start.14 = (f32[2,2,256,256]{3,2,1,0:T(8,128)}, f32[2,2,256,256]{3,2,1,0:T(8,128)S(1)}, u32[]{:S(2)}, u32[]{:S(2)}) collective-permute-start(f32[2,2,256,256]{3,2,1,0:T(8,128)} %get-tuple-element.41), channel_id=1, source_target_pairs={{0,4},{4,0},{8,12},{12,8},{16,20},{20,16},{24,28},{28,24},{1,5},{5... | collective-permute-start | bytes 3145736 | tf_op jit(solution)/shard_map/ppermute | solution.py:407
  (10 other events, 15.2 us)

commit v2 on v1

v2 whole, which is shorter than its diff:
```python
import functools
import jax
import jax.numpy as jnp
from jax import lax
from jax.experimental import pallas as pl
from jax.experimental.pallas import tpu as pltpu
from jax.sharding import PartitionSpec as P

MIB = 1024 * 1024


def halves(value):
    high = value.astype(jnp.bfloat16)
    low = (value - high.astype(jnp.float32)).astype(jnp.bfloat16)
    return high, low


def parts_of(block):
    real, imag = block
    return [halves(real), halves(imag), halves(0.5 * real + 0.5 * imag)]


def left_form(block):
    return [jnp.concatenate([high, high, low], axis=1) for high, low in parts_of(block)]


def right_form(block, axis=0):
    return [jnp.concatenate([high, low, high], axis=axis) for high, low in parts_of(block)]


def three_products(left, right, flipped):
    dims = (((1,), (1 if flipped else 0,)), ((), ()))
    by_real, by_imag, by_mean = (
        lax.dot_general(a, b, dimension_numbers=dims, preferred_element_type=jnp.float32)
        for a, b in zip(left, right)
    )
    return by_real - by_imag, 4.0 * (by_mean - 0.25 * by_real - 0.25 * by_imag)


def product(former, latter):
    return three_products(left_form(former), right_form(latter), False)


def sandwich(link, inner):
    half_way = three_products(left_form(link), right_form(inner), False)
    return three_products(left_form(half_way), right_form(link, 1), True)


def added(first, second):
    return first[0] + second[0], first[1] + second[1]


def pair_of(ref, *where):
    return ref[(*where, 0)], ref[(*where, 1)]


def put(ref, value, *where):
    ref[(*where, 0)] = value[0]
    ref[(*where, 1)] = value[1]


def call(kernel, room, out_shapes, *operands, **more):
    return pl.pallas_call(
        kernel,
        out_shape=out_shapes,
        compiler_params=pltpu.CompilerParams(vmem_limit_bytes=room * MIB),
        **more,
    )(*operands)


def shape(*dims):
    return jax.ShapeDtypeStruct(dims, jnp.float32)


def gather_kernel(rows, peers, mine, field, perm, charge, before, after, owner, out):
    total, depth = charge.shape
    count, orbitals = owner.shape
    height = total // count
    cross = rows * peers
    row_ids = lax.broadcasted_iota(jnp.int32, (total, depth), 0) % rows
    lane_ids = lax.broadcasted_iota(jnp.int32, (total, depth), 1)

    def neighbours(inner, first, last):
        down = jnp.concatenate([first, inner[:-rows]], axis=0)
        up = jnp.concatenate([inner[rows:], last], axis=0)
        left = jnp.where(lane_ids == 0, 0.0, pltpu.roll(inner, 1, axis=1))
        right = jnp.where(lane_ids == depth - 1, 0.0, pltpu.roll(inner, depth - 1, axis=1))
        low = jnp.where(row_ids == 0, 0.0, pltpu.roll(inner, 1, axis=0))
        high = jnp.where(row_ids == rows - 1, 0.0, pltpu.roll(inner, total - 1, axis=0))
        return (down + up) + (left + right) + (low + high)

    first, last = (before[0], before[1]), (after[0], after[1])
    field_now, perm_now = field[...], perm[...]
    both = perm_now * field_now
    own = [
        charge[...],
        perm_now,
        neighbours(field_now, first[0], last[0]),
        neighbours(both, first[0] * first[1], last[0] * last[1]),
        neighbours(perm_now, first[1], last[1]),
    ]
    beside = [jnp.zeros_like(both), jnp.zeros_like(both), field_now, both, perm_now]
    kinds = len(own)
    places = lax.broadcasted_iota(jnp.int32, (2 * height, orbitals), 0)
    depths = lax.broadcasted_iota(jnp.int32, (depth, orbitals), 0)
    first_row = mine[0] * rows
    step = 0
    for slab in range(count):
        cells = owner[slab : slab + 1, :]
        lane, line = cells % depth, cells // depth
        across, along = line % cross - first_row, line // cross * rows
        key = jnp.where(across == rows, height + along + rows - 1, -1)
        key = jnp.where(across == -1, height + along, key)
        key = jnp.where((across >= 0) & (across < rows), along + across, key)
        cut = slice(slab * height, (slab + 1) * height)
        table = jnp.concatenate(
            [
                jnp.concatenate([t[cut] for t in own], axis=1),
                jnp.concatenate([t[cut] for t in beside], axis=1),
            ],
            axis=0,
        ).T
        high, rest = halves(table)
        middle = rest.astype(jnp.float32)
        lowest = ((table - high.astype(jnp.float32)) - middle).astype(jnp.bfloat16)
        hit = jnp.where(places == key, 1.0, 0.0).astype(jnp.bfloat16)
        found = jnp.dot(
            jnp.concatenate([high, rest, lowest], axis=1),
            jnp.concatenate([hit, hit, hit], axis=0),
            preferred_element_type=jnp.float32,
        )
        for kind in range(kinds):
            part = found[kind * depth : (kind + 1) * depth]
            value = jnp.sum(jnp.where(depths == lane, part, 0.0), axis=0, keepdims=True)
            for piece in range(orbitals // depth):
                row = sums_row(kind, slab, count, orbitals // depth) + piece
                out[row : row + 1, :] = value[:, piece * depth : (piece + 1) * depth]
    start = kinds * count * (orbitals // depth)
    for array in (field, perm):
        for end in (0, rows - 1):
            out[start : start + total // rows, :] = array[pl.ds(end, total // rows, stride=rows), :]
            start += total // rows


def sums_row(kind, slab, count, pieces):
    return (kind * count + slab) * pieces


def potential_of(sums, slab, count, orbitals):
    pieces = orbitals // sums.shape[1]

    def value(kind):
        first = sums_row(kind, slab, count, pieces)
        return jnp.concatenate([sums[pl.ds(first + p, 1), :] for p in range(pieces)], axis=1)

    charge, perm, fields, both, perms = (value(kind) for kind in range(5))
    return (charge + 0.5 * (perm * fields + both)) / (3.0 * perm + 0.5 * perms)


def source_of(block, potential):
    scaled = (block[0] * potential, block[1] * potential)
    return added(block, product(scaled, block))


def linkage_kernel(free, coupling, link, whole_map):
    count = free.shape[0]
    links = []
    for slab in range(count):
        links.append(product(pair_of(free, slab), pair_of(coupling, slab)))
        put(link, links[-1], slab)
    while len(links) > 1:
        paired = [product(b, a) for a, b in zip(links[0::2], links[1::2])]
        links = paired + links[len(paired) * 2 :]
    put(whole_map, links[0])


def source_kernel(free, link, sums, source, whole_source):
    count = free.shape[0]
    state = None
    for slab in range(count):
        row = potential_of(sums, slab, count, free.shape[-1])
        now = source_of(pair_of(free, slab), row)
        put(source, now, slab)
        state = now if state is None else added(sandwich(pair_of(link, slab), state), now)
    put(whole_source, state)


def hop_kernel(whole_map, whole_source, carried, out):
    put(out, added(sandwich(pair_of(whole_map), pair_of(carried)), pair_of(whole_source)))


def beside_kernel(first, count, free, coupling, sums, link, source):
    block = pair_of(free, 0)
    put(link, product(block, pair_of(coupling, 0)), 0)
    row = potential_of(sums, first + pl.program_id(0), count, free.shape[-1])
    put(source, source_of(block, row), 0)


def greens_kernel(link, source, carried, greens, state):
    @pl.when(pl.program_id(0) == 0)
    def _():
        state[...] = carried[...]

    now = added(sandwich(pair_of(link, 0), pair_of(state)), pair_of(source, 0))
    put(state, now)
    put(greens, now, 0)


def mixing_kernel(pick, link, source, carried, own, first, weights, here, there, state):
    @pl.when(pl.program_id(0) == 0)
    def _():
        state[...] = carried[...]

    second = added(sandwich(pair_of(link, 0), pair_of(state)), pair_of(source, 0))
    put(state, second)
    for part in range(2):
        first_now = first[0, part]
        here[0, part] = weights[0] * first_now + weights[1] * second[part]
        picked = jnp.where(pick[0] == 0, first_now, second[part])
        there[0, part] = weights[2] * own[0, part] + weights[3] * picked


def relaxed(field, perm, charge, halos):
    numerator = charge
    denominator = jnp.zeros_like(charge)
    for dim in range(3):
        length = charge.shape[dim]
        before, after = halos[dim]
        for side in range(2):
            sides = []
            for which, array in enumerate((field, perm)):
                if side == 0:
                    kept = lax.slice_in_dim(array, 1, length, axis=dim)
                    parts = [kept, after[which]]
                else:
                    kept = lax.slice_in_dim(array, 0, length - 1, axis=dim)
                    parts = [before[which], kept]
                sides.append(jnp.concatenate(parts, axis=dim))
            face = 0.5 * (perm + sides[1])
            numerator = numerator + face * sides[0]
            denominator = denominator + face
    return numerator / denominator


def end_planes(array, dim):
    length = array.shape[dim]
    return (
        lax.slice_in_dim(array, 0, 1, axis=dim),
        lax.slice_in_dim(array, length - 1, length, axis=dim),
    )


def exchanged(payload, head):
    peers, mine = lax.axis_size("energy"), lax.axis_index("energy")
    assert peers & (peers - 1) == 0
    rest = payload[head:]
    before = after = jnp.zeros_like(rest)
    is_head = lax.broadcasted_iota(jnp.int32, payload.shape, 0) < head
    mask = 1
    while mask < peers:
        arrived = lax.ppermute(payload, "energy", [(e, e ^ mask) for e in range(peers)])
        before = jnp.where((mine ^ mask) == mine - 1, arrived[head:], before)
        after = jnp.where((mine ^ mask) == mine + 1, arrived[head:], after)
        payload = jnp.where(is_head, payload + arrived, payload)
        mask = 2 * mask + 1
    return payload, before, after


def per_device(
    potential_old,
    charge,
    permittivity,
    owner_cell,
    green_free,
    coupling,
    shifts,
    occupation,
    mode_tiles,
):
    energies, peers = lax.axis_size("energy"), lax.axis_size("slab")
    mine = lax.axis_index("energy")
    free = green_free[0]
    count, _, width, _ = free.shape
    whole = shape(2, width, width)
    blocks = shape(count, 2, width, width)

    everyone = range(energies)
    relayed = energies == 8
    if relayed:
        first_pairs = [(e, e ^ 2) for e in everyone]
        second_pairs = [(2, 4), (3, 5), (4, 2), (5, 3)]
        relay_pairs = [(0, 4), (1, 5), (6, 2), (7, 3)]
        turned = (mine // 2) % 2
    else:
        first_pairs = [(e, e - 2) for e in everyone if e >= 2]
        second_pairs = [(e, e + 2) for e in everyone if e + 2 < energies]
        relay_pairs = None
        turned = jnp.zeros_like(mine)
    twin_pairs = [(e, e ^ 1) for e in everyone]

    half = count // 2
    cuts = [free[:half], free[half:]]
    free_first = [lax.ppermute(cuts[0], "energy", first_pairs)]

    wire_up = [(i, i + 1) for i in range(peers - 1)]
    wire_down = [(j, i) for i, j in wire_up]
    stacked = jnp.stack([potential_old, permittivity])
    lower, upper = end_planes(stacked, 1)
    wire_before = lax.ppermute(upper, "slab", wire_up)
    wire_after = lax.ppermute(lower, "slab", wire_down)
    link, whole_map = call(linkage_kernel, 24, (blocks, whole), free, coupling)

    cells, rows, depth = charge.shape
    head = 5 * count * (width // depth)
    payload = call(
        functools.partial(gather_kernel, rows, energies),
        16,
        shape(head + 4 * cells, depth),
        jnp.reshape(mine, (1,)),
        *(array.reshape(-1, depth) for array in (potential_old, permittivity, charge)),
        wire_before.reshape(2, rows, depth),
        wire_after.reshape(2, rows, depth),
        owner_cell,
        in_specs=[pl.BlockSpec(memory_space=pltpu.SMEM)]
        + [pl.BlockSpec(memory_space=pltpu.VMEM)] * 6,
    )
    sums, ends_before, ends_after = exchanged(payload, head)

    cut, arrived, sums = lax.optimization_barrier((cuts[1], free_first[0], sums))
    free_first = [arrived, lax.ppermute(cut, "energy", first_pairs)]
    if relayed:
        free_second = [lax.ppermute(part, "energy", relay_pairs) for part in free_first]
    else:
        free_second = [lax.ppermute(part, "energy", second_pairs) for part in (cuts[0], cut)]
    source, whole_source = call(source_kernel, 24, (blocks, whole), free, link, sums)

    ends_before = ends_before.reshape(2, 2, cells, 1, depth)
    ends_after = ends_after.reshape(2, 2, cells, 1, depth)
    edge = jnp.zeros((2, cells, rows, 1), jnp.float32)
    halos = ((wire_before, wire_after), (ends_before[:, 1], ends_after[:, 0]), (edge, edge))
    potential_new = relaxed(potential_old, permittivity, charge, halos)

    leaving = whole_source
    for _ in range(peers - 2):
        carried = lax.ppermute(leaving, "slab", wire_up)
        leaving = call(hop_kernel, 12, whole, whole_map, whole_source, carried)

    def both(pairs):
        return [(a * peers + i, b * peers + j) for a, b in pairs for i, j in wire_up]

    carried = lax.ppermute(leaving, "slab", wire_up)
    carried_first = lax.ppermute(leaving, ("energy", "slab"), both(first_pairs))
    carried_second = lax.ppermute(leaving, ("energy", "slab"), both(second_pairs))

    block = pl.BlockSpec((1, 2, width, width), lambda s: (s, 0, 0, 0))
    one_state = pl.BlockSpec((2, width, width), lambda s: (0, 0, 0))
    own_block = [
        pl.BlockSpec((1, 2, width, width), lambda s, first=i * half: (first + s, 0, 0, 0))
        for i in range(2)
    ]

    def beside(parts):
        made = []
        for index, part in enumerate(parts):
            made.append(
                call(
                    functools.partial(beside_kernel, index * half, count),
                    16,
                    (shape(half, 2, width, width), shape(half, 2, width, width)),
                    part,
                    coupling,
                    sums,
                    grid=(half,),
                    in_specs=[block, own_block[index], pl.BlockSpec(sums.shape, lambda s: (0, 0))],
                    out_specs=(block, block),
                )
            )
        return made

    beside_first, beside_second = beside(free_first), beside(free_second)

    def greens_of(link, source, carried):
        return call(
            greens_kernel,
            16,
            (shape(*link.shape), whole),
            link,
            source,
            carried,
            grid=(link.shape[0],),
            in_specs=[block, block, one_state],
            out_specs=(block, one_state),
        )

    greens, _ = greens_of(link, source, carried)
    greens_first = []
    for part in beside_first:
        made, carried_first = greens_of(*part, carried_first)
        greens_first.append(made)

    odd = mine % 2
    distance = jnp.array([2, 2, 1, 1], jnp.int32)
    lowered = jnp.stack([turned, 1 - turned, 1 - odd, odd]).astype(jnp.float32)
    factors = (shifts[None, :] == distance[:, None]) * (occupation[None, :] + lowered[:, None])
    weights = jnp.sum(factors[:, :, None, None] * mode_tiles[None], axis=1)
    pick = jnp.reshape(turned ^ odd, (1,)).astype(jnp.int32)

    outputs = []
    for index, part in enumerate(beside_second):
        here, there, carried_second = call(
            mixing_kernel,
            20,
            (shape(half, 2, width, width), shape(half, 2, width, width), whole),
            pick,
            *part,
            carried_second,
            greens,
            greens_first[index],
            weights,
            grid=(half,),
            in_specs=[
                pl.BlockSpec(memory_space=pltpu.SMEM),
                block,
                block,
                one_state,
                own_block[index],
                block,
                pl.BlockSpec((4, width, width), lambda s: (0, 0, 0)),
            ],
            out_specs=(block, block, one_state),
        )
        outputs.append(here + lax.ppermute(there, "energy", twin_pairs))
    return potential_new, jnp.concatenate(outputs, axis=0)[None]


def solution(mesh):
    in_specs = (
        P("slab", "energy", None),
        P("slab", "energy", None),
        P("slab", "energy", None),
        P("slab", None),
        P("energy", "slab", None, None, None),
        P("slab", None, None, None),
        P(),
        P(),
        P(),
    )
    out_specs = (P("slab", "energy", None), P("energy", "slab", None, None, None))
    return jax.shard_map(
        per_device, mesh=mesh, in_specs=in_specs, out_specs=out_specs, check_vma=False
    )
```

time: 172 us -> 138 us (0.80)
  the two profiles are of different devices: /device:TPU:0 before, /device:TPU:13 now
where the time goes in v2:
time: 138 us; the launch traced here: 137 us
  waiting for transfers between devices  51.9 us (38%)
  Pallas kernels  39.9 us (29%)
  starting transfers between devices  33.8 us (24%)
  local copies, waits for them, and re-layouts  7.27 us (5%)
  other arithmetic  3.34 us (2%)
    pallas_call x14, Pallas kernels, call(): pl.pallas_call(kernel, out_shape=out_shapes, compiler_params=pltpu.Compil...  39.9 us
    ppermute x3, waiting for transfers between devices, per_device(): carried = lax.ppermute(leaving, 'slab', wire_up)  26.5 us
    ppermute x3, waiting for transfers between devices, exchanged(): lax.ppermute(payload, 'energy', [(e, e ^ mask) for e in range(peers)])  16.9 us
    ppermute x3, starting transfers between devices, per_device(): carried = lax.ppermute(leaving, 'slab', wire_up)  9.73 us
    ppermute x2, starting transfers between devices, per_device(): outputs.append(here + lax.ppermute(there, 'energy', twin_pairs))  4.51 us
    ppermute x1, waiting for transfers between devices, per_device(): lax.ppermute(leaving, ('energy', 'slab'), both(second_pairs))  3.96 us
    ppermute x3, starting transfers between devices, exchanged(): lax.ppermute(payload, 'energy', [(e, e ^ mask) for e in range(peers)])  3.25 us
    ppermute x1, starting transfers between devices, per_device(): wire_before = lax.ppermute(upper, 'slab', wire_up)  3.2 us
  transfers between devices with their start and end apart: 16, of which 10 were waited for; matrix products, arithmetic and copies ran while one was open for 2% of the time, Pallas kernels for 29%

profile of v2, /device:TPU:13, one launch (start us, length us, event | category | flops | bytes accessed | tf_op | source)
XLA Modules:
  0.0 137.5 jit_solution(7850005971034321135)
XLA Ops:
  0.7 2.9 %slice_bitcast_fusion = (f32[2,2,256,256]{3,2,1,0:T(8,128)S(1)}, f32[2,2,256,256]{3,2,1,0:T(8,128)}) fusion(f32[1,4,2,256,256]{4,3,2,1,0:T(8,128)} %param.14), kind=kLoop, calls=%fused_computation.2 | loop fusion | bytes 4194304 | tf_op jit(solution)/shard_map/slice | solution.py:302
  4.8 3.2 %collective-permute-start.1 = (f32[2,1,4,128]{3,2,0,1:T(4,128)S(1)}, f32[2,1,4,128]{3,2,0,1:T(4,128)S(1)}, u32[]{:S(2)}, u32[]{:S(2)}) collective-permute-start(f32[2,1,4,128]{3,2,0,1:T(4,128)S(1)} %get-tuple-element.54), channel_id=1, source_target_pairs={{0,1},{1,2},{2,3},{4,5},{5,6},{6,7},{8,9},{9,10},{10,11},{12,13},{... | collective-permute-start | bytes 12296 | tf_op jit(solution)/shard_map/ppermute | solution.py:309
  8.0 2.1 %collective-permute-start = (f32[2,1,4,128]{3,2,0,1:T(4,128)S(1)}, f32[2,1,4,128]{3,2,0,1:T(4,128)S(1)}, u32[]{:S(2)}, u32[]{:S(2)}) collective-permute-start(f32[2,1,4,128]{3,2,0,1:T(4,128)S(1)} %get-tuple-element.55), channel_id=1, source_target_pairs={{1,0},{2,1},{3,2},{5,4},{6,5},{7,6},{9,8},{10,9},{11,10},{13,12},{... | collective-permute-start | bytes 12296 | tf_op jit(solution)/shard_map/ppermute | solution.py:310
  10.1 2.7 %collective-permute-done = f32[2,1,4,128]{3,2,0,1:T(4,128)S(1)} collective-permute-done((f32[2,1,4,128]{3,2,0,1:T(4,128)S(1)}, f32[2,1,4,128]{3,2,0,1:T(4,128)S(1)}, u32[]{:S(2)}, u32[]{:S(2)}) %collective-permute-start) | collective-permute-done | bytes 4128 | tf_op jit(solution)/shard_map/ppermute | solution.py:310
  13.9 2.0 %collective-permute-start.2 = (f32[104,128]{1,0:T(8,128)S(1)}, f32[104,128]{1,0:T(8,128)S(1)}, u32[]{:S(2)}, u32[]{:S(2)}) collective-permute-start(f32[104,128]{1,0:T(8,128)S(1)} %shard_map.113), channel_id=1, source_target_pairs={{0,4},{4,0},{8,12},{12,8},{16,20},{20,16},{24,28},{28,24},{1,5},{5... | collective-permute-start | bytes 159752 | tf_op jit(solution)/shard_map/ppermute | solution.py:261
  17.5 12.1 %collective-permute-done.3 = f32[104,128]{1,0:T(8,128)S(1)} collective-permute-done((f32[104,128]{1,0:T(8,128)S(1)}, f32[104,128]{1,0:T(8,128)S(1)}, u32[]{:S(2)}, u32[]{:S(2)}) %collective-permute-start.3) | collective-permute-done | bytes 53280 | tf_op jit(solution)/shard_map/ppermute | solution.py:261
  30.3 3.9 %collective-permute-done.4 = f32[104,128]{1,0:T(8,128)S(1)} collective-permute-done((f32[104,128]{1,0:T(8,128)S(1)}, f32[104,128]{1,0:T(8,128)S(1)}, u32[]{:S(2)}, u32[]{:S(2)}) %collective-permute-start.4) | collective-permute-done | bytes 53280 | tf_op jit(solution)/shard_map/ppermute | solution.py:261
  35.6 1.6 %copy-done.1 = f32[1,4,2,256,256]{4,3,2,1,0:T(8,128)S(1)} copy-done((f32[1,4,2,256,256]{4,3,2,1,0:T(8,128)S(1)}, f32[1,4,2,256,256]{4,3,2,1,0:T(8,128)}, u32[]{:S(2)}) %copy-start.1) | copy-done | bytes 2097176
  37.2 2.6 %shard_map.115 = (f32[4,2,256,256]{3,2,1,0:T(8,128)S(1)}, f32[2,256,256]{2,1,0:T(8,128)S(1)}) custom-call(f32[4,2,256,256]{3,2,1,0:T(8,128)S(1)} %bitcast.38, f32[4,2,256,256]{3,2,1,0:T(8,128)S(1)} %copy-done), custom_call_target="tpu_custom_call" | custom-call | tf_op jit(solution)/shard_map/pallas_call | solution.py:63
  39.8 4.1 %shard_map.116 = (f32[4,2,256,256]{3,2,1,0:T(8,128)S(1)}, f32[2,256,256]{2,1,0:T(8,128)S(1)}) custom-call(f32[4,2,256,256]{3,2,1,0:T(8,128)S(1)} %bitcast.39, f32[4,2,256,256]{3,2,1,0:T(8,128)S(1)} %get-tuple-element.31.link, f32[104,128]{1,0:T(8,128)S(1)} %add_select_fusion.sums), custom_call_target="tpu_custom_call" | custom-call | tf_op jit(solution)/shard_map/pallas_call | solution.py:63
  45.2 3.3 %collective-permute-start.7 = (f32[2,256,256]{2,1,0:T(8,128)S(1)}, f32[2,256,256]{2,1,0:T(8,128)}, u32[]{:S(2)}, u32[]{:S(2)}) collective-permute-start(f32[2,256,256]{2,1,0:T(8,128)S(1)} %get-tuple-element.32.whole_source), channel_id=1, source_target_pairs={{0,1},{1,2},{2,3},{4,5},{5,6},{6,7},{8,9},{9,10},{10,11},{12,13},{... | collective-permute-start | bytes 1572872 | tf_op jit(solution)/shard_map/ppermute | solution.py:345
  49.3 11.8 %collective-permute-done.7.carried = f32[2,256,256]{2,1,0:T(8,128)} collective-permute-done((f32[2,256,256]{2,1,0:T(8,128)S(1)}, f32[2,256,256]{2,1,0:T(8,128)}, u32[]{:S(2)}, u32[]{:S(2)}) %collective-permute-start.7) | collective-permute-done | bytes 524320 | tf_op jit(solution)/shard_map/ppermute | solution.py:345
  61.0 2.0 %shard_map.117 = f32[2,256,256]{2,1,0:T(8,128)S(1)} custom-call(f32[2,256,256]{2,1,0:T(8,128)S(1)} %get-tuple-element.30.whole_map, f32[2,256,256]{2,1,0:T(8,128)S(1)} %get-tuple-element.32.whole_source, f32[2,256,256]{2,1,0:T(8,128)} %collective-permute-done.7.carried), custom_call_target="tpu_custom_call" | custom-call | tf_op jit(solution)/shard_map/pallas_call | solution.py:63
  63.1 3.2 %collective-permute-start.8 = (f32[2,256,256]{2,1,0:T(8,128)S(1)}, f32[2,256,256]{2,1,0:T(8,128)S(1)}, u32[]{:S(2)}, u32[]{:S(2)}) collective-permute-start(f32[2,256,256]{2,1,0:T(8,128)S(1)} %shard_map.117), channel_id=1, source_target_pairs={{0,1},{1,2},{2,3},{4,5},{5,6},{6,7},{8,9},{9,10},{10,11},{12,13},{... | collective-permute-start | bytes 1572872 | tf_op jit(solution)/shard_map/ppermute | solution.py:345
  69.7 8.1 %collective-permute-done.8.carried = f32[2,256,256]{2,1,0:T(8,128)S(1)} collective-permute-done((f32[2,256,256]{2,1,0:T(8,128)S(1)}, f32[2,256,256]{2,1,0:T(8,128)S(1)}, u32[]{:S(2)}, u32[]{:S(2)}) %collective-permute-start.8) | collective-permute-done | bytes 524320 | tf_op jit(solution)/shard_map/ppermute | solution.py:345
  77.9 1.7 %shard_map.118 = f32[2,256,256]{2,1,0:T(8,128)} custom-call(f32[2,256,256]{2,1,0:T(8,128)S(1)} %get-tuple-element.30.whole_map, f32[2,256,256]{2,1,0:T(8,128)S(1)} %get-tuple-element.32.whole_source, f32[2,256,256]{2,1,0:T(8,128)S(1)} %collective-permute-done.8.carried), custom_call_target="tpu_custom_call" | custom-call | tf_op jit(solution)/shard_map/pallas_call | solution.py:63
  79.5 2.9 %collective-permute-start.11 = (f32[2,256,256]{2,1,0:T(8,128)}, f32[2,256,256]{2,1,0:T(8,128)}, u32[]{:S(2)}, u32[]{:S(2)}) collective-permute-start(f32[2,256,256]{2,1,0:T(8,128)} %shard_map.118), channel_id=1, source_target_pairs={{0,9},{1,10},{2,11},{4,13},{5,14},{6,15},{8,1},{9,2},{10,3},{12,5}... | collective-permute-start | bytes 1572872 | tf_op jit(solution)/shard_map/ppermute | solution.py:352
  82.4 3.2 %collective-permute-start.10 = (f32[2,256,256]{2,1,0:T(8,128)}, f32[2,256,256]{2,1,0:T(8,128)}, u32[]{:S(2)}, u32[]{:S(2)}) collective-permute-start(f32[2,256,256]{2,1,0:T(8,128)} %shard_map.118), channel_id=1, source_target_pairs={{0,1},{1,2},{2,3},{4,5},{5,6},{6,7},{8,9},{9,10},{10,11},{12,13},{... | collective-permute-start | bytes 1572872 | tf_op jit(solution)/shard_map/ppermute | solution.py:351
  85.6 3.2 %collective-permute-start.9 = (f32[2,256,256]{2,1,0:T(8,128)}, f32[2,256,256]{2,1,0:T(8,128)}, u32[]{:S(2)}, u32[]{:S(2)}) collective-permute-start(f32[2,256,256]{2,1,0:T(8,128)} %shard_map.118), channel_id=1, source_target_pairs={{8,17},{9,18},{10,19},{12,21},{13,22},{14,23},{16,9},{17,10},{18,1... | collective-permute-start | bytes 1572872 | tf_op jit(solution)/shard_map/ppermute | solution.py:353
  89.3 2.7 %shard_map.120 = (f32[2,2,256,256]{3,2,1,0:T(8,128)S(1)}, f32[2,2,256,256]{3,2,1,0:T(8,128)S(1)}) custom-call(f32[2,2,256,256]{3,2,1,0:T(8,128)} %collective-permute-done.5.free, f32[4,2,256,256]{3,2,1,0:T(8,128)S(1)} %copy-done, f32[104,128]{1,0:T(8,128)S(1)} %add_select_fusion.sums), custom_call_target="tpu_custom_call" | custom-call | tf_op jit(solution)/shard_map/pallas_call | solution.py:63
  92.0 2.9 %shard_map.124 = (f32[2,2,256,256]{3,2,1,0:T(8,128)S(1)}, f32[2,2,256,256]{3,2,1,0:T(8,128)S(1)}) custom-call(f32[2,2,256,256]{3,2,1,0:T(8,128)} %collective-permute-done.13.free, f32[4,2,256,256]{3,2,1,0:T(8,128)S(1)} %copy-done, f32[104,128]{1,0:T(8,128)S(1)} %add_select_fusion.sums), custom_call_target="tpu_custom_call" | custom-call | tf_op jit(solution)/shard_map/pallas_call | solution.py:63
  94.9 2.9 %shard_map.114 = (f32[2,2,256,256]{3,2,1,0:T(8,128)S(1)}, f32[2,2,256,256]{3,2,1,0:T(8,128)S(1)}) custom-call(f32[2,2,256,256]{3,2,1,0:T(8,128)} %collective-permute-done.6.free, f32[4,2,256,256]{3,2,1,0:T(8,128)S(1)} %copy-done, f32[104,128]{1,0:T(8,128)S(1)} %add_select_fusion.sums), custom_call_target="tpu_custom_call" | custom-call | tf_op jit(solution)/shard_map/pallas_call | solution.py:63
  97.8 6.6 %collective-permute-done.10.carried = f32[2,256,256]{2,1,0:T(8,128)} collective-permute-done((f32[2,256,256]{2,1,0:T(8,128)}, f32[2,256,256]{2,1,0:T(8,128)}, u32[]{:S(2)}, u32[]{:S(2)}) %collective-permute-start.10) | collective-permute-done | bytes 524320 | tf_op jit(solution)/shard_map/ppermute | solution.py:351
  104.4 5.5 %shard_map.119 = (f32[4,2,256,256]{3,2,1,0:T(8,128)S(1)}, f32[2,256,256]{2,1,0:T(8,128)}) custom-call(f32[4,2,256,256]{3,2,1,0:T(8,128)S(1)} %copy-done.4, f32[4,2,256,256]{3,2,1,0:T(8,128)S(1)} %copy-done.7, f32[2,256,256]{2,1,0:T(8,128)} %collective-permute-done.10.carried), custom_call_target="tpu_custom_call" | custom-call | tf_op jit(solution)/shard_map/pallas_call | solution.py:63
  109.9 2.9 %shard_map.121 = (f32[2,2,256,256]{3,2,1,0:T(8,128)S(1)}, f32[2,256,256]{2,1,0:T(8,128)S(1)}) custom-call(f32[2,2,256,256]{3,2,1,0:T(8,128)S(1)} %get-tuple-element.35.link, f32[2,2,256,256]{3,2,1,0:T(8,128)S(1)} %get-tuple-element.36.source, f32[2,256,256]{2,1,0:T(8,128)} %collective-permute-done.11.carried), custom_call_target="tpu_custom_call" | custom-call | tf_op jit(solution)/shard_map/pallas_call | solution.py:63
  112.8 4.0 %collective-permute-done.9.carried = f32[2,256,256]{2,1,0:T(8,128)} collective-permute-done((f32[2,256,256]{2,1,0:T(8,128)}, f32[2,256,256]{2,1,0:T(8,128)}, u32[]{:S(2)}, u32[]{:S(2)}) %collective-permute-start.9) | collective-permute-done | bytes 524320 | tf_op jit(solution)/shard_map/ppermute | solution.py:353
  116.8 3.2 %shard_map.122 = (f32[2,2,256,256]{3,2,1,0:T(8,128)S(1)}, f32[2,2,256,256]{3,2,1,0:T(8,128)S(1)}, f32[2,256,256]{2,1,0:T(8,128)S(1)}) custom-call(s32[1]{0:T(128)} %bitcast.22.pick, f32[2,2,256,256]{3,2,1,0:T(8,128)S(1)} %get-tuple-element.28.link, f32[2,2,256,256]{3,2,1,0:T(8,128)S(1)} %get-tuple-element.29.source, ...), custom_call_target="tpu_custom_call" | custom-call | tf_op jit(solution)/shard_map/pallas_call | solution.py:63
  120.0 2.6 %collective-permute-start.12 = (f32[2,2,256,256]{3,2,1,0:T(8,128)S(1)}, f32[2,2,256,256]{3,2,1,0:T(8,128)S(1)}, u32[]{:S(2)}, u32[]{:S(2)}) collective-permute-start(f32[2,2,256,256]{3,2,1,0:T(8,128)S(1)} %get-tuple-element.39), channel_id=1, source_target_pairs={{0,4},{4,0},{8,12},{12,8},{16,20},{20,16},{24,28},{28,24},{1,5},{5... | collective-permute-start | bytes 3145736 | tf_op jit(solution)/shard_map/ppermute | solution.py:432
  122.7 2.7 %shard_map.125 = (f32[2,2,256,256]{3,2,1,0:T(8,128)S(1)}, f32[2,256,256]{2,1,0:T(8,128)}) custom-call(f32[2,2,256,256]{3,2,1,0:T(8,128)S(1)} %get-tuple-element.44.link, f32[2,2,256,256]{3,2,1,0:T(8,128)S(1)} %get-tuple-element.45.source, f32[2,256,256]{2,1,0:T(8,128)S(1)} %get-tuple-element.46.carried), custom_call_target="tpu_custom_call" | custom-call | tf_op jit(solution)/shard_map/pallas_call | solution.py:63
  126.0 2.7 %shard_map.123 = (f32[2,2,256,256]{3,2,1,0:T(8,128)S(1)}, f32[2,2,256,256]{3,2,1,0:T(8,128)S(1)}) custom-call(f32[2,2,256,256]{3,2,1,0:T(8,128)} %collective-permute-done.14.free, f32[4,2,256,256]{3,2,1,0:T(8,128)S(1)} %copy-done, f32[104,128]{1,0:T(8,128)S(1)} %add_select_fusion.sums), custom_call_target="tpu_custom_call" | custom-call | tf_op jit(solution)/shard_map/pallas_call | solution.py:63
  128.8 3.0 %shard_map.126 = (f32[2,2,256,256]{3,2,1,0:T(8,128)S(1)}, f32[2,2,256,256]{3,2,1,0:T(8,128)S(1)}, f32[2,256,256]{2,1,0:T(8,128)}) custom-call(s32[1]{0:T(128)} %bitcast.22.pick, f32[2,2,256,256]{3,2,1,0:T(8,128)S(1)} %get-tuple-element.41.link, f32[2,2,256,256]{3,2,1,0:T(8,128)S(1)} %get-tuple-element.42.source, ...), custom_call_target="tpu_custom_call" | custom-call | tf_op jit(solution)/shard_map/pallas_call | solution.py:63
  131.7 1.9 %collective-permute-start.15 = (f32[2,2,256,256]{3,2,1,0:T(8,128)S(1)}, f32[2,2,256,256]{3,2,1,0:T(8,128)S(1)}, u32[]{:S(2)}, u32[]{:S(2)}) collective-permute-start(f32[2,2,256,256]{3,2,1,0:T(8,128)S(1)} %get-tuple-element.49), channel_id=1, source_target_pairs={{0,4},{4,0},{8,12},{12,8},{16,20},{20,16},{24,28},{28,24},{1,5},{5... | collective-permute-start | bytes 3145736 | tf_op jit(solution)/shard_map/ppermute | solution.py:432
  (77 shorter events, 16.4 us)
Async XLA Ops:
  0.6 4.1 %copy-start.8 = (f32[16,4,128]{2,1,0:T(4,128)S(1)}, f32[16,4,128]{2,1,0:T(4,128)}, u32[]{:S(2)}) copy-start(f32[16,4,128]{2,1,0:T(4,128)} %param.10) | copy-start | bytes 98308
  0.7 12.1 %copy-start.9 = (f32[16,4,128]{2,1,0:T(4,128)S(1)}, f32[16,4,128]{2,1,0:T(4,128)}, u32[]{:S(2)}) copy-start(f32[16,4,128]{2,1,0:T(4,128)} %param.11) | copy-start | bytes 98308
  0.7 12.1 %copy-start.10 = (s32[4,256]{1,0:T(4,128)S(1)}, s32[4,256]{1,0:T(4,128)}, u32[]{:S(2)}) copy-start(s32[4,256]{1,0:T(4,128)} %owner.1) | copy-start | bytes 12292
  0.7 34.9 %copy-start = (f32[4,2,256,256]{3,2,1,0:T(8,128)S(1)}, f32[4,2,256,256]{3,2,1,0:T(8,128)}, u32[]{:S(2)}) copy-start(f32[4,2,256,256]{3,2,1,0:T(8,128)} %coupling.9) | copy-start | bytes 6291460
  3.6 30.7 %collective-permute-start.5 = (f32[2,2,256,256]{3,2,1,0:T(8,128)S(1)}, f32[2,2,256,256]{3,2,1,0:T(8,128)}, u32[]{:S(2)}, u32[]{:S(2)}) collective-permute-start(f32[2,2,256,256]{3,2,1,0:T(8,128)S(1)} %get-tuple-element.50), channel_id=1, source_target_pairs={{0,8},{4,12},{8,0},{12,4},{16,24},{20,28},{24,16},{28,20},{1,9},{5... | collective-permute-start | bytes 3145736 | tf_op jit(solution)/shard_map/ppermute | solution.py:303
  4.8 5.3 %collective-permute-start.1 = (f32[2,1,4,128]{3,2,0,1:T(4,128)S(1)}, f32[2,1,4,128]{3,2,0,1:T(4,128)S(1)}, u32[]{:S(2)}, u32[]{:S(2)}) collective-permute-start(f32[2,1,4,128]{3,2,0,1:T(4,128)S(1)} %get-tuple-element.54), channel_id=1, source_target_pairs={{0,1},{1,2},{2,3},{4,5},{5,6},{6,7},{8,9},{9,10},{10,11},{12,13},{... | collective-permute-start | bytes 12296 | tf_op jit(solution)/shard_map/ppermute | solution.py:309
  8.0 4.8 %collective-permute-start = (f32[2,1,4,128]{3,2,0,1:T(4,128)S(1)}, f32[2,1,4,128]{3,2,0,1:T(4,128)S(1)}, u32[]{:S(2)}, u32[]{:S(2)}) collective-permute-start(f32[2,1,4,128]{3,2,0,1:T(4,128)S(1)} %get-tuple-element.55), channel_id=1, source_target_pairs={{1,0},{2,1},{3,2},{5,4},{6,5},{7,6},{9,8},{10,9},{11,10},{13,12},{... | collective-permute-start | bytes 12296 | tf_op jit(solution)/shard_map/ppermute | solution.py:310
  13.9 2.9 %collective-permute-start.2 = (f32[104,128]{1,0:T(8,128)S(1)}, f32[104,128]{1,0:T(8,128)S(1)}, u32[]{:S(2)}, u32[]{:S(2)}) collective-permute-start(f32[104,128]{1,0:T(8,128)S(1)} %shard_map.113), channel_id=1, source_target_pairs={{0,4},{4,0},{8,12},{12,8},{16,20},{20,16},{24,28},{28,24},{1,5},{5... | collective-permute-start | bytes 159752 | tf_op jit(solution)/shard_map/ppermute | solution.py:261
  16.9 12.7 %collective-permute-start.3 = (f32[104,128]{1,0:T(8,128)S(1)}, f32[104,128]{1,0:T(8,128)S(1)}, u32[]{:S(2)}, u32[]{:S(2)}) collective-permute-start(f32[104,128]{1,0:T(8,128)S(1)} %add_select_fusion.2), channel_id=1, source_target_pairs={{0,12},{4,8},{8,4},{12,0},{16,28},{20,24},{24,20},{28,16},{1,13},{... | collective-permute-start | bytes 159752 | tf_op jit(solution)/shard_map/ppermute | solution.py:261
  29.7 4.5 %collective-permute-start.4 = (f32[104,128]{1,0:T(8,128)S(1)}, f32[104,128]{1,0:T(8,128)S(1)}, u32[]{:S(2)}, u32[]{:S(2)}) collective-permute-start(f32[104,128]{1,0:T(8,128)S(1)} %add_select_fusion.1), channel_id=1, source_target_pairs={{0,28},{4,24},{8,20},{12,16},{16,12},{20,8},{24,4},{28,0},{1,29},{... | collective-permute-start | bytes 159752 | tf_op jit(solution)/shard_map/ppermute | solution.py:261
  34.3 33.3 %collective-permute-start.13 = (f32[2,2,256,256]{3,2,1,0:T(8,128)}, f32[2,2,256,256]{3,2,1,0:T(8,128)}, u32[]{:S(2)}, u32[]{:S(2)}) collective-permute-start(f32[2,2,256,256]{3,2,1,0:T(8,128)} %get-tuple-element.40), channel_id=1, source_target_pairs={{0,8},{4,12},{8,0},{12,4},{16,24},{20,28},{24,16},{28,20},{1,9},{5... | collective-permute-start | bytes 3145736 | tf_op jit(solution)/shard_map/ppermute | solution.py:330
  45.2 23.7 %copy-start.18 = (f32[4]{0:T(128)S(1)}, f32[4]{0:T(128)}, u32[]{:S(2)}) copy-start(f32[4]{0:T(128)} %param.17) | copy-start | bytes 52
  45.2 23.7 %copy-start.19 = (s32[4]{0:T(128)S(1)}, s32[4]{0:T(128)}, u32[]{:S(2)}) copy-start(s32[4]{0:T(128)} %param.16) | copy-start | bytes 52
  45.2 23.7 %copy-start.20 = (s32[4]{0:T(128)S(1)}, s32[4]{0:T(128)}, u32[]{:S(2)}) copy-start(s32[4]{0:T(128)} %constant.51.clone) | copy-start | bytes 52
  45.2 15.8 %collective-permute-start.7 = (f32[2,256,256]{2,1,0:T(8,128)S(1)}, f32[2,256,256]{2,1,0:T(8,128)}, u32[]{:S(2)}, u32[]{:S(2)}) collective-permute-start(f32[2,256,256]{2,1,0:T(8,128)S(1)} %get-tuple-element.32.whole_source), channel_id=1, source_target_pairs={{0,1},{1,2},{2,3},{4,5},{5,6},{6,7},{8,9},{9,10},{10,11},{12,13},{... | collective-permute-start | bytes 1572872 | tf_op jit(solution)/shard_map/ppermute | solution.py:345
  61.0 27.8 %copy-start.11 = (f32[4,256,256]{2,1,0:T(8,128)S(1)}, f32[4,256,256]{2,1,0:T(8,128)}, u32[]{:S(2)}) copy-start(f32[4,256,256]{2,1,0:T(8,128)} %param.18) | copy-start | bytes 3145732
  63.1 14.8 %collective-permute-start.8 = (f32[2,256,256]{2,1,0:T(8,128)S(1)}, f32[2,256,256]{2,1,0:T(8,128)S(1)}, u32[]{:S(2)}, u32[]{:S(2)}) collective-permute-start(f32[2,256,256]{2,1,0:T(8,128)S(1)} %shard_map.117), channel_id=1, source_target_pairs={{0,1},{1,2},{2,3},{4,5},{5,6},{6,7},{8,9},{9,10},{10,11},{12,13},{... | collective-permute-start | bytes 1572872 | tf_op jit(solution)/shard_map/ppermute | solution.py:345
  66.4 28.6 %collective-permute-start.6 = (f32[2,2,256,256]{3,2,1,0:T(8,128)}, f32[2,2,256,256]{3,2,1,0:T(8,128)}, u32[]{:S(2)}, u32[]{:S(2)}) collective-permute-start(f32[2,2,256,256]{3,2,1,0:T(8,128)} %collective-permute-done.5.free), channel_id=1, source_target_pairs={{0,16},{4,20},{24,8},{28,12},{1,17},{5,21},{25,9},{29,13},{2,18},{... | collective-permute-start | bytes 3145736 | tf_op jit(solution)/shard_map/ppermute | solution.py:332
  67.7 58.3 %collective-permute-start.14 = (f32[2,2,256,256]{3,2,1,0:T(8,128)}, f32[2,2,256,256]{3,2,1,0:T(8,128)}, u32[]{:S(2)}, u32[]{:S(2)}) collective-permute-start(f32[2,2,256,256]{3,2,1,0:T(8,128)} %collective-permute-done.13.free), channel_id=1, source_target_pairs={{0,16},{4,20},{24,8},{28,12},{1,17},{5,21},{25,9},{29,13},{2,18},{... | collective-permute-start | bytes 3145736 | tf_op jit(solution)/shard_map/ppermute | solution.py:332
  79.5 30.4 %collective-permute-start.11 = (f32[2,256,256]{2,1,0:T(8,128)}, f32[2,256,256]{2,1,0:T(8,128)}, u32[]{:S(2)}, u32[]{:S(2)}) collective-permute-start(f32[2,256,256]{2,1,0:T(8,128)} %shard_map.118), channel_id=1, source_target_pairs={{0,9},{1,10},{2,11},{4,13},{5,14},{6,15},{8,1},{9,2},{10,3},{12,5}... | collective-permute-start | bytes 1572872 | tf_op jit(solution)/shard_map/ppermute | solution.py:352
  82.4 22.0 %collective-permute-start.10 = (f32[2,256,256]{2,1,0:T(8,128)}, f32[2,256,256]{2,1,0:T(8,128)}, u32[]{:S(2)}, u32[]{:S(2)}) collective-permute-start(f32[2,256,256]{2,1,0:T(8,128)} %shard_map.118), channel_id=1, source_target_pairs={{0,1},{1,2},{2,3},{4,5},{5,6},{6,7},{8,9},{9,10},{10,11},{12,13},{... | collective-permute-start | bytes 1572872 | tf_op jit(solution)/shard_map/ppermute | solution.py:351
  85.6 31.2 %collective-permute-start.9 = (f32[2,256,256]{2,1,0:T(8,128)}, f32[2,256,256]{2,1,0:T(8,128)}, u32[]{:S(2)}, u32[]{:S(2)}) collective-permute-start(f32[2,256,256]{2,1,0:T(8,128)} %shard_map.118), channel_id=1, source_target_pairs={{8,17},{9,18},{10,19},{12,21},{13,22},{14,23},{16,9},{17,10},{18,1... | collective-permute-start | bytes 1572872 | tf_op jit(solution)/shard_map/ppermute | solution.py:353
  92.0 12.4 %copy-start.7 = (f32[4,2,256,256]{3,2,1,0:T(8,128)S(1)}, f32[4,2,256,256]{3,2,1,0:T(8,128)}, u32[]{:S(2)}) copy-start(f32[4,2,256,256]{3,2,1,0:T(8,128)} %copy-done.6) | copy-start | bytes 6291460
  94.9 9.5 %copy-start.4 = (f32[4,2,256,256]{3,2,1,0:T(8,128)S(1)}, f32[4,2,256,256]{3,2,1,0:T(8,128)}, u32[]{:S(2)}) copy-start(f32[4,2,256,256]{3,2,1,0:T(8,128)} %copy-done.3) | copy-start | bytes 6291460
  120.0 14.5 %collective-permute-start.12 = (f32[2,2,256,256]{3,2,1,0:T(8,128)S(1)}, f32[2,2,256,256]{3,2,1,0:T(8,128)S(1)}, u32[]{:S(2)}, u32[]{:S(2)}) collective-permute-start(f32[2,2,256,256]{3,2,1,0:T(8,128)S(1)} %get-tuple-element.39), channel_id=1, source_target_pairs={{0,4},{4,0},{8,12},{12,8},{16,20},{20,16},{24,28},{28,24},{1,5},{5... | collective-permute-start | bytes 3145736 | tf_op jit(solution)/shard_map/ppermute | solution.py:432
  128.7 5.0 %copy-start.12 = (f32[16,4,127]{2,1,0:T(4,128)S(1)}, f32[16,4,127]{2,1,0:T(4,128)}, u32[]{:S(2)}) copy-start(f32[16,4,127]{2,1,0:T(4,128)} %get-tuple-element.76) | copy-start | bytes 97540
  128.7 5.0 %copy-start.13 = (f32[16,4,127]{2,1,0:T(4,128)S(1)}, f32[16,4,127]{2,1,0:T(4,128)}, u32[]{:S(2)}) copy-start(f32[16,4,127]{2,1,0:T(4,128)} %get-tuple-element.77) | copy-start | bytes 97540
  128.7 5.0 %copy-start.14 = (f32[15,4,128]{2,1,0:T(4,128)S(1)}, f32[15,4,128]{2,1,0:T(4,128)}, u32[]{:S(2)}) copy-start(f32[15,4,128]{2,1,0:T(4,128)} %get-tuple-element.60) | copy-start | bytes 92164
  128.7 5.0 %copy-start.15 = (f32[15,4,128]{2,1,0:T(4,128)S(1)}, f32[15,4,128]{2,1,0:T(4,128)}, u32[]{:S(2)}) copy-start(f32[15,4,128]{2,1,0:T(4,128)} %get-tuple-element.61) | copy-start | bytes 92164
  128.7 5.0 %copy-start.16 = (f32[15,4,128]{2,1,0:T(4,128)S(1)}, f32[15,4,128]{2,1,0:T(4,128)}, u32[]{:S(2)}) copy-start(f32[15,4,128]{2,1,0:T(4,128)} %get-tuple-element.78) | copy-start | bytes 92164
  128.7 5.0 %copy-start.17 = (f32[15,4,128]{2,1,0:T(4,128)S(1)}, f32[15,4,128]{2,1,0:T(4,128)}, u32[]{:S(2)}) copy-start(f32[15,4,128]{2,1,0:T(4,128)} %get-tuple-element.79) | copy-start | bytes 92164
  131.7 4.2 %collective-permute-start.15 = (f32[2,2,256,256]{3,2,1,0:T(8,128)S(1)}, f32[2,2,256,256]{3,2,1,0:T(8,128)S(1)}, u32[]{:S(2)}, u32[]{:S(2)}) collective-permute-start(f32[2,2,256,256]{3,2,1,0:T(8,128)S(1)} %get-tuple-element.49), channel_id=1, source_target_pairs={{0,4},{4,0},{8,12},{12,8},{16,20},{20,16},{24,28},{28,24},{1,5},{5... | collective-permute-start | bytes 3145736 | tf_op jit(solution)/shard_map/ppermute | solution.py:432
  (5 other events, 13.8 us)

commit v3 on v2

--- a/solution.py
+++ b/solution.py
@@ -1,4 +1,5 @@
 import functools
+import math
 import jax
 import jax.numpy as jnp
 from jax import lax
@@ -59,10 +60,14 @@
     ref[(*where, 1)] = value[1]
 
 
-def call(kernel, room, out_shapes, *operands, **more):
+def call(kernel, room, products, out_shapes, *operands, **more):
+    flops = products * 9 * 2 * max(x.shape[-1] for x in operands) ** 3
+    moved = sum(4 * math.prod(x.shape) for x in jax.tree.leaves((operands, out_shapes)))
+    cost = pl.CostEstimate(flops=flops, bytes_accessed=moved, transcendentals=0)
     return pl.pallas_call(
         kernel,
         out_shape=out_shapes,
+        cost_estimate=cost,
         compiler_params=pltpu.CompilerParams(vmem_limit_bytes=room * MIB),
         **more,
     )(*operands)
@@ -189,11 +194,16 @@
     put(out, added(sandwich(pair_of(whole_map), pair_of(carried)), pair_of(whole_source)))
 
 
-def beside_kernel(first, count, free, coupling, sums, link, source):
-    block = pair_of(free, 0)
-    put(link, product(block, pair_of(coupling, 0)), 0)
-    row = potential_of(sums, first + pl.program_id(0), count, free.shape[-1])
-    put(source, source_of(block, row), 0)
+def beside_kernel(start, count, parts, *refs):
+    frees, (coupling, sums, link, source) = refs[:parts], refs[parts:]
+    slab = 0
+    for free in frees:
+        for place in range(free.shape[0]):
+            block = pair_of(free, place)
+            put(link, product(block, pair_of(coupling, slab)), slab)
+            row = potential_of(sums, start + slab, count, free.shape[-1])
+            put(source, source_of(block, row), slab)
+            slab += 1
 
 
 def greens_kernel(link, source, carried, greens, state):
@@ -206,17 +216,17 @@
     put(greens, now, 0)
 
 
-def mixing_kernel(pick, link, source, carried, own, first, weights, here, there, state):
+def mixing_kernel(pick, link, source, carried, own, second, weights, here, there, state):
     @pl.when(pl.program_id(0) == 0)
     def _():
         state[...] = carried[...]
 
-    second = added(sandwich(pair_of(link, 0), pair_of(state)), pair_of(source, 0))
-    put(state, second)
+    first = added(sandwich(pair_of(link, 0), pair_of(state)), pair_of(source, 0))
+    put(state, first)
     for part in range(2):
-        first_now = first[0, part]
-        here[0, part] = weights[0] * first_now + weights[1] * second[part]
-        picked = jnp.where(pick[0] == 0, first_now, second[part])
+        second_now = second[0, part]
+        here[0, part] = weights[0] * first[part] + weights[1] * second_now
+        picked = jnp.where(pick[0] == 0, first[part], second_now)
         there[0, part] = weights[2] * own[0, part] + weights[3] * picked
 
 
@@ -299,7 +309,7 @@
     twin_pairs = [(e, e ^ 1) for e in everyone]
 
     half = count // 2
-    cuts = [free[:half], free[half:]]
+    cuts = [free[:1], free[1:half], free[half:]]
     free_first = [lax.ppermute(cuts[0], "energy", first_pairs)]
 
     wire_up = [(i, i + 1) for i in range(peers - 1)]
@@ -308,13 +318,17 @@
     lower, upper = end_planes(stacked, 1)
     wire_before = lax.ppermute(upper, "slab", wire_up)
     wire_after = lax.ppermute(lower, "slab", wire_down)
-    link, whole_map = call(linkage_kernel, 24, (blocks, whole), free, coupling)
-
+    link, whole_map = call(linkage_kernel, 24, 2 * count - 1, (blocks, whole), free, coupling)
+
+    wire_before, wire_after, link, whole_map = lax.optimization_barrier(
+        (wire_before, wire_after, link, whole_map)
+    )
     cells, rows, depth = charge.shape
     head = 5 * count * (width // depth)
     payload = call(
         functools.partial(gather_kernel, rows, energies),
         16,
+        1,
         shape(head + 4 * cells, depth),
         jnp.reshape(mine, (1,)),
         *(array.reshape(-1, depth) for array in (potential_old, permittivity, charge)),
@@ -326,13 +340,11 @@
     )
     sums, ends_before, ends_after = exchanged(payload, head)
 
-    cut, arrived, sums = lax.optimization_barrier((cuts[1], free_first[0], sums))
-    free_first = [arrived, lax.ppermute(cut, "energy", first_pairs)]
-    if relayed:
-        free_second = [lax.ppermute(part, "energy", relay_pairs) for part in free_first]
-    else:
-        free_second = [lax.ppermute(part, "energy", second_pairs) for part in (cuts[0], cut)]
-    source, whole_source = call(source_kernel, 24, (blocks, whole), free, link, sums)
+    first_arrived, middle, sums = lax.optimization_barrier((free_first[0], cuts[1], sums))
+    free_first = [first_arrived, lax.ppermute(middle, "energy", first_pairs)]
+    relay, relayed_cuts = (relay_pairs, free_first) if relayed else (second_pairs, cuts)
+    free_second = [lax.ppermute(part, "energy", relay) for part in relayed_cuts[:2]]
+    source, whole_source = call(source_kernel, 24, 3 * count - 2, (blocks, whole), free, link, sums)
 
     ends_before = ends_before.reshape(2, 2, cells, 1, depth)
     ends_after = ends_after.reshape(2, 2, cells, 1, depth)
@@ -340,17 +352,12 @@
     halos = ((wire_before, wire_after), (ends_before[:, 1], ends_after[:, 0]), (edge, edge))
     potential_new = relaxed(potential_old, permittivity, charge, halos)
 
-    leaving = whole_source
-    for _ in range(peers - 2):
-        carried = lax.ppermute(leaving, "slab", wire_up)
-        leaving = call(hop_kernel, 12, whole, whole_map, whole_source, carried)
-
-    def both(pairs):
-        return [(a * peers + i, b * peers + j) for a, b in pairs for i, j in wire_up]
-
-    carried = lax.ppermute(leaving, "slab", wire_up)
-    carried_first = lax.ppermute(leaving, ("energy", "slab"), both(first_pairs))
-    carried_second = lax.ppermute(leaving, ("energy", "slab"), both(second_pairs))
+    odd = mine % 2
+    distance = jnp.array([2, 2, 1, 1], jnp.int32)
+    lowered = jnp.stack([turned, 1 - turned, 1 - odd, odd]).astype(jnp.float32)
+    factors = (shifts[None, :] == distance[:, None]) * (occupation[None, :] + lowered[:, None])
+    weights = jnp.sum(factors[:, :, None, None] * mode_tiles[None], axis=1)
+    pick = jnp.reshape(turned ^ odd, (1,)).astype(jnp.int32)
 
     block = pl.BlockSpec((1, 2, width, width), lambda s: (s, 0, 0, 0))
     one_state = pl.BlockSpec((2, width, width), lambda s: (0, 0, 0))
@@ -359,30 +366,31 @@
         for i in range(2)
     ]
 
-    def beside(parts):
-        made = []
-        for index, part in enumerate(parts):
-            made.append(
-                call(
-                    functools.partial(beside_kernel, index * half, count),
-                    16,
-                    (shape(half, 2, width, width), shape(half, 2, width, width)),
-                    part,
-                    coupling,
-                    sums,
-                    grid=(half,),
-                    in_specs=[block, own_block[index], pl.BlockSpec(sums.shape, lambda s: (0, 0))],
-                    out_specs=(block, block),
-                )
-            )
-        return made
-
-    beside_first, beside_second = beside(free_first), beside(free_second)
+    def beside(index, parts):
+        made = shape(half, 2, width, width)
+        whole_spec = pl.BlockSpec((half, 2, width, width), lambda s: (0, 0, 0, 0))
+        return call(
+            functools.partial(beside_kernel, index * half, count, len(parts)),
+            24,
+            2 * half,
+            (made, made),
+            *parts,
+            coupling,
+            sums,
+            grid=(1,),
+            in_specs=[pl.BlockSpec(part.shape, lambda s: (0, 0, 0, 0)) for part in parts]
+            + [
+                pl.BlockSpec((half, 2, width, width), lambda s: (index, 0, 0, 0)),
+                pl.BlockSpec(sums.shape, lambda s: (0, 0)),
+            ],
+            out_specs=(whole_spec, whole_spec),
+        )
 
     def greens_of(link, source, carried):
         return call(
             greens_kernel,
             16,
+            2 * link.shape[0],
             (shape(*link.shape), whole),
             link,
             source,
@@ -392,30 +400,59 @@
             out_specs=(block, one_state),
         )
 
+    leaving = whole_source
+    beside_first, beside_second = [None, None], [None, None]
+    for hop in range(peers - 2):
+        carried = lax.ppermute(leaving, "slab", wire_up)
+        if hop == 0:
+            free_first[1], last = lax.optimization_barrier((free_first[1], cuts[2]))
+            free_first.append(lax.ppermute(last, "energy", first_pairs))
+            carried, potential_new, weights, free_first[1], free_second[0] = (
+                lax.optimization_barrier(
+                    (carried, potential_new, weights, free_first[1], free_second[0])
+                )
+            )
+        if hop == 1:
+            beside_first[0] = beside(0, free_first[:2])
+            carried, beside_first[0] = lax.optimization_barrier((carried, beside_first[0]))
+        leaving = call(hop_kernel, 12, 2, whole, whole_map, whole_source, carried)
+
+    def both(pairs):
+        return [(a * peers + i, b * peers + j) for a, b in pairs for i, j in wire_up]
+
+    carried = lax.ppermute(leaving, "slab", wire_up)
+    carried_second = lax.ppermute(leaving, ("energy", "slab"), both(second_pairs))
+    beside_second[0] = beside(0, free_second[:2])
+    leaving, last = lax.optimization_barrier((leaving, free_first[2] if relayed else last))
+    free_second.append(lax.ppermute(last, "energy", relay))
+    beside_first[1] = beside(1, free_first[2:])
+    carried, beside_first[1], beside_second[0] = lax.optimization_barrier(
+        (carried, beside_first[1], beside_second[0])
+    )
+    carried_first = lax.ppermute(carried, "energy", first_pairs)
     greens, _ = greens_of(link, source, carried)
-    greens_first = []
-    for part in beside_first:
-        made, carried_first = greens_of(*part, carried_first)
-        greens_first.append(made)
-
-    odd = mine % 2
-    distance = jnp.array([2, 2, 1, 1], jnp.int32)
-    lowered = jnp.stack([turned, 1 - turned, 1 - odd, odd]).astype(jnp.float32)
-    factors = (shifts[None, :] == distance[:, None]) * (occupation[None, :] + lowered[:, None])
-    weights = jnp.sum(factors[:, :, None, None] * mode_tiles[None], axis=1)
-    pick = jnp.reshape(turned ^ odd, (1,)).astype(jnp.int32)
+    beside_second[1] = beside(1, free_second[2:])
+    carried_second, greens = lax.optimization_barrier((carried_second, greens))
+    greens_second = []
+    for part in beside_second:
+        made, carried_second = greens_of(*part, carried_second)
+        greens_second.append(made)
+    carried_first, greens_second[0], beside_second[1] = lax.optimization_barrier(
+        (carried_first, greens_second[0], beside_second[1])
+    )
 
     outputs = []
-    for index, part in enumerate(beside_second):
-        here, there, carried_second = call(
+    for index, part in enumerate(beside_first):
+        here, there, carried_first = call(
             mixing_kernel,
             20,
+            2 * half,
             (shape(half, 2, width, width), shape(half, 2, width, width), whole),
             pick,
             *part,
-            carried_second,
+            carried_first,
             greens,
-            greens_first[index],
+            greens_second[index],
             weights,
             grid=(half,),
             in_specs=[
@@ -429,6 +466,8 @@
             ],
             out_specs=(block, block, one_state),
         )
+        if outputs:
+            outputs[0], there = lax.optimization_barrier((outputs[0], there))
         outputs.append(here + lax.ppermute(there, "energy", twin_pairs))
     return potential_new, jnp.concatenate(outputs, axis=0)[None]
 

time: 138 us -> 128 us (0.928)
  waiting for transfers between devices: 51.9 us -> 34.3 us
  local copies, waits for them, and re-layouts: 7.27 us -> 16.9 us
  Pallas kernels: 39.9 us -> 37.5 us
  other arithmetic: 3.34 us -> 4.99 us
  starting transfers between devices: 33.8 us -> 32.4 us
    ppermute x3, waiting for transfers between devices: 26.5 us -> 14.9 us  [per_device(): carried = lax.ppermute(leaving, 'slab', wire_up)]
    unnamed x42 -> x74, local copies, waits for them, and re-layouts: 3.01 us -> 12.1 us
    ppermute x3, waiting for transfers between devices: 16.9 us -> 8.01 us  [exchanged(): lax.ppermute(payload, 'energy', [(e, e ^ mask) for e in range(peers)])]
    ppermute x4 -> x6, waiting for transfers between devices: 0.65 us -> 8.17 us  [the longest x1 6.14 us: per_device(): free_second.append(lax.ppermute(last, 'energy', relay))]
    ppermute x1, waiting for transfers between devices: 3.96 us -> 0.62 us  [per_device(): lax.ppermute(leaving, ('energy', 'slab'), both(second_pairs))]
    ppermute x1, waiting for transfers between devices: 2.65 us -> 0.01 us  [per_device(): wire_after = lax.ppermute(lower, 'slab', wire_down)]
    pallas_call x14, Pallas kernels: 39.9 us -> 37.5 us  [call(): pl.pallas_call(kernel, out_shape=out_shapes, cost_estimate=cost, compiler...]
    slice x1 -> x2, local copies, waits for them, and re-layouts: 2.88 us -> 3.33 us  [per_device(): cuts = [free[:1], free[1:half], free[half:]]]
  transfers between devices with their start and end apart: 16 -> 18, of which waited for: 10 -> 10; matrix products, arithmetic and copies ran while one was open for 2% -> 6% of each run, Pallas kernels for 29% -> 27%
where the time goes in v3:
time: 128 us; the launch traced here: 127 us
  Pallas kernels  37.5 us (29%)
  waiting for transfers between devices  34.3 us (27%)
  starting transfers between devices  32.4 us (25%)
  local copies, waits for them, and re-layouts  16.9 us (13%)
  other arithmetic  4.99 us (4%)
    pallas_call x14, Pallas kernels, call(): pl.pallas_call(kernel, out_shape=out_shapes, cost_estimate=cost, compiler...  37.5 us
    ppermute x3, waiting for transfers between devices, per_device(): carried = lax.ppermute(leaving, 'slab', wire_up)  14.9 us
    unnamed x74, local copies, waits for them, and re-layouts  12.1 us
    ppermute x3, starting transfers between devices, per_device(): carried = lax.ppermute(leaving, 'slab', wire_up)  9.71 us
    ppermute x3, waiting for transfers between devices, exchanged(): lax.ppermute(payload, 'energy', [(e, e ^ mask) for e in range(peers)])  8.01 us
    ppermute x1, waiting for transfers between devices, per_device(): free_second.append(lax.ppermute(last, 'energy', relay))  6.14 us
    ppermute x1, starting transfers between devices, per_device(): wire_before = lax.ppermute(upper, 'slab', wire_up)  3.34 us
    ppermute x1, starting transfers between devices, per_device(): lax.ppermute(leaving, ('energy', 'slab'), both(second_pairs))  3.33 us
  transfers between devices with their start and end apart: 18, of which 10 were waited for; matrix products, arithmetic and copies ran while one was open for 6% of the time, Pallas kernels for 27%

profile of v3, /device:TPU:13, one launch (start us, length us, event | category | flops | bytes accessed | tf_op | source)
XLA Modules:
  0.0 127.3 jit_solution(409543704226143296)
XLA Ops:
  1.5 2.1 %collective-permute-start.1 = (f32[2,1,4,128]{3,2,0,1:T(4,128)S(1)}, f32[2,1,4,128]{3,2,0,1:T(4,128)S(1)}, u32[]{:S(2)}, u32[]{:S(2)}) collective-permute-start(f32[2,1,4,128]{3,2,0,1:T(4,128)S(1)} %get-tuple-element.106), channel_id=1, source_target_pairs={{1,0},{2,1},{3,2},{5,4},{6,5},{7,6},{9,8},{10,9},{11,10},{13,12},{... | collective-permute-start | bytes 12296 | tf_op jit(solution)/shard_map/ppermute | solution.py:320
  3.7 3.3 %collective-permute-start = (f32[2,1,4,128]{3,2,0,1:T(4,128)S(1)}, f32[2,1,4,128]{3,2,0,1:T(4,128)S(1)}, u32[]{:S(2)}, u32[]{:S(2)}) collective-permute-start(f32[2,1,4,128]{3,2,0,1:T(4,128)S(1)} %get-tuple-element.107), channel_id=1, source_target_pairs={{0,1},{1,2},{2,3},{4,5},{5,6},{6,7},{8,9},{9,10},{10,11},{12,13},{... | collective-permute-start | bytes 12296 | tf_op jit(solution)/shard_map/ppermute | solution.py:319
  7.0 2.3 %slice_bitcast_fusion.1 = (f32[1,2,256,256]{3,2,1,0:T(8,128)}, f32[1,2,256,256]{3,2,1,0:T(8,128)}) fusion(f32[1,4,2,256,256]{4,3,2,1,0:T(8,128)} %param.14), kind=kLoop, calls=%fused_computation.3 | loop fusion | bytes 2097152 | tf_op jit(solution)/shard_map/slice | solution.py:312
  13.1 1.6 %copy-done.8 = f32[4,2,256,256]{3,2,1,0:T(8,128)S(1)} copy-done((f32[4,2,256,256]{3,2,1,0:T(8,128)S(1)}, f32[4,2,256,256]{3,2,1,0:T(8,128)}, u32[]{:S(2)}) %copy-start.8) | copy-done | bytes 2097176
  14.7 2.6 %shard_map.113 = (f32[4,2,256,256]{3,2,1,0:T(8,128)S(1)}, f32[2,256,256]{2,1,0:T(8,128)S(1)}) custom-call(f32[4,2,256,256]{3,2,1,0:T(8,128)S(1)} %bitcast.40, f32[4,2,256,256]{3,2,1,0:T(8,128)S(1)} %copy-done.8), custom_call_target="tpu_custom_call" | custom-call | flops 2113929216 | bytes 6815744 | tf_op jit(solution)/shard_map/pallas_call | solution.py:67
  19.9 1.6 %collective-permute-start.3 = (f32[104,128]{1,0:T(8,128)S(1)}, f32[104,128]{1,0:T(8,128)S(1)}, u32[]{:S(2)}, u32[]{:S(2)}) collective-permute-start(f32[104,128]{1,0:T(8,128)S(1)} %shard_map.114), channel_id=1, source_target_pairs={{0,4},{4,0},{8,12},{12,8},{16,20},{20,16},{24,28},{28,24},{1,5},{5... | collective-permute-start | bytes 159752 | tf_op jit(solution)/shard_map/ppermute | solution.py:271
  23.4 2.9 %collective-permute-done.4 = f32[104,128]{1,0:T(8,128)S(1)} collective-permute-done((f32[104,128]{1,0:T(8,128)S(1)}, f32[104,128]{1,0:T(8,128)S(1)}, u32[]{:S(2)}, u32[]{:S(2)}) %collective-permute-start.4) | collective-permute-done | bytes 53280 | tf_op jit(solution)/shard_map/ppermute | solution.py:271
  26.9 4.2 %collective-permute-done.5 = f32[104,128]{1,0:T(8,128)S(1)} collective-permute-done((f32[104,128]{1,0:T(8,128)S(1)}, f32[104,128]{1,0:T(8,128)S(1)}, u32[]{:S(2)}, u32[]{:S(2)}) %collective-permute-start.5) | collective-permute-done | bytes 53280 | tf_op jit(solution)/shard_map/ppermute | solution.py:271
  33.7 1.6 %copy-done.19 = f32[4,2,256,256]{3,2,1,0:T(8,128)S(1)} copy-done((f32[4,2,256,256]{3,2,1,0:T(8,128)S(1)}, f32[4,2,256,256]{3,2,1,0:T(8,128)}, u32[]{:S(2)}) %copy-start.19) | copy-done | bytes 2097176
  35.3 3.8 %shard_map.115 = (f32[4,2,256,256]{3,2,1,0:T(8,128)S(1)}, f32[2,256,256]{2,1,0:T(8,128)S(1)}) custom-call(f32[4,2,256,256]{3,2,1,0:T(8,128)S(1)} %bitcast.41, f32[4,2,256,256]{3,2,1,0:T(8,128)S(1)} %copy-done.19, f32[104,128]{1,0:T(8,128)S(1)} %add_select_fusion.sums.refs_3_.refs_2_), custom_call_target="tpu_custom_call" | custom-call | flops 3019898880 | bytes 6868992 | tf_op jit(solution)/shard_map/pallas_call | solution.py:67
  40.5 3.3 %collective-permute-start.6 = (f32[2,256,256]{2,1,0:T(8,128)S(1)}, f32[2,256,256]{2,1,0:T(8,128)S(1)}, u32[]{:S(2)}, u32[]{:S(2)}) collective-permute-start(f32[2,256,256]{2,1,0:T(8,128)S(1)} %get-tuple-element.58.whole_source), channel_id=1, source_target_pairs={{0,1},{1,2},{2,3},{4,5},{5,6},{6,7},{8,9},{9,10},{10,11},{12,13},{... | collective-permute-start | bytes 1572872 | tf_op jit(solution)/shard_map/ppermute | solution.py:406
  43.8 1.5 %collective-permute-done.7.refs_1_ = f32[1,2,256,256]{3,2,1,0:T(8,128)S(1)} collective-permute-done((f32[1,2,256,256]{3,2,1,0:T(8,128)}, f32[1,2,256,256]{3,2,1,0:T(8,128)S(1)}, u32[]{:S(2)}, u32[]{:S(2)}) %collective-permute-start.7) | collective-permute-done | bytes 524320 | tf_op jit(solution)/shard_map/ppermute | solution.py:344
  47.3 8.1 %collective-permute-done.6.carried = f32[2,256,256]{2,1,0:T(8,128)S(1)} collective-permute-done((f32[2,256,256]{2,1,0:T(8,128)S(1)}, f32[2,256,256]{2,1,0:T(8,128)S(1)}, u32[]{:S(2)}, u32[]{:S(2)}) %collective-permute-start.6) | collective-permute-done | bytes 524320 | tf_op jit(solution)/shard_map/ppermute | solution.py:406
  56.4 3.2 %collective-permute-start.9 = (f32[2,256,256]{2,1,0:T(8,128)S(1)}, f32[2,256,256]{2,1,0:T(8,128)S(1)}, u32[]{:S(2)}, u32[]{:S(2)}) collective-permute-start(f32[2,256,256]{2,1,0:T(8,128)S(1)} %shard_map.116), channel_id=1, source_target_pairs={{0,1},{1,2},{2,3},{4,5},{5,6},{6,7},{8,9},{9,10},{10,11},{12,13},{... | collective-permute-start | bytes 1572872 | tf_op jit(solution)/shard_map/ppermute | solution.py:406
  61.1 2.6 %shard_map.117 = (f32[2,2,256,256]{3,2,1,0:T(8,128)S(1)}, f32[2,2,256,256]{3,2,1,0:T(8,128)S(1)}) custom-call(f32[1,2,256,256]{3,2,1,0:T(8,128)} %collective-permute-done.2.refs_0_, f32[1,2,256,256]{3,2,1,0:T(8,128)S(1)} %collective-permute-done.7.refs_1_, f32[4,2,256,256]{3,2,1,0:T(8,128)S(1)} %copy-done.9, f32[104,128]{1,0:T(8,128)S(1)} %add_select_fusion.sums.refs_3_.refs_2_), custom_call_target="tpu_custom_call" | custom-call | flops 1207959552 | bytes 5296128 | tf_op jit(solution)/shard_map/pallas_call | solution.py:67
  63.6 6.8 %collective-permute-done.9.carried = f32[2,256,256]{2,1,0:T(8,128)S(1)} collective-permute-done((f32[2,256,256]{2,1,0:T(8,128)S(1)}, f32[2,256,256]{2,1,0:T(8,128)S(1)}, u32[]{:S(2)}, u32[]{:S(2)}) %collective-permute-start.9) | collective-permute-done | bytes 524320 | tf_op jit(solution)/shard_map/ppermute | solution.py:406
  70.4 1.7 %shard_map.118 = f32[2,256,256]{2,1,0:T(8,128)} custom-call(f32[2,256,256]{2,1,0:T(8,128)S(1)} %copy-done.13, f32[2,256,256]{2,1,0:T(8,128)S(1)} %get-tuple-element.58.whole_source, f32[2,256,256]{2,1,0:T(8,128)S(1)} %collective-permute-done.9.carried), custom_call_target="tpu_custom_call" | custom-call | flops 603979776 | bytes 2097152 | tf_op jit(solution)/shard_map/pallas_call | solution.py:67
  73.4 3.2 %collective-permute-start.10 = (f32[2,256,256]{2,1,0:T(8,128)}, f32[2,256,256]{2,1,0:T(8,128)}, u32[]{:S(2)}, u32[]{:S(2)}) collective-permute-start(f32[2,256,256]{2,1,0:T(8,128)} %shard_map.118), channel_id=1, source_target_pairs={{0,1},{1,2},{2,3},{4,5},{5,6},{6,7},{8,9},{9,10},{10,11},{12,13},{... | collective-permute-start | bytes 1572872 | tf_op jit(solution)/shard_map/ppermute | solution.py:423
  76.6 3.3 %collective-permute-start.14 = (f32[2,256,256]{2,1,0:T(8,128)}, f32[2,256,256]{2,1,0:T(8,128)}, u32[]{:S(2)}, u32[]{:S(2)}) collective-permute-start(f32[2,256,256]{2,1,0:T(8,128)} %shard_map.118), channel_id=1, source_target_pairs={{8,17},{9,18},{10,19},{12,21},{13,22},{14,23},{16,9},{17,10},{18,1... | collective-permute-start | bytes 1572872 | tf_op jit(solution)/shard_map/ppermute | solution.py:424
  82.5 3.1 %shard_map.119 = (f32[2,2,256,256]{3,2,1,0:T(8,128)S(1)}, f32[2,2,256,256]{3,2,1,0:T(8,128)S(1)}) custom-call(f32[2,2,256,256]{3,2,1,0:T(8,128)} %collective-permute-done.11.refs_0_, f32[4,2,256,256]{3,2,1,0:T(8,128)S(1)} %copy-done.9, f32[104,128]{1,0:T(8,128)S(1)} %add_select_fusion.sums.refs_3_.refs_2_), custom_call_target="tpu_custom_call" | custom-call | flops 1207959552 | bytes 5296128 | tf_op jit(solution)/shard_map/pallas_call | solution.py:67
  87.7 1.7 %collective-permute-start.13 = (f32[2,256,256]{2,1,0:T(8,128)}, f32[2,256,256]{2,1,0:T(8,128)}, u32[]{:S(2)}, u32[]{:S(2)}) collective-permute-start(f32[2,256,256]{2,1,0:T(8,128)} %collective-permute-done.10.carried), channel_id=1, source_target_pairs={{0,8},{4,12},{8,0},{12,4},{16,24},{20,28},{24,16},{28,20},{1,9},{5... | collective-permute-start | bytes 1572872 | tf_op jit(solution)/shard_map/ppermute | solution.py:432
  89.4 1.6 %copy-done.20 = f32[4,2,256,256]{3,2,1,0:T(8,128)S(1)} copy-done((f32[4,2,256,256]{3,2,1,0:T(8,128)S(1)}, f32[4,2,256,256]{3,2,1,0:T(8,128)}, u32[]{:S(2)}) %copy-start.20) | copy-done | bytes 2097176
  90.9 1.6 %copy-done.22 = f32[4,2,256,256]{3,2,1,0:T(8,128)S(1)} copy-done((f32[4,2,256,256]{3,2,1,0:T(8,128)S(1)}, f32[4,2,256,256]{3,2,1,0:T(8,128)}, u32[]{:S(2)}) %copy-start.22) | copy-done | bytes 2097176
  92.5 5.6 %shard_map.121 = (f32[4,2,256,256]{3,2,1,0:T(8,128)S(1)}, f32[2,256,256]{2,1,0:T(8,128)}) custom-call(f32[4,2,256,256]{3,2,1,0:T(8,128)S(1)} %copy-done.20, f32[4,2,256,256]{3,2,1,0:T(8,128)S(1)} %copy-done.22, f32[2,256,256]{2,1,0:T(8,128)} %collective-permute-done.10.carried), custom_call_target="tpu_custom_call" | custom-call | flops 2415919104 | bytes 7340032 | tf_op jit(solution)/shard_map/pallas_call | solution.py:67
  98.8 3.1 %shard_map.122 = (f32[2,2,256,256]{3,2,1,0:T(8,128)S(1)}, f32[2,256,256]{2,1,0:T(8,128)S(1)}) custom-call(f32[2,2,256,256]{3,2,1,0:T(8,128)S(1)} %copy-done.15, f32[2,2,256,256]{3,2,1,0:T(8,128)S(1)} %copy-done.17, f32[2,256,256]{2,1,0:T(8,128)} %collective-permute-done.14.carried), custom_call_target="tpu_custom_call" | custom-call | flops 1207959552 | bytes 4194304 | tf_op jit(solution)/shard_map/pallas_call | solution.py:67
  101.9 6.1 %collective-permute-done.15.refs_0_ = f32[2,2,256,256]{3,2,1,0:T(8,128)} collective-permute-done((f32[2,2,256,256]{3,2,1,0:T(8,128)}, f32[2,2,256,256]{3,2,1,0:T(8,128)}, u32[]{:S(2)}, u32[]{:S(2)}) %collective-permute-start.15) | collective-permute-done | bytes 1048608 | tf_op jit(solution)/shard_map/ppermute | solution.py:427
  108.0 2.7 %shard_map.123 = (f32[2,2,256,256]{3,2,1,0:T(8,128)S(1)}, f32[2,2,256,256]{3,2,1,0:T(8,128)S(1)}) custom-call(f32[2,2,256,256]{3,2,1,0:T(8,128)} %collective-permute-done.15.refs_0_, f32[4,2,256,256]{3,2,1,0:T(8,128)S(1)} %copy-done.10, f32[104,128]{1,0:T(8,128)S(1)} %add_select_fusion.sums.refs_3_.refs_2_), custom_call_target="tpu_custom_call" | custom-call | flops 1207959552 | bytes 5296128 | tf_op jit(solution)/shard_map/pallas_call | solution.py:67
  110.7 3.2 %shard_map.124 = (f32[2,2,256,256]{3,2,1,0:T(8,128)S(1)}, f32[2,2,256,256]{3,2,1,0:T(8,128)S(1)}, f32[2,256,256]{2,1,0:T(8,128)S(1)}) custom-call(s32[1]{0:T(128)} %bitcast.30.pick, f32[2,2,256,256]{3,2,1,0:T(8,128)S(1)} %get-tuple-element.68.link, f32[2,2,256,256]{3,2,1,0:T(8,128)S(1)} %get-tuple-element.69.source, ...), custom_call_target="tpu_custom_call" | custom-call | flops 1207959552 | bytes 9437188 | tf_op jit(solution)/shard_map/pallas_call | solution.py:67
  113.9 3.2 %collective-permute-start.16 = (f32[2,2,256,256]{3,2,1,0:T(8,128)S(1)}, f32[2,2,256,256]{3,2,1,0:T(8,128)S(1)}, u32[]{:S(2)}, u32[]{:S(2)}) collective-permute-start(f32[2,2,256,256]{3,2,1,0:T(8,128)S(1)} %get-tuple-element.92), channel_id=1, source_target_pairs={{0,4},{4,0},{8,12},{12,8},{16,20},{20,16},{24,28},{28,24},{1,5},{5... | collective-permute-start | bytes 3145736 | tf_op jit(solution)/shard_map/ppermute | solution.py:471
  117.1 2.7 %shard_map.125 = (f32[2,2,256,256]{3,2,1,0:T(8,128)S(1)}, f32[2,256,256]{2,1,0:T(8,128)}) custom-call(f32[2,2,256,256]{3,2,1,0:T(8,128)S(1)} %get-tuple-element.85.link, f32[2,2,256,256]{3,2,1,0:T(8,128)S(1)} %get-tuple-element.86.source, f32[2,256,256]{2,1,0:T(8,128)S(1)} %get-tuple-element.96.carried), custom_call_target="tpu_custom_call" | custom-call | flops 1207959552 | bytes 4194304 | tf_op jit(solution)/shard_map/pallas_call | solution.py:67
  119.8 2.9 %shard_map.126 = (f32[2,2,256,256]{3,2,1,0:T(8,128)S(1)}, f32[2,2,256,256]{3,2,1,0:T(8,128)S(1)}, f32[2,256,256]{2,1,0:T(8,128)}) custom-call(s32[1]{0:T(128)} %bitcast.30.pick, f32[2,2,256,256]{3,2,1,0:T(8,128)S(1)} %copy-done.4, f32[2,2,256,256]{3,2,1,0:T(8,128)S(1)} %copy-done.6, f32[2,256,256]{2,1,0:T(8,128)S(1)} %get-tuple-element.95.carried, ...), custom_call_target="tpu_custom_call" | custom-call | flops 1207959552 | bytes 9437188 | tf_op jit(solution)/shard_map/pallas_call | solution.py:67
  122.9 2.6 %collective-permute-done.17 = f32[2,2,256,256]{3,2,1,0:T(8,128)S(1)} collective-permute-done((f32[2,2,256,256]{3,2,1,0:T(8,128)S(1)}, f32[2,2,256,256]{3,2,1,0:T(8,128)S(1)}, u32[]{:S(2)}, u32[]{:S(2)}) %collective-permute-start.17) | collective-permute-done | bytes 1048608 | tf_op jit(solution)/shard_map/ppermute | solution.py:471
  (113 shorter events, 26.3 us)
Async XLA Ops:
  0.6 9.9 %copy-start.2 = (f32[16,4,128]{2,1,0:T(4,128)S(1)}, f32[16,4,128]{2,1,0:T(4,128)}, u32[]{:S(2)}) copy-start(f32[16,4,128]{2,1,0:T(4,128)} %param.10) | copy-start | bytes 98308
  0.6 9.9 %copy-start.1 = (f32[16,4,128]{2,1,0:T(4,128)S(1)}, f32[16,4,128]{2,1,0:T(4,128)}, u32[]{:S(2)}) copy-start(f32[16,4,128]{2,1,0:T(4,128)} %param.12) | copy-start | bytes 98308
  0.6 11.3 %copy-start = (f32[1,4,2,256,256]{4,3,2,1,0:T(8,128)S(1)}, f32[1,4,2,256,256]{4,3,2,1,0:T(8,128)}, u32[]{:S(2)}) copy-start(f32[1,4,2,256,256]{4,3,2,1,0:T(8,128)} %param.14) | copy-start | bytes 6291460
  1.5 17.1 %collective-permute-start.1 = (f32[2,1,4,128]{3,2,0,1:T(4,128)S(1)}, f32[2,1,4,128]{3,2,0,1:T(4,128)S(1)}, u32[]{:S(2)}, u32[]{:S(2)}) collective-permute-start(f32[2,1,4,128]{3,2,0,1:T(4,128)S(1)} %get-tuple-element.106), channel_id=1, source_target_pairs={{1,0},{2,1},{3,2},{5,4},{6,5},{7,6},{9,8},{10,9},{11,10},{13,12},{... | collective-permute-start | bytes 12296 | tf_op jit(solution)/shard_map/ppermute | solution.py:320
  3.7 15.0 %collective-permute-start = (f32[2,1,4,128]{3,2,0,1:T(4,128)S(1)}, f32[2,1,4,128]{3,2,0,1:T(4,128)S(1)}, u32[]{:S(2)}, u32[]{:S(2)}) collective-permute-start(f32[2,1,4,128]{3,2,0,1:T(4,128)S(1)} %get-tuple-element.107), channel_id=1, source_target_pairs={{0,1},{1,2},{2,3},{4,5},{5,6},{6,7},{8,9},{9,10},{10,11},{12,13},{... | collective-permute-start | bytes 12296 | tf_op jit(solution)/shard_map/ppermute | solution.py:319
  9.3 22.6 %collective-permute-start.2 = (f32[1,2,256,256]{3,2,1,0:T(8,128)}, f32[1,2,256,256]{3,2,1,0:T(8,128)}, u32[]{:S(2)}, u32[]{:S(2)}) collective-permute-start(f32[1,2,256,256]{3,2,1,0:T(8,128)} %get-tuple-element.103), channel_id=1, source_target_pairs={{0,8},{4,12},{8,0},{12,4},{16,24},{20,28},{24,16},{28,20},{1,9},{5... | collective-permute-start | bytes 1572872 | tf_op jit(solution)/shard_map/ppermute | solution.py:313
  19.9 2.5 %collective-permute-start.3 = (f32[104,128]{1,0:T(8,128)S(1)}, f32[104,128]{1,0:T(8,128)S(1)}, u32[]{:S(2)}, u32[]{:S(2)}) collective-permute-start(f32[104,128]{1,0:T(8,128)S(1)} %shard_map.114), channel_id=1, source_target_pairs={{0,4},{4,0},{8,12},{12,8},{16,20},{20,16},{24,28},{28,24},{1,5},{5... | collective-permute-start | bytes 159752 | tf_op jit(solution)/shard_map/ppermute | solution.py:271
  22.4 3.9 %collective-permute-start.4 = (f32[104,128]{1,0:T(8,128)S(1)}, f32[104,128]{1,0:T(8,128)S(1)}, u32[]{:S(2)}, u32[]{:S(2)}) collective-permute-start(f32[104,128]{1,0:T(8,128)S(1)} %add_select_fusion.2), channel_id=1, source_target_pairs={{0,12},{4,8},{8,4},{12,0},{16,28},{20,24},{24,20},{28,16},{1,13},{... | collective-permute-start | bytes 159752 | tf_op jit(solution)/shard_map/ppermute | solution.py:271
  26.4 4.8 %collective-permute-start.5 = (f32[104,128]{1,0:T(8,128)S(1)}, f32[104,128]{1,0:T(8,128)S(1)}, u32[]{:S(2)}, u32[]{:S(2)}) collective-permute-start(f32[104,128]{1,0:T(8,128)S(1)} %add_select_fusion.1), channel_id=1, source_target_pairs={{0,28},{4,24},{8,20},{12,16},{16,12},{20,8},{24,4},{28,0},{1,29},{... | collective-permute-start | bytes 159752 | tf_op jit(solution)/shard_map/ppermute | solution.py:271
  31.9 13.4 %collective-permute-start.7 = (f32[1,2,256,256]{3,2,1,0:T(8,128)}, f32[1,2,256,256]{3,2,1,0:T(8,128)S(1)}, u32[]{:S(2)}, u32[]{:S(2)}) collective-permute-start(f32[1,2,256,256]{3,2,1,0:T(8,128)} %get-tuple-element.59), channel_id=1, source_target_pairs={{0,8},{4,12},{8,0},{12,4},{16,24},{20,28},{24,16},{28,20},{1,9},{5... | collective-permute-start | bytes 1572872 | tf_op jit(solution)/shard_map/ppermute | solution.py:344
  32.2 23.2 %copy-start.13 = (f32[2,256,256]{2,1,0:T(8,128)S(1)}, f32[2,256,256]{2,1,0:T(8,128)}, u32[]{:S(2)}) copy-start(f32[2,256,256]{2,1,0:T(8,128)} %copy-done.12) | copy-start | bytes 1572868
  32.2 15.1 %collective-permute-start.8 = (f32[1,2,256,256]{3,2,1,0:T(8,128)}, f32[1,2,256,256]{3,2,1,0:T(8,128)S(1)}, u32[]{:S(2)}, u32[]{:S(2)}) collective-permute-start(f32[1,2,256,256]{3,2,1,0:T(8,128)} %collective-permute-done.2.refs_0_), channel_id=1, source_target_pairs={{0,16},{4,20},{24,8},{28,12},{1,17},{5,21},{25,9},{29,13},{2,18},{... | collective-permute-start | bytes 1572872 | tf_op jit(solution)/shard_map/ppermute | solution.py:346
  35.3 10.1 %copy-start.24 = (f32[2,2,256,256]{3,2,1,0:T(8,128)S(1)}, f32[2,2,256,256]{3,2,1,0:T(8,128)}, u32[]{:S(2)}) copy-start(f32[2,2,256,256]{3,2,1,0:T(8,128)} %slice_bitcast_fusion) | copy-start | bytes 3145732
  35.3 10.7 %copy-start.25 = (f32[16,4,127]{2,1,0:T(4,128)S(1)}, f32[16,4,127]{2,1,0:T(4,128)}, u32[]{:S(2)}) copy-start(f32[16,4,127]{2,1,0:T(4,128)} %get-tuple-element.108) | copy-start | bytes 97540
  35.3 10.7 %copy-start.26 = (f32[16,4,127]{2,1,0:T(4,128)S(1)}, f32[16,4,127]{2,1,0:T(4,128)}, u32[]{:S(2)}) copy-start(f32[16,4,127]{2,1,0:T(4,128)} %get-tuple-element.109) | copy-start | bytes 97540
  35.3 10.7 %copy-start.27 = (f32[16,4,127]{2,1,0:T(4,128)S(1)}, f32[16,4,127]{2,1,0:T(4,128)}, u32[]{:S(2)}) copy-start(f32[16,4,127]{2,1,0:T(4,128)} %get-tuple-element.130) | copy-start | bytes 97540
  35.3 10.7 %copy-start.28 = (f32[16,4,127]{2,1,0:T(4,128)S(1)}, f32[16,4,127]{2,1,0:T(4,128)}, u32[]{:S(2)}) copy-start(f32[16,4,127]{2,1,0:T(4,128)} %get-tuple-element.131) | copy-start | bytes 97540
  35.3 10.7 %copy-start.29 = (f32[15,4,128]{2,1,0:T(4,128)S(1)}, f32[15,4,128]{2,1,0:T(4,128)}, u32[]{:S(2)}) copy-start(f32[15,4,128]{2,1,0:T(4,128)} %get-tuple-element.112) | copy-start | bytes 92164
  35.3 10.7 %copy-start.30 = (f32[15,4,128]{2,1,0:T(4,128)S(1)}, f32[15,4,128]{2,1,0:T(4,128)}, u32[]{:S(2)}) copy-start(f32[15,4,128]{2,1,0:T(4,128)} %get-tuple-element.113) | copy-start | bytes 92164
  35.3 10.7 %copy-start.31 = (f32[15,4,128]{2,1,0:T(4,128)S(1)}, f32[15,4,128]{2,1,0:T(4,128)}, u32[]{:S(2)}) copy-start(f32[15,4,128]{2,1,0:T(4,128)} %get-tuple-element.132) | copy-start | bytes 92164
  35.3 10.7 %copy-start.32 = (f32[15,4,128]{2,1,0:T(4,128)S(1)}, f32[15,4,128]{2,1,0:T(4,128)}, u32[]{:S(2)}) copy-start(f32[15,4,128]{2,1,0:T(4,128)} %get-tuple-element.133) | copy-start | bytes 92164
  40.5 20.6 %copy-start.9 = (f32[4,2,256,256]{3,2,1,0:T(8,128)S(1)}, f32[4,2,256,256]{3,2,1,0:T(8,128)}, u32[]{:S(2)}) copy-start(f32[4,2,256,256]{3,2,1,0:T(8,128)} %refs_1_.3) | copy-start | bytes 6291460
  40.5 15.0 %collective-permute-start.6 = (f32[2,256,256]{2,1,0:T(8,128)S(1)}, f32[2,256,256]{2,1,0:T(8,128)S(1)}, u32[]{:S(2)}, u32[]{:S(2)}) collective-permute-start(f32[2,256,256]{2,1,0:T(8,128)S(1)} %get-tuple-element.58.whole_source), channel_id=1, source_target_pairs={{0,1},{1,2},{2,3},{4,5},{5,6},{6,7},{8,9},{9,10},{10,11},{12,13},{... | collective-permute-start | bytes 1572872 | tf_op jit(solution)/shard_map/ppermute | solution.py:406
  45.3 26.8 %collective-permute-start.11 = (f32[2,2,256,256]{3,2,1,0:T(8,128)S(1)}, f32[2,2,256,256]{3,2,1,0:T(8,128)}, u32[]{:S(2)}, u32[]{:S(2)}) collective-permute-start(f32[2,2,256,256]{3,2,1,0:T(8,128)S(1)} %copy-done.24), channel_id=1, source_target_pairs={{0,8},{4,12},{8,0},{12,4},{16,24},{20,28},{24,16},{28,20},{1,9},{5... | collective-permute-start | bytes 3145736 | tf_op jit(solution)/shard_map/ppermute | solution.py:409
  56.4 14.0 %collective-permute-start.9 = (f32[2,256,256]{2,1,0:T(8,128)S(1)}, f32[2,256,256]{2,1,0:T(8,128)S(1)}, u32[]{:S(2)}, u32[]{:S(2)}) collective-permute-start(f32[2,256,256]{2,1,0:T(8,128)S(1)} %shard_map.116), channel_id=1, source_target_pairs={{0,1},{1,2},{2,3},{4,5},{5,6},{6,7},{8,9},{9,10},{10,11},{12,13},{... | collective-permute-start | bytes 1572872 | tf_op jit(solution)/shard_map/ppermute | solution.py:406
  59.6 20.4 %collective-permute-start.12 = (f32[1,2,256,256]{3,2,1,0:T(8,128)S(1)}, f32[1,2,256,256]{3,2,1,0:T(8,128)S(1)}, u32[]{:S(2)}, u32[]{:S(2)}) collective-permute-start(f32[1,2,256,256]{3,2,1,0:T(8,128)S(1)} %collective-permute-done.7.refs_1_), channel_id=1, source_target_pairs={{0,16},{4,20},{24,8},{28,12},{1,17},{5,21},{25,9},{29,13},{2,18},{... | collective-permute-start | bytes 1572872 | tf_op jit(solution)/shard_map/ppermute | solution.py:346
  72.1 35.9 %collective-permute-start.15 = (f32[2,2,256,256]{3,2,1,0:T(8,128)}, f32[2,2,256,256]{3,2,1,0:T(8,128)}, u32[]{:S(2)}, u32[]{:S(2)}) collective-permute-start(f32[2,2,256,256]{3,2,1,0:T(8,128)} %collective-permute-done.11.refs_0_), channel_id=1, source_target_pairs={{0,16},{4,20},{24,8},{28,12},{1,17},{5,21},{25,9},{29,13},{2,18},{... | collective-permute-start | bytes 3145736 | tf_op jit(solution)/shard_map/ppermute | solution.py:427
  73.4 14.2 %collective-permute-start.10 = (f32[2,256,256]{2,1,0:T(8,128)}, f32[2,256,256]{2,1,0:T(8,128)}, u32[]{:S(2)}, u32[]{:S(2)}) collective-permute-start(f32[2,256,256]{2,1,0:T(8,128)} %shard_map.118), channel_id=1, source_target_pairs={{0,1},{1,2},{2,3},{4,5},{5,6},{6,7},{8,9},{9,10},{10,11},{12,13},{... | collective-permute-start | bytes 1572872 | tf_op jit(solution)/shard_map/ppermute | solution.py:423
  76.6 22.2 %collective-permute-start.14 = (f32[2,256,256]{2,1,0:T(8,128)}, f32[2,256,256]{2,1,0:T(8,128)}, u32[]{:S(2)}, u32[]{:S(2)}) collective-permute-start(f32[2,256,256]{2,1,0:T(8,128)} %shard_map.118), channel_id=1, source_target_pairs={{8,17},{9,18},{10,19},{12,21},{13,22},{14,23},{16,9},{17,10},{18,1... | collective-permute-start | bytes 1572872 | tf_op jit(solution)/shard_map/ppermute | solution.py:424
  87.7 23.0 %collective-permute-start.13 = (f32[2,256,256]{2,1,0:T(8,128)}, f32[2,256,256]{2,1,0:T(8,128)}, u32[]{:S(2)}, u32[]{:S(2)}) collective-permute-start(f32[2,256,256]{2,1,0:T(8,128)} %collective-permute-done.10.carried), channel_id=1, source_target_pairs={{0,8},{4,12},{8,0},{12,4},{16,24},{20,28},{24,16},{28,20},{1,9},{5... | collective-permute-start | bytes 1572872 | tf_op jit(solution)/shard_map/ppermute | solution.py:432
  113.9 8.8 %collective-permute-start.16 = (f32[2,2,256,256]{3,2,1,0:T(8,128)S(1)}, f32[2,2,256,256]{3,2,1,0:T(8,128)S(1)}, u32[]{:S(2)}, u32[]{:S(2)}) collective-permute-start(f32[2,2,256,256]{3,2,1,0:T(8,128)S(1)} %get-tuple-element.92), channel_id=1, source_target_pairs={{0,4},{4,0},{8,12},{12,8},{16,20},{20,16},{24,28},{28,24},{1,5},{5... | collective-permute-start | bytes 3145736 | tf_op jit(solution)/shard_map/ppermute | solution.py:471
  122.8 2.7 %collective-permute-start.17 = (f32[2,2,256,256]{3,2,1,0:T(8,128)S(1)}, f32[2,2,256,256]{3,2,1,0:T(8,128)S(1)}, u32[]{:S(2)}, u32[]{:S(2)}) collective-permute-start(f32[2,2,256,256]{3,2,1,0:T(8,128)S(1)} %get-tuple-element.101), channel_id=1, source_target_pairs={{0,4},{4,0},{8,12},{12,8},{16,20},{20,16},{24,28},{28,24},{1,5},{5... | collective-permute-start | bytes 3145736 | tf_op jit(solution)/shard_map/ppermute | solution.py:471
  (23 other events, 95.9 us)

commit v4 on v3

--- a/solution.py
+++ b/solution.py
@@ -167,31 +167,67 @@
     return added(block, product(scaled, block))
 
 
-def linkage_kernel(free, coupling, link, whole_map):
+def copies(pairs, sems):
+    made = [pltpu.make_async_copy(a, b, sems.at[i]) for i, (a, b) in enumerate(pairs)]
+    for copy in made:
+        copy.start()
+    return made
+
+
+def linkage_kernel(free_far, coupling_far, link_far, whole_map, free, coupling, link, here, gone):
     count = free.shape[0]
+    pairs = []
+    for slab in range(count):
+        pairs.append((free_far.at[slab], free.at[slab]))
+        pairs.append((coupling_far.at[slab], coupling.at[slab]))
+    loads = copies(pairs, here)
     links = []
     for slab in range(count):
+        if slab <= count // 2:
+            for load in loads[2 * slab : 2 * slab + 2 if slab < count // 2 else None]:
+                load.wait()
         links.append(product(pair_of(free, slab), pair_of(coupling, slab)))
         put(link, links[-1], slab)
     while len(links) > 1:
         paired = [product(b, a) for a, b in zip(links[0::2], links[1::2])]
         links = paired + links[len(paired) * 2 :]
     put(whole_map, links[0])
-
-
-def source_kernel(free, link, sums, source, whole_source):
+    for store in copies([(link.at[slab], link_far.at[slab]) for slab in range(count)], gone):
+        store.wait()
+
+
+def source_kernel(
+    free_far, link_far, sums, source_far, whole_source, free, link, source, here, gone
+):
     count = free.shape[0]
-    state = None
+    pairs = [(free_far.at[slab], free.at[slab]) for slab in range(count)]
+    pairs += [(link_far.at[slab], link.at[slab]) for slab in range(1, count)]
+    loads = copies(pairs, here)
+    state, stores = None, []
     for slab in range(count):
+        if slab <= 1:
+            for load in loads[slab : slab + 1 if slab == 0 else None]:
+                load.wait()
         row = potential_of(sums, slab, count, free.shape[-1])
         now = source_of(pair_of(free, slab), row)
         put(source, now, slab)
         state = now if state is None else added(sandwich(pair_of(link, slab), state), now)
     put(whole_source, state)
-
-
-def hop_kernel(whole_map, whole_source, carried, out):
-    put(out, added(sandwich(pair_of(whole_map), pair_of(carried)), pair_of(whole_source)))
+    for store in copies([(source.at[slab], source_far.at[slab]) for slab in range(count)], gone):
+        store.wait()
+
+
+def hop_kernel(here, whole_map, whole_source, arrived, kept, out, kept_out):
+    state = []
+    for part in range(2):
+        before = jnp.zeros_like(arrived[part]) if kept is None else kept[part]
+        state.append(jnp.where(here[0] != 0, arrived[part], before))
+    put(kept_out, state)
+    put(out, added(sandwich(pair_of(whole_map), state), pair_of(whole_source)))
+
+
+def first_hop_kernel(here, whole_map, whole_source, arrived, out, kept_out):
+    hop_kernel(here, whole_map, whole_source, arrived, None, out, kept_out)
 
 
 def beside_kernel(start, count, parts, *refs):
@@ -224,7 +260,7 @@
     first = added(sandwich(pair_of(link, 0), pair_of(state)), pair_of(source, 0))
     put(state, first)
     for part in range(2):
-        second_now = second[0, part]
+        second_now = jnp.where(pick[1] != 0, second[0, part], 0.0)
         here[0, part] = weights[0] * first[part] + weights[1] * second_now
         picked = jnp.where(pick[0] == 0, first[part], second_now)
         there[0, part] = weights[2] * own[0, part] + weights[3] * picked
@@ -260,7 +296,7 @@
     )
 
 
-def exchanged(payload, head):
+def exchanged(payload, head, beside):
     peers, mine = lax.axis_size("energy"), lax.axis_index("energy")
     assert peers & (peers - 1) == 0
     rest = payload[head:]
@@ -268,12 +304,14 @@
     is_head = lax.broadcasted_iota(jnp.int32, payload.shape, 0) < head
     mask = 1
     while mask < peers:
+        if mask * 2 > peers // 2:
+            payload, beside = lax.optimization_barrier((payload, beside))
         arrived = lax.ppermute(payload, "energy", [(e, e ^ mask) for e in range(peers)])
         before = jnp.where((mine ^ mask) == mine - 1, arrived[head:], before)
         after = jnp.where((mine ^ mask) == mine + 1, arrived[head:], after)
         payload = jnp.where(is_head, payload + arrived, payload)
         mask = 2 * mask + 1
-    return payload, before, after
+    return payload, before, after, beside
 
 
 def per_device(
@@ -299,30 +337,35 @@
     if relayed:
         first_pairs = [(e, e ^ 2) for e in everyone]
         second_pairs = [(2, 4), (3, 5), (4, 2), (5, 3)]
-        relay_pairs = [(0, 4), (1, 5), (6, 2), (7, 3)]
+        relay_pairs = [(e, e ^ 4) for e in everyone]
         turned = (mine // 2) % 2
+        has_second = jnp.where((mine >= 2) & (mine < 6), 1, 0)
     else:
         first_pairs = [(e, e - 2) for e in everyone if e >= 2]
         second_pairs = [(e, e + 2) for e in everyone if e + 2 < energies]
-        relay_pairs = None
+        relay_pairs = second_pairs
         turned = jnp.zeros_like(mine)
+        has_second = jnp.ones_like(mine)
     twin_pairs = [(e, e ^ 1) for e in everyone]
 
     half = count // 2
-    cuts = [free[:1], free[1:half], free[half:]]
-    free_first = [lax.ppermute(cuts[0], "energy", first_pairs)]
-
+    free_first = [lax.ppermute(free[:1], "energy", first_pairs)]
+
+    place = lax.axis_index("slab")
     wire_up = [(i, i + 1) for i in range(peers - 1)]
-    wire_down = [(j, i) for i, j in wire_up]
+
+    def swaps(start):
+        pairs = [(i, i + 1) for i in range(start, peers - 1, 2)]
+        return pairs + [(j, i) for i, j in pairs]
+
     stacked = jnp.stack([potential_old, permittivity])
     lower, upper = end_planes(stacked, 1)
-    wire_before = lax.ppermute(upper, "slab", wire_up)
-    wire_after = lax.ppermute(lower, "slab", wire_down)
-    link, whole_map = call(linkage_kernel, 24, 2 * count - 1, (blocks, whole), free, coupling)
-
-    wire_before, wire_after, link, whole_map = lax.optimization_barrier(
-        (wire_before, wire_after, link, whole_map)
-    )
+    even = place % 2 == 0
+    arrived = lax.ppermute(jnp.where(even, upper, lower), "slab", swaps(0))
+    crossed = lax.ppermute(jnp.where(even, lower, upper), "slab", swaps(1))
+    wire_before = jnp.where(even, crossed, arrived)
+    wire_after = jnp.where(even, arrived, crossed)
+
     cells, rows, depth = charge.shape
     head = 5 * count * (width // depth)
     payload = call(
@@ -338,26 +381,75 @@
         in_specs=[pl.BlockSpec(memory_space=pltpu.SMEM)]
         + [pl.BlockSpec(memory_space=pltpu.VMEM)] * 6,
     )
-    sums, ends_before, ends_after = exchanged(payload, head)
-
-    first_arrived, middle, sums = lax.optimization_barrier((free_first[0], cuts[1], sums))
-    free_first = [first_arrived, lax.ppermute(middle, "energy", first_pairs)]
-    relay, relayed_cuts = (relay_pairs, free_first) if relayed else (second_pairs, cuts)
-    free_second = [lax.ppermute(part, "energy", relay) for part in relayed_cuts[:2]]
-    source, whole_source = call(source_kernel, 24, 3 * count - 2, (blocks, whole), free, link, sums)
+    payload, *at_gather = lax.optimization_barrier((payload, free, coupling))
+    far, near = pl.BlockSpec(memory_space=pl.ANY), pl.BlockSpec(memory_space=pltpu.VMEM)
+    held = pltpu.VMEM((count, 2, width, width), jnp.float32)
+    link, whole_map = call(
+        linkage_kernel,
+        56,
+        2 * count - 1,
+        (blocks, whole),
+        *at_gather,
+        in_specs=[far, far],
+        out_specs=(far, near),
+        scratch_shapes=[
+            held,
+            held,
+            held,
+            pltpu.SemaphoreType.DMA((2 * count,)),
+            pltpu.SemaphoreType.DMA((count,)),
+        ],
+    )
+    sums, ends_before, ends_after, (link, whole_map) = exchanged(payload, head, (link, whole_map))
+
+    arrived, free_then, field, perm, sums = lax.optimization_barrier(
+        (free_first[0], free, potential_old, permittivity, sums)
+    )
+    free_first = [arrived, lax.ppermute(free_then[1:2], "energy", first_pairs)]
+    free_second = [lax.ppermute(arrived if relayed else free_then[:1], "energy", relay_pairs)]
+
+    def sent_on(part):
+        given = free_first[part] if relayed else free_then[part : part + 1]
+        free_second.append(lax.ppermute(given, "energy", relay_pairs))
+
+    def sent_after(part, *others):
+        tied = lax.optimization_barrier((free_first[part - 1], free_then, *others))
+        free_first[part - 1] = tied[0]
+        cut = tied[1][part : part + 1]
+        free_first.append(lax.ppermute(cut, "energy", first_pairs))
+        return tied[2:]
+
+    source, whole_source = call(
+        source_kernel,
+        56,
+        3 * count - 2,
+        (blocks, whole),
+        free,
+        link,
+        sums,
+        in_specs=[far, far, near],
+        out_specs=(far, near),
+        scratch_shapes=[
+            held,
+            held,
+            held,
+            pltpu.SemaphoreType.DMA((2 * count - 1,)),
+            pltpu.SemaphoreType.DMA((count,)),
+        ],
+    )
 
     ends_before = ends_before.reshape(2, 2, cells, 1, depth)
     ends_after = ends_after.reshape(2, 2, cells, 1, depth)
     edge = jnp.zeros((2, cells, rows, 1), jnp.float32)
     halos = ((wire_before, wire_after), (ends_before[:, 1], ends_after[:, 0]), (edge, edge))
-    potential_new = relaxed(potential_old, permittivity, charge, halos)
+    potential_new = relaxed(field, perm, charge, halos)
 
     odd = mine % 2
     distance = jnp.array([2, 2, 1, 1], jnp.int32)
     lowered = jnp.stack([turned, 1 - turned, 1 - odd, odd]).astype(jnp.float32)
     factors = (shifts[None, :] == distance[:, None]) * (occupation[None, :] + lowered[:, None])
     weights = jnp.sum(factors[:, :, None, None] * mode_tiles[None], axis=1)
-    pick = jnp.reshape(turned ^ odd, (1,)).astype(jnp.int32)
+    pick = jnp.stack([turned ^ odd, has_second]).astype(jnp.int32)
 
     block = pl.BlockSpec((1, 2, width, width), lambda s: (s, 0, 0, 0))
     one_state = pl.BlockSpec((2, width, width), lambda s: (0, 0, 0))
@@ -386,10 +478,10 @@
             out_specs=(whole_spec, whole_spec),
         )
 
-    def greens_of(link, source, carried):
+    def greens_of(room, link, source, carried):
         return call(
             greens_kernel,
-            16,
+            room,
             2 * link.shape[0],
             (shape(*link.shape), whole),
             link,
@@ -400,46 +492,62 @@
             out_specs=(block, one_state),
         )
 
-    leaving = whole_source
+    leaving, kept = whole_source, None
     beside_first, beside_second = [None, None], [None, None]
-    for hop in range(peers - 2):
-        carried = lax.ppermute(leaving, "slab", wire_up)
-        if hop == 0:
-            free_first[1], last = lax.optimization_barrier((free_first[1], cuts[2]))
-            free_first.append(lax.ppermute(last, "energy", first_pairs))
-            carried, potential_new, weights, free_first[1], free_second[0] = (
+    flag = pl.BlockSpec(memory_space=pltpu.SMEM)
+    for hop in range(1, peers - 1):
+        arrived = lax.ppermute(leaving, "slab", swaps((hop - 1) % 2))
+        if hop == 1:
+            sent_on(1)
+            sent_after(2)
+            arrived, potential_new, weights, free_first[1], free_second[0] = (
                 lax.optimization_barrier(
-                    (carried, potential_new, weights, free_first[1], free_second[0])
+                    (arrived, potential_new, weights, free_first[1], free_second[0])
                 )
             )
-        if hop == 1:
+        if hop == 2:
+            sent_on(2)
+            sent_after(3)
             beside_first[0] = beside(0, free_first[:2])
-            carried, beside_first[0] = lax.optimization_barrier((carried, beside_first[0]))
-        leaving = call(hop_kernel, 12, 2, whole, whole_map, whole_source, carried)
+            arrived, beside_first[0], free_first[2], free_second[1] = lax.optimization_barrier(
+                (arrived, beside_first[0], free_first[2], free_second[1])
+            )
+        here = jnp.reshape(place == hop, (1,)).astype(jnp.int32)
+        states = (arrived,) if kept is None else (arrived, kept)
+        leaving, kept = call(
+            first_hop_kernel if kept is None else hop_kernel,
+            12,
+            2,
+            (whole, whole),
+            here,
+            whole_map,
+            whole_source,
+            *states,
+            in_specs=[flag] + [near] * (2 + len(states)),
+            out_specs=(near, near),
+        )
 
     def both(pairs):
         return [(a * peers + i, b * peers + j) for a, b in pairs for i, j in wire_up]
 
-    carried = lax.ppermute(leaving, "slab", wire_up)
+    arrived = lax.ppermute(leaving, "slab", swaps((peers - 2) % 2))
     carried_second = lax.ppermute(leaving, ("energy", "slab"), both(second_pairs))
     beside_second[0] = beside(0, free_second[:2])
-    leaving, last = lax.optimization_barrier((leaving, free_first[2] if relayed else last))
-    free_second.append(lax.ppermute(last, "energy", relay))
+    sent_on(3)
     beside_first[1] = beside(1, free_first[2:])
-    carried, beside_first[1], beside_second[0] = lax.optimization_barrier(
-        (carried, beside_first[1], beside_second[0])
-    )
+    arrived, beside_first[1], beside_second[0], free_second[2] = lax.optimization_barrier(
+        (arrived, beside_first[1], beside_second[0], free_second[2])
+    )
+    carried = jnp.where(place == peers - 1, arrived, kept)
     carried_first = lax.ppermute(carried, "energy", first_pairs)
-    greens, _ = greens_of(link, source, carried)
+    greens, _ = greens_of(56, link, source, carried)
     beside_second[1] = beside(1, free_second[2:])
     carried_second, greens = lax.optimization_barrier((carried_second, greens))
     greens_second = []
     for part in beside_second:
-        made, carried_second = greens_of(*part, carried_second)
+        made, carried_second = greens_of(16, *part, carried_second)
         greens_second.append(made)
-    carried_first, greens_second[0], beside_second[1] = lax.optimization_barrier(
-        (carried_first, greens_second[0], beside_second[1])
-    )
+    carried_first, greens_second[0] = lax.optimization_barrier((carried_first, greens_second[0]))
 
     outputs = []
     for index, part in enumerate(beside_first):

time: 128 us -> 144 us (1.12); the launches traced: 127 us -> 142 us
  Pallas kernels: 37.5 us -> 48.9 us
  starting transfers between devices: 32.4 us -> 24.1 us
  waiting for transfers between devices: 34.3 us -> 41 us
  local copies, waits for them, and re-layouts: 16.9 us -> 20.3 us
    pallas_call x14, Pallas kernels: 37.5 us -> 48.9 us  [call(): pl.pallas_call(kernel, out_shape=out_shapes, cost_estimate=cost, compiler...]
    ppermute x1, waiting for transfers between devices: 0.01 us -> 8.63 us  [per_device(): carried_first = lax.ppermute(carried, 'energy', first_pairs)]
    ppermute x11 -> x13, starting transfers between devices: 21.5 us -> 15.4 us  [the longest x3 4.18 us: sent_on(): free_second.append(lax.ppermute(given, 'energy', relay_pairs))]
    slice x2 -> x4, local copies, waits for them, and re-layouts: 3.33 us -> 6.14 us  [the longest x2 3.8 us: sent_after(): cut = tied[1][part:part + 1]]
    ppermute x3, waiting for transfers between devices: 8.01 us -> 5.32 us  [exchanged(): lax.ppermute(payload, 'energy', [(e, e ^ mask) for e in range(peers)])]
    ppermute x2, starting transfers between devices: 3.3 us -> 1.28 us  [per_device(): outputs.append(here + lax.ppermute(there, 'energy', twin_pairs))]
    unnamed x74 -> x68, local copies, waits for them, and re-layouts: 12.1 us -> 14 us
    ppermute x1, starting transfers between devices: 1.7 us -> 0.01 us  [per_device(): carried_first = lax.ppermute(carried, 'energy', first_pairs)]
  transfers between devices with their start and end apart: 18 -> 20, of which waited for: 10 -> 9; matrix products, arithmetic and copies ran while one was open for 6% -> 6% of each run, Pallas kernels for 27% -> 32%
where the time goes in v4:
time: 144 us; the launch traced here: 142 us
  Pallas kernels  48.9 us (34%)
  waiting for transfers between devices  41 us (28%)
  starting transfers between devices  24.1 us (17%)
  local copies, waits for them, and re-layouts  20.3 us (14%)
  other arithmetic  6.36 us (4%)
    pallas_call x14, Pallas kernels, call(): pl.pallas_call(kernel, out_shape=out_shapes, cost_estimate=cost, compiler...  48.9 us
    unnamed x68, local copies, waits for them, and re-layouts  14 us
    ppermute x3, waiting for transfers between devices, sent_on(): free_second.append(lax.ppermute(given, 'energy', relay_pairs))  12.4 us
    ppermute x1, waiting for transfers between devices, per_device(): carried_first = lax.ppermute(carried, 'energy', first_pairs)  8.63 us
    ppermute x2, waiting for transfers between devices, per_device(): arrived = lax.ppermute(leaving, 'slab', swaps((hop - 1) % 2))  8.54 us
    ppermute x3, waiting for transfers between devices, exchanged(): lax.ppermute(payload, 'energy', [(e, e ^ mask) for e in range(peers)])  5.32 us
    ppermute x3, starting transfers between devices, sent_on(): free_second.append(lax.ppermute(given, 'energy', relay_pairs))  4.18 us
    ppermute x3, starting transfers between devices, exchanged(): lax.ppermute(payload, 'energy', [(e, e ^ mask) for e in range(peers)])  3.8 us
  transfers between devices with their start and end apart: 20, of which 9 were waited for; matrix products, arithmetic and copies ran while one was open for 6% of the time, Pallas kernels for 32%

profile of v4, /device:TPU:13, one launch (start us, length us, event | category | flops | bytes accessed | tf_op | source)
XLA Modules:
  0.0 141.6 jit_solution(15842179112708979687)
XLA Ops:
  1.4 3.2 %collective-permute-start = (f32[2,1,4,128]{3,2,0,1:T(4,128)S(1)}, f32[2,1,4,128]{3,2,0,1:T(4,128)S(1)}, u32[]{:S(2)}, u32[]{:S(2)}) collective-permute-start(f32[2,1,4,128]{3,2,0,1:T(4,128)S(1)} %bitcast.68), channel_id=1, source_target_pairs={{1,2},{2,1},{5,6},{6,5},{9,10},{10,9},{13,14},{14,13},{17,18},{18,... | collective-permute-start | bytes 12296 | tf_op jit(solution)/shard_map/ppermute | solution.py:365
  5.8 1.3 collective-permute-start.4
  12.0 1.4 collective-permute-start.2
  13.4 5.4 %shard_map.114 = (f32[4,2,256,256]{3,2,1,0:T(8,128)}, f32[2,256,256]{2,1,0:T(8,128)}) custom-call(f32[4,2,256,256]{3,2,1,0:T(8,128)} %bitcast.55, f32[4,2,256,256]{3,2,1,0:T(8,128)} %refs_2_.7), custom_call_target="tpu_custom_call" | custom-call | flops 2113929216 | bytes 6815744 | tf_op jit(solution)/shard_map/pallas_call | solution.py:67
  20.6 2.0 %collective-permute-done.3 = f32[104,128]{1,0:T(8,128)S(1)} collective-permute-done((f32[104,128]{1,0:T(8,128)S(1)}, f32[104,128]{1,0:T(8,128)S(1)}, u32[]{:S(2)}, u32[]{:S(2)}) %collective-permute-start.3) | collective-permute-done | bytes 53280 | tf_op jit(solution)/shard_map/ppermute | solution.py:309
  23.9 3.3 %collective-permute-done.5 = f32[104,128]{1,0:T(8,128)S(1)} collective-permute-done((f32[104,128]{1,0:T(8,128)S(1)}, f32[104,128]{1,0:T(8,128)S(1)}, u32[]{:S(2)}, u32[]{:S(2)}) %collective-permute-start.5) | collective-permute-done | bytes 53280 | tf_op jit(solution)/shard_map/ppermute | solution.py:309
  30.8 7.8 %shard_map.115 = (f32[4,2,256,256]{3,2,1,0:T(8,128)}, f32[2,256,256]{2,1,0:T(8,128)}) custom-call(f32[4,2,256,256]{3,2,1,0:T(8,128)} %bitcast.57, f32[4,2,256,256]{3,2,1,0:T(8,128)} %get-tuple-element.75.link_far.link, f32[104,128]{1,0:T(8,128)} %add_select_fusion.sums.refs_3_), custom_call_target="tpu_custom_call" | custom-call | flops 3019898880 | bytes 6868992 | tf_op jit(solution)/shard_map/pallas_call | solution.py:67
  39.5 3.4 %collective-permute-done.7.refs_1_ = f32[1,2,256,256]{3,2,1,0:T(8,128)} collective-permute-done((f32[1,2,256,256]{3,2,1,0:T(8,128)S(1)}, f32[1,2,256,256]{3,2,1,0:T(8,128)}, u32[]{:S(2)}, u32[]{:S(2)}) %collective-permute-start.7) | collective-permute-done | bytes 524320 | tf_op jit(solution)/shard_map/ppermute | solution.py:408
  42.9 1.9 %slice.131 = f32[1,2,256,256]{3,2,1,0:T(8,128)} slice(f32[4,2,256,256]{3,2,1,0:T(8,128)} %bitcast.58), slice={[2:3], [0:2], [0:256], [0:256]} | slice | bytes 1048576 | tf_op jit(solution)/shard_map/slice | solution.py:418
  46.8 5.0 %collective-permute-done.6.arrived = f32[2,256,256]{2,1,0:T(8,128)S(1)} collective-permute-done((f32[2,256,256]{2,1,0:T(8,128)}, f32[2,256,256]{2,1,0:T(8,128)S(1)}, u32[]{:S(2)}, u32[]{:S(2)}) %collective-permute-start.6) | collective-permute-done | bytes 524320 | tf_op jit(solution)/shard_map/ppermute | solution.py:499
  53.1 1.8 %shard_map.116 = (f32[2,256,256]{2,1,0:T(8,128)}, f32[2,256,256]{2,1,0:T(8,128)S(1)}) custom-call(s32[1]{0:T(128)} %bitcast.30.here, f32[2,256,256]{2,1,0:T(8,128)S(1)} %copy-done.25, f32[2,256,256]{2,1,0:T(8,128)S(1)} %copy-done.22, f32[2,256,256]{2,1,0:T(8,128)S(1)} %collective-permute-done.6.arrived), custom_call_target="tpu_custom_call" | custom-call | flops 603979776 | bytes 2621444 | tf_op jit(solution)/shard_map/pallas_call | solution.py:67
  55.7 2.2 %collective-permute-start.9 = (f32[2,256,256]{2,1,0:T(8,128)}, f32[2,256,256]{2,1,0:T(8,128)}, u32[]{:S(2)}, u32[]{:S(2)}) collective-permute-start(f32[2,256,256]{2,1,0:T(8,128)} %get-tuple-element.87), channel_id=1, source_target_pairs={{1,2},{2,1},{5,6},{6,5},{9,10},{10,9},{13,14},{14,13},{17,18},{18,... | collective-permute-start | bytes 1572872 | tf_op jit(solution)/shard_map/ppermute | solution.py:499
  57.9 1.9 %slice.132 = f32[1,2,256,256]{3,2,1,0:T(8,128)} slice(f32[4,2,256,256]{3,2,1,0:T(8,128)} %bitcast.59), slice={[3:4], [0:2], [0:256], [0:256]} | slice | bytes 1048576 | tf_op jit(solution)/shard_map/slice | solution.py:418
  60.8 1.6 %copy-done.14 = f32[4,2,256,256]{3,2,1,0:T(8,128)S(1)} copy-done((f32[4,2,256,256]{3,2,1,0:T(8,128)S(1)}, f32[4,2,256,256]{3,2,1,0:T(8,128)}, u32[]{:S(2)}) %copy-start.14) | copy-done | bytes 2097176
  63.4 2.6 %shard_map.117 = (f32[2,2,256,256]{3,2,1,0:T(8,128)S(1)}, f32[2,2,256,256]{3,2,1,0:T(8,128)S(1)}) custom-call(f32[1,2,256,256]{3,2,1,0:T(8,128)S(1)} %copy-done.19, f32[1,2,256,256]{3,2,1,0:T(8,128)} %collective-permute-done.7.refs_1_, f32[4,2,256,256]{3,2,1,0:T(8,128)S(1)} %copy-done.14, f32[104,128]{1,0:T(8,128)S(1)} %copy-done.11), custom_call_target="tpu_custom_call" | custom-call | flops 1207959552 | bytes 5296128 | tf_op jit(solution)/shard_map/pallas_call | solution.py:67
  66.1 3.5 %collective-permute-done.9.arrived = f32[2,256,256]{2,1,0:T(8,128)} collective-permute-done((f32[2,256,256]{2,1,0:T(8,128)}, f32[2,256,256]{2,1,0:T(8,128)}, u32[]{:S(2)}, u32[]{:S(2)}) %collective-permute-start.9) | collective-permute-done | bytes 524320 | tf_op jit(solution)/shard_map/ppermute | solution.py:499
  69.8 2.8 %shard_map.118 = (f32[2,256,256]{2,1,0:T(8,128)}, f32[2,256,256]{2,1,0:T(8,128)S(1)}) custom-call(s32[1]{0:T(128)} %bitcast.31.here, f32[2,256,256]{2,1,0:T(8,128)S(1)} %copy-done.26, f32[2,256,256]{2,1,0:T(8,128)S(1)} %copy-done.23, f32[2,256,256]{2,1,0:T(8,128)} %collective-permute-done.9.arrived, f32[2,256,256]{2,1,0:T(8,128)S(1)} %copy-done.28), custom_call_target="tpu_custom_call" | custom-call | flops 603979776 | bytes 3145732 | tf_op jit(solution)/shard_map/pallas_call | solution.py:67
  73.4 3.6 %collective-permute-start.16 = (f32[2,256,256]{2,1,0:T(8,128)}, f32[2,256,256]{2,1,0:T(8,128)}, u32[]{:S(2)}, u32[]{:S(2)}) collective-permute-start(f32[2,256,256]{2,1,0:T(8,128)} %get-tuple-element.97), channel_id=1, source_target_pairs={{8,17},{9,18},{10,19},{12,21},{13,22},{14,23},{16,9},{17,10},{18,1... | collective-permute-start | bytes 1572872 | tf_op jit(solution)/shard_map/ppermute | solution.py:534
  77.0 1.6 %copy-done.15 = f32[4,2,256,256]{3,2,1,0:T(8,128)S(1)} copy-done((f32[4,2,256,256]{3,2,1,0:T(8,128)S(1)}, f32[4,2,256,256]{3,2,1,0:T(8,128)}, u32[]{:S(2)}) %copy-start.15) | copy-done | bytes 2097176
  79.7 2.7 %shard_map.120 = (f32[2,2,256,256]{3,2,1,0:T(8,128)S(1)}, f32[2,2,256,256]{3,2,1,0:T(8,128)S(1)}) custom-call(f32[1,2,256,256]{3,2,1,0:T(8,128)S(1)} %copy-done.21, f32[1,2,256,256]{3,2,1,0:T(8,128)} %collective-permute-done.11.refs_1_, f32[4,2,256,256]{3,2,1,0:T(8,128)S(1)} %copy-done.15, f32[104,128]{1,0:T(8,128)S(1)} %copy-done.11), custom_call_target="tpu_custom_call" | custom-call | flops 1207959552 | bytes 5296128 | tf_op jit(solution)/shard_map/pallas_call | solution.py:67
  84.4 2.8 %shard_map.119 = (f32[2,2,256,256]{3,2,1,0:T(8,128)S(1)}, f32[2,2,256,256]{3,2,1,0:T(8,128)S(1)}) custom-call(f32[1,2,256,256]{3,2,1,0:T(8,128)} %collective-permute-done.10.refs_0_, f32[1,2,256,256]{3,2,1,0:T(8,128)} %collective-permute-done.13.refs_1_, f32[4,2,256,256]{3,2,1,0:T(8,128)S(1)} %copy-done.16, f32[104,128]{1,0:T(8,128)S(1)} %copy-done.11), custom_call_target="tpu_custom_call" | custom-call | flops 1207959552 | bytes 5296128 | tf_op jit(solution)/shard_map/pallas_call | solution.py:67
  90.2 6.7 %shard_map.121 = (f32[4,2,256,256]{3,2,1,0:T(8,128)}, f32[2,256,256]{2,1,0:T(8,128)}) custom-call(f32[4,2,256,256]{3,2,1,0:T(8,128)} %get-tuple-element.75.link_far.link, f32[4,2,256,256]{3,2,1,0:T(8,128)} %get-tuple-element.110.source, f32[2,256,256]{2,1,0:T(8,128)} %broadcast_select_fusion.carried), custom_call_target="tpu_custom_call" | custom-call | flops 2415919104 | bytes 7340032 | tf_op jit(solution)/shard_map/pallas_call | solution.py:67
  97.3 3.1 %shard_map.122 = (f32[2,2,256,256]{3,2,1,0:T(8,128)S(1)}, f32[2,256,256]{2,1,0:T(8,128)S(1)}) custom-call(f32[2,2,256,256]{3,2,1,0:T(8,128)S(1)} %copy-done.30, f32[2,2,256,256]{3,2,1,0:T(8,128)S(1)} %copy-done.32, f32[2,256,256]{2,1,0:T(8,128)} %collective-permute-done.16.carried), custom_call_target="tpu_custom_call" | custom-call | flops 1207959552 | bytes 4194304 | tf_op jit(solution)/shard_map/pallas_call | solution.py:67
  100.4 8.6 %collective-permute-done.15.carried = f32[2,256,256]{2,1,0:T(8,128)} collective-permute-done((f32[2,256,256]{2,1,0:T(8,128)}, f32[2,256,256]{2,1,0:T(8,128)}, u32[]{:S(2)}, u32[]{:S(2)}) %collective-permute-start.15) | collective-permute-done | bytes 524320 | tf_op jit(solution)/shard_map/ppermute | solution.py:542
  109.0 3.4 %shard_map.123 = (f32[2,2,256,256]{3,2,1,0:T(8,128)S(1)}, f32[2,2,256,256]{3,2,1,0:T(8,128)S(1)}, f32[2,256,256]{2,1,0:T(8,128)S(1)}) custom-call(s32[2]{0:T(128)S(1)} %pad_add_fusion.pick, f32[2,2,256,256]{3,2,1,0:T(8,128)S(1)} %get-tuple-element.93.link, f32[2,2,256,256]{3,2,1,0:T(8,128)S(1)} %get-tuple-element.94.source, ...), custom_call_target="tpu_custom_call" | custom-call | flops 1207959552 | bytes 9437192 | tf_op jit(solution)/shard_map/pallas_call | solution.py:67
  113.0 2.7 %collective-permute-start.18 = (f32[1,2,256,256]{3,2,1,0:T(8,128)}, f32[1,2,256,256]{3,2,1,0:T(8,128)S(1)}, u32[]{:S(2)}, u32[]{:S(2)}) collective-permute-start(f32[1,2,256,256]{3,2,1,0:T(8,128)} %collective-permute-done.13.refs_1_), channel_id=1, source_target_pairs={{0,16},{4,20},{8,24},{12,28},{16,0},{20,4},{24,8},{28,12},{1,17},{... | collective-permute-start | bytes 1572872 | tf_op jit(solution)/shard_map/ppermute | solution.py:413
  115.7 12.4 %collective-permute-done.18.refs_1_ = f32[1,2,256,256]{3,2,1,0:T(8,128)S(1)} collective-permute-done((f32[1,2,256,256]{3,2,1,0:T(8,128)}, f32[1,2,256,256]{3,2,1,0:T(8,128)S(1)}, u32[]{:S(2)}, u32[]{:S(2)}) %collective-permute-start.18) | collective-permute-done | bytes 524320 | tf_op jit(solution)/shard_map/ppermute | solution.py:413
  128.1 2.6 %shard_map.124 = (f32[2,2,256,256]{3,2,1,0:T(8,128)S(1)}, f32[2,2,256,256]{3,2,1,0:T(8,128)S(1)}) custom-call(f32[1,2,256,256]{3,2,1,0:T(8,128)} %collective-permute-done.14.refs_0_, f32[1,2,256,256]{3,2,1,0:T(8,128)S(1)} %collective-permute-done.18.refs_1_, f32[4,2,256,256]{3,2,1,0:T(8,128)S(1)} %copy-done.17, f32[104,128]{1,0:T(8,128)S(1)} %copy-done.11), custom_call_target="tpu_custom_call" | custom-call | flops 1207959552 | bytes 5296128 | tf_op jit(solution)/shard_map/pallas_call | solution.py:67
  130.7 2.7 %shard_map.125 = (f32[2,2,256,256]{3,2,1,0:T(8,128)S(1)}, f32[2,256,256]{2,1,0:T(8,128)}) custom-call(f32[2,2,256,256]{3,2,1,0:T(8,128)S(1)} %get-tuple-element.124.link, f32[2,2,256,256]{3,2,1,0:T(8,128)S(1)} %get-tuple-element.125.source, f32[2,256,256]{2,1,0:T(8,128)S(1)} %get-tuple-element.126.carried), custom_call_target="tpu_custom_call" | custom-call | flops 1207959552 | bytes 4194304 | tf_op jit(solution)/shard_map/pallas_call | solution.py:67
  133.4 3.5 %shard_map.126 = (f32[2,2,256,256]{3,2,1,0:T(8,128)S(1)}, f32[2,2,256,256]{3,2,1,0:T(8,128)S(1)}, f32[2,256,256]{2,1,0:T(8,128)}) custom-call(s32[2]{0:T(128)S(1)} %pad_add_fusion.pick, f32[2,2,256,256]{3,2,1,0:T(8,128)S(1)} %copy-done.6, f32[2,2,256,256]{3,2,1,0:T(8,128)S(1)} %copy-done.8, f32[2,256,256]{2,1,0:T(8,128)S(1)} %get-tuple-element.122.carried, ...), custom_call_target="tpu_custom_call" | custom-call | flops 1207959552 | bytes 9437192 | tf_op jit(solution)/shard_map/pallas_call | solution.py:67
  137.7 2.3 %collective-permute-done.19 = f32[2,2,256,256]{3,2,1,0:T(8,128)S(1)} collective-permute-done((f32[2,2,256,256]{3,2,1,0:T(8,128)S(1)}, f32[2,2,256,256]{3,2,1,0:T(8,128)S(1)}, u32[]{:S(2)}, u32[]{:S(2)}) %collective-permute-start.19) | collective-permute-done | bytes 1048608 | tf_op jit(solution)/shard_map/ppermute | solution.py:579
  140.2 1.5 %maximum_bitcast_fusion = f32[1,4,2,256,256]{4,3,2,1,0:T(8,128)} fusion(f32[2,2,256,256]{3,2,1,0:T(8,128)S(1)} %add.136, f32[2,2,256,256]{3,2,1,0:T(8,128)S(1)} %add.135), kind=kLoop, calls=%fused_computation.1 | loop fusion | flops 524288 | bytes 4194304 | tf_op jit(solution)/shard_map/broadcast_in_dim | solution.py:580
  (117 shorter events, 29.4 us)
Async XLA Ops:
  1.4 6.5 %collective-permute-start = (f32[2,1,4,128]{3,2,0,1:T(4,128)S(1)}, f32[2,1,4,128]{3,2,0,1:T(4,128)S(1)}, u32[]{:S(2)}, u32[]{:S(2)}) collective-permute-start(f32[2,1,4,128]{3,2,0,1:T(4,128)S(1)} %bitcast.68), channel_id=1, source_target_pairs={{1,2},{2,1},{5,6},{6,5},{9,10},{10,9},{13,14},{14,13},{17,18},{18,... | collective-permute-start | bytes 12296 | tf_op jit(solution)/shard_map/ppermute | solution.py:365
  4.6 3.3 %collective-permute-start.1 = (f32[2,1,4,128]{3,2,0,1:T(4,128)S(1)}, f32[2,1,4,128]{3,2,0,1:T(4,128)S(1)}, u32[]{:S(2)}, u32[]{:S(2)}) collective-permute-start(f32[2,1,4,128]{3,2,0,1:T(4,128)S(1)} %get-tuple-element.132), channel_id=1, source_target_pairs={{0,1},{2,3},{1,0},{3,2},{4,5},{6,7},{5,4},{7,6},{8,9},{10,11},{9,8... | collective-permute-start | bytes 12296 | tf_op jit(solution)/shard_map/ppermute | solution.py:364
  5.8 22.2 %collective-permute-start.4 = (f32[1,2,256,256]{3,2,1,0:T(8,128)S(1)}, f32[1,2,256,256]{3,2,1,0:T(8,128)S(1)}, u32[]{:S(2)}, u32[]{:S(2)}) collective-permute-start(f32[1,2,256,256]{3,2,1,0:T(8,128)S(1)} %slice_bitcast_fusion), channel_id=1, source_target_pairs={{0,8},{4,12},{8,0},{12,4},{16,24},{20,28},{24,16},{28,20},{1,9},{5... | collective-permute-start | bytes 1572872 | tf_op jit(solution)/shard_map/ppermute | solution.py:352
  12.0 8.2 %copy-start.33 = (f32[4,256,256]{2,1,0:T(8,128)S(1)}, f32[4,256,256]{2,1,0:T(8,128)}, u32[]{:S(2)}) copy-start(f32[4,256,256]{2,1,0:T(8,128)} %param.18) | copy-start | bytes 3145732
  12.0 6.8 %collective-permute-start.2 = (f32[104,128]{1,0:T(8,128)S(1)}, f32[104,128]{1,0:T(8,128)S(1)}, u32[]{:S(2)}, u32[]{:S(2)}) collective-permute-start(f32[104,128]{1,0:T(8,128)S(1)} %shard_map.113), channel_id=1, source_target_pairs={{0,4},{4,0},{8,12},{12,8},{16,20},{20,16},{24,28},{28,24},{1,5},{5... | collective-permute-start | bytes 159752 | tf_op jit(solution)/shard_map/ppermute | solution.py:309
  18.9 3.6 %collective-permute-start.3 = (f32[104,128]{1,0:T(8,128)S(1)}, f32[104,128]{1,0:T(8,128)S(1)}, u32[]{:S(2)}, u32[]{:S(2)}) collective-permute-start(f32[104,128]{1,0:T(8,128)S(1)} %add_select_fusion.2), channel_id=1, source_target_pairs={{0,12},{4,8},{8,4},{12,0},{16,28},{20,24},{24,20},{28,16},{1,13},{... | collective-permute-start | bytes 159752 | tf_op jit(solution)/shard_map/ppermute | solution.py:309
  22.7 4.5 %collective-permute-start.5 = (f32[104,128]{1,0:T(8,128)S(1)}, f32[104,128]{1,0:T(8,128)S(1)}, u32[]{:S(2)}, u32[]{:S(2)}) collective-permute-start(f32[104,128]{1,0:T(8,128)S(1)} %add_select_fusion.1), channel_id=1, source_target_pairs={{0,28},{4,24},{8,20},{12,16},{16,12},{20,8},{24,4},{28,0},{1,29},{... | collective-permute-start | bytes 159752 | tf_op jit(solution)/shard_map/ppermute | solution.py:309
  27.9 10.6 %copy-start.18 = (f32[1,2,256,256]{3,2,1,0:T(8,128)}, f32[1,2,256,256]{3,2,1,0:T(8,128)S(1)}, u32[]{:S(2)}) copy-start(f32[1,2,256,256]{3,2,1,0:T(8,128)S(1)} %collective-permute-done.4.refs_0_) | copy-start | bytes 1572868
  29.2 10.1 %copy-start.2 = (f32[16,4,128]{2,1,0:T(4,128)S(1)}, f32[16,4,128]{2,1,0:T(4,128)}, u32[]{:S(2)}) copy-start(f32[16,4,128]{2,1,0:T(4,128)} %param.12) | copy-start | bytes 98308
  29.2 10.1 %copy-start.4 = (f32[16,4,128]{2,1,0:T(4,128)S(1)}, f32[16,4,128]{2,1,0:T(4,128)}, u32[]{:S(2)}) copy-start(f32[16,4,128]{2,1,0:T(4,128)} %param.10) | copy-start | bytes 98308
  29.2 16.8 %copy-start.13 = (f32[16,4,128]{2,1,0:T(4,128)S(1)}, f32[16,4,128]{2,1,0:T(4,128)}, u32[]{:S(2)}) copy-start(f32[16,4,128]{2,1,0:T(4,128)} %param.11) | copy-start | bytes 98308
  29.3 13.6 %collective-permute-start.7 = (f32[1,2,256,256]{3,2,1,0:T(8,128)S(1)}, f32[1,2,256,256]{3,2,1,0:T(8,128)}, u32[]{:S(2)}, u32[]{:S(2)}) collective-permute-start(f32[1,2,256,256]{3,2,1,0:T(8,128)S(1)} %slice.130), channel_id=1, source_target_pairs={{0,8},{4,12},{8,0},{12,4},{16,24},{20,28},{24,16},{28,20},{1,9},{5... | collective-permute-start | bytes 1572872 | tf_op jit(solution)/shard_map/ppermute | solution.py:408
  30.5 16.3 %collective-permute-start.8 = (f32[1,2,256,256]{3,2,1,0:T(8,128)S(1)}, f32[1,2,256,256]{3,2,1,0:T(8,128)S(1)}, u32[]{:S(2)}, u32[]{:S(2)}) collective-permute-start(f32[1,2,256,256]{3,2,1,0:T(8,128)S(1)} %collective-permute-done.4.refs_0_), channel_id=1, source_target_pairs={{0,16},{4,20},{8,24},{12,28},{16,0},{20,4},{24,8},{28,12},{1,17},{... | collective-permute-start | bytes 1572872 | tf_op jit(solution)/shard_map/ppermute | solution.py:409
  38.6 14.5 %copy-start.22 = (f32[2,256,256]{2,1,0:T(8,128)S(1)}, f32[2,256,256]{2,1,0:T(8,128)}, u32[]{:S(2)}) copy-start(f32[2,256,256]{2,1,0:T(8,128)} %get-tuple-element.78.whole_source) | copy-start | bytes 1572868
  38.6 14.5 %copy-start.25 = (f32[2,256,256]{2,1,0:T(8,128)S(1)}, f32[2,256,256]{2,1,0:T(8,128)}, u32[]{:S(2)}) copy-start(f32[2,256,256]{2,1,0:T(8,128)} %get-tuple-element.85.whole_map) | copy-start | bytes 1572868
  38.6 13.2 %collective-permute-start.6 = (f32[2,256,256]{2,1,0:T(8,128)}, f32[2,256,256]{2,1,0:T(8,128)S(1)}, u32[]{:S(2)}, u32[]{:S(2)}) collective-permute-start(f32[2,256,256]{2,1,0:T(8,128)} %get-tuple-element.78.whole_source), channel_id=1, source_target_pairs={{0,1},{2,3},{1,0},{3,2},{4,5},{6,7},{5,4},{7,6},{8,9},{10,11},{9,8... | collective-permute-start | bytes 1572872 | tf_op jit(solution)/shard_map/ppermute | solution.py:499
  44.8 16.0 %copy-start.11 = (f32[104,128]{1,0:T(8,128)S(1)}, f32[104,128]{1,0:T(8,128)}, u32[]{:S(2)}) copy-start(f32[104,128]{1,0:T(8,128)} %add_select_fusion.sums.refs_3_) | copy-start | bytes 159748
  44.8 13.1 %collective-permute-start.10 = (f32[1,2,256,256]{3,2,1,0:T(8,128)}, f32[1,2,256,256]{3,2,1,0:T(8,128)}, u32[]{:S(2)}, u32[]{:S(2)}) collective-permute-start(f32[1,2,256,256]{3,2,1,0:T(8,128)} %slice.131), channel_id=1, source_target_pairs={{0,8},{4,12},{8,0},{12,4},{16,24},{20,28},{24,16},{28,20},{1,9},{5... | collective-permute-start | bytes 1572872 | tf_op jit(solution)/shard_map/ppermute | solution.py:419
  46.8 13.0 %copy-start.20 = (f32[1,2,256,256]{3,2,1,0:T(8,128)}, f32[1,2,256,256]{3,2,1,0:T(8,128)S(1)}, u32[]{:S(2)}) copy-start(f32[1,2,256,256]{3,2,1,0:T(8,128)S(1)} %collective-permute-done.8.refs_0_) | copy-start | bytes 1572868
  51.8 14.3 %collective-permute-start.11 = (f32[1,2,256,256]{3,2,1,0:T(8,128)}, f32[1,2,256,256]{3,2,1,0:T(8,128)}, u32[]{:S(2)}, u32[]{:S(2)}) collective-permute-start(f32[1,2,256,256]{3,2,1,0:T(8,128)} %collective-permute-done.7.refs_1_), channel_id=1, source_target_pairs={{0,16},{4,20},{8,24},{12,28},{16,0},{20,4},{24,8},{28,12},{1,17},{... | collective-permute-start | bytes 1572872 | tf_op jit(solution)/shard_map/ppermute | solution.py:413
  55.7 13.9 %collective-permute-start.9 = (f32[2,256,256]{2,1,0:T(8,128)}, f32[2,256,256]{2,1,0:T(8,128)}, u32[]{:S(2)}, u32[]{:S(2)}) collective-permute-start(f32[2,256,256]{2,1,0:T(8,128)} %get-tuple-element.87), channel_id=1, source_target_pairs={{1,2},{2,1},{5,6},{6,5},{9,10},{10,9},{13,14},{14,13},{17,18},{18,... | collective-permute-start | bytes 1572872 | tf_op jit(solution)/shard_map/ppermute | solution.py:499
  59.8 24.6 %collective-permute-start.13 = (f32[1,2,256,256]{3,2,1,0:T(8,128)}, f32[1,2,256,256]{3,2,1,0:T(8,128)}, u32[]{:S(2)}, u32[]{:S(2)}) collective-permute-start(f32[1,2,256,256]{3,2,1,0:T(8,128)} %slice.132), channel_id=1, source_target_pairs={{0,8},{4,12},{8,0},{12,4},{16,24},{20,28},{24,16},{28,20},{1,9},{5... | collective-permute-start | bytes 1572872 | tf_op jit(solution)/shard_map/ppermute | solution.py:419
  69.6 19.6 %collective-permute-start.14 = (f32[1,2,256,256]{3,2,1,0:T(8,128)}, f32[1,2,256,256]{3,2,1,0:T(8,128)}, u32[]{:S(2)}, u32[]{:S(2)}) collective-permute-start(f32[1,2,256,256]{3,2,1,0:T(8,128)} %collective-permute-done.10.refs_0_), channel_id=1, source_target_pairs={{0,16},{4,20},{8,24},{12,28},{16,0},{20,4},{24,8},{28,12},{1,17},{... | collective-permute-start | bytes 1572872 | tf_op jit(solution)/shard_map/ppermute | solution.py:413
  73.4 15.8 %collective-permute-start.12 = (f32[2,256,256]{2,1,0:T(8,128)}, f32[2,256,256]{2,1,0:T(8,128)}, u32[]{:S(2)}, u32[]{:S(2)}) collective-permute-start(f32[2,256,256]{2,1,0:T(8,128)} %get-tuple-element.97), channel_id=1, source_target_pairs={{0,1},{2,3},{1,0},{3,2},{4,5},{6,7},{5,4},{7,6},{8,9},{10,11},{9,8... | collective-permute-start | bytes 1572872 | tf_op jit(solution)/shard_map/ppermute | solution.py:533
  73.4 23.9 %collective-permute-start.16 = (f32[2,256,256]{2,1,0:T(8,128)}, f32[2,256,256]{2,1,0:T(8,128)}, u32[]{:S(2)}, u32[]{:S(2)}) collective-permute-start(f32[2,256,256]{2,1,0:T(8,128)} %get-tuple-element.97), channel_id=1, source_target_pairs={{8,17},{9,18},{10,19},{12,21},{13,22},{14,23},{16,9},{17,10},{18,1... | collective-permute-start | bytes 1572872 | tf_op jit(solution)/shard_map/ppermute | solution.py:534
  90.1 18.9 %collective-permute-start.15 = (f32[2,256,256]{2,1,0:T(8,128)}, f32[2,256,256]{2,1,0:T(8,128)}, u32[]{:S(2)}, u32[]{:S(2)}) collective-permute-start(f32[2,256,256]{2,1,0:T(8,128)} %broadcast_select_fusion.carried), channel_id=1, source_target_pairs={{0,8},{4,12},{8,0},{12,4},{16,24},{20,28},{24,16},{28,20},{1,9},{5... | collective-permute-start | bytes 1572872 | tf_op jit(solution)/shard_map/ppermute | solution.py:542
  90.2 7.1 %copy-start.32 = (f32[2,2,256,256]{3,2,1,0:T(8,128)S(1)}, f32[2,2,256,256]{3,2,1,0:T(8,128)}, u32[]{:S(2)}) copy-start(f32[2,2,256,256]{3,2,1,0:T(8,128)} %copy-done.31) | copy-start | bytes 3145732
  97.3 11.7 %copy-start = (f32[4,2,256,256]{3,2,1,0:T(8,128)S(1)}, f32[4,2,256,256]{3,2,1,0:T(8,128)}, u32[]{:S(2)}) copy-start(f32[4,2,256,256]{3,2,1,0:T(8,128)} %get-tuple-element.115.own) | copy-start | bytes 6291460
  109.0 19.1 %copy-start.17 = (f32[4,2,256,256]{3,2,1,0:T(8,128)S(1)}, f32[4,2,256,256]{3,2,1,0:T(8,128)}, u32[]{:S(2)}) copy-start(f32[4,2,256,256]{3,2,1,0:T(8,128)} %refs_2_.7) | copy-start | bytes 6291460
  112.4 24.5 %collective-permute-start.17 = (f32[2,2,256,256]{3,2,1,0:T(8,128)S(1)}, f32[2,2,256,256]{3,2,1,0:T(8,128)S(1)}, u32[]{:S(2)}, u32[]{:S(2)}) collective-permute-start(f32[2,2,256,256]{3,2,1,0:T(8,128)S(1)} %get-tuple-element.119), channel_id=1, source_target_pairs={{0,4},{4,0},{8,12},{12,8},{16,20},{20,16},{24,28},{28,24},{1,5},{5... | collective-permute-start | bytes 3145736 | tf_op jit(solution)/shard_map/ppermute | solution.py:579
  113.0 15.1 %collective-permute-start.18 = (f32[1,2,256,256]{3,2,1,0:T(8,128)}, f32[1,2,256,256]{3,2,1,0:T(8,128)S(1)}, u32[]{:S(2)}, u32[]{:S(2)}) collective-permute-start(f32[1,2,256,256]{3,2,1,0:T(8,128)} %collective-permute-done.13.refs_1_), channel_id=1, source_target_pairs={{0,16},{4,20},{8,24},{12,28},{16,0},{20,4},{24,8},{28,12},{1,17},{... | collective-permute-start | bytes 1572872 | tf_op jit(solution)/shard_map/ppermute | solution.py:413
  137.0 3.0 %collective-permute-start.19 = (f32[2,2,256,256]{3,2,1,0:T(8,128)S(1)}, f32[2,2,256,256]{3,2,1,0:T(8,128)S(1)}, u32[]{:S(2)}, u32[]{:S(2)}) collective-permute-start(f32[2,2,256,256]{3,2,1,0:T(8,128)S(1)} %get-tuple-element.131), channel_id=1, source_target_pairs={{0,4},{4,0},{8,12},{12,8},{16,20},{20,16},{24,28},{28,24},{1,5},{5... | collective-permute-start | bytes 3145736 | tf_op jit(solution)/shard_map/ppermute | solution.py:579
  (22 other events, 55.1 us)

commit v5 on v4

--- a/solution.py
+++ b/solution.py
@@ -181,18 +181,18 @@
         pairs.append((free_far.at[slab], free.at[slab]))
         pairs.append((coupling_far.at[slab], coupling.at[slab]))
     loads = copies(pairs, here)
-    links = []
+    links, stores = [], []
     for slab in range(count):
-        if slab <= count // 2:
-            for load in loads[2 * slab : 2 * slab + 2 if slab < count // 2 else None]:
-                load.wait()
+        for load in loads[2 * slab : 2 * slab + 2]:
+            load.wait()
         links.append(product(pair_of(free, slab), pair_of(coupling, slab)))
         put(link, links[-1], slab)
+        stores += copies([(link.at[slab], link_far.at[slab])], gone.at[slab : slab + 1])
     while len(links) > 1:
         paired = [product(b, a) for a, b in zip(links[0::2], links[1::2])]
         links = paired + links[len(paired) * 2 :]
     put(whole_map, links[0])
-    for store in copies([(link.at[slab], link_far.at[slab]) for slab in range(count)], gone):
+    for store in stores:
         store.wait()
 
 
@@ -203,31 +203,25 @@
     pairs = [(free_far.at[slab], free.at[slab]) for slab in range(count)]
     pairs += [(link_far.at[slab], link.at[slab]) for slab in range(1, count)]
     loads = copies(pairs, here)
-    state, stores = None, []
+    sources, stores = [], []
     for slab in range(count):
-        if slab <= 1:
-            for load in loads[slab : slab + 1 if slab == 0 else None]:
-                load.wait()
+        loads[slab].wait()
         row = potential_of(sums, slab, count, free.shape[-1])
-        now = source_of(pair_of(free, slab), row)
-        put(source, now, slab)
-        state = now if state is None else added(sandwich(pair_of(link, slab), state), now)
+        sources.append(source_of(pair_of(free, slab), row))
+        put(source, sources[-1], slab)
+        stores += copies([(source.at[slab], source_far.at[slab])], gone.at[slab : slab + 1])
+    for load in loads[count:]:
+        load.wait()
+    state = sources[0]
+    for slab in range(1, count):
+        state = added(sandwich(pair_of(link, slab), state), sources[slab])
     put(whole_source, state)
-    for store in copies([(source.at[slab], source_far.at[slab]) for slab in range(count)], gone):
+    for store in stores:
         store.wait()
 
 
-def hop_kernel(here, whole_map, whole_source, arrived, kept, out, kept_out):
-    state = []
-    for part in range(2):
-        before = jnp.zeros_like(arrived[part]) if kept is None else kept[part]
-        state.append(jnp.where(here[0] != 0, arrived[part], before))
-    put(kept_out, state)
-    put(out, added(sandwich(pair_of(whole_map), state), pair_of(whole_source)))
-
-
-def first_hop_kernel(here, whole_map, whole_source, arrived, out, kept_out):
-    hop_kernel(here, whole_map, whole_source, arrived, None, out, kept_out)
+def hop_kernel(whole_map, whole_source, carried, out):
+    put(out, added(sandwich(pair_of(whole_map), pair_of(carried)), pair_of(whole_source)))
 
 
 def beside_kernel(start, count, parts, *refs):
@@ -338,18 +332,21 @@
         first_pairs = [(e, e ^ 2) for e in everyone]
         second_pairs = [(2, 4), (3, 5), (4, 2), (5, 3)]
         relay_pairs = [(e, e ^ 4) for e in everyone]
+        around_pairs = [(2, 6), (3, 7), (4, 0), (5, 1)]
+        back_pairs = [(6, 4), (7, 5), (0, 2), (1, 3)]
         turned = (mine // 2) % 2
         has_second = jnp.where((mine >= 2) & (mine < 6), 1, 0)
     else:
         first_pairs = [(e, e - 2) for e in everyone if e >= 2]
         second_pairs = [(e, e + 2) for e in everyone if e + 2 < energies]
-        relay_pairs = second_pairs
+        relay_pairs = back_pairs = second_pairs
         turned = jnp.zeros_like(mine)
         has_second = jnp.ones_like(mine)
     twin_pairs = [(e, e ^ 1) for e in everyone]
 
     half = count // 2
-    free_first = [lax.ppermute(free[:1], "energy", first_pairs)]
+    cuts = [free[slab : slab + 1] for slab in range(count)]
+    free_first = [lax.ppermute(cuts[0], "energy", first_pairs)]
 
     place = lax.axis_index("slab")
     wire_up = [(i, i + 1) for i in range(peers - 1)]
@@ -370,7 +367,7 @@
     head = 5 * count * (width // depth)
     payload = call(
         functools.partial(gather_kernel, rows, energies),
-        16,
+        56,
         1,
         shape(head + 4 * cells, depth),
         jnp.reshape(mine, (1,)),
@@ -402,22 +399,20 @@
     )
     sums, ends_before, ends_after, (link, whole_map) = exchanged(payload, head, (link, whole_map))
 
-    arrived, free_then, field, perm, sums = lax.optimization_barrier(
-        (free_first[0], free, potential_old, permittivity, sums)
-    )
-    free_first = [arrived, lax.ppermute(free_then[1:2], "energy", first_pairs)]
-    free_second = [lax.ppermute(arrived if relayed else free_then[:1], "energy", relay_pairs)]
+    arrived, *cuts[1:], field, perm, sums = lax.optimization_barrier(
+        (free_first[0], *cuts[1:], potential_old, permittivity, sums)
+    )
+    free_first = [arrived, lax.ppermute(cuts[1], "energy", first_pairs)]
+    free_second = [lax.ppermute(arrived if relayed else cuts[0], "energy", relay_pairs)]
+    around = lax.ppermute(cuts[-1], "energy", around_pairs) if relayed else cuts[-1]
 
     def sent_on(part):
-        given = free_first[part] if relayed else free_then[part : part + 1]
+        given = free_first[part] if relayed else cuts[part]
         free_second.append(lax.ppermute(given, "energy", relay_pairs))
 
-    def sent_after(part, *others):
-        tied = lax.optimization_barrier((free_first[part - 1], free_then, *others))
-        free_first[part - 1] = tied[0]
-        cut = tied[1][part : part + 1]
+    def sent_after(part):
+        free_first[part - 1], cut = lax.optimization_barrier((free_first[part - 1], cuts[part]))
         free_first.append(lax.ppermute(cut, "energy", first_pairs))
-        return tied[2:]
 
     source, whole_source = call(
         source_kernel,
@@ -492,17 +487,16 @@
             out_specs=(block, one_state),
         )
 
-    leaving, kept = whole_source, None
+    leaving = whole_source
     beside_first, beside_second = [None, None], [None, None]
-    flag = pl.BlockSpec(memory_space=pltpu.SMEM)
     for hop in range(1, peers - 1):
-        arrived = lax.ppermute(leaving, "slab", swaps((hop - 1) % 2))
+        arrived = lax.ppermute(leaving, "slab", wire_up)
         if hop == 1:
             sent_on(1)
             sent_after(2)
-            arrived, potential_new, weights, free_first[1], free_second[0] = (
+            arrived, potential_new, weights, free_first[1], free_second[0], around = (
                 lax.optimization_barrier(
-                    (arrived, potential_new, weights, free_first[1], free_second[0])
+                    (arrived, potential_new, weights, free_first[1], free_second[0], around)
                 )
             )
         if hop == 2:
@@ -512,34 +506,22 @@
             arrived, beside_first[0], free_first[2], free_second[1] = lax.optimization_barrier(
                 (arrived, beside_first[0], free_first[2], free_second[1])
             )
-        here = jnp.reshape(place == hop, (1,)).astype(jnp.int32)
-        states = (arrived,) if kept is None else (arrived, kept)
-        leaving, kept = call(
-            first_hop_kernel if kept is None else hop_kernel,
-            12,
-            2,
-            (whole, whole),
-            here,
-            whole_map,
-            whole_source,
-            *states,
-            in_specs=[flag] + [near] * (2 + len(states)),
-            out_specs=(near, near),
-        )
+        leaving = call(hop_kernel, 12, 2, whole, whole_map, whole_source, arrived)
 
     def both(pairs):
         return [(a * peers + i, b * peers + j) for a, b in pairs for i, j in wire_up]
 
-    arrived = lax.ppermute(leaving, "slab", swaps((peers - 2) % 2))
+    carried = lax.ppermute(leaving, "slab", wire_up)
     carried_second = lax.ppermute(leaving, ("energy", "slab"), both(second_pairs))
     beside_second[0] = beside(0, free_second[:2])
-    sent_on(3)
     beside_first[1] = beside(1, free_first[2:])
-    arrived, beside_first[1], beside_second[0], free_second[2] = lax.optimization_barrier(
-        (arrived, beside_first[1], beside_second[0], free_second[2])
-    )
-    carried = jnp.where(place == peers - 1, arrived, kept)
+    free_first[3], around = lax.optimization_barrier((free_first[3], around))
+    free_second.append(lax.ppermute(around, "energy", back_pairs))
+    carried, beside_first[1], beside_second[0], free_second[2] = lax.optimization_barrier(
+        (carried, beside_first[1], beside_second[0], free_second[2])
+    )
     carried_first = lax.ppermute(carried, "energy", first_pairs)
+    carried, free_second[3] = lax.optimization_barrier((carried, free_second[3]))
     greens, _ = greens_of(56, link, source, carried)
     beside_second[1] = beside(1, free_second[2:])
     carried_second, greens = lax.optimization_barrier((carried_second, greens))

time: 144 us -> 129 us (0.90)
  local copies, waits for them, and re-layouts: 20.3 us -> 7.56 us
  starting transfers between devices: 24.1 us -> 30 us
  Pallas kernels: 48.9 us -> 44.9 us
  waiting for transfers between devices: 41 us -> 37.3 us
    unnamed x68 -> x58, local copies, waits for them, and re-layouts: 14 us -> 4.92 us
    ppermute x6 -> x8, starting transfers between devices: 5.77 us -> 14.6 us  [the longest x2 4.69 us: per_device(): arrived = lax.ppermute(leaving, 'slab', wire_up)]
    ppermute x3 -> x2, waiting for transfers between devices: 12.4 us -> 6.6 us  [sent_on(): free_second.append(lax.ppermute(given, 'energy', relay_pairs))]
    pallas_call x14, Pallas kernels: 48.9 us -> 44.9 us  [call(): pl.pallas_call(kernel, out_shape=out_shapes, cost_estimate=cost, compiler...]
    slice x4 -> x1, local copies, waits for them, and re-layouts: 6.14 us -> 2.49 us  [per_device(): cuts = [free[slab:slab + 1] for slab in range(count)]]
    ppermute x3 -> x2, starting transfers between devices: 4.18 us -> 1.1 us  [sent_on(): free_second.append(lax.ppermute(given, 'energy', relay_pairs))]
    ppermute x1, waiting for transfers between devices: 0.39 us -> 2.78 us  [per_device(): lax.ppermute(leaving, ('energy', 'slab'), both(second_pairs))]
    ppermute x1, waiting for transfers between devices: 8.63 us -> 6.25 us  [per_device(): carried_first = lax.ppermute(carried, 'energy', first_pairs)]
  transfers between devices with their start and end apart: 20 -> 21, of which waited for: 9 -> 9; matrix products, arithmetic and copies ran while one was open for 6% -> 4% of each run, Pallas kernels for 32% -> 33%
where the time goes in v5:
time: 129 us; the launch traced here: 126 us
  Pallas kernels  44.9 us (35%)
  waiting for transfers between devices  37.3 us (29%)
  starting transfers between devices  30 us (23%)
  local copies, waits for them, and re-layouts  7.56 us (6%)
  other arithmetic  5.38 us (4%)
    pallas_call x14, Pallas kernels, call(): pl.pallas_call(kernel, out_shape=out_shapes, cost_estimate=cost, compiler...  44.9 us
    ppermute x1, waiting for transfers between devices, per_device(): lax.ppermute(cuts[-1], 'energy', around_pairs)  6.71 us
    ppermute x2, waiting for transfers between devices, sent_on(): free_second.append(lax.ppermute(given, 'energy', relay_pairs))  6.6 us
    ppermute x2, waiting for transfers between devices, per_device(): arrived = lax.ppermute(leaving, 'slab', wire_up)  6.49 us
    ppermute x1, waiting for transfers between devices, per_device(): carried_first = lax.ppermute(carried, 'energy', first_pairs)  6.25 us
    ppermute x3, waiting for transfers between devices, exchanged(): lax.ppermute(payload, 'energy', [(e, e ^ mask) for e in range(peers)])  5.84 us
    unnamed x58, local copies, waits for them, and re-layouts  4.92 us
    ppermute x2, starting transfers between devices, per_device(): arrived = lax.ppermute(leaving, 'slab', wire_up)  4.69 us
  transfers between devices with their start and end apart: 21, of which 9 were waited for; matrix products, arithmetic and copies ran while one was open for 4% of the time, Pallas kernels for 33%

profile of v5, /device:TPU:13, one launch (start us, length us, event | category | flops | bytes accessed | tf_op | source)
XLA Modules:
  0.0 126.2 jit_solution(8877139452455132894)
XLA Ops:
  1.4 3.2 %collective-permute-start = (f32[2,1,4,128]{3,2,0,1:T(4,128)S(1)}, f32[2,1,4,128]{3,2,0,1:T(4,128)S(1)}, u32[]{:S(2)}, u32[]{:S(2)}) collective-permute-start(f32[2,1,4,128]{3,2,0,1:T(4,128)S(1)} %bitcast.69), channel_id=1, source_target_pairs={{1,2},{2,1},{5,6},{6,5},{9,10},{10,9},{13,14},{14,13},{17,18},{18,... | collective-permute-start | bytes 12296 | tf_op jit(solution)/shard_map/ppermute | solution.py:362
  4.7 2.5 %slice_bitcast_fusion = (f32[1,2,256,256]{3,2,1,0:T(8,128)}, f32[1,2,256,256]{3,2,1,0:T(8,128)S(1)}, f32[1,2,256,256]{3,2,1,0:T(8,128)S(1)}, f32[1,2,256,256]{3,2,1,0:T(8,128)S(1)}) fusion(f32[1,4,2,256,256]{4,3,2,1,0:T(8,128)} %param.14), kind=kLoop, calls=%fused_computation.2 | loop fusion | bytes 4194304 | tf_op jit(solution)/shard_map/slice | solution.py:348
  9.2 2.5 %shard_map.113 = f32[104,128]{1,0:T(8,128)} custom-call(s32[1]{0:T(128)} %bitcast.1.mine, f32[64,128]{1,0:T(8,128)} %bitcast.55, f32[64,128]{1,0:T(8,128)} %bitcast.53, f32[64,128]{1,0:T(8,128)} %bitcast.62, f32[2,4,128]{2,1,0:T(4,128)} %bitcast.67, f32[2,4,128]{2,1,0:T(4,128)} %bitcast.65, s32[4,256]{1,0:T(4,128)} %owner.1), custom_call_target="tpu_custom_call" | custom-call | flops 301989888 | bytes 163844 | tf_op jit(solution)/shard_map/pallas_call | solution.py:67
  12.9 5.5 %shard_map.114 = (f32[4,2,256,256]{3,2,1,0:T(8,128)}, f32[2,256,256]{2,1,0:T(8,128)}) custom-call(f32[4,2,256,256]{3,2,1,0:T(8,128)} %bitcast.50, f32[4,2,256,256]{3,2,1,0:T(8,128)} %refs_2_.7), custom_call_target="tpu_custom_call" | custom-call | flops 2113929216 | bytes 6815744 | tf_op jit(solution)/shard_map/pallas_call | solution.py:67
  19.6 2.5 %collective-permute-done.3 = f32[104,128]{1,0:T(8,128)S(1)} collective-permute-done((f32[104,128]{1,0:T(8,128)S(1)}, f32[104,128]{1,0:T(8,128)S(1)}, u32[]{:S(2)}, u32[]{:S(2)}) %collective-permute-start.3) | collective-permute-done | bytes 53280 | tf_op jit(solution)/shard_map/ppermute | solution.py:303
  23.5 3.3 %collective-permute-done.5 = f32[104,128]{1,0:T(8,128)S(1)} collective-permute-done((f32[104,128]{1,0:T(8,128)S(1)}, f32[104,128]{1,0:T(8,128)S(1)}, u32[]{:S(2)}, u32[]{:S(2)}) %collective-permute-start.5) | collective-permute-done | bytes 53280 | tf_op jit(solution)/shard_map/ppermute | solution.py:303
  29.1 3.9 %collective-permute-start.9 = (f32[1,2,256,256]{3,2,1,0:T(8,128)}, f32[1,2,256,256]{3,2,1,0:T(8,128)}, u32[]{:S(2)}, u32[]{:S(2)}) collective-permute-start(f32[1,2,256,256]{3,2,1,0:T(8,128)} %get-tuple-element.100), channel_id=1, source_target_pairs={{8,24},{12,28},{16,0},{20,4},{9,25},{13,29},{17,1},{21,5},{10,26},... | collective-permute-start | bytes 1572872 | tf_op jit(solution)/shard_map/ppermute | solution.py:407
  33.0 7.8 %shard_map.115 = (f32[4,2,256,256]{3,2,1,0:T(8,128)}, f32[2,256,256]{2,1,0:T(8,128)}) custom-call(f32[4,2,256,256]{3,2,1,0:T(8,128)} %bitcast.51, f32[4,2,256,256]{3,2,1,0:T(8,128)} %get-tuple-element.77.link_far.link, f32[104,128]{1,0:T(8,128)} %add_select_fusion.sums.refs_3_), custom_call_target="tpu_custom_call" | custom-call | flops 3019898880 | bytes 6868992 | tf_op jit(solution)/shard_map/pallas_call | solution.py:67
  40.9 2.3 %collective-permute-start.6 = (f32[2,256,256]{2,1,0:T(8,128)}, f32[2,256,256]{2,1,0:T(8,128)S(1)}, u32[]{:S(2)}, u32[]{:S(2)}) collective-permute-start(f32[2,256,256]{2,1,0:T(8,128)} %get-tuple-element.80.whole_source), channel_id=1, source_target_pairs={{0,1},{1,2},{2,3},{4,5},{5,6},{6,7},{8,9},{9,10},{10,11},{12,13},{... | collective-permute-start | bytes 1572872 | tf_op jit(solution)/shard_map/ppermute | solution.py:493
  44.3 6.7 %collective-permute-done.9 = f32[1,2,256,256]{3,2,1,0:T(8,128)} collective-permute-done((f32[1,2,256,256]{3,2,1,0:T(8,128)}, f32[1,2,256,256]{3,2,1,0:T(8,128)}, u32[]{:S(2)}, u32[]{:S(2)}) %collective-permute-start.9) | collective-permute-done | bytes 524320 | tf_op jit(solution)/shard_map/ppermute | solution.py:407
  51.0 4.5 %collective-permute-done.6.carried = f32[2,256,256]{2,1,0:T(8,128)S(1)} collective-permute-done((f32[2,256,256]{2,1,0:T(8,128)}, f32[2,256,256]{2,1,0:T(8,128)S(1)}, u32[]{:S(2)}, u32[]{:S(2)}) %collective-permute-start.6) | collective-permute-done | bytes 524320 | tf_op jit(solution)/shard_map/ppermute | solution.py:493
  57.5 2.4 %collective-permute-start.10 = (f32[2,256,256]{2,1,0:T(8,128)S(1)}, f32[2,256,256]{2,1,0:T(8,128)S(1)}, u32[]{:S(2)}, u32[]{:S(2)}) collective-permute-start(f32[2,256,256]{2,1,0:T(8,128)S(1)} %shard_map.116), channel_id=1, source_target_pairs={{0,1},{1,2},{2,3},{4,5},{5,6},{6,7},{8,9},{9,10},{10,11},{12,13},{... | collective-permute-start | bytes 1572872 | tf_op jit(solution)/shard_map/ppermute | solution.py:493
  60.6 1.6 %shard_map.117 = (f32[2,2,256,256]{3,2,1,0:T(8,128)S(1)}, f32[2,2,256,256]{3,2,1,0:T(8,128)S(1)}) custom-call(f32[1,2,256,256]{3,2,1,0:T(8,128)S(1)} %copy-done.9, f32[1,2,256,256]{3,2,1,0:T(8,128)S(1)} %collective-permute-done.7.refs_1_, f32[4,2,256,256]{3,2,1,0:T(8,128)S(1)} %copy-done.6, f32[104,128]{1,0:T(8,128)S(1)} %copy-done.5), custom_call_target="tpu_custom_call" | custom-call | flops 1207959552 | bytes 5296128 | tf_op jit(solution)/shard_map/pallas_call | solution.py:67
  62.2 6.6 %collective-permute-done.12.refs_1_ = f32[1,2,256,256]{3,2,1,0:T(8,128)S(1)} collective-permute-done((f32[1,2,256,256]{3,2,1,0:T(8,128)S(1)}, f32[1,2,256,256]{3,2,1,0:T(8,128)S(1)}, u32[]{:S(2)}, u32[]{:S(2)}) %collective-permute-start.12) | collective-permute-done | bytes 524320 | tf_op jit(solution)/shard_map/ppermute | solution.py:411
  68.8 2.0 %collective-permute-done.10.carried = f32[2,256,256]{2,1,0:T(8,128)S(1)} collective-permute-done((f32[2,256,256]{2,1,0:T(8,128)S(1)}, f32[2,256,256]{2,1,0:T(8,128)S(1)}, u32[]{:S(2)}, u32[]{:S(2)}) %collective-permute-start.10) | collective-permute-done | bytes 524320 | tf_op jit(solution)/shard_map/ppermute | solution.py:493
  70.8 1.7 %shard_map.118 = f32[2,256,256]{2,1,0:T(8,128)} custom-call(f32[2,256,256]{2,1,0:T(8,128)S(1)} %copy-done.14, f32[2,256,256]{2,1,0:T(8,128)S(1)} %copy-done.11, f32[2,256,256]{2,1,0:T(8,128)S(1)} %collective-permute-done.10.carried), custom_call_target="tpu_custom_call" | custom-call | flops 603979776 | bytes 2097152 | tf_op jit(solution)/shard_map/pallas_call | solution.py:67
  73.6 2.0 %collective-permute-start.13 = (f32[2,256,256]{2,1,0:T(8,128)}, f32[2,256,256]{2,1,0:T(8,128)}, u32[]{:S(2)}, u32[]{:S(2)}) collective-permute-start(f32[2,256,256]{2,1,0:T(8,128)} %shard_map.118), channel_id=1, source_target_pairs={{0,1},{1,2},{2,3},{4,5},{5,6},{6,7},{8,9},{9,10},{10,11},{12,13},{... | collective-permute-start | bytes 1572872 | tf_op jit(solution)/shard_map/ppermute | solution.py:514
  75.6 1.3 %collective-permute-start.18 = (f32[1,2,256,256]{3,2,1,0:T(8,128)}, f32[1,2,256,256]{3,2,1,0:T(8,128)}, u32[]{:S(2)}, u32[]{:S(2)}) collective-permute-start(f32[1,2,256,256]{3,2,1,0:T(8,128)} %collective-permute-done.9), channel_id=1, source_target_pairs={{24,16},{28,20},{0,8},{4,12},{25,17},{29,21},{1,9},{5,13},{26,18},... | collective-permute-start | bytes 1572872 | tf_op jit(solution)/shard_map/ppermute | solution.py:519
  76.9 4.2 %collective-permute-start.17 = (f32[2,256,256]{2,1,0:T(8,128)}, f32[2,256,256]{2,1,0:T(8,128)}, u32[]{:S(2)}, u32[]{:S(2)}) collective-permute-start(f32[2,256,256]{2,1,0:T(8,128)} %shard_map.118), channel_id=1, source_target_pairs={{8,17},{9,18},{10,19},{12,21},{13,22},{14,23},{16,9},{17,10},{18,1... | collective-permute-start | bytes 1572872 | tf_op jit(solution)/shard_map/ppermute | solution.py:515
  81.1 1.5 %shard_map.120 = (f32[2,2,256,256]{3,2,1,0:T(8,128)S(1)}, f32[2,2,256,256]{3,2,1,0:T(8,128)S(1)}) custom-call(f32[1,2,256,256]{3,2,1,0:T(8,128)S(1)} %collective-permute-done.8.refs_0_, f32[1,2,256,256]{3,2,1,0:T(8,128)S(1)} %collective-permute-done.12.refs_1_, f32[4,2,256,256]{3,2,1,0:T(8,128)S(1)} %copy-done.6, f32[104,128]{1,0:T(8,128)S(1)} %copy-done.5), custom_call_target="tpu_custom_call" | custom-call | flops 1207959552 | bytes 5296128 | tf_op jit(solution)/shard_map/pallas_call | solution.py:67
  83.6 1.5 %shard_map.119 = (f32[2,2,256,256]{3,2,1,0:T(8,128)S(1)}, f32[2,2,256,256]{3,2,1,0:T(8,128)S(1)}) custom-call(f32[1,2,256,256]{3,2,1,0:T(8,128)S(1)} %collective-permute-done.11.refs_0_, f32[1,2,256,256]{3,2,1,0:T(8,128)S(1)} %collective-permute-done.14.refs_1_, f32[4,2,256,256]{3,2,1,0:T(8,128)S(1)} %copy-done.6, f32[104,128]{1,0:T(8,128)S(1)} %copy-done.5), custom_call_target="tpu_custom_call" | custom-call | flops 1207959552 | bytes 5296128 | tf_op jit(solution)/shard_map/pallas_call | solution.py:67
  88.2 6.8 %shard_map.121 = (f32[4,2,256,256]{3,2,1,0:T(8,128)}, f32[2,256,256]{2,1,0:T(8,128)}) custom-call(f32[4,2,256,256]{3,2,1,0:T(8,128)} %get-tuple-element.77.link_far.link, f32[4,2,256,256]{3,2,1,0:T(8,128)} %get-tuple-element.110.source, f32[2,256,256]{2,1,0:T(8,128)} %collective-permute-done.13.carried), custom_call_target="tpu_custom_call" | custom-call | flops 2415919104 | bytes 7340032 | tf_op jit(solution)/shard_map/pallas_call | solution.py:67
  94.9 2.8 %collective-permute-done.17.carried = f32[2,256,256]{2,1,0:T(8,128)} collective-permute-done((f32[2,256,256]{2,1,0:T(8,128)}, f32[2,256,256]{2,1,0:T(8,128)}, u32[]{:S(2)}, u32[]{:S(2)}) %collective-permute-start.17) | collective-permute-done | bytes 524320 | tf_op jit(solution)/shard_map/ppermute | solution.py:515
  97.7 3.1 %shard_map.122 = (f32[2,2,256,256]{3,2,1,0:T(8,128)S(1)}, f32[2,256,256]{2,1,0:T(8,128)S(1)}) custom-call(f32[2,2,256,256]{3,2,1,0:T(8,128)S(1)} %copy-done.16, f32[2,2,256,256]{3,2,1,0:T(8,128)S(1)} %copy-done.18, f32[2,256,256]{2,1,0:T(8,128)} %collective-permute-done.17.carried), custom_call_target="tpu_custom_call" | custom-call | flops 1207959552 | bytes 4194304 | tf_op jit(solution)/shard_map/pallas_call | solution.py:67
  100.8 6.3 %collective-permute-done.16.carried = f32[2,256,256]{2,1,0:T(8,128)} collective-permute-done((f32[2,256,256]{2,1,0:T(8,128)}, f32[2,256,256]{2,1,0:T(8,128)}, u32[]{:S(2)}, u32[]{:S(2)}) %collective-permute-start.16) | collective-permute-done | bytes 524320 | tf_op jit(solution)/shard_map/ppermute | solution.py:523
  107.1 3.4 %shard_map.123 = (f32[2,2,256,256]{3,2,1,0:T(8,128)S(1)}, f32[2,2,256,256]{3,2,1,0:T(8,128)S(1)}, f32[2,256,256]{2,1,0:T(8,128)S(1)}) custom-call(s32[2]{0:T(128)S(1)} %pad_add_fusion.pick, f32[2,2,256,256]{3,2,1,0:T(8,128)S(1)} %get-tuple-element.96.link, f32[2,2,256,256]{3,2,1,0:T(8,128)S(1)} %get-tuple-element.97.source, ...), custom_call_target="tpu_custom_call" | custom-call | flops 1207959552 | bytes 9437192 | tf_op jit(solution)/shard_map/pallas_call | solution.py:67
  110.4 2.6 %collective-permute-start.19 = (f32[2,2,256,256]{3,2,1,0:T(8,128)S(1)}, f32[2,2,256,256]{3,2,1,0:T(8,128)S(1)}, u32[]{:S(2)}, u32[]{:S(2)}) collective-permute-start(f32[2,2,256,256]{3,2,1,0:T(8,128)S(1)} %get-tuple-element.122), channel_id=1, source_target_pairs={{0,4},{4,0},{8,12},{12,8},{16,20},{20,16},{24,28},{28,24},{1,5},{5... | collective-permute-start | bytes 3145736 | tf_op jit(solution)/shard_map/ppermute | solution.py:561
  113.0 2.6 %shard_map.124 = (f32[2,2,256,256]{3,2,1,0:T(8,128)S(1)}, f32[2,2,256,256]{3,2,1,0:T(8,128)S(1)}) custom-call(f32[1,2,256,256]{3,2,1,0:T(8,128)S(1)} %copy-done.13, f32[1,2,256,256]{3,2,1,0:T(8,128)} %collective-permute-done.18.refs_1_, f32[4,2,256,256]{3,2,1,0:T(8,128)S(1)} %copy-done.7, f32[104,128]{1,0:T(8,128)S(1)} %copy-done.5), custom_call_target="tpu_custom_call" | custom-call | flops 1207959552 | bytes 5296128 | tf_op jit(solution)/shard_map/pallas_call | solution.py:67
  115.6 2.6 %shard_map.125 = (f32[2,2,256,256]{3,2,1,0:T(8,128)S(1)}, f32[2,256,256]{2,1,0:T(8,128)}) custom-call(f32[2,2,256,256]{3,2,1,0:T(8,128)S(1)} %get-tuple-element.128.link, f32[2,2,256,256]{3,2,1,0:T(8,128)S(1)} %get-tuple-element.129.source, f32[2,256,256]{2,1,0:T(8,128)S(1)} %get-tuple-element.130.carried), custom_call_target="tpu_custom_call" | custom-call | flops 1207959552 | bytes 4194304 | tf_op jit(solution)/shard_map/pallas_call | solution.py:67
  118.3 3.5 %shard_map.126 = (f32[2,2,256,256]{3,2,1,0:T(8,128)S(1)}, f32[2,2,256,256]{3,2,1,0:T(8,128)S(1)}, f32[2,256,256]{2,1,0:T(8,128)}) custom-call(s32[2]{0:T(128)S(1)} %pad_add_fusion.pick, f32[2,2,256,256]{3,2,1,0:T(8,128)S(1)} %copy-done.2, f32[2,2,256,256]{3,2,1,0:T(8,128)S(1)} %copy-done.4, f32[2,256,256]{2,1,0:T(8,128)S(1)} %get-tuple-element.125.carried, ...), custom_call_target="tpu_custom_call" | custom-call | flops 1207959552 | bytes 9437192 | tf_op jit(solution)/shard_map/pallas_call | solution.py:67
  122.0 2.6 %collective-permute-done.20 = f32[2,2,256,256]{3,2,1,0:T(8,128)S(1)} collective-permute-done((f32[2,2,256,256]{3,2,1,0:T(8,128)S(1)}, f32[2,2,256,256]{3,2,1,0:T(8,128)S(1)}, u32[]{:S(2)}, u32[]{:S(2)}) %collective-permute-start.20) | collective-permute-done | bytes 1048608 | tf_op jit(solution)/shard_map/ppermute | solution.py:561
  124.8 1.5 %maximum_bitcast_fusion = f32[1,4,2,256,256]{4,3,2,1,0:T(8,128)} fusion(f32[2,2,256,256]{3,2,1,0:T(8,128)S(1)} %add.136, f32[2,2,256,256]{3,2,1,0:T(8,128)S(1)} %add.135), kind=kLoop, calls=%fused_computation.1 | loop fusion | flops 524288 | bytes 4194304 | tf_op jit(solution)/shard_map/broadcast_in_dim | solution.py:562
  (105 shorter events, 17.9 us)
Async XLA Ops:
  1.4 7.2 %collective-permute-start = (f32[2,1,4,128]{3,2,0,1:T(4,128)S(1)}, f32[2,1,4,128]{3,2,0,1:T(4,128)S(1)}, u32[]{:S(2)}, u32[]{:S(2)}) collective-permute-start(f32[2,1,4,128]{3,2,0,1:T(4,128)S(1)} %bitcast.69), channel_id=1, source_target_pairs={{1,2},{2,1},{5,6},{6,5},{9,10},{10,9},{13,14},{14,13},{17,18},{18,... | collective-permute-start | bytes 12296 | tf_op jit(solution)/shard_map/ppermute | solution.py:362
  4.6 4.0 %collective-permute-start.1 = (f32[2,1,4,128]{3,2,0,1:T(4,128)S(1)}, f32[2,1,4,128]{3,2,0,1:T(4,128)S(1)}, u32[]{:S(2)}, u32[]{:S(2)}) collective-permute-start(f32[2,1,4,128]{3,2,0,1:T(4,128)S(1)} %get-tuple-element.136), channel_id=1, source_target_pairs={{0,1},{2,3},{1,0},{3,2},{4,5},{6,7},{5,4},{7,6},{8,9},{10,11},{9,8... | collective-permute-start | bytes 12296 | tf_op jit(solution)/shard_map/ppermute | solution.py:361
  7.2 20.3 %collective-permute-start.4 = (f32[1,2,256,256]{3,2,1,0:T(8,128)S(1)}, f32[1,2,256,256]{3,2,1,0:T(8,128)S(1)}, u32[]{:S(2)}, u32[]{:S(2)}) collective-permute-start(f32[1,2,256,256]{3,2,1,0:T(8,128)S(1)} %get-tuple-element.141), channel_id=1, source_target_pairs={{0,8},{4,12},{8,0},{12,4},{16,24},{20,28},{24,16},{28,20},{1,9},{5... | collective-permute-start | bytes 1572872 | tf_op jit(solution)/shard_map/ppermute | solution.py:349
  11.7 6.7 %collective-permute-start.2 = (f32[104,128]{1,0:T(8,128)}, f32[104,128]{1,0:T(8,128)S(1)}, u32[]{:S(2)}, u32[]{:S(2)}) collective-permute-start(f32[104,128]{1,0:T(8,128)} %shard_map.113), channel_id=1, source_target_pairs={{0,4},{4,0},{8,12},{12,8},{16,20},{20,16},{24,28},{28,24},{1,5},{5... | collective-permute-start | bytes 159752 | tf_op jit(solution)/shard_map/ppermute | solution.py:303
  18.5 3.6 %collective-permute-start.3 = (f32[104,128]{1,0:T(8,128)S(1)}, f32[104,128]{1,0:T(8,128)S(1)}, u32[]{:S(2)}, u32[]{:S(2)}) collective-permute-start(f32[104,128]{1,0:T(8,128)S(1)} %add_select_fusion.2), channel_id=1, source_target_pairs={{0,12},{4,8},{8,4},{12,0},{16,28},{20,24},{24,20},{28,16},{1,13},{... | collective-permute-start | bytes 159752 | tf_op jit(solution)/shard_map/ppermute | solution.py:303
  22.3 4.5 %collective-permute-start.5 = (f32[104,128]{1,0:T(8,128)S(1)}, f32[104,128]{1,0:T(8,128)S(1)}, u32[]{:S(2)}, u32[]{:S(2)}) collective-permute-start(f32[104,128]{1,0:T(8,128)S(1)} %add_select_fusion.1), channel_id=1, source_target_pairs={{0,28},{4,24},{8,20},{12,16},{16,12},{20,8},{24,4},{28,0},{1,29},{... | collective-permute-start | bytes 159752 | tf_op jit(solution)/shard_map/ppermute | solution.py:303
  27.5 13.3 %copy-start.8 = (f32[1,2,256,256]{3,2,1,0:T(8,128)}, f32[1,2,256,256]{3,2,1,0:T(8,128)S(1)}, u32[]{:S(2)}) copy-start(f32[1,2,256,256]{3,2,1,0:T(8,128)S(1)} %collective-permute-done.4.refs_0_) | copy-start | bytes 1572868
  27.5 15.7 %copy-start.19 = (f32[16,4,128]{2,1,0:T(4,128)S(1)}, f32[16,4,128]{2,1,0:T(4,128)}, u32[]{:S(2)}) copy-start(f32[16,4,128]{2,1,0:T(4,128)} %param.12) | copy-start | bytes 98308
  27.5 15.7 %copy-start.20 = (f32[16,4,128]{2,1,0:T(4,128)S(1)}, f32[16,4,128]{2,1,0:T(4,128)}, u32[]{:S(2)}) copy-start(f32[16,4,128]{2,1,0:T(4,128)} %param.10) | copy-start | bytes 98308
  27.6 16.0 %copy-start.23 = (f32[16,4,128]{2,1,0:T(4,128)S(1)}, f32[16,4,128]{2,1,0:T(4,128)}, u32[]{:S(2)}) copy-start(f32[16,4,128]{2,1,0:T(4,128)} %param.11) | copy-start | bytes 98308
  27.6 27.9 %copy-start.14 = (f32[2,256,256]{2,1,0:T(8,128)S(1)}, f32[2,256,256]{2,1,0:T(8,128)}, u32[]{:S(2)}) copy-start(f32[2,256,256]{2,1,0:T(8,128)} %get-tuple-element.89.whole_map) | copy-start | bytes 1572868
  27.6 15.8 %collective-permute-start.7 = (f32[1,2,256,256]{3,2,1,0:T(8,128)S(1)}, f32[1,2,256,256]{3,2,1,0:T(8,128)S(1)}, u32[]{:S(2)}, u32[]{:S(2)}) collective-permute-start(f32[1,2,256,256]{3,2,1,0:T(8,128)S(1)} %get-tuple-element.83), channel_id=1, source_target_pairs={{0,8},{4,12},{8,0},{12,4},{16,24},{20,28},{24,16},{28,20},{1,9},{5... | collective-permute-start | bytes 1572872 | tf_op jit(solution)/shard_map/ppermute | solution.py:405
  28.9 15.4 %collective-permute-start.8 = (f32[1,2,256,256]{3,2,1,0:T(8,128)S(1)}, f32[1,2,256,256]{3,2,1,0:T(8,128)S(1)}, u32[]{:S(2)}, u32[]{:S(2)}) collective-permute-start(f32[1,2,256,256]{3,2,1,0:T(8,128)S(1)} %collective-permute-done.4.refs_0_), channel_id=1, source_target_pairs={{0,16},{4,20},{8,24},{12,28},{16,0},{20,4},{24,8},{28,12},{1,17},{... | collective-permute-start | bytes 1572872 | tf_op jit(solution)/shard_map/ppermute | solution.py:406
  29.1 21.9 %collective-permute-start.9 = (f32[1,2,256,256]{3,2,1,0:T(8,128)}, f32[1,2,256,256]{3,2,1,0:T(8,128)}, u32[]{:S(2)}, u32[]{:S(2)}) collective-permute-start(f32[1,2,256,256]{3,2,1,0:T(8,128)} %get-tuple-element.100), channel_id=1, source_target_pairs={{8,24},{12,28},{16,0},{20,4},{9,25},{13,29},{17,1},{21,5},{10,26},... | collective-permute-start | bytes 1572872 | tf_op jit(solution)/shard_map/ppermute | solution.py:407
  40.9 19.7 %copy-start.5 = (f32[104,128]{1,0:T(8,128)S(1)}, f32[104,128]{1,0:T(8,128)}, u32[]{:S(2)}) copy-start(f32[104,128]{1,0:T(8,128)} %add_select_fusion.sums.refs_3_) | copy-start | bytes 159748
  40.9 19.7 %copy-start.6 = (f32[4,2,256,256]{3,2,1,0:T(8,128)S(1)}, f32[4,2,256,256]{3,2,1,0:T(8,128)}, u32[]{:S(2)}) copy-start(f32[4,2,256,256]{3,2,1,0:T(8,128)} %refs_2_.7) | copy-start | bytes 6291460
  40.9 19.7 %copy-start.9 = (f32[1,2,256,256]{3,2,1,0:T(8,128)S(1)}, f32[1,2,256,256]{3,2,1,0:T(8,128)}, u32[]{:S(2)}) copy-start(f32[1,2,256,256]{3,2,1,0:T(8,128)} %copy-done.8) | copy-start | bytes 1572868
  40.9 14.6 %collective-permute-start.6 = (f32[2,256,256]{2,1,0:T(8,128)}, f32[2,256,256]{2,1,0:T(8,128)S(1)}, u32[]{:S(2)}, u32[]{:S(2)}) collective-permute-start(f32[2,256,256]{2,1,0:T(8,128)} %get-tuple-element.80.whole_source), channel_id=1, source_target_pairs={{0,1},{1,2},{2,3},{4,5},{5,6},{6,7},{8,9},{9,10},{10,11},{12,13},{... | collective-permute-start | bytes 1572872 | tf_op jit(solution)/shard_map/ppermute | solution.py:493
  43.4 16.5 %collective-permute-start.11 = (f32[1,2,256,256]{3,2,1,0:T(8,128)S(1)}, f32[1,2,256,256]{3,2,1,0:T(8,128)S(1)}, u32[]{:S(2)}, u32[]{:S(2)}) collective-permute-start(f32[1,2,256,256]{3,2,1,0:T(8,128)S(1)} %get-tuple-element.94), channel_id=1, source_target_pairs={{0,8},{4,12},{8,0},{12,4},{16,24},{20,28},{24,16},{28,20},{1,9},{5... | collective-permute-start | bytes 1572872 | tf_op jit(solution)/shard_map/ppermute | solution.py:415
  57.4 13.4 %copy-start.11 = (f32[2,256,256]{2,1,0:T(8,128)S(1)}, f32[2,256,256]{2,1,0:T(8,128)}, u32[]{:S(2)}) copy-start(f32[2,256,256]{2,1,0:T(8,128)} %get-tuple-element.80.whole_source) | copy-start | bytes 1572868
  57.4 11.3 %collective-permute-start.12 = (f32[1,2,256,256]{3,2,1,0:T(8,128)S(1)}, f32[1,2,256,256]{3,2,1,0:T(8,128)S(1)}, u32[]{:S(2)}, u32[]{:S(2)}) collective-permute-start(f32[1,2,256,256]{3,2,1,0:T(8,128)S(1)} %collective-permute-done.7.refs_1_), channel_id=1, source_target_pairs={{0,16},{4,20},{8,24},{12,28},{16,0},{20,4},{24,8},{28,12},{1,17},{... | collective-permute-start | bytes 1572872 | tf_op jit(solution)/shard_map/ppermute | solution.py:411
  57.5 13.3 %collective-permute-start.10 = (f32[2,256,256]{2,1,0:T(8,128)S(1)}, f32[2,256,256]{2,1,0:T(8,128)S(1)}, u32[]{:S(2)}, u32[]{:S(2)}) collective-permute-start(f32[2,256,256]{2,1,0:T(8,128)S(1)} %shard_map.116), channel_id=1, source_target_pairs={{0,1},{1,2},{2,3},{4,5},{5,6},{6,7},{8,9},{9,10},{10,11},{12,13},{... | collective-permute-start | bytes 1572872 | tf_op jit(solution)/shard_map/ppermute | solution.py:493
  59.9 15.7 %collective-permute-start.14 = (f32[1,2,256,256]{3,2,1,0:T(8,128)}, f32[1,2,256,256]{3,2,1,0:T(8,128)S(1)}, u32[]{:S(2)}, u32[]{:S(2)}) collective-permute-start(f32[1,2,256,256]{3,2,1,0:T(8,128)} %get-tuple-element.100), channel_id=1, source_target_pairs={{0,8},{4,12},{8,0},{12,4},{16,24},{20,28},{24,16},{28,20},{1,9},{5... | collective-permute-start | bytes 1572872 | tf_op jit(solution)/shard_map/ppermute | solution.py:415
  72.5 14.6 %collective-permute-start.15 = (f32[1,2,256,256]{3,2,1,0:T(8,128)S(1)}, f32[1,2,256,256]{3,2,1,0:T(8,128)S(1)}, u32[]{:S(2)}, u32[]{:S(2)}) collective-permute-start(f32[1,2,256,256]{3,2,1,0:T(8,128)S(1)} %collective-permute-done.11.refs_0_), channel_id=1, source_target_pairs={{0,16},{4,20},{8,24},{12,28},{16,0},{20,4},{24,8},{28,12},{1,17},{... | collective-permute-start | bytes 1572872 | tf_op jit(solution)/shard_map/ppermute | solution.py:411
  73.6 14.4 %collective-permute-start.13 = (f32[2,256,256]{2,1,0:T(8,128)}, f32[2,256,256]{2,1,0:T(8,128)}, u32[]{:S(2)}, u32[]{:S(2)}) collective-permute-start(f32[2,256,256]{2,1,0:T(8,128)} %shard_map.118), channel_id=1, source_target_pairs={{0,1},{1,2},{2,3},{4,5},{5,6},{6,7},{8,9},{9,10},{10,11},{12,13},{... | collective-permute-start | bytes 1572872 | tf_op jit(solution)/shard_map/ppermute | solution.py:514
  75.6 12.6 %collective-permute-start.18 = (f32[1,2,256,256]{3,2,1,0:T(8,128)}, f32[1,2,256,256]{3,2,1,0:T(8,128)}, u32[]{:S(2)}, u32[]{:S(2)}) collective-permute-start(f32[1,2,256,256]{3,2,1,0:T(8,128)} %collective-permute-done.9), channel_id=1, source_target_pairs={{24,16},{28,20},{0,8},{4,12},{25,17},{29,21},{1,9},{5,13},{26,18},... | collective-permute-start | bytes 1572872 | tf_op jit(solution)/shard_map/ppermute | solution.py:519
  76.9 20.8 %collective-permute-start.17 = (f32[2,256,256]{2,1,0:T(8,128)}, f32[2,256,256]{2,1,0:T(8,128)}, u32[]{:S(2)}, u32[]{:S(2)}) collective-permute-start(f32[2,256,256]{2,1,0:T(8,128)} %shard_map.118), channel_id=1, source_target_pairs={{8,17},{9,18},{10,19},{12,21},{13,22},{14,23},{16,9},{17,10},{18,1... | collective-permute-start | bytes 1572872 | tf_op jit(solution)/shard_map/ppermute | solution.py:515
  88.0 19.1 %collective-permute-start.16 = (f32[2,256,256]{2,1,0:T(8,128)}, f32[2,256,256]{2,1,0:T(8,128)}, u32[]{:S(2)}, u32[]{:S(2)}) collective-permute-start(f32[2,256,256]{2,1,0:T(8,128)} %collective-permute-done.13.carried), channel_id=1, source_target_pairs={{0,8},{4,12},{8,0},{12,4},{16,24},{20,28},{24,16},{28,20},{1,9},{5... | collective-permute-start | bytes 1572872 | tf_op jit(solution)/shard_map/ppermute | solution.py:523
  88.2 9.5 %copy-start.16 = (f32[2,2,256,256]{3,2,1,0:T(8,128)S(1)}, f32[2,2,256,256]{3,2,1,0:T(8,128)}, u32[]{:S(2)}) copy-start(f32[2,2,256,256]{3,2,1,0:T(8,128)} %copy-done.15) | copy-start | bytes 3145732
  88.2 9.5 %copy-start.18 = (f32[2,2,256,256]{3,2,1,0:T(8,128)S(1)}, f32[2,2,256,256]{3,2,1,0:T(8,128)}, u32[]{:S(2)}) copy-start(f32[2,2,256,256]{3,2,1,0:T(8,128)} %copy-done.17) | copy-start | bytes 3145732
  110.4 11.3 %collective-permute-start.19 = (f32[2,2,256,256]{3,2,1,0:T(8,128)S(1)}, f32[2,2,256,256]{3,2,1,0:T(8,128)S(1)}, u32[]{:S(2)}, u32[]{:S(2)}) collective-permute-start(f32[2,2,256,256]{3,2,1,0:T(8,128)S(1)} %get-tuple-element.122), channel_id=1, source_target_pairs={{0,4},{4,0},{8,12},{12,8},{16,20},{20,16},{24,28},{28,24},{1,5},{5... | collective-permute-start | bytes 3145736 | tf_op jit(solution)/shard_map/ppermute | solution.py:561
  121.9 2.7 %collective-permute-start.20 = (f32[2,2,256,256]{3,2,1,0:T(8,128)S(1)}, f32[2,2,256,256]{3,2,1,0:T(8,128)S(1)}, u32[]{:S(2)}, u32[]{:S(2)}) collective-permute-start(f32[2,2,256,256]{3,2,1,0:T(8,128)S(1)} %get-tuple-element.135), channel_id=1, source_target_pairs={{0,4},{4,0},{8,12},{12,8},{16,20},{20,16},{24,28},{28,24},{1,5},{5... | collective-permute-start | bytes 3145736 | tf_op jit(solution)/shard_map/ppermute | solution.py:561
  (18 other events, 69.1 us)

commit v6 on v5

--- a/solution.py
+++ b/solution.py
@@ -167,57 +167,19 @@
     return added(block, product(scaled, block))
 
 
-def copies(pairs, sems):
-    made = [pltpu.make_async_copy(a, b, sems.at[i]) for i, (a, b) in enumerate(pairs)]
-    for copy in made:
-        copy.start()
-    return made
-
-
-def linkage_kernel(free_far, coupling_far, link_far, whole_map, free, coupling, link, here, gone):
+def own_kernel(free, coupling, sums, whole_map, whole_source):
     count = free.shape[0]
-    pairs = []
+    links, state = [], None
     for slab in range(count):
-        pairs.append((free_far.at[slab], free.at[slab]))
-        pairs.append((coupling_far.at[slab], coupling.at[slab]))
-    loads = copies(pairs, here)
-    links, stores = [], []
-    for slab in range(count):
-        for load in loads[2 * slab : 2 * slab + 2]:
-            load.wait()
-        links.append(product(pair_of(free, slab), pair_of(coupling, slab)))
-        put(link, links[-1], slab)
-        stores += copies([(link.at[slab], link_far.at[slab])], gone.at[slab : slab + 1])
+        block = pair_of(free, slab)
+        links.append(product(block, pair_of(coupling, slab)))
+        source = source_of(block, potential_of(sums, slab, count, free.shape[-1]))
+        state = source if state is None else added(sandwich(links[slab], state), source)
+    put(whole_source, state)
     while len(links) > 1:
         paired = [product(b, a) for a, b in zip(links[0::2], links[1::2])]
         links = paired + links[len(paired) * 2 :]
     put(whole_map, links[0])
-    for store in stores:
-        store.wait()
-
-
-def source_kernel(
-    free_far, link_far, sums, source_far, whole_source, free, link, source, here, gone
-):
-    count = free.shape[0]
-    pairs = [(free_far.at[slab], free.at[slab]) for slab in range(count)]
-    pairs += [(link_far.at[slab], link.at[slab]) for slab in range(1, count)]
-    loads = copies(pairs, here)
-    sources, stores = [], []
-    for slab in range(count):
-        loads[slab].wait()
-        row = potential_of(sums, slab, count, free.shape[-1])
-        sources.append(source_of(pair_of(free, slab), row))
-        put(source, sources[-1], slab)
-        stores += copies([(source.at[slab], source_far.at[slab])], gone.at[slab : slab + 1])
-    for load in loads[count:]:
-        load.wait()
-    state = sources[0]
-    for slab in range(1, count):
-        state = added(sandwich(pair_of(link, slab), state), sources[slab])
-    put(whole_source, state)
-    for store in stores:
-        store.wait()
 
 
 def hop_kernel(whole_map, whole_source, carried, out):
@@ -242,6 +204,19 @@
         state[...] = carried[...]
 
     now = added(sandwich(pair_of(link, 0), pair_of(state)), pair_of(source, 0))
+    put(state, now)
+    put(greens, now, 0)
+
+
+def own_greens_kernel(count, free, coupling, sums, carried, greens, state):
+    @pl.when(pl.program_id(0) == 0)
+    def _():
+        state[...] = carried[...]
+
+    block = pair_of(free, 0)
+    link = product(block, pair_of(coupling, 0))
+    row = potential_of(sums, pl.program_id(0), count, free.shape[-1])
+    now = added(sandwich(link, pair_of(state)), source_of(block, row))
     put(state, now)
     put(greens, now, 0)
 
@@ -290,7 +265,7 @@
     )
 
 
-def exchanged(payload, head, beside):
+def exchanged(payload, head, early):
     peers, mine = lax.axis_size("energy"), lax.axis_index("energy")
     assert peers & (peers - 1) == 0
     rest = payload[head:]
@@ -298,14 +273,14 @@
     is_head = lax.broadcasted_iota(jnp.int32, payload.shape, 0) < head
     mask = 1
     while mask < peers:
-        if mask * 2 > peers // 2:
-            payload, beside = lax.optimization_barrier((payload, beside))
+        if mask > 1:
+            payload, early = lax.optimization_barrier((payload, early))
         arrived = lax.ppermute(payload, "energy", [(e, e ^ mask) for e in range(peers)])
         before = jnp.where((mine ^ mask) == mine - 1, arrived[head:], before)
         after = jnp.where((mine ^ mask) == mine + 1, arrived[head:], after)
         payload = jnp.where(is_head, payload + arrived, payload)
         mask = 2 * mask + 1
-    return payload, before, after, beside
+    return payload, before, after, early
 
 
 def per_device(
@@ -355,7 +330,9 @@
         pairs = [(i, i + 1) for i in range(start, peers - 1, 2)]
         return pairs + [(j, i) for i, j in pairs]
 
-    stacked = jnp.stack([potential_old, permittivity])
+    cuts[0], stacked = lax.optimization_barrier(
+        (cuts[0], jnp.stack([potential_old, permittivity]))
+    )
     lower, upper = end_planes(stacked, 1)
     even = place % 2 == 0
     arrived = lax.ppermute(jnp.where(even, upper, lower), "slab", swaps(0))
@@ -378,26 +355,7 @@
         in_specs=[pl.BlockSpec(memory_space=pltpu.SMEM)]
         + [pl.BlockSpec(memory_space=pltpu.VMEM)] * 6,
     )
-    payload, *at_gather = lax.optimization_barrier((payload, free, coupling))
-    far, near = pl.BlockSpec(memory_space=pl.ANY), pl.BlockSpec(memory_space=pltpu.VMEM)
-    held = pltpu.VMEM((count, 2, width, width), jnp.float32)
-    link, whole_map = call(
-        linkage_kernel,
-        56,
-        2 * count - 1,
-        (blocks, whole),
-        *at_gather,
-        in_specs=[far, far],
-        out_specs=(far, near),
-        scratch_shapes=[
-            held,
-            held,
-            held,
-            pltpu.SemaphoreType.DMA((2 * count,)),
-            pltpu.SemaphoreType.DMA((count,)),
-        ],
-    )
-    sums, ends_before, ends_after, (link, whole_map) = exchanged(payload, head, (link, whole_map))
+    sums, ends_before, ends_after, free_first[0] = exchanged(payload, head, free_first[0])
 
     arrived, *cuts[1:], field, perm, sums = lax.optimization_barrier(
         (free_first[0], *cuts[1:], potential_old, permittivity, sums)
@@ -414,23 +372,14 @@
         free_first[part - 1], cut = lax.optimization_barrier((free_first[part - 1], cuts[part]))
         free_first.append(lax.ppermute(cut, "energy", first_pairs))
 
-    source, whole_source = call(
-        source_kernel,
-        56,
-        3 * count - 2,
-        (blocks, whole),
+    whole_map, whole_source = call(
+        own_kernel,
+        32,
+        5 * count - 3,
+        (whole, whole),
         free,
-        link,
+        coupling,
         sums,
-        in_specs=[far, far, near],
-        out_specs=(far, near),
-        scratch_shapes=[
-            held,
-            held,
-            held,
-            pltpu.SemaphoreType.DMA((2 * count - 1,)),
-            pltpu.SemaphoreType.DMA((count,)),
-        ],
     )
 
     ends_before = ends_before.reshape(2, 2, cells, 1, depth)
@@ -494,17 +443,17 @@
         if hop == 1:
             sent_on(1)
             sent_after(2)
-            arrived, potential_new, weights, free_first[1], free_second[0], around = (
-                lax.optimization_barrier(
-                    (arrived, potential_new, weights, free_first[1], free_second[0], around)
-                )
+            arrived, potential_new, weights, free_first[1] = lax.optimization_barrier(
+                (arrived, potential_new, weights, free_first[1])
             )
         if hop == 2:
             sent_on(2)
             sent_after(3)
             beside_first[0] = beside(0, free_first[:2])
-            arrived, beside_first[0], free_first[2], free_second[1] = lax.optimization_barrier(
-                (arrived, beside_first[0], free_first[2], free_second[1])
+            arrived, beside_first[0], free_first[2], free_second[0], around = (
+                lax.optimization_barrier(
+                    (arrived, beside_first[0], free_first[2], free_second[0], around)
+                )
             )
         leaving = call(hop_kernel, 12, 2, whole, whole_map, whole_source, arrived)
 
@@ -522,14 +471,26 @@
     )
     carried_first = lax.ppermute(carried, "energy", first_pairs)
     carried, free_second[3] = lax.optimization_barrier((carried, free_second[3]))
-    greens, _ = greens_of(56, link, source, carried)
+    greens, _ = call(
+        functools.partial(own_greens_kernel, count),
+        24,
+        4 * count,
+        (blocks, whole),
+        free,
+        coupling,
+        sums,
+        carried,
+        grid=(count,),
+        in_specs=[block, block, pl.BlockSpec(sums.shape, lambda s: (0, 0)), one_state],
+        out_specs=(block, one_state),
+    )
     beside_second[1] = beside(1, free_second[2:])
     carried_second, greens = lax.optimization_barrier((carried_second, greens))
     greens_second = []
     for part in beside_second:
         made, carried_second = greens_of(16, *part, carried_second)
         greens_second.append(made)
-    carried_first, greens_second[0] = lax.optimization_barrier((carried_first, greens_second[0]))
+    carried_first, greens_second = lax.optimization_barrier((carried_first, greens_second))
 
     outputs = []
     for index, part in enumerate(beside_first):

time: 129 us -> 130 us (level)
  starting transfers between devices: 30 us -> 42.4 us
  waiting for transfers between devices: 37.3 us -> 26.1 us
  local copies, waits for them, and re-layouts: 7.56 us -> 11.7 us
  Pallas kernels: 44.9 us -> 40.9 us
    ppermute x2, starting transfers between devices: 2.69 us -> 11 us  [per_device(): outputs.append(here + lax.ppermute(there, 'energy', twin_pairs))]
    ppermute x1, waiting for transfers between devices: 0.01 us -> 7.44 us  [per_device(): free_first = [arrived, lax.ppermute(cuts[1], 'energy', first_pairs)]]
    ppermute x2, waiting for transfers between devices: 0.01 us -> 7.1 us  [sent_after(): free_first.append(lax.ppermute(cut, 'energy', first_pairs))]
    ppermute x1, waiting for transfers between devices: 6.71 us -> 0.01 us  [per_device(): lax.ppermute(cuts[-1], 'energy', around_pairs)]
    ppermute x2, waiting for transfers between devices: 6.49 us -> 0.01 us  [per_device(): arrived = lax.ppermute(leaving, 'slab', wire_up)]
    ppermute x1, waiting for transfers between devices: 6.25 us -> 0.01 us  [per_device(): carried_first = lax.ppermute(carried, 'energy', first_pairs)]
    pallas_call x14 -> x13, Pallas kernels: 44.9 us -> 40.9 us  [call(): pl.pallas_call(kernel, out_shape=out_shapes, cost_estimate=cost, compiler...]
    ppermute x2, waiting for transfers between devices: 6.6 us -> 2.63 us  [sent_on(): free_second.append(lax.ppermute(given, 'energy', relay_pairs))]
  transfers between devices with their start and end apart: 21 -> 21, of which waited for: 9 -> 8; matrix products, arithmetic and copies ran while one was open for 4% -> 3% of each run, Pallas kernels for 33% -> 25%
where the time goes in v6:
time: 130 us; the launch traced here: 128 us
  starting transfers between devices  42.4 us (33%)
  Pallas kernels  40.9 us (31%)
  waiting for transfers between devices  26.1 us (20%)
  local copies, waits for them, and re-layouts  11.7 us (9%)
  other arithmetic  6.15 us (5%)
    pallas_call x13, Pallas kernels, call(): pl.pallas_call(kernel, out_shape=out_shapes, cost_estimate=cost, compiler...  40.9 us
    ppermute x2, starting transfers between devices, per_device(): outputs.append(here + lax.ppermute(there, 'energy', twin_pairs))  11 us
    unnamed x54, local copies, waits for them, and re-layouts  8.69 us
    ppermute x1, waiting for transfers between devices, per_device(): free_first = [arrived, lax.ppermute(cuts[1], 'energy', first_pairs)]  7.44 us
    ppermute x2, waiting for transfers between devices, sent_after(): free_first.append(lax.ppermute(cut, 'energy', first_pairs))  7.1 us
    ppermute x2, starting transfers between devices, per_device(): arrived = lax.ppermute(leaving, 'slab', wire_up)  5.76 us
    ppermute x3, waiting for transfers between devices, exchanged(): lax.ppermute(payload, 'energy', [(e, e ^ mask) for e in range(peers)])  5.24 us
    ppermute x3, starting transfers between devices, exchanged(): lax.ppermute(payload, 'energy', [(e, e ^ mask) for e in range(peers)])  4.5 us
  transfers between devices with their start and end apart: 21, of which 8 were waited for; matrix products, arithmetic and copies ran while one was open for 3% of the time, Pallas kernels for 25%

profile of v6, /device:TPU:13, one launch (start us, length us, event | category | flops | bytes accessed | tf_op | source)
XLA Modules:
  0.0 128.4 jit_solution(3790006210695787998)
XLA Ops:
  0.7 2.9 %slice_bitcast_fusion = (f32[1,2,256,256]{3,2,1,0:T(8,128)}, f32[1,2,256,256]{3,2,1,0:T(8,128)}, f32[1,2,256,256]{3,2,1,0:T(8,128)}, f32[1,2,256,256]{3,2,1,0:T(8,128)}) fusion(f32[1,4,2,256,256]{4,3,2,1,0:T(8,128)} %param.14), kind=kLoop, calls=%fused_computation.2 | loop fusion | bytes 4194304 | tf_op jit(solution)/shard_map/slice | solution.py:323
  5.1 4.3 %collective-permute-start = (f32[2,1,4,128]{3,2,0,1:T(4,128)S(1)}, f32[2,1,4,128]{3,2,0,1:T(4,128)S(1)}, u32[]{:S(2)}, u32[]{:S(2)}) collective-permute-start(f32[2,1,4,128]{3,2,0,1:T(4,128)S(1)} %get-tuple-element.131), channel_id=1, source_target_pairs={{1,2},{2,1},{5,6},{6,5},{9,10},{10,9},{13,14},{14,13},{17,18},{18,... | collective-permute-start | bytes 12296 | tf_op jit(solution)/shard_map/ppermute | solution.py:339
  11.3 2.7 %shard_map.113 = f32[104,128]{1,0:T(8,128)} custom-call(s32[1]{0:T(128)} %bitcast.1.mine, f32[64,128]{1,0:T(8,128)} %bitcast.51, f32[64,128]{1,0:T(8,128)} %bitcast.49, f32[64,128]{1,0:T(8,128)} %bitcast.59, f32[2,4,128]{2,1,0:T(4,128)} %bitcast.62, f32[2,4,128]{2,1,0:T(4,128)} %bitcast.60, s32[4,256]{1,0:T(4,128)} %owner.1), custom_call_target="tpu_custom_call" | custom-call | flops 301989888 | bytes 163844 | tf_op jit(solution)/shard_map/pallas_call | solution.py:67
  14.0 1.8 %collective-permute-start.2 = (f32[104,128]{1,0:T(8,128)}, f32[104,128]{1,0:T(8,128)S(1)}, u32[]{:S(2)}, u32[]{:S(2)}) collective-permute-start(f32[104,128]{1,0:T(8,128)} %shard_map.113), channel_id=1, source_target_pairs={{0,4},{4,0},{8,12},{12,8},{16,20},{20,16},{24,28},{28,24},{1,5},{5... | collective-permute-start | bytes 159752 | tf_op jit(solution)/shard_map/ppermute | solution.py:278
  18.6 1.5 %collective-permute-start.4 = (f32[104,128]{1,0:T(8,128)S(1)}, f32[104,128]{1,0:T(8,128)S(1)}, u32[]{:S(2)}, u32[]{:S(2)}) collective-permute-start(f32[104,128]{1,0:T(8,128)S(1)} %add_select_fusion.2), channel_id=1, source_target_pairs={{0,12},{4,8},{8,4},{12,0},{16,28},{20,24},{24,20},{28,16},{1,13},{... | collective-permute-start | bytes 159752 | tf_op jit(solution)/shard_map/ppermute | solution.py:278
  20.0 1.7 %multiply_reduce_fusion.weights = f32[4,256,256]{2,1,0:T(8,128)S(1)} fusion(f32[4,256,256]{2,1,0:T(8,128)} %param.18, f32[4,4]{1,0:T(4,128)S(1)} %add_select_fusion.3), kind=kLoop, calls=%fused_computation | loop fusion | flops 1835008 | bytes 2097216 | tf_op jit(solution)/shard_map/reduce_sum | solution.py:395
  23.7 3.5 %collective-permute-done.5 = f32[104,128]{1,0:T(8,128)S(1)} collective-permute-done((f32[104,128]{1,0:T(8,128)S(1)}, f32[104,128]{1,0:T(8,128)S(1)}, u32[]{:S(2)}, u32[]{:S(2)}) %collective-permute-start.5) | collective-permute-done | bytes 53280 | tf_op jit(solution)/shard_map/ppermute | solution.py:278
  27.4 1.6 %copy-done.5 = f32[4,2,256,256]{3,2,1,0:T(8,128)S(1)} copy-done((f32[4,2,256,256]{3,2,1,0:T(8,128)S(1)}, f32[4,2,256,256]{3,2,1,0:T(8,128)}, u32[]{:S(2)}) %copy-start.5) | copy-done | bytes 2097176
  29.0 6.2 %shard_map.114 = (f32[2,256,256]{2,1,0:T(8,128)S(1)}, f32[2,256,256]{2,1,0:T(8,128)S(1)}) custom-call(f32[4,2,256,256]{3,2,1,0:T(8,128)S(1)} %bitcast.47, f32[4,2,256,256]{3,2,1,0:T(8,128)S(1)} %copy-done.5, f32[104,128]{1,0:T(8,128)S(1)} %add_select_fusion.sums.refs_3_), custom_call_target="tpu_custom_call" | custom-call | flops 5133828096 | bytes 5296128 | tf_op jit(solution)/shard_map/pallas_call | solution.py:67
  35.2 3.6 %collective-permute-start.6 = (f32[2,256,256]{2,1,0:T(8,128)S(1)}, f32[2,256,256]{2,1,0:T(8,128)S(1)}, u32[]{:S(2)}, u32[]{:S(2)}) collective-permute-start(f32[2,256,256]{2,1,0:T(8,128)S(1)} %get-tuple-element.69.whole_source), channel_id=1, source_target_pairs={{0,1},{1,2},{2,3},{4,5},{5,6},{6,7},{8,9},{9,10},{10,11},{12,13},{... | collective-permute-start | bytes 1572872 | tf_op jit(solution)/shard_map/ppermute | solution.py:442
  40.5 3.9 %collective-permute-start.11 = (f32[1,2,256,256]{3,2,1,0:T(8,128)S(1)}, f32[1,2,256,256]{3,2,1,0:T(8,128)}, u32[]{:S(2)}, u32[]{:S(2)}) collective-permute-start(f32[1,2,256,256]{3,2,1,0:T(8,128)S(1)} %copy-done.18), channel_id=1, source_target_pairs={{8,24},{12,28},{16,0},{20,4},{9,25},{13,29},{17,1},{21,5},{10,26},... | collective-permute-start | bytes 1572872 | tf_op jit(solution)/shard_map/ppermute | solution.py:365
  44.4 7.4 %collective-permute-done.7.refs_1_ = f32[1,2,256,256]{3,2,1,0:T(8,128)} collective-permute-done((f32[1,2,256,256]{3,2,1,0:T(8,128)S(1)}, f32[1,2,256,256]{3,2,1,0:T(8,128)}, u32[]{:S(2)}, u32[]{:S(2)}) %collective-permute-start.7) | collective-permute-done | bytes 524320 | tf_op jit(solution)/shard_map/ppermute | solution.py:363
  54.6 2.2 %collective-permute-start.8 = (f32[2,256,256]{2,1,0:T(8,128)S(1)}, f32[2,256,256]{2,1,0:T(8,128)S(1)}, u32[]{:S(2)}, u32[]{:S(2)}) collective-permute-start(f32[2,256,256]{2,1,0:T(8,128)S(1)} %shard_map.115), channel_id=1, source_target_pairs={{0,1},{1,2},{2,3},{4,5},{5,6},{6,7},{8,9},{9,10},{10,11},{12,13},{... | collective-permute-start | bytes 1572872 | tf_op jit(solution)/shard_map/ppermute | solution.py:442
  56.8 7.1 %collective-permute-done.9.refs_0_ = f32[1,2,256,256]{3,2,1,0:T(8,128)} collective-permute-done((f32[1,2,256,256]{3,2,1,0:T(8,128)S(1)}, f32[1,2,256,256]{3,2,1,0:T(8,128)}, u32[]{:S(2)}, u32[]{:S(2)}) %collective-permute-start.9) | collective-permute-done | bytes 524320 | tf_op jit(solution)/shard_map/ppermute | solution.py:373
  65.2 2.5 %shard_map.116 = (f32[2,2,256,256]{3,2,1,0:T(8,128)S(1)}, f32[2,2,256,256]{3,2,1,0:T(8,128)S(1)}) custom-call(f32[1,2,256,256]{3,2,1,0:T(8,128)S(1)} %copy-done.9, f32[1,2,256,256]{3,2,1,0:T(8,128)} %collective-permute-done.7.refs_1_, f32[4,2,256,256]{3,2,1,0:T(8,128)S(1)} %copy-done.5, f32[104,128]{1,0:T(8,128)S(1)} %add_select_fusion.sums.refs_3_), custom_call_target="tpu_custom_call" | custom-call | flops 1207959552 | bytes 5296128 | tf_op jit(solution)/shard_map/pallas_call | solution.py:67
  70.5 1.7 %shard_map.117 = f32[2,256,256]{2,1,0:T(8,128)} custom-call(f32[2,256,256]{2,1,0:T(8,128)S(1)} %get-tuple-element.76.whole_map, f32[2,256,256]{2,1,0:T(8,128)S(1)} %get-tuple-element.69.whole_source, f32[2,256,256]{2,1,0:T(8,128)S(1)} %collective-permute-done.8.carried), custom_call_target="tpu_custom_call" | custom-call | flops 603979776 | bytes 2097152 | tf_op jit(solution)/shard_map/pallas_call | solution.py:67
  72.2 2.0 %collective-permute-start.12 = (f32[2,256,256]{2,1,0:T(8,128)}, f32[2,256,256]{2,1,0:T(8,128)}, u32[]{:S(2)}, u32[]{:S(2)}) collective-permute-start(f32[2,256,256]{2,1,0:T(8,128)} %shard_map.117), channel_id=1, source_target_pairs={{0,1},{1,2},{2,3},{4,5},{5,6},{6,7},{8,9},{9,10},{10,11},{12,13},{... | collective-permute-start | bytes 1572872 | tf_op jit(solution)/shard_map/ppermute | solution.py:463
  76.3 1.3 collective-permute-start.18
  77.6 3.1 %collective-permute-start.17 = (f32[2,256,256]{2,1,0:T(8,128)}, f32[2,256,256]{2,1,0:T(8,128)S(1)}, u32[]{:S(2)}, u32[]{:S(2)}) collective-permute-start(f32[2,256,256]{2,1,0:T(8,128)} %shard_map.117), channel_id=1, source_target_pairs={{8,17},{9,18},{10,19},{12,21},{13,22},{14,23},{16,9},{17,10},{18,1... | collective-permute-start | bytes 1572872 | tf_op jit(solution)/shard_map/ppermute | solution.py:464
  80.7 1.6 %copy-done.6 = f32[4,2,256,256]{3,2,1,0:T(8,128)S(1)} copy-done((f32[4,2,256,256]{3,2,1,0:T(8,128)S(1)}, f32[4,2,256,256]{3,2,1,0:T(8,128)}, u32[]{:S(2)}) %copy-start.6) | copy-done | bytes 2097176
  83.4 2.6 %shard_map.119 = (f32[2,2,256,256]{3,2,1,0:T(8,128)S(1)}, f32[2,2,256,256]{3,2,1,0:T(8,128)S(1)}) custom-call(f32[1,2,256,256]{3,2,1,0:T(8,128)S(1)} %copy-done.11, f32[1,2,256,256]{3,2,1,0:T(8,128)} %collective-permute-done.14.refs_1_, f32[4,2,256,256]{3,2,1,0:T(8,128)S(1)} %copy-done.6, f32[104,128]{1,0:T(8,128)S(1)} %add_select_fusion.sums.refs_3_), custom_call_target="tpu_custom_call" | custom-call | flops 1207959552 | bytes 5296128 | tf_op jit(solution)/shard_map/pallas_call | solution.py:67
  86.0 2.5 %shard_map.118 = (f32[2,2,256,256]{3,2,1,0:T(8,128)S(1)}, f32[2,2,256,256]{3,2,1,0:T(8,128)S(1)}) custom-call(f32[1,2,256,256]{3,2,1,0:T(8,128)} %collective-permute-done.9.refs_0_, f32[1,2,256,256]{3,2,1,0:T(8,128)S(1)} %copy-done.13, f32[4,2,256,256]{3,2,1,0:T(8,128)S(1)} %copy-done.7, f32[104,128]{1,0:T(8,128)S(1)} %add_select_fusion.sums.refs_3_), custom_call_target="tpu_custom_call" | custom-call | flops 1207959552 | bytes 5296128 | tf_op jit(solution)/shard_map/pallas_call | solution.py:67
  88.6 2.6 %collective-permute-done.15.refs_0_ = f32[1,2,256,256]{3,2,1,0:T(8,128)} collective-permute-done((f32[1,2,256,256]{3,2,1,0:T(8,128)}, f32[1,2,256,256]{3,2,1,0:T(8,128)}, u32[]{:S(2)}, u32[]{:S(2)}) %collective-permute-start.15) | collective-permute-done | bytes 524320 | tf_op jit(solution)/shard_map/ppermute | solution.py:369
  91.2 8.6 %shard_map.120 = (f32[4,2,256,256]{3,2,1,0:T(8,128)S(1)}, f32[2,256,256]{2,1,0:T(8,128)}) custom-call(f32[4,2,256,256]{3,2,1,0:T(8,128)S(1)} %bitcast.48, f32[4,2,256,256]{3,2,1,0:T(8,128)S(1)} %copy-done.7, f32[104,128]{1,0:T(8,128)S(1)} %add_select_fusion.sums.refs_3_, f32[2,256,256]{2,1,0:T(8,128)} %collective-permute-done.12.carried), custom_call_target="tpu_custom_call" | custom-call | flops 4831838208 | bytes 7393280 | tf_op jit(solution)/shard_map/pallas_call | solution.py:67
  99.8 2.7 %shard_map.122 = (f32[2,2,256,256]{3,2,1,0:T(8,128)S(1)}, f32[2,2,256,256]{3,2,1,0:T(8,128)S(1)}) custom-call(f32[1,2,256,256]{3,2,1,0:T(8,128)} %collective-permute-done.15.refs_0_, f32[1,2,256,256]{3,2,1,0:T(8,128)} %collective-permute-done.18.refs_1_, f32[4,2,256,256]{3,2,1,0:T(8,128)S(1)} %copy-done.7, f32[104,128]{1,0:T(8,128)S(1)} %add_select_fusion.sums.refs_3_), custom_call_target="tpu_custom_call" | custom-call | flops 1207959552 | bytes 5296128 | tf_op jit(solution)/shard_map/pallas_call | solution.py:67
  102.4 1.9 %shard_map.121 = (f32[2,2,256,256]{3,2,1,0:T(8,128)S(1)}, f32[2,256,256]{2,1,0:T(8,128)S(1)}) custom-call(f32[2,2,256,256]{3,2,1,0:T(8,128)S(1)} %get-tuple-element.96.link, f32[2,2,256,256]{3,2,1,0:T(8,128)S(1)} %get-tuple-element.97.source, f32[2,256,256]{2,1,0:T(8,128)S(1)} %collective-permute-done.17.carried), custom_call_target="tpu_custom_call" | custom-call | flops 1207959552 | bytes 4194304 | tf_op jit(solution)/shard_map/pallas_call | solution.py:67
  104.3 2.6 %shard_map.123 = (f32[2,2,256,256]{3,2,1,0:T(8,128)S(1)}, f32[2,256,256]{2,1,0:T(8,128)}) custom-call(f32[2,2,256,256]{3,2,1,0:T(8,128)S(1)} %get-tuple-element.106.link, f32[2,2,256,256]{3,2,1,0:T(8,128)S(1)} %get-tuple-element.107.source, f32[2,256,256]{2,1,0:T(8,128)S(1)} %get-tuple-element.108.carried), custom_call_target="tpu_custom_call" | custom-call | flops 1207959552 | bytes 4194304 | tf_op jit(solution)/shard_map/pallas_call | solution.py:67
  107.0 2.7 %shard_map.124 = (f32[2,2,256,256]{3,2,1,0:T(8,128)S(1)}, f32[2,2,256,256]{3,2,1,0:T(8,128)S(1)}, f32[2,256,256]{2,1,0:T(8,128)S(1)}) custom-call(s32[2]{0:T(128)S(1)} %pad_add_fusion.pick, f32[2,2,256,256]{3,2,1,0:T(8,128)S(1)} %copy-done.2, f32[2,2,256,256]{3,2,1,0:T(8,128)S(1)} %copy-done.4, f32[2,256,256]{2,1,0:T(8,128)S(1)} %collective-permute-done.16.carried, ...), custom_call_target="tpu_custom_call" | custom-call | flops 1207959552 | bytes 9437192 | tf_op jit(solution)/shard_map/pallas_call | solution.py:67
  109.6 10.9 %collective-permute-start.19 = (f32[2,2,256,256]{3,2,1,0:T(8,128)S(1)}, f32[2,2,256,256]{3,2,1,0:T(8,128)S(1)}, u32[]{:S(2)}, u32[]{:S(2)}) collective-permute-start(f32[2,2,256,256]{3,2,1,0:T(8,128)S(1)} %get-tuple-element.115), channel_id=1, source_target_pairs={{0,4},{4,0},{8,12},{12,8},{16,20},{20,16},{24,28},{28,24},{1,5},{5... | collective-permute-start | bytes 3145736 | tf_op jit(solution)/shard_map/ppermute | solution.py:522
  120.6 3.4 %shard_map.125 = (f32[2,2,256,256]{3,2,1,0:T(8,128)S(1)}, f32[2,2,256,256]{3,2,1,0:T(8,128)S(1)}, f32[2,256,256]{2,1,0:T(8,128)}) custom-call(s32[2]{0:T(128)S(1)} %pad_add_fusion.pick, f32[2,2,256,256]{3,2,1,0:T(8,128)S(1)} %get-tuple-element.116.link, f32[2,2,256,256]{3,2,1,0:T(8,128)S(1)} %get-tuple-element.117.source, ...), custom_call_target="tpu_custom_call" | custom-call | flops 1207959552 | bytes 9437192 | tf_op jit(solution)/shard_map/pallas_call | solution.py:67
  124.2 2.6 %collective-permute-done.20 = f32[2,2,256,256]{3,2,1,0:T(8,128)S(1)} collective-permute-done((f32[2,2,256,256]{3,2,1,0:T(8,128)S(1)}, f32[2,2,256,256]{3,2,1,0:T(8,128)S(1)}, u32[]{:S(2)}, u32[]{:S(2)}) %collective-permute-start.20) | collective-permute-done | bytes 1048608 | tf_op jit(solution)/shard_map/ppermute | solution.py:522
  127.0 1.5 %maximum_bitcast_fusion = f32[1,4,2,256,256]{4,3,2,1,0:T(8,128)} fusion(f32[2,2,256,256]{3,2,1,0:T(8,128)S(1)} %add.136, f32[2,2,256,256]{3,2,1,0:T(8,128)S(1)} %add.135), kind=kLoop, calls=%fused_computation.1 | loop fusion | flops 524288 | bytes 4194304 | tf_op jit(solution)/shard_map/broadcast_in_dim | solution.py:523
  (100 shorter events, 20.2 us)
Async XLA Ops:
  0.6 8.9 %copy-start.26 = (s32[4]{0:T(128)S(1)}, s32[4]{0:T(128)}, u32[]{:S(2)}) copy-start(s32[4]{0:T(128)} %constant.61.clone) | copy-start | bytes 52
  3.6 23.8 %copy-start.15 = (f32[16,4,128]{2,1,0:T(4,128)S(1)}, f32[16,4,128]{2,1,0:T(4,128)}, u32[]{:S(2)}) copy-start(f32[16,4,128]{2,1,0:T(4,128)} %param.12) | copy-start | bytes 98308
  3.6 23.8 %copy-start.17 = (f32[16,4,128]{2,1,0:T(4,128)S(1)}, f32[16,4,128]{2,1,0:T(4,128)}, u32[]{:S(2)}) copy-start(f32[16,4,128]{2,1,0:T(4,128)} %param.10) | copy-start | bytes 98308
  3.6 14.2 %collective-permute-start.3 = (f32[1,2,256,256]{3,2,1,0:T(8,128)}, f32[1,2,256,256]{3,2,1,0:T(8,128)S(1)}, u32[]{:S(2)}, u32[]{:S(2)}) collective-permute-start(f32[1,2,256,256]{3,2,1,0:T(8,128)} %get-tuple-element.126), channel_id=1, source_target_pairs={{0,8},{4,12},{8,0},{12,4},{16,24},{20,28},{24,16},{28,20},{1,9},{5... | collective-permute-start | bytes 1572872 | tf_op jit(solution)/shard_map/ppermute | solution.py:324
  4.9 4.8 %collective-permute-start.1 = (f32[2,1,4,128]{3,2,0,1:T(4,128)S(1)}, f32[2,1,4,128]{3,2,0,1:T(4,128)S(1)}, u32[]{:S(2)}, u32[]{:S(2)}) collective-permute-start(f32[2,1,4,128]{3,2,0,1:T(4,128)S(1)} %get-tuple-element.130), channel_id=1, source_target_pairs={{0,1},{2,3},{1,0},{3,2},{4,5},{6,7},{5,4},{7,6},{8,9},{10,11},{9,8... | collective-permute-start | bytes 12296 | tf_op jit(solution)/shard_map/ppermute | solution.py:338
  5.1 5.6 %collective-permute-start = (f32[2,1,4,128]{3,2,0,1:T(4,128)S(1)}, f32[2,1,4,128]{3,2,0,1:T(4,128)S(1)}, u32[]{:S(2)}, u32[]{:S(2)}) collective-permute-start(f32[2,1,4,128]{3,2,0,1:T(4,128)S(1)} %get-tuple-element.131), channel_id=1, source_target_pairs={{1,2},{2,1},{5,6},{6,5},{9,10},{10,9},{13,14},{14,13},{17,18},{18,... | collective-permute-start | bytes 12296 | tf_op jit(solution)/shard_map/ppermute | solution.py:339
  11.3 12.4 %copy-start.22 = (f32[1,1,8,128]{3,2,0,1:T(8,128)S(1)}, f32[1,1,8,128]{3,2,0,1:T(8,128)}, u32[]{:S(2)}) copy-start(f32[1,1,8,128]{3,2,0,1:T(8,128)} %get-tuple-element.162) | copy-start | bytes 12292
  11.3 12.4 %copy-start.23 = (f32[1,1,8,128]{3,2,0,1:T(8,128)S(1)}, f32[1,1,8,128]{3,2,0,1:T(8,128)}, u32[]{:S(2)}) copy-start(f32[1,1,8,128]{3,2,0,1:T(8,128)} %get-tuple-element.163) | copy-start | bytes 12292
  11.3 16.1 %copy-start = (f32[1,4,2,256,256]{4,3,2,1,0:T(8,128)S(1)}, f32[1,4,2,256,256]{4,3,2,1,0:T(8,128)}, u32[]{:S(2)}) copy-start(f32[1,4,2,256,256]{4,3,2,1,0:T(8,128)} %param.14) | copy-start | bytes 6291460
  14.0 2.9 %collective-permute-start.2 = (f32[104,128]{1,0:T(8,128)}, f32[104,128]{1,0:T(8,128)S(1)}, u32[]{:S(2)}, u32[]{:S(2)}) collective-permute-start(f32[104,128]{1,0:T(8,128)} %shard_map.113), channel_id=1, source_target_pairs={{0,4},{4,0},{8,12},{12,8},{16,20},{20,16},{24,28},{28,24},{1,5},{5... | collective-permute-start | bytes 159752 | tf_op jit(solution)/shard_map/ppermute | solution.py:278
  18.6 3.8 %collective-permute-start.4 = (f32[104,128]{1,0:T(8,128)S(1)}, f32[104,128]{1,0:T(8,128)S(1)}, u32[]{:S(2)}, u32[]{:S(2)}) collective-permute-start(f32[104,128]{1,0:T(8,128)S(1)} %add_select_fusion.2), channel_id=1, source_target_pairs={{0,12},{4,8},{8,4},{12,0},{16,28},{20,24},{24,20},{28,16},{1,13},{... | collective-permute-start | bytes 159752 | tf_op jit(solution)/shard_map/ppermute | solution.py:278
  22.5 4.8 %collective-permute-start.5 = (f32[104,128]{1,0:T(8,128)S(1)}, f32[104,128]{1,0:T(8,128)S(1)}, u32[]{:S(2)}, u32[]{:S(2)}) collective-permute-start(f32[104,128]{1,0:T(8,128)S(1)} %add_select_fusion.1), channel_id=1, source_target_pairs={{0,28},{4,24},{8,20},{12,16},{16,12},{20,8},{24,4},{28,0},{1,29},{... | collective-permute-start | bytes 159752 | tf_op jit(solution)/shard_map/ppermute | solution.py:278
  29.0 9.8 %copy-start.20 = (f32[1,2,256,256]{3,2,1,0:T(8,128)S(1)}, f32[1,2,256,256]{3,2,1,0:T(8,128)}, u32[]{:S(2)}) copy-start(f32[1,2,256,256]{3,2,1,0:T(8,128)} %get-tuple-element.72) | copy-start | bytes 1572868
  29.0 11.1 %copy-start.9 = (f32[1,2,256,256]{3,2,1,0:T(8,128)S(1)}, f32[1,2,256,256]{3,2,1,0:T(8,128)}, u32[]{:S(2)}) copy-start(f32[1,2,256,256]{3,2,1,0:T(8,128)} %copy-done.8) | copy-start | bytes 1572868
  29.0 11.5 %copy-start.18 = (f32[1,2,256,256]{3,2,1,0:T(8,128)S(1)}, f32[1,2,256,256]{3,2,1,0:T(8,128)}, u32[]{:S(2)}) copy-start(f32[1,2,256,256]{3,2,1,0:T(8,128)} %get-tuple-element.89) | copy-start | bytes 1572868
  29.0 22.8 %copy-start.19 = (f32[1,2,256,256]{3,2,1,0:T(8,128)S(1)}, f32[1,2,256,256]{3,2,1,0:T(8,128)}, u32[]{:S(2)}) copy-start(f32[1,2,256,256]{3,2,1,0:T(8,128)} %get-tuple-element.82) | copy-start | bytes 1572868
  29.0 23.9 %copy-start.21 = (f32[16,4,128]{2,1,0:T(4,128)S(1)}, f32[16,4,128]{2,1,0:T(4,128)}, u32[]{:S(2)}) copy-start(f32[16,4,128]{2,1,0:T(4,128)} %param.11) | copy-start | bytes 98308
  35.2 18.5 %collective-permute-start.6 = (f32[2,256,256]{2,1,0:T(8,128)S(1)}, f32[2,256,256]{2,1,0:T(8,128)S(1)}, u32[]{:S(2)}, u32[]{:S(2)}) collective-permute-start(f32[2,256,256]{2,1,0:T(8,128)S(1)} %get-tuple-element.69.whole_source), channel_id=1, source_target_pairs={{0,1},{1,2},{2,3},{4,5},{5,6},{6,7},{8,9},{9,10},{10,11},{12,13},{... | collective-permute-start | bytes 1572872 | tf_op jit(solution)/shard_map/ppermute | solution.py:442
  38.8 13.0 %collective-permute-start.7 = (f32[1,2,256,256]{3,2,1,0:T(8,128)S(1)}, f32[1,2,256,256]{3,2,1,0:T(8,128)}, u32[]{:S(2)}, u32[]{:S(2)}) collective-permute-start(f32[1,2,256,256]{3,2,1,0:T(8,128)S(1)} %copy-done.20), channel_id=1, source_target_pairs={{0,8},{4,12},{8,0},{12,4},{16,24},{20,28},{24,16},{28,20},{1,9},{5... | collective-permute-start | bytes 1572872 | tf_op jit(solution)/shard_map/ppermute | solution.py:363
  40.2 29.5 %collective-permute-start.10 = (f32[1,2,256,256]{3,2,1,0:T(8,128)S(1)}, f32[1,2,256,256]{3,2,1,0:T(8,128)S(1)}, u32[]{:S(2)}, u32[]{:S(2)}) collective-permute-start(f32[1,2,256,256]{3,2,1,0:T(8,128)S(1)} %copy-done.9), channel_id=1, source_target_pairs={{0,16},{4,20},{8,24},{12,28},{16,0},{20,4},{24,8},{28,12},{1,17},{... | collective-permute-start | bytes 1572872 | tf_op jit(solution)/shard_map/ppermute | solution.py:364
  40.5 30.0 %collective-permute-start.11 = (f32[1,2,256,256]{3,2,1,0:T(8,128)S(1)}, f32[1,2,256,256]{3,2,1,0:T(8,128)}, u32[]{:S(2)}, u32[]{:S(2)}) collective-permute-start(f32[1,2,256,256]{3,2,1,0:T(8,128)S(1)} %copy-done.18), channel_id=1, source_target_pairs={{8,24},{12,28},{16,0},{20,4},{9,25},{13,29},{17,1},{21,5},{10,26},... | collective-permute-start | bytes 1572872 | tf_op jit(solution)/shard_map/ppermute | solution.py:365
  51.9 12.0 %collective-permute-start.9 = (f32[1,2,256,256]{3,2,1,0:T(8,128)S(1)}, f32[1,2,256,256]{3,2,1,0:T(8,128)}, u32[]{:S(2)}, u32[]{:S(2)}) collective-permute-start(f32[1,2,256,256]{3,2,1,0:T(8,128)S(1)} %copy-done.19), channel_id=1, source_target_pairs={{0,8},{4,12},{8,0},{12,4},{16,24},{20,28},{24,16},{28,20},{1,9},{5... | collective-permute-start | bytes 1572872 | tf_op jit(solution)/shard_map/ppermute | solution.py:373
  54.6 15.9 %collective-permute-start.8 = (f32[2,256,256]{2,1,0:T(8,128)S(1)}, f32[2,256,256]{2,1,0:T(8,128)S(1)}, u32[]{:S(2)}, u32[]{:S(2)}) collective-permute-start(f32[2,256,256]{2,1,0:T(8,128)S(1)} %shard_map.115), channel_id=1, source_target_pairs={{0,1},{1,2},{2,3},{4,5},{5,6},{6,7},{8,9},{9,10},{10,11},{12,13},{... | collective-permute-start | bytes 1572872 | tf_op jit(solution)/shard_map/ppermute | solution.py:442
  63.9 11.6 %collective-permute-start.13 = (f32[1,2,256,256]{3,2,1,0:T(8,128)S(1)}, f32[1,2,256,256]{3,2,1,0:T(8,128)S(1)}, u32[]{:S(2)}, u32[]{:S(2)}) collective-permute-start(f32[1,2,256,256]{3,2,1,0:T(8,128)S(1)} %copy-done.18), channel_id=1, source_target_pairs={{0,8},{4,12},{8,0},{12,4},{16,24},{20,28},{24,16},{28,20},{1,9},{5... | collective-permute-start | bytes 1572872 | tf_op jit(solution)/shard_map/ppermute | solution.py:373
  64.9 15.8 %collective-permute-start.14 = (f32[1,2,256,256]{3,2,1,0:T(8,128)}, f32[1,2,256,256]{3,2,1,0:T(8,128)}, u32[]{:S(2)}, u32[]{:S(2)}) collective-permute-start(f32[1,2,256,256]{3,2,1,0:T(8,128)} %collective-permute-done.7.refs_1_), channel_id=1, source_target_pairs={{0,16},{4,20},{8,24},{12,28},{16,0},{20,4},{24,8},{28,12},{1,17},{... | collective-permute-start | bytes 1572872 | tf_op jit(solution)/shard_map/ppermute | solution.py:369
  72.2 16.4 %collective-permute-start.12 = (f32[2,256,256]{2,1,0:T(8,128)}, f32[2,256,256]{2,1,0:T(8,128)}, u32[]{:S(2)}, u32[]{:S(2)}) collective-permute-start(f32[2,256,256]{2,1,0:T(8,128)} %shard_map.117), channel_id=1, source_target_pairs={{0,1},{1,2},{2,3},{4,5},{5,6},{6,7},{8,9},{9,10},{10,11},{12,13},{... | collective-permute-start | bytes 1572872 | tf_op jit(solution)/shard_map/ppermute | solution.py:463
  74.2 17.0 %collective-permute-start.15 = (f32[1,2,256,256]{3,2,1,0:T(8,128)}, f32[1,2,256,256]{3,2,1,0:T(8,128)}, u32[]{:S(2)}, u32[]{:S(2)}) collective-permute-start(f32[1,2,256,256]{3,2,1,0:T(8,128)} %collective-permute-done.9.refs_0_), channel_id=1, source_target_pairs={{0,16},{4,20},{8,24},{12,28},{16,0},{20,4},{24,8},{28,12},{1,17},{... | collective-permute-start | bytes 1572872 | tf_op jit(solution)/shard_map/ppermute | solution.py:369
  76.3 14.9 %collective-permute-start.18 = (f32[1,2,256,256]{3,2,1,0:T(8,128)}, f32[1,2,256,256]{3,2,1,0:T(8,128)}, u32[]{:S(2)}, u32[]{:S(2)}) collective-permute-start(f32[1,2,256,256]{3,2,1,0:T(8,128)} %collective-permute-done.11), channel_id=1, source_target_pairs={{24,16},{28,20},{0,8},{4,12},{25,17},{29,21},{1,9},{5,13},{26,18},... | collective-permute-start | bytes 1572872 | tf_op jit(solution)/shard_map/ppermute | solution.py:468
  77.6 22.1 %collective-permute-start.17 = (f32[2,256,256]{2,1,0:T(8,128)}, f32[2,256,256]{2,1,0:T(8,128)S(1)}, u32[]{:S(2)}, u32[]{:S(2)}) collective-permute-start(f32[2,256,256]{2,1,0:T(8,128)} %shard_map.117), channel_id=1, source_target_pairs={{8,17},{9,18},{10,19},{12,21},{13,22},{14,23},{16,9},{17,10},{18,1... | collective-permute-start | bytes 1572872 | tf_op jit(solution)/shard_map/ppermute | solution.py:464
  91.2 15.8 %collective-permute-start.16 = (f32[2,256,256]{2,1,0:T(8,128)}, f32[2,256,256]{2,1,0:T(8,128)S(1)}, u32[]{:S(2)}, u32[]{:S(2)}) collective-permute-start(f32[2,256,256]{2,1,0:T(8,128)} %collective-permute-done.12.carried), channel_id=1, source_target_pairs={{0,8},{4,12},{8,0},{12,4},{16,24},{20,28},{24,16},{28,20},{1,9},{5... | collective-permute-start | bytes 1572872 | tf_op jit(solution)/shard_map/ppermute | solution.py:472
  109.6 14.3 %collective-permute-start.19 = (f32[2,2,256,256]{3,2,1,0:T(8,128)S(1)}, f32[2,2,256,256]{3,2,1,0:T(8,128)S(1)}, u32[]{:S(2)}, u32[]{:S(2)}) collective-permute-start(f32[2,2,256,256]{3,2,1,0:T(8,128)S(1)} %get-tuple-element.115), channel_id=1, source_target_pairs={{0,4},{4,0},{8,12},{12,8},{16,20},{20,16},{24,28},{28,24},{1,5},{5... | collective-permute-start | bytes 3145736 | tf_op jit(solution)/shard_map/ppermute | solution.py:522
  124.1 2.7 %collective-permute-start.20 = (f32[2,2,256,256]{3,2,1,0:T(8,128)S(1)}, f32[2,2,256,256]{3,2,1,0:T(8,128)S(1)}, u32[]{:S(2)}, u32[]{:S(2)}) collective-permute-start(f32[2,2,256,256]{3,2,1,0:T(8,128)S(1)} %get-tuple-element.123), channel_id=1, source_target_pairs={{0,4},{4,0},{8,12},{12,8},{16,20},{20,16},{24,28},{28,24},{1,5},{5... | collective-permute-start | bytes 3145736 | tf_op jit(solution)/shard_map/ppermute | solution.py:522
  (16 other events, 45.4 us)

commit v7 on v6

--- a/solution.py
+++ b/solution.py
@@ -77,7 +77,13 @@
     return jax.ShapeDtypeStruct(dims, jnp.float32)
 
 
-def gather_kernel(rows, peers, mine, field, perm, charge, before, after, owner, out):
+def gather_kernel(rows, peers, sizes, mine, field, perm, charge, before, after, owner, free, *refs):
+    out, ends, *parts, sems = refs
+    taken = []
+    for index, part in enumerate(parts):
+        cut = free.at[pl.ds(sum(sizes[:index]), sizes[index])]
+        taken.append(pltpu.make_async_copy(cut, part, sems.at[index]))
+        taken[-1].start()
     total, depth = charge.shape
     count, orbitals = owner.shape
     height = total // count
@@ -140,11 +146,15 @@
             for piece in range(orbitals // depth):
                 row = sums_row(kind, slab, count, orbitals // depth) + piece
                 out[row : row + 1, :] = value[:, piece * depth : (piece + 1) * depth]
-    start = kinds * count * (orbitals // depth)
+    start = 0
     for array in (field, perm):
         for end in (0, rows - 1):
-            out[start : start + total // rows, :] = array[pl.ds(end, total // rows, stride=rows), :]
+            ends[start : start + total // rows, :] = array[
+                pl.ds(end, total // rows, stride=rows), :
+            ]
             start += total // rows
+    for copy in taken:
+        copy.wait()
 
 
 def sums_row(kind, slab, count, pieces):
@@ -265,22 +275,20 @@
     )
 
 
-def exchanged(payload, head, early):
-    peers, mine = lax.axis_size("energy"), lax.axis_index("energy")
-    assert peers & (peers - 1) == 0
-    rest = payload[head:]
-    before = after = jnp.zeros_like(rest)
-    is_head = lax.broadcasted_iota(jnp.int32, payload.shape, 0) < head
-    mask = 1
-    while mask < peers:
-        if mask > 1:
-            payload, early = lax.optimization_barrier((payload, early))
-        arrived = lax.ppermute(payload, "energy", [(e, e ^ mask) for e in range(peers)])
-        before = jnp.where((mine ^ mask) == mine - 1, arrived[head:], before)
-        after = jnp.where((mine ^ mask) == mine + 1, arrived[head:], after)
-        payload = jnp.where(is_head, payload + arrived, payload)
-        mask = 2 * mask + 1
-    return payload, before, after, early
+def exchanged(sums, ends):
+    peers = lax.axis_size("energy")
+    assert peers >= 4 and peers & (peers - 1) == 0
+    masks = [2, 1] + [1 << k for k in range(2, peers.bit_length() - 1)]
+    rows, twin_ends = sums.shape[0], None
+    first = None
+    for mask in masks:
+        given = jnp.concatenate([sums, ends]) if mask == 1 else sums
+        arrived = lax.ppermute(given, "energy", [(e, e ^ mask) for e in range(peers)])
+        if mask == 1:
+            twin_ends = arrived[rows:]
+        sums = sums + arrived[:rows]
+        first = sums if first is None else first
+    return sums, twin_ends, first
 
 
 def per_device(
@@ -320,8 +328,7 @@
     twin_pairs = [(e, e ^ 1) for e in everyone]
 
     half = count // 2
-    cuts = [free[slab : slab + 1] for slab in range(count)]
-    free_first = [lax.ppermute(cuts[0], "energy", first_pairs)]
+    sizes = (half,) + (1,) * (count - half)
 
     place = lax.axis_index("slab")
     wire_up = [(i, i + 1) for i in range(peers - 1)]
@@ -330,9 +337,7 @@
         pairs = [(i, i + 1) for i in range(start, peers - 1, 2)]
         return pairs + [(j, i) for i, j in pairs]
 
-    cuts[0], stacked = lax.optimization_barrier(
-        (cuts[0], jnp.stack([potential_old, permittivity]))
-    )
+    stacked = jnp.stack([potential_old, permittivity])
     lower, upper = end_planes(stacked, 1)
     even = place % 2 == 0
     arrived = lax.ppermute(jnp.where(even, upper, lower), "slab", swaps(0))
@@ -341,28 +346,33 @@
     wire_after = jnp.where(even, arrived, crossed)
 
     cells, rows, depth = charge.shape
-    head = 5 * count * (width // depth)
-    payload = call(
-        functools.partial(gather_kernel, rows, energies),
+    far, near = pl.BlockSpec(memory_space=pl.ANY), pl.BlockSpec(memory_space=pltpu.VMEM)
+    sums, ends, *cuts = call(
+        functools.partial(gather_kernel, rows, energies, sizes),
         56,
         1,
-        shape(head + 4 * cells, depth),
+        (
+            shape(5 * count * (width // depth), depth),
+            shape(4 * cells, depth),
+            *(shape(size, 2, width, width) for size in sizes),
+        ),
         jnp.reshape(mine, (1,)),
         *(array.reshape(-1, depth) for array in (potential_old, permittivity, charge)),
         wire_before.reshape(2, rows, depth),
         wire_after.reshape(2, rows, depth),
         owner_cell,
-        in_specs=[pl.BlockSpec(memory_space=pltpu.SMEM)]
-        + [pl.BlockSpec(memory_space=pltpu.VMEM)] * 6,
-    )
-    sums, ends_before, ends_after, free_first[0] = exchanged(payload, head, free_first[0])
-
-    arrived, *cuts[1:], field, perm, sums = lax.optimization_barrier(
-        (free_first[0], *cuts[1:], potential_old, permittivity, sums)
-    )
-    free_first = [arrived, lax.ppermute(cuts[1], "energy", first_pairs)]
-    free_second = [lax.ppermute(arrived if relayed else cuts[0], "energy", relay_pairs)]
+        free,
+        in_specs=[pl.BlockSpec(memory_space=pltpu.SMEM)] + [near] * 6 + [far],
+        out_specs=(near, near, *(far for _ in sizes)),
+        scratch_shapes=[pltpu.SemaphoreType.DMA((len(sizes),))],
+    )
+    sums, twin_ends, crossed = exchanged(sums, ends)
+
+    crossed, cuts[0] = lax.optimization_barrier((crossed, cuts[0]))
+    free_first = [lax.ppermute(cuts[0], "energy", first_pairs)]
+    sums, cuts[-1] = lax.optimization_barrier((sums, cuts[-1]))
     around = lax.ppermute(cuts[-1], "energy", around_pairs) if relayed else cuts[-1]
+    free_second = []
 
     def sent_on(part):
         given = free_first[part] if relayed else cuts[part]
@@ -382,8 +392,14 @@
         sums,
     )
 
-    ends_before = ends_before.reshape(2, 2, cells, 1, depth)
-    ends_after = ends_after.reshape(2, 2, cells, 1, depth)
+    whole_source, field, perm, ends, mode_tiles = lax.optimization_barrier(
+        (whole_source, potential_old, permittivity, ends, mode_tiles)
+    )
+    beyond = [(e, e + 1) for e in range(1, energies - 1, 2)]
+    other_ends = lax.ppermute(ends, "energy", beyond + [(b, a) for a, b in beyond])
+    is_odd = mine % 2 == 1
+    ends_before = jnp.where(is_odd, twin_ends, other_ends).reshape(2, 2, cells, 1, depth)
+    ends_after = jnp.where(is_odd, other_ends, twin_ends).reshape(2, 2, cells, 1, depth)
     edge = jnp.zeros((2, cells, rows, 1), jnp.float32)
     halos = ((wire_before, wire_after), (ends_before[:, 1], ends_after[:, 0]), (edge, edge))
     potential_new = relaxed(field, perm, charge, halos)
@@ -441,19 +457,16 @@
     for hop in range(1, peers - 1):
         arrived = lax.ppermute(leaving, "slab", wire_up)
         if hop == 1:
-            sent_on(1)
-            sent_after(2)
-            arrived, potential_new, weights, free_first[1] = lax.optimization_barrier(
-                (arrived, potential_new, weights, free_first[1])
+            sent_on(0)
+            sent_after(1)
+            arrived, weights, free_first[0] = lax.optimization_barrier(
+                (arrived, weights, free_first[0])
             )
         if hop == 2:
-            sent_on(2)
-            sent_after(3)
-            beside_first[0] = beside(0, free_first[:2])
-            arrived, beside_first[0], free_first[2], free_second[0], around = (
-                lax.optimization_barrier(
-                    (arrived, beside_first[0], free_first[2], free_second[0], around)
-                )
+            sent_after(2)
+            beside_first[0] = beside(0, free_first[:1])
+            arrived, beside_first[0], free_first[1], around = lax.optimization_barrier(
+                (arrived, beside_first[0], free_first[1], around)
             )
         leaving = call(hop_kernel, 12, 2, whole, whole_map, whole_source, arrived)
 
@@ -462,15 +475,18 @@
 
     carried = lax.ppermute(leaving, "slab", wire_up)
     carried_second = lax.ppermute(leaving, ("energy", "slab"), both(second_pairs))
-    beside_second[0] = beside(0, free_second[:2])
-    beside_first[1] = beside(1, free_first[2:])
-    free_first[3], around = lax.optimization_barrier((free_first[3], around))
+    sent_on(1)
+    beside_second[0] = beside(0, free_second[:1])
+    beside_first[1] = beside(1, free_first[1:])
+    free_first[2], around = lax.optimization_barrier((free_first[2], around))
     free_second.append(lax.ppermute(around, "energy", back_pairs))
-    carried, beside_first[1], beside_second[0], free_second[2] = lax.optimization_barrier(
-        (carried, beside_first[1], beside_second[0], free_second[2])
+    carried, beside_first[1], beside_second[0], potential_new = lax.optimization_barrier(
+        (carried, beside_first[1], beside_second[0], potential_new)
     )
     carried_first = lax.ppermute(carried, "energy", first_pairs)
-    carried, free_second[3] = lax.optimization_barrier((carried, free_second[3]))
+    carried, free_second[1], free_second[2] = lax.optimization_barrier(
+        (carried, free_second[1], free_second[2])
+    )
     greens, _ = call(
         functools.partial(own_greens_kernel, count),
         24,
@@ -484,7 +500,7 @@
         in_specs=[block, block, pl.BlockSpec(sums.shape, lambda s: (0, 0)), one_state],
         out_specs=(block, one_state),
     )
-    beside_second[1] = beside(1, free_second[2:])
+    beside_second[1] = beside(1, free_second[1:])
     carried_second, greens = lax.optimization_barrier((carried_second, greens))
     greens_second = []
     for part in beside_second:

time: 130 us -> 186 us (1.43)
  Pallas kernels: 40.9 us -> 98.6 us
  waiting for transfers between devices: 26.1 us -> 40.2 us
  local copies, waits for them, and re-layouts: 11.7 us -> 1.8 us
  starting transfers between devices: 42.4 us -> 37.2 us
    pallas_call x13, Pallas kernels: 40.9 us -> 98.6 us  [call(): pl.pallas_call(kernel, out_shape=out_shapes, cost_estimate=cost, compiler...]
    ppermute x2, waiting for transfers between devices: 2.63 us -> 18.2 us  [sent_on(): free_second.append(lax.ppermute(given, 'energy', relay_pairs))]
    ppermute x5 -> x4, waiting for transfers between devices: 12.7 us -> 4.25 us  [the longest x3 4.25 us: exchanged(): lax.ppermute(given, 'energy', [(e, e ^ mask) for e in range(peers)])]
    ppermute x2, starting transfers between devices: 11 us -> 2.87 us  [per_device(): outputs.append(here + lax.ppermute(there, 'energy', twin_pairs))]
    unnamed x54 -> x30, local copies, waits for them, and re-layouts: 8.69 us -> 1.65 us
    ppermute x1, waiting for transfers between devices: 0.01 us -> 3.92 us  [per_device(): free_first = [lax.ppermute(cuts[0], 'energy', first_pairs)]]
    slice x1 -> x0, local copies, waits for them, and re-layouts: 2.9 us -> none  [per_device(): cuts = [free[slab:slab + 1] for slab in range(count)]]
    ppermute x1, starting transfers between devices: 1.97 us -> 3.83 us  [per_device(): carried = lax.ppermute(leaving, 'slab', wire_up)]
  transfers between devices with their start and end apart: 21 -> 20, of which waited for: 8 -> 9; matrix products, arithmetic and copies ran while one was open for 3% -> 1% of each run, Pallas kernels for 25% -> 16%
where the time goes in v7:
time: 186 us; the launch traced here: 185 us
  Pallas kernels  98.6 us (53%)
  waiting for transfers between devices  40.2 us (22%)
  starting transfers between devices  37.2 us (20%)
  other arithmetic  6.14 us (3%)
    pallas_call x13, Pallas kernels, call(): pl.pallas_call(kernel, out_shape=out_shapes, cost_estimate=cost, compiler...  98.6 us
    ppermute x2, waiting for transfers between devices, sent_on(): free_second.append(lax.ppermute(given, 'energy', relay_pairs))  18.2 us
    ppermute x2, waiting for transfers between devices, sent_after(): free_first.append(lax.ppermute(cut, 'energy', first_pairs))  8.94 us
    ppermute x2, starting transfers between devices, per_device(): arrived = lax.ppermute(leaving, 'slab', wire_up)  7.28 us
    ppermute x3, starting transfers between devices, exchanged(): lax.ppermute(given, 'energy', [(e, e ^ mask) for e in range(peers)])  4.54 us
    ppermute x1, starting transfers between devices, per_device(): crossed = lax.ppermute(jnp.where(even, lower, upper), 'slab', swaps(1))  4.32 us
    ppermute x3, waiting for transfers between devices, exchanged(): lax.ppermute(given, 'energy', [(e, e ^ mask) for e in range(peers)])  4.25 us
    ppermute x1, waiting for transfers between devices, per_device(): free_first = [lax.ppermute(cuts[0], 'energy', first_pairs)]  3.92 us
  transfers between devices with their start and end apart: 20, of which 9 were waited for; matrix products, arithmetic and copies ran while one was open for 1% of the time, Pallas kernels for 16%

profile of v7, /device:TPU:13, one launch (start us, length us, event | category | flops | bytes accessed | tf_op | source)
XLA Modules:
  0.0 185.0 jit_solution(2166407418630046471)
XLA Ops:
  1.7 4.3 %collective-permute-start = (f32[2,1,4,128]{3,2,0,1:T(4,128)S(1)}, f32[2,1,4,128]{3,2,0,1:T(4,128)S(1)}, u32[]{:S(2)}, u32[]{:S(2)}) collective-permute-start(f32[2,1,4,128]{3,2,0,1:T(4,128)S(1)} %bitcast.62), channel_id=1, source_target_pairs={{1,2},{2,1},{5,6},{6,5},{9,10},{10,9},{13,14},{14,13},{17,18},{18,... | collective-permute-start | bytes 12296 | tf_op jit(solution)/shard_map/ppermute | solution.py:344
  7.7 66.1 %shard_map.113 = (f32[40,128]{1,0:T(8,128)}, f32[64,128]{1,0:T(8,128)}, f32[2,2,256,256]{3,2,1,0:T(8,128)}, f32[1,2,256,256]{3,2,1,0:T(8,128)}, f32[1,2,256,256]{3,2,1,0:T(8,128)}) custom-call(s32[1]{0:T(128)} %bitcast.1.mine, f32[64,128]{1,0:T(8,128)} %bitcast.48, f32[64,128]{1,0:T(8,128)} %bitcast.46, f32[64,128]{1,0:T(8,128)} %bitcast.49, ...), custom_call_target="tpu_custom_call" | custom-call | flops 301989888 | bytes 4358148 | tf_op jit(solution)/shard_map/pallas_call | solution.py:67
  73.7 1.3 collective-permute-start.2
  75.1 1.6 collective-permute-done.2
  78.1 3.0 %collective-permute-start.3 = (f32[104,128]{1,0:T(8,128)S(1)}, f32[104,128]{1,0:T(8,128)S(1)}, u32[]{:S(2)}, u32[]{:S(2)}) collective-permute-start(f32[104,128]{1,0:T(8,128)S(1)} %pad_maximum_fusion), channel_id=1, source_target_pairs={{0,4},{4,0},{8,12},{12,8},{16,20},{20,16},{24,28},{28,24},{1,5},{5... | collective-permute-start | bytes 159752 | tf_op jit(solution)/shard_map/ppermute | solution.py:286
  82.7 2.7 %collective-permute-done.4 = f32[40,128]{1,0:T(8,128)S(1)} collective-permute-done((f32[40,128]{1,0:T(8,128)S(1)}, f32[40,128]{1,0:T(8,128)S(1)}, u32[]{:S(2)}, u32[]{:S(2)}) %collective-permute-start.4) | collective-permute-done | bytes 20512 | tf_op jit(solution)/shard_map/ppermute | solution.py:286
  85.4 1.6 copy-done.1
  87.0 6.2 %shard_map.114 = (f32[2,256,256]{2,1,0:T(8,128)S(1)}, f32[2,256,256]{2,1,0:T(8,128)S(1)}) custom-call(f32[4,2,256,256]{3,2,1,0:T(8,128)S(1)} %bitcast.43, f32[4,2,256,256]{3,2,1,0:T(8,128)S(1)} %copy-done.1, f32[40,128]{1,0:T(8,128)S(1)} %add.106.sums.refs_2_.refs_3_), custom_call_target="tpu_custom_call" | custom-call | flops 5133828096 | bytes 5263360 | tf_op jit(solution)/shard_map/pallas_call | solution.py:67
  93.2 3.6 %collective-permute-start.5 = (f32[2,256,256]{2,1,0:T(8,128)S(1)}, f32[2,256,256]{2,1,0:T(8,128)S(1)}, u32[]{:S(2)}, u32[]{:S(2)}) collective-permute-start(f32[2,256,256]{2,1,0:T(8,128)S(1)} %get-tuple-element.69.whole_source), channel_id=1, source_target_pairs={{0,1},{1,2},{2,3},{4,5},{5,6},{6,7},{8,9},{9,10},{10,11},{12,13},{... | collective-permute-start | bytes 1572872 | tf_op jit(solution)/shard_map/ppermute | solution.py:458
  96.9 2.2 %collective-permute-start.9 = (f32[1,2,256,256]{3,2,1,0:T(8,128)S(1)}, f32[1,2,256,256]{3,2,1,0:T(8,128)S(1)}, u32[]{:S(2)}, u32[]{:S(2)}) collective-permute-start(f32[1,2,256,256]{3,2,1,0:T(8,128)S(1)} %copy-done.13), channel_id=1, source_target_pairs={{8,24},{12,28},{16,0},{20,4},{9,25},{13,29},{17,1},{21,5},{10,26},... | collective-permute-start | bytes 1572872 | tf_op jit(solution)/shard_map/ppermute | solution.py:374
  99.1 3.2 %collective-permute-start.13 = (f32[64,128]{1,0:T(8,128)S(1)}, f32[64,128]{1,0:T(8,128)S(1)}, u32[]{:S(2)}, u32[]{:S(2)}) collective-permute-start(f32[64,128]{1,0:T(8,128)S(1)} %copy-done.9), channel_id=1, source_target_pairs={{4,8},{12,16},{20,24},{8,4},{16,12},{24,20},{5,9},{13,17},{21,25},... | collective-permute-start | bytes 98312 | tf_op jit(solution)/shard_map/ppermute | solution.py:399
  102.3 3.9 %collective-permute-done.6.refs_0_ = f32[2,2,256,256]{3,2,1,0:T(8,128)S(1)} collective-permute-done((f32[2,2,256,256]{3,2,1,0:T(8,128)}, f32[2,2,256,256]{3,2,1,0:T(8,128)S(1)}, u32[]{:S(2)}, u32[]{:S(2)}) %collective-permute-start.6) | collective-permute-done | bytes 1048608 | tf_op jit(solution)/shard_map/ppermute | solution.py:372
  108.9 3.6 %collective-permute-start.7 = (f32[2,256,256]{2,1,0:T(8,128)S(1)}, f32[2,256,256]{2,1,0:T(8,128)S(1)}, u32[]{:S(2)}, u32[]{:S(2)}) collective-permute-start(f32[2,256,256]{2,1,0:T(8,128)S(1)} %shard_map.115), channel_id=1, source_target_pairs={{0,1},{1,2},{2,3},{4,5},{5,6},{6,7},{8,9},{9,10},{10,11},{12,13},{... | collective-permute-start | bytes 1572872 | tf_op jit(solution)/shard_map/ppermute | solution.py:458
  112.8 6.0 %collective-permute-done.8.refs_0_ = f32[1,2,256,256]{3,2,1,0:T(8,128)S(1)} collective-permute-done((f32[1,2,256,256]{3,2,1,0:T(8,128)S(1)}, f32[1,2,256,256]{3,2,1,0:T(8,128)S(1)}, u32[]{:S(2)}, u32[]{:S(2)}) %collective-permute-start.8) | collective-permute-done | bytes 524320 | tf_op jit(solution)/shard_map/ppermute | solution.py:383
  119.7 1.6 shard_map.116
  121.3 1.3 collective-permute-done.7.carried
  123.6 3.8 %collective-permute-start.10 = (f32[2,256,256]{2,1,0:T(8,128)S(1)}, f32[2,256,256]{2,1,0:T(8,128)S(1)}, u32[]{:S(2)}, u32[]{:S(2)}) collective-permute-start(f32[2,256,256]{2,1,0:T(8,128)S(1)} %shard_map.117), channel_id=1, source_target_pairs={{0,1},{1,2},{2,3},{4,5},{5,6},{6,7},{8,9},{9,10},{10,11},{12,13},{... | collective-permute-start | bytes 1572872 | tf_op jit(solution)/shard_map/ppermute | solution.py:476
  127.7 2.9 %collective-permute-done.11.refs_1_ = f32[1,2,256,256]{3,2,1,0:T(8,128)S(1)} collective-permute-done((f32[1,2,256,256]{3,2,1,0:T(8,128)S(1)}, f32[1,2,256,256]{3,2,1,0:T(8,128)S(1)}, u32[]{:S(2)}, u32[]{:S(2)}) %collective-permute-start.11) | collective-permute-done | bytes 524320 | tf_op jit(solution)/shard_map/ppermute | solution.py:383
  130.6 1.3 collective-permute-start.17
  132.7 3.7 %collective-permute-start.15 = (f32[2,256,256]{2,1,0:T(8,128)S(1)}, f32[2,256,256]{2,1,0:T(8,128)S(1)}, u32[]{:S(2)}, u32[]{:S(2)}) collective-permute-start(f32[2,256,256]{2,1,0:T(8,128)S(1)} %shard_map.117), channel_id=1, source_target_pairs={{8,17},{9,18},{10,19},{12,21},{13,22},{14,23},{16,9},{17,10},{18,1... | collective-permute-start | bytes 1572872 | tf_op jit(solution)/shard_map/ppermute | solution.py:477
  136.4 1.6 shard_map.119
  138.0 1.6 shard_map.118
  139.7 18.2 %collective-permute-done.16.refs_0_ = f32[1,2,256,256]{3,2,1,0:T(8,128)S(1)} collective-permute-done((f32[1,2,256,256]{3,2,1,0:T(8,128)S(1)}, f32[1,2,256,256]{3,2,1,0:T(8,128)S(1)}, u32[]{:S(2)}, u32[]{:S(2)}) %collective-permute-start.16) | collective-permute-done | bytes 524320 | tf_op jit(solution)/shard_map/ppermute | solution.py:379
  157.9 7.5 %shard_map.120 = (f32[4,2,256,256]{3,2,1,0:T(8,128)S(1)}, f32[2,256,256]{2,1,0:T(8,128)}) custom-call(f32[4,2,256,256]{3,2,1,0:T(8,128)S(1)} %bitcast.44, f32[4,2,256,256]{3,2,1,0:T(8,128)S(1)} %copy-done.2, f32[40,128]{1,0:T(8,128)S(1)} %add.106.sums.refs_2_.refs_3_, f32[2,256,256]{2,1,0:T(8,128)S(1)} %collective-permute-done.10.carried), custom_call_target="tpu_custom_call" | custom-call | flops 4831838208 | bytes 7360512 | tf_op jit(solution)/shard_map/pallas_call | solution.py:67
  165.5 1.5 shard_map.122
  167.0 1.9 %shard_map.121 = (f32[2,2,256,256]{3,2,1,0:T(8,128)S(1)}, f32[2,256,256]{2,1,0:T(8,128)S(1)}) custom-call(f32[2,2,256,256]{3,2,1,0:T(8,128)S(1)} %get-tuple-element.96.link, f32[2,2,256,256]{3,2,1,0:T(8,128)S(1)} %get-tuple-element.97.source, f32[2,256,256]{2,1,0:T(8,128)S(1)} %collective-permute-done.15.carried), custom_call_target="tpu_custom_call" | custom-call | flops 1207959552 | bytes 4194304 | tf_op jit(solution)/shard_map/pallas_call | solution.py:67
  168.9 2.6 %shard_map.123 = (f32[2,2,256,256]{3,2,1,0:T(8,128)S(1)}, f32[2,256,256]{2,1,0:T(8,128)}) custom-call(f32[2,2,256,256]{3,2,1,0:T(8,128)S(1)} %get-tuple-element.106.link, f32[2,2,256,256]{3,2,1,0:T(8,128)S(1)} %get-tuple-element.107.source, f32[2,256,256]{2,1,0:T(8,128)S(1)} %get-tuple-element.108.carried), custom_call_target="tpu_custom_call" | custom-call | flops 1207959552 | bytes 4194304 | tf_op jit(solution)/shard_map/pallas_call | solution.py:67
  171.5 2.7 %shard_map.124 = (f32[2,2,256,256]{3,2,1,0:T(8,128)S(1)}, f32[2,2,256,256]{3,2,1,0:T(8,128)S(1)}, f32[2,256,256]{2,1,0:T(8,128)S(1)}) custom-call(s32[2]{0:T(128)S(1)} %pad_add_fusion.pick, f32[2,2,256,256]{3,2,1,0:T(8,128)S(1)} %get-tuple-element.93.link, f32[2,2,256,256]{3,2,1,0:T(8,128)S(1)} %get-tuple-element.94.source, ...), custom_call_target="tpu_custom_call" | custom-call | flops 1207959552 | bytes 9437192 | tf_op jit(solution)/shard_map/pallas_call | solution.py:67
  174.3 2.8 %collective-permute-start.18 = (f32[2,2,256,256]{3,2,1,0:T(8,128)S(1)}, f32[2,2,256,256]{3,2,1,0:T(8,128)S(1)}, u32[]{:S(2)}, u32[]{:S(2)}) collective-permute-start(f32[2,2,256,256]{3,2,1,0:T(8,128)S(1)} %get-tuple-element.115), channel_id=1, source_target_pairs={{0,4},{4,0},{8,12},{12,8},{16,20},{20,16},{24,28},{28,24},{1,5},{5... | collective-permute-start | bytes 3145736 | tf_op jit(solution)/shard_map/ppermute | solution.py:538
  177.0 3.5 %shard_map.125 = (f32[2,2,256,256]{3,2,1,0:T(8,128)S(1)}, f32[2,2,256,256]{3,2,1,0:T(8,128)S(1)}, f32[2,256,256]{2,1,0:T(8,128)}) custom-call(s32[2]{0:T(128)S(1)} %pad_add_fusion.pick, f32[2,2,256,256]{3,2,1,0:T(8,128)S(1)} %get-tuple-element.116.link, f32[2,2,256,256]{3,2,1,0:T(8,128)S(1)} %get-tuple-element.117.source, ...), custom_call_target="tpu_custom_call" | custom-call | flops 1207959552 | bytes 9437192 | tf_op jit(solution)/shard_map/pallas_call | solution.py:67
  180.8 2.6 %collective-permute-done.19 = f32[2,2,256,256]{3,2,1,0:T(8,128)S(1)} collective-permute-done((f32[2,2,256,256]{3,2,1,0:T(8,128)S(1)}, f32[2,2,256,256]{3,2,1,0:T(8,128)S(1)}, u32[]{:S(2)}, u32[]{:S(2)}) %collective-permute-start.19) | collective-permute-done | bytes 1048608 | tf_op jit(solution)/shard_map/ppermute | solution.py:538
  183.6 1.5 maximum_bitcast_fusion
  (73 shorter events, 12.0 us)
Async XLA Ops:
  0.6 74.4 %copy-start.12 = (s32[4]{0:T(128)S(1)}, s32[4]{0:T(128)}, u32[]{:S(2)}) copy-start(s32[4]{0:T(128)} %constant.55.clone) | copy-start | bytes 52
  0.6 84.8 %copy-start = (f32[1,4,2,256,256]{4,3,2,1,0:T(8,128)S(1)}, f32[1,4,2,256,256]{4,3,2,1,0:T(8,128)}, u32[]{:S(2)}) copy-start(f32[1,4,2,256,256]{4,3,2,1,0:T(8,128)} %param.14) | copy-start | bytes 6291460
  0.7 74.4 %copy-start.10 = (f32[4]{0:T(128)S(1)}, f32[4]{0:T(128)}, u32[]{:S(2)}) copy-start(f32[4]{0:T(128)} %param.17) | copy-start | bytes 52
  0.7 74.4 %copy-start.11 = (s32[4]{0:T(128)S(1)}, s32[4]{0:T(128)}, u32[]{:S(2)}) copy-start(s32[4]{0:T(128)} %param.16) | copy-start | bytes 52
  1.6 4.6 %collective-permute-start.1 = (f32[2,1,4,128]{3,2,0,1:T(4,128)S(1)}, f32[2,1,4,128]{3,2,0,1:T(4,128)S(1)}, u32[]{:S(2)}, u32[]{:S(2)}) collective-permute-start(f32[2,1,4,128]{3,2,0,1:T(4,128)S(1)} %get-tuple-element.124), channel_id=1, source_target_pairs={{0,1},{2,3},{1,0},{3,2},{4,5},{6,7},{5,4},{7,6},{8,9},{10,11},{9,8... | collective-permute-start | bytes 12296 | tf_op jit(solution)/shard_map/ppermute | solution.py:343
  1.7 5.3 %collective-permute-start = (f32[2,1,4,128]{3,2,0,1:T(4,128)S(1)}, f32[2,1,4,128]{3,2,0,1:T(4,128)S(1)}, u32[]{:S(2)}, u32[]{:S(2)}) collective-permute-start(f32[2,1,4,128]{3,2,0,1:T(4,128)S(1)} %bitcast.62), channel_id=1, source_target_pairs={{1,2},{2,1},{5,6},{6,5},{9,10},{10,9},{13,14},{14,13},{17,18},{18,... | collective-permute-start | bytes 12296 | tf_op jit(solution)/shard_map/ppermute | solution.py:344
  7.7 75.1 %copy-start.7 = (f32[1,1,8,128]{3,2,0,1:T(8,128)S(1)}, f32[1,1,8,128]{3,2,0,1:T(8,128)}, u32[]{:S(2)}) copy-start(f32[1,1,8,128]{3,2,0,1:T(8,128)} %get-tuple-element.159) | copy-start | bytes 12292
  7.7 75.1 %copy-start.8 = (f32[1,1,8,128]{3,2,0,1:T(8,128)S(1)}, f32[1,1,8,128]{3,2,0,1:T(8,128)}, u32[]{:S(2)}) copy-start(f32[1,1,8,128]{3,2,0,1:T(8,128)} %get-tuple-element.160) | copy-start | bytes 12292
  73.7 2.9 %collective-permute-start.2 = (f32[40,128]{1,0:T(8,128)}, f32[40,128]{1,0:T(8,128)S(1)}, u32[]{:S(2)}, u32[]{:S(2)}) collective-permute-start(f32[40,128]{1,0:T(8,128)} %get-tuple-element.63), channel_id=1, source_target_pairs={{0,8},{4,12},{8,0},{12,4},{16,24},{20,28},{24,16},{28,20},{1,9},{5... | collective-permute-start | bytes 61448 | tf_op jit(solution)/shard_map/ppermute | solution.py:286
  78.1 4.3 %collective-permute-start.3 = (f32[104,128]{1,0:T(8,128)S(1)}, f32[104,128]{1,0:T(8,128)S(1)}, u32[]{:S(2)}, u32[]{:S(2)}) collective-permute-start(f32[104,128]{1,0:T(8,128)S(1)} %pad_maximum_fusion), channel_id=1, source_target_pairs={{0,4},{4,0},{8,12},{12,8},{16,20},{20,16},{24,28},{28,24},{1,5},{5... | collective-permute-start | bytes 159752 | tf_op jit(solution)/shard_map/ppermute | solution.py:286
  81.2 25.0 %collective-permute-start.6 = (f32[2,2,256,256]{3,2,1,0:T(8,128)}, f32[2,2,256,256]{3,2,1,0:T(8,128)S(1)}, u32[]{:S(2)}, u32[]{:S(2)}) collective-permute-start(f32[2,2,256,256]{3,2,1,0:T(8,128)} %get-tuple-element.72), channel_id=1, source_target_pairs={{0,8},{4,12},{8,0},{12,4},{16,24},{20,28},{24,16},{28,20},{1,9},{5... | collective-permute-start | bytes 3145736 | tf_op jit(solution)/shard_map/ppermute | solution.py:372
  82.4 3.0 %collective-permute-start.4 = (f32[40,128]{1,0:T(8,128)S(1)}, f32[40,128]{1,0:T(8,128)S(1)}, u32[]{:S(2)}, u32[]{:S(2)}) collective-permute-start(f32[40,128]{1,0:T(8,128)S(1)} %slice_add_fusion), channel_id=1, source_target_pairs={{0,16},{4,20},{8,24},{12,28},{16,0},{20,4},{24,8},{28,12},{1,17},{... | collective-permute-start | bytes 61448 | tf_op jit(solution)/shard_map/ppermute | solution.py:286
  87.0 12.0 %copy-start.9 = (f32[64,128]{1,0:T(8,128)S(1)}, f32[64,128]{1,0:T(8,128)}, u32[]{:S(2)}) copy-start(f32[64,128]{1,0:T(8,128)} %get-tuple-element.91) | copy-start | bytes 98308
  87.0 15.2 %copy-start.3 = (f32[16,4,128]{2,1,0:T(4,128)S(1)}, f32[16,4,128]{2,1,0:T(4,128)}, u32[]{:S(2)}) copy-start(f32[16,4,128]{2,1,0:T(4,128)} %param.12) | copy-start | bytes 98308
  87.0 15.2 %copy-start.4 = (f32[16,4,128]{2,1,0:T(4,128)S(1)}, f32[16,4,128]{2,1,0:T(4,128)}, u32[]{:S(2)}) copy-start(f32[16,4,128]{2,1,0:T(4,128)} %param.10) | copy-start | bytes 98308
  87.0 19.2 %copy-start.14 = (f32[1,2,256,256]{3,2,1,0:T(8,128)S(1)}, f32[1,2,256,256]{3,2,1,0:T(8,128)}, u32[]{:S(2)}) copy-start(f32[1,2,256,256]{3,2,1,0:T(8,128)} %get-tuple-element.79) | copy-start | bytes 1572868
  87.0 20.4 %copy-start.5 = (f32[4,256,256]{2,1,0:T(8,128)S(1)}, f32[4,256,256]{2,1,0:T(8,128)}, u32[]{:S(2)}) copy-start(f32[4,256,256]{2,1,0:T(8,128)} %param.18) | copy-start | bytes 3145732
  93.2 14.7 %collective-permute-start.5 = (f32[2,256,256]{2,1,0:T(8,128)S(1)}, f32[2,256,256]{2,1,0:T(8,128)S(1)}, u32[]{:S(2)}, u32[]{:S(2)}) collective-permute-start(f32[2,256,256]{2,1,0:T(8,128)S(1)} %get-tuple-element.69.whole_source), channel_id=1, source_target_pairs={{0,1},{1,2},{2,3},{4,5},{5,6},{6,7},{8,9},{9,10},{10,11},{12,13},{... | collective-permute-start | bytes 1572872 | tf_op jit(solution)/shard_map/ppermute | solution.py:458
  96.9 24.4 %collective-permute-start.9 = (f32[1,2,256,256]{3,2,1,0:T(8,128)S(1)}, f32[1,2,256,256]{3,2,1,0:T(8,128)S(1)}, u32[]{:S(2)}, u32[]{:S(2)}) collective-permute-start(f32[1,2,256,256]{3,2,1,0:T(8,128)S(1)} %copy-done.13), channel_id=1, source_target_pairs={{8,24},{12,28},{16,0},{20,4},{9,25},{13,29},{17,1},{21,5},{10,26},... | collective-permute-start | bytes 1572872 | tf_op jit(solution)/shard_map/ppermute | solution.py:374
  99.1 20.6 %collective-permute-start.13 = (f32[64,128]{1,0:T(8,128)S(1)}, f32[64,128]{1,0:T(8,128)S(1)}, u32[]{:S(2)}, u32[]{:S(2)}) collective-permute-start(f32[64,128]{1,0:T(8,128)S(1)} %copy-done.9), channel_id=1, source_target_pairs={{4,8},{12,16},{20,24},{8,4},{16,12},{24,20},{5,9},{13,17},{21,25},... | collective-permute-start | bytes 98312 | tf_op jit(solution)/shard_map/ppermute | solution.py:399
  106.2 13.5 %copy-start.2 = (f32[4,2,256,256]{3,2,1,0:T(8,128)S(1)}, f32[4,2,256,256]{3,2,1,0:T(8,128)}, u32[]{:S(2)}) copy-start(f32[4,2,256,256]{3,2,1,0:T(8,128)} %refs_2_.3) | copy-start | bytes 6291460
  106.2 12.7 %collective-permute-start.8 = (f32[1,2,256,256]{3,2,1,0:T(8,128)S(1)}, f32[1,2,256,256]{3,2,1,0:T(8,128)S(1)}, u32[]{:S(2)}, u32[]{:S(2)}) collective-permute-start(f32[1,2,256,256]{3,2,1,0:T(8,128)S(1)} %copy-done.14), channel_id=1, source_target_pairs={{0,8},{4,12},{8,0},{12,4},{16,24},{20,28},{24,16},{28,20},{1,9},{5... | collective-permute-start | bytes 1572872 | tf_op jit(solution)/shard_map/ppermute | solution.py:383
  108.9 13.8 %collective-permute-start.7 = (f32[2,256,256]{2,1,0:T(8,128)S(1)}, f32[2,256,256]{2,1,0:T(8,128)S(1)}, u32[]{:S(2)}, u32[]{:S(2)}) collective-permute-start(f32[2,256,256]{2,1,0:T(8,128)S(1)} %shard_map.115), channel_id=1, source_target_pairs={{0,1},{1,2},{2,3},{4,5},{5,6},{6,7},{8,9},{9,10},{10,11},{12,13},{... | collective-permute-start | bytes 1572872 | tf_op jit(solution)/shard_map/ppermute | solution.py:458
  112.5 23.9 %collective-permute-start.12 = (f32[2,2,256,256]{3,2,1,0:T(8,128)S(1)}, f32[2,2,256,256]{3,2,1,0:T(8,128)S(1)}, u32[]{:S(2)}, u32[]{:S(2)}) collective-permute-start(f32[2,2,256,256]{3,2,1,0:T(8,128)S(1)} %collective-permute-done.6.refs_0_), channel_id=1, source_target_pairs={{0,16},{4,20},{8,24},{12,28},{16,0},{20,4},{24,8},{28,12},{1,17},{... | collective-permute-start | bytes 3145736 | tf_op jit(solution)/shard_map/ppermute | solution.py:379
  118.9 11.7 %collective-permute-start.11 = (f32[1,2,256,256]{3,2,1,0:T(8,128)S(1)}, f32[1,2,256,256]{3,2,1,0:T(8,128)S(1)}, u32[]{:S(2)}, u32[]{:S(2)}) collective-permute-start(f32[1,2,256,256]{3,2,1,0:T(8,128)S(1)} %copy-done.13), channel_id=1, source_target_pairs={{0,8},{4,12},{8,0},{12,4},{16,24},{20,28},{24,16},{28,20},{1,9},{5... | collective-permute-start | bytes 1572872 | tf_op jit(solution)/shard_map/ppermute | solution.py:383
  123.6 16.0 %collective-permute-start.10 = (f32[2,256,256]{2,1,0:T(8,128)S(1)}, f32[2,256,256]{2,1,0:T(8,128)S(1)}, u32[]{:S(2)}, u32[]{:S(2)}) collective-permute-start(f32[2,256,256]{2,1,0:T(8,128)S(1)} %shard_map.117), channel_id=1, source_target_pairs={{0,1},{1,2},{2,3},{4,5},{5,6},{6,7},{8,9},{9,10},{10,11},{12,13},{... | collective-permute-start | bytes 1572872 | tf_op jit(solution)/shard_map/ppermute | solution.py:476
  127.4 30.5 %collective-permute-start.16 = (f32[1,2,256,256]{3,2,1,0:T(8,128)S(1)}, f32[1,2,256,256]{3,2,1,0:T(8,128)S(1)}, u32[]{:S(2)}, u32[]{:S(2)}) collective-permute-start(f32[1,2,256,256]{3,2,1,0:T(8,128)S(1)} %collective-permute-done.8.refs_0_), channel_id=1, source_target_pairs={{0,16},{4,20},{8,24},{12,28},{16,0},{20,4},{24,8},{28,12},{1,17},{... | collective-permute-start | bytes 1572872 | tf_op jit(solution)/shard_map/ppermute | solution.py:379
  130.6 27.3 %collective-permute-start.17 = (f32[1,2,256,256]{3,2,1,0:T(8,128)S(1)}, f32[1,2,256,256]{3,2,1,0:T(8,128)S(1)}, u32[]{:S(2)}, u32[]{:S(2)}) collective-permute-start(f32[1,2,256,256]{3,2,1,0:T(8,128)S(1)} %collective-permute-done.9), channel_id=1, source_target_pairs={{24,16},{28,20},{0,8},{4,12},{25,17},{29,21},{1,9},{5,13},{26,18},... | collective-permute-start | bytes 1572872 | tf_op jit(solution)/shard_map/ppermute | solution.py:482
  132.7 32.8 %collective-permute-start.15 = (f32[2,256,256]{2,1,0:T(8,128)S(1)}, f32[2,256,256]{2,1,0:T(8,128)S(1)}, u32[]{:S(2)}, u32[]{:S(2)}) collective-permute-start(f32[2,256,256]{2,1,0:T(8,128)S(1)} %shard_map.117), channel_id=1, source_target_pairs={{8,17},{9,18},{10,19},{12,21},{13,22},{14,23},{16,9},{17,10},{18,1... | collective-permute-start | bytes 1572872 | tf_op jit(solution)/shard_map/ppermute | solution.py:477
  139.6 31.9 %collective-permute-start.14 = (f32[2,256,256]{2,1,0:T(8,128)S(1)}, f32[2,256,256]{2,1,0:T(8,128)S(1)}, u32[]{:S(2)}, u32[]{:S(2)}) collective-permute-start(f32[2,256,256]{2,1,0:T(8,128)S(1)} %collective-permute-done.10.carried), channel_id=1, source_target_pairs={{0,8},{4,12},{8,0},{12,4},{16,24},{20,28},{24,16},{28,20},{1,9},{5... | collective-permute-start | bytes 1572872 | tf_op jit(solution)/shard_map/ppermute | solution.py:486
  174.3 6.3 %collective-permute-start.18 = (f32[2,2,256,256]{3,2,1,0:T(8,128)S(1)}, f32[2,2,256,256]{3,2,1,0:T(8,128)S(1)}, u32[]{:S(2)}, u32[]{:S(2)}) collective-permute-start(f32[2,2,256,256]{3,2,1,0:T(8,128)S(1)} %get-tuple-element.115), channel_id=1, source_target_pairs={{0,4},{4,0},{8,12},{12,8},{16,20},{20,16},{24,28},{28,24},{1,5},{5... | collective-permute-start | bytes 3145736 | tf_op jit(solution)/shard_map/ppermute | solution.py:538
  180.7 2.7 %collective-permute-start.19 = (f32[2,2,256,256]{3,2,1,0:T(8,128)S(1)}, f32[2,2,256,256]{3,2,1,0:T(8,128)S(1)}, u32[]{:S(2)}, u32[]{:S(2)}) collective-permute-start(f32[2,2,256,256]{3,2,1,0:T(8,128)S(1)} %get-tuple-element.123), channel_id=1, source_target_pairs={{0,4},{4,0},{8,12},{12,8},{16,20},{20,16},{24,28},{28,24},{1,5},{5... | collective-permute-start | bytes 3145736 | tf_op jit(solution)/shard_map/ppermute | solution.py:538
  (3 other events, 22.0 us)

commit v8 on v7

--- a/solution.py
+++ b/solution.py
@@ -77,13 +77,15 @@
     return jax.ShapeDtypeStruct(dims, jnp.float32)
 
 
-def gather_kernel(rows, peers, sizes, mine, field, perm, charge, before, after, owner, free, *refs):
-    out, ends, *parts, sems = refs
-    taken = []
-    for index, part in enumerate(parts):
-        cut = free.at[pl.ds(sum(sizes[:index]), sizes[index])]
-        taken.append(pltpu.make_async_copy(cut, part, sems.at[index]))
-        taken[-1].start()
+def gather_kernel(rows, peers, mine, field, perm, charge, before, after, owner, free, *refs):
+    out, ends, *parts, held, here, gone = refs
+    loads, stores = [], []
+    for index in range(len(parts)):
+        slab = free.at[index + 1 : index + 2]
+        loads.append(
+            pltpu.make_async_copy(slab, held.at[index : index + 1], here.at[index])
+        )
+        loads[-1].start()
     total, depth = charge.shape
     count, orbitals = owner.shape
     height = total // count
@@ -117,6 +119,13 @@
     first_row = mine[0] * rows
     step = 0
     for slab in range(count):
+        if slab == count // 2:
+            for index, part in enumerate(parts):
+                loads[index].wait()
+                stores.append(
+                    pltpu.make_async_copy(held.at[index : index + 1], part, gone.at[index])
+                )
+                stores[-1].start()
         cells = owner[slab : slab + 1, :]
         lane, line = cells % depth, cells // depth
         across, along = line % cross - first_row, line // cross * rows
@@ -153,8 +162,8 @@
                 pl.ds(end, total // rows, stride=rows), :
             ]
             start += total // rows
-    for copy in taken:
-        copy.wait()
+    for store in stores:
+        store.wait()
 
 
 def sums_row(kind, slab, count, pieces):
@@ -275,12 +284,13 @@
     )
 
 
-def exchanged(sums, ends):
+def exchanged(sums, ends, early):
     peers = lax.axis_size("energy")
     assert peers >= 4 and peers & (peers - 1) == 0
     masks = [2, 1] + [1 << k for k in range(2, peers.bit_length() - 1)]
     rows, twin_ends = sums.shape[0], None
     first = None
+    sums, early = lax.optimization_barrier((sums, early))
     for mask in masks:
         given = jnp.concatenate([sums, ends]) if mask == 1 else sums
         arrived = lax.ppermute(given, "energy", [(e, e ^ mask) for e in range(peers)])
@@ -288,7 +298,7 @@
             twin_ends = arrived[rows:]
         sums = sums + arrived[:rows]
         first = sums if first is None else first
-    return sums, twin_ends, first
+    return sums, twin_ends, first, early
 
 
 def per_device(
@@ -315,20 +325,20 @@
         first_pairs = [(e, e ^ 2) for e in everyone]
         second_pairs = [(2, 4), (3, 5), (4, 2), (5, 3)]
         relay_pairs = [(e, e ^ 4) for e in everyone]
-        around_pairs = [(2, 6), (3, 7), (4, 0), (5, 1)]
-        back_pairs = [(6, 4), (7, 5), (0, 2), (1, 3)]
         turned = (mine // 2) % 2
         has_second = jnp.where((mine >= 2) & (mine < 6), 1, 0)
     else:
         first_pairs = [(e, e - 2) for e in everyone if e >= 2]
         second_pairs = [(e, e + 2) for e in everyone if e + 2 < energies]
-        relay_pairs = back_pairs = second_pairs
+        relay_pairs = second_pairs
         turned = jnp.zeros_like(mine)
         has_second = jnp.ones_like(mine)
     twin_pairs = [(e, e ^ 1) for e in everyone]
 
     half = count // 2
-    sizes = (half,) + (1,) * (count - half)
+    one_slab = shape(1, 2, width, width)
+    first_cut = free[:1]
+    free_first = [lax.ppermute(first_cut, "energy", first_pairs)]
 
     place = lax.axis_index("slab")
     wire_up = [(i, i + 1) for i in range(peers - 1)]
@@ -337,7 +347,9 @@
         pairs = [(i, i + 1) for i in range(start, peers - 1, 2)]
         return pairs + [(j, i) for i, j in pairs]
 
-    stacked = jnp.stack([potential_old, permittivity])
+    first_cut, stacked = lax.optimization_barrier(
+        (first_cut, jnp.stack([potential_old, permittivity]))
+    )
     lower, upper = end_planes(stacked, 1)
     even = place % 2 == 0
     arrived = lax.ppermute(jnp.where(even, upper, lower), "slab", swaps(0))
@@ -348,13 +360,13 @@
     cells, rows, depth = charge.shape
     far, near = pl.BlockSpec(memory_space=pl.ANY), pl.BlockSpec(memory_space=pltpu.VMEM)
     sums, ends, *cuts = call(
-        functools.partial(gather_kernel, rows, energies, sizes),
+        functools.partial(gather_kernel, rows, energies),
         56,
         1,
         (
             shape(5 * count * (width // depth), depth),
             shape(4 * cells, depth),
-            *(shape(size, 2, width, width) for size in sizes),
+            *[one_slab] * (count - 1),
         ),
         jnp.reshape(mine, (1,)),
         *(array.reshape(-1, depth) for array in (potential_old, permittivity, charge)),
@@ -363,15 +375,19 @@
         owner_cell,
         free,
         in_specs=[pl.BlockSpec(memory_space=pltpu.SMEM)] + [near] * 6 + [far],
-        out_specs=(near, near, *(far for _ in sizes)),
-        scratch_shapes=[pltpu.SemaphoreType.DMA((len(sizes),))],
-    )
-    sums, twin_ends, crossed = exchanged(sums, ends)
-
-    crossed, cuts[0] = lax.optimization_barrier((crossed, cuts[0]))
-    free_first = [lax.ppermute(cuts[0], "energy", first_pairs)]
-    sums, cuts[-1] = lax.optimization_barrier((sums, cuts[-1]))
-    around = lax.ppermute(cuts[-1], "energy", around_pairs) if relayed else cuts[-1]
+        out_specs=(near, near, *[far] * (count - 1)),
+        scratch_shapes=[
+            pltpu.VMEM((count - 1, 2, width, width), jnp.float32),
+            pltpu.SemaphoreType.DMA((count - 1,)),
+            pltpu.SemaphoreType.DMA((count - 1,)),
+        ],
+    )
+    cuts = [first_cut, *cuts]
+    sums, twin_ends, crossed, arrived = exchanged(sums, ends, free_first[0])
+
+    crossed, cuts[1] = lax.optimization_barrier((crossed, cuts[1]))
+    sums, arrived = lax.optimization_barrier((sums, arrived))
+    free_first = [arrived, lax.ppermute(cuts[1], "energy", first_pairs)]
     free_second = []
 
     def sent_on(part):
@@ -382,6 +398,7 @@
         free_first[part - 1], cut = lax.optimization_barrier((free_first[part - 1], cuts[part]))
         free_first.append(lax.ppermute(cut, "energy", first_pairs))
 
+    sent_on(0)
     whole_map, whole_source = call(
         own_kernel,
         32,
@@ -457,16 +474,17 @@
     for hop in range(1, peers - 1):
         arrived = lax.ppermute(leaving, "slab", wire_up)
         if hop == 1:
-            sent_on(0)
-            sent_after(1)
-            arrived, weights, free_first[0] = lax.optimization_barrier(
-                (arrived, weights, free_first[0])
+            sent_on(1)
+            sent_after(2)
+            arrived, weights, free_first[1] = lax.optimization_barrier(
+                (arrived, weights, free_first[1])
             )
         if hop == 2:
-            sent_after(2)
-            beside_first[0] = beside(0, free_first[:1])
-            arrived, beside_first[0], free_first[1], around = lax.optimization_barrier(
-                (arrived, beside_first[0], free_first[1], around)
+            sent_on(2)
+            sent_after(3)
+            beside_first[0] = beside(0, free_first[:2])
+            arrived, beside_first[0], free_first[2], *free_second[:2] = lax.optimization_barrier(
+                (arrived, beside_first[0], free_first[2], *free_second[:2])
             )
         leaving = call(hop_kernel, 12, 2, whole, whole_map, whole_source, arrived)
 
@@ -475,18 +493,16 @@
 
     carried = lax.ppermute(leaving, "slab", wire_up)
     carried_second = lax.ppermute(leaving, ("energy", "slab"), both(second_pairs))
-    sent_on(1)
-    beside_second[0] = beside(0, free_second[:1])
-    beside_first[1] = beside(1, free_first[1:])
-    free_first[2], around = lax.optimization_barrier((free_first[2], around))
-    free_second.append(lax.ppermute(around, "energy", back_pairs))
-    carried, beside_first[1], beside_second[0], potential_new = lax.optimization_barrier(
-        (carried, beside_first[1], beside_second[0], potential_new)
+    sent_on(3)
+    beside_second[0] = beside(0, free_second[:2])
+    beside_first[1] = beside(1, free_first[2:])
+    carried, beside_first[1], beside_second[0], potential_new, free_second[2] = (
+        lax.optimization_barrier(
+            (carried, beside_first[1], beside_second[0], potential_new, free_second[2])
+        )
     )
     carried_first = lax.ppermute(carried, "energy", first_pairs)
-    carried, free_second[1], free_second[2] = lax.optimization_barrier(
-        (carried, free_second[1], free_second[2])
-    )
+    carried, free_second[3] = lax.optimization_barrier((carried, free_second[3]))
     greens, _ = call(
         functools.partial(own_greens_kernel, count),
         24,
@@ -500,7 +516,7 @@
         in_specs=[block, block, pl.BlockSpec(sums.shape, lambda s: (0, 0)), one_state],
         out_specs=(block, one_state),
     )
-    beside_second[1] = beside(1, free_second[1:])
+    beside_second[1] = beside(1, free_second[2:])
     carried_second, greens = lax.optimization_barrier((carried_second, greens))
     greens_second = []
     for part in beside_second:

time: 186 us -> 121 us (0.65)
  Pallas kernels: 98.6 us -> 35.9 us
    pallas_call x13, Pallas kernels: 98.6 us -> 35.9 us  [call(): pl.pallas_call(kernel, out_shape=out_shapes, cost_estimate=cost, compiler...]
    ppermute x2 -> x4, starting transfers between devices: 0.57 us -> 4.6 us  [sent_on(): free_second.append(lax.ppermute(given, 'energy', relay_pairs))]
    ppermute x3 -> x2, waiting for transfers between devices: 3.93 us -> 0.66 us  [the longest x1 0.65 us: per_device(): free_first = [lax.ppermute(first_cut, 'energy', first_pairs)]]
    ppermute x2, waiting for transfers between devices: 1.35 us -> 3.91 us  [per_device(): arrived = lax.ppermute(leaving, 'slab', wire_up)]
    ppermute x3 -> x2, starting transfers between devices: 4.67 us -> 2.55 us  [the longest x1 1.28 us: per_device(): free_first = [lax.ppermute(first_cut, 'energy', first_pairs)]]
    ppermute x2, starting transfers between devices: 2.04 us -> 0.07 us  [sent_after(): free_first.append(lax.ppermute(cut, 'energy', first_pairs))]
    ppermute x2 -> x4, waiting for transfers between devices: 18.2 us -> 18.9 us  [sent_on(): free_second.append(lax.ppermute(given, 'energy', relay_pairs))]
  transfers between devices with their start and end apart: 20 -> 21, of which waited for: 9 -> 12; matrix products, arithmetic and copies ran while one was open for 1% -> 2% of each run, Pallas kernels for 16% -> 28%
where the time goes in v8:
time: 121 us
  waiting for transfers between devices  39 us (32%)
  Pallas kernels  35.9 us (30%)
  starting transfers between devices  35.5 us (29%)
  other arithmetic  6.09 us (5%)
  local copies, waits for them, and re-layouts  3.02 us (2%)
    pallas_call x13, Pallas kernels, call(): pl.pallas_call(kernel, out_shape=out_shapes, cost_estimate=cost, compiler...  35.9 us
    ppermute x4, waiting for transfers between devices, sent_on(): free_second.append(lax.ppermute(given, 'energy', relay_pairs))  18.9 us
    ppermute x2, waiting for transfers between devices, sent_after(): free_first.append(lax.ppermute(cut, 'energy', first_pairs))  8.23 us
    ppermute x2, starting transfers between devices, per_device(): arrived = lax.ppermute(leaving, 'slab', wire_up)  6.83 us
    ppermute x1, starting transfers between devices, per_device(): lax.ppermute(ends, 'energy', beyond + [(b, a) for a, b in beyond])  4.94 us
    ppermute x4, starting transfers between devices, sent_on(): free_second.append(lax.ppermute(given, 'energy', relay_pairs))  4.6 us
    ppermute x1, starting transfers between devices, per_device(): crossed = lax.ppermute(jnp.where(even, lower, upper), 'slab', swaps(1))  4.32 us
    ppermute x3, starting transfers between devices, exchanged(): lax.ppermute(given, 'energy', [(e, e ^ mask) for e in range(peers)])  4.13 us
  transfers between devices with their start and end apart: 21, of which 12 were waited for; matrix products, arithmetic and copies ran while one was open for 2% of the time, Pallas kernels for 28%

profile of v8, /device:TPU:13, one launch (start us, length us, event | category | flops | bytes accessed | tf_op | source)
XLA Modules:
  0.0 120.6 jit_solution(7847837534531033694)
XLA Ops:
  1.9 1.3 %collective-permute-start.2 = (f32[1,2,256,256]{3,2,1,0:T(8,128)S(1)}, f32[1,2,256,256]{3,2,1,0:T(8,128)S(1)}, u32[]{:S(2)}, u32[]{:S(2)}) collective-permute-start(f32[1,2,256,256]{3,2,1,0:T(8,128)S(1)} %slice_bitcast_fusion), channel_id=1, source_target_pairs={{0,8},{4,12},{8,0},{12,4},{16,24},{20,28},{24,16},{28,20},{1,9},{5... | collective-permute-start | bytes 1572872 | tf_op jit(solution)/shard_map/ppermute | solution.py:341
  4.2 4.3 %collective-permute-start = (f32[2,1,4,128]{3,2,0,1:T(4,128)S(1)}, f32[2,1,4,128]{3,2,0,1:T(4,128)S(1)}, u32[]{:S(2)}, u32[]{:S(2)}) collective-permute-start(f32[2,1,4,128]{3,2,0,1:T(4,128)S(1)} %get-tuple-element.133), channel_id=1, source_target_pairs={{1,2},{2,1},{5,6},{6,5},{9,10},{10,9},{13,14},{14,13},{17,18},{18,... | collective-permute-start | bytes 12296 | tf_op jit(solution)/shard_map/ppermute | solution.py:356
  10.4 3.7 %shard_map.113 = (f32[40,128]{1,0:T(8,128)}, f32[64,128]{1,0:T(8,128)}, f32[1,2,256,256]{3,2,1,0:T(8,128)}, f32[1,2,256,256]{3,2,1,0:T(8,128)}, f32[1,2,256,256]{3,2,1,0:T(8,128)}) custom-call(s32[1]{0:T(128)} %bitcast.1.mine, f32[64,128]{1,0:T(8,128)} %bitcast.47, f32[64,128]{1,0:T(8,128)} %bitcast.45, f32[64,128]{1,0:T(8,128)} %bitcast.48, ...), custom_call_target="tpu_custom_call" | custom-call | flops 301989888 | bytes 3833860 | tf_op jit(solution)/shard_map/pallas_call | solution.py:67
  16.0 1.6 %collective-permute-done.3 = f32[40,128]{1,0:T(8,128)S(1)} collective-permute-done((f32[40,128]{1,0:T(8,128)}, f32[40,128]{1,0:T(8,128)S(1)}, u32[]{:S(2)}, u32[]{:S(2)}) %collective-permute-start.3) | collective-permute-done | bytes 20512 | tf_op jit(solution)/shard_map/ppermute | solution.py:296
  19.1 2.7 %collective-permute-start.4 = (f32[104,128]{1,0:T(8,128)S(1)}, f32[104,128]{1,0:T(8,128)S(1)}, u32[]{:S(2)}, u32[]{:S(2)}) collective-permute-start(f32[104,128]{1,0:T(8,128)S(1)} %pad_maximum_fusion.1), channel_id=1, source_target_pairs={{0,4},{4,0},{8,12},{12,8},{16,20},{20,16},{24,28},{28,24},{1,5},{5... | collective-permute-start | bytes 159752 | tf_op jit(solution)/shard_map/ppermute | solution.py:296
  22.9 1.3 %collective-permute-start.7 = (f32[1,2,256,256]{3,2,1,0:T(8,128)}, f32[1,2,256,256]{3,2,1,0:T(8,128)S(1)}, u32[]{:S(2)}, u32[]{:S(2)}) collective-permute-start(f32[1,2,256,256]{3,2,1,0:T(8,128)} %get-tuple-element.77), channel_id=1, source_target_pairs={{0,8},{4,12},{8,0},{12,4},{16,24},{20,28},{24,16},{28,20},{1,9},{5... | collective-permute-start | bytes 1572872 | tf_op jit(solution)/shard_map/ppermute | solution.py:390
  25.3 1.6 %copy-done.1 = f32[4,2,256,256]{3,2,1,0:T(8,128)S(1)} copy-done((f32[4,2,256,256]{3,2,1,0:T(8,128)S(1)}, f32[4,2,256,256]{3,2,1,0:T(8,128)}, u32[]{:S(2)}) %copy-start.1) | copy-done | bytes 2097176
  26.9 6.3 %shard_map.114 = (f32[2,256,256]{2,1,0:T(8,128)S(1)}, f32[2,256,256]{2,1,0:T(8,128)S(1)}) custom-call(f32[4,2,256,256]{3,2,1,0:T(8,128)S(1)} %bitcast.42, f32[4,2,256,256]{3,2,1,0:T(8,128)S(1)} %copy-done.1, f32[40,128]{1,0:T(8,128)S(1)} %add.106.sums.refs_3_), custom_call_target="tpu_custom_call" | custom-call | flops 5133828096 | bytes 5263360 | tf_op jit(solution)/shard_map/pallas_call | solution.py:67
  33.2 3.3 %collective-permute-start.6 = (f32[2,256,256]{2,1,0:T(8,128)S(1)}, f32[2,256,256]{2,1,0:T(8,128)S(1)}, u32[]{:S(2)}, u32[]{:S(2)}) collective-permute-start(f32[2,256,256]{2,1,0:T(8,128)S(1)} %get-tuple-element.74.whole_source), channel_id=1, source_target_pairs={{0,1},{1,2},{2,3},{4,5},{5,6},{6,7},{8,9},{9,10},{10,11},{12,13},{... | collective-permute-start | bytes 1572872 | tf_op jit(solution)/shard_map/ppermute | solution.py:475
  36.9 4.9 %collective-permute-start.14 = (f32[64,128]{1,0:T(8,128)S(1)}, f32[64,128]{1,0:T(8,128)S(1)}, u32[]{:S(2)}, u32[]{:S(2)}) collective-permute-start(f32[64,128]{1,0:T(8,128)S(1)} %copy-done.9), channel_id=1, source_target_pairs={{4,8},{12,16},{20,24},{8,4},{16,12},{24,20},{5,9},{13,17},{21,25},... | collective-permute-start | bytes 98312 | tf_op jit(solution)/shard_map/ppermute | solution.py:416
  42.5 1.6 %collective-permute-start.11 = (f32[1,2,256,256]{3,2,1,0:T(8,128)S(1)}, f32[1,2,256,256]{3,2,1,0:T(8,128)S(1)}, u32[]{:S(2)}, u32[]{:S(2)}) collective-permute-start(f32[1,2,256,256]{3,2,1,0:T(8,128)S(1)} %collective-permute-done.7.refs_1_), channel_id=1, source_target_pairs={{0,16},{4,20},{8,24},{12,28},{16,0},{20,4},{24,8},{28,12},{1,17},{... | collective-permute-start | bytes 1572872 | tf_op jit(solution)/shard_map/ppermute | solution.py:395
  44.1 2.9 %collective-permute-done.6.carried = f32[2,256,256]{2,1,0:T(8,128)S(1)} collective-permute-done((f32[2,256,256]{2,1,0:T(8,128)S(1)}, f32[2,256,256]{2,1,0:T(8,128)S(1)}, u32[]{:S(2)}, u32[]{:S(2)}) %collective-permute-start.6) | collective-permute-done | bytes 524320 | tf_op jit(solution)/shard_map/ppermute | solution.py:475
  48.0 3.5 %collective-permute-start.8 = (f32[2,256,256]{2,1,0:T(8,128)S(1)}, f32[2,256,256]{2,1,0:T(8,128)S(1)}, u32[]{:S(2)}, u32[]{:S(2)}) collective-permute-start(f32[2,256,256]{2,1,0:T(8,128)S(1)} %shard_map.115), channel_id=1, source_target_pairs={{0,1},{1,2},{2,3},{4,5},{5,6},{6,7},{8,9},{9,10},{10,11},{12,13},{... | collective-permute-start | bytes 1572872 | tf_op jit(solution)/shard_map/ppermute | solution.py:475
  51.5 4.3 %collective-permute-done.9.refs_0_ = f32[1,2,256,256]{3,2,1,0:T(8,128)S(1)} collective-permute-done((f32[1,2,256,256]{3,2,1,0:T(8,128)S(1)}, f32[1,2,256,256]{3,2,1,0:T(8,128)S(1)}, u32[]{:S(2)}, u32[]{:S(2)}) %collective-permute-start.9) | collective-permute-done | bytes 524320 | tf_op jit(solution)/shard_map/ppermute | solution.py:399
  55.8 1.5 %shard_map.116 = (f32[2,2,256,256]{3,2,1,0:T(8,128)S(1)}, f32[2,2,256,256]{3,2,1,0:T(8,128)S(1)}) custom-call(f32[1,2,256,256]{3,2,1,0:T(8,128)S(1)} %collective-permute-done.2.refs_0_, f32[1,2,256,256]{3,2,1,0:T(8,128)S(1)} %collective-permute-done.7.refs_1_, f32[4,2,256,256]{3,2,1,0:T(8,128)S(1)} %copy-done.2, f32[40,128]{1,0:T(8,128)S(1)} %add.106.sums.refs_3_), custom_call_target="tpu_custom_call" | custom-call | flops 1207959552 | bytes 5263360 | tf_op jit(solution)/shard_map/pallas_call | solution.py:67
  57.4 1.5 %collective-permute-start.15 = (f32[1,2,256,256]{3,2,1,0:T(8,128)S(1)}, f32[1,2,256,256]{3,2,1,0:T(8,128)S(1)}, u32[]{:S(2)}, u32[]{:S(2)}) collective-permute-start(f32[1,2,256,256]{3,2,1,0:T(8,128)S(1)} %collective-permute-done.9.refs_0_), channel_id=1, source_target_pairs={{0,16},{4,20},{8,24},{12,28},{16,0},{20,4},{24,8},{28,12},{1,17},{... | collective-permute-start | bytes 1572872 | tf_op jit(solution)/shard_map/ppermute | solution.py:395
  61.8 3.3 %collective-permute-start.12 = (f32[2,256,256]{2,1,0:T(8,128)S(1)}, f32[2,256,256]{2,1,0:T(8,128)S(1)}, u32[]{:S(2)}, u32[]{:S(2)}) collective-permute-start(f32[2,256,256]{2,1,0:T(8,128)S(1)} %shard_map.117), channel_id=1, source_target_pairs={{0,1},{1,2},{2,3},{4,5},{5,6},{6,7},{8,9},{9,10},{10,11},{12,13},{... | collective-permute-start | bytes 1572872 | tf_op jit(solution)/shard_map/ppermute | solution.py:494
  65.1 3.9 %collective-permute-done.13.refs_1_ = f32[1,2,256,256]{3,2,1,0:T(8,128)S(1)} collective-permute-done((f32[1,2,256,256]{3,2,1,0:T(8,128)S(1)}, f32[1,2,256,256]{3,2,1,0:T(8,128)S(1)}, u32[]{:S(2)}, u32[]{:S(2)}) %collective-permute-start.13) | collective-permute-done | bytes 524320 | tf_op jit(solution)/shard_map/ppermute | solution.py:399
  69.0 1.2 %collective-permute-start.18 = (f32[1,2,256,256]{3,2,1,0:T(8,128)S(1)}, f32[1,2,256,256]{3,2,1,0:T(8,128)S(1)}, u32[]{:S(2)}, u32[]{:S(2)}) collective-permute-start(f32[1,2,256,256]{3,2,1,0:T(8,128)S(1)} %collective-permute-done.13.refs_1_), channel_id=1, source_target_pairs={{0,16},{4,20},{8,24},{12,28},{16,0},{20,4},{24,8},{28,12},{1,17},{... | collective-permute-start | bytes 1572872 | tf_op jit(solution)/shard_map/ppermute | solution.py:395
  71.1 2.3 %collective-permute-start.17 = (f32[2,256,256]{2,1,0:T(8,128)S(1)}, f32[2,256,256]{2,1,0:T(8,128)S(1)}, u32[]{:S(2)}, u32[]{:S(2)}) collective-permute-start(f32[2,256,256]{2,1,0:T(8,128)S(1)} %shard_map.117), channel_id=1, source_target_pairs={{8,17},{9,18},{10,19},{12,21},{13,22},{14,23},{16,9},{17,10},{18,1... | collective-permute-start | bytes 1572872 | tf_op jit(solution)/shard_map/ppermute | solution.py:495
  73.4 1.4 %shard_map.119 = (f32[2,2,256,256]{3,2,1,0:T(8,128)S(1)}, f32[2,2,256,256]{3,2,1,0:T(8,128)S(1)}) custom-call(f32[1,2,256,256]{3,2,1,0:T(8,128)S(1)} %collective-permute-done.10.refs_0_, f32[1,2,256,256]{3,2,1,0:T(8,128)S(1)} %collective-permute-done.11.refs_1_, f32[4,2,256,256]{3,2,1,0:T(8,128)S(1)} %copy-done.2, f32[40,128]{1,0:T(8,128)S(1)} %add.106.sums.refs_3_), custom_call_target="tpu_custom_call" | custom-call | flops 1207959552 | bytes 5263360 | tf_op jit(solution)/shard_map/pallas_call | solution.py:67
  74.9 1.4 %shard_map.118 = (f32[2,2,256,256]{3,2,1,0:T(8,128)S(1)}, f32[2,2,256,256]{3,2,1,0:T(8,128)S(1)}) custom-call(f32[1,2,256,256]{3,2,1,0:T(8,128)S(1)} %collective-permute-done.9.refs_0_, f32[1,2,256,256]{3,2,1,0:T(8,128)S(1)} %collective-permute-done.13.refs_1_, f32[4,2,256,256]{3,2,1,0:T(8,128)S(1)} %copy-done.2, f32[40,128]{1,0:T(8,128)S(1)} %add.106.sums.refs_3_), custom_call_target="tpu_custom_call" | custom-call | flops 1207959552 | bytes 5263360 | tf_op jit(solution)/shard_map/pallas_call | solution.py:67
  76.4 17.8 %collective-permute-done.18.refs_1_ = f32[1,2,256,256]{3,2,1,0:T(8,128)S(1)} collective-permute-done((f32[1,2,256,256]{3,2,1,0:T(8,128)S(1)}, f32[1,2,256,256]{3,2,1,0:T(8,128)S(1)}, u32[]{:S(2)}, u32[]{:S(2)}) %collective-permute-start.18) | collective-permute-done | bytes 524320 | tf_op jit(solution)/shard_map/ppermute | solution.py:395
  94.3 7.5 %shard_map.120 = (f32[4,2,256,256]{3,2,1,0:T(8,128)S(1)}, f32[2,256,256]{2,1,0:T(8,128)}) custom-call(f32[4,2,256,256]{3,2,1,0:T(8,128)S(1)} %bitcast.43, f32[4,2,256,256]{3,2,1,0:T(8,128)S(1)} %copy-done.2, f32[40,128]{1,0:T(8,128)S(1)} %add.106.sums.refs_3_, f32[2,256,256]{2,1,0:T(8,128)S(1)} %collective-permute-done.12.carried), custom_call_target="tpu_custom_call" | custom-call | flops 4831838208 | bytes 7360512 | tf_op jit(solution)/shard_map/pallas_call | solution.py:67
  101.8 1.5 %shard_map.122 = (f32[2,2,256,256]{3,2,1,0:T(8,128)S(1)}, f32[2,2,256,256]{3,2,1,0:T(8,128)S(1)}) custom-call(f32[1,2,256,256]{3,2,1,0:T(8,128)S(1)} %collective-permute-done.15.refs_0_, f32[1,2,256,256]{3,2,1,0:T(8,128)S(1)} %collective-permute-done.18.refs_1_, f32[4,2,256,256]{3,2,1,0:T(8,128)S(1)} %copy-done.2, f32[40,128]{1,0:T(8,128)S(1)} %add.106.sums.refs_3_), custom_call_target="tpu_custom_call" | custom-call | flops 1207959552 | bytes 5263360 | tf_op jit(solution)/shard_map/pallas_call | solution.py:67
  103.3 1.9 %shard_map.121 = (f32[2,2,256,256]{3,2,1,0:T(8,128)S(1)}, f32[2,256,256]{2,1,0:T(8,128)S(1)}) custom-call(f32[2,2,256,256]{3,2,1,0:T(8,128)S(1)} %get-tuple-element.104.link, f32[2,2,256,256]{3,2,1,0:T(8,128)S(1)} %get-tuple-element.105.source, f32[2,256,256]{2,1,0:T(8,128)S(1)} %collective-permute-done.17.carried), custom_call_target="tpu_custom_call" | custom-call | flops 1207959552 | bytes 4194304 | tf_op jit(solution)/shard_map/pallas_call | solution.py:67
  105.2 2.7 %shard_map.123 = (f32[2,2,256,256]{3,2,1,0:T(8,128)S(1)}, f32[2,256,256]{2,1,0:T(8,128)}) custom-call(f32[2,2,256,256]{3,2,1,0:T(8,128)S(1)} %get-tuple-element.112.link, f32[2,2,256,256]{3,2,1,0:T(8,128)S(1)} %get-tuple-element.113.source, f32[2,256,256]{2,1,0:T(8,128)S(1)} %get-tuple-element.114.carried), custom_call_target="tpu_custom_call" | custom-call | flops 1207959552 | bytes 4194304 | tf_op jit(solution)/shard_map/pallas_call | solution.py:67
  107.9 2.6 %shard_map.124 = (f32[2,2,256,256]{3,2,1,0:T(8,128)S(1)}, f32[2,2,256,256]{3,2,1,0:T(8,128)S(1)}, f32[2,256,256]{2,1,0:T(8,128)S(1)}) custom-call(s32[2]{0:T(128)S(1)} %pad_add_fusion.pick, f32[2,2,256,256]{3,2,1,0:T(8,128)S(1)} %get-tuple-element.101.link, f32[2,2,256,256]{3,2,1,0:T(8,128)S(1)} %get-tuple-element.102.source, ...), custom_call_target="tpu_custom_call" | custom-call | flops 1207959552 | bytes 9437192 | tf_op jit(solution)/shard_map/pallas_call | solution.py:67
  110.6 2.0 %collective-permute-start.19 = (f32[2,2,256,256]{3,2,1,0:T(8,128)S(1)}, f32[2,2,256,256]{3,2,1,0:T(8,128)S(1)}, u32[]{:S(2)}, u32[]{:S(2)}) collective-permute-start(f32[2,2,256,256]{3,2,1,0:T(8,128)S(1)} %get-tuple-element.121), channel_id=1, source_target_pairs={{0,4},{4,0},{8,12},{12,8},{16,20},{20,16},{24,28},{28,24},{1,5},{5... | collective-permute-start | bytes 3145736 | tf_op jit(solution)/shard_map/ppermute | solution.py:554
  112.6 3.5 %shard_map.125 = (f32[2,2,256,256]{3,2,1,0:T(8,128)S(1)}, f32[2,2,256,256]{3,2,1,0:T(8,128)S(1)}, f32[2,256,256]{2,1,0:T(8,128)}) custom-call(s32[2]{0:T(128)S(1)} %pad_add_fusion.pick, f32[2,2,256,256]{3,2,1,0:T(8,128)S(1)} %get-tuple-element.122.link, f32[2,2,256,256]{3,2,1,0:T(8,128)S(1)} %get-tuple-element.123.source, ...), custom_call_target="tpu_custom_call" | custom-call | flops 1207959552 | bytes 9437192 | tf_op jit(solution)/shard_map/pallas_call | solution.py:67
  116.3 2.6 %collective-permute-done.20 = f32[2,2,256,256]{3,2,1,0:T(8,128)S(1)} collective-permute-done((f32[2,2,256,256]{3,2,1,0:T(8,128)S(1)}, f32[2,2,256,256]{3,2,1,0:T(8,128)S(1)}, u32[]{:S(2)}, u32[]{:S(2)}) %collective-permute-start.20) | collective-permute-done | bytes 1048608 | tf_op jit(solution)/shard_map/ppermute | solution.py:554
  119.1 1.5 %maximum_bitcast_fusion = f32[1,4,2,256,256]{4,3,2,1,0:T(8,128)} fusion(f32[2,2,256,256]{3,2,1,0:T(8,128)S(1)} %add.130, f32[2,2,256,256]{3,2,1,0:T(8,128)S(1)} %add.129), kind=kLoop, calls=%fused_computation.1 | loop fusion | flops 524288 | bytes 4194304 | tf_op jit(solution)/shard_map/broadcast_in_dim | solution.py:555
  (76 shorter events, 15.8 us)
Async XLA Ops:
  0.6 15.3 %copy-start.12 = (s32[4]{0:T(128)S(1)}, s32[4]{0:T(128)}, u32[]{:S(2)}) copy-start(s32[4]{0:T(128)} %constant.55.clone) | copy-start | bytes 52
  0.6 24.7 %copy-start = (f32[1,4,2,256,256]{4,3,2,1,0:T(8,128)S(1)}, f32[1,4,2,256,256]{4,3,2,1,0:T(8,128)}, u32[]{:S(2)}) copy-start(f32[1,4,2,256,256]{4,3,2,1,0:T(8,128)} %param.14) | copy-start | bytes 6291460
  0.7 15.3 %copy-start.10 = (f32[4]{0:T(128)S(1)}, f32[4]{0:T(128)}, u32[]{:S(2)}) copy-start(f32[4]{0:T(128)} %param.17) | copy-start | bytes 52
  0.7 15.3 %copy-start.11 = (s32[4]{0:T(128)S(1)}, s32[4]{0:T(128)}, u32[]{:S(2)}) copy-start(s32[4]{0:T(128)} %param.16) | copy-start | bytes 52
  1.9 12.9 %collective-permute-start.2 = (f32[1,2,256,256]{3,2,1,0:T(8,128)S(1)}, f32[1,2,256,256]{3,2,1,0:T(8,128)S(1)}, u32[]{:S(2)}, u32[]{:S(2)}) collective-permute-start(f32[1,2,256,256]{3,2,1,0:T(8,128)S(1)} %slice_bitcast_fusion), channel_id=1, source_target_pairs={{0,8},{4,12},{8,0},{12,4},{16,24},{20,28},{24,16},{28,20},{1,9},{5... | collective-permute-start | bytes 1572872 | tf_op jit(solution)/shard_map/ppermute | solution.py:341
  4.0 4.7 %collective-permute-start.1 = (f32[2,1,4,128]{3,2,0,1:T(4,128)S(1)}, f32[2,1,4,128]{3,2,0,1:T(4,128)S(1)}, u32[]{:S(2)}, u32[]{:S(2)}) collective-permute-start(f32[2,1,4,128]{3,2,0,1:T(4,128)S(1)} %get-tuple-element.132), channel_id=1, source_target_pairs={{0,1},{2,3},{1,0},{3,2},{4,5},{6,7},{5,4},{7,6},{8,9},{10,11},{9,8... | collective-permute-start | bytes 12296 | tf_op jit(solution)/shard_map/ppermute | solution.py:355
  4.2 5.6 %collective-permute-start = (f32[2,1,4,128]{3,2,0,1:T(4,128)S(1)}, f32[2,1,4,128]{3,2,0,1:T(4,128)S(1)}, u32[]{:S(2)}, u32[]{:S(2)}) collective-permute-start(f32[2,1,4,128]{3,2,0,1:T(4,128)S(1)} %get-tuple-element.133), channel_id=1, source_target_pairs={{1,2},{2,1},{5,6},{6,5},{9,10},{10,9},{13,14},{14,13},{17,18},{18,... | collective-permute-start | bytes 12296 | tf_op jit(solution)/shard_map/ppermute | solution.py:356
  14.8 2.8 %collective-permute-start.3 = (f32[40,128]{1,0:T(8,128)}, f32[40,128]{1,0:T(8,128)S(1)}, u32[]{:S(2)}, u32[]{:S(2)}) collective-permute-start(f32[40,128]{1,0:T(8,128)} %get-tuple-element.68), channel_id=1, source_target_pairs={{0,8},{4,12},{8,0},{12,4},{16,24},{20,28},{24,16},{28,20},{1,9},{5... | collective-permute-start | bytes 61448 | tf_op jit(solution)/shard_map/ppermute | solution.py:296
  19.1 3.6 %collective-permute-start.4 = (f32[104,128]{1,0:T(8,128)S(1)}, f32[104,128]{1,0:T(8,128)S(1)}, u32[]{:S(2)}, u32[]{:S(2)}) collective-permute-start(f32[104,128]{1,0:T(8,128)S(1)} %pad_maximum_fusion.1), channel_id=1, source_target_pairs={{0,4},{4,0},{8,12},{12,8},{16,20},{20,16},{24,28},{28,24},{1,5},{5... | collective-permute-start | bytes 159752 | tf_op jit(solution)/shard_map/ppermute | solution.py:296
  22.7 2.6 %collective-permute-start.5 = (f32[40,128]{1,0:T(8,128)S(1)}, f32[40,128]{1,0:T(8,128)S(1)}, u32[]{:S(2)}, u32[]{:S(2)}) collective-permute-start(f32[40,128]{1,0:T(8,128)S(1)} %slice_add_fusion), channel_id=1, source_target_pairs={{0,16},{4,20},{8,24},{12,28},{16,0},{20,4},{24,8},{28,12},{1,17},{... | collective-permute-start | bytes 61448 | tf_op jit(solution)/shard_map/ppermute | solution.py:296
  22.9 18.9 %collective-permute-start.7 = (f32[1,2,256,256]{3,2,1,0:T(8,128)}, f32[1,2,256,256]{3,2,1,0:T(8,128)S(1)}, u32[]{:S(2)}, u32[]{:S(2)}) collective-permute-start(f32[1,2,256,256]{3,2,1,0:T(8,128)} %get-tuple-element.77), channel_id=1, source_target_pairs={{0,8},{4,12},{8,0},{12,4},{16,24},{20,28},{24,16},{28,20},{1,9},{5... | collective-permute-start | bytes 1572872 | tf_op jit(solution)/shard_map/ppermute | solution.py:390
  26.9 14.9 %copy-start.3 = (f32[16,4,128]{2,1,0:T(4,128)S(1)}, f32[16,4,128]{2,1,0:T(4,128)}, u32[]{:S(2)}) copy-start(f32[16,4,128]{2,1,0:T(4,128)} %param.12) | copy-start | bytes 98308
  26.9 14.9 %copy-start.4 = (f32[16,4,128]{2,1,0:T(4,128)S(1)}, f32[16,4,128]{2,1,0:T(4,128)}, u32[]{:S(2)}) copy-start(f32[16,4,128]{2,1,0:T(4,128)} %param.10) | copy-start | bytes 98308
  26.9 14.9 %copy-start.14 = (f32[1,2,256,256]{3,2,1,0:T(8,128)S(1)}, f32[1,2,256,256]{3,2,1,0:T(8,128)}, u32[]{:S(2)}) copy-start(f32[1,2,256,256]{3,2,1,0:T(8,128)} %get-tuple-element.85) | copy-start | bytes 1572868
  26.9 15.1 %copy-start.5 = (f32[4,256,256]{2,1,0:T(8,128)S(1)}, f32[4,256,256]{2,1,0:T(8,128)}, u32[]{:S(2)}) copy-start(f32[4,256,256]{2,1,0:T(8,128)} %param.18) | copy-start | bytes 3145732
  33.2 13.8 %collective-permute-start.6 = (f32[2,256,256]{2,1,0:T(8,128)S(1)}, f32[2,256,256]{2,1,0:T(8,128)S(1)}, u32[]{:S(2)}, u32[]{:S(2)}) collective-permute-start(f32[2,256,256]{2,1,0:T(8,128)S(1)} %get-tuple-element.74.whole_source), channel_id=1, source_target_pairs={{0,1},{1,2},{2,3},{4,5},{5,6},{6,7},{8,9},{9,10},{10,11},{12,13},{... | collective-permute-start | bytes 1572872 | tf_op jit(solution)/shard_map/ppermute | solution.py:475
  36.6 22.2 %collective-permute-start.10 = (f32[1,2,256,256]{3,2,1,0:T(8,128)S(1)}, f32[1,2,256,256]{3,2,1,0:T(8,128)S(1)}, u32[]{:S(2)}, u32[]{:S(2)}) collective-permute-start(f32[1,2,256,256]{3,2,1,0:T(8,128)S(1)} %collective-permute-done.2.refs_0_), channel_id=1, source_target_pairs={{0,16},{4,20},{8,24},{12,28},{16,0},{20,4},{24,8},{28,12},{1,17},{... | collective-permute-start | bytes 1572872 | tf_op jit(solution)/shard_map/ppermute | solution.py:395
  36.9 18.9 %collective-permute-start.14 = (f32[64,128]{1,0:T(8,128)S(1)}, f32[64,128]{1,0:T(8,128)S(1)}, u32[]{:S(2)}, u32[]{:S(2)}) collective-permute-start(f32[64,128]{1,0:T(8,128)S(1)} %copy-done.9), channel_id=1, source_target_pairs={{4,8},{12,16},{20,24},{8,4},{16,12},{24,20},{5,9},{13,17},{21,25},... | collective-permute-start | bytes 98312 | tf_op jit(solution)/shard_map/ppermute | solution.py:416
  41.9 13.9 %copy-start.13 = (f32[1,2,256,256]{3,2,1,0:T(8,128)S(1)}, f32[1,2,256,256]{3,2,1,0:T(8,128)}, u32[]{:S(2)}) copy-start(f32[1,2,256,256]{3,2,1,0:T(8,128)} %get-tuple-element.90) | copy-start | bytes 1572868
  41.9 13.9 %copy-start.2 = (f32[4,2,256,256]{3,2,1,0:T(8,128)S(1)}, f32[4,2,256,256]{3,2,1,0:T(8,128)}, u32[]{:S(2)}) copy-start(f32[4,2,256,256]{3,2,1,0:T(8,128)} %refs_2_.7) | copy-start | bytes 6291460
  41.9 13.9 %collective-permute-start.9 = (f32[1,2,256,256]{3,2,1,0:T(8,128)S(1)}, f32[1,2,256,256]{3,2,1,0:T(8,128)S(1)}, u32[]{:S(2)}, u32[]{:S(2)}) collective-permute-start(f32[1,2,256,256]{3,2,1,0:T(8,128)S(1)} %copy-done.14), channel_id=1, source_target_pairs={{0,8},{4,12},{8,0},{12,4},{16,24},{20,28},{24,16},{28,20},{1,9},{5... | collective-permute-start | bytes 1572872 | tf_op jit(solution)/shard_map/ppermute | solution.py:399
  42.5 17.3 %collective-permute-start.11 = (f32[1,2,256,256]{3,2,1,0:T(8,128)S(1)}, f32[1,2,256,256]{3,2,1,0:T(8,128)S(1)}, u32[]{:S(2)}, u32[]{:S(2)}) collective-permute-start(f32[1,2,256,256]{3,2,1,0:T(8,128)S(1)} %collective-permute-done.7.refs_1_), channel_id=1, source_target_pairs={{0,16},{4,20},{8,24},{12,28},{16,0},{20,4},{24,8},{28,12},{1,17},{... | collective-permute-start | bytes 1572872 | tf_op jit(solution)/shard_map/ppermute | solution.py:395
  48.0 12.9 %collective-permute-start.8 = (f32[2,256,256]{2,1,0:T(8,128)S(1)}, f32[2,256,256]{2,1,0:T(8,128)S(1)}, u32[]{:S(2)}, u32[]{:S(2)}) collective-permute-start(f32[2,256,256]{2,1,0:T(8,128)S(1)} %shard_map.115), channel_id=1, source_target_pairs={{0,1},{1,2},{2,3},{4,5},{5,6},{6,7},{8,9},{9,10},{10,11},{12,13},{... | collective-permute-start | bytes 1572872 | tf_op jit(solution)/shard_map/ppermute | solution.py:475
  55.8 13.3 %collective-permute-start.13 = (f32[1,2,256,256]{3,2,1,0:T(8,128)S(1)}, f32[1,2,256,256]{3,2,1,0:T(8,128)S(1)}, u32[]{:S(2)}, u32[]{:S(2)}) collective-permute-start(f32[1,2,256,256]{3,2,1,0:T(8,128)S(1)} %copy-done.13), channel_id=1, source_target_pairs={{0,8},{4,12},{8,0},{12,4},{16,24},{20,28},{24,16},{28,20},{1,9},{5... | collective-permute-start | bytes 1572872 | tf_op jit(solution)/shard_map/ppermute | solution.py:399
  57.3 12.9 %copy-start.6 = (f32[16,4,128]{2,1,0:T(4,128)S(1)}, f32[16,4,128]{2,1,0:T(4,128)}, u32[]{:S(2)}) copy-start(f32[16,4,128]{2,1,0:T(4,128)} %param.11) | copy-start | bytes 98308
  57.4 19.0 %collective-permute-start.15 = (f32[1,2,256,256]{3,2,1,0:T(8,128)S(1)}, f32[1,2,256,256]{3,2,1,0:T(8,128)S(1)}, u32[]{:S(2)}, u32[]{:S(2)}) collective-permute-start(f32[1,2,256,256]{3,2,1,0:T(8,128)S(1)} %collective-permute-done.9.refs_0_), channel_id=1, source_target_pairs={{0,16},{4,20},{8,24},{12,28},{16,0},{20,4},{24,8},{28,12},{1,17},{... | collective-permute-start | bytes 1572872 | tf_op jit(solution)/shard_map/ppermute | solution.py:395
  61.8 14.6 %collective-permute-start.12 = (f32[2,256,256]{2,1,0:T(8,128)S(1)}, f32[2,256,256]{2,1,0:T(8,128)S(1)}, u32[]{:S(2)}, u32[]{:S(2)}) collective-permute-start(f32[2,256,256]{2,1,0:T(8,128)S(1)} %shard_map.117), channel_id=1, source_target_pairs={{0,1},{1,2},{2,3},{4,5},{5,6},{6,7},{8,9},{9,10},{10,11},{12,13},{... | collective-permute-start | bytes 1572872 | tf_op jit(solution)/shard_map/ppermute | solution.py:494
  69.0 25.2 %collective-permute-start.18 = (f32[1,2,256,256]{3,2,1,0:T(8,128)S(1)}, f32[1,2,256,256]{3,2,1,0:T(8,128)S(1)}, u32[]{:S(2)}, u32[]{:S(2)}) collective-permute-start(f32[1,2,256,256]{3,2,1,0:T(8,128)S(1)} %collective-permute-done.13.refs_1_), channel_id=1, source_target_pairs={{0,16},{4,20},{8,24},{12,28},{16,0},{20,4},{24,8},{28,12},{1,17},{... | collective-permute-start | bytes 1572872 | tf_op jit(solution)/shard_map/ppermute | solution.py:395
  71.1 30.7 %collective-permute-start.17 = (f32[2,256,256]{2,1,0:T(8,128)S(1)}, f32[2,256,256]{2,1,0:T(8,128)S(1)}, u32[]{:S(2)}, u32[]{:S(2)}) collective-permute-start(f32[2,256,256]{2,1,0:T(8,128)S(1)} %shard_map.117), channel_id=1, source_target_pairs={{8,17},{9,18},{10,19},{12,21},{13,22},{14,23},{16,9},{17,10},{18,1... | collective-permute-start | bytes 1572872 | tf_op jit(solution)/shard_map/ppermute | solution.py:495
  76.4 31.6 %collective-permute-start.16 = (f32[2,256,256]{2,1,0:T(8,128)S(1)}, f32[2,256,256]{2,1,0:T(8,128)S(1)}, u32[]{:S(2)}, u32[]{:S(2)}) collective-permute-start(f32[2,256,256]{2,1,0:T(8,128)S(1)} %collective-permute-done.12.carried), channel_id=1, source_target_pairs={{0,8},{4,12},{8,0},{12,4},{16,24},{20,28},{24,16},{28,20},{1,9},{5... | collective-permute-start | bytes 1572872 | tf_op jit(solution)/shard_map/ppermute | solution.py:504
  110.6 5.5 %collective-permute-start.19 = (f32[2,2,256,256]{3,2,1,0:T(8,128)S(1)}, f32[2,2,256,256]{3,2,1,0:T(8,128)S(1)}, u32[]{:S(2)}, u32[]{:S(2)}) collective-permute-start(f32[2,2,256,256]{3,2,1,0:T(8,128)S(1)} %get-tuple-element.121), channel_id=1, source_target_pairs={{0,4},{4,0},{8,12},{12,8},{16,20},{20,16},{24,28},{28,24},{1,5},{5... | collective-permute-start | bytes 3145736 | tf_op jit(solution)/shard_map/ppermute | solution.py:554
  116.2 2.7 %collective-permute-start.20 = (f32[2,2,256,256]{3,2,1,0:T(8,128)S(1)}, f32[2,2,256,256]{3,2,1,0:T(8,128)S(1)}, u32[]{:S(2)}, u32[]{:S(2)}) collective-permute-start(f32[2,2,256,256]{3,2,1,0:T(8,128)S(1)} %get-tuple-element.129), channel_id=1, source_target_pairs={{0,4},{4,0},{8,12},{12,8},{16,20},{20,16},{24,28},{28,24},{1,5},{5... | collective-permute-start | bytes 3145736 | tf_op jit(solution)/shard_map/ppermute | solution.py:554
  (4 other events, 36.5 us)

commit v9 on v8

--- a/solution.py
+++ b/solution.py
@@ -205,6 +205,12 @@
     put(out, added(sandwich(pair_of(whole_map), pair_of(carried)), pair_of(whole_source)))
 
 
+def last_hop_kernel(odd, whole_map, whole_source, carried, before, out, onward):
+    now = added(sandwich(pair_of(whole_map), pair_of(carried)), pair_of(whole_source))
+    put(out, now)
+    put(onward, [jnp.where(odd[0] != 0, before[part], now[part]) for part in range(2)])
+
+
 def beside_kernel(start, count, parts, *refs):
     frees, (coupling, sums, link, source) = refs[:parts], refs[parts:]
     slab = 0
@@ -409,18 +415,7 @@
         sums,
     )
 
-    whole_source, field, perm, ends, mode_tiles = lax.optimization_barrier(
-        (whole_source, potential_old, permittivity, ends, mode_tiles)
-    )
-    beyond = [(e, e + 1) for e in range(1, energies - 1, 2)]
-    other_ends = lax.ppermute(ends, "energy", beyond + [(b, a) for a, b in beyond])
-    is_odd = mine % 2 == 1
-    ends_before = jnp.where(is_odd, twin_ends, other_ends).reshape(2, 2, cells, 1, depth)
-    ends_after = jnp.where(is_odd, other_ends, twin_ends).reshape(2, 2, cells, 1, depth)
-    edge = jnp.zeros((2, cells, rows, 1), jnp.float32)
-    halos = ((wire_before, wire_after), (ends_before[:, 1], ends_after[:, 0]), (edge, edge))
-    potential_new = relaxed(field, perm, charge, halos)
-
+    whole_source, mode_tiles = lax.optimization_barrier((whole_source, mode_tiles))
     odd = mine % 2
     distance = jnp.array([2, 2, 1, 1], jnp.int32)
     lowered = jnp.stack([turned, 1 - turned, 1 - odd, odd]).astype(jnp.float32)
@@ -469,10 +464,11 @@
             out_specs=(block, one_state),
         )
 
-    leaving = whole_source
+    assert peers % 2 == 0
+    leaving, previous, before = whole_source, None, None
     beside_first, beside_second = [None, None], [None, None]
     for hop in range(1, peers - 1):
-        arrived = lax.ppermute(leaving, "slab", wire_up)
+        arrived = lax.ppermute(leaving, "slab", swaps((hop - 1) % 2))
         if hop == 1:
             sent_on(1)
             sent_after(2)
@@ -486,23 +482,36 @@
             arrived, beside_first[0], free_first[2], *free_second[:2] = lax.optimization_barrier(
                 (arrived, beside_first[0], free_first[2], *free_second[:2])
             )
-        leaving = call(hop_kernel, 12, 2, whole, whole_map, whole_source, arrived)
+        previous, before = arrived, leaving
+        if hop < peers - 2:
+            leaving = call(hop_kernel, 12, 2, whole, whole_map, whole_source, arrived)
+    leaving, onward = call(
+        last_hop_kernel,
+        12,
+        2,
+        (whole, whole),
+        jnp.reshape(place % 2, (1,)),
+        whole_map,
+        whole_source,
+        previous,
+        before,
+        in_specs=[pl.BlockSpec(memory_space=pltpu.SMEM)] + [near] * 4,
+        out_specs=(near, near),
+    )
 
     def both(pairs):
         return [(a * peers + i, b * peers + j) for a, b in pairs for i, j in wire_up]
 
-    carried = lax.ppermute(leaving, "slab", wire_up)
-    carried_second = lax.ppermute(leaving, ("energy", "slab"), both(second_pairs))
+    arrived = lax.ppermute(leaving, "slab", swaps((peers - 2) % 2))
+    carried_second = lax.ppermute(onward, ("energy", "slab"), both(second_pairs))
     sent_on(3)
     beside_second[0] = beside(0, free_second[:2])
     beside_first[1] = beside(1, free_first[2:])
-    carried, beside_first[1], beside_second[0], potential_new, free_second[2] = (
-        lax.optimization_barrier(
-            (carried, beside_first[1], beside_second[0], potential_new, free_second[2])
-        )
-    )
+    arrived, beside_first[1], beside_second[0], free_second[2] = lax.optimization_barrier(
+        (arrived, beside_first[1], beside_second[0], free_second[2])
+    )
+    carried = jnp.where(place % 2 == 1, arrived, previous)
     carried_first = lax.ppermute(carried, "energy", first_pairs)
-    carried, free_second[3] = lax.optimization_barrier((carried, free_second[3]))
     greens, _ = call(
         functools.partial(own_greens_kernel, count),
         24,
@@ -516,13 +525,26 @@
         in_specs=[block, block, pl.BlockSpec(sums.shape, lambda s: (0, 0)), one_state],
         out_specs=(block, one_state),
     )
+    carried_second, greens, free_second[3], ends, field, perm = lax.optimization_barrier(
+        (carried_second, greens, free_second[3], ends, potential_old, permittivity)
+    )
+
+    beyond = [(e, e + 1) for e in range(1, energies - 1, 2)]
+    other_ends = lax.ppermute(ends, "energy", beyond + [(b, a) for a, b in beyond])
+    ends_before = jnp.where(odd == 1, twin_ends, other_ends).reshape(2, 2, cells, 1, depth)
+    ends_after = jnp.where(odd == 1, other_ends, twin_ends).reshape(2, 2, cells, 1, depth)
+    edge = jnp.zeros((2, cells, rows, 1), jnp.float32)
+    halos = ((wire_before, wire_after), (ends_before[:, 1], ends_after[:, 0]), (edge, edge))
+    potential_new = relaxed(field, perm, charge, halos)
+
     beside_second[1] = beside(1, free_second[2:])
-    carried_second, greens = lax.optimization_barrier((carried_second, greens))
     greens_second = []
     for part in beside_second:
         made, carried_second = greens_of(16, *part, carried_second)
         greens_second.append(made)
-    carried_first, greens_second = lax.optimization_barrier((carried_first, greens_second))
+    carried_first, greens_second, potential_new = lax.optimization_barrier(
+        (carried_first, greens_second, potential_new)
+    )
 
     outputs = []
     for index, part in enumerate(beside_first):

time: 121 us -> 117 us (0.967); the launches traced: 121 us -> 115 us
  waiting for transfers between devices: 39 us -> 31.9 us
  Pallas kernels: 35.9 us -> 41.5 us
  starting transfers between devices: 35.5 us -> 29.9 us
  local copies, waits for them, and re-layouts: 3.02 us -> 4.62 us
    ppermute x4, waiting for transfers between devices: 18.9 us -> 7.46 us  [sent_on(): free_second.append(lax.ppermute(given, 'energy', relay_pairs))]
    ppermute x4, waiting for transfers between devices: 3.91 us -> 13.6 us  [the longest x2 9.72 us: per_device(): arrived = lax.ppermute(leaving, 'slab', swaps((hop - 1) % 2))]
    ppermute x2, waiting for transfers between devices: 8.23 us -> 0.01 us  [sent_after(): free_first.append(lax.ppermute(cut, 'energy', first_pairs))]
    pallas_call x13, Pallas kernels: 35.9 us -> 41.5 us  [call(): pl.pallas_call(kernel, out_shape=out_shapes, cost_estimate=cost, compiler...]
    ppermute x4, starting transfers between devices: 12.5 us -> 7.77 us  [the longest x1 4.07 us: per_device(): lax.ppermute(onward, ('energy', 'slab'), both(second_pairs))]
    ppermute x4, starting transfers between devices: 4.6 us -> 1.75 us  [sent_on(): free_second.append(lax.ppermute(given, 'energy', relay_pairs))]
    ppermute x1, waiting for transfers between devices: 0.01 us -> 2.47 us  [per_device(): free_first = [arrived, lax.ppermute(cuts[1], 'energy', first_pairs)]]
    ppermute x2, starting transfers between devices: 0.07 us -> 2.47 us  [sent_after(): free_first.append(lax.ppermute(cut, 'energy', first_pairs))]
  transfers between devices with their start and end apart: 21 -> 21, of which waited for: 12 -> 13; matrix products, arithmetic and copies ran while one was open for 2% -> 3% of each run, Pallas kernels for 28% -> 34%
where the time goes in v9:
time: 117 us; the launch traced here: 115 us
  Pallas kernels  41.5 us (35%)
  waiting for transfers between devices  31.9 us (27%)
  starting transfers between devices  29.9 us (26%)
  other arithmetic  6.11 us (5%)
  local copies, waits for them, and re-layouts  4.62 us (4%)
    pallas_call x13, Pallas kernels, call(): pl.pallas_call(kernel, out_shape=out_shapes, cost_estimate=cost, compiler...  41.5 us
    ppermute x2, waiting for transfers between devices, per_device(): arrived = lax.ppermute(leaving, 'slab', swaps((hop - 1) % 2))  9.72 us
    ppermute x4, waiting for transfers between devices, sent_on(): free_second.append(lax.ppermute(given, 'energy', relay_pairs))  7.46 us
    ppermute x1, starting transfers between devices, per_device(): lax.ppermute(ends, 'energy', beyond + [(b, a) for a, b in beyond])  4.46 us
    ppermute x1, starting transfers between devices, per_device(): crossed = lax.ppermute(jnp.where(even, lower, upper), 'slab', swaps(1))  4.32 us
    ppermute x3, starting transfers between devices, exchanged(): lax.ppermute(given, 'energy', [(e, e ^ mask) for e in range(peers)])  4.13 us
    ppermute x1, starting transfers between devices, per_device(): lax.ppermute(onward, ('energy', 'slab'), both(second_pairs))  4.07 us
    ppermute x3, waiting for transfers between devices, exchanged(): lax.ppermute(given, 'energy', [(e, e ^ mask) for e in range(peers)])  3.71 us
  transfers between devices with their start and end apart: 21, of which 13 were waited for; matrix products, arithmetic and copies ran while one was open for 3% of the time, Pallas kernels for 34%

profile of v9, /device:TPU:13, one launch (start us, length us, event | category | flops | bytes accessed | tf_op | source)
XLA Modules:
  0.0 115.1 jit_solution(16361254061810501485)
XLA Ops:
  1.9 1.3 %collective-permute-start.2 = (f32[1,2,256,256]{3,2,1,0:T(8,128)S(1)}, f32[1,2,256,256]{3,2,1,0:T(8,128)}, u32[]{:S(2)}, u32[]{:S(2)}) collective-permute-start(f32[1,2,256,256]{3,2,1,0:T(8,128)S(1)} %slice_bitcast_fusion), channel_id=1, source_target_pairs={{0,8},{4,12},{8,0},{12,4},{16,24},{20,28},{24,16},{28,20},{1,9},{5... | collective-permute-start | bytes 1572872 | tf_op jit(solution)/shard_map/ppermute | solution.py:347
  4.2 4.3 %collective-permute-start = (f32[2,1,4,128]{3,2,0,1:T(4,128)S(1)}, f32[2,1,4,128]{3,2,0,1:T(4,128)S(1)}, u32[]{:S(2)}, u32[]{:S(2)}) collective-permute-start(f32[2,1,4,128]{3,2,0,1:T(4,128)S(1)} %get-tuple-element.135), channel_id=1, source_target_pairs={{1,2},{2,1},{5,6},{6,5},{9,10},{10,9},{13,14},{14,13},{17,18},{18,... | collective-permute-start | bytes 12296 | tf_op jit(solution)/shard_map/ppermute | solution.py:362
  8.5 1.4 %collective-permute-done = f32[2,1,4,128]{3,2,0,1:T(4,128)S(1)} collective-permute-done((f32[2,1,4,128]{3,2,0,1:T(4,128)S(1)}, f32[2,1,4,128]{3,2,0,1:T(4,128)S(1)}, u32[]{:S(2)}, u32[]{:S(2)}) %collective-permute-start) | collective-permute-done | bytes 4128 | tf_op jit(solution)/shard_map/ppermute | solution.py:362
  10.5 3.7 %shard_map.113 = (f32[40,128]{1,0:T(8,128)}, f32[64,128]{1,0:T(8,128)}, f32[1,2,256,256]{3,2,1,0:T(8,128)}, f32[1,2,256,256]{3,2,1,0:T(8,128)}, f32[1,2,256,256]{3,2,1,0:T(8,128)}) custom-call(s32[1]{0:T(128)} %bitcast.2.mine, f32[64,128]{1,0:T(8,128)} %bitcast.48, f32[64,128]{1,0:T(8,128)} %bitcast.46, f32[64,128]{1,0:T(8,128)} %bitcast.49, ...), custom_call_target="tpu_custom_call" | custom-call | flops 301989888 | bytes 3833860 | tf_op jit(solution)/shard_map/pallas_call | solution.py:67
  16.0 1.6 %collective-permute-done.3 = f32[40,128]{1,0:T(8,128)S(1)} collective-permute-done((f32[40,128]{1,0:T(8,128)}, f32[40,128]{1,0:T(8,128)S(1)}, u32[]{:S(2)}, u32[]{:S(2)}) %collective-permute-start.3) | collective-permute-done | bytes 20512 | tf_op jit(solution)/shard_map/ppermute | solution.py:302
  19.2 2.7 %collective-permute-start.4 = (f32[104,128]{1,0:T(8,128)S(1)}, f32[104,128]{1,0:T(8,128)S(1)}, u32[]{:S(2)}, u32[]{:S(2)}) collective-permute-start(f32[104,128]{1,0:T(8,128)S(1)} %pad_maximum_fusion.1), channel_id=1, source_target_pairs={{0,4},{4,0},{8,12},{12,8},{16,20},{20,16},{24,28},{28,24},{1,5},{5... | collective-permute-start | bytes 159752 | tf_op jit(solution)/shard_map/ppermute | solution.py:302
  25.4 1.6 %copy-done.1 = f32[4,2,256,256]{3,2,1,0:T(8,128)S(1)} copy-done((f32[4,2,256,256]{3,2,1,0:T(8,128)S(1)}, f32[4,2,256,256]{3,2,1,0:T(8,128)}, u32[]{:S(2)}) %copy-start.1) | copy-done | bytes 2097176
  27.0 6.2 %shard_map.114 = (f32[2,256,256]{2,1,0:T(8,128)S(1)}, f32[2,256,256]{2,1,0:T(8,128)S(1)}) custom-call(f32[4,2,256,256]{3,2,1,0:T(8,128)S(1)} %bitcast.43, f32[4,2,256,256]{3,2,1,0:T(8,128)S(1)} %copy-done.1, f32[40,128]{1,0:T(8,128)S(1)} %add.107.sums.refs_3_), custom_call_target="tpu_custom_call" | custom-call | flops 5133828096 | bytes 5263360 | tf_op jit(solution)/shard_map/pallas_call | solution.py:67
  33.7 2.5 %collective-permute-done.7.refs_1_ = f32[1,2,256,256]{3,2,1,0:T(8,128)} collective-permute-done((f32[1,2,256,256]{3,2,1,0:T(8,128)}, f32[1,2,256,256]{3,2,1,0:T(8,128)}, u32[]{:S(2)}, u32[]{:S(2)}) %collective-permute-start.7) | collective-permute-done | bytes 524320 | tf_op jit(solution)/shard_map/ppermute | solution.py:396
  37.8 1.3 %collective-permute-start.11 = (f32[1,2,256,256]{3,2,1,0:T(8,128)}, f32[1,2,256,256]{3,2,1,0:T(8,128)}, u32[]{:S(2)}, u32[]{:S(2)}) collective-permute-start(f32[1,2,256,256]{3,2,1,0:T(8,128)} %collective-permute-done.7.refs_1_), channel_id=1, source_target_pairs={{0,16},{4,20},{8,24},{12,28},{16,0},{20,4},{24,8},{28,12},{1,17},{... | collective-permute-start | bytes 1572872 | tf_op jit(solution)/shard_map/ppermute | solution.py:401
  39.1 6.2 %collective-permute-done.6.carried = f32[2,256,256]{2,1,0:T(8,128)S(1)} collective-permute-done((f32[2,256,256]{2,1,0:T(8,128)S(1)}, f32[2,256,256]{2,1,0:T(8,128)S(1)}, u32[]{:S(2)}, u32[]{:S(2)}) %collective-permute-start.6) | collective-permute-done | bytes 524320 | tf_op jit(solution)/shard_map/ppermute | solution.py:471
  45.3 1.7 %shard_map.115.before = f32[2,256,256]{2,1,0:T(8,128)} custom-call(f32[2,256,256]{2,1,0:T(8,128)S(1)} %get-tuple-element.73.whole_map, f32[2,256,256]{2,1,0:T(8,128)S(1)} %get-tuple-element.75.whole_source, f32[2,256,256]{2,1,0:T(8,128)S(1)} %collective-permute-done.6.carried), custom_call_target="tpu_custom_call" | custom-call | flops 603979776 | bytes 2097152 | tf_op jit(solution)/shard_map/pallas_call | solution.py:67
  47.0 3.4 %collective-permute-start.8 = (f32[2,256,256]{2,1,0:T(8,128)}, f32[2,256,256]{2,1,0:T(8,128)}, u32[]{:S(2)}, u32[]{:S(2)}) collective-permute-start(f32[2,256,256]{2,1,0:T(8,128)} %shard_map.115.before), channel_id=1, source_target_pairs={{1,2},{2,1},{5,6},{6,5},{9,10},{10,9},{13,14},{14,13},{17,18},{18,... | collective-permute-start | bytes 1572872 | tf_op jit(solution)/shard_map/ppermute | solution.py:471
  50.4 1.3 %collective-permute-start.13 = (f32[1,2,256,256]{3,2,1,0:T(8,128)}, f32[1,2,256,256]{3,2,1,0:T(8,128)S(1)}, u32[]{:S(2)}, u32[]{:S(2)}) collective-permute-start(f32[1,2,256,256]{3,2,1,0:T(8,128)} %get-tuple-element.92), channel_id=1, source_target_pairs={{0,8},{4,12},{8,0},{12,4},{16,24},{20,28},{24,16},{28,20},{1,9},{5... | collective-permute-start | bytes 1572872 | tf_op jit(solution)/shard_map/ppermute | solution.py:405
  51.7 1.6 %copy-done.2 = f32[4,2,256,256]{3,2,1,0:T(8,128)S(1)} copy-done((f32[4,2,256,256]{3,2,1,0:T(8,128)S(1)}, f32[4,2,256,256]{3,2,1,0:T(8,128)}, u32[]{:S(2)}) %copy-start.2) | copy-done | bytes 2097176
  53.3 2.8 %shard_map.116 = (f32[2,2,256,256]{3,2,1,0:T(8,128)S(1)}, f32[2,2,256,256]{3,2,1,0:T(8,128)S(1)}) custom-call(f32[1,2,256,256]{3,2,1,0:T(8,128)} %collective-permute-done.2.refs_0_, f32[1,2,256,256]{3,2,1,0:T(8,128)} %collective-permute-done.7.refs_1_, f32[4,2,256,256]{3,2,1,0:T(8,128)S(1)} %copy-done.2, f32[40,128]{1,0:T(8,128)S(1)} %add.107.sums.refs_3_), custom_call_target="tpu_custom_call" | custom-call | flops 1207959552 | bytes 5263360 | tf_op jit(solution)/shard_map/pallas_call | solution.py:67
  56.8 3.5 %collective-permute-done.8.carried = f32[2,256,256]{2,1,0:T(8,128)} collective-permute-done((f32[2,256,256]{2,1,0:T(8,128)}, f32[2,256,256]{2,1,0:T(8,128)}, u32[]{:S(2)}, u32[]{:S(2)}) %collective-permute-start.8) | collective-permute-done | bytes 524320 | tf_op jit(solution)/shard_map/ppermute | solution.py:471
  60.3 2.1 %shard_map.117 = (f32[2,256,256]{2,1,0:T(8,128)S(1)}, f32[2,256,256]{2,1,0:T(8,128)S(1)}) custom-call(s32[1]{0:T(128)} %bitcast.odd, f32[2,256,256]{2,1,0:T(8,128)S(1)} %copy-done.7, f32[2,256,256]{2,1,0:T(8,128)S(1)} %copy-done.5, f32[2,256,256]{2,1,0:T(8,128)} %collective-permute-done.8.carried, f32[2,256,256]{2,1,0:T(8,128)} %shard_map.115.before), custom_call_target="tpu_custom_call" | custom-call | flops 603979776 | bytes 3145732 | tf_op jit(solution)/shard_map/pallas_call | solution.py:67
  62.6 4.1 %collective-permute-start.16 = (f32[2,256,256]{2,1,0:T(8,128)S(1)}, f32[2,256,256]{2,1,0:T(8,128)S(1)}, u32[]{:S(2)}, u32[]{:S(2)}) collective-permute-start(f32[2,256,256]{2,1,0:T(8,128)S(1)} %get-tuple-element.102), channel_id=1, source_target_pairs={{8,17},{9,18},{10,19},{12,21},{13,22},{14,23},{16,9},{17,10},{18,1... | collective-permute-start | bytes 1572872 | tf_op jit(solution)/shard_map/ppermute | solution.py:506
  66.7 2.7 %shard_map.119 = (f32[2,2,256,256]{3,2,1,0:T(8,128)S(1)}, f32[2,2,256,256]{3,2,1,0:T(8,128)S(1)}) custom-call(f32[1,2,256,256]{3,2,1,0:T(8,128)} %collective-permute-done.10.refs_0_, f32[1,2,256,256]{3,2,1,0:T(8,128)} %collective-permute-done.11.refs_1_, f32[4,2,256,256]{3,2,1,0:T(8,128)S(1)} %copy-done.3, f32[40,128]{1,0:T(8,128)S(1)} %add.107.sums.refs_3_), custom_call_target="tpu_custom_call" | custom-call | flops 1207959552 | bytes 5263360 | tf_op jit(solution)/shard_map/pallas_call | solution.py:67
  69.5 2.5 %shard_map.118 = (f32[2,2,256,256]{3,2,1,0:T(8,128)S(1)}, f32[2,2,256,256]{3,2,1,0:T(8,128)S(1)}) custom-call(f32[1,2,256,256]{3,2,1,0:T(8,128)} %collective-permute-done.9.refs_0_, f32[1,2,256,256]{3,2,1,0:T(8,128)S(1)} %collective-permute-done.13.refs_1_, f32[4,2,256,256]{3,2,1,0:T(8,128)S(1)} %copy-done.3, f32[40,128]{1,0:T(8,128)S(1)} %add.107.sums.refs_3_), custom_call_target="tpu_custom_call" | custom-call | flops 1207959552 | bytes 5263360 | tf_op jit(solution)/shard_map/pallas_call | solution.py:67
  74.0 7.5 %shard_map.120 = (f32[4,2,256,256]{3,2,1,0:T(8,128)S(1)}, f32[2,256,256]{2,1,0:T(8,128)}) custom-call(f32[4,2,256,256]{3,2,1,0:T(8,128)S(1)} %bitcast.44, f32[4,2,256,256]{3,2,1,0:T(8,128)S(1)} %copy-done.3, f32[40,128]{1,0:T(8,128)S(1)} %add.107.sums.refs_3_, f32[2,256,256]{2,1,0:T(8,128)S(1)} %broadcast_select_fusion.carried), custom_call_target="tpu_custom_call" | custom-call | flops 4831838208 | bytes 7360512 | tf_op jit(solution)/shard_map/pallas_call | solution.py:67
  81.5 3.3 %collective-permute-done.16.carried = f32[2,256,256]{2,1,0:T(8,128)S(1)} collective-permute-done((f32[2,256,256]{2,1,0:T(8,128)S(1)}, f32[2,256,256]{2,1,0:T(8,128)S(1)}, u32[]{:S(2)}, u32[]{:S(2)}) %collective-permute-start.16) | collective-permute-done | bytes 524320 | tf_op jit(solution)/shard_map/ppermute | solution.py:506
  84.8 7.1 %collective-permute-done.17.refs_1_ = f32[1,2,256,256]{3,2,1,0:T(8,128)S(1)} collective-permute-done((f32[1,2,256,256]{3,2,1,0:T(8,128)S(1)}, f32[1,2,256,256]{3,2,1,0:T(8,128)S(1)}, u32[]{:S(2)}, u32[]{:S(2)}) %collective-permute-start.17) | collective-permute-done | bytes 524320 | tf_op jit(solution)/shard_map/ppermute | solution.py:401
  92.1 4.5 %collective-permute-start.18 = (f32[64,128]{1,0:T(8,128)S(1)}, f32[64,128]{1,0:T(8,128)S(1)}, u32[]{:S(2)}, u32[]{:S(2)}) collective-permute-start(f32[64,128]{1,0:T(8,128)S(1)} %copy-done.14), channel_id=1, source_target_pairs={{4,8},{12,16},{20,24},{8,4},{16,12},{24,20},{5,9},{13,17},{21,25},... | collective-permute-start | bytes 98312 | tf_op jit(solution)/shard_map/ppermute | solution.py:533
  96.5 1.5 %shard_map.122 = (f32[2,2,256,256]{3,2,1,0:T(8,128)S(1)}, f32[2,2,256,256]{3,2,1,0:T(8,128)S(1)}) custom-call(f32[1,2,256,256]{3,2,1,0:T(8,128)S(1)} %collective-permute-done.14.refs_0_, f32[1,2,256,256]{3,2,1,0:T(8,128)S(1)} %collective-permute-done.17.refs_1_, f32[4,2,256,256]{3,2,1,0:T(8,128)S(1)} %copy-done.3, f32[40,128]{1,0:T(8,128)S(1)} %add.107.sums.refs_3_), custom_call_target="tpu_custom_call" | custom-call | flops 1207959552 | bytes 5263360 | tf_op jit(solution)/shard_map/pallas_call | solution.py:67
  98.1 1.9 %shard_map.121 = (f32[2,2,256,256]{3,2,1,0:T(8,128)S(1)}, f32[2,256,256]{2,1,0:T(8,128)S(1)}) custom-call(f32[2,2,256,256]{3,2,1,0:T(8,128)S(1)} %get-tuple-element.100.link, f32[2,2,256,256]{3,2,1,0:T(8,128)S(1)} %get-tuple-element.101.source, f32[2,256,256]{2,1,0:T(8,128)S(1)} %collective-permute-done.16.carried), custom_call_target="tpu_custom_call" | custom-call | flops 1207959552 | bytes 4194304 | tf_op jit(solution)/shard_map/pallas_call | solution.py:67
  100.0 2.6 %shard_map.123 = (f32[2,2,256,256]{3,2,1,0:T(8,128)S(1)}, f32[2,256,256]{2,1,0:T(8,128)}) custom-call(f32[2,2,256,256]{3,2,1,0:T(8,128)S(1)} %get-tuple-element.108.link, f32[2,2,256,256]{3,2,1,0:T(8,128)S(1)} %get-tuple-element.109.source, f32[2,256,256]{2,1,0:T(8,128)S(1)} %get-tuple-element.110.carried), custom_call_target="tpu_custom_call" | custom-call | flops 1207959552 | bytes 4194304 | tf_op jit(solution)/shard_map/pallas_call | solution.py:67
  103.5 2.7 %shard_map.124 = (f32[2,2,256,256]{3,2,1,0:T(8,128)S(1)}, f32[2,2,256,256]{3,2,1,0:T(8,128)S(1)}, f32[2,256,256]{2,1,0:T(8,128)S(1)}) custom-call(s32[2]{0:T(128)S(1)} %pad_add_fusion.pick, f32[2,2,256,256]{3,2,1,0:T(8,128)S(1)} %get-tuple-element.116.link, f32[2,2,256,256]{3,2,1,0:T(8,128)S(1)} %get-tuple-element.117.source, ...), custom_call_target="tpu_custom_call" | custom-call | flops 1207959552 | bytes 9437192 | tf_op jit(solution)/shard_map/pallas_call | solution.py:67
  107.1 3.5 %shard_map.125 = (f32[2,2,256,256]{3,2,1,0:T(8,128)S(1)}, f32[2,2,256,256]{3,2,1,0:T(8,128)S(1)}, f32[2,256,256]{2,1,0:T(8,128)}) custom-call(s32[2]{0:T(128)S(1)} %pad_add_fusion.pick, f32[2,2,256,256]{3,2,1,0:T(8,128)S(1)} %get-tuple-element.124.link, f32[2,2,256,256]{3,2,1,0:T(8,128)S(1)} %get-tuple-element.125.source, ...), custom_call_target="tpu_custom_call" | custom-call | flops 1207959552 | bytes 9437192 | tf_op jit(solution)/shard_map/pallas_call | solution.py:67
  110.8 2.6 %collective-permute-done.20 = f32[2,2,256,256]{3,2,1,0:T(8,128)S(1)} collective-permute-done((f32[2,2,256,256]{3,2,1,0:T(8,128)S(1)}, f32[2,2,256,256]{3,2,1,0:T(8,128)S(1)}, u32[]{:S(2)}, u32[]{:S(2)}) %collective-permute-start.20) | collective-permute-done | bytes 1048608 | tf_op jit(solution)/shard_map/ppermute | solution.py:576
  113.6 1.5 %maximum_bitcast_fusion = f32[1,4,2,256,256]{4,3,2,1,0:T(8,128)} fusion(f32[2,2,256,256]{3,2,1,0:T(8,128)S(1)} %add.131, f32[2,2,256,256]{3,2,1,0:T(8,128)S(1)} %add.130), kind=kLoop, calls=%fused_computation.1 | loop fusion | flops 524288 | bytes 4194304 | tf_op jit(solution)/shard_map/broadcast_in_dim | solution.py:577
  (83 shorter events, 16.9 us)
Async XLA Ops:
  0.6 24.8 %copy-start = (f32[1,4,2,256,256]{4,3,2,1,0:T(8,128)S(1)}, f32[1,4,2,256,256]{4,3,2,1,0:T(8,128)}, u32[]{:S(2)}) copy-start(f32[1,4,2,256,256]{4,3,2,1,0:T(8,128)} %param.14) | copy-start | bytes 6291460
  1.9 13.0 %collective-permute-start.2 = (f32[1,2,256,256]{3,2,1,0:T(8,128)S(1)}, f32[1,2,256,256]{3,2,1,0:T(8,128)}, u32[]{:S(2)}, u32[]{:S(2)}) collective-permute-start(f32[1,2,256,256]{3,2,1,0:T(8,128)S(1)} %slice_bitcast_fusion), channel_id=1, source_target_pairs={{0,8},{4,12},{8,0},{12,4},{16,24},{20,28},{24,16},{28,20},{1,9},{5... | collective-permute-start | bytes 1572872 | tf_op jit(solution)/shard_map/ppermute | solution.py:347
  4.0 4.6 %collective-permute-start.1 = (f32[2,1,4,128]{3,2,0,1:T(4,128)S(1)}, f32[2,1,4,128]{3,2,0,1:T(4,128)S(1)}, u32[]{:S(2)}, u32[]{:S(2)}) collective-permute-start(f32[2,1,4,128]{3,2,0,1:T(4,128)S(1)} %get-tuple-element.134), channel_id=1, source_target_pairs={{0,1},{2,3},{1,0},{3,2},{4,5},{6,7},{5,4},{7,6},{8,9},{10,11},{9,8... | collective-permute-start | bytes 12296 | tf_op jit(solution)/shard_map/ppermute | solution.py:361
  4.2 5.7 %collective-permute-start = (f32[2,1,4,128]{3,2,0,1:T(4,128)S(1)}, f32[2,1,4,128]{3,2,0,1:T(4,128)S(1)}, u32[]{:S(2)}, u32[]{:S(2)}) collective-permute-start(f32[2,1,4,128]{3,2,0,1:T(4,128)S(1)} %get-tuple-element.135), channel_id=1, source_target_pairs={{1,2},{2,1},{5,6},{6,5},{9,10},{10,9},{13,14},{14,13},{17,18},{18,... | collective-permute-start | bytes 12296 | tf_op jit(solution)/shard_map/ppermute | solution.py:362
  14.8 2.8 %collective-permute-start.3 = (f32[40,128]{1,0:T(8,128)}, f32[40,128]{1,0:T(8,128)S(1)}, u32[]{:S(2)}, u32[]{:S(2)}) collective-permute-start(f32[40,128]{1,0:T(8,128)} %get-tuple-element.69), channel_id=1, source_target_pairs={{0,8},{4,12},{8,0},{12,4},{16,24},{20,28},{24,16},{28,20},{1,9},{5... | collective-permute-start | bytes 61448 | tf_op jit(solution)/shard_map/ppermute | solution.py:302
  19.2 3.6 %collective-permute-start.4 = (f32[104,128]{1,0:T(8,128)S(1)}, f32[104,128]{1,0:T(8,128)S(1)}, u32[]{:S(2)}, u32[]{:S(2)}) collective-permute-start(f32[104,128]{1,0:T(8,128)S(1)} %pad_maximum_fusion.1), channel_id=1, source_target_pairs={{0,4},{4,0},{8,12},{12,8},{16,20},{20,16},{24,28},{28,24},{1,5},{5... | collective-permute-start | bytes 159752 | tf_op jit(solution)/shard_map/ppermute | solution.py:302
  22.8 2.6 %collective-permute-start.5 = (f32[40,128]{1,0:T(8,128)S(1)}, f32[40,128]{1,0:T(8,128)S(1)}, u32[]{:S(2)}, u32[]{:S(2)}) collective-permute-start(f32[40,128]{1,0:T(8,128)S(1)} %slice_add_fusion), channel_id=1, source_target_pairs={{0,16},{4,20},{8,24},{12,28},{16,0},{20,4},{24,8},{28,12},{1,17},{... | collective-permute-start | bytes 61448 | tf_op jit(solution)/shard_map/ppermute | solution.py:302
  23.0 13.2 %collective-permute-start.7 = (f32[1,2,256,256]{3,2,1,0:T(8,128)}, f32[1,2,256,256]{3,2,1,0:T(8,128)}, u32[]{:S(2)}, u32[]{:S(2)}) collective-permute-start(f32[1,2,256,256]{3,2,1,0:T(8,128)} %get-tuple-element.78), channel_id=1, source_target_pairs={{0,8},{4,12},{8,0},{12,4},{16,24},{20,28},{24,16},{28,20},{1,9},{5... | collective-permute-start | bytes 1572872 | tf_op jit(solution)/shard_map/ppermute | solution.py:396
  27.0 6.5 %copy-start.17 = (s32[4]{0:T(128)S(1)}, s32[4]{0:T(128)}, u32[]{:S(2)}) copy-start(s32[4]{0:T(128)} %constant.57.clone) | copy-start | bytes 52
  27.0 10.4 %copy-start.10 = (f32[4,256,256]{2,1,0:T(8,128)S(1)}, f32[4,256,256]{2,1,0:T(8,128)}, u32[]{:S(2)}) copy-start(f32[4,256,256]{2,1,0:T(8,128)} %param.18) | copy-start | bytes 3145732
  33.2 13.8 %copy-start.4 = (f32[2,256,256]{2,1,0:T(8,128)}, f32[2,256,256]{2,1,0:T(8,128)S(1)}, u32[]{:S(2)}) copy-start(f32[2,256,256]{2,1,0:T(8,128)S(1)} %get-tuple-element.75.whole_source) | copy-start | bytes 1572868
  33.2 13.8 %copy-start.6 = (f32[2,256,256]{2,1,0:T(8,128)}, f32[2,256,256]{2,1,0:T(8,128)S(1)}, u32[]{:S(2)}) copy-start(f32[2,256,256]{2,1,0:T(8,128)S(1)} %get-tuple-element.73.whole_map) | copy-start | bytes 1572868
  33.2 12.1 %collective-permute-start.6 = (f32[2,256,256]{2,1,0:T(8,128)S(1)}, f32[2,256,256]{2,1,0:T(8,128)S(1)}, u32[]{:S(2)}, u32[]{:S(2)}) collective-permute-start(f32[2,256,256]{2,1,0:T(8,128)S(1)} %get-tuple-element.75.whole_source), channel_id=1, source_target_pairs={{0,1},{2,3},{1,0},{3,2},{4,5},{6,7},{5,4},{7,6},{8,9},{10,11},{9,8... | collective-permute-start | bytes 1572872 | tf_op jit(solution)/shard_map/ppermute | solution.py:471
  33.6 22.8 %collective-permute-start.10 = (f32[1,2,256,256]{3,2,1,0:T(8,128)}, f32[1,2,256,256]{3,2,1,0:T(8,128)}, u32[]{:S(2)}, u32[]{:S(2)}) collective-permute-start(f32[1,2,256,256]{3,2,1,0:T(8,128)} %collective-permute-done.2.refs_0_), channel_id=1, source_target_pairs={{0,16},{4,20},{8,24},{12,28},{16,0},{20,4},{24,8},{28,12},{1,17},{... | collective-permute-start | bytes 1572872 | tf_op jit(solution)/shard_map/ppermute | solution.py:401
  36.1 14.3 %collective-permute-start.9 = (f32[1,2,256,256]{3,2,1,0:T(8,128)}, f32[1,2,256,256]{3,2,1,0:T(8,128)}, u32[]{:S(2)}, u32[]{:S(2)}) collective-permute-start(f32[1,2,256,256]{3,2,1,0:T(8,128)} %get-tuple-element.86), channel_id=1, source_target_pairs={{0,8},{4,12},{8,0},{12,4},{16,24},{20,28},{24,16},{28,20},{1,9},{5... | collective-permute-start | bytes 1572872 | tf_op jit(solution)/shard_map/ppermute | solution.py:405
  37.8 19.0 %collective-permute-start.11 = (f32[1,2,256,256]{3,2,1,0:T(8,128)}, f32[1,2,256,256]{3,2,1,0:T(8,128)}, u32[]{:S(2)}, u32[]{:S(2)}) collective-permute-start(f32[1,2,256,256]{3,2,1,0:T(8,128)} %collective-permute-done.7.refs_1_), channel_id=1, source_target_pairs={{0,16},{4,20},{8,24},{12,28},{16,0},{20,4},{24,8},{28,12},{1,17},{... | collective-permute-start | bytes 1572872 | tf_op jit(solution)/shard_map/ppermute | solution.py:401
  47.0 13.3 %collective-permute-start.8 = (f32[2,256,256]{2,1,0:T(8,128)}, f32[2,256,256]{2,1,0:T(8,128)}, u32[]{:S(2)}, u32[]{:S(2)}) collective-permute-start(f32[2,256,256]{2,1,0:T(8,128)} %shard_map.115.before), channel_id=1, source_target_pairs={{1,2},{2,1},{5,6},{6,5},{9,10},{10,9},{13,14},{14,13},{17,18},{18,... | collective-permute-start | bytes 1572872 | tf_op jit(solution)/shard_map/ppermute | solution.py:471
  50.4 19.0 %collective-permute-start.13 = (f32[1,2,256,256]{3,2,1,0:T(8,128)}, f32[1,2,256,256]{3,2,1,0:T(8,128)S(1)}, u32[]{:S(2)}, u32[]{:S(2)}) collective-permute-start(f32[1,2,256,256]{3,2,1,0:T(8,128)} %get-tuple-element.92), channel_id=1, source_target_pairs={{0,8},{4,12},{8,0},{12,4},{16,24},{20,28},{24,16},{28,20},{1,9},{5... | collective-permute-start | bytes 1572872 | tf_op jit(solution)/shard_map/ppermute | solution.py:405
  53.3 7.0 %copy-start.5 = (f32[2,256,256]{2,1,0:T(8,128)S(1)}, f32[2,256,256]{2,1,0:T(8,128)}, u32[]{:S(2)}) copy-start(f32[2,256,256]{2,1,0:T(8,128)} %copy-done.4) | copy-start | bytes 1572868
  53.3 7.0 %copy-start.7 = (f32[2,256,256]{2,1,0:T(8,128)S(1)}, f32[2,256,256]{2,1,0:T(8,128)}, u32[]{:S(2)}) copy-start(f32[2,256,256]{2,1,0:T(8,128)} %copy-done.6) | copy-start | bytes 1572868
  56.1 10.5 %copy-start.3 = (f32[4,2,256,256]{3,2,1,0:T(8,128)S(1)}, f32[4,2,256,256]{3,2,1,0:T(8,128)}, u32[]{:S(2)}) copy-start(f32[4,2,256,256]{3,2,1,0:T(8,128)} %refs_2_.7) | copy-start | bytes 6291460
  56.1 15.9 %collective-permute-start.14 = (f32[1,2,256,256]{3,2,1,0:T(8,128)}, f32[1,2,256,256]{3,2,1,0:T(8,128)S(1)}, u32[]{:S(2)}, u32[]{:S(2)}) collective-permute-start(f32[1,2,256,256]{3,2,1,0:T(8,128)} %collective-permute-done.9.refs_0_), channel_id=1, source_target_pairs={{0,16},{4,20},{8,24},{12,28},{16,0},{20,4},{24,8},{28,12},{1,17},{... | collective-permute-start | bytes 1572872 | tf_op jit(solution)/shard_map/ppermute | solution.py:401
  62.4 10.2 %collective-permute-start.12 = (f32[2,256,256]{2,1,0:T(8,128)S(1)}, f32[2,256,256]{2,1,0:T(8,128)S(1)}, u32[]{:S(2)}, u32[]{:S(2)}) collective-permute-start(f32[2,256,256]{2,1,0:T(8,128)S(1)} %get-tuple-element.90), channel_id=1, source_target_pairs={{0,1},{2,3},{1,0},{3,2},{4,5},{6,7},{5,4},{7,6},{8,9},{10,11},{9,8... | collective-permute-start | bytes 1572872 | tf_op jit(solution)/shard_map/ppermute | solution.py:505
  62.6 22.2 %collective-permute-start.16 = (f32[2,256,256]{2,1,0:T(8,128)S(1)}, f32[2,256,256]{2,1,0:T(8,128)S(1)}, u32[]{:S(2)}, u32[]{:S(2)}) collective-permute-start(f32[2,256,256]{2,1,0:T(8,128)S(1)} %get-tuple-element.102), channel_id=1, source_target_pairs={{8,17},{9,18},{10,19},{12,21},{13,22},{14,23},{16,9},{17,10},{18,1... | collective-permute-start | bytes 1572872 | tf_op jit(solution)/shard_map/ppermute | solution.py:506
  69.4 22.5 %collective-permute-start.17 = (f32[1,2,256,256]{3,2,1,0:T(8,128)S(1)}, f32[1,2,256,256]{3,2,1,0:T(8,128)S(1)}, u32[]{:S(2)}, u32[]{:S(2)}) collective-permute-start(f32[1,2,256,256]{3,2,1,0:T(8,128)S(1)} %collective-permute-done.13.refs_1_), channel_id=1, source_target_pairs={{0,16},{4,20},{8,24},{12,28},{16,0},{20,4},{24,8},{28,12},{1,17},{... | collective-permute-start | bytes 1572872 | tf_op jit(solution)/shard_map/ppermute | solution.py:401
  72.7 19.2 %copy-start.8 = (f32[16,4,128]{2,1,0:T(4,128)S(1)}, f32[16,4,128]{2,1,0:T(4,128)}, u32[]{:S(2)}) copy-start(f32[16,4,128]{2,1,0:T(4,128)} %param.12) | copy-start | bytes 98308
  72.7 19.2 %copy-start.9 = (f32[16,4,128]{2,1,0:T(4,128)S(1)}, f32[16,4,128]{2,1,0:T(4,128)}, u32[]{:S(2)}) copy-start(f32[16,4,128]{2,1,0:T(4,128)} %param.10) | copy-start | bytes 98308
  72.7 19.3 %copy-start.14 = (f32[64,128]{1,0:T(8,128)S(1)}, f32[64,128]{1,0:T(8,128)}, u32[]{:S(2)}) copy-start(f32[64,128]{1,0:T(8,128)} %get-tuple-element.114) | copy-start | bytes 98308
  72.8 30.7 %collective-permute-start.15 = (f32[2,256,256]{2,1,0:T(8,128)S(1)}, f32[2,256,256]{2,1,0:T(8,128)S(1)}, u32[]{:S(2)}, u32[]{:S(2)}) collective-permute-start(f32[2,256,256]{2,1,0:T(8,128)S(1)} %broadcast_select_fusion.carried), channel_id=1, source_target_pairs={{0,8},{4,12},{8,0},{12,4},{16,24},{20,28},{24,16},{28,20},{1,9},{5... | collective-permute-start | bytes 1572872 | tf_op jit(solution)/shard_map/ppermute | solution.py:514
  92.1 10.6 %collective-permute-start.18 = (f32[64,128]{1,0:T(8,128)S(1)}, f32[64,128]{1,0:T(8,128)S(1)}, u32[]{:S(2)}, u32[]{:S(2)}) collective-permute-start(f32[64,128]{1,0:T(8,128)S(1)} %copy-done.14), channel_id=1, source_target_pairs={{4,8},{12,16},{20,24},{8,4},{16,12},{24,20},{5,9},{13,17},{21,25},... | collective-permute-start | bytes 98312 | tf_op jit(solution)/shard_map/ppermute | solution.py:533
  106.2 4.4 %collective-permute-start.19 = (f32[2,2,256,256]{3,2,1,0:T(8,128)S(1)}, f32[2,2,256,256]{3,2,1,0:T(8,128)S(1)}, u32[]{:S(2)}, u32[]{:S(2)}) collective-permute-start(f32[2,2,256,256]{3,2,1,0:T(8,128)S(1)} %get-tuple-element.123), channel_id=1, source_target_pairs={{0,4},{4,0},{8,12},{12,8},{16,20},{20,16},{24,28},{28,24},{1,5},{5... | collective-permute-start | bytes 3145736 | tf_op jit(solution)/shard_map/ppermute | solution.py:576
  110.7 2.7 %collective-permute-start.20 = (f32[2,2,256,256]{3,2,1,0:T(8,128)S(1)}, f32[2,2,256,256]{3,2,1,0:T(8,128)S(1)}, u32[]{:S(2)}, u32[]{:S(2)}) collective-permute-start(f32[2,2,256,256]{3,2,1,0:T(8,128)S(1)} %get-tuple-element.131), channel_id=1, source_target_pairs={{0,4},{4,0},{8,12},{12,8},{16,20},{20,16},{24,28},{28,24},{1,5},{5... | collective-permute-start | bytes 3145736 | tf_op jit(solution)/shard_map/ppermute | solution.py:576
  (7 other events, 31.9 us)

commit v10 on v9

--- a/solution.py
+++ b/solution.py
@@ -472,15 +472,15 @@
         if hop == 1:
             sent_on(1)
             sent_after(2)
-            arrived, weights, free_first[1] = lax.optimization_barrier(
-                (arrived, weights, free_first[1])
+            beside_first[0] = beside(0, free_first[:2])
+            arrived, weights, beside_first[0] = lax.optimization_barrier(
+                (arrived, weights, beside_first[0])
             )
         if hop == 2:
             sent_on(2)
             sent_after(3)
-            beside_first[0] = beside(0, free_first[:2])
-            arrived, beside_first[0], free_first[2], *free_second[:2] = lax.optimization_barrier(
-                (arrived, beside_first[0], free_first[2], *free_second[:2])
+            arrived, free_first[2], *free_second[:2] = lax.optimization_barrier(
+                (arrived, free_first[2], *free_second[:2])
             )
         previous, before = arrived, leaving
         if hop < peers - 2:
@@ -537,11 +537,10 @@
     halos = ((wire_before, wire_after), (ends_before[:, 1], ends_after[:, 0]), (edge, edge))
     potential_new = relaxed(field, perm, charge, halos)
 
+    greens_second = [None, None]
+    greens_second[0], carried_second = greens_of(16, *beside_second[0], carried_second)
     beside_second[1] = beside(1, free_second[2:])
-    greens_second = []
-    for part in beside_second:
-        made, carried_second = greens_of(16, *part, carried_second)
-        greens_second.append(made)
+    greens_second[1], _ = greens_of(16, *beside_second[1], carried_second)
     carried_first, greens_second, potential_new = lax.optimization_barrier(
         (carried_first, greens_second, potential_new)
     )

time: 117 us -> 119 us (1.017)
  local copies, waits for them, and re-layouts: 4.62 us -> 7.11 us
    ppermute x4, waiting for transfers between devices: 7.46 us -> 12.3 us  [sent_on(): free_second.append(lax.ppermute(given, 'energy', relay_pairs))]
    ppermute x2, waiting for transfers between devices: 9.72 us -> 5.59 us  [per_device(): arrived = lax.ppermute(leaving, 'slab', swaps((hop - 1) % 2))]
    unnamed x36 -> x44, local copies, waits for them, and re-layouts: 3.25 us -> 5.74 us
  transfers between devices with their start and end apart: 21 -> 21, of which waited for: 13 -> 13; matrix products, arithmetic and copies ran while one was open for 3% -> 3% of each run, Pallas kernels for 34% -> 33%
where the time goes in v10:
time: 119 us; the launch traced here: 117 us
  Pallas kernels  41.5 us (35%)
  waiting for transfers between devices  32 us (27%)
  starting transfers between devices  29.4 us (25%)
  local copies, waits for them, and re-layouts  7.11 us (6%)
  other arithmetic  6.11 us (5%)
    pallas_call x13, Pallas kernels, call(): pl.pallas_call(kernel, out_shape=out_shapes, cost_estimate=cost, compiler...  41.5 us
    ppermute x4, waiting for transfers between devices, sent_on(): free_second.append(lax.ppermute(given, 'energy', relay_pairs))  12.3 us
    unnamed x44, local copies, waits for them, and re-layouts  5.74 us
    ppermute x2, waiting for transfers between devices, per_device(): arrived = lax.ppermute(leaving, 'slab', swaps((hop - 1) % 2))  5.59 us
    ppermute x1, starting transfers between devices, per_device(): crossed = lax.ppermute(jnp.where(even, lower, upper), 'slab', swaps(1))  4.32 us
    ppermute x1, starting transfers between devices, per_device(): lax.ppermute(ends, 'energy', beyond + [(b, a) for a, b in beyond])  4.22 us
    ppermute x3, starting transfers between devices, exchanged(): lax.ppermute(given, 'energy', [(e, e ^ mask) for e in range(peers)])  4.13 us
    ppermute x1, starting transfers between devices, per_device(): lax.ppermute(onward, ('energy', 'slab'), both(second_pairs))  4.07 us
  transfers between devices with their start and end apart: 21, of which 13 were waited for; matrix products, arithmetic and copies ran while one was open for 3% of the time, Pallas kernels for 33%

profile of v10, /device:TPU:13, one launch (start us, length us, event | category | flops | bytes accessed | tf_op | source)
XLA Modules:
  0.0 117.2 jit_solution(3262160578384972582)
XLA Ops:
  1.9 1.3 %collective-permute-start.2 = (f32[1,2,256,256]{3,2,1,0:T(8,128)S(1)}, f32[1,2,256,256]{3,2,1,0:T(8,128)}, u32[]{:S(2)}, u32[]{:S(2)}) collective-permute-start(f32[1,2,256,256]{3,2,1,0:T(8,128)S(1)} %slice_bitcast_fusion), channel_id=1, source_target_pairs={{0,8},{4,12},{8,0},{12,4},{16,24},{20,28},{24,16},{28,20},{1,9},{5... | collective-permute-start | bytes 1572872 | tf_op jit(solution)/shard_map/ppermute | solution.py:347
  4.2 4.3 %collective-permute-start = (f32[2,1,4,128]{3,2,0,1:T(4,128)S(1)}, f32[2,1,4,128]{3,2,0,1:T(4,128)S(1)}, u32[]{:S(2)}, u32[]{:S(2)}) collective-permute-start(f32[2,1,4,128]{3,2,0,1:T(4,128)S(1)} %get-tuple-element.133), channel_id=1, source_target_pairs={{1,2},{2,1},{5,6},{6,5},{9,10},{10,9},{13,14},{14,13},{17,18},{18,... | collective-permute-start | bytes 12296 | tf_op jit(solution)/shard_map/ppermute | solution.py:362
  8.5 1.4 %collective-permute-done = f32[2,1,4,128]{3,2,0,1:T(4,128)S(1)} collective-permute-done((f32[2,1,4,128]{3,2,0,1:T(4,128)S(1)}, f32[2,1,4,128]{3,2,0,1:T(4,128)S(1)}, u32[]{:S(2)}, u32[]{:S(2)}) %collective-permute-start) | collective-permute-done | bytes 4128 | tf_op jit(solution)/shard_map/ppermute | solution.py:362
  10.5 3.7 %shard_map.113 = (f32[40,128]{1,0:T(8,128)}, f32[64,128]{1,0:T(8,128)}, f32[1,2,256,256]{3,2,1,0:T(8,128)}, f32[1,2,256,256]{3,2,1,0:T(8,128)}, f32[1,2,256,256]{3,2,1,0:T(8,128)}) custom-call(s32[1]{0:T(128)} %bitcast.2.mine, f32[64,128]{1,0:T(8,128)} %bitcast.48, f32[64,128]{1,0:T(8,128)} %bitcast.46, f32[64,128]{1,0:T(8,128)} %bitcast.49, ...), custom_call_target="tpu_custom_call" | custom-call | flops 301989888 | bytes 3833860 | tf_op jit(solution)/shard_map/pallas_call | solution.py:67
  16.0 1.6 %collective-permute-done.3 = f32[40,128]{1,0:T(8,128)S(1)} collective-permute-done((f32[40,128]{1,0:T(8,128)}, f32[40,128]{1,0:T(8,128)S(1)}, u32[]{:S(2)}, u32[]{:S(2)}) %collective-permute-start.3) | collective-permute-done | bytes 20512 | tf_op jit(solution)/shard_map/ppermute | solution.py:302
  19.2 2.7 %collective-permute-start.4 = (f32[104,128]{1,0:T(8,128)S(1)}, f32[104,128]{1,0:T(8,128)S(1)}, u32[]{:S(2)}, u32[]{:S(2)}) collective-permute-start(f32[104,128]{1,0:T(8,128)S(1)} %pad_maximum_fusion.1), channel_id=1, source_target_pairs={{0,4},{4,0},{8,12},{12,8},{16,20},{20,16},{24,28},{28,24},{1,5},{5... | collective-permute-start | bytes 159752 | tf_op jit(solution)/shard_map/ppermute | solution.py:302
  25.4 1.6 %copy-done.5 = f32[4,2,256,256]{3,2,1,0:T(8,128)S(1)} copy-done((f32[4,2,256,256]{3,2,1,0:T(8,128)S(1)}, f32[4,2,256,256]{3,2,1,0:T(8,128)}, u32[]{:S(2)}) %copy-start.5) | copy-done | bytes 2097176
  27.0 6.2 %shard_map.114 = (f32[2,256,256]{2,1,0:T(8,128)S(1)}, f32[2,256,256]{2,1,0:T(8,128)S(1)}) custom-call(f32[4,2,256,256]{3,2,1,0:T(8,128)S(1)} %bitcast.43, f32[4,2,256,256]{3,2,1,0:T(8,128)S(1)} %copy-done.5, f32[40,128]{1,0:T(8,128)S(1)} %add.107.sums.refs_3_), custom_call_target="tpu_custom_call" | custom-call | flops 5133828096 | bytes 5263360 | tf_op jit(solution)/shard_map/pallas_call | solution.py:67
  34.1 2.2 %collective-permute-done.7.refs_1_ = f32[1,2,256,256]{3,2,1,0:T(8,128)} collective-permute-done((f32[1,2,256,256]{3,2,1,0:T(8,128)}, f32[1,2,256,256]{3,2,1,0:T(8,128)}, u32[]{:S(2)}, u32[]{:S(2)}) %collective-permute-start.7) | collective-permute-done | bytes 524320 | tf_op jit(solution)/shard_map/ppermute | solution.py:396
  37.4 1.2 %collective-permute-start.11 = (f32[1,2,256,256]{3,2,1,0:T(8,128)}, f32[1,2,256,256]{3,2,1,0:T(8,128)}, u32[]{:S(2)}, u32[]{:S(2)}) collective-permute-start(f32[1,2,256,256]{3,2,1,0:T(8,128)} %collective-permute-done.7.refs_1_), channel_id=1, source_target_pairs={{0,16},{4,20},{8,24},{12,28},{16,0},{20,4},{24,8},{28,12},{1,17},{... | collective-permute-start | bytes 1572872 | tf_op jit(solution)/shard_map/ppermute | solution.py:401
  38.7 2.7 %shard_map.115 = (f32[2,2,256,256]{3,2,1,0:T(8,128)S(1)}, f32[2,2,256,256]{3,2,1,0:T(8,128)S(1)}) custom-call(f32[1,2,256,256]{3,2,1,0:T(8,128)} %collective-permute-done.2.refs_0_, f32[1,2,256,256]{3,2,1,0:T(8,128)} %collective-permute-done.7.refs_1_, f32[4,2,256,256]{3,2,1,0:T(8,128)S(1)} %copy-done.5, f32[40,128]{1,0:T(8,128)S(1)} %add.107.sums.refs_3_), custom_call_target="tpu_custom_call" | custom-call | flops 1207959552 | bytes 5263360 | tf_op jit(solution)/shard_map/pallas_call | solution.py:67
  43.3 2.0 %collective-permute-done.6.carried = f32[2,256,256]{2,1,0:T(8,128)S(1)} collective-permute-done((f32[2,256,256]{2,1,0:T(8,128)S(1)}, f32[2,256,256]{2,1,0:T(8,128)S(1)}, u32[]{:S(2)}, u32[]{:S(2)}) %collective-permute-start.6) | collective-permute-done | bytes 524320 | tf_op jit(solution)/shard_map/ppermute | solution.py:471
  45.3 1.7 %shard_map.116.before = f32[2,256,256]{2,1,0:T(8,128)} custom-call(f32[2,256,256]{2,1,0:T(8,128)S(1)} %get-tuple-element.72.whole_map, f32[2,256,256]{2,1,0:T(8,128)S(1)} %get-tuple-element.74.whole_source, f32[2,256,256]{2,1,0:T(8,128)S(1)} %collective-permute-done.6.carried), custom_call_target="tpu_custom_call" | custom-call | flops 603979776 | bytes 2097152 | tf_op jit(solution)/shard_map/pallas_call | solution.py:67
  47.0 3.4 %collective-permute-start.8 = (f32[2,256,256]{2,1,0:T(8,128)}, f32[2,256,256]{2,1,0:T(8,128)}, u32[]{:S(2)}, u32[]{:S(2)}) collective-permute-start(f32[2,256,256]{2,1,0:T(8,128)} %shard_map.116.before), channel_id=1, source_target_pairs={{1,2},{2,1},{5,6},{6,5},{9,10},{10,9},{13,14},{14,13},{17,18},{18,... | collective-permute-start | bytes 1572872 | tf_op jit(solution)/shard_map/ppermute | solution.py:471
  50.4 1.2 %collective-permute-start.13 = (f32[1,2,256,256]{3,2,1,0:T(8,128)}, f32[1,2,256,256]{3,2,1,0:T(8,128)}, u32[]{:S(2)}, u32[]{:S(2)}) collective-permute-start(f32[1,2,256,256]{3,2,1,0:T(8,128)} %get-tuple-element.90), channel_id=1, source_target_pairs={{0,8},{4,12},{8,0},{12,4},{16,24},{20,28},{24,16},{28,20},{1,9},{5... | collective-permute-start | bytes 1572872 | tf_op jit(solution)/shard_map/ppermute | solution.py:405
  51.9 4.8 %collective-permute-done.11.refs_1_ = f32[1,2,256,256]{3,2,1,0:T(8,128)} collective-permute-done((f32[1,2,256,256]{3,2,1,0:T(8,128)}, f32[1,2,256,256]{3,2,1,0:T(8,128)}, u32[]{:S(2)}, u32[]{:S(2)}) %collective-permute-start.11) | collective-permute-done | bytes 524320 | tf_op jit(solution)/shard_map/ppermute | solution.py:401
  56.7 3.6 %collective-permute-done.8.carried = f32[2,256,256]{2,1,0:T(8,128)} collective-permute-done((f32[2,256,256]{2,1,0:T(8,128)}, f32[2,256,256]{2,1,0:T(8,128)}, u32[]{:S(2)}, u32[]{:S(2)}) %collective-permute-start.8) | collective-permute-done | bytes 524320 | tf_op jit(solution)/shard_map/ppermute | solution.py:471
  62.4 2.1 %shard_map.117 = (f32[2,256,256]{2,1,0:T(8,128)S(1)}, f32[2,256,256]{2,1,0:T(8,128)S(1)}) custom-call(s32[1]{0:T(128)} %bitcast.odd, f32[2,256,256]{2,1,0:T(8,128)S(1)} %copy-done.10, f32[2,256,256]{2,1,0:T(8,128)S(1)} %copy-done.8, f32[2,256,256]{2,1,0:T(8,128)} %collective-permute-done.8.carried, f32[2,256,256]{2,1,0:T(8,128)} %shard_map.116.before), custom_call_target="tpu_custom_call" | custom-call | flops 603979776 | bytes 3145732 | tf_op jit(solution)/shard_map/pallas_call | solution.py:67
  64.7 4.1 %collective-permute-start.16 = (f32[2,256,256]{2,1,0:T(8,128)S(1)}, f32[2,256,256]{2,1,0:T(8,128)S(1)}, u32[]{:S(2)}, u32[]{:S(2)}) collective-permute-start(f32[2,256,256]{2,1,0:T(8,128)S(1)} %get-tuple-element.100), channel_id=1, source_target_pairs={{8,17},{9,18},{10,19},{12,21},{13,22},{14,23},{16,9},{17,10},{18,1... | collective-permute-start | bytes 1572872 | tf_op jit(solution)/shard_map/ppermute | solution.py:506
  68.8 2.7 %shard_map.119 = (f32[2,2,256,256]{3,2,1,0:T(8,128)S(1)}, f32[2,2,256,256]{3,2,1,0:T(8,128)S(1)}) custom-call(f32[1,2,256,256]{3,2,1,0:T(8,128)} %collective-permute-done.10.refs_0_, f32[1,2,256,256]{3,2,1,0:T(8,128)} %collective-permute-done.11.refs_1_, f32[4,2,256,256]{3,2,1,0:T(8,128)S(1)} %copy-done.6, f32[40,128]{1,0:T(8,128)S(1)} %add.107.sums.refs_3_), custom_call_target="tpu_custom_call" | custom-call | flops 1207959552 | bytes 5263360 | tf_op jit(solution)/shard_map/pallas_call | solution.py:67
  71.6 2.7 %shard_map.118 = (f32[2,2,256,256]{3,2,1,0:T(8,128)S(1)}, f32[2,2,256,256]{3,2,1,0:T(8,128)S(1)}) custom-call(f32[1,2,256,256]{3,2,1,0:T(8,128)} %collective-permute-done.9.refs_0_, f32[1,2,256,256]{3,2,1,0:T(8,128)} %collective-permute-done.13.refs_1_, f32[4,2,256,256]{3,2,1,0:T(8,128)S(1)} %copy-done.6, f32[40,128]{1,0:T(8,128)S(1)} %add.107.sums.refs_3_), custom_call_target="tpu_custom_call" | custom-call | flops 1207959552 | bytes 5263360 | tf_op jit(solution)/shard_map/pallas_call | solution.py:67
  76.1 7.5 %shard_map.120 = (f32[4,2,256,256]{3,2,1,0:T(8,128)S(1)}, f32[2,256,256]{2,1,0:T(8,128)}) custom-call(f32[4,2,256,256]{3,2,1,0:T(8,128)S(1)} %bitcast.44, f32[4,2,256,256]{3,2,1,0:T(8,128)S(1)} %copy-done.6, f32[40,128]{1,0:T(8,128)S(1)} %add.107.sums.refs_3_, f32[2,256,256]{2,1,0:T(8,128)S(1)} %broadcast_select_fusion.carried), custom_call_target="tpu_custom_call" | custom-call | flops 4831838208 | bytes 7360512 | tf_op jit(solution)/shard_map/pallas_call | solution.py:67
  83.6 3.2 %collective-permute-done.16.carried = f32[2,256,256]{2,1,0:T(8,128)S(1)} collective-permute-done((f32[2,256,256]{2,1,0:T(8,128)S(1)}, f32[2,256,256]{2,1,0:T(8,128)S(1)}, u32[]{:S(2)}, u32[]{:S(2)}) %collective-permute-start.16) | collective-permute-done | bytes 524320 | tf_op jit(solution)/shard_map/ppermute | solution.py:506
  86.9 7.5 %collective-permute-done.17.refs_1_ = f32[1,2,256,256]{3,2,1,0:T(8,128)S(1)} collective-permute-done((f32[1,2,256,256]{3,2,1,0:T(8,128)}, f32[1,2,256,256]{3,2,1,0:T(8,128)S(1)}, u32[]{:S(2)}, u32[]{:S(2)}) %collective-permute-start.17) | collective-permute-done | bytes 524320 | tf_op jit(solution)/shard_map/ppermute | solution.py:401
  94.5 4.2 %collective-permute-start.18 = (f32[64,128]{1,0:T(8,128)S(1)}, f32[64,128]{1,0:T(8,128)S(1)}, u32[]{:S(2)}, u32[]{:S(2)}) collective-permute-start(f32[64,128]{1,0:T(8,128)S(1)} %copy-done.17), channel_id=1, source_target_pairs={{4,8},{12,16},{20,24},{8,4},{16,12},{24,20},{5,9},{13,17},{21,25},... | collective-permute-start | bytes 98312 | tf_op jit(solution)/shard_map/ppermute | solution.py:533
  98.7 1.5 %shard_map.122 = (f32[2,2,256,256]{3,2,1,0:T(8,128)S(1)}, f32[2,2,256,256]{3,2,1,0:T(8,128)S(1)}) custom-call(f32[1,2,256,256]{3,2,1,0:T(8,128)S(1)} %collective-permute-done.14.refs_0_, f32[1,2,256,256]{3,2,1,0:T(8,128)S(1)} %collective-permute-done.17.refs_1_, f32[4,2,256,256]{3,2,1,0:T(8,128)S(1)} %copy-done.6, f32[40,128]{1,0:T(8,128)S(1)} %add.107.sums.refs_3_), custom_call_target="tpu_custom_call" | custom-call | flops 1207959552 | bytes 5263360 | tf_op jit(solution)/shard_map/pallas_call | solution.py:67
  100.3 1.9 %shard_map.121 = (f32[2,2,256,256]{3,2,1,0:T(8,128)S(1)}, f32[2,256,256]{2,1,0:T(8,128)S(1)}) custom-call(f32[2,2,256,256]{3,2,1,0:T(8,128)S(1)} %get-tuple-element.98.link, f32[2,2,256,256]{3,2,1,0:T(8,128)S(1)} %get-tuple-element.99.source, f32[2,256,256]{2,1,0:T(8,128)S(1)} %collective-permute-done.16.carried), custom_call_target="tpu_custom_call" | custom-call | flops 1207959552 | bytes 4194304 | tf_op jit(solution)/shard_map/pallas_call | solution.py:67
  102.2 2.6 %shard_map.123 = (f32[2,2,256,256]{3,2,1,0:T(8,128)S(1)}, f32[2,256,256]{2,1,0:T(8,128)}) custom-call(f32[2,2,256,256]{3,2,1,0:T(8,128)S(1)} %get-tuple-element.106.link, f32[2,2,256,256]{3,2,1,0:T(8,128)S(1)} %get-tuple-element.107.source, f32[2,256,256]{2,1,0:T(8,128)S(1)} %get-tuple-element.108.carried), custom_call_target="tpu_custom_call" | custom-call | flops 1207959552 | bytes 4194304 | tf_op jit(solution)/shard_map/pallas_call | solution.py:67
  105.7 2.7 %shard_map.124 = (f32[2,2,256,256]{3,2,1,0:T(8,128)S(1)}, f32[2,2,256,256]{3,2,1,0:T(8,128)S(1)}, f32[2,256,256]{2,1,0:T(8,128)S(1)}) custom-call(s32[2]{0:T(128)S(1)} %pad_add_fusion.pick, f32[2,2,256,256]{3,2,1,0:T(8,128)S(1)} %copy-done.2, f32[2,2,256,256]{3,2,1,0:T(8,128)S(1)} %copy-done.4, f32[2,256,256]{2,1,0:T(8,128)S(1)} %collective-permute-done.15.carried, ...), custom_call_target="tpu_custom_call" | custom-call | flops 1207959552 | bytes 9437192 | tf_op jit(solution)/shard_map/pallas_call | solution.py:67
  109.2 3.5 %shard_map.125 = (f32[2,2,256,256]{3,2,1,0:T(8,128)S(1)}, f32[2,2,256,256]{3,2,1,0:T(8,128)S(1)}, f32[2,256,256]{2,1,0:T(8,128)}) custom-call(s32[2]{0:T(128)S(1)} %pad_add_fusion.pick, f32[2,2,256,256]{3,2,1,0:T(8,128)S(1)} %get-tuple-element.122.link, f32[2,2,256,256]{3,2,1,0:T(8,128)S(1)} %get-tuple-element.123.source, ...), custom_call_target="tpu_custom_call" | custom-call | flops 1207959552 | bytes 9437192 | tf_op jit(solution)/shard_map/pallas_call | solution.py:67
  113.0 2.6 %collective-permute-done.20 = f32[2,2,256,256]{3,2,1,0:T(8,128)S(1)} collective-permute-done((f32[2,2,256,256]{3,2,1,0:T(8,128)S(1)}, f32[2,2,256,256]{3,2,1,0:T(8,128)S(1)}, u32[]{:S(2)}, u32[]{:S(2)}) %collective-permute-start.20) | collective-permute-done | bytes 1048608 | tf_op jit(solution)/shard_map/ppermute | solution.py:575
  115.7 1.5 %maximum_bitcast_fusion = f32[1,4,2,256,256]{4,3,2,1,0:T(8,128)} fusion(f32[2,2,256,256]{3,2,1,0:T(8,128)S(1)} %add.131, f32[2,2,256,256]{3,2,1,0:T(8,128)S(1)} %add.130), kind=kLoop, calls=%fused_computation.1 | loop fusion | flops 524288 | bytes 4194304 | tf_op jit(solution)/shard_map/broadcast_in_dim | solution.py:576
  (91 shorter events, 20.3 us)
Async XLA Ops:
  0.6 24.8 %copy-start = (f32[1,4,2,256,256]{4,3,2,1,0:T(8,128)S(1)}, f32[1,4,2,256,256]{4,3,2,1,0:T(8,128)}, u32[]{:S(2)}) copy-start(f32[1,4,2,256,256]{4,3,2,1,0:T(8,128)} %param.14) | copy-start | bytes 6291460
  1.9 13.0 %collective-permute-start.2 = (f32[1,2,256,256]{3,2,1,0:T(8,128)S(1)}, f32[1,2,256,256]{3,2,1,0:T(8,128)}, u32[]{:S(2)}, u32[]{:S(2)}) collective-permute-start(f32[1,2,256,256]{3,2,1,0:T(8,128)S(1)} %slice_bitcast_fusion), channel_id=1, source_target_pairs={{0,8},{4,12},{8,0},{12,4},{16,24},{20,28},{24,16},{28,20},{1,9},{5... | collective-permute-start | bytes 1572872 | tf_op jit(solution)/shard_map/ppermute | solution.py:347
  4.0 4.6 %collective-permute-start.1 = (f32[2,1,4,128]{3,2,0,1:T(4,128)S(1)}, f32[2,1,4,128]{3,2,0,1:T(4,128)S(1)}, u32[]{:S(2)}, u32[]{:S(2)}) collective-permute-start(f32[2,1,4,128]{3,2,0,1:T(4,128)S(1)} %get-tuple-element.132), channel_id=1, source_target_pairs={{0,1},{2,3},{1,0},{3,2},{4,5},{6,7},{5,4},{7,6},{8,9},{10,11},{9,8... | collective-permute-start | bytes 12296 | tf_op jit(solution)/shard_map/ppermute | solution.py:361
  4.2 5.7 %collective-permute-start = (f32[2,1,4,128]{3,2,0,1:T(4,128)S(1)}, f32[2,1,4,128]{3,2,0,1:T(4,128)S(1)}, u32[]{:S(2)}, u32[]{:S(2)}) collective-permute-start(f32[2,1,4,128]{3,2,0,1:T(4,128)S(1)} %get-tuple-element.133), channel_id=1, source_target_pairs={{1,2},{2,1},{5,6},{6,5},{9,10},{10,9},{13,14},{14,13},{17,18},{18,... | collective-permute-start | bytes 12296 | tf_op jit(solution)/shard_map/ppermute | solution.py:362
  14.8 2.8 %collective-permute-start.3 = (f32[40,128]{1,0:T(8,128)}, f32[40,128]{1,0:T(8,128)S(1)}, u32[]{:S(2)}, u32[]{:S(2)}) collective-permute-start(f32[40,128]{1,0:T(8,128)} %get-tuple-element.68), channel_id=1, source_target_pairs={{0,8},{4,12},{8,0},{12,4},{16,24},{20,28},{24,16},{28,20},{1,9},{5... | collective-permute-start | bytes 61448 | tf_op jit(solution)/shard_map/ppermute | solution.py:302
  19.2 3.6 %collective-permute-start.4 = (f32[104,128]{1,0:T(8,128)S(1)}, f32[104,128]{1,0:T(8,128)S(1)}, u32[]{:S(2)}, u32[]{:S(2)}) collective-permute-start(f32[104,128]{1,0:T(8,128)S(1)} %pad_maximum_fusion.1), channel_id=1, source_target_pairs={{0,4},{4,0},{8,12},{12,8},{16,20},{20,16},{24,28},{28,24},{1,5},{5... | collective-permute-start | bytes 159752 | tf_op jit(solution)/shard_map/ppermute | solution.py:302
  22.8 2.6 %collective-permute-start.5 = (f32[40,128]{1,0:T(8,128)S(1)}, f32[40,128]{1,0:T(8,128)S(1)}, u32[]{:S(2)}, u32[]{:S(2)}) collective-permute-start(f32[40,128]{1,0:T(8,128)S(1)} %slice_add_fusion), channel_id=1, source_target_pairs={{0,16},{4,20},{8,24},{12,28},{16,0},{20,4},{24,8},{28,12},{1,17},{... | collective-permute-start | bytes 61448 | tf_op jit(solution)/shard_map/ppermute | solution.py:302
  23.1 13.2 %collective-permute-start.7 = (f32[1,2,256,256]{3,2,1,0:T(8,128)}, f32[1,2,256,256]{3,2,1,0:T(8,128)}, u32[]{:S(2)}, u32[]{:S(2)}) collective-permute-start(f32[1,2,256,256]{3,2,1,0:T(8,128)} %get-tuple-element.78), channel_id=1, source_target_pairs={{0,8},{4,12},{8,0},{12,4},{16,24},{20,28},{24,16},{28,20},{1,9},{5... | collective-permute-start | bytes 1572872 | tf_op jit(solution)/shard_map/ppermute | solution.py:396
  27.0 6.4 %copy-start.20 = (s32[4]{0:T(128)S(1)}, s32[4]{0:T(128)}, u32[]{:S(2)}) copy-start(s32[4]{0:T(128)} %constant.57.clone) | copy-start | bytes 52
  27.0 6.7 %copy-start.13 = (f32[4,256,256]{2,1,0:T(8,128)S(1)}, f32[4,256,256]{2,1,0:T(8,128)}, u32[]{:S(2)}) copy-start(f32[4,256,256]{2,1,0:T(8,128)} %param.18) | copy-start | bytes 3145732
  33.2 12.1 %copy-start.7 = (f32[2,256,256]{2,1,0:T(8,128)}, f32[2,256,256]{2,1,0:T(8,128)S(1)}, u32[]{:S(2)}) copy-start(f32[2,256,256]{2,1,0:T(8,128)S(1)} %get-tuple-element.74.whole_source) | copy-start | bytes 1572868
  33.2 12.1 %copy-start.9 = (f32[2,256,256]{2,1,0:T(8,128)}, f32[2,256,256]{2,1,0:T(8,128)S(1)}, u32[]{:S(2)}) copy-start(f32[2,256,256]{2,1,0:T(8,128)S(1)} %get-tuple-element.72.whole_map) | copy-start | bytes 1572868
  33.2 12.1 %collective-permute-start.6 = (f32[2,256,256]{2,1,0:T(8,128)S(1)}, f32[2,256,256]{2,1,0:T(8,128)S(1)}, u32[]{:S(2)}, u32[]{:S(2)}) collective-permute-start(f32[2,256,256]{2,1,0:T(8,128)S(1)} %get-tuple-element.74.whole_source), channel_id=1, source_target_pairs={{0,1},{2,3},{1,0},{3,2},{4,5},{6,7},{5,4},{7,6},{8,9},{10,11},{9,8... | collective-permute-start | bytes 1572872 | tf_op jit(solution)/shard_map/ppermute | solution.py:471
  33.5 18.4 %collective-permute-start.10 = (f32[1,2,256,256]{3,2,1,0:T(8,128)}, f32[1,2,256,256]{3,2,1,0:T(8,128)}, u32[]{:S(2)}, u32[]{:S(2)}) collective-permute-start(f32[1,2,256,256]{3,2,1,0:T(8,128)} %collective-permute-done.2.refs_0_), channel_id=1, source_target_pairs={{0,16},{4,20},{8,24},{12,28},{16,0},{20,4},{24,8},{28,12},{1,17},{... | collective-permute-start | bytes 1572872 | tf_op jit(solution)/shard_map/ppermute | solution.py:401
  36.2 14.2 %collective-permute-start.9 = (f32[1,2,256,256]{3,2,1,0:T(8,128)S(1)}, f32[1,2,256,256]{3,2,1,0:T(8,128)}, u32[]{:S(2)}, u32[]{:S(2)}) collective-permute-start(f32[1,2,256,256]{3,2,1,0:T(8,128)S(1)} %copy-done.21), channel_id=1, source_target_pairs={{0,8},{4,12},{8,0},{12,4},{16,24},{20,28},{24,16},{28,20},{1,9},{5... | collective-permute-start | bytes 1572872 | tf_op jit(solution)/shard_map/ppermute | solution.py:405
  37.4 19.3 %collective-permute-start.11 = (f32[1,2,256,256]{3,2,1,0:T(8,128)}, f32[1,2,256,256]{3,2,1,0:T(8,128)}, u32[]{:S(2)}, u32[]{:S(2)}) collective-permute-start(f32[1,2,256,256]{3,2,1,0:T(8,128)} %collective-permute-done.7.refs_1_), channel_id=1, source_target_pairs={{0,16},{4,20},{8,24},{12,28},{16,0},{20,4},{24,8},{28,12},{1,17},{... | collective-permute-start | bytes 1572872 | tf_op jit(solution)/shard_map/ppermute | solution.py:401
  45.3 19.4 %copy-start.15 = (f32[1,1,8,128]{3,2,0,1:T(8,128)S(1)}, f32[1,1,8,128]{3,2,0,1:T(8,128)}, u32[]{:S(2)}) copy-start(f32[1,1,8,128]{3,2,0,1:T(8,128)} %get-tuple-element.164) | copy-start | bytes 12292
  45.3 19.4 %copy-start.16 = (f32[1,1,8,128]{3,2,0,1:T(8,128)S(1)}, f32[1,1,8,128]{3,2,0,1:T(8,128)}, u32[]{:S(2)}) copy-start(f32[1,1,8,128]{3,2,0,1:T(8,128)} %get-tuple-element.165) | copy-start | bytes 12292
  47.0 13.3 %collective-permute-start.8 = (f32[2,256,256]{2,1,0:T(8,128)}, f32[2,256,256]{2,1,0:T(8,128)}, u32[]{:S(2)}, u32[]{:S(2)}) collective-permute-start(f32[2,256,256]{2,1,0:T(8,128)} %shard_map.116.before), channel_id=1, source_target_pairs={{1,2},{2,1},{5,6},{6,5},{9,10},{10,9},{13,14},{14,13},{17,18},{18,... | collective-permute-start | bytes 1572872 | tf_op jit(solution)/shard_map/ppermute | solution.py:471
  50.4 21.1 %collective-permute-start.13 = (f32[1,2,256,256]{3,2,1,0:T(8,128)}, f32[1,2,256,256]{3,2,1,0:T(8,128)}, u32[]{:S(2)}, u32[]{:S(2)}) collective-permute-start(f32[1,2,256,256]{3,2,1,0:T(8,128)} %get-tuple-element.90), channel_id=1, source_target_pairs={{0,8},{4,12},{8,0},{12,4},{16,24},{20,28},{24,16},{28,20},{1,9},{5... | collective-permute-start | bytes 1572872 | tf_op jit(solution)/shard_map/ppermute | solution.py:405
  51.7 17.1 %copy-start.6 = (f32[4,2,256,256]{3,2,1,0:T(8,128)S(1)}, f32[4,2,256,256]{3,2,1,0:T(8,128)}, u32[]{:S(2)}) copy-start(f32[4,2,256,256]{3,2,1,0:T(8,128)} %refs_2_.7) | copy-start | bytes 6291460
  51.7 22.6 %collective-permute-start.14 = (f32[1,2,256,256]{3,2,1,0:T(8,128)}, f32[1,2,256,256]{3,2,1,0:T(8,128)S(1)}, u32[]{:S(2)}, u32[]{:S(2)}) collective-permute-start(f32[1,2,256,256]{3,2,1,0:T(8,128)} %collective-permute-done.9.refs_0_), channel_id=1, source_target_pairs={{0,16},{4,20},{8,24},{12,28},{16,0},{20,4},{24,8},{28,12},{1,17},{... | collective-permute-start | bytes 1572872 | tf_op jit(solution)/shard_map/ppermute | solution.py:401
  64.5 10.2 %collective-permute-start.12 = (f32[2,256,256]{2,1,0:T(8,128)S(1)}, f32[2,256,256]{2,1,0:T(8,128)S(1)}, u32[]{:S(2)}, u32[]{:S(2)}) collective-permute-start(f32[2,256,256]{2,1,0:T(8,128)S(1)} %get-tuple-element.88), channel_id=1, source_target_pairs={{0,1},{2,3},{1,0},{3,2},{4,5},{6,7},{5,4},{7,6},{8,9},{10,11},{9,8... | collective-permute-start | bytes 1572872 | tf_op jit(solution)/shard_map/ppermute | solution.py:505
  64.7 22.2 %collective-permute-start.16 = (f32[2,256,256]{2,1,0:T(8,128)S(1)}, f32[2,256,256]{2,1,0:T(8,128)S(1)}, u32[]{:S(2)}, u32[]{:S(2)}) collective-permute-start(f32[2,256,256]{2,1,0:T(8,128)S(1)} %get-tuple-element.100), channel_id=1, source_target_pairs={{8,17},{9,18},{10,19},{12,21},{13,22},{14,23},{16,9},{17,10},{18,1... | collective-permute-start | bytes 1572872 | tf_op jit(solution)/shard_map/ppermute | solution.py:506
  71.5 22.8 %collective-permute-start.17 = (f32[1,2,256,256]{3,2,1,0:T(8,128)}, f32[1,2,256,256]{3,2,1,0:T(8,128)S(1)}, u32[]{:S(2)}, u32[]{:S(2)}) collective-permute-start(f32[1,2,256,256]{3,2,1,0:T(8,128)} %collective-permute-done.13.refs_1_), channel_id=1, source_target_pairs={{0,16},{4,20},{8,24},{12,28},{16,0},{20,4},{24,8},{28,12},{1,17},{... | collective-permute-start | bytes 1572872 | tf_op jit(solution)/shard_map/ppermute | solution.py:401
  74.8 19.5 %copy-start.11 = (f32[16,4,128]{2,1,0:T(4,128)S(1)}, f32[16,4,128]{2,1,0:T(4,128)}, u32[]{:S(2)}) copy-start(f32[16,4,128]{2,1,0:T(4,128)} %param.12) | copy-start | bytes 98308
  74.9 19.5 %copy-start.12 = (f32[16,4,128]{2,1,0:T(4,128)S(1)}, f32[16,4,128]{2,1,0:T(4,128)}, u32[]{:S(2)}) copy-start(f32[16,4,128]{2,1,0:T(4,128)} %param.10) | copy-start | bytes 98308
  74.9 19.6 %copy-start.17 = (f32[64,128]{1,0:T(8,128)S(1)}, f32[64,128]{1,0:T(8,128)}, u32[]{:S(2)}) copy-start(f32[64,128]{1,0:T(8,128)} %get-tuple-element.112) | copy-start | bytes 98308
  74.9 30.8 %collective-permute-start.15 = (f32[2,256,256]{2,1,0:T(8,128)S(1)}, f32[2,256,256]{2,1,0:T(8,128)S(1)}, u32[]{:S(2)}, u32[]{:S(2)}) collective-permute-start(f32[2,256,256]{2,1,0:T(8,128)S(1)} %broadcast_select_fusion.carried), channel_id=1, source_target_pairs={{0,8},{4,12},{8,0},{12,4},{16,24},{20,28},{24,16},{28,20},{1,9},{5... | collective-permute-start | bytes 1572872 | tf_op jit(solution)/shard_map/ppermute | solution.py:514
  94.5 10.4 %collective-permute-start.18 = (f32[64,128]{1,0:T(8,128)S(1)}, f32[64,128]{1,0:T(8,128)S(1)}, u32[]{:S(2)}, u32[]{:S(2)}) collective-permute-start(f32[64,128]{1,0:T(8,128)S(1)} %copy-done.17), channel_id=1, source_target_pairs={{4,8},{12,16},{20,24},{8,4},{16,12},{24,20},{5,9},{13,17},{21,25},... | collective-permute-start | bytes 98312 | tf_op jit(solution)/shard_map/ppermute | solution.py:533
  108.4 4.3 %collective-permute-start.19 = (f32[2,2,256,256]{3,2,1,0:T(8,128)S(1)}, f32[2,2,256,256]{3,2,1,0:T(8,128)S(1)}, u32[]{:S(2)}, u32[]{:S(2)}) collective-permute-start(f32[2,2,256,256]{3,2,1,0:T(8,128)S(1)} %get-tuple-element.121), channel_id=1, source_target_pairs={{0,4},{4,0},{8,12},{12,8},{16,20},{20,16},{24,28},{28,24},{1,5},{5... | collective-permute-start | bytes 3145736 | tf_op jit(solution)/shard_map/ppermute | solution.py:575
  112.9 2.7 %collective-permute-start.20 = (f32[2,2,256,256]{3,2,1,0:T(8,128)S(1)}, f32[2,2,256,256]{3,2,1,0:T(8,128)S(1)}, u32[]{:S(2)}, u32[]{:S(2)}) collective-permute-start(f32[2,2,256,256]{3,2,1,0:T(8,128)S(1)} %get-tuple-element.129), channel_id=1, source_target_pairs={{0,4},{4,0},{8,12},{12,8},{16,20},{20,16},{24,28},{28,24},{1,5},{5... | collective-permute-start | bytes 3145736 | tf_op jit(solution)/shard_map/ppermute | solution.py:575
  (11 other events, 31.3 us)

commit v11 on v10

--- a/solution.py
+++ b/solution.py
@@ -290,21 +290,21 @@
     )
 
 
-def exchanged(sums, ends, early):
+def exchanged(sums, ends, early, crossing):
     peers = lax.axis_size("energy")
     assert peers >= 4 and peers & (peers - 1) == 0
-    masks = [2, 1] + [1 << k for k in range(2, peers.bit_length() - 1)]
-    rows, twin_ends = sums.shape[0], None
-    first = None
+    masks = [1 << k for k in range(1, peers.bit_length() - 1)] + [1]
+    rows = sums.shape[0]
     sums, early = lax.optimization_barrier((sums, early))
-    for mask in masks:
+    for index, mask in enumerate(masks):
         given = jnp.concatenate([sums, ends]) if mask == 1 else sums
         arrived = lax.ppermute(given, "energy", [(e, e ^ mask) for e in range(peers)])
         if mask == 1:
             twin_ends = arrived[rows:]
         sums = sums + arrived[:rows]
-        first = sums if first is None else first
-    return sums, twin_ends, first, early
+        if mask != 1:
+            sums = crossing(sums, early, index)
+    return sums, twin_ends
 
 
 def per_device(
@@ -389,12 +389,16 @@
         ],
     )
     cuts = [first_cut, *cuts]
-    sums, twin_ends, crossed, arrived = exchanged(sums, ends, free_first[0])
-
-    crossed, cuts[1] = lax.optimization_barrier((crossed, cuts[1]))
-    sums, arrived = lax.optimization_barrier((sums, arrived))
-    free_first = [arrived, lax.ppermute(cuts[1], "energy", first_pairs)]
-    free_second = []
+    free_first, free_second = free_first[:1], []
+
+    def crossing(sums, early, index):
+        if index == 0:
+            sums, cuts[1] = lax.optimization_barrier((sums, cuts[1]))
+            free_first.append(lax.ppermute(cuts[1], "energy", first_pairs))
+        if index == 1:
+            sums, free_first[0] = lax.optimization_barrier((sums, early))
+            sent_on(0)
+        return sums
 
     def sent_on(part):
         given = free_first[part] if relayed else cuts[part]
@@ -404,7 +408,8 @@
         free_first[part - 1], cut = lax.optimization_barrier((free_first[part - 1], cuts[part]))
         free_first.append(lax.ppermute(cut, "energy", first_pairs))
 
-    sent_on(0)
+    sums, twin_ends = exchanged(sums, ends, free_first[0], crossing)
+
     whole_map, whole_source = call(
         own_kernel,
         32,
@@ -472,15 +477,15 @@
         if hop == 1:
             sent_on(1)
             sent_after(2)
-            beside_first[0] = beside(0, free_first[:2])
-            arrived, weights, beside_first[0] = lax.optimization_barrier(
-                (arrived, weights, beside_first[0])
+            arrived, weights, free_first[1], free_second[0] = lax.optimization_barrier(
+                (arrived, weights, free_first[1], free_second[0])
             )
         if hop == 2:
             sent_on(2)
             sent_after(3)
-            arrived, free_first[2], *free_second[:2] = lax.optimization_barrier(
-                (arrived, free_first[2], *free_second[:2])
+            beside_first[0] = beside(0, free_first[:2])
+            arrived, beside_first[0], free_first[2], free_second[1] = lax.optimization_barrier(
+                (arrived, beside_first[0], free_first[2], free_second[1])
             )
         previous, before = arrived, leaving
         if hop < peers - 2:

time: 119 us -> 121 us (1.017)
  waiting for transfers between devices: 32 us -> 34.3 us
  local copies, waits for them, and re-layouts: 7.11 us -> 5.42 us
    ppermute x4, waiting for transfers between devices: 12.3 us -> 5.9 us  [sent_on(): free_second.append(lax.ppermute(given, 'energy', relay_pairs))]
    ppermute x2, waiting for transfers between devices: 5.59 us -> 10.6 us  [per_device(): arrived = lax.ppermute(leaving, 'slab', swaps((hop - 1) % 2))]
    ppermute x1, waiting for transfers between devices: 2.16 us -> 4.23 us  [crossing(): free_first.append(lax.ppermute(cuts[1], 'energy', first_pairs))]
    unnamed x44 -> x40, local copies, waits for them, and re-layouts: 5.74 us -> 4.05 us
    ppermute x1, waiting for transfers between devices: 0.46 us -> 1.72 us  [per_device(): arrived = lax.ppermute(leaving, 'slab', swaps((peers - 2) % 2))]
  transfers between devices with their start and end apart: 21 -> 21, of which waited for: 13 -> 11; matrix products, arithmetic and copies ran while one was open for 3% -> 3% of each run, Pallas kernels for 33% -> 33%
where the time goes in v11:
time: 121 us; the launch traced here: 119 us
  Pallas kernels  41.4 us (34%)
  waiting for transfers between devices  34.3 us (28%)
  starting transfers between devices  30.5 us (25%)
  other arithmetic  6.11 us (5%)
  local copies, waits for them, and re-layouts  5.42 us (4%)
    pallas_call x13, Pallas kernels, call(): pl.pallas_call(kernel, out_shape=out_shapes, cost_estimate=cost, compiler...  41.4 us
    ppermute x2, waiting for transfers between devices, per_device(): arrived = lax.ppermute(leaving, 'slab', swaps((hop - 1) % 2))  10.6 us
    ppermute x4, waiting for transfers between devices, sent_on(): free_second.append(lax.ppermute(given, 'energy', relay_pairs))  5.9 us
    ppermute x3, starting transfers between devices, exchanged(): lax.ppermute(given, 'energy', [(e, e ^ mask) for e in range(peers)])  5.28 us
    ppermute x1, starting transfers between devices, per_device(): lax.ppermute(ends, 'energy', beyond + [(b, a) for a, b in beyond])  4.44 us
    ppermute x1, starting transfers between devices, per_device(): crossed = lax.ppermute(jnp.where(even, lower, upper), 'slab', swaps(1))  4.32 us
    ppermute x1, waiting for transfers between devices, crossing(): free_first.append(lax.ppermute(cuts[1], 'energy', first_pairs))  4.23 us
    ppermute x1, starting transfers between devices, per_device(): lax.ppermute(onward, ('energy', 'slab'), both(second_pairs))  4.13 us
  transfers between devices with their start and end apart: 21, of which 11 were waited for; matrix products, arithmetic and copies ran while one was open for 3% of the time, Pallas kernels for 33%

profile of v11, /device:TPU:13, one launch (start us, length us, event | category | flops | bytes accessed | tf_op | source)
XLA Modules:
  0.0 118.7 jit_solution(12279301079318935754)
XLA Ops:
  4.2 4.3 %collective-permute-start = (f32[2,1,4,128]{3,2,0,1:T(4,128)S(1)}, f32[2,1,4,128]{3,2,0,1:T(4,128)S(1)}, u32[]{:S(2)}, u32[]{:S(2)}) collective-permute-start(f32[2,1,4,128]{3,2,0,1:T(4,128)S(1)} %get-tuple-element.137), channel_id=1, source_target_pairs={{1,2},{2,1},{5,6},{6,5},{9,10},{10,9},{13,14},{14,13},{17,18},{18,... | collective-permute-start | bytes 12296 | tf_op jit(solution)/shard_map/ppermute | solution.py:362
  8.5 1.4 %collective-permute-done = f32[2,1,4,128]{3,2,0,1:T(4,128)S(1)} collective-permute-done((f32[2,1,4,128]{3,2,0,1:T(4,128)S(1)}, f32[2,1,4,128]{3,2,0,1:T(4,128)S(1)}, u32[]{:S(2)}, u32[]{:S(2)}) %collective-permute-start) | collective-permute-done | bytes 4128 | tf_op jit(solution)/shard_map/ppermute | solution.py:362
  10.5 3.7 %shard_map.113 = (f32[40,128]{1,0:T(8,128)}, f32[64,128]{1,0:T(8,128)}, f32[1,2,256,256]{3,2,1,0:T(8,128)}, f32[1,2,256,256]{3,2,1,0:T(8,128)}, f32[1,2,256,256]{3,2,1,0:T(8,128)}) custom-call(s32[1]{0:T(128)} %bitcast.2.mine, f32[64,128]{1,0:T(8,128)} %bitcast.48, f32[64,128]{1,0:T(8,128)} %bitcast.46, f32[64,128]{1,0:T(8,128)} %bitcast.49, ...), custom_call_target="tpu_custom_call" | custom-call | flops 301989888 | bytes 3833860 | tf_op jit(solution)/shard_map/pallas_call | solution.py:67
  16.0 1.6 %collective-permute-done.3 = f32[40,128]{1,0:T(8,128)S(1)} collective-permute-done((f32[40,128]{1,0:T(8,128)}, f32[40,128]{1,0:T(8,128)S(1)}, u32[]{:S(2)}, u32[]{:S(2)}) %collective-permute-start.3) | collective-permute-done | bytes 20512 | tf_op jit(solution)/shard_map/ppermute | solution.py:301
  18.6 2.4 %collective-permute-done.4 = f32[40,128]{1,0:T(8,128)S(1)} collective-permute-done((f32[40,128]{1,0:T(8,128)S(1)}, f32[40,128]{1,0:T(8,128)S(1)}, u32[]{:S(2)}, u32[]{:S(2)}) %collective-permute-start.4) | collective-permute-done | bytes 20512 | tf_op jit(solution)/shard_map/ppermute | solution.py:301
  21.8 3.8 %collective-permute-start.5 = (f32[104,128]{1,0:T(8,128)S(1)}, f32[104,128]{1,0:T(8,128)S(1)}, u32[]{:S(2)}, u32[]{:S(2)}) collective-permute-start(f32[104,128]{1,0:T(8,128)S(1)} %pad_maximum_fusion.1), channel_id=1, source_target_pairs={{0,4},{4,0},{8,12},{12,8},{16,20},{20,16},{24,28},{28,24},{1,5},{5... | collective-permute-start | bytes 159752 | tf_op jit(solution)/shard_map/ppermute | solution.py:301
  27.1 1.6 %copy-done.1 = f32[4,2,256,256]{3,2,1,0:T(8,128)S(1)} copy-done((f32[4,2,256,256]{3,2,1,0:T(8,128)S(1)}, f32[4,2,256,256]{3,2,1,0:T(8,128)}, u32[]{:S(2)}) %copy-start.1) | copy-done | bytes 2097176
  28.7 6.2 %shard_map.114 = (f32[2,256,256]{2,1,0:T(8,128)S(1)}, f32[2,256,256]{2,1,0:T(8,128)S(1)}) custom-call(f32[4,2,256,256]{3,2,1,0:T(8,128)S(1)} %bitcast.43, f32[4,2,256,256]{3,2,1,0:T(8,128)S(1)} %copy-done.1, f32[40,128]{1,0:T(8,128)S(1)} %slice_add_fusion.sums.refs_3_), custom_call_target="tpu_custom_call" | custom-call | flops 5133828096 | bytes 5263360 | tf_op jit(solution)/shard_map/pallas_call | solution.py:67
  35.3 4.2 %collective-permute-done.7.refs_1_ = f32[1,2,256,256]{3,2,1,0:T(8,128)} collective-permute-done((f32[1,2,256,256]{3,2,1,0:T(8,128)}, f32[1,2,256,256]{3,2,1,0:T(8,128)}, u32[]{:S(2)}, u32[]{:S(2)}) %collective-permute-start.7) | collective-permute-done | bytes 524320 | tf_op jit(solution)/shard_map/ppermute | solution.py:397
  42.2 5.8 %collective-permute-done.6.carried = f32[2,256,256]{2,1,0:T(8,128)S(1)} collective-permute-done((f32[2,256,256]{2,1,0:T(8,128)S(1)}, f32[2,256,256]{2,1,0:T(8,128)S(1)}, u32[]{:S(2)}, u32[]{:S(2)}) %collective-permute-start.6) | collective-permute-done | bytes 524320 | tf_op jit(solution)/shard_map/ppermute | solution.py:476
  48.0 1.7 %shard_map.115.before = f32[2,256,256]{2,1,0:T(8,128)} custom-call(f32[2,256,256]{2,1,0:T(8,128)S(1)} %get-tuple-element.76.whole_map, f32[2,256,256]{2,1,0:T(8,128)S(1)} %get-tuple-element.78.whole_source, f32[2,256,256]{2,1,0:T(8,128)S(1)} %collective-permute-done.6.carried), custom_call_target="tpu_custom_call" | custom-call | flops 603979776 | bytes 2097152 | tf_op jit(solution)/shard_map/pallas_call | solution.py:67
  49.7 3.4 %collective-permute-start.9 = (f32[2,256,256]{2,1,0:T(8,128)}, f32[2,256,256]{2,1,0:T(8,128)}, u32[]{:S(2)}, u32[]{:S(2)}) collective-permute-start(f32[2,256,256]{2,1,0:T(8,128)} %shard_map.115.before), channel_id=1, source_target_pairs={{1,2},{2,1},{5,6},{6,5},{9,10},{10,9},{13,14},{14,13},{17,18},{18,... | collective-permute-start | bytes 1572872 | tf_op jit(solution)/shard_map/ppermute | solution.py:476
  54.1 1.6 %copy-done.2 = f32[4,2,256,256]{3,2,1,0:T(8,128)S(1)} copy-done((f32[4,2,256,256]{3,2,1,0:T(8,128)S(1)}, f32[4,2,256,256]{3,2,1,0:T(8,128)}, u32[]{:S(2)}) %copy-start.2) | copy-done | bytes 2097176
  55.7 2.8 %shard_map.116 = (f32[2,2,256,256]{3,2,1,0:T(8,128)S(1)}, f32[2,2,256,256]{3,2,1,0:T(8,128)S(1)}) custom-call(f32[1,2,256,256]{3,2,1,0:T(8,128)} %collective-permute-done.2.refs_0_, f32[1,2,256,256]{3,2,1,0:T(8,128)} %collective-permute-done.7.refs_1_, f32[4,2,256,256]{3,2,1,0:T(8,128)S(1)} %copy-done.2, f32[40,128]{1,0:T(8,128)S(1)} %slice_add_fusion.sums.refs_3_), custom_call_target="tpu_custom_call" | custom-call | flops 1207959552 | bytes 5263360 | tf_op jit(solution)/shard_map/pallas_call | solution.py:67
  59.2 4.8 %collective-permute-done.9.carried = f32[2,256,256]{2,1,0:T(8,128)} collective-permute-done((f32[2,256,256]{2,1,0:T(8,128)}, f32[2,256,256]{2,1,0:T(8,128)}, u32[]{:S(2)}, u32[]{:S(2)}) %collective-permute-start.9) | collective-permute-done | bytes 524320 | tf_op jit(solution)/shard_map/ppermute | solution.py:476
  64.0 2.1 %shard_map.117 = (f32[2,256,256]{2,1,0:T(8,128)S(1)}, f32[2,256,256]{2,1,0:T(8,128)S(1)}) custom-call(s32[1]{0:T(128)} %bitcast.odd, f32[2,256,256]{2,1,0:T(8,128)S(1)} %copy-done.9, f32[2,256,256]{2,1,0:T(8,128)S(1)} %copy-done.7, f32[2,256,256]{2,1,0:T(8,128)} %collective-permute-done.9.carried, f32[2,256,256]{2,1,0:T(8,128)} %shard_map.115.before), custom_call_target="tpu_custom_call" | custom-call | flops 603979776 | bytes 3145732 | tf_op jit(solution)/shard_map/pallas_call | solution.py:67
  66.3 4.1 %collective-permute-start.16 = (f32[2,256,256]{2,1,0:T(8,128)S(1)}, f32[2,256,256]{2,1,0:T(8,128)S(1)}, u32[]{:S(2)}, u32[]{:S(2)}) collective-permute-start(f32[2,256,256]{2,1,0:T(8,128)S(1)} %get-tuple-element.104), channel_id=1, source_target_pairs={{8,17},{9,18},{10,19},{12,21},{13,22},{14,23},{16,9},{17,10},{18,1... | collective-permute-start | bytes 1572872 | tf_op jit(solution)/shard_map/ppermute | solution.py:511
  70.5 2.5 %shard_map.119 = (f32[2,2,256,256]{3,2,1,0:T(8,128)S(1)}, f32[2,2,256,256]{3,2,1,0:T(8,128)S(1)}) custom-call(f32[1,2,256,256]{3,2,1,0:T(8,128)S(1)} %copy-done.5, f32[1,2,256,256]{3,2,1,0:T(8,128)} %collective-permute-done.11.refs_1_, f32[4,2,256,256]{3,2,1,0:T(8,128)S(1)} %copy-done.3, f32[40,128]{1,0:T(8,128)S(1)} %slice_add_fusion.sums.refs_3_), custom_call_target="tpu_custom_call" | custom-call | flops 1207959552 | bytes 5263360 | tf_op jit(solution)/shard_map/pallas_call | solution.py:67
  73.1 2.5 %shard_map.118 = (f32[2,2,256,256]{3,2,1,0:T(8,128)S(1)}, f32[2,2,256,256]{3,2,1,0:T(8,128)S(1)}) custom-call(f32[1,2,256,256]{3,2,1,0:T(8,128)} %collective-permute-done.10.refs_0_, f32[1,2,256,256]{3,2,1,0:T(8,128)S(1)} %collective-permute-done.13.refs_1_, f32[4,2,256,256]{3,2,1,0:T(8,128)S(1)} %copy-done.3, f32[40,128]{1,0:T(8,128)S(1)} %slice_add_fusion.sums.refs_3_), custom_call_target="tpu_custom_call" | custom-call | flops 1207959552 | bytes 5263360 | tf_op jit(solution)/shard_map/pallas_call | solution.py:67
  75.7 1.7 %collective-permute-done.12 = f32[2,256,256]{2,1,0:T(8,128)S(1)} collective-permute-done((f32[2,256,256]{2,1,0:T(8,128)S(1)}, f32[2,256,256]{2,1,0:T(8,128)S(1)}, u32[]{:S(2)}, u32[]{:S(2)}) %collective-permute-start.12) | collective-permute-done | bytes 524320 | tf_op jit(solution)/shard_map/ppermute | solution.py:510
  77.5 1.4 %collective-permute-start.15 = (f32[2,256,256]{2,1,0:T(8,128)S(1)}, f32[2,256,256]{2,1,0:T(8,128)S(1)}, u32[]{:S(2)}, u32[]{:S(2)}) collective-permute-start(f32[2,256,256]{2,1,0:T(8,128)S(1)} %broadcast_select_fusion.carried), channel_id=1, source_target_pairs={{0,8},{4,12},{8,0},{12,4},{16,24},{20,28},{24,16},{28,20},{1,9},{5... | collective-permute-start | bytes 1572872 | tf_op jit(solution)/shard_map/ppermute | solution.py:519
  78.9 7.5 %shard_map.120 = (f32[4,2,256,256]{3,2,1,0:T(8,128)S(1)}, f32[2,256,256]{2,1,0:T(8,128)}) custom-call(f32[4,2,256,256]{3,2,1,0:T(8,128)S(1)} %bitcast.44, f32[4,2,256,256]{3,2,1,0:T(8,128)S(1)} %copy-done.3, f32[40,128]{1,0:T(8,128)S(1)} %slice_add_fusion.sums.refs_3_, f32[2,256,256]{2,1,0:T(8,128)S(1)} %broadcast_select_fusion.carried), custom_call_target="tpu_custom_call" | custom-call | flops 4831838208 | bytes 7360512 | tf_op jit(solution)/shard_map/pallas_call | solution.py:67
  86.4 3.2 %collective-permute-done.16.carried = f32[2,256,256]{2,1,0:T(8,128)S(1)} collective-permute-done((f32[2,256,256]{2,1,0:T(8,128)S(1)}, f32[2,256,256]{2,1,0:T(8,128)S(1)}, u32[]{:S(2)}, u32[]{:S(2)}) %collective-permute-start.16) | collective-permute-done | bytes 524320 | tf_op jit(solution)/shard_map/ppermute | solution.py:511
  89.6 5.9 %collective-permute-done.17.refs_1_ = f32[1,2,256,256]{3,2,1,0:T(8,128)S(1)} collective-permute-done((f32[1,2,256,256]{3,2,1,0:T(8,128)S(1)}, f32[1,2,256,256]{3,2,1,0:T(8,128)S(1)}, u32[]{:S(2)}, u32[]{:S(2)}) %collective-permute-start.17) | collective-permute-done | bytes 524320 | tf_op jit(solution)/shard_map/ppermute | solution.py:405
  95.6 4.4 %collective-permute-start.18 = (f32[64,128]{1,0:T(8,128)S(1)}, f32[64,128]{1,0:T(8,128)S(1)}, u32[]{:S(2)}, u32[]{:S(2)}) collective-permute-start(f32[64,128]{1,0:T(8,128)S(1)} %copy-done.16), channel_id=1, source_target_pairs={{4,8},{12,16},{20,24},{8,4},{16,12},{24,20},{5,9},{13,17},{21,25},... | collective-permute-start | bytes 98312 | tf_op jit(solution)/shard_map/ppermute | solution.py:538
  100.1 1.5 %shard_map.122 = (f32[2,2,256,256]{3,2,1,0:T(8,128)S(1)}, f32[2,2,256,256]{3,2,1,0:T(8,128)S(1)}) custom-call(f32[1,2,256,256]{3,2,1,0:T(8,128)S(1)} %collective-permute-done.14.refs_0_, f32[1,2,256,256]{3,2,1,0:T(8,128)S(1)} %collective-permute-done.17.refs_1_, f32[4,2,256,256]{3,2,1,0:T(8,128)S(1)} %copy-done.3, f32[40,128]{1,0:T(8,128)S(1)} %slice_add_fusion.sums.refs_3_), custom_call_target="tpu_custom_call" | custom-call | flops 1207959552 | bytes 5263360 | tf_op jit(solution)/shard_map/pallas_call | solution.py:67
  101.6 1.9 %shard_map.121 = (f32[2,2,256,256]{3,2,1,0:T(8,128)S(1)}, f32[2,256,256]{2,1,0:T(8,128)S(1)}) custom-call(f32[2,2,256,256]{3,2,1,0:T(8,128)S(1)} %get-tuple-element.102.link, f32[2,2,256,256]{3,2,1,0:T(8,128)S(1)} %get-tuple-element.103.source, f32[2,256,256]{2,1,0:T(8,128)S(1)} %collective-permute-done.16.carried), custom_call_target="tpu_custom_call" | custom-call | flops 1207959552 | bytes 4194304 | tf_op jit(solution)/shard_map/pallas_call | solution.py:67
  103.6 2.6 %shard_map.123 = (f32[2,2,256,256]{3,2,1,0:T(8,128)S(1)}, f32[2,256,256]{2,1,0:T(8,128)}) custom-call(f32[2,2,256,256]{3,2,1,0:T(8,128)S(1)} %get-tuple-element.110.link, f32[2,2,256,256]{3,2,1,0:T(8,128)S(1)} %get-tuple-element.111.source, f32[2,256,256]{2,1,0:T(8,128)S(1)} %get-tuple-element.112.carried), custom_call_target="tpu_custom_call" | custom-call | flops 1207959552 | bytes 4194304 | tf_op jit(solution)/shard_map/pallas_call | solution.py:67
  107.0 2.7 %shard_map.124 = (f32[2,2,256,256]{3,2,1,0:T(8,128)S(1)}, f32[2,2,256,256]{3,2,1,0:T(8,128)S(1)}, f32[2,256,256]{2,1,0:T(8,128)S(1)}) custom-call(s32[2]{0:T(128)S(1)} %pad_add_fusion.pick, f32[2,2,256,256]{3,2,1,0:T(8,128)S(1)} %get-tuple-element.118.link, f32[2,2,256,256]{3,2,1,0:T(8,128)S(1)} %get-tuple-element.119.source, ...), custom_call_target="tpu_custom_call" | custom-call | flops 1207959552 | bytes 9437192 | tf_op jit(solution)/shard_map/pallas_call | solution.py:67
  110.7 3.5 %shard_map.125 = (f32[2,2,256,256]{3,2,1,0:T(8,128)S(1)}, f32[2,2,256,256]{3,2,1,0:T(8,128)S(1)}, f32[2,256,256]{2,1,0:T(8,128)}) custom-call(s32[2]{0:T(128)S(1)} %pad_add_fusion.pick, f32[2,2,256,256]{3,2,1,0:T(8,128)S(1)} %get-tuple-element.126.link, f32[2,2,256,256]{3,2,1,0:T(8,128)S(1)} %get-tuple-element.127.source, ...), custom_call_target="tpu_custom_call" | custom-call | flops 1207959552 | bytes 9437192 | tf_op jit(solution)/shard_map/pallas_call | solution.py:67
  114.5 2.6 %collective-permute-done.20 = f32[2,2,256,256]{3,2,1,0:T(8,128)S(1)} collective-permute-done((f32[2,2,256,256]{3,2,1,0:T(8,128)S(1)}, f32[2,2,256,256]{3,2,1,0:T(8,128)S(1)}, u32[]{:S(2)}, u32[]{:S(2)}) %collective-permute-start.20) | collective-permute-done | bytes 1048608 | tf_op jit(solution)/shard_map/ppermute | solution.py:580
  117.3 1.5 %maximum_bitcast_fusion = f32[1,4,2,256,256]{4,3,2,1,0:T(8,128)} fusion(f32[2,2,256,256]{3,2,1,0:T(8,128)S(1)} %add.131, f32[2,2,256,256]{3,2,1,0:T(8,128)S(1)} %add.130), kind=kLoop, calls=%fused_computation.1 | loop fusion | flops 524288 | bytes 4194304 | tf_op jit(solution)/shard_map/broadcast_in_dim | solution.py:581
  (87 shorter events, 16.5 us)
Async XLA Ops:
  0.6 26.5 %copy-start = (f32[1,4,2,256,256]{4,3,2,1,0:T(8,128)S(1)}, f32[1,4,2,256,256]{4,3,2,1,0:T(8,128)}, u32[]{:S(2)}) copy-start(f32[1,4,2,256,256]{4,3,2,1,0:T(8,128)} %param.14) | copy-start | bytes 6291460
  1.9 13.0 %collective-permute-start.2 = (f32[1,2,256,256]{3,2,1,0:T(8,128)S(1)}, f32[1,2,256,256]{3,2,1,0:T(8,128)}, u32[]{:S(2)}, u32[]{:S(2)}) collective-permute-start(f32[1,2,256,256]{3,2,1,0:T(8,128)S(1)} %slice_bitcast_fusion), channel_id=1, source_target_pairs={{0,8},{4,12},{8,0},{12,4},{16,24},{20,28},{24,16},{28,20},{1,9},{5... | collective-permute-start | bytes 1572872 | tf_op jit(solution)/shard_map/ppermute | solution.py:347
  4.0 4.6 %collective-permute-start.1 = (f32[2,1,4,128]{3,2,0,1:T(4,128)S(1)}, f32[2,1,4,128]{3,2,0,1:T(4,128)S(1)}, u32[]{:S(2)}, u32[]{:S(2)}) collective-permute-start(f32[2,1,4,128]{3,2,0,1:T(4,128)S(1)} %get-tuple-element.136), channel_id=1, source_target_pairs={{0,1},{2,3},{1,0},{3,2},{4,5},{6,7},{5,4},{7,6},{8,9},{10,11},{9,8... | collective-permute-start | bytes 12296 | tf_op jit(solution)/shard_map/ppermute | solution.py:361
  4.2 5.7 %collective-permute-start = (f32[2,1,4,128]{3,2,0,1:T(4,128)S(1)}, f32[2,1,4,128]{3,2,0,1:T(4,128)S(1)}, u32[]{:S(2)}, u32[]{:S(2)}) collective-permute-start(f32[2,1,4,128]{3,2,0,1:T(4,128)S(1)} %get-tuple-element.137), channel_id=1, source_target_pairs={{1,2},{2,1},{5,6},{6,5},{9,10},{10,9},{13,14},{14,13},{17,18},{18,... | collective-permute-start | bytes 12296 | tf_op jit(solution)/shard_map/ppermute | solution.py:362
  14.8 2.8 %collective-permute-start.3 = (f32[40,128]{1,0:T(8,128)}, f32[40,128]{1,0:T(8,128)S(1)}, u32[]{:S(2)}, u32[]{:S(2)}) collective-permute-start(f32[40,128]{1,0:T(8,128)} %get-tuple-element.70), channel_id=1, source_target_pairs={{0,8},{4,12},{8,0},{12,4},{16,24},{20,28},{24,16},{28,20},{1,9},{5... | collective-permute-start | bytes 61448 | tf_op jit(solution)/shard_map/ppermute | solution.py:301
  18.4 2.6 %collective-permute-start.4 = (f32[40,128]{1,0:T(8,128)S(1)}, f32[40,128]{1,0:T(8,128)S(1)}, u32[]{:S(2)}, u32[]{:S(2)}) collective-permute-start(f32[40,128]{1,0:T(8,128)S(1)} %add.105), channel_id=1, source_target_pairs={{0,16},{4,20},{8,24},{12,28},{16,0},{20,4},{24,8},{28,12},{1,17},{... | collective-permute-start | bytes 61448 | tf_op jit(solution)/shard_map/ppermute | solution.py:301
  21.8 5.3 %collective-permute-start.5 = (f32[104,128]{1,0:T(8,128)S(1)}, f32[104,128]{1,0:T(8,128)S(1)}, u32[]{:S(2)}, u32[]{:S(2)}) collective-permute-start(f32[104,128]{1,0:T(8,128)S(1)} %pad_maximum_fusion.1), channel_id=1, source_target_pairs={{0,4},{4,0},{8,12},{12,8},{16,20},{20,16},{24,28},{28,24},{1,5},{5... | collective-permute-start | bytes 159752 | tf_op jit(solution)/shard_map/ppermute | solution.py:301
  25.7 13.9 %collective-permute-start.7 = (f32[1,2,256,256]{3,2,1,0:T(8,128)}, f32[1,2,256,256]{3,2,1,0:T(8,128)}, u32[]{:S(2)}, u32[]{:S(2)}) collective-permute-start(f32[1,2,256,256]{3,2,1,0:T(8,128)} %get-tuple-element.80), channel_id=1, source_target_pairs={{0,8},{4,12},{8,0},{12,4},{16,24},{20,28},{24,16},{28,20},{1,9},{5... | collective-permute-start | bytes 1572872 | tf_op jit(solution)/shard_map/ppermute | solution.py:397
  26.9 14.6 %collective-permute-start.8 = (f32[1,2,256,256]{3,2,1,0:T(8,128)}, f32[1,2,256,256]{3,2,1,0:T(8,128)S(1)}, u32[]{:S(2)}, u32[]{:S(2)}) collective-permute-start(f32[1,2,256,256]{3,2,1,0:T(8,128)} %collective-permute-done.2.refs_0_), channel_id=1, source_target_pairs={{0,16},{4,20},{8,24},{12,28},{16,0},{20,4},{24,8},{28,12},{1,17},{... | collective-permute-start | bytes 1572872 | tf_op jit(solution)/shard_map/ppermute | solution.py:405
  28.7 12.0 %copy-start.12 = (f32[4,256,256]{2,1,0:T(8,128)S(1)}, f32[4,256,256]{2,1,0:T(8,128)}, u32[]{:S(2)}) copy-start(f32[4,256,256]{2,1,0:T(8,128)} %param.18) | copy-start | bytes 3145732
  34.9 14.8 %copy-start.6 = (f32[2,256,256]{2,1,0:T(8,128)}, f32[2,256,256]{2,1,0:T(8,128)S(1)}, u32[]{:S(2)}) copy-start(f32[2,256,256]{2,1,0:T(8,128)S(1)} %get-tuple-element.78.whole_source) | copy-start | bytes 1572868
  34.9 14.8 %copy-start.8 = (f32[2,256,256]{2,1,0:T(8,128)}, f32[2,256,256]{2,1,0:T(8,128)S(1)}, u32[]{:S(2)}) copy-start(f32[2,256,256]{2,1,0:T(8,128)S(1)} %get-tuple-element.76.whole_map) | copy-start | bytes 1572868
  34.9 13.1 %collective-permute-start.6 = (f32[2,256,256]{2,1,0:T(8,128)S(1)}, f32[2,256,256]{2,1,0:T(8,128)S(1)}, u32[]{:S(2)}, u32[]{:S(2)}) collective-permute-start(f32[2,256,256]{2,1,0:T(8,128)S(1)} %get-tuple-element.78.whole_source), channel_id=1, source_target_pairs={{0,1},{2,3},{1,0},{3,2},{4,5},{6,7},{5,4},{7,6},{8,9},{10,11},{9,8... | collective-permute-start | bytes 1572872 | tf_op jit(solution)/shard_map/ppermute | solution.py:476
  39.5 13.6 %collective-permute-start.10 = (f32[1,2,256,256]{3,2,1,0:T(8,128)}, f32[1,2,256,256]{3,2,1,0:T(8,128)}, u32[]{:S(2)}, u32[]{:S(2)}) collective-permute-start(f32[1,2,256,256]{3,2,1,0:T(8,128)} %get-tuple-element.88), channel_id=1, source_target_pairs={{0,8},{4,12},{8,0},{12,4},{16,24},{20,28},{24,16},{28,20},{1,9},{5... | collective-permute-start | bytes 1572872 | tf_op jit(solution)/shard_map/ppermute | solution.py:409
  41.1 18.1 %collective-permute-start.11 = (f32[1,2,256,256]{3,2,1,0:T(8,128)}, f32[1,2,256,256]{3,2,1,0:T(8,128)}, u32[]{:S(2)}, u32[]{:S(2)}) collective-permute-start(f32[1,2,256,256]{3,2,1,0:T(8,128)} %collective-permute-done.7.refs_1_), channel_id=1, source_target_pairs={{0,16},{4,20},{8,24},{12,28},{16,0},{20,4},{24,8},{28,12},{1,17},{... | collective-permute-start | bytes 1572872 | tf_op jit(solution)/shard_map/ppermute | solution.py:405
  49.7 14.3 %collective-permute-start.9 = (f32[2,256,256]{2,1,0:T(8,128)}, f32[2,256,256]{2,1,0:T(8,128)}, u32[]{:S(2)}, u32[]{:S(2)}) collective-permute-start(f32[2,256,256]{2,1,0:T(8,128)} %shard_map.115.before), channel_id=1, source_target_pairs={{1,2},{2,1},{5,6},{6,5},{9,10},{10,9},{13,14},{14,13},{17,18},{18,... | collective-permute-start | bytes 1572872 | tf_op jit(solution)/shard_map/ppermute | solution.py:476
  53.1 19.9 %collective-permute-start.13 = (f32[1,2,256,256]{3,2,1,0:T(8,128)}, f32[1,2,256,256]{3,2,1,0:T(8,128)S(1)}, u32[]{:S(2)}, u32[]{:S(2)}) collective-permute-start(f32[1,2,256,256]{3,2,1,0:T(8,128)} %get-tuple-element.94), channel_id=1, source_target_pairs={{0,8},{4,12},{8,0},{12,4},{16,24},{20,28},{24,16},{28,20},{1,9},{5... | collective-permute-start | bytes 1572872 | tf_op jit(solution)/shard_map/ppermute | solution.py:409
  55.7 8.3 %copy-start.7 = (f32[2,256,256]{2,1,0:T(8,128)S(1)}, f32[2,256,256]{2,1,0:T(8,128)}, u32[]{:S(2)}) copy-start(f32[2,256,256]{2,1,0:T(8,128)} %copy-done.6) | copy-start | bytes 1572868
  55.7 8.3 %copy-start.9 = (f32[2,256,256]{2,1,0:T(8,128)S(1)}, f32[2,256,256]{2,1,0:T(8,128)}, u32[]{:S(2)}) copy-start(f32[2,256,256]{2,1,0:T(8,128)} %copy-done.8) | copy-start | bytes 1572868
  55.7 14.8 %copy-start.5 = (f32[1,2,256,256]{3,2,1,0:T(8,128)S(1)}, f32[1,2,256,256]{3,2,1,0:T(8,128)}, u32[]{:S(2)}) copy-start(f32[1,2,256,256]{3,2,1,0:T(8,128)} %copy-done.4) | copy-start | bytes 1572868
  58.6 11.9 %copy-start.3 = (f32[4,2,256,256]{3,2,1,0:T(8,128)S(1)}, f32[4,2,256,256]{3,2,1,0:T(8,128)}, u32[]{:S(2)}) copy-start(f32[4,2,256,256]{3,2,1,0:T(8,128)} %refs_2_.7) | copy-start | bytes 6291460
  58.6 17.1 %collective-permute-start.14 = (f32[1,2,256,256]{3,2,1,0:T(8,128)}, f32[1,2,256,256]{3,2,1,0:T(8,128)S(1)}, u32[]{:S(2)}, u32[]{:S(2)}) collective-permute-start(f32[1,2,256,256]{3,2,1,0:T(8,128)} %collective-permute-done.10.refs_0_), channel_id=1, source_target_pairs={{0,16},{4,20},{8,24},{12,28},{16,0},{20,4},{24,8},{28,12},{1,17},{... | collective-permute-start | bytes 1572872 | tf_op jit(solution)/shard_map/ppermute | solution.py:405
  66.2 11.2 %collective-permute-start.12 = (f32[2,256,256]{2,1,0:T(8,128)S(1)}, f32[2,256,256]{2,1,0:T(8,128)S(1)}, u32[]{:S(2)}, u32[]{:S(2)}) collective-permute-start(f32[2,256,256]{2,1,0:T(8,128)S(1)} %get-tuple-element.92), channel_id=1, source_target_pairs={{0,1},{2,3},{1,0},{3,2},{4,5},{6,7},{5,4},{7,6},{8,9},{10,11},{9,8... | collective-permute-start | bytes 1572872 | tf_op jit(solution)/shard_map/ppermute | solution.py:510
  66.3 23.3 %collective-permute-start.16 = (f32[2,256,256]{2,1,0:T(8,128)S(1)}, f32[2,256,256]{2,1,0:T(8,128)S(1)}, u32[]{:S(2)}, u32[]{:S(2)}) collective-permute-start(f32[2,256,256]{2,1,0:T(8,128)S(1)} %get-tuple-element.104), channel_id=1, source_target_pairs={{8,17},{9,18},{10,19},{12,21},{13,22},{14,23},{16,9},{17,10},{18,1... | collective-permute-start | bytes 1572872 | tf_op jit(solution)/shard_map/ppermute | solution.py:511
  73.0 22.4 %collective-permute-start.17 = (f32[1,2,256,256]{3,2,1,0:T(8,128)S(1)}, f32[1,2,256,256]{3,2,1,0:T(8,128)S(1)}, u32[]{:S(2)}, u32[]{:S(2)}) collective-permute-start(f32[1,2,256,256]{3,2,1,0:T(8,128)S(1)} %collective-permute-done.13.refs_1_), channel_id=1, source_target_pairs={{0,16},{4,20},{8,24},{12,28},{16,0},{20,4},{24,8},{28,12},{1,17},{... | collective-permute-start | bytes 1572872 | tf_op jit(solution)/shard_map/ppermute | solution.py:405
  77.5 18.0 %copy-start.10 = (f32[16,4,128]{2,1,0:T(4,128)S(1)}, f32[16,4,128]{2,1,0:T(4,128)}, u32[]{:S(2)}) copy-start(f32[16,4,128]{2,1,0:T(4,128)} %param.12) | copy-start | bytes 98308
  77.5 18.0 %copy-start.11 = (f32[16,4,128]{2,1,0:T(4,128)S(1)}, f32[16,4,128]{2,1,0:T(4,128)}, u32[]{:S(2)}) copy-start(f32[16,4,128]{2,1,0:T(4,128)} %param.10) | copy-start | bytes 98308
  77.5 18.1 %copy-start.16 = (f32[64,128]{1,0:T(8,128)S(1)}, f32[64,128]{1,0:T(8,128)}, u32[]{:S(2)}) copy-start(f32[64,128]{1,0:T(8,128)} %get-tuple-element.116) | copy-start | bytes 98308
  77.5 29.5 %collective-permute-start.15 = (f32[2,256,256]{2,1,0:T(8,128)S(1)}, f32[2,256,256]{2,1,0:T(8,128)S(1)}, u32[]{:S(2)}, u32[]{:S(2)}) collective-permute-start(f32[2,256,256]{2,1,0:T(8,128)S(1)} %broadcast_select_fusion.carried), channel_id=1, source_target_pairs={{0,8},{4,12},{8,0},{12,4},{16,24},{20,28},{24,16},{28,20},{1,9},{5... | collective-permute-start | bytes 1572872 | tf_op jit(solution)/shard_map/ppermute | solution.py:519
  95.6 10.6 %collective-permute-start.18 = (f32[64,128]{1,0:T(8,128)S(1)}, f32[64,128]{1,0:T(8,128)S(1)}, u32[]{:S(2)}, u32[]{:S(2)}) collective-permute-start(f32[64,128]{1,0:T(8,128)S(1)} %copy-done.16), channel_id=1, source_target_pairs={{4,8},{12,16},{20,24},{8,4},{16,12},{24,20},{5,9},{13,17},{21,25},... | collective-permute-start | bytes 98312 | tf_op jit(solution)/shard_map/ppermute | solution.py:538
  109.8 4.5 %collective-permute-start.19 = (f32[2,2,256,256]{3,2,1,0:T(8,128)S(1)}, f32[2,2,256,256]{3,2,1,0:T(8,128)S(1)}, u32[]{:S(2)}, u32[]{:S(2)}) collective-permute-start(f32[2,2,256,256]{3,2,1,0:T(8,128)S(1)} %get-tuple-element.125), channel_id=1, source_target_pairs={{0,4},{4,0},{8,12},{12,8},{16,20},{20,16},{24,28},{28,24},{1,5},{5... | collective-permute-start | bytes 3145736 | tf_op jit(solution)/shard_map/ppermute | solution.py:580
  114.4 2.7 %collective-permute-start.20 = (f32[2,2,256,256]{3,2,1,0:T(8,128)S(1)}, f32[2,2,256,256]{3,2,1,0:T(8,128)S(1)}, u32[]{:S(2)}, u32[]{:S(2)}) collective-permute-start(f32[2,2,256,256]{3,2,1,0:T(8,128)S(1)} %get-tuple-element.133), channel_id=1, source_target_pairs={{0,4},{4,0},{8,12},{12,8},{16,20},{20,16},{24,28},{28,24},{1,5},{5... | collective-permute-start | bytes 3145736 | tf_op jit(solution)/shard_map/ppermute | solution.py:580
  (9 other events, 41.7 us)

commit v12 on v9

--- a/solution.py
+++ b/solution.py
@@ -404,7 +404,6 @@
         free_first[part - 1], cut = lax.optimization_barrier((free_first[part - 1], cuts[part]))
         free_first.append(lax.ppermute(cut, "energy", first_pairs))
 
-    sent_on(0)
     whole_map, whole_source = call(
         own_kernel,
         32,
@@ -470,6 +469,12 @@
     for hop in range(1, peers - 1):
         arrived = lax.ppermute(leaving, "slab", swaps((hop - 1) % 2))
         if hop == 1:
+            if relayed:
+                begins = (mine >= 2) & (mine < 6)
+                given = jnp.where(begins, cuts[-1], free_first[0])
+                free_second.append(lax.ppermute(given, "energy", relay_pairs))
+            else:
+                sent_on(0)
             sent_on(1)
             sent_after(2)
             arrived, weights, free_first[1] = lax.optimization_barrier(
@@ -478,6 +483,7 @@
         if hop == 2:
             sent_on(2)
             sent_after(3)
+            free_first[:3] = lax.optimization_barrier(free_first[:3])
             beside_first[0] = beside(0, free_first[:2])
             arrived, beside_first[0], free_first[2], *free_second[:2] = lax.optimization_barrier(
                 (arrived, beside_first[0], free_first[2], *free_second[:2])
@@ -504,7 +510,10 @@
 
     arrived = lax.ppermute(leaving, "slab", swaps((peers - 2) % 2))
     carried_second = lax.ppermute(onward, ("energy", "slab"), both(second_pairs))
-    sent_on(3)
+    free_first[3], around = lax.optimization_barrier(
+        (free_first[3], free_second[0] if relayed else cuts[-1])
+    )
+    free_second.append(lax.ppermute(around, "energy", first_pairs if relayed else second_pairs))
     beside_second[0] = beside(0, free_second[:2])
     beside_first[1] = beside(1, free_first[2:])
     arrived, beside_first[1], beside_second[0], free_second[2] = lax.optimization_barrier(
@@ -536,6 +545,7 @@
     edge = jnp.zeros((2, cells, rows, 1), jnp.float32)
     halos = ((wire_before, wire_after), (ends_before[:, 1], ends_after[:, 0]), (edge, edge))
     potential_new = relaxed(field, perm, charge, halos)
+
 
     beside_second[1] = beside(1, free_second[2:])
     greens_second = []

time: 117 us -> 120 us (1.026); the launches traced: 115 us -> 120 us
  starting transfers between devices: 29.9 us -> 35.1 us
  waiting for transfers between devices: 31.9 us -> 26.7 us
  other arithmetic: 6.11 us -> 8.14 us
  Pallas kernels: 41.5 us -> 42.9 us
    ppermute x4 -> x2, waiting for transfers between devices: 7.46 us -> 0.07 us  [sent_on(): free_second.append(lax.ppermute(given, 'energy', relay_pairs))]
    ppermute x1, starting transfers between devices: 4.46 us -> 10.1 us  [per_device(): lax.ppermute(ends, 'energy', beyond + [(b, a) for a, b in beyond])]
    ppermute x0 -> x2, waiting for transfers between devices: none -> 5.26 us  [the longest x1 5.25 us: per_device(): lax.ppermute(around, 'energy', first_pairs if relayed else second_pairs)]
    select_n x0 -> x1, other arithmetic: none -> 2 us  [per_device(): given = jnp.where(begins, cuts[-1], free_first[0])]
    ppermute x1, waiting for transfers between devices: 2.47 us -> 0.71 us  [per_device(): free_first = [arrived, lax.ppermute(cuts[1], 'energy', first_pairs)]]
    pallas_call x13, Pallas kernels: 41.5 us -> 42.9 us  [call(): pl.pallas_call(kernel, out_shape=out_shapes, cost_estimate=cost, compiler...]
    unnamed x36 -> x38, local copies, waits for them, and re-layouts: 3.25 us -> 4.29 us
  transfers between devices with their start and end apart: 21 -> 21, of which waited for: 13 -> 13; matrix products, arithmetic and copies ran while one was open for 3% -> 4% of each run, Pallas kernels for 34% -> 34%
where the time goes in v12:
time: 120 us
  Pallas kernels  42.9 us (36%)
  starting transfers between devices  35.1 us (29%)
  waiting for transfers between devices  26.7 us (22%)
  other arithmetic  8.14 us (7%)
  local copies, waits for them, and re-layouts  5.67 us (5%)
    pallas_call x13, Pallas kernels, call(): pl.pallas_call(kernel, out_shape=out_shapes, cost_estimate=cost, compiler...  42.9 us
    ppermute x1, starting transfers between devices, per_device(): lax.ppermute(ends, 'energy', beyond + [(b, a) for a, b in beyond])  10.1 us
    ppermute x2, waiting for transfers between devices, per_device(): arrived = lax.ppermute(leaving, 'slab', swaps((hop - 1) % 2))  9.18 us
    ppermute x1, waiting for transfers between devices, per_device(): lax.ppermute(around, 'energy', first_pairs if relayed else second_pairs)  5.25 us
    ppermute x1, starting transfers between devices, per_device(): crossed = lax.ppermute(jnp.where(even, lower, upper), 'slab', swaps(1))  4.32 us
    unnamed x38, local copies, waits for them, and re-layouts  4.29 us
    ppermute x3, starting transfers between devices, exchanged(): lax.ppermute(given, 'energy', [(e, e ^ mask) for e in range(peers)])  4.13 us
    ppermute x1, starting transfers between devices, per_device(): lax.ppermute(onward, ('energy', 'slab'), both(second_pairs))  4.07 us
  transfers between devices with their start and end apart: 21, of which 13 were waited for; matrix products, arithmetic and copies ran while one was open for 4% of the time, Pallas kernels for 34%

profile of v12, /device:TPU:13, one launch (start us, length us, event | category | flops | bytes accessed | tf_op | source)
XLA Modules:
  0.0 119.5 jit_solution(15825259163039655938)
XLA Ops:
  1.9 1.3 %collective-permute-start.2 = (f32[1,2,256,256]{3,2,1,0:T(8,128)S(1)}, f32[1,2,256,256]{3,2,1,0:T(8,128)S(1)}, u32[]{:S(2)}, u32[]{:S(2)}) collective-permute-start(f32[1,2,256,256]{3,2,1,0:T(8,128)S(1)} %slice_bitcast_fusion), channel_id=1, source_target_pairs={{0,8},{4,12},{8,0},{12,4},{16,24},{20,28},{24,16},{28,20},{1,9},{5... | collective-permute-start | bytes 1572872 | tf_op jit(solution)/shard_map/ppermute | solution.py:347
  4.2 4.3 %collective-permute-start = (f32[2,1,4,128]{3,2,0,1:T(4,128)S(1)}, f32[2,1,4,128]{3,2,0,1:T(4,128)S(1)}, u32[]{:S(2)}, u32[]{:S(2)}) collective-permute-start(f32[2,1,4,128]{3,2,0,1:T(4,128)S(1)} %get-tuple-element.145), channel_id=1, source_target_pairs={{1,2},{2,1},{5,6},{6,5},{9,10},{10,9},{13,14},{14,13},{17,18},{18,... | collective-permute-start | bytes 12296 | tf_op jit(solution)/shard_map/ppermute | solution.py:362
  8.5 1.3 %collective-permute-done = f32[2,1,4,128]{3,2,0,1:T(4,128)S(1)} collective-permute-done((f32[2,1,4,128]{3,2,0,1:T(4,128)S(1)}, f32[2,1,4,128]{3,2,0,1:T(4,128)S(1)}, u32[]{:S(2)}, u32[]{:S(2)}) %collective-permute-start) | collective-permute-done | bytes 4128 | tf_op jit(solution)/shard_map/ppermute | solution.py:362
  10.4 3.7 %shard_map.113 = (f32[40,128]{1,0:T(8,128)}, f32[64,128]{1,0:T(8,128)}, f32[1,2,256,256]{3,2,1,0:T(8,128)}, f32[1,2,256,256]{3,2,1,0:T(8,128)}, f32[1,2,256,256]{3,2,1,0:T(8,128)}) custom-call(s32[1]{0:T(128)} %bitcast.2.mine, f32[64,128]{1,0:T(8,128)} %bitcast.48, f32[64,128]{1,0:T(8,128)} %bitcast.46, f32[64,128]{1,0:T(8,128)} %bitcast.49, ...), custom_call_target="tpu_custom_call" | custom-call | flops 301989888 | bytes 3833860 | tf_op jit(solution)/shard_map/pallas_call | solution.py:67
  15.9 1.6 %collective-permute-done.3 = f32[40,128]{1,0:T(8,128)S(1)} collective-permute-done((f32[40,128]{1,0:T(8,128)}, f32[40,128]{1,0:T(8,128)S(1)}, u32[]{:S(2)}, u32[]{:S(2)}) %collective-permute-start.3) | collective-permute-done | bytes 20512 | tf_op jit(solution)/shard_map/ppermute | solution.py:302
  19.1 2.7 %collective-permute-start.4 = (f32[104,128]{1,0:T(8,128)S(1)}, f32[104,128]{1,0:T(8,128)S(1)}, u32[]{:S(2)}, u32[]{:S(2)}) collective-permute-start(f32[104,128]{1,0:T(8,128)S(1)} %pad_maximum_fusion.1), channel_id=1, source_target_pairs={{0,4},{4,0},{8,12},{12,8},{16,20},{20,16},{24,28},{28,24},{1,5},{5... | collective-permute-start | bytes 159752 | tf_op jit(solution)/shard_map/ppermute | solution.py:302
  25.3 1.6 %copy-done.3 = f32[4,2,256,256]{3,2,1,0:T(8,128)S(1)} copy-done((f32[4,2,256,256]{3,2,1,0:T(8,128)S(1)}, f32[4,2,256,256]{3,2,1,0:T(8,128)}, u32[]{:S(2)}) %copy-start.3) | copy-done | bytes 2097176
  26.9 6.2 %shard_map.114 = (f32[2,256,256]{2,1,0:T(8,128)S(1)}, f32[2,256,256]{2,1,0:T(8,128)}) custom-call(f32[4,2,256,256]{3,2,1,0:T(8,128)S(1)} %bitcast.43, f32[4,2,256,256]{3,2,1,0:T(8,128)S(1)} %copy-done.3, f32[40,128]{1,0:T(8,128)S(1)} %add.107.sums.refs_3_), custom_call_target="tpu_custom_call" | custom-call | flops 5133828096 | bytes 5263360 | tf_op jit(solution)/shard_map/pallas_call | solution.py:67
  33.4 2.0 %broadcast_select_fusion = f32[1,2,256,256]{3,2,1,0:T(8,128)} fusion(f32[1,2,256,256]{3,2,1,0:T(8,128)} %get-tuple-element.100, f32[1,2,256,256]{3,2,1,0:T(8,128)S(1)} %collective-permute-done.2.refs_0_, pred[]{:T(512)S(6)} %and.30), kind=kLoop, calls=%fused_computation.3 | loop fusion | flops 131072 | bytes 1572865 | tf_op jit(solution)/shard_map/jit(_where)/select_n | solution.py:474
  37.7 1.3 %collective-permute-start.11 = (f32[1,2,256,256]{3,2,1,0:T(8,128)}, f32[1,2,256,256]{3,2,1,0:T(8,128)}, u32[]{:S(2)}, u32[]{:S(2)}) collective-permute-start(f32[1,2,256,256]{3,2,1,0:T(8,128)} %collective-permute-done.7.refs_1_), channel_id=1, source_target_pairs={{0,16},{4,20},{8,24},{12,28},{16,0},{20,4},{24,8},{28,12},{1,17},{... | collective-permute-start | bytes 1572872 | tf_op jit(solution)/shard_map/ppermute | solution.py:401
  39.0 6.3 %collective-permute-done.6.carried = f32[2,256,256]{2,1,0:T(8,128)} collective-permute-done((f32[2,256,256]{2,1,0:T(8,128)}, f32[2,256,256]{2,1,0:T(8,128)}, u32[]{:S(2)}, u32[]{:S(2)}) %collective-permute-start.6) | collective-permute-done | bytes 524320 | tf_op jit(solution)/shard_map/ppermute | solution.py:470
  45.4 2.9 %shard_map.115.before = f32[2,256,256]{2,1,0:T(8,128)} custom-call(f32[2,256,256]{2,1,0:T(8,128)S(1)} %copy-done.7, f32[2,256,256]{2,1,0:T(8,128)} %get-tuple-element.80.whole_source, f32[2,256,256]{2,1,0:T(8,128)} %collective-permute-done.6.carried), custom_call_target="tpu_custom_call" | custom-call | flops 603979776 | bytes 2097152 | tf_op jit(solution)/shard_map/pallas_call | solution.py:67
  48.3 3.5 %collective-permute-start.8 = (f32[2,256,256]{2,1,0:T(8,128)}, f32[2,256,256]{2,1,0:T(8,128)}, u32[]{:S(2)}, u32[]{:S(2)}) collective-permute-start(f32[2,256,256]{2,1,0:T(8,128)} %shard_map.115.before), channel_id=1, source_target_pairs={{1,2},{2,1},{5,6},{6,5},{9,10},{10,9},{13,14},{14,13},{17,18},{18,... | collective-permute-start | bytes 1572872 | tf_op jit(solution)/shard_map/ppermute | solution.py:470
  54.0 1.6 %copy-done.4 = f32[4,2,256,256]{3,2,1,0:T(8,128)S(1)} copy-done((f32[4,2,256,256]{3,2,1,0:T(8,128)S(1)}, f32[4,2,256,256]{3,2,1,0:T(8,128)}, u32[]{:S(2)}) %copy-start.4) | copy-done | bytes 2097176
  55.6 2.6 %shard_map.116 = (f32[2,2,256,256]{3,2,1,0:T(8,128)S(1)}, f32[2,2,256,256]{3,2,1,0:T(8,128)S(1)}) custom-call(f32[1,2,256,256]{3,2,1,0:T(8,128)S(1)} %copy-done.2, f32[1,2,256,256]{3,2,1,0:T(8,128)} %collective-permute-done.7.refs_1_, f32[4,2,256,256]{3,2,1,0:T(8,128)S(1)} %copy-done.4, f32[40,128]{1,0:T(8,128)S(1)} %add.107.sums.refs_3_), custom_call_target="tpu_custom_call" | custom-call | flops 1207959552 | bytes 5263360 | tf_op jit(solution)/shard_map/pallas_call | solution.py:67
  58.6 2.9 %collective-permute-done.8.carried = f32[2,256,256]{2,1,0:T(8,128)} collective-permute-done((f32[2,256,256]{2,1,0:T(8,128)}, f32[2,256,256]{2,1,0:T(8,128)}, u32[]{:S(2)}, u32[]{:S(2)}) %collective-permute-start.8) | collective-permute-done | bytes 524320 | tf_op jit(solution)/shard_map/ppermute | solution.py:470
  61.5 2.3 %shard_map.117 = (f32[2,256,256]{2,1,0:T(8,128)S(1)}, f32[2,256,256]{2,1,0:T(8,128)S(1)}) custom-call(s32[1]{0:T(128)} %bitcast.odd, f32[2,256,256]{2,1,0:T(8,128)S(1)} %copy-done.8, f32[2,256,256]{2,1,0:T(8,128)} %get-tuple-element.80.whole_source, f32[2,256,256]{2,1,0:T(8,128)} %collective-permute-done.8.carried, f32[2,256,256]{2,1,0:T(8,128)} %shard_map.115.before), custom_call_target="tpu_custom_call" | custom-call | flops 603979776 | bytes 3145732 | tf_op jit(solution)/shard_map/pallas_call | solution.py:67
  63.9 4.1 %collective-permute-start.16 = (f32[2,256,256]{2,1,0:T(8,128)S(1)}, f32[2,256,256]{2,1,0:T(8,128)S(1)}, u32[]{:S(2)}, u32[]{:S(2)}) collective-permute-start(f32[2,256,256]{2,1,0:T(8,128)S(1)} %get-tuple-element.111), channel_id=1, source_target_pairs={{8,17},{9,18},{10,19},{12,21},{13,22},{14,23},{16,9},{17,10},{18,1... | collective-permute-start | bytes 1572872 | tf_op jit(solution)/shard_map/ppermute | solution.py:512
  68.0 2.7 %shard_map.119 = (f32[2,2,256,256]{3,2,1,0:T(8,128)S(1)}, f32[2,2,256,256]{3,2,1,0:T(8,128)S(1)}) custom-call(f32[1,2,256,256]{3,2,1,0:T(8,128)} %collective-permute-done.10.refs_0_, f32[1,2,256,256]{3,2,1,0:T(8,128)} %collective-permute-done.11.refs_1_, f32[4,2,256,256]{3,2,1,0:T(8,128)S(1)} %copy-done.5, f32[40,128]{1,0:T(8,128)S(1)} %add.107.sums.refs_3_), custom_call_target="tpu_custom_call" | custom-call | flops 1207959552 | bytes 5263360 | tf_op jit(solution)/shard_map/pallas_call | solution.py:67
  70.8 2.6 %shard_map.118 = (f32[2,2,256,256]{3,2,1,0:T(8,128)S(1)}, f32[2,2,256,256]{3,2,1,0:T(8,128)S(1)}) custom-call(f32[1,2,256,256]{3,2,1,0:T(8,128)} %collective-permute-done.9.refs_0_, f32[1,2,256,256]{3,2,1,0:T(8,128)S(1)} %collective-permute-done.13.refs_1_, f32[4,2,256,256]{3,2,1,0:T(8,128)S(1)} %copy-done.5, f32[40,128]{1,0:T(8,128)S(1)} %add.107.sums.refs_3_), custom_call_target="tpu_custom_call" | custom-call | flops 1207959552 | bytes 5263360 | tf_op jit(solution)/shard_map/pallas_call | solution.py:67
  74.0 1.3 %collective-permute-start.15 = (f32[2,256,256]{2,1,0:T(8,128)S(1)}, f32[2,256,256]{2,1,0:T(8,128)S(1)}, u32[]{:S(2)}, u32[]{:S(2)}) collective-permute-start(f32[2,256,256]{2,1,0:T(8,128)S(1)} %broadcast_select_fusion.1.carried), channel_id=1, source_target_pairs={{0,8},{4,12},{8,0},{12,4},{16,24},{20,28},{24,16},{28,20},{1,9},{5... | collective-permute-start | bytes 1572872 | tf_op jit(solution)/shard_map/ppermute | solution.py:523
  75.3 7.5 %shard_map.120 = (f32[4,2,256,256]{3,2,1,0:T(8,128)S(1)}, f32[2,256,256]{2,1,0:T(8,128)}) custom-call(f32[4,2,256,256]{3,2,1,0:T(8,128)S(1)} %bitcast.44, f32[4,2,256,256]{3,2,1,0:T(8,128)S(1)} %copy-done.5, f32[40,128]{1,0:T(8,128)S(1)} %add.107.sums.refs_3_, f32[2,256,256]{2,1,0:T(8,128)S(1)} %broadcast_select_fusion.1.carried), custom_call_target="tpu_custom_call" | custom-call | flops 4831838208 | bytes 7360512 | tf_op jit(solution)/shard_map/pallas_call | solution.py:67
  82.8 3.2 %collective-permute-done.16.carried = f32[2,256,256]{2,1,0:T(8,128)S(1)} collective-permute-done((f32[2,256,256]{2,1,0:T(8,128)S(1)}, f32[2,256,256]{2,1,0:T(8,128)S(1)}, u32[]{:S(2)}, u32[]{:S(2)}) %collective-permute-start.16) | collective-permute-done | bytes 524320 | tf_op jit(solution)/shard_map/ppermute | solution.py:512
  86.0 5.3 %collective-permute-done.17.refs_1_ = f32[1,2,256,256]{3,2,1,0:T(8,128)S(1)} collective-permute-done((f32[1,2,256,256]{3,2,1,0:T(8,128)}, f32[1,2,256,256]{3,2,1,0:T(8,128)S(1)}, u32[]{:S(2)}, u32[]{:S(2)}) %collective-permute-start.17) | collective-permute-done | bytes 524320 | tf_op jit(solution)/shard_map/ppermute | solution.py:516
  91.5 10.1 %collective-permute-start.18 = (f32[64,128]{1,0:T(8,128)S(1)}, f32[64,128]{1,0:T(8,128)S(1)}, u32[]{:S(2)}, u32[]{:S(2)}) collective-permute-start(f32[64,128]{1,0:T(8,128)S(1)} %copy-done.15), channel_id=1, source_target_pairs={{4,8},{12,16},{20,24},{8,4},{16,12},{24,20},{5,9},{13,17},{21,25},... | collective-permute-start | bytes 98312 | tf_op jit(solution)/shard_map/ppermute | solution.py:542
  101.6 1.6 %shard_map.122 = (f32[2,2,256,256]{3,2,1,0:T(8,128)S(1)}, f32[2,2,256,256]{3,2,1,0:T(8,128)S(1)}) custom-call(f32[1,2,256,256]{3,2,1,0:T(8,128)S(1)} %collective-permute-done.14.refs_0_, f32[1,2,256,256]{3,2,1,0:T(8,128)S(1)} %collective-permute-done.17.refs_1_, f32[4,2,256,256]{3,2,1,0:T(8,128)S(1)} %copy-done.5, f32[40,128]{1,0:T(8,128)S(1)} %add.107.sums.refs_3_), custom_call_target="tpu_custom_call" | custom-call | flops 1207959552 | bytes 5263360 | tf_op jit(solution)/shard_map/pallas_call | solution.py:67
  103.2 1.9 %shard_map.121 = (f32[2,2,256,256]{3,2,1,0:T(8,128)S(1)}, f32[2,256,256]{2,1,0:T(8,128)S(1)}) custom-call(f32[2,2,256,256]{3,2,1,0:T(8,128)S(1)} %get-tuple-element.109.link, f32[2,2,256,256]{3,2,1,0:T(8,128)S(1)} %get-tuple-element.110.source, f32[2,256,256]{2,1,0:T(8,128)S(1)} %collective-permute-done.16.carried), custom_call_target="tpu_custom_call" | custom-call | flops 1207959552 | bytes 4194304 | tf_op jit(solution)/shard_map/pallas_call | solution.py:67
  105.1 2.7 %shard_map.123 = (f32[2,2,256,256]{3,2,1,0:T(8,128)S(1)}, f32[2,256,256]{2,1,0:T(8,128)}) custom-call(f32[2,2,256,256]{3,2,1,0:T(8,128)S(1)} %get-tuple-element.118.link, f32[2,2,256,256]{3,2,1,0:T(8,128)S(1)} %get-tuple-element.119.source, f32[2,256,256]{2,1,0:T(8,128)S(1)} %get-tuple-element.120.carried), custom_call_target="tpu_custom_call" | custom-call | flops 1207959552 | bytes 4194304 | tf_op jit(solution)/shard_map/pallas_call | solution.py:67
  108.6 2.7 %shard_map.124 = (f32[2,2,256,256]{3,2,1,0:T(8,128)S(1)}, f32[2,2,256,256]{3,2,1,0:T(8,128)S(1)}, f32[2,256,256]{2,1,0:T(8,128)S(1)}) custom-call(s32[2]{0:T(128)S(1)} %pad_add_fusion.pick, f32[2,2,256,256]{3,2,1,0:T(8,128)S(1)} %get-tuple-element.126.link, f32[2,2,256,256]{3,2,1,0:T(8,128)S(1)} %get-tuple-element.127.source, ...), custom_call_target="tpu_custom_call" | custom-call | flops 1207959552 | bytes 9437192 | tf_op jit(solution)/shard_map/pallas_call | solution.py:67
  111.4 3.5 %shard_map.125 = (f32[2,2,256,256]{3,2,1,0:T(8,128)S(1)}, f32[2,2,256,256]{3,2,1,0:T(8,128)S(1)}, f32[2,256,256]{2,1,0:T(8,128)}) custom-call(s32[2]{0:T(128)S(1)} %pad_add_fusion.pick, f32[2,2,256,256]{3,2,1,0:T(8,128)S(1)} %get-tuple-element.134.link, f32[2,2,256,256]{3,2,1,0:T(8,128)S(1)} %get-tuple-element.135.source, ...), custom_call_target="tpu_custom_call" | custom-call | flops 1207959552 | bytes 9437192 | tf_op jit(solution)/shard_map/pallas_call | solution.py:67
  115.7 2.3 %collective-permute-done.20 = f32[2,2,256,256]{3,2,1,0:T(8,128)S(1)} collective-permute-done((f32[2,2,256,256]{3,2,1,0:T(8,128)S(1)}, f32[2,2,256,256]{3,2,1,0:T(8,128)S(1)}, u32[]{:S(2)}, u32[]{:S(2)}) %collective-permute-start.20) | collective-permute-done | bytes 1048608 | tf_op jit(solution)/shard_map/ppermute | solution.py:586
  118.1 1.5 %maximum_bitcast_fusion = f32[1,4,2,256,256]{4,3,2,1,0:T(8,128)} fusion(f32[2,2,256,256]{3,2,1,0:T(8,128)S(1)} %add.131, f32[2,2,256,256]{3,2,1,0:T(8,128)S(1)} %add.130), kind=kLoop, calls=%fused_computation.1 | loop fusion | flops 524288 | bytes 4194304 | tf_op jit(solution)/shard_map/broadcast_in_dim | solution.py:587
  (86 shorter events, 17.6 us)
Async XLA Ops:
  0.6 24.7 %copy-start = (f32[1,4,2,256,256]{4,3,2,1,0:T(8,128)S(1)}, f32[1,4,2,256,256]{4,3,2,1,0:T(8,128)}, u32[]{:S(2)}) copy-start(f32[1,4,2,256,256]{4,3,2,1,0:T(8,128)} %param.14) | copy-start | bytes 6291460
  1.9 12.9 %collective-permute-start.2 = (f32[1,2,256,256]{3,2,1,0:T(8,128)S(1)}, f32[1,2,256,256]{3,2,1,0:T(8,128)S(1)}, u32[]{:S(2)}, u32[]{:S(2)}) collective-permute-start(f32[1,2,256,256]{3,2,1,0:T(8,128)S(1)} %slice_bitcast_fusion), channel_id=1, source_target_pairs={{0,8},{4,12},{8,0},{12,4},{16,24},{20,28},{24,16},{28,20},{1,9},{5... | collective-permute-start | bytes 1572872 | tf_op jit(solution)/shard_map/ppermute | solution.py:347
  4.0 4.6 %collective-permute-start.1 = (f32[2,1,4,128]{3,2,0,1:T(4,128)S(1)}, f32[2,1,4,128]{3,2,0,1:T(4,128)S(1)}, u32[]{:S(2)}, u32[]{:S(2)}) collective-permute-start(f32[2,1,4,128]{3,2,0,1:T(4,128)S(1)} %get-tuple-element.144), channel_id=1, source_target_pairs={{0,1},{2,3},{1,0},{3,2},{4,5},{6,7},{5,4},{7,6},{8,9},{10,11},{9,8... | collective-permute-start | bytes 12296 | tf_op jit(solution)/shard_map/ppermute | solution.py:361
  4.2 5.6 %collective-permute-start = (f32[2,1,4,128]{3,2,0,1:T(4,128)S(1)}, f32[2,1,4,128]{3,2,0,1:T(4,128)S(1)}, u32[]{:S(2)}, u32[]{:S(2)}) collective-permute-start(f32[2,1,4,128]{3,2,0,1:T(4,128)S(1)} %get-tuple-element.145), channel_id=1, source_target_pairs={{1,2},{2,1},{5,6},{6,5},{9,10},{10,9},{13,14},{14,13},{17,18},{18,... | collective-permute-start | bytes 12296 | tf_op jit(solution)/shard_map/ppermute | solution.py:362
  14.7 18.7 %copy-start.1 = (f32[1,2,256,256]{3,2,1,0:T(8,128)}, f32[1,2,256,256]{3,2,1,0:T(8,128)S(1)}, u32[]{:S(2)}) copy-start(f32[1,2,256,256]{3,2,1,0:T(8,128)S(1)} %collective-permute-done.2.refs_0_) | copy-start | bytes 1572868
  14.7 2.8 %collective-permute-start.3 = (f32[40,128]{1,0:T(8,128)}, f32[40,128]{1,0:T(8,128)S(1)}, u32[]{:S(2)}, u32[]{:S(2)}) collective-permute-start(f32[40,128]{1,0:T(8,128)} %get-tuple-element.74), channel_id=1, source_target_pairs={{0,8},{4,12},{8,0},{12,4},{16,24},{20,28},{24,16},{28,20},{1,9},{5... | collective-permute-start | bytes 61448 | tf_op jit(solution)/shard_map/ppermute | solution.py:302
  19.1 3.6 %collective-permute-start.4 = (f32[104,128]{1,0:T(8,128)S(1)}, f32[104,128]{1,0:T(8,128)S(1)}, u32[]{:S(2)}, u32[]{:S(2)}) collective-permute-start(f32[104,128]{1,0:T(8,128)S(1)} %pad_maximum_fusion.1), channel_id=1, source_target_pairs={{0,4},{4,0},{8,12},{12,8},{16,20},{20,16},{24,28},{28,24},{1,5},{5... | collective-permute-start | bytes 159752 | tf_op jit(solution)/shard_map/ppermute | solution.py:302
  22.7 2.6 %collective-permute-start.5 = (f32[40,128]{1,0:T(8,128)S(1)}, f32[40,128]{1,0:T(8,128)S(1)}, u32[]{:S(2)}, u32[]{:S(2)}) collective-permute-start(f32[40,128]{1,0:T(8,128)S(1)} %slice_add_fusion), channel_id=1, source_target_pairs={{0,16},{4,20},{8,24},{12,28},{16,0},{20,4},{24,8},{28,12},{1,17},{... | collective-permute-start | bytes 61448 | tf_op jit(solution)/shard_map/ppermute | solution.py:302
  23.0 13.2 %collective-permute-start.7 = (f32[1,2,256,256]{3,2,1,0:T(8,128)}, f32[1,2,256,256]{3,2,1,0:T(8,128)}, u32[]{:S(2)}, u32[]{:S(2)}) collective-permute-start(f32[1,2,256,256]{3,2,1,0:T(8,128)} %get-tuple-element.83), channel_id=1, source_target_pairs={{0,8},{4,12},{8,0},{12,4},{16,24},{20,28},{24,16},{28,20},{1,9},{5... | collective-permute-start | bytes 1572872 | tf_op jit(solution)/shard_map/ppermute | solution.py:396
  26.9 6.4 %copy-start.16 = (f32[4]{0:T(128)S(1)}, f32[4]{0:T(128)}, u32[]{:S(2)}) copy-start(f32[4]{0:T(128)} %param.17) | copy-start | bytes 52
  26.9 6.4 %copy-start.17 = (s32[4]{0:T(128)S(1)}, s32[4]{0:T(128)}, u32[]{:S(2)}) copy-start(s32[4]{0:T(128)} %param.16) | copy-start | bytes 52
  26.9 6.4 %copy-start.18 = (s32[4]{0:T(128)S(1)}, s32[4]{0:T(128)}, u32[]{:S(2)}) copy-start(s32[4]{0:T(128)} %constant.57.clone) | copy-start | bytes 52
  33.1 12.3 %collective-permute-start.6 = (f32[2,256,256]{2,1,0:T(8,128)}, f32[2,256,256]{2,1,0:T(8,128)}, u32[]{:S(2)}, u32[]{:S(2)}) collective-permute-start(f32[2,256,256]{2,1,0:T(8,128)} %get-tuple-element.80.whole_source), channel_id=1, source_target_pairs={{0,1},{2,3},{1,0},{3,2},{4,5},{6,7},{5,4},{7,6},{8,9},{10,11},{9,8... | collective-permute-start | bytes 1572872 | tf_op jit(solution)/shard_map/ppermute | solution.py:470
  35.4 23.1 %collective-permute-start.10 = (f32[1,2,256,256]{3,2,1,0:T(8,128)}, f32[1,2,256,256]{3,2,1,0:T(8,128)}, u32[]{:S(2)}, u32[]{:S(2)}) collective-permute-start(f32[1,2,256,256]{3,2,1,0:T(8,128)} %broadcast_select_fusion), channel_id=1, source_target_pairs={{0,16},{4,20},{8,24},{12,28},{16,0},{20,4},{24,8},{28,12},{1,17},{... | collective-permute-start | bytes 1572872 | tf_op jit(solution)/shard_map/ppermute | solution.py:475
  36.1 15.7 %collective-permute-start.9 = (f32[1,2,256,256]{3,2,1,0:T(8,128)}, f32[1,2,256,256]{3,2,1,0:T(8,128)}, u32[]{:S(2)}, u32[]{:S(2)}) collective-permute-start(f32[1,2,256,256]{3,2,1,0:T(8,128)} %get-tuple-element.89), channel_id=1, source_target_pairs={{0,8},{4,12},{8,0},{12,4},{16,24},{20,28},{24,16},{28,20},{1,9},{5... | collective-permute-start | bytes 1572872 | tf_op jit(solution)/shard_map/ppermute | solution.py:405
  37.3 8.0 %copy-start.7 = (f32[2,256,256]{2,1,0:T(8,128)S(1)}, f32[2,256,256]{2,1,0:T(8,128)}, u32[]{:S(2)}) copy-start(f32[2,256,256]{2,1,0:T(8,128)} %copy-done.6) | copy-start | bytes 1572868
  37.7 20.8 %collective-permute-start.11 = (f32[1,2,256,256]{3,2,1,0:T(8,128)}, f32[1,2,256,256]{3,2,1,0:T(8,128)}, u32[]{:S(2)}, u32[]{:S(2)}) collective-permute-start(f32[1,2,256,256]{3,2,1,0:T(8,128)} %collective-permute-done.7.refs_1_), channel_id=1, source_target_pairs={{0,16},{4,20},{8,24},{12,28},{16,0},{20,4},{24,8},{28,12},{1,17},{... | collective-permute-start | bytes 1572872 | tf_op jit(solution)/shard_map/ppermute | solution.py:401
  48.3 13.2 %collective-permute-start.8 = (f32[2,256,256]{2,1,0:T(8,128)}, f32[2,256,256]{2,1,0:T(8,128)}, u32[]{:S(2)}, u32[]{:S(2)}) collective-permute-start(f32[2,256,256]{2,1,0:T(8,128)} %shard_map.115.before), channel_id=1, source_target_pairs={{1,2},{2,1},{5,6},{6,5},{9,10},{10,9},{13,14},{14,13},{17,18},{18,... | collective-permute-start | bytes 1572872 | tf_op jit(solution)/shard_map/ppermute | solution.py:470
  51.8 18.9 %collective-permute-start.13 = (f32[1,2,256,256]{3,2,1,0:T(8,128)}, f32[1,2,256,256]{3,2,1,0:T(8,128)S(1)}, u32[]{:S(2)}, u32[]{:S(2)}) collective-permute-start(f32[1,2,256,256]{3,2,1,0:T(8,128)} %get-tuple-element.100), channel_id=1, source_target_pairs={{0,8},{4,12},{8,0},{12,4},{16,24},{20,28},{24,16},{28,20},{1,9},{5... | collective-permute-start | bytes 1572872 | tf_op jit(solution)/shard_map/ppermute | solution.py:405
  55.6 5.9 %copy-start.8 = (f32[2,256,256]{2,1,0:T(8,128)S(1)}, f32[2,256,256]{2,1,0:T(8,128)}, u32[]{:S(2)}) copy-start(f32[2,256,256]{2,1,0:T(8,128)} %copy-done.6) | copy-start | bytes 1572868
  58.2 9.8 %copy-start.5 = (f32[4,2,256,256]{3,2,1,0:T(8,128)S(1)}, f32[4,2,256,256]{3,2,1,0:T(8,128)}, u32[]{:S(2)}) copy-start(f32[4,2,256,256]{3,2,1,0:T(8,128)} %refs_2_.7) | copy-start | bytes 6291460
  58.2 15.2 %collective-permute-start.14 = (f32[1,2,256,256]{3,2,1,0:T(8,128)}, f32[1,2,256,256]{3,2,1,0:T(8,128)S(1)}, u32[]{:S(2)}, u32[]{:S(2)}) collective-permute-start(f32[1,2,256,256]{3,2,1,0:T(8,128)} %collective-permute-done.9.refs_0_), channel_id=1, source_target_pairs={{0,16},{4,20},{8,24},{12,28},{16,0},{20,4},{24,8},{28,12},{1,17},{... | collective-permute-start | bytes 1572872 | tf_op jit(solution)/shard_map/ppermute | solution.py:401
  63.7 10.1 %collective-permute-start.12 = (f32[2,256,256]{2,1,0:T(8,128)S(1)}, f32[2,256,256]{2,1,0:T(8,128)S(1)}, u32[]{:S(2)}, u32[]{:S(2)}) collective-permute-start(f32[2,256,256]{2,1,0:T(8,128)S(1)} %get-tuple-element.98), channel_id=1, source_target_pairs={{0,1},{2,3},{1,0},{3,2},{4,5},{6,7},{5,4},{7,6},{8,9},{10,11},{9,8... | collective-permute-start | bytes 1572872 | tf_op jit(solution)/shard_map/ppermute | solution.py:511
  63.9 22.1 %collective-permute-start.16 = (f32[2,256,256]{2,1,0:T(8,128)S(1)}, f32[2,256,256]{2,1,0:T(8,128)S(1)}, u32[]{:S(2)}, u32[]{:S(2)}) collective-permute-start(f32[2,256,256]{2,1,0:T(8,128)S(1)} %get-tuple-element.111), channel_id=1, source_target_pairs={{8,17},{9,18},{10,19},{12,21},{13,22},{14,23},{16,9},{17,10},{18,1... | collective-permute-start | bytes 1572872 | tf_op jit(solution)/shard_map/ppermute | solution.py:512
  70.7 20.6 %collective-permute-start.17 = (f32[1,2,256,256]{3,2,1,0:T(8,128)}, f32[1,2,256,256]{3,2,1,0:T(8,128)S(1)}, u32[]{:S(2)}, u32[]{:S(2)}) collective-permute-start(f32[1,2,256,256]{3,2,1,0:T(8,128)} %collective-permute-done.10.refs_0_), channel_id=1, source_target_pairs={{0,8},{4,12},{8,0},{12,4},{16,24},{20,28},{24,16},{28,20},{1,9},{5... | collective-permute-start | bytes 1572872 | tf_op jit(solution)/shard_map/ppermute | solution.py:516
  74.0 17.3 %copy-start.9 = (f32[16,4,128]{2,1,0:T(4,128)S(1)}, f32[16,4,128]{2,1,0:T(4,128)}, u32[]{:S(2)}) copy-start(f32[16,4,128]{2,1,0:T(4,128)} %param.12) | copy-start | bytes 98308
  74.0 17.3 %copy-start.10 = (f32[16,4,128]{2,1,0:T(4,128)S(1)}, f32[16,4,128]{2,1,0:T(4,128)}, u32[]{:S(2)}) copy-start(f32[16,4,128]{2,1,0:T(4,128)} %param.10) | copy-start | bytes 98308
  74.0 17.5 %copy-start.15 = (f32[64,128]{1,0:T(8,128)S(1)}, f32[64,128]{1,0:T(8,128)}, u32[]{:S(2)}) copy-start(f32[64,128]{1,0:T(8,128)} %get-tuple-element.124) | copy-start | bytes 98308
  74.0 34.6 %collective-permute-start.15 = (f32[2,256,256]{2,1,0:T(8,128)S(1)}, f32[2,256,256]{2,1,0:T(8,128)S(1)}, u32[]{:S(2)}, u32[]{:S(2)}) collective-permute-start(f32[2,256,256]{2,1,0:T(8,128)S(1)} %broadcast_select_fusion.1.carried), channel_id=1, source_target_pairs={{0,8},{4,12},{8,0},{12,4},{16,24},{20,28},{24,16},{28,20},{1,9},{5... | collective-permute-start | bytes 1572872 | tf_op jit(solution)/shard_map/ppermute | solution.py:523
  91.5 16.3 %collective-permute-start.18 = (f32[64,128]{1,0:T(8,128)S(1)}, f32[64,128]{1,0:T(8,128)S(1)}, u32[]{:S(2)}, u32[]{:S(2)}) collective-permute-start(f32[64,128]{1,0:T(8,128)S(1)} %copy-done.15), channel_id=1, source_target_pairs={{4,8},{12,16},{20,24},{8,4},{16,12},{24,20},{5,9},{13,17},{21,25},... | collective-permute-start | bytes 98312 | tf_op jit(solution)/shard_map/ppermute | solution.py:542
  111.3 3.6 %collective-permute-start.19 = (f32[2,2,256,256]{3,2,1,0:T(8,128)S(1)}, f32[2,2,256,256]{3,2,1,0:T(8,128)S(1)}, u32[]{:S(2)}, u32[]{:S(2)}) collective-permute-start(f32[2,2,256,256]{3,2,1,0:T(8,128)S(1)} %get-tuple-element.133), channel_id=1, source_target_pairs={{0,4},{4,0},{8,12},{12,8},{16,20},{20,16},{24,28},{28,24},{1,5},{5... | collective-permute-start | bytes 3145736 | tf_op jit(solution)/shard_map/ppermute | solution.py:586
  115.1 2.8 %collective-permute-start.20 = (f32[2,2,256,256]{3,2,1,0:T(8,128)S(1)}, f32[2,2,256,256]{3,2,1,0:T(8,128)S(1)}, u32[]{:S(2)}, u32[]{:S(2)}) collective-permute-start(f32[2,2,256,256]{3,2,1,0:T(8,128)S(1)} %get-tuple-element.141), channel_id=1, source_target_pairs={{0,4},{4,0},{8,12},{12,8},{16,20},{20,16},{24,28},{28,24},{1,5},{5... | collective-permute-start | bytes 3145736 | tf_op jit(solution)/shard_map/ppermute | solution.py:586
  (8 other events, 25.4 us)

commit v13 on v9

--- a/solution.py
+++ b/solution.py
@@ -525,12 +525,15 @@
         in_specs=[block, block, pl.BlockSpec(sums.shape, lambda s: (0, 0)), one_state],
         out_specs=(block, one_state),
     )
-    carried_second, greens, free_second[3], ends, field, perm = lax.optimization_barrier(
-        (carried_second, greens, free_second[3], ends, potential_old, permittivity)
+    greens, ends, field, perm = lax.optimization_barrier(
+        (greens, ends, potential_old, permittivity)
     )
 
     beyond = [(e, e + 1) for e in range(1, energies - 1, 2)]
     other_ends = lax.ppermute(ends, "energy", beyond + [(b, a) for a, b in beyond])
+    carried_second, other_ends, free_second[3] = lax.optimization_barrier(
+        (carried_second, other_ends, free_second[3])
+    )
     ends_before = jnp.where(odd == 1, twin_ends, other_ends).reshape(2, 2, cells, 1, depth)
     ends_after = jnp.where(odd == 1, other_ends, twin_ends).reshape(2, 2, cells, 1, depth)
     edge = jnp.zeros((2, cells, rows, 1), jnp.float32)

time: 117 us -> 118 us (level)
  the two profiles are of different devices: /device:TPU:13 before, /device:TPU:21 now
where the time goes in v13:
time: 118 us
  Pallas kernels  41.6 us (35%)
  waiting for transfers between devices  31.9 us (27%)
  starting transfers between devices  31.4 us (27%)
  other arithmetic  7.15 us (6%)
  local copies, waits for them, and re-layouts  4.62 us (4%)
    pallas_call x13, Pallas kernels, call(): pl.pallas_call(kernel, out_shape=out_shapes, cost_estimate=cost, compiler...  41.6 us
    ppermute x4, waiting for transfers between devices, sent_on(): free_second.append(lax.ppermute(given, 'energy', relay_pairs))  10.9 us
    ppermute x2, waiting for transfers between devices, per_device(): arrived = lax.ppermute(leaving, 'slab', swaps((hop - 1) % 2))  8.63 us
    ppermute x1, starting transfers between devices, per_device(): lax.ppermute(ends, 'energy', beyond + [(b, a) for a, b in beyond])  8.26 us
    ppermute x1, starting transfers between devices, per_device(): lax.ppermute(onward, ('energy', 'slab'), both(second_pairs))  4.2 us
    ppermute x3, starting transfers between devices, exchanged(): lax.ppermute(given, 'energy', [(e, e ^ mask) for e in range(peers)])  4.15 us
    ppermute x3, waiting for transfers between devices, exchanged(): lax.ppermute(given, 'energy', [(e, e ^ mask) for e in range(peers)])  3.73 us
    ppermute x2, starting transfers between devices, per_device(): arrived = lax.ppermute(leaving, 'slab', swaps((hop - 1) % 2))  3.58 us
  transfers between devices with their start and end apart: 21, of which 12 were waited for; matrix products, arithmetic and copies ran while one was open for 3% of the time, Pallas kernels for 33%

profile of v13, /device:TPU:21, one launch (start us, length us, event | category | flops | bytes accessed | tf_op | source)
XLA Modules:
  0.0 117.7 jit_solution(9356990855907877468)
XLA Ops:
  4.0 1.4 %collective-permute-start.1 = (f32[2,1,4,128]{3,2,0,1:T(4,128)S(1)}, f32[2,1,4,128]{3,2,0,1:T(4,128)S(1)}, u32[]{:S(2)}, u32[]{:S(2)}) collective-permute-start(f32[2,1,4,128]{3,2,0,1:T(4,128)S(1)} %get-tuple-element.136), channel_id=1, source_target_pairs={{0,1},{2,3},{1,0},{3,2},{4,5},{6,7},{5,4},{7,6},{8,9},{10,11},{9,8... | collective-permute-start | bytes 12296 | tf_op jit(solution)/shard_map/ppermute | solution.py:361
  5.3 1.9 %collective-permute-start = (f32[2,1,4,128]{3,2,0,1:T(4,128)S(1)}, f32[2,1,4,128]{3,2,0,1:T(4,128)S(1)}, u32[]{:S(2)}, u32[]{:S(2)}) collective-permute-start(f32[2,1,4,128]{3,2,0,1:T(4,128)S(1)} %get-tuple-element.137), channel_id=1, source_target_pairs={{1,2},{2,1},{5,6},{6,5},{9,10},{10,9},{13,14},{14,13},{17,18},{18,... | collective-permute-start | bytes 12296 | tf_op jit(solution)/shard_map/ppermute | solution.py:362
  7.3 2.8 %collective-permute-done = f32[2,1,4,128]{3,2,0,1:T(4,128)S(1)} collective-permute-done((f32[2,1,4,128]{3,2,0,1:T(4,128)S(1)}, f32[2,1,4,128]{3,2,0,1:T(4,128)S(1)}, u32[]{:S(2)}, u32[]{:S(2)}) %collective-permute-start) | collective-permute-done | bytes 4128 | tf_op jit(solution)/shard_map/ppermute | solution.py:362
  10.7 3.7 %shard_map.113 = (f32[40,128]{1,0:T(8,128)}, f32[64,128]{1,0:T(8,128)}, f32[1,2,256,256]{3,2,1,0:T(8,128)}, f32[1,2,256,256]{3,2,1,0:T(8,128)}, f32[1,2,256,256]{3,2,1,0:T(8,128)}) custom-call(s32[1]{0:T(128)} %bitcast.2.mine, f32[64,128]{1,0:T(8,128)} %bitcast.48, f32[64,128]{1,0:T(8,128)} %bitcast.46, f32[64,128]{1,0:T(8,128)} %bitcast.49, ...), custom_call_target="tpu_custom_call" | custom-call | flops 301989888 | bytes 3833860 | tf_op jit(solution)/shard_map/pallas_call | solution.py:67
  16.0 1.6 %collective-permute-done.3 = f32[40,128]{1,0:T(8,128)S(1)} collective-permute-done((f32[40,128]{1,0:T(8,128)}, f32[40,128]{1,0:T(8,128)S(1)}, u32[]{:S(2)}, u32[]{:S(2)}) %collective-permute-start.3) | collective-permute-done | bytes 20512 | tf_op jit(solution)/shard_map/ppermute | solution.py:302
  19.2 2.7 %collective-permute-start.4 = (f32[104,128]{1,0:T(8,128)S(1)}, f32[104,128]{1,0:T(8,128)S(1)}, u32[]{:S(2)}, u32[]{:S(2)}) collective-permute-start(f32[104,128]{1,0:T(8,128)S(1)} %pad_maximum_fusion.1), channel_id=1, source_target_pairs={{0,4},{4,0},{8,12},{12,8},{16,20},{20,16},{24,28},{28,24},{1,5},{5... | collective-permute-start | bytes 159752 | tf_op jit(solution)/shard_map/ppermute | solution.py:302
  25.4 1.6 %copy-done.1 = f32[4,2,256,256]{3,2,1,0:T(8,128)S(1)} copy-done((f32[4,2,256,256]{3,2,1,0:T(8,128)S(1)}, f32[4,2,256,256]{3,2,1,0:T(8,128)}, u32[]{:S(2)}) %copy-start.1) | copy-done | bytes 2097176
  27.0 6.2 %shard_map.114 = (f32[2,256,256]{2,1,0:T(8,128)S(1)}, f32[2,256,256]{2,1,0:T(8,128)S(1)}) custom-call(f32[4,2,256,256]{3,2,1,0:T(8,128)S(1)} %bitcast.43, f32[4,2,256,256]{3,2,1,0:T(8,128)S(1)} %copy-done.1, f32[40,128]{1,0:T(8,128)S(1)} %add.107.sums.refs_3_), custom_call_target="tpu_custom_call" | custom-call | flops 5133828096 | bytes 5263360 | tf_op jit(solution)/shard_map/pallas_call | solution.py:67
  33.2 1.3 %collective-permute-start.6 = (f32[2,256,256]{2,1,0:T(8,128)S(1)}, f32[2,256,256]{2,1,0:T(8,128)S(1)}, u32[]{:S(2)}, u32[]{:S(2)}) collective-permute-start(f32[2,256,256]{2,1,0:T(8,128)S(1)} %get-tuple-element.76.whole_source), channel_id=1, source_target_pairs={{0,1},{2,3},{1,0},{3,2},{4,5},{6,7},{5,4},{7,6},{8,9},{10,11},{9,8... | collective-permute-start | bytes 1572872 | tf_op jit(solution)/shard_map/ppermute | solution.py:471
  37.8 1.3 %collective-permute-start.11 = (f32[1,2,256,256]{3,2,1,0:T(8,128)}, f32[1,2,256,256]{3,2,1,0:T(8,128)}, u32[]{:S(2)}, u32[]{:S(2)}) collective-permute-start(f32[1,2,256,256]{3,2,1,0:T(8,128)} %collective-permute-done.7.refs_1_), channel_id=1, source_target_pairs={{0,16},{4,20},{8,24},{12,28},{16,0},{20,4},{24,8},{28,12},{1,17},{... | collective-permute-start | bytes 1572872 | tf_op jit(solution)/shard_map/ppermute | solution.py:401
  39.1 6.2 %collective-permute-done.6.carried = f32[2,256,256]{2,1,0:T(8,128)S(1)} collective-permute-done((f32[2,256,256]{2,1,0:T(8,128)S(1)}, f32[2,256,256]{2,1,0:T(8,128)S(1)}, u32[]{:S(2)}, u32[]{:S(2)}) %collective-permute-start.6) | collective-permute-done | bytes 524320 | tf_op jit(solution)/shard_map/ppermute | solution.py:471
  45.3 1.7 %shard_map.115.before = f32[2,256,256]{2,1,0:T(8,128)} custom-call(f32[2,256,256]{2,1,0:T(8,128)S(1)} %get-tuple-element.74.whole_map, f32[2,256,256]{2,1,0:T(8,128)S(1)} %get-tuple-element.76.whole_source, f32[2,256,256]{2,1,0:T(8,128)S(1)} %collective-permute-done.6.carried), custom_call_target="tpu_custom_call" | custom-call | flops 603979776 | bytes 2097152 | tf_op jit(solution)/shard_map/pallas_call | solution.py:67
  47.0 2.2 %collective-permute-start.8 = (f32[2,256,256]{2,1,0:T(8,128)}, f32[2,256,256]{2,1,0:T(8,128)}, u32[]{:S(2)}, u32[]{:S(2)}) collective-permute-start(f32[2,256,256]{2,1,0:T(8,128)} %shard_map.115.before), channel_id=1, source_target_pairs={{1,2},{2,1},{5,6},{6,5},{9,10},{10,9},{13,14},{14,13},{17,18},{18,... | collective-permute-start | bytes 1572872 | tf_op jit(solution)/shard_map/ppermute | solution.py:471
  50.5 1.6 %copy-done.2 = f32[4,2,256,256]{3,2,1,0:T(8,128)S(1)} copy-done((f32[4,2,256,256]{3,2,1,0:T(8,128)S(1)}, f32[4,2,256,256]{3,2,1,0:T(8,128)}, u32[]{:S(2)}) %copy-start.2) | copy-done | bytes 2097176
  52.1 2.8 %shard_map.116 = (f32[2,2,256,256]{3,2,1,0:T(8,128)S(1)}, f32[2,2,256,256]{3,2,1,0:T(8,128)S(1)}) custom-call(f32[1,2,256,256]{3,2,1,0:T(8,128)} %collective-permute-done.2.refs_0_, f32[1,2,256,256]{3,2,1,0:T(8,128)} %collective-permute-done.7.refs_1_, f32[4,2,256,256]{3,2,1,0:T(8,128)S(1)} %copy-done.2, f32[40,128]{1,0:T(8,128)S(1)} %add.107.sums.refs_3_), custom_call_target="tpu_custom_call" | custom-call | flops 1207959552 | bytes 5263360 | tf_op jit(solution)/shard_map/pallas_call | solution.py:67
  55.3 2.6 %collective-permute-done.11.refs_1_ = f32[1,2,256,256]{3,2,1,0:T(8,128)} collective-permute-done((f32[1,2,256,256]{3,2,1,0:T(8,128)}, f32[1,2,256,256]{3,2,1,0:T(8,128)}, u32[]{:S(2)}, u32[]{:S(2)}) %collective-permute-start.11) | collective-permute-done | bytes 524320 | tf_op jit(solution)/shard_map/ppermute | solution.py:401
  57.9 2.4 %collective-permute-done.8.carried = f32[2,256,256]{2,1,0:T(8,128)} collective-permute-done((f32[2,256,256]{2,1,0:T(8,128)}, f32[2,256,256]{2,1,0:T(8,128)}, u32[]{:S(2)}, u32[]{:S(2)}) %collective-permute-start.8) | collective-permute-done | bytes 524320 | tf_op jit(solution)/shard_map/ppermute | solution.py:471
  60.3 2.1 %shard_map.117 = (f32[2,256,256]{2,1,0:T(8,128)S(1)}, f32[2,256,256]{2,1,0:T(8,128)S(1)}) custom-call(s32[1]{0:T(128)} %bitcast.odd, f32[2,256,256]{2,1,0:T(8,128)S(1)} %copy-done.7, f32[2,256,256]{2,1,0:T(8,128)S(1)} %copy-done.5, f32[2,256,256]{2,1,0:T(8,128)} %collective-permute-done.8.carried, f32[2,256,256]{2,1,0:T(8,128)} %shard_map.115.before), custom_call_target="tpu_custom_call" | custom-call | flops 603979776 | bytes 3145732 | tf_op jit(solution)/shard_map/pallas_call | solution.py:67
  62.6 4.2 %collective-permute-start.16 = (f32[2,256,256]{2,1,0:T(8,128)S(1)}, f32[2,256,256]{2,1,0:T(8,128)S(1)}, u32[]{:S(2)}, u32[]{:S(2)}) collective-permute-start(f32[2,256,256]{2,1,0:T(8,128)S(1)} %get-tuple-element.103), channel_id=1, source_target_pairs={{8,17},{9,18},{10,19},{12,21},{13,22},{14,23},{16,9},{17,10},{18,1... | collective-permute-start | bytes 1572872 | tf_op jit(solution)/shard_map/ppermute | solution.py:506
  66.8 2.7 %shard_map.119 = (f32[2,2,256,256]{3,2,1,0:T(8,128)S(1)}, f32[2,2,256,256]{3,2,1,0:T(8,128)S(1)}) custom-call(f32[1,2,256,256]{3,2,1,0:T(8,128)} %collective-permute-done.10.refs_0_, f32[1,2,256,256]{3,2,1,0:T(8,128)} %collective-permute-done.11.refs_1_, f32[4,2,256,256]{3,2,1,0:T(8,128)S(1)} %copy-done.3, f32[40,128]{1,0:T(8,128)S(1)} %add.107.sums.refs_3_), custom_call_target="tpu_custom_call" | custom-call | flops 1207959552 | bytes 5263360 | tf_op jit(solution)/shard_map/pallas_call | solution.py:67
  69.6 2.5 %shard_map.118 = (f32[2,2,256,256]{3,2,1,0:T(8,128)S(1)}, f32[2,2,256,256]{3,2,1,0:T(8,128)S(1)}) custom-call(f32[1,2,256,256]{3,2,1,0:T(8,128)} %collective-permute-done.9.refs_0_, f32[1,2,256,256]{3,2,1,0:T(8,128)S(1)} %collective-permute-done.13.refs_1_, f32[4,2,256,256]{3,2,1,0:T(8,128)S(1)} %copy-done.3, f32[40,128]{1,0:T(8,128)S(1)} %add.107.sums.refs_3_), custom_call_target="tpu_custom_call" | custom-call | flops 1207959552 | bytes 5263360 | tf_op jit(solution)/shard_map/pallas_call | solution.py:67
  72.2 8.3 %collective-permute-done.14.refs_0_ = f32[1,2,256,256]{3,2,1,0:T(8,128)S(1)} collective-permute-done((f32[1,2,256,256]{3,2,1,0:T(8,128)}, f32[1,2,256,256]{3,2,1,0:T(8,128)S(1)}, u32[]{:S(2)}, u32[]{:S(2)}) %collective-permute-start.14) | collective-permute-done | bytes 524320 | tf_op jit(solution)/shard_map/ppermute | solution.py:401
  81.7 7.5 %shard_map.120 = (f32[4,2,256,256]{3,2,1,0:T(8,128)S(1)}, f32[2,256,256]{2,1,0:T(8,128)}) custom-call(f32[4,2,256,256]{3,2,1,0:T(8,128)S(1)} %bitcast.44, f32[4,2,256,256]{3,2,1,0:T(8,128)S(1)} %copy-done.3, f32[40,128]{1,0:T(8,128)S(1)} %add.107.sums.refs_3_, f32[2,256,256]{2,1,0:T(8,128)S(1)} %broadcast_select_fusion.carried), custom_call_target="tpu_custom_call" | custom-call | flops 4831838208 | bytes 7360512 | tf_op jit(solution)/shard_map/pallas_call | solution.py:67
  89.3 8.3 %collective-permute-start.17 = (f32[64,128]{1,0:T(8,128)S(1)}, f32[64,128]{1,0:T(8,128)S(1)}, u32[]{:S(2)}, u32[]{:S(2)}) collective-permute-start(f32[64,128]{1,0:T(8,128)S(1)} %copy-done.14), channel_id=1, source_target_pairs={{4,8},{12,16},{20,24},{8,4},{16,12},{24,20},{5,9},{13,17},{21,25},... | collective-permute-start | bytes 98312 | tf_op jit(solution)/shard_map/ppermute | solution.py:533
  97.7 1.5 %collective-permute-done.17 = f32[64,128]{1,0:T(8,128)S(1)} collective-permute-done((f32[64,128]{1,0:T(8,128)S(1)}, f32[64,128]{1,0:T(8,128)S(1)}, u32[]{:S(2)}, u32[]{:S(2)}) %collective-permute-start.17) | collective-permute-done | bytes 32800 | tf_op jit(solution)/shard_map/ppermute | solution.py:533
  99.2 1.5 %shard_map.122 = (f32[2,2,256,256]{3,2,1,0:T(8,128)S(1)}, f32[2,2,256,256]{3,2,1,0:T(8,128)S(1)}) custom-call(f32[1,2,256,256]{3,2,1,0:T(8,128)S(1)} %collective-permute-done.14.refs_0_, f32[1,2,256,256]{3,2,1,0:T(8,128)S(1)} %collective-permute-done.18.refs_1_, f32[4,2,256,256]{3,2,1,0:T(8,128)S(1)} %copy-done.3, f32[40,128]{1,0:T(8,128)S(1)} %add.107.sums.refs_3_), custom_call_target="tpu_custom_call" | custom-call | flops 1207959552 | bytes 5263360 | tf_op jit(solution)/shard_map/pallas_call | solution.py:67
  100.8 1.9 %shard_map.121 = (f32[2,2,256,256]{3,2,1,0:T(8,128)S(1)}, f32[2,256,256]{2,1,0:T(8,128)S(1)}) custom-call(f32[2,2,256,256]{3,2,1,0:T(8,128)S(1)} %get-tuple-element.101.link, f32[2,2,256,256]{3,2,1,0:T(8,128)S(1)} %get-tuple-element.102.source, f32[2,256,256]{2,1,0:T(8,128)S(1)} %collective-permute-done.16.carried), custom_call_target="tpu_custom_call" | custom-call | flops 1207959552 | bytes 4194304 | tf_op jit(solution)/shard_map/pallas_call | solution.py:67
  102.7 2.6 %shard_map.123 = (f32[2,2,256,256]{3,2,1,0:T(8,128)S(1)}, f32[2,256,256]{2,1,0:T(8,128)}) custom-call(f32[2,2,256,256]{3,2,1,0:T(8,128)S(1)} %get-tuple-element.110.link, f32[2,2,256,256]{3,2,1,0:T(8,128)S(1)} %get-tuple-element.111.source, f32[2,256,256]{2,1,0:T(8,128)S(1)} %get-tuple-element.112.carried), custom_call_target="tpu_custom_call" | custom-call | flops 1207959552 | bytes 4194304 | tf_op jit(solution)/shard_map/pallas_call | solution.py:67
  106.1 2.7 %shard_map.124 = (f32[2,2,256,256]{3,2,1,0:T(8,128)S(1)}, f32[2,2,256,256]{3,2,1,0:T(8,128)S(1)}, f32[2,256,256]{2,1,0:T(8,128)S(1)}) custom-call(s32[2]{0:T(128)S(1)} %pad_add_fusion.pick, f32[2,2,256,256]{3,2,1,0:T(8,128)S(1)} %get-tuple-element.118.link, f32[2,2,256,256]{3,2,1,0:T(8,128)S(1)} %get-tuple-element.119.source, ...), custom_call_target="tpu_custom_call" | custom-call | flops 1207959552 | bytes 9437192 | tf_op jit(solution)/shard_map/pallas_call | solution.py:67
  109.7 3.5 %shard_map.125 = (f32[2,2,256,256]{3,2,1,0:T(8,128)S(1)}, f32[2,2,256,256]{3,2,1,0:T(8,128)S(1)}, f32[2,256,256]{2,1,0:T(8,128)}) custom-call(s32[2]{0:T(128)S(1)} %pad_add_fusion.pick, f32[2,2,256,256]{3,2,1,0:T(8,128)S(1)} %get-tuple-element.126.link, f32[2,2,256,256]{3,2,1,0:T(8,128)S(1)} %get-tuple-element.127.source, ...), custom_call_target="tpu_custom_call" | custom-call | flops 1207959552 | bytes 9437192 | tf_op jit(solution)/shard_map/pallas_call | solution.py:67
  113.4 2.6 %collective-permute-done.20 = f32[2,2,256,256]{3,2,1,0:T(8,128)S(1)} collective-permute-done((f32[2,2,256,256]{3,2,1,0:T(8,128)S(1)}, f32[2,2,256,256]{3,2,1,0:T(8,128)S(1)}, u32[]{:S(2)}, u32[]{:S(2)}) %collective-permute-start.20) | collective-permute-done | bytes 1048608 | tf_op jit(solution)/shard_map/ppermute | solution.py:579
  116.2 1.5 %maximum_bitcast_fusion = f32[1,4,2,256,256]{4,3,2,1,0:T(8,128)} fusion(f32[2,2,256,256]{3,2,1,0:T(8,128)S(1)} %add.131, f32[2,2,256,256]{3,2,1,0:T(8,128)S(1)} %add.130), kind=kLoop, calls=%fused_computation.1 | loop fusion | flops 524288 | bytes 4194304 | tf_op jit(solution)/shard_map/broadcast_in_dim | solution.py:580
  (83 shorter events, 19.0 us)
Async XLA Ops:
  0.6 24.8 %copy-start = (f32[1,4,2,256,256]{4,3,2,1,0:T(8,128)S(1)}, f32[1,4,2,256,256]{4,3,2,1,0:T(8,128)}, u32[]{:S(2)}) copy-start(f32[1,4,2,256,256]{4,3,2,1,0:T(8,128)} %param.14) | copy-start | bytes 6291460
  1.9 13.0 %collective-permute-start.2 = (f32[1,2,256,256]{3,2,1,0:T(8,128)S(1)}, f32[1,2,256,256]{3,2,1,0:T(8,128)}, u32[]{:S(2)}, u32[]{:S(2)}) collective-permute-start(f32[1,2,256,256]{3,2,1,0:T(8,128)S(1)} %slice_bitcast_fusion), channel_id=1, source_target_pairs={{0,8},{4,12},{8,0},{12,4},{16,24},{20,28},{24,16},{28,20},{1,9},{5... | collective-permute-start | bytes 1572872 | tf_op jit(solution)/shard_map/ppermute | solution.py:347
  4.0 3.3 %collective-permute-start.1 = (f32[2,1,4,128]{3,2,0,1:T(4,128)S(1)}, f32[2,1,4,128]{3,2,0,1:T(4,128)S(1)}, u32[]{:S(2)}, u32[]{:S(2)}) collective-permute-start(f32[2,1,4,128]{3,2,0,1:T(4,128)S(1)} %get-tuple-element.136), channel_id=1, source_target_pairs={{0,1},{2,3},{1,0},{3,2},{4,5},{6,7},{5,4},{7,6},{8,9},{10,11},{9,8... | collective-permute-start | bytes 12296 | tf_op jit(solution)/shard_map/ppermute | solution.py:361
  5.3 4.7 %collective-permute-start = (f32[2,1,4,128]{3,2,0,1:T(4,128)S(1)}, f32[2,1,4,128]{3,2,0,1:T(4,128)S(1)}, u32[]{:S(2)}, u32[]{:S(2)}) collective-permute-start(f32[2,1,4,128]{3,2,0,1:T(4,128)S(1)} %get-tuple-element.137), channel_id=1, source_target_pairs={{1,2},{2,1},{5,6},{6,5},{9,10},{10,9},{13,14},{14,13},{17,18},{18,... | collective-permute-start | bytes 12296 | tf_op jit(solution)/shard_map/ppermute | solution.py:362
  14.8 2.8 %collective-permute-start.3 = (f32[40,128]{1,0:T(8,128)}, f32[40,128]{1,0:T(8,128)S(1)}, u32[]{:S(2)}, u32[]{:S(2)}) collective-permute-start(f32[40,128]{1,0:T(8,128)} %get-tuple-element.70), channel_id=1, source_target_pairs={{0,8},{4,12},{8,0},{12,4},{16,24},{20,28},{24,16},{28,20},{1,9},{5... | collective-permute-start | bytes 61448 | tf_op jit(solution)/shard_map/ppermute | solution.py:302
  19.2 3.6 %collective-permute-start.4 = (f32[104,128]{1,0:T(8,128)S(1)}, f32[104,128]{1,0:T(8,128)S(1)}, u32[]{:S(2)}, u32[]{:S(2)}) collective-permute-start(f32[104,128]{1,0:T(8,128)S(1)} %pad_maximum_fusion.1), channel_id=1, source_target_pairs={{0,4},{4,0},{8,12},{12,8},{16,20},{20,16},{24,28},{28,24},{1,5},{5... | collective-permute-start | bytes 159752 | tf_op jit(solution)/shard_map/ppermute | solution.py:302
  22.8 2.6 %collective-permute-start.5 = (f32[40,128]{1,0:T(8,128)S(1)}, f32[40,128]{1,0:T(8,128)S(1)}, u32[]{:S(2)}, u32[]{:S(2)}) collective-permute-start(f32[40,128]{1,0:T(8,128)S(1)} %slice_add_fusion), channel_id=1, source_target_pairs={{0,16},{4,20},{8,24},{12,28},{16,0},{20,4},{24,8},{28,12},{1,17},{... | collective-permute-start | bytes 61448 | tf_op jit(solution)/shard_map/ppermute | solution.py:302
  23.0 13.2 %collective-permute-start.7 = (f32[1,2,256,256]{3,2,1,0:T(8,128)}, f32[1,2,256,256]{3,2,1,0:T(8,128)}, u32[]{:S(2)}, u32[]{:S(2)}) collective-permute-start(f32[1,2,256,256]{3,2,1,0:T(8,128)} %get-tuple-element.79), channel_id=1, source_target_pairs={{0,8},{4,12},{8,0},{12,4},{16,24},{20,28},{24,16},{28,20},{1,9},{5... | collective-permute-start | bytes 1572872 | tf_op jit(solution)/shard_map/ppermute | solution.py:396
  27.0 10.3 %copy-start.10 = (f32[4,256,256]{2,1,0:T(8,128)S(1)}, f32[4,256,256]{2,1,0:T(8,128)}, u32[]{:S(2)}) copy-start(f32[4,256,256]{2,1,0:T(8,128)} %param.18) | copy-start | bytes 3145732
  33.2 13.8 %copy-start.4 = (f32[2,256,256]{2,1,0:T(8,128)}, f32[2,256,256]{2,1,0:T(8,128)S(1)}, u32[]{:S(2)}) copy-start(f32[2,256,256]{2,1,0:T(8,128)S(1)} %get-tuple-element.76.whole_source) | copy-start | bytes 1572868
  33.2 13.8 %copy-start.6 = (f32[2,256,256]{2,1,0:T(8,128)}, f32[2,256,256]{2,1,0:T(8,128)S(1)}, u32[]{:S(2)}) copy-start(f32[2,256,256]{2,1,0:T(8,128)S(1)} %get-tuple-element.74.whole_map) | copy-start | bytes 1572868
  33.2 12.1 %collective-permute-start.6 = (f32[2,256,256]{2,1,0:T(8,128)S(1)}, f32[2,256,256]{2,1,0:T(8,128)S(1)}, u32[]{:S(2)}, u32[]{:S(2)}) collective-permute-start(f32[2,256,256]{2,1,0:T(8,128)S(1)} %get-tuple-element.76.whole_source), channel_id=1, source_target_pairs={{0,1},{2,3},{1,0},{3,2},{4,5},{6,7},{5,4},{7,6},{8,9},{10,11},{9,8... | collective-permute-start | bytes 1572872 | tf_op jit(solution)/shard_map/ppermute | solution.py:471
  34.7 20.6 %collective-permute-start.10 = (f32[1,2,256,256]{3,2,1,0:T(8,128)}, f32[1,2,256,256]{3,2,1,0:T(8,128)}, u32[]{:S(2)}, u32[]{:S(2)}) collective-permute-start(f32[1,2,256,256]{3,2,1,0:T(8,128)} %collective-permute-done.2.refs_0_), channel_id=1, source_target_pairs={{0,16},{4,20},{8,24},{12,28},{16,0},{20,4},{24,8},{28,12},{1,17},{... | collective-permute-start | bytes 1572872 | tf_op jit(solution)/shard_map/ppermute | solution.py:401
  36.2 13.1 %collective-permute-start.9 = (f32[1,2,256,256]{3,2,1,0:T(8,128)}, f32[1,2,256,256]{3,2,1,0:T(8,128)}, u32[]{:S(2)}, u32[]{:S(2)}) collective-permute-start(f32[1,2,256,256]{3,2,1,0:T(8,128)} %get-tuple-element.87), channel_id=1, source_target_pairs={{0,8},{4,12},{8,0},{12,4},{16,24},{20,28},{24,16},{28,20},{1,9},{5... | collective-permute-start | bytes 1572872 | tf_op jit(solution)/shard_map/ppermute | solution.py:405
  37.8 20.2 %collective-permute-start.11 = (f32[1,2,256,256]{3,2,1,0:T(8,128)}, f32[1,2,256,256]{3,2,1,0:T(8,128)}, u32[]{:S(2)}, u32[]{:S(2)}) collective-permute-start(f32[1,2,256,256]{3,2,1,0:T(8,128)} %collective-permute-done.7.refs_1_), channel_id=1, source_target_pairs={{0,16},{4,20},{8,24},{12,28},{16,0},{20,4},{24,8},{28,12},{1,17},{... | collective-permute-start | bytes 1572872 | tf_op jit(solution)/shard_map/ppermute | solution.py:401
  47.0 13.3 %collective-permute-start.8 = (f32[2,256,256]{2,1,0:T(8,128)}, f32[2,256,256]{2,1,0:T(8,128)}, u32[]{:S(2)}, u32[]{:S(2)}) collective-permute-start(f32[2,256,256]{2,1,0:T(8,128)} %shard_map.115.before), channel_id=1, source_target_pairs={{1,2},{2,1},{5,6},{6,5},{9,10},{10,9},{13,14},{14,13},{17,18},{18,... | collective-permute-start | bytes 1572872 | tf_op jit(solution)/shard_map/ppermute | solution.py:471
  49.3 20.3 %collective-permute-start.13 = (f32[1,2,256,256]{3,2,1,0:T(8,128)}, f32[1,2,256,256]{3,2,1,0:T(8,128)S(1)}, u32[]{:S(2)}, u32[]{:S(2)}) collective-permute-start(f32[1,2,256,256]{3,2,1,0:T(8,128)} %get-tuple-element.93), channel_id=1, source_target_pairs={{0,8},{4,12},{8,0},{12,4},{16,24},{20,28},{24,16},{28,20},{1,9},{5... | collective-permute-start | bytes 1572872 | tf_op jit(solution)/shard_map/ppermute | solution.py:405
  52.1 8.2 %copy-start.5 = (f32[2,256,256]{2,1,0:T(8,128)S(1)}, f32[2,256,256]{2,1,0:T(8,128)}, u32[]{:S(2)}) copy-start(f32[2,256,256]{2,1,0:T(8,128)} %copy-done.4) | copy-start | bytes 1572868
  52.1 8.2 %copy-start.7 = (f32[2,256,256]{2,1,0:T(8,128)S(1)}, f32[2,256,256]{2,1,0:T(8,128)}, u32[]{:S(2)}) copy-start(f32[2,256,256]{2,1,0:T(8,128)} %copy-done.6) | copy-start | bytes 1572868
  55.0 7.6 %copy-start.12 = (f32[1,1,8,128]{3,2,0,1:T(8,128)S(1)}, f32[1,1,8,128]{3,2,0,1:T(8,128)}, u32[]{:S(2)}) copy-start(f32[1,1,8,128]{3,2,0,1:T(8,128)} %get-tuple-element.168) | copy-start | bytes 12292
  55.0 11.8 %copy-start.3 = (f32[4,2,256,256]{3,2,1,0:T(8,128)S(1)}, f32[4,2,256,256]{3,2,1,0:T(8,128)}, u32[]{:S(2)}) copy-start(f32[4,2,256,256]{3,2,1,0:T(8,128)} %refs_2_.7) | copy-start | bytes 6291460
  55.0 25.5 %collective-permute-start.14 = (f32[1,2,256,256]{3,2,1,0:T(8,128)}, f32[1,2,256,256]{3,2,1,0:T(8,128)S(1)}, u32[]{:S(2)}, u32[]{:S(2)}) collective-permute-start(f32[1,2,256,256]{3,2,1,0:T(8,128)} %collective-permute-done.9.refs_0_), channel_id=1, source_target_pairs={{0,16},{4,20},{8,24},{12,28},{16,0},{20,4},{24,8},{28,12},{1,17},{... | collective-permute-start | bytes 1572872 | tf_op jit(solution)/shard_map/ppermute | solution.py:401
  62.4 18.1 %collective-permute-start.12 = (f32[2,256,256]{2,1,0:T(8,128)S(1)}, f32[2,256,256]{2,1,0:T(8,128)S(1)}, u32[]{:S(2)}, u32[]{:S(2)}) collective-permute-start(f32[2,256,256]{2,1,0:T(8,128)S(1)} %get-tuple-element.91), channel_id=1, source_target_pairs={{0,1},{2,3},{1,0},{3,2},{4,5},{6,7},{5,4},{7,6},{8,9},{10,11},{9,8... | collective-permute-start | bytes 1572872 | tf_op jit(solution)/shard_map/ppermute | solution.py:505
  62.6 35.1 %collective-permute-start.16 = (f32[2,256,256]{2,1,0:T(8,128)S(1)}, f32[2,256,256]{2,1,0:T(8,128)S(1)}, u32[]{:S(2)}, u32[]{:S(2)}) collective-permute-start(f32[2,256,256]{2,1,0:T(8,128)S(1)} %get-tuple-element.103), channel_id=1, source_target_pairs={{8,17},{9,18},{10,19},{12,21},{13,22},{14,23},{16,9},{17,10},{18,1... | collective-permute-start | bytes 1572872 | tf_op jit(solution)/shard_map/ppermute | solution.py:506
  69.5 29.7 %collective-permute-start.18 = (f32[1,2,256,256]{3,2,1,0:T(8,128)S(1)}, f32[1,2,256,256]{3,2,1,0:T(8,128)S(1)}, u32[]{:S(2)}, u32[]{:S(2)}) collective-permute-start(f32[1,2,256,256]{3,2,1,0:T(8,128)S(1)} %collective-permute-done.13.refs_1_), channel_id=1, source_target_pairs={{0,16},{4,20},{8,24},{12,28},{16,0},{20,4},{24,8},{28,12},{1,17},{... | collective-permute-start | bytes 1572872 | tf_op jit(solution)/shard_map/ppermute | solution.py:401
  81.6 7.7 %copy-start.14 = (f32[64,128]{1,0:T(8,128)S(1)}, f32[64,128]{1,0:T(8,128)}, u32[]{:S(2)}) copy-start(f32[64,128]{1,0:T(8,128)} %get-tuple-element.105) | copy-start | bytes 98308
  81.6 15.9 %copy-start.8 = (f32[16,4,128]{2,1,0:T(4,128)S(1)}, f32[16,4,128]{2,1,0:T(4,128)}, u32[]{:S(2)}) copy-start(f32[16,4,128]{2,1,0:T(4,128)} %param.12) | copy-start | bytes 98308
  81.7 15.9 %copy-start.9 = (f32[16,4,128]{2,1,0:T(4,128)S(1)}, f32[16,4,128]{2,1,0:T(4,128)}, u32[]{:S(2)}) copy-start(f32[16,4,128]{2,1,0:T(4,128)} %param.10) | copy-start | bytes 98308
  81.7 24.5 %collective-permute-start.15 = (f32[2,256,256]{2,1,0:T(8,128)S(1)}, f32[2,256,256]{2,1,0:T(8,128)S(1)}, u32[]{:S(2)}, u32[]{:S(2)}) collective-permute-start(f32[2,256,256]{2,1,0:T(8,128)S(1)} %broadcast_select_fusion.carried), channel_id=1, source_target_pairs={{0,8},{4,12},{8,0},{12,4},{16,24},{20,28},{24,16},{28,20},{1,9},{5... | collective-permute-start | bytes 1572872 | tf_op jit(solution)/shard_map/ppermute | solution.py:514
  89.3 9.9 %collective-permute-start.17 = (f32[64,128]{1,0:T(8,128)S(1)}, f32[64,128]{1,0:T(8,128)S(1)}, u32[]{:S(2)}, u32[]{:S(2)}) collective-permute-start(f32[64,128]{1,0:T(8,128)S(1)} %copy-done.14), channel_id=1, source_target_pairs={{4,8},{12,16},{20,24},{8,4},{16,12},{24,20},{5,9},{13,17},{21,25},... | collective-permute-start | bytes 98312 | tf_op jit(solution)/shard_map/ppermute | solution.py:533
  108.9 4.3 %collective-permute-start.19 = (f32[2,2,256,256]{3,2,1,0:T(8,128)S(1)}, f32[2,2,256,256]{3,2,1,0:T(8,128)S(1)}, u32[]{:S(2)}, u32[]{:S(2)}) collective-permute-start(f32[2,2,256,256]{3,2,1,0:T(8,128)S(1)} %get-tuple-element.125), channel_id=1, source_target_pairs={{0,4},{4,0},{8,12},{12,8},{16,20},{20,16},{24,28},{28,24},{1,5},{5... | collective-permute-start | bytes 3145736 | tf_op jit(solution)/shard_map/ppermute | solution.py:579
  113.3 2.7 %collective-permute-start.20 = (f32[2,2,256,256]{3,2,1,0:T(8,128)S(1)}, f32[2,2,256,256]{3,2,1,0:T(8,128)S(1)}, u32[]{:S(2)}, u32[]{:S(2)}) collective-permute-start(f32[2,2,256,256]{3,2,1,0:T(8,128)S(1)} %get-tuple-element.133), channel_id=1, source_target_pairs={{0,4},{4,0},{8,12},{12,8},{16,20},{20,16},{24,28},{28,24},{1,5},{5... | collective-permute-start | bytes 3145736 | tf_op jit(solution)/shard_map/ppermute | solution.py:579
  (7 other events, 36.4 us)

commit v14 on v13

--- a/solution.py
+++ b/solution.py
@@ -504,7 +504,6 @@
 
     arrived = lax.ppermute(leaving, "slab", swaps((peers - 2) % 2))
     carried_second = lax.ppermute(onward, ("energy", "slab"), both(second_pairs))
-    sent_on(3)
     beside_second[0] = beside(0, free_second[:2])
     beside_first[1] = beside(1, free_first[2:])
     arrived, beside_first[1], beside_second[0], free_second[2] = lax.optimization_barrier(
@@ -512,6 +511,8 @@
     )
     carried = jnp.where(place % 2 == 1, arrived, previous)
     carried_first = lax.ppermute(carried, "energy", first_pairs)
+    carried, free_first[3] = lax.optimization_barrier((carried, free_first[3]))
+    sent_on(3)
     greens, _ = call(
         functools.partial(own_greens_kernel, count),
         24,

time: 118 us -> 118 us (level)
  the two profiles are of different devices: /device:TPU:21 before, /device:TPU:13 now
where the time goes in v14:
time: 118 us; the launch traced here: 116 us
  Pallas kernels  41.5 us (35%)
  starting transfers between devices  38.2 us (32%)
  waiting for transfers between devices  24.6 us (21%)
  other arithmetic  6.11 us (5%)
  local copies, waits for them, and re-layouts  4.62 us (4%)
    pallas_call x13, Pallas kernels, call(): pl.pallas_call(kernel, out_shape=out_shapes, cost_estimate=cost, compiler...  41.5 us
    ppermute x1, starting transfers between devices, per_device(): lax.ppermute(ends, 'energy', beyond + [(b, a) for a, b in beyond])  10.3 us
    ppermute x2, waiting for transfers between devices, per_device(): arrived = lax.ppermute(leaving, 'slab', swaps((hop - 1) % 2))  9.72 us
    ppermute x1, starting transfers between devices, per_device(): crossed = lax.ppermute(jnp.where(even, lower, upper), 'slab', swaps(1))  4.32 us
    ppermute x3, starting transfers between devices, exchanged(): lax.ppermute(given, 'energy', [(e, e ^ mask) for e in range(peers)])  4.13 us
    ppermute x1, starting transfers between devices, per_device(): lax.ppermute(onward, ('energy', 'slab'), both(second_pairs))  4.07 us
    ppermute x3, waiting for transfers between devices, exchanged(): lax.ppermute(given, 'energy', [(e, e ^ mask) for e in range(peers)])  3.71 us
    ppermute x2, starting transfers between devices, per_device(): arrived = lax.ppermute(leaving, 'slab', swaps((hop - 1) % 2))  3.63 us
  transfers between devices with their start and end apart: 21, of which 13 were waited for; matrix products, arithmetic and copies ran while one was open for 3% of the time, Pallas kernels for 33%

profile of v14, /device:TPU:13, one launch (start us, length us, event | category | flops | bytes accessed | tf_op | source)
XLA Modules:
  0.0 116.1 jit_solution(2325413199244874801)
XLA Ops:
  1.9 1.3 %collective-permute-start.2 = (f32[1,2,256,256]{3,2,1,0:T(8,128)S(1)}, f32[1,2,256,256]{3,2,1,0:T(8,128)}, u32[]{:S(2)}, u32[]{:S(2)}) collective-permute-start(f32[1,2,256,256]{3,2,1,0:T(8,128)S(1)} %slice_bitcast_fusion), channel_id=1, source_target_pairs={{0,8},{4,12},{8,0},{12,4},{16,24},{20,28},{24,16},{28,20},{1,9},{5... | collective-permute-start | bytes 1572872 | tf_op jit(solution)/shard_map/ppermute | solution.py:347
  4.2 4.3 %collective-permute-start = (f32[2,1,4,128]{3,2,0,1:T(4,128)S(1)}, f32[2,1,4,128]{3,2,0,1:T(4,128)S(1)}, u32[]{:S(2)}, u32[]{:S(2)}) collective-permute-start(f32[2,1,4,128]{3,2,0,1:T(4,128)S(1)} %get-tuple-element.141), channel_id=1, source_target_pairs={{1,2},{2,1},{5,6},{6,5},{9,10},{10,9},{13,14},{14,13},{17,18},{18,... | collective-permute-start | bytes 12296 | tf_op jit(solution)/shard_map/ppermute | solution.py:362
  8.5 1.4 %collective-permute-done = f32[2,1,4,128]{3,2,0,1:T(4,128)S(1)} collective-permute-done((f32[2,1,4,128]{3,2,0,1:T(4,128)S(1)}, f32[2,1,4,128]{3,2,0,1:T(4,128)S(1)}, u32[]{:S(2)}, u32[]{:S(2)}) %collective-permute-start) | collective-permute-done | bytes 4128 | tf_op jit(solution)/shard_map/ppermute | solution.py:362
  10.5 3.7 %shard_map.113 = (f32[40,128]{1,0:T(8,128)}, f32[64,128]{1,0:T(8,128)}, f32[1,2,256,256]{3,2,1,0:T(8,128)}, f32[1,2,256,256]{3,2,1,0:T(8,128)}, f32[1,2,256,256]{3,2,1,0:T(8,128)}) custom-call(s32[1]{0:T(128)} %bitcast.2.mine, f32[64,128]{1,0:T(8,128)} %bitcast.48, f32[64,128]{1,0:T(8,128)} %bitcast.46, f32[64,128]{1,0:T(8,128)} %bitcast.49, ...), custom_call_target="tpu_custom_call" | custom-call | flops 301989888 | bytes 3833860 | tf_op jit(solution)/shard_map/pallas_call | solution.py:67
  16.0 1.6 %collective-permute-done.3 = f32[40,128]{1,0:T(8,128)S(1)} collective-permute-done((f32[40,128]{1,0:T(8,128)}, f32[40,128]{1,0:T(8,128)S(1)}, u32[]{:S(2)}, u32[]{:S(2)}) %collective-permute-start.3) | collective-permute-done | bytes 20512 | tf_op jit(solution)/shard_map/ppermute | solution.py:302
  19.2 2.7 %collective-permute-start.4 = (f32[104,128]{1,0:T(8,128)S(1)}, f32[104,128]{1,0:T(8,128)S(1)}, u32[]{:S(2)}, u32[]{:S(2)}) collective-permute-start(f32[104,128]{1,0:T(8,128)S(1)} %pad_maximum_fusion.1), channel_id=1, source_target_pairs={{0,4},{4,0},{8,12},{12,8},{16,20},{20,16},{24,28},{28,24},{1,5},{5... | collective-permute-start | bytes 159752 | tf_op jit(solution)/shard_map/ppermute | solution.py:302
  25.4 1.6 %copy-done.1 = f32[4,2,256,256]{3,2,1,0:T(8,128)S(1)} copy-done((f32[4,2,256,256]{3,2,1,0:T(8,128)S(1)}, f32[4,2,256,256]{3,2,1,0:T(8,128)}, u32[]{:S(2)}) %copy-start.1) | copy-done | bytes 2097176
  27.0 6.2 %shard_map.114 = (f32[2,256,256]{2,1,0:T(8,128)S(1)}, f32[2,256,256]{2,1,0:T(8,128)S(1)}) custom-call(f32[4,2,256,256]{3,2,1,0:T(8,128)S(1)} %bitcast.43, f32[4,2,256,256]{3,2,1,0:T(8,128)S(1)} %copy-done.1, f32[40,128]{1,0:T(8,128)S(1)} %add.107.sums.refs_3_), custom_call_target="tpu_custom_call" | custom-call | flops 5133828096 | bytes 5263360 | tf_op jit(solution)/shard_map/pallas_call | solution.py:67
  33.7 2.5 %collective-permute-done.7.refs_1_ = f32[1,2,256,256]{3,2,1,0:T(8,128)} collective-permute-done((f32[1,2,256,256]{3,2,1,0:T(8,128)}, f32[1,2,256,256]{3,2,1,0:T(8,128)}, u32[]{:S(2)}, u32[]{:S(2)}) %collective-permute-start.7) | collective-permute-done | bytes 524320 | tf_op jit(solution)/shard_map/ppermute | solution.py:396
  37.8 1.3 %collective-permute-start.11 = (f32[1,2,256,256]{3,2,1,0:T(8,128)}, f32[1,2,256,256]{3,2,1,0:T(8,128)}, u32[]{:S(2)}, u32[]{:S(2)}) collective-permute-start(f32[1,2,256,256]{3,2,1,0:T(8,128)} %collective-permute-done.7.refs_1_), channel_id=1, source_target_pairs={{0,16},{4,20},{8,24},{12,28},{16,0},{20,4},{24,8},{28,12},{1,17},{... | collective-permute-start | bytes 1572872 | tf_op jit(solution)/shard_map/ppermute | solution.py:401
  39.1 6.2 %collective-permute-done.6.carried = f32[2,256,256]{2,1,0:T(8,128)S(1)} collective-permute-done((f32[2,256,256]{2,1,0:T(8,128)S(1)}, f32[2,256,256]{2,1,0:T(8,128)S(1)}, u32[]{:S(2)}, u32[]{:S(2)}) %collective-permute-start.6) | collective-permute-done | bytes 524320 | tf_op jit(solution)/shard_map/ppermute | solution.py:471
  45.3 1.7 %shard_map.115.before = f32[2,256,256]{2,1,0:T(8,128)} custom-call(f32[2,256,256]{2,1,0:T(8,128)S(1)} %get-tuple-element.76.whole_map, f32[2,256,256]{2,1,0:T(8,128)S(1)} %get-tuple-element.78.whole_source, f32[2,256,256]{2,1,0:T(8,128)S(1)} %collective-permute-done.6.carried), custom_call_target="tpu_custom_call" | custom-call | flops 603979776 | bytes 2097152 | tf_op jit(solution)/shard_map/pallas_call | solution.py:67
  47.0 3.4 %collective-permute-start.8 = (f32[2,256,256]{2,1,0:T(8,128)}, f32[2,256,256]{2,1,0:T(8,128)}, u32[]{:S(2)}, u32[]{:S(2)}) collective-permute-start(f32[2,256,256]{2,1,0:T(8,128)} %shard_map.115.before), channel_id=1, source_target_pairs={{1,2},{2,1},{5,6},{6,5},{9,10},{10,9},{13,14},{14,13},{17,18},{18,... | collective-permute-start | bytes 1572872 | tf_op jit(solution)/shard_map/ppermute | solution.py:471
  51.7 1.6 %copy-done.2 = f32[4,2,256,256]{3,2,1,0:T(8,128)S(1)} copy-done((f32[4,2,256,256]{3,2,1,0:T(8,128)S(1)}, f32[4,2,256,256]{3,2,1,0:T(8,128)}, u32[]{:S(2)}) %copy-start.2) | copy-done | bytes 2097176
  53.3 2.8 %shard_map.116 = (f32[2,2,256,256]{3,2,1,0:T(8,128)S(1)}, f32[2,2,256,256]{3,2,1,0:T(8,128)S(1)}) custom-call(f32[1,2,256,256]{3,2,1,0:T(8,128)} %collective-permute-done.2.refs_0_, f32[1,2,256,256]{3,2,1,0:T(8,128)} %collective-permute-done.7.refs_1_, f32[4,2,256,256]{3,2,1,0:T(8,128)S(1)} %copy-done.2, f32[40,128]{1,0:T(8,128)S(1)} %add.107.sums.refs_3_), custom_call_target="tpu_custom_call" | custom-call | flops 1207959552 | bytes 5263360 | tf_op jit(solution)/shard_map/pallas_call | solution.py:67
  56.8 3.5 %collective-permute-done.8.carried = f32[2,256,256]{2,1,0:T(8,128)} collective-permute-done((f32[2,256,256]{2,1,0:T(8,128)}, f32[2,256,256]{2,1,0:T(8,128)}, u32[]{:S(2)}, u32[]{:S(2)}) %collective-permute-start.8) | collective-permute-done | bytes 524320 | tf_op jit(solution)/shard_map/ppermute | solution.py:471
  60.3 2.1 %shard_map.117 = (f32[2,256,256]{2,1,0:T(8,128)S(1)}, f32[2,256,256]{2,1,0:T(8,128)S(1)}) custom-call(s32[1]{0:T(128)} %bitcast.odd, f32[2,256,256]{2,1,0:T(8,128)S(1)} %copy-done.7, f32[2,256,256]{2,1,0:T(8,128)S(1)} %copy-done.5, f32[2,256,256]{2,1,0:T(8,128)} %collective-permute-done.8.carried, f32[2,256,256]{2,1,0:T(8,128)} %shard_map.115.before), custom_call_target="tpu_custom_call" | custom-call | flops 603979776 | bytes 3145732 | tf_op jit(solution)/shard_map/pallas_call | solution.py:67
  62.6 4.1 %collective-permute-start.16 = (f32[2,256,256]{2,1,0:T(8,128)S(1)}, f32[2,256,256]{2,1,0:T(8,128)S(1)}, u32[]{:S(2)}, u32[]{:S(2)}) collective-permute-start(f32[2,256,256]{2,1,0:T(8,128)S(1)} %get-tuple-element.105), channel_id=1, source_target_pairs={{8,17},{9,18},{10,19},{12,21},{13,22},{14,23},{16,9},{17,10},{18,1... | collective-permute-start | bytes 1572872 | tf_op jit(solution)/shard_map/ppermute | solution.py:506
  66.7 2.7 %shard_map.119 = (f32[2,2,256,256]{3,2,1,0:T(8,128)S(1)}, f32[2,2,256,256]{3,2,1,0:T(8,128)S(1)}) custom-call(f32[1,2,256,256]{3,2,1,0:T(8,128)} %collective-permute-done.10.refs_0_, f32[1,2,256,256]{3,2,1,0:T(8,128)} %collective-permute-done.11.refs_1_, f32[4,2,256,256]{3,2,1,0:T(8,128)S(1)} %copy-done.3, f32[40,128]{1,0:T(8,128)S(1)} %add.107.sums.refs_3_), custom_call_target="tpu_custom_call" | custom-call | flops 1207959552 | bytes 5263360 | tf_op jit(solution)/shard_map/pallas_call | solution.py:67
  69.4 2.5 %shard_map.118 = (f32[2,2,256,256]{3,2,1,0:T(8,128)S(1)}, f32[2,2,256,256]{3,2,1,0:T(8,128)S(1)}) custom-call(f32[1,2,256,256]{3,2,1,0:T(8,128)} %collective-permute-done.9.refs_0_, f32[1,2,256,256]{3,2,1,0:T(8,128)S(1)} %collective-permute-done.13.refs_1_, f32[4,2,256,256]{3,2,1,0:T(8,128)S(1)} %copy-done.3, f32[40,128]{1,0:T(8,128)S(1)} %add.107.sums.refs_3_), custom_call_target="tpu_custom_call" | custom-call | flops 1207959552 | bytes 5263360 | tf_op jit(solution)/shard_map/pallas_call | solution.py:67
  74.3 7.5 %shard_map.120 = (f32[4,2,256,256]{3,2,1,0:T(8,128)S(1)}, f32[2,256,256]{2,1,0:T(8,128)}) custom-call(f32[4,2,256,256]{3,2,1,0:T(8,128)S(1)} %bitcast.44, f32[4,2,256,256]{3,2,1,0:T(8,128)S(1)} %copy-done.3, f32[40,128]{1,0:T(8,128)S(1)} %add.107.sums.refs_3_, f32[2,256,256]{2,1,0:T(8,128)S(1)} %broadcast_select_fusion.carried), custom_call_target="tpu_custom_call" | custom-call | flops 4831838208 | bytes 7360512 | tf_op jit(solution)/shard_map/pallas_call | solution.py:67
  81.8 10.3 %collective-permute-start.17 = (f32[64,128]{1,0:T(8,128)S(1)}, f32[64,128]{1,0:T(8,128)S(1)}, u32[]{:S(2)}, u32[]{:S(2)}) collective-permute-start(f32[64,128]{1,0:T(8,128)S(1)} %copy-done.14), channel_id=1, source_target_pairs={{4,8},{12,16},{20,24},{8,4},{16,12},{24,20},{5,9},{13,17},{21,25},... | collective-permute-start | bytes 98312 | tf_op jit(solution)/shard_map/ppermute | solution.py:534
  92.3 1.5 %collective-permute-done.17 = f32[64,128]{1,0:T(8,128)S(1)} collective-permute-done((f32[64,128]{1,0:T(8,128)S(1)}, f32[64,128]{1,0:T(8,128)S(1)}, u32[]{:S(2)}, u32[]{:S(2)}) %collective-permute-start.17) | collective-permute-done | bytes 32800 | tf_op jit(solution)/shard_map/ppermute | solution.py:534
  93.8 1.4 %collective-permute-done.18.refs_1_ = f32[1,2,256,256]{3,2,1,0:T(8,128)S(1)} collective-permute-done((f32[1,2,256,256]{3,2,1,0:T(8,128)S(1)}, f32[1,2,256,256]{3,2,1,0:T(8,128)S(1)}, u32[]{:S(2)}, u32[]{:S(2)}) %collective-permute-start.18) | collective-permute-done | bytes 524320 | tf_op jit(solution)/shard_map/ppermute | solution.py:401
  95.2 1.5 %shard_map.122 = (f32[2,2,256,256]{3,2,1,0:T(8,128)S(1)}, f32[2,2,256,256]{3,2,1,0:T(8,128)S(1)}) custom-call(f32[1,2,256,256]{3,2,1,0:T(8,128)S(1)} %collective-permute-done.14.refs_0_, f32[1,2,256,256]{3,2,1,0:T(8,128)S(1)} %collective-permute-done.18.refs_1_, f32[4,2,256,256]{3,2,1,0:T(8,128)S(1)} %copy-done.3, f32[40,128]{1,0:T(8,128)S(1)} %add.107.sums.refs_3_), custom_call_target="tpu_custom_call" | custom-call | flops 1207959552 | bytes 5263360 | tf_op jit(solution)/shard_map/pallas_call | solution.py:67
  96.8 1.9 %shard_map.121 = (f32[2,2,256,256]{3,2,1,0:T(8,128)S(1)}, f32[2,256,256]{2,1,0:T(8,128)S(1)}) custom-call(f32[2,2,256,256]{3,2,1,0:T(8,128)S(1)} %get-tuple-element.103.link, f32[2,2,256,256]{3,2,1,0:T(8,128)S(1)} %get-tuple-element.104.source, f32[2,256,256]{2,1,0:T(8,128)S(1)} %collective-permute-done.16.carried), custom_call_target="tpu_custom_call" | custom-call | flops 1207959552 | bytes 4194304 | tf_op jit(solution)/shard_map/pallas_call | solution.py:67
  98.7 2.6 %shard_map.123 = (f32[2,2,256,256]{3,2,1,0:T(8,128)S(1)}, f32[2,256,256]{2,1,0:T(8,128)}) custom-call(f32[2,2,256,256]{3,2,1,0:T(8,128)S(1)} %get-tuple-element.114.link, f32[2,2,256,256]{3,2,1,0:T(8,128)S(1)} %get-tuple-element.115.source, f32[2,256,256]{2,1,0:T(8,128)S(1)} %get-tuple-element.116.carried), custom_call_target="tpu_custom_call" | custom-call | flops 1207959552 | bytes 4194304 | tf_op jit(solution)/shard_map/pallas_call | solution.py:67
  102.1 2.7 %shard_map.124 = (f32[2,2,256,256]{3,2,1,0:T(8,128)S(1)}, f32[2,2,256,256]{3,2,1,0:T(8,128)S(1)}, f32[2,256,256]{2,1,0:T(8,128)S(1)}) custom-call(s32[2]{0:T(128)S(1)} %pad_add_fusion.pick, f32[2,2,256,256]{3,2,1,0:T(8,128)S(1)} %get-tuple-element.122.link, f32[2,2,256,256]{3,2,1,0:T(8,128)S(1)} %get-tuple-element.123.source, ...), custom_call_target="tpu_custom_call" | custom-call | flops 1207959552 | bytes 9437192 | tf_op jit(solution)/shard_map/pallas_call | solution.py:67
  104.9 3.2 %collective-permute-start.19 = (f32[2,2,256,256]{3,2,1,0:T(8,128)S(1)}, f32[2,2,256,256]{3,2,1,0:T(8,128)S(1)}, u32[]{:S(2)}, u32[]{:S(2)}) collective-permute-start(f32[2,2,256,256]{3,2,1,0:T(8,128)S(1)} %get-tuple-element.129), channel_id=1, source_target_pairs={{0,4},{4,0},{8,12},{12,8},{16,20},{20,16},{24,28},{28,24},{1,5},{5... | collective-permute-start | bytes 3145736 | tf_op jit(solution)/shard_map/ppermute | solution.py:580
  108.1 3.5 %shard_map.125 = (f32[2,2,256,256]{3,2,1,0:T(8,128)S(1)}, f32[2,2,256,256]{3,2,1,0:T(8,128)S(1)}, f32[2,256,256]{2,1,0:T(8,128)}) custom-call(s32[2]{0:T(128)S(1)} %pad_add_fusion.pick, f32[2,2,256,256]{3,2,1,0:T(8,128)S(1)} %get-tuple-element.130.link, f32[2,2,256,256]{3,2,1,0:T(8,128)S(1)} %get-tuple-element.131.source, ...), custom_call_target="tpu_custom_call" | custom-call | flops 1207959552 | bytes 9437192 | tf_op jit(solution)/shard_map/pallas_call | solution.py:67
  111.8 2.6 %collective-permute-done.20 = f32[2,2,256,256]{3,2,1,0:T(8,128)S(1)} collective-permute-done((f32[2,2,256,256]{3,2,1,0:T(8,128)S(1)}, f32[2,2,256,256]{3,2,1,0:T(8,128)S(1)}, u32[]{:S(2)}, u32[]{:S(2)}) %collective-permute-start.20) | collective-permute-done | bytes 1048608 | tf_op jit(solution)/shard_map/ppermute | solution.py:580
  114.6 1.5 %maximum_bitcast_fusion = f32[1,4,2,256,256]{4,3,2,1,0:T(8,128)} fusion(f32[2,2,256,256]{3,2,1,0:T(8,128)S(1)} %add.131, f32[2,2,256,256]{3,2,1,0:T(8,128)S(1)} %add.130), kind=kLoop, calls=%fused_computation.1 | loop fusion | flops 524288 | bytes 4194304 | tf_op jit(solution)/shard_map/broadcast_in_dim | solution.py:581
  (83 shorter events, 17.5 us)
Async XLA Ops:
  0.6 24.8 %copy-start = (f32[1,4,2,256,256]{4,3,2,1,0:T(8,128)S(1)}, f32[1,4,2,256,256]{4,3,2,1,0:T(8,128)}, u32[]{:S(2)}) copy-start(f32[1,4,2,256,256]{4,3,2,1,0:T(8,128)} %param.14) | copy-start | bytes 6291460
  1.9 13.0 %collective-permute-start.2 = (f32[1,2,256,256]{3,2,1,0:T(8,128)S(1)}, f32[1,2,256,256]{3,2,1,0:T(8,128)}, u32[]{:S(2)}, u32[]{:S(2)}) collective-permute-start(f32[1,2,256,256]{3,2,1,0:T(8,128)S(1)} %slice_bitcast_fusion), channel_id=1, source_target_pairs={{0,8},{4,12},{8,0},{12,4},{16,24},{20,28},{24,16},{28,20},{1,9},{5... | collective-permute-start | bytes 1572872 | tf_op jit(solution)/shard_map/ppermute | solution.py:347
  4.0 4.6 %collective-permute-start.1 = (f32[2,1,4,128]{3,2,0,1:T(4,128)S(1)}, f32[2,1,4,128]{3,2,0,1:T(4,128)S(1)}, u32[]{:S(2)}, u32[]{:S(2)}) collective-permute-start(f32[2,1,4,128]{3,2,0,1:T(4,128)S(1)} %get-tuple-element.140), channel_id=1, source_target_pairs={{0,1},{2,3},{1,0},{3,2},{4,5},{6,7},{5,4},{7,6},{8,9},{10,11},{9,8... | collective-permute-start | bytes 12296 | tf_op jit(solution)/shard_map/ppermute | solution.py:361
  4.2 5.7 %collective-permute-start = (f32[2,1,4,128]{3,2,0,1:T(4,128)S(1)}, f32[2,1,4,128]{3,2,0,1:T(4,128)S(1)}, u32[]{:S(2)}, u32[]{:S(2)}) collective-permute-start(f32[2,1,4,128]{3,2,0,1:T(4,128)S(1)} %get-tuple-element.141), channel_id=1, source_target_pairs={{1,2},{2,1},{5,6},{6,5},{9,10},{10,9},{13,14},{14,13},{17,18},{18,... | collective-permute-start | bytes 12296 | tf_op jit(solution)/shard_map/ppermute | solution.py:362
  14.8 2.8 %collective-permute-start.3 = (f32[40,128]{1,0:T(8,128)}, f32[40,128]{1,0:T(8,128)S(1)}, u32[]{:S(2)}, u32[]{:S(2)}) collective-permute-start(f32[40,128]{1,0:T(8,128)} %get-tuple-element.72), channel_id=1, source_target_pairs={{0,8},{4,12},{8,0},{12,4},{16,24},{20,28},{24,16},{28,20},{1,9},{5... | collective-permute-start | bytes 61448 | tf_op jit(solution)/shard_map/ppermute | solution.py:302
  19.2 3.6 %collective-permute-start.4 = (f32[104,128]{1,0:T(8,128)S(1)}, f32[104,128]{1,0:T(8,128)S(1)}, u32[]{:S(2)}, u32[]{:S(2)}) collective-permute-start(f32[104,128]{1,0:T(8,128)S(1)} %pad_maximum_fusion.1), channel_id=1, source_target_pairs={{0,4},{4,0},{8,12},{12,8},{16,20},{20,16},{24,28},{28,24},{1,5},{5... | collective-permute-start | bytes 159752 | tf_op jit(solution)/shard_map/ppermute | solution.py:302
  22.8 2.6 %collective-permute-start.5 = (f32[40,128]{1,0:T(8,128)S(1)}, f32[40,128]{1,0:T(8,128)S(1)}, u32[]{:S(2)}, u32[]{:S(2)}) collective-permute-start(f32[40,128]{1,0:T(8,128)S(1)} %slice_add_fusion), channel_id=1, source_target_pairs={{0,16},{4,20},{8,24},{12,28},{16,0},{20,4},{24,8},{28,12},{1,17},{... | collective-permute-start | bytes 61448 | tf_op jit(solution)/shard_map/ppermute | solution.py:302
  23.0 13.2 %collective-permute-start.7 = (f32[1,2,256,256]{3,2,1,0:T(8,128)}, f32[1,2,256,256]{3,2,1,0:T(8,128)}, u32[]{:S(2)}, u32[]{:S(2)}) collective-permute-start(f32[1,2,256,256]{3,2,1,0:T(8,128)} %get-tuple-element.81), channel_id=1, source_target_pairs={{0,8},{4,12},{8,0},{12,4},{16,24},{20,28},{24,16},{28,20},{1,9},{5... | collective-permute-start | bytes 1572872 | tf_op jit(solution)/shard_map/ppermute | solution.py:396
  27.0 6.5 %copy-start.17 = (s32[4]{0:T(128)S(1)}, s32[4]{0:T(128)}, u32[]{:S(2)}) copy-start(s32[4]{0:T(128)} %constant.57.clone) | copy-start | bytes 52
  27.0 10.4 %copy-start.10 = (f32[4,256,256]{2,1,0:T(8,128)S(1)}, f32[4,256,256]{2,1,0:T(8,128)}, u32[]{:S(2)}) copy-start(f32[4,256,256]{2,1,0:T(8,128)} %param.18) | copy-start | bytes 3145732
  33.2 13.8 %copy-start.4 = (f32[2,256,256]{2,1,0:T(8,128)}, f32[2,256,256]{2,1,0:T(8,128)S(1)}, u32[]{:S(2)}) copy-start(f32[2,256,256]{2,1,0:T(8,128)S(1)} %get-tuple-element.78.whole_source) | copy-start | bytes 1572868
  33.2 13.8 %copy-start.6 = (f32[2,256,256]{2,1,0:T(8,128)}, f32[2,256,256]{2,1,0:T(8,128)S(1)}, u32[]{:S(2)}) copy-start(f32[2,256,256]{2,1,0:T(8,128)S(1)} %get-tuple-element.76.whole_map) | copy-start | bytes 1572868
  33.2 12.1 %collective-permute-start.6 = (f32[2,256,256]{2,1,0:T(8,128)S(1)}, f32[2,256,256]{2,1,0:T(8,128)S(1)}, u32[]{:S(2)}, u32[]{:S(2)}) collective-permute-start(f32[2,256,256]{2,1,0:T(8,128)S(1)} %get-tuple-element.78.whole_source), channel_id=1, source_target_pairs={{0,1},{2,3},{1,0},{3,2},{4,5},{6,7},{5,4},{7,6},{8,9},{10,11},{9,8... | collective-permute-start | bytes 1572872 | tf_op jit(solution)/shard_map/ppermute | solution.py:471
  33.6 22.8 %collective-permute-start.10 = (f32[1,2,256,256]{3,2,1,0:T(8,128)}, f32[1,2,256,256]{3,2,1,0:T(8,128)}, u32[]{:S(2)}, u32[]{:S(2)}) collective-permute-start(f32[1,2,256,256]{3,2,1,0:T(8,128)} %collective-permute-done.2.refs_0_), channel_id=1, source_target_pairs={{0,16},{4,20},{8,24},{12,28},{16,0},{20,4},{24,8},{28,12},{1,17},{... | collective-permute-start | bytes 1572872 | tf_op jit(solution)/shard_map/ppermute | solution.py:401
  36.1 14.3 %collective-permute-start.9 = (f32[1,2,256,256]{3,2,1,0:T(8,128)}, f32[1,2,256,256]{3,2,1,0:T(8,128)}, u32[]{:S(2)}, u32[]{:S(2)}) collective-permute-start(f32[1,2,256,256]{3,2,1,0:T(8,128)} %get-tuple-element.89), channel_id=1, source_target_pairs={{0,8},{4,12},{8,0},{12,4},{16,24},{20,28},{24,16},{28,20},{1,9},{5... | collective-permute-start | bytes 1572872 | tf_op jit(solution)/shard_map/ppermute | solution.py:405
  37.8 19.0 %collective-permute-start.11 = (f32[1,2,256,256]{3,2,1,0:T(8,128)}, f32[1,2,256,256]{3,2,1,0:T(8,128)}, u32[]{:S(2)}, u32[]{:S(2)}) collective-permute-start(f32[1,2,256,256]{3,2,1,0:T(8,128)} %collective-permute-done.7.refs_1_), channel_id=1, source_target_pairs={{0,16},{4,20},{8,24},{12,28},{16,0},{20,4},{24,8},{28,12},{1,17},{... | collective-permute-start | bytes 1572872 | tf_op jit(solution)/shard_map/ppermute | solution.py:401
  47.0 13.3 %collective-permute-start.8 = (f32[2,256,256]{2,1,0:T(8,128)}, f32[2,256,256]{2,1,0:T(8,128)}, u32[]{:S(2)}, u32[]{:S(2)}) collective-permute-start(f32[2,256,256]{2,1,0:T(8,128)} %shard_map.115.before), channel_id=1, source_target_pairs={{1,2},{2,1},{5,6},{6,5},{9,10},{10,9},{13,14},{14,13},{17,18},{18,... | collective-permute-start | bytes 1572872 | tf_op jit(solution)/shard_map/ppermute | solution.py:471
  50.4 19.0 %collective-permute-start.13 = (f32[1,2,256,256]{3,2,1,0:T(8,128)}, f32[1,2,256,256]{3,2,1,0:T(8,128)S(1)}, u32[]{:S(2)}, u32[]{:S(2)}) collective-permute-start(f32[1,2,256,256]{3,2,1,0:T(8,128)} %get-tuple-element.95), channel_id=1, source_target_pairs={{0,8},{4,12},{8,0},{12,4},{16,24},{20,28},{24,16},{28,20},{1,9},{5... | collective-permute-start | bytes 1572872 | tf_op jit(solution)/shard_map/ppermute | solution.py:405
  53.3 7.0 %copy-start.5 = (f32[2,256,256]{2,1,0:T(8,128)S(1)}, f32[2,256,256]{2,1,0:T(8,128)}, u32[]{:S(2)}) copy-start(f32[2,256,256]{2,1,0:T(8,128)} %copy-done.4) | copy-start | bytes 1572868
  53.3 7.0 %copy-start.7 = (f32[2,256,256]{2,1,0:T(8,128)S(1)}, f32[2,256,256]{2,1,0:T(8,128)}, u32[]{:S(2)}) copy-start(f32[2,256,256]{2,1,0:T(8,128)} %copy-done.6) | copy-start | bytes 1572868
  56.1 10.6 %copy-start.3 = (f32[4,2,256,256]{3,2,1,0:T(8,128)S(1)}, f32[4,2,256,256]{3,2,1,0:T(8,128)}, u32[]{:S(2)}) copy-start(f32[4,2,256,256]{3,2,1,0:T(8,128)} %refs_2_.7) | copy-start | bytes 6291460
  56.1 15.8 %collective-permute-start.14 = (f32[1,2,256,256]{3,2,1,0:T(8,128)}, f32[1,2,256,256]{3,2,1,0:T(8,128)S(1)}, u32[]{:S(2)}, u32[]{:S(2)}) collective-permute-start(f32[1,2,256,256]{3,2,1,0:T(8,128)} %collective-permute-done.9.refs_0_), channel_id=1, source_target_pairs={{0,16},{4,20},{8,24},{12,28},{16,0},{20,4},{24,8},{28,12},{1,17},{... | collective-permute-start | bytes 1572872 | tf_op jit(solution)/shard_map/ppermute | solution.py:401
  62.4 10.2 %collective-permute-start.12 = (f32[2,256,256]{2,1,0:T(8,128)S(1)}, f32[2,256,256]{2,1,0:T(8,128)S(1)}, u32[]{:S(2)}, u32[]{:S(2)}) collective-permute-start(f32[2,256,256]{2,1,0:T(8,128)S(1)} %get-tuple-element.93), channel_id=1, source_target_pairs={{0,1},{2,3},{1,0},{3,2},{4,5},{6,7},{5,4},{7,6},{8,9},{10,11},{9,8... | collective-permute-start | bytes 1572872 | tf_op jit(solution)/shard_map/ppermute | solution.py:505
  62.6 29.7 %collective-permute-start.16 = (f32[2,256,256]{2,1,0:T(8,128)S(1)}, f32[2,256,256]{2,1,0:T(8,128)S(1)}, u32[]{:S(2)}, u32[]{:S(2)}) collective-permute-start(f32[2,256,256]{2,1,0:T(8,128)S(1)} %get-tuple-element.105), channel_id=1, source_target_pairs={{8,17},{9,18},{10,19},{12,21},{13,22},{14,23},{16,9},{17,10},{18,1... | collective-permute-start | bytes 1572872 | tf_op jit(solution)/shard_map/ppermute | solution.py:506
  72.7 9.1 %copy-start.14 = (f32[64,128]{1,0:T(8,128)S(1)}, f32[64,128]{1,0:T(8,128)}, u32[]{:S(2)}) copy-start(f32[64,128]{1,0:T(8,128)} %get-tuple-element.108) | copy-start | bytes 98308
  72.7 19.3 %copy-start.8 = (f32[16,4,128]{2,1,0:T(4,128)S(1)}, f32[16,4,128]{2,1,0:T(4,128)}, u32[]{:S(2)}) copy-start(f32[16,4,128]{2,1,0:T(4,128)} %param.12) | copy-start | bytes 98308
  72.8 19.3 %copy-start.9 = (f32[16,4,128]{2,1,0:T(4,128)S(1)}, f32[16,4,128]{2,1,0:T(4,128)}, u32[]{:S(2)}) copy-start(f32[16,4,128]{2,1,0:T(4,128)} %param.10) | copy-start | bytes 98308
  72.8 29.4 %collective-permute-start.15 = (f32[2,256,256]{2,1,0:T(8,128)S(1)}, f32[2,256,256]{2,1,0:T(8,128)S(1)}, u32[]{:S(2)}, u32[]{:S(2)}) collective-permute-start(f32[2,256,256]{2,1,0:T(8,128)S(1)} %broadcast_select_fusion.carried), channel_id=1, source_target_pairs={{0,8},{4,12},{8,0},{12,4},{16,24},{20,28},{24,16},{28,20},{1,9},{5... | collective-permute-start | bytes 1572872 | tf_op jit(solution)/shard_map/ppermute | solution.py:513
  74.0 21.2 %collective-permute-start.18 = (f32[1,2,256,256]{3,2,1,0:T(8,128)S(1)}, f32[1,2,256,256]{3,2,1,0:T(8,128)S(1)}, u32[]{:S(2)}, u32[]{:S(2)}) collective-permute-start(f32[1,2,256,256]{3,2,1,0:T(8,128)S(1)} %collective-permute-done.13.refs_1_), channel_id=1, source_target_pairs={{0,16},{4,20},{8,24},{12,28},{16,0},{20,4},{24,8},{28,12},{1,17},{... | collective-permute-start | bytes 1572872 | tf_op jit(solution)/shard_map/ppermute | solution.py:401
  81.8 12.0 %collective-permute-start.17 = (f32[64,128]{1,0:T(8,128)S(1)}, f32[64,128]{1,0:T(8,128)S(1)}, u32[]{:S(2)}, u32[]{:S(2)}) collective-permute-start(f32[64,128]{1,0:T(8,128)S(1)} %copy-done.14), channel_id=1, source_target_pairs={{4,8},{12,16},{20,24},{8,4},{16,12},{24,20},{5,9},{13,17},{21,25},... | collective-permute-start | bytes 98312 | tf_op jit(solution)/shard_map/ppermute | solution.py:534
  104.9 6.7 %collective-permute-start.19 = (f32[2,2,256,256]{3,2,1,0:T(8,128)S(1)}, f32[2,2,256,256]{3,2,1,0:T(8,128)S(1)}, u32[]{:S(2)}, u32[]{:S(2)}) collective-permute-start(f32[2,2,256,256]{3,2,1,0:T(8,128)S(1)} %get-tuple-element.129), channel_id=1, source_target_pairs={{0,4},{4,0},{8,12},{12,8},{16,20},{20,16},{24,28},{28,24},{1,5},{5... | collective-permute-start | bytes 3145736 | tf_op jit(solution)/shard_map/ppermute | solution.py:580
  111.7 2.7 %collective-permute-start.20 = (f32[2,2,256,256]{3,2,1,0:T(8,128)S(1)}, f32[2,2,256,256]{3,2,1,0:T(8,128)S(1)}, u32[]{:S(2)}, u32[]{:S(2)}) collective-permute-start(f32[2,2,256,256]{3,2,1,0:T(8,128)S(1)} %get-tuple-element.137), channel_id=1, source_target_pairs={{0,4},{4,0},{8,12},{12,8},{16,20},{20,16},{24,28},{28,24},{1,5},{5... | collective-permute-start | bytes 3145736 | tf_op jit(solution)/shard_map/ppermute | solution.py:580
  (7 other events, 31.8 us)

commit v15 on v9

--- a/solution.py
+++ b/solution.py
@@ -78,7 +78,7 @@
 
 
 def gather_kernel(rows, peers, mine, field, perm, charge, before, after, owner, free, *refs):
-    out, ends, *parts, held, here, gone = refs
+    out, *parts, held, here, gone = refs
     loads, stores = [], []
     for index in range(len(parts)):
         slab = free.at[index + 1 : index + 2]
@@ -155,12 +155,10 @@
             for piece in range(orbitals // depth):
                 row = sums_row(kind, slab, count, orbitals // depth) + piece
                 out[row : row + 1, :] = value[:, piece * depth : (piece + 1) * depth]
-    start = 0
+    start = kinds * count * (orbitals // depth)
     for array in (field, perm):
         for end in (0, rows - 1):
-            ends[start : start + total // rows, :] = array[
-                pl.ds(end, total // rows, stride=rows), :
-            ]
+            out[start : start + total // rows, :] = array[pl.ds(end, total // rows, stride=rows), :]
             start += total // rows
     for store in stores:
         store.wait()
@@ -290,21 +288,22 @@
     )
 
 
-def exchanged(sums, ends, early):
-    peers = lax.axis_size("energy")
+def exchanged(payload, head, early):
+    peers, mine = lax.axis_size("energy"), lax.axis_index("energy")
     assert peers >= 4 and peers & (peers - 1) == 0
-    masks = [2, 1] + [1 << k for k in range(2, peers.bit_length() - 1)]
-    rows, twin_ends = sums.shape[0], None
-    first = None
-    sums, early = lax.optimization_barrier((sums, early))
+    masks = [(1 << k) - 1 for k in range(2, peers.bit_length())] + [1]
+    rest = payload[head:]
+    before = after = jnp.zeros_like(rest)
+    is_head = lax.broadcasted_iota(jnp.int32, payload.shape, 0) < head
+    payload, early = lax.optimization_barrier((payload, early))
     for mask in masks:
-        given = jnp.concatenate([sums, ends]) if mask == 1 else sums
-        arrived = lax.ppermute(given, "energy", [(e, e ^ mask) for e in range(peers)])
-        if mask == 1:
-            twin_ends = arrived[rows:]
-        sums = sums + arrived[:rows]
-        first = sums if first is None else first
-    return sums, twin_ends, first, early
+        arrived = lax.ppermute(payload, "energy", [(e, e ^ mask) for e in range(peers)])
+        before = jnp.where((mine ^ mask) == mine - 1, arrived[head:], before)
+        after = jnp.where((mine ^ mask) == mine + 1, arrived[head:], after)
+        payload = jnp.where(is_head, payload + arrived, payload)
+        if mask != 1:
+            crossed = payload
+    return payload, before, after, crossed, early
 
 
 def per_device(
@@ -365,13 +364,13 @@
 
     cells, rows, depth = charge.shape
     far, near = pl.BlockSpec(memory_space=pl.ANY), pl.BlockSpec(memory_space=pltpu.VMEM)
-    sums, ends, *cuts = call(
+    head = 5 * count * (width // depth)
+    payload, *cuts = call(
         functools.partial(gather_kernel, rows, energies),
         56,
         1,
         (
-            shape(5 * count * (width // depth), depth),
-            shape(4 * cells, depth),
+            shape(head + 4 * cells, depth),
             *[one_slab] * (count - 1),
         ),
         jnp.reshape(mine, (1,)),
@@ -381,7 +380,7 @@
         owner_cell,
         free,
         in_specs=[pl.BlockSpec(memory_space=pltpu.SMEM)] + [near] * 6 + [far],
-        out_specs=(near, near, *[far] * (count - 1)),
+        out_specs=(near, *[far] * (count - 1)),
         scratch_shapes=[
             pltpu.VMEM((count - 1, 2, width, width), jnp.float32),
             pltpu.SemaphoreType.DMA((count - 1,)),
@@ -389,7 +388,7 @@
         ],
     )
     cuts = [first_cut, *cuts]
-    sums, twin_ends, crossed, arrived = exchanged(sums, ends, free_first[0])
+    sums, ends_before, ends_after, crossed, arrived = exchanged(payload, head, free_first[0])
 
     crossed, cuts[1] = lax.optimization_barrier((crossed, cuts[1]))
     sums, arrived = lax.optimization_barrier((sums, arrived))
@@ -415,7 +414,15 @@
         sums,
     )
 
-    whole_source, mode_tiles = lax.optimization_barrier((whole_source, mode_tiles))
+    whole_source, mode_tiles, field, perm, ends_before, ends_after = lax.optimization_barrier(
+        (whole_source, mode_tiles, potential_old, permittivity, ends_before, ends_after)
+    )
+    ends_before = ends_before.reshape(2, 2, cells, 1, depth)
+    ends_after = ends_after.reshape(2, 2, cells, 1, depth)
+    edge = jnp.zeros((2, cells, rows, 1), jnp.float32)
+    halos = ((wire_before, wire_after), (ends_before[:, 1], ends_after[:, 0]), (edge, edge))
+    potential_new = relaxed(field, perm, charge, halos)
+
     odd = mine % 2
     distance = jnp.array([2, 2, 1, 1], jnp.int32)
     lowered = jnp.stack([turned, 1 - turned, 1 - odd, odd]).astype(jnp.float32)
@@ -472,8 +479,8 @@
         if hop == 1:
             sent_on(1)
             sent_after(2)
-            arrived, weights, free_first[1] = lax.optimization_barrier(
-                (arrived, weights, free_first[1])
+            arrived, weights, free_first[1], potential_new = lax.optimization_barrier(
+                (arrived, weights, free_first[1], potential_new)
             )
         if hop == 2:
             sent_on(2)
@@ -525,26 +532,16 @@
         in_specs=[block, block, pl.BlockSpec(sums.shape, lambda s: (0, 0)), one_state],
         out_specs=(block, one_state),
     )
-    carried_second, greens, free_second[3], ends, field, perm = lax.optimization_barrier(
-        (carried_second, greens, free_second[3], ends, potential_old, permittivity)
-    )
-
-    beyond = [(e, e + 1) for e in range(1, energies - 1, 2)]
-    other_ends = lax.ppermute(ends, "energy", beyond + [(b, a) for a, b in beyond])
-    ends_before = jnp.where(odd == 1, twin_ends, other_ends).reshape(2, 2, cells, 1, depth)
-    ends_after = jnp.where(odd == 1, other_ends, twin_ends).reshape(2, 2, cells, 1, depth)
-    edge = jnp.zeros((2, cells, rows, 1), jnp.float32)
-    halos = ((wire_before, wire_after), (ends_before[:, 1], ends_after[:, 0]), (edge, edge))
-    potential_new = relaxed(field, perm, charge, halos)
+    carried_second, greens, free_second[3] = lax.optimization_barrier(
+        (carried_second, greens, free_second[3])
+    )
 
     beside_second[1] = beside(1, free_second[2:])
     greens_second = []
     for part in beside_second:
         made, carried_second = greens_of(16, *part, carried_second)
         greens_second.append(made)
-    carried_first, greens_second, potential_new = lax.optimization_barrier(
-        (carried_first, greens_second, potential_new)
-    )
+    carried_first, greens_second = lax.optimization_barrier((carried_first, greens_second))
 
     outputs = []
     for index, part in enumerate(beside_first):

time: 117 us -> 121 us (1.034); the launches traced: 115 us -> 121 us
  local copies, waits for them, and re-layouts: 4.62 us -> 10.3 us
  waiting for transfers between devices: 31.9 us -> 37.4 us
  starting transfers between devices: 29.9 us -> 24.8 us
    unnamed x36 -> x50, local copies, waits for them, and re-layouts: 3.25 us -> 8.93 us
    ppermute x4 -> x3, starting transfers between devices: 8.6 us -> 4.07 us  [exchanged(): lax.ppermute(payload, 'energy', [(e, e ^ mask) for e in range(peers)])]
    ppermute x4 -> x3, waiting for transfers between devices: 3.72 us -> 6.88 us  [exchanged(): lax.ppermute(payload, 'energy', [(e, e ^ mask) for e in range(peers)])]
    ppermute x4, waiting for transfers between devices: 7.46 us -> 10.5 us  [sent_on(): free_second.append(lax.ppermute(given, 'energy', relay_pairs))]
    ppermute x1, waiting for transfers between devices: 3.26 us -> 1.26 us  [per_device(): lax.ppermute(onward, ('energy', 'slab'), both(second_pairs))]
    ppermute x2, starting transfers between devices: 2.47 us -> 1.18 us  [sent_after(): free_first.append(lax.ppermute(cut, 'energy', first_pairs))]
    pallas_call x13, Pallas kernels: 41.5 us -> 40.3 us  [call(): pl.pallas_call(kernel, out_shape=out_shapes, cost_estimate=cost, compiler...]
  transfers between devices with their start and end apart: 21 -> 20, of which waited for: 13 -> 12; matrix products, arithmetic and copies ran while one was open for 3% -> 3% of each run, Pallas kernels for 34% -> 31%
where the time goes in v15:
time: 121 us
  Pallas kernels  40.3 us (33%)
  waiting for transfers between devices  37.4 us (31%)
  starting transfers between devices  24.8 us (20%)
  local copies, waits for them, and re-layouts  10.3 us (9%)
  other arithmetic  6.77 us (6%)
    pallas_call x13, Pallas kernels, call(): pl.pallas_call(kernel, out_shape=out_shapes, cost_estimate=cost, compiler...  40.3 us
    ppermute x4, waiting for transfers between devices, sent_on(): free_second.append(lax.ppermute(given, 'energy', relay_pairs))  10.5 us
    ppermute x2, waiting for transfers between devices, per_device(): arrived = lax.ppermute(leaving, 'slab', swaps((hop - 1) % 2))  10.5 us
    unnamed x50, local copies, waits for them, and re-layouts  8.93 us
    ppermute x3, waiting for transfers between devices, exchanged(): lax.ppermute(payload, 'energy', [(e, e ^ mask) for e in range(peers)])  6.88 us
    ppermute x1, starting transfers between devices, per_device(): lax.ppermute(onward, ('energy', 'slab'), both(second_pairs))  4.35 us
    ppermute x1, starting transfers between devices, per_device(): crossed = lax.ppermute(jnp.where(even, lower, upper), 'slab', swaps(1))  4.32 us
    ppermute x3, starting transfers between devices, exchanged(): lax.ppermute(payload, 'energy', [(e, e ^ mask) for e in range(peers)])  4.07 us
  transfers between devices with their start and end apart: 20, of which 12 were waited for; matrix products, arithmetic and copies ran while one was open for 3% of the time, Pallas kernels for 31%

profile of v15, /device:TPU:13, one launch (start us, length us, event | category | flops | bytes accessed | tf_op | source)
XLA Modules:
  0.0 120.6 jit_solution(15130664148889400189)
XLA Ops:
  0.7 1.2 %slice_bitcast_fusion = f32[1,2,256,256]{3,2,1,0:T(8,128)S(1)} fusion(f32[1,4,2,256,256]{4,3,2,1,0:T(8,128)} %param.14), kind=kLoop, calls=%fused_computation.2 | loop fusion | bytes 1048576 | tf_op jit(solution)/shard_map/slice | solution.py:345
  1.9 1.3 %collective-permute-start.2 = (f32[1,2,256,256]{3,2,1,0:T(8,128)S(1)}, f32[1,2,256,256]{3,2,1,0:T(8,128)}, u32[]{:S(2)}, u32[]{:S(2)}) collective-permute-start(f32[1,2,256,256]{3,2,1,0:T(8,128)S(1)} %slice_bitcast_fusion), channel_id=1, source_target_pairs={{0,8},{4,12},{8,0},{12,4},{16,24},{20,28},{24,16},{28,20},{1,9},{5... | collective-permute-start | bytes 1572872 | tf_op jit(solution)/shard_map/ppermute | solution.py:346
  4.2 4.3 %collective-permute-start = (f32[2,1,4,128]{3,2,0,1:T(4,128)S(1)}, f32[2,1,4,128]{3,2,0,1:T(4,128)S(1)}, u32[]{:S(2)}, u32[]{:S(2)}) collective-permute-start(f32[2,1,4,128]{3,2,0,1:T(4,128)S(1)} %get-tuple-element.135), channel_id=1, source_target_pairs={{1,2},{2,1},{5,6},{6,5},{9,10},{10,9},{13,14},{14,13},{17,18},{18,... | collective-permute-start | bytes 12296 | tf_op jit(solution)/shard_map/ppermute | solution.py:361
  8.6 1.3 %collective-permute-done = f32[2,1,4,128]{3,2,0,1:T(4,128)S(1)} collective-permute-done((f32[2,1,4,128]{3,2,0,1:T(4,128)S(1)}, f32[2,1,4,128]{3,2,0,1:T(4,128)S(1)}, u32[]{:S(2)}, u32[]{:S(2)}) %collective-permute-start) | collective-permute-done | bytes 4128 | tf_op jit(solution)/shard_map/ppermute | solution.py:361
  10.5 3.7 %shard_map.113 = (f32[104,128]{1,0:T(8,128)}, f32[1,2,256,256]{3,2,1,0:T(8,128)}, f32[1,2,256,256]{3,2,1,0:T(8,128)}, f32[1,2,256,256]{3,2,1,0:T(8,128)}) custom-call(s32[1]{0:T(128)} %bitcast.1.mine, f32[64,128]{1,0:T(8,128)} %bitcast.48, f32[64,128]{1,0:T(8,128)} %bitcast.46, f32[64,128]{1,0:T(8,128)} %bitcast.49, f32[2,4,128]{2,1,0:T(4,128)} %bitcast.54, ...), custom_call_target="tpu_custom_call" | custom-call | flops 301989888 | bytes 3833860 | tf_op jit(solution)/shard_map/pallas_call | solution.py:67
  14.9 2.6 %collective-permute-start.3 = (f32[104,128]{1,0:T(8,128)}, f32[104,128]{1,0:T(8,128)S(1)}, u32[]{:S(2)}, u32[]{:S(2)}) collective-permute-start(f32[104,128]{1,0:T(8,128)} %get-tuple-element.69), channel_id=1, source_target_pairs={{0,12},{4,8},{8,4},{12,0},{16,28},{20,24},{24,20},{28,16},{1,13},{... | collective-permute-start | bytes 159752 | tf_op jit(solution)/shard_map/ppermute | solution.py:300
  17.6 2.7 %collective-permute-done.3 = f32[104,128]{1,0:T(8,128)S(1)} collective-permute-done((f32[104,128]{1,0:T(8,128)}, f32[104,128]{1,0:T(8,128)S(1)}, u32[]{:S(2)}, u32[]{:S(2)}) %collective-permute-start.3) | collective-permute-done | bytes 53280 | tf_op jit(solution)/shard_map/ppermute | solution.py:300
  22.3 3.7 %collective-permute-done.4 = f32[104,128]{1,0:T(8,128)S(1)} collective-permute-done((f32[104,128]{1,0:T(8,128)S(1)}, f32[104,128]{1,0:T(8,128)S(1)}, u32[]{:S(2)}, u32[]{:S(2)}) %collective-permute-start.4) | collective-permute-done | bytes 53280 | tf_op jit(solution)/shard_map/ppermute | solution.py:300
  27.6 1.6 %copy-done.7 = f32[4,2,256,256]{3,2,1,0:T(8,128)S(1)} copy-done((f32[4,2,256,256]{3,2,1,0:T(8,128)S(1)}, f32[4,2,256,256]{3,2,1,0:T(8,128)}, u32[]{:S(2)}) %copy-start.7) | copy-done | bytes 2097176
  29.2 6.2 %shard_map.114 = (f32[2,256,256]{2,1,0:T(8,128)S(1)}, f32[2,256,256]{2,1,0:T(8,128)S(1)}) custom-call(f32[4,2,256,256]{3,2,1,0:T(8,128)S(1)} %bitcast.43, f32[4,2,256,256]{3,2,1,0:T(8,128)S(1)} %copy-done.7, f32[104,128]{1,0:T(8,128)S(1)} %add_select_fusion.sums.refs_3_), custom_call_target="tpu_custom_call" | custom-call | flops 5133828096 | bytes 5296128 | tf_op jit(solution)/shard_map/pallas_call | solution.py:67
  36.6 3.6 %collective-permute-done.7.refs_1_ = f32[1,2,256,256]{3,2,1,0:T(8,128)S(1)} collective-permute-done((f32[1,2,256,256]{3,2,1,0:T(8,128)}, f32[1,2,256,256]{3,2,1,0:T(8,128)S(1)}, u32[]{:S(2)}, u32[]{:S(2)}) %collective-permute-start.7) | collective-permute-done | bytes 524320 | tf_op jit(solution)/shard_map/ppermute | solution.py:395
  41.7 7.1 %collective-permute-done.6.carried = f32[2,256,256]{2,1,0:T(8,128)S(1)} collective-permute-done((f32[2,256,256]{2,1,0:T(8,128)S(1)}, f32[2,256,256]{2,1,0:T(8,128)S(1)}, u32[]{:S(2)}, u32[]{:S(2)}) %collective-permute-start.6) | collective-permute-done | bytes 524320 | tf_op jit(solution)/shard_map/ppermute | solution.py:478
  49.7 3.4 %collective-permute-start.8 = (f32[2,256,256]{2,1,0:T(8,128)S(1)}, f32[2,256,256]{2,1,0:T(8,128)S(1)}, u32[]{:S(2)}, u32[]{:S(2)}) collective-permute-start(f32[2,256,256]{2,1,0:T(8,128)S(1)} %shard_map.115.before), channel_id=1, source_target_pairs={{1,2},{2,1},{5,6},{6,5},{9,10},{10,9},{13,14},{14,13},{17,18},{18,... | collective-permute-start | bytes 1572872 | tf_op jit(solution)/shard_map/ppermute | solution.py:478
  53.8 2.5 %shard_map.116 = (f32[2,2,256,256]{3,2,1,0:T(8,128)S(1)}, f32[2,2,256,256]{3,2,1,0:T(8,128)S(1)}) custom-call(f32[1,2,256,256]{3,2,1,0:T(8,128)} %collective-permute-done.2.refs_0_, f32[1,2,256,256]{3,2,1,0:T(8,128)S(1)} %collective-permute-done.7.refs_1_, f32[4,2,256,256]{3,2,1,0:T(8,128)S(1)} %copy-done.7, f32[104,128]{1,0:T(8,128)S(1)} %add_select_fusion.sums.refs_3_), custom_call_target="tpu_custom_call" | custom-call | flops 1207959552 | bytes 5296128 | tf_op jit(solution)/shard_map/pallas_call | solution.py:67
  58.3 1.2 %collective-permute-start.14 = (f32[1,2,256,256]{3,2,1,0:T(8,128)}, f32[1,2,256,256]{3,2,1,0:T(8,128)}, u32[]{:S(2)}, u32[]{:S(2)}) collective-permute-start(f32[1,2,256,256]{3,2,1,0:T(8,128)} %collective-permute-done.9.refs_0_), channel_id=1, source_target_pairs={{0,16},{4,20},{8,24},{12,28},{16,0},{20,4},{24,8},{28,12},{1,17},{... | collective-permute-start | bytes 1572872 | tf_op jit(solution)/shard_map/ppermute | solution.py:400
  60.3 3.4 %collective-permute-done.8.carried = f32[2,256,256]{2,1,0:T(8,128)S(1)} collective-permute-done((f32[2,256,256]{2,1,0:T(8,128)S(1)}, f32[2,256,256]{2,1,0:T(8,128)S(1)}, u32[]{:S(2)}, u32[]{:S(2)}) %collective-permute-start.8) | collective-permute-done | bytes 524320 | tf_op jit(solution)/shard_map/ppermute | solution.py:478
  63.7 1.7 %shard_map.117 = (f32[2,256,256]{2,1,0:T(8,128)}, f32[2,256,256]{2,1,0:T(8,128)S(1)}) custom-call(s32[1]{0:T(128)} %bitcast.30.odd, f32[2,256,256]{2,1,0:T(8,128)S(1)} %get-tuple-element.84.whole_map, f32[2,256,256]{2,1,0:T(8,128)S(1)} %get-tuple-element.73.whole_source, f32[2,256,256]{2,1,0:T(8,128)S(1)} %collective-permute-done.8.carried, ...), custom_call_target="tpu_custom_call" | custom-call | flops 603979776 | bytes 3145732 | tf_op jit(solution)/shard_map/pallas_call | solution.py:67
  67.1 4.4 %collective-permute-start.16 = (f32[2,256,256]{2,1,0:T(8,128)}, f32[2,256,256]{2,1,0:T(8,128)S(1)}, u32[]{:S(2)}, u32[]{:S(2)}) collective-permute-start(f32[2,256,256]{2,1,0:T(8,128)} %copy-done.14), channel_id=1, source_target_pairs={{8,17},{9,18},{10,19},{12,21},{13,22},{14,23},{16,9},{17,10},{18,1... | collective-permute-start | bytes 1572872 | tf_op jit(solution)/shard_map/ppermute | solution.py:513
  71.5 1.6 %copy-done.8 = f32[4,2,256,256]{3,2,1,0:T(8,128)S(1)} copy-done((f32[4,2,256,256]{3,2,1,0:T(8,128)S(1)}, f32[4,2,256,256]{3,2,1,0:T(8,128)}, u32[]{:S(2)}) %copy-start.8) | copy-done | bytes 2097176
  75.2 1.6 %shard_map.119 = (f32[2,2,256,256]{3,2,1,0:T(8,128)S(1)}, f32[2,2,256,256]{3,2,1,0:T(8,128)S(1)}) custom-call(f32[1,2,256,256]{3,2,1,0:T(8,128)S(1)} %copy-done.11, f32[1,2,256,256]{3,2,1,0:T(8,128)S(1)} %copy-done.13, f32[4,2,256,256]{3,2,1,0:T(8,128)S(1)} %copy-done.8, f32[104,128]{1,0:T(8,128)S(1)} %add_select_fusion.sums.refs_3_), custom_call_target="tpu_custom_call" | custom-call | flops 1207959552 | bytes 5296128 | tf_op jit(solution)/shard_map/pallas_call | solution.py:67
  76.9 2.8 %shard_map.118 = (f32[2,2,256,256]{3,2,1,0:T(8,128)S(1)}, f32[2,2,256,256]{3,2,1,0:T(8,128)S(1)}) custom-call(f32[1,2,256,256]{3,2,1,0:T(8,128)} %collective-permute-done.9.refs_0_, f32[1,2,256,256]{3,2,1,0:T(8,128)} %collective-permute-done.13.refs_1_, f32[4,2,256,256]{3,2,1,0:T(8,128)S(1)} %copy-done.9, f32[104,128]{1,0:T(8,128)S(1)} %add_select_fusion.sums.refs_3_), custom_call_target="tpu_custom_call" | custom-call | flops 1207959552 | bytes 5296128 | tf_op jit(solution)/shard_map/pallas_call | solution.py:67
  82.0 7.6 %shard_map.120 = (f32[4,2,256,256]{3,2,1,0:T(8,128)S(1)}, f32[2,256,256]{2,1,0:T(8,128)}) custom-call(f32[4,2,256,256]{3,2,1,0:T(8,128)S(1)} %bitcast.44, f32[4,2,256,256]{3,2,1,0:T(8,128)S(1)} %copy-done.9, f32[104,128]{1,0:T(8,128)S(1)} %add_select_fusion.sums.refs_3_, f32[2,256,256]{2,1,0:T(8,128)S(1)} %broadcast_select_fusion.carried), custom_call_target="tpu_custom_call" | custom-call | flops 4831838208 | bytes 7393280 | tf_op jit(solution)/shard_map/pallas_call | solution.py:67
  89.6 1.3 %collective-permute-done.16.carried = f32[2,256,256]{2,1,0:T(8,128)S(1)} collective-permute-done((f32[2,256,256]{2,1,0:T(8,128)}, f32[2,256,256]{2,1,0:T(8,128)S(1)}, u32[]{:S(2)}, u32[]{:S(2)}) %collective-permute-start.16) | collective-permute-done | bytes 524320 | tf_op jit(solution)/shard_map/ppermute | solution.py:513
  90.8 9.7 %collective-permute-done.17.refs_1_ = f32[1,2,256,256]{3,2,1,0:T(8,128)S(1)} collective-permute-done((f32[1,2,256,256]{3,2,1,0:T(8,128)}, f32[1,2,256,256]{3,2,1,0:T(8,128)S(1)}, u32[]{:S(2)}, u32[]{:S(2)}) %collective-permute-start.17) | collective-permute-done | bytes 524320 | tf_op jit(solution)/shard_map/ppermute | solution.py:400
  100.5 2.6 %shard_map.122 = (f32[2,2,256,256]{3,2,1,0:T(8,128)S(1)}, f32[2,2,256,256]{3,2,1,0:T(8,128)S(1)}) custom-call(f32[1,2,256,256]{3,2,1,0:T(8,128)} %collective-permute-done.14.refs_0_, f32[1,2,256,256]{3,2,1,0:T(8,128)S(1)} %collective-permute-done.17.refs_1_, f32[4,2,256,256]{3,2,1,0:T(8,128)S(1)} %copy-done.9, f32[104,128]{1,0:T(8,128)S(1)} %add_select_fusion.sums.refs_3_), custom_call_target="tpu_custom_call" | custom-call | flops 1207959552 | bytes 5296128 | tf_op jit(solution)/shard_map/pallas_call | solution.py:67
  103.1 1.9 %shard_map.121 = (f32[2,2,256,256]{3,2,1,0:T(8,128)S(1)}, f32[2,256,256]{2,1,0:T(8,128)S(1)}) custom-call(f32[2,2,256,256]{3,2,1,0:T(8,128)S(1)} %get-tuple-element.106.link, f32[2,2,256,256]{3,2,1,0:T(8,128)S(1)} %get-tuple-element.107.source, f32[2,256,256]{2,1,0:T(8,128)S(1)} %collective-permute-done.16.carried), custom_call_target="tpu_custom_call" | custom-call | flops 1207959552 | bytes 4194304 | tf_op jit(solution)/shard_map/pallas_call | solution.py:67
  105.1 2.7 %shard_map.123 = (f32[2,2,256,256]{3,2,1,0:T(8,128)S(1)}, f32[2,256,256]{2,1,0:T(8,128)}) custom-call(f32[2,2,256,256]{3,2,1,0:T(8,128)S(1)} %get-tuple-element.114.link, f32[2,2,256,256]{3,2,1,0:T(8,128)S(1)} %get-tuple-element.115.source, f32[2,256,256]{2,1,0:T(8,128)S(1)} %get-tuple-element.116.carried), custom_call_target="tpu_custom_call" | custom-call | flops 1207959552 | bytes 4194304 | tf_op jit(solution)/shard_map/pallas_call | solution.py:67
  107.8 2.7 %shard_map.124 = (f32[2,2,256,256]{3,2,1,0:T(8,128)S(1)}, f32[2,2,256,256]{3,2,1,0:T(8,128)S(1)}, f32[2,256,256]{2,1,0:T(8,128)S(1)}) custom-call(s32[2]{0:T(128)S(1)} %pad_add_fusion.pick, f32[2,2,256,256]{3,2,1,0:T(8,128)S(1)} %copy-done.2, f32[2,2,256,256]{3,2,1,0:T(8,128)S(1)} %copy-done.4, f32[2,256,256]{2,1,0:T(8,128)S(1)} %collective-permute-done.15.carried, ...), custom_call_target="tpu_custom_call" | custom-call | flops 1207959552 | bytes 9437192 | tf_op jit(solution)/shard_map/pallas_call | solution.py:67
  110.5 2.0 %collective-permute-start.18 = (f32[2,2,256,256]{3,2,1,0:T(8,128)S(1)}, f32[2,2,256,256]{3,2,1,0:T(8,128)S(1)}, u32[]{:S(2)}, u32[]{:S(2)}) collective-permute-start(f32[2,2,256,256]{3,2,1,0:T(8,128)S(1)} %get-tuple-element.123), channel_id=1, source_target_pairs={{0,4},{4,0},{8,12},{12,8},{16,20},{20,16},{24,28},{28,24},{1,5},{5... | collective-permute-start | bytes 3145736 | tf_op jit(solution)/shard_map/ppermute | solution.py:573
  112.6 3.5 %shard_map.125 = (f32[2,2,256,256]{3,2,1,0:T(8,128)S(1)}, f32[2,2,256,256]{3,2,1,0:T(8,128)S(1)}, f32[2,256,256]{2,1,0:T(8,128)}) custom-call(s32[2]{0:T(128)S(1)} %pad_add_fusion.pick, f32[2,2,256,256]{3,2,1,0:T(8,128)S(1)} %get-tuple-element.124.link, f32[2,2,256,256]{3,2,1,0:T(8,128)S(1)} %get-tuple-element.125.source, ...), custom_call_target="tpu_custom_call" | custom-call | flops 1207959552 | bytes 9437192 | tf_op jit(solution)/shard_map/pallas_call | solution.py:67
  116.3 2.6 %collective-permute-done.19 = f32[2,2,256,256]{3,2,1,0:T(8,128)S(1)} collective-permute-done((f32[2,2,256,256]{3,2,1,0:T(8,128)S(1)}, f32[2,2,256,256]{3,2,1,0:T(8,128)S(1)}, u32[]{:S(2)}, u32[]{:S(2)}) %collective-permute-start.19) | collective-permute-done | bytes 1048608 | tf_op jit(solution)/shard_map/ppermute | solution.py:573
  119.1 1.5 %maximum_bitcast_fusion = f32[1,4,2,256,256]{4,3,2,1,0:T(8,128)} fusion(f32[2,2,256,256]{3,2,1,0:T(8,128)S(1)} %add.138, f32[2,2,256,256]{3,2,1,0:T(8,128)S(1)} %add.137), kind=kLoop, calls=%fused_computation.1 | loop fusion | flops 524288 | bytes 4194304 | tf_op jit(solution)/shard_map/broadcast_in_dim | solution.py:574
  (95 shorter events, 19.5 us)
Async XLA Ops:
  0.6 21.6 %copy-start.23 = (s32[4]{0:T(128)S(1)}, s32[4]{0:T(128)}, u32[]{:S(2)}) copy-start(s32[4]{0:T(128)} %constant.65.clone) | copy-start | bytes 52
  0.6 26.9 %copy-start = (f32[1,4,2,256,256]{4,3,2,1,0:T(8,128)S(1)}, f32[1,4,2,256,256]{4,3,2,1,0:T(8,128)}, u32[]{:S(2)}) copy-start(f32[1,4,2,256,256]{4,3,2,1,0:T(8,128)} %param.14) | copy-start | bytes 6291460
  0.7 21.5 %copy-start.21 = (f32[4]{0:T(128)S(1)}, f32[4]{0:T(128)}, u32[]{:S(2)}) copy-start(f32[4]{0:T(128)} %param.17) | copy-start | bytes 52
  0.7 21.5 %copy-start.22 = (s32[4]{0:T(128)S(1)}, s32[4]{0:T(128)}, u32[]{:S(2)}) copy-start(s32[4]{0:T(128)} %param.16) | copy-start | bytes 52
  1.9 13.0 %collective-permute-start.2 = (f32[1,2,256,256]{3,2,1,0:T(8,128)S(1)}, f32[1,2,256,256]{3,2,1,0:T(8,128)}, u32[]{:S(2)}, u32[]{:S(2)}) collective-permute-start(f32[1,2,256,256]{3,2,1,0:T(8,128)S(1)} %slice_bitcast_fusion), channel_id=1, source_target_pairs={{0,8},{4,12},{8,0},{12,4},{16,24},{20,28},{24,16},{28,20},{1,9},{5... | collective-permute-start | bytes 1572872 | tf_op jit(solution)/shard_map/ppermute | solution.py:346
  4.0 4.6 %collective-permute-start.1 = (f32[2,1,4,128]{3,2,0,1:T(4,128)S(1)}, f32[2,1,4,128]{3,2,0,1:T(4,128)S(1)}, u32[]{:S(2)}, u32[]{:S(2)}) collective-permute-start(f32[2,1,4,128]{3,2,0,1:T(4,128)S(1)} %get-tuple-element.134), channel_id=1, source_target_pairs={{0,1},{2,3},{1,0},{3,2},{4,5},{6,7},{5,4},{7,6},{8,9},{10,11},{9,8... | collective-permute-start | bytes 12296 | tf_op jit(solution)/shard_map/ppermute | solution.py:360
  4.2 5.7 %collective-permute-start = (f32[2,1,4,128]{3,2,0,1:T(4,128)S(1)}, f32[2,1,4,128]{3,2,0,1:T(4,128)S(1)}, u32[]{:S(2)}, u32[]{:S(2)}) collective-permute-start(f32[2,1,4,128]{3,2,0,1:T(4,128)S(1)} %get-tuple-element.135), channel_id=1, source_target_pairs={{1,2},{2,1},{5,6},{6,5},{9,10},{10,9},{13,14},{14,13},{17,18},{18,... | collective-permute-start | bytes 12296 | tf_op jit(solution)/shard_map/ppermute | solution.py:361
  10.5 16.0 %copy-start.19 = (f32[1,1,8,128]{3,2,0,1:T(8,128)S(1)}, f32[1,1,8,128]{3,2,0,1:T(8,128)}, u32[]{:S(2)}) copy-start(f32[1,1,8,128]{3,2,0,1:T(8,128)} %get-tuple-element.166) | copy-start | bytes 12292
  10.5 16.0 %copy-start.20 = (f32[1,1,8,128]{3,2,0,1:T(8,128)S(1)}, f32[1,1,8,128]{3,2,0,1:T(8,128)}, u32[]{:S(2)}) copy-start(f32[1,1,8,128]{3,2,0,1:T(8,128)} %get-tuple-element.167) | copy-start | bytes 12292
  14.9 5.4 %collective-permute-start.3 = (f32[104,128]{1,0:T(8,128)}, f32[104,128]{1,0:T(8,128)S(1)}, u32[]{:S(2)}, u32[]{:S(2)}) collective-permute-start(f32[104,128]{1,0:T(8,128)} %get-tuple-element.69), channel_id=1, source_target_pairs={{0,12},{4,8},{8,4},{12,0},{16,28},{20,24},{24,20},{28,16},{1,13},{... | collective-permute-start | bytes 159752 | tf_op jit(solution)/shard_map/ppermute | solution.py:300
  21.2 4.8 %collective-permute-start.4 = (f32[104,128]{1,0:T(8,128)S(1)}, f32[104,128]{1,0:T(8,128)S(1)}, u32[]{:S(2)}, u32[]{:S(2)}) collective-permute-start(f32[104,128]{1,0:T(8,128)S(1)} %add_select_fusion.2), channel_id=1, source_target_pairs={{0,28},{4,24},{8,20},{12,16},{16,12},{20,8},{24,4},{28,0},{1,29},{... | collective-permute-start | bytes 159752 | tf_op jit(solution)/shard_map/ppermute | solution.py:300
  26.1 1.3 %collective-permute-start.5 = (f32[104,128]{1,0:T(8,128)S(1)}, f32[104,128]{1,0:T(8,128)S(1)}, u32[]{:S(2)}, u32[]{:S(2)}) collective-permute-start(f32[104,128]{1,0:T(8,128)S(1)} %add_select_fusion.1), channel_id=1, source_target_pairs={{0,4},{4,0},{8,12},{12,8},{16,20},{20,16},{24,28},{28,24},{1,5},{5... | collective-permute-start | bytes 159752 | tf_op jit(solution)/shard_map/ppermute | solution.py:300
  26.6 13.7 %collective-permute-start.7 = (f32[1,2,256,256]{3,2,1,0:T(8,128)}, f32[1,2,256,256]{3,2,1,0:T(8,128)S(1)}, u32[]{:S(2)}, u32[]{:S(2)}) collective-permute-start(f32[1,2,256,256]{3,2,1,0:T(8,128)} %get-tuple-element.76), channel_id=1, source_target_pairs={{0,8},{4,12},{8,0},{12,4},{16,24},{20,28},{24,16},{28,20},{1,9},{5... | collective-permute-start | bytes 1572872 | tf_op jit(solution)/shard_map/ppermute | solution.py:395
  29.1 6.2 %copy-start.15 = (f32[16,4,128]{2,1,0:T(4,128)S(1)}, f32[16,4,128]{2,1,0:T(4,128)}, u32[]{:S(2)}) copy-start(f32[16,4,128]{2,1,0:T(4,128)} %param.12) | copy-start | bytes 98308
  29.1 6.2 %copy-start.16 = (f32[16,4,128]{2,1,0:T(4,128)S(1)}, f32[16,4,128]{2,1,0:T(4,128)}, u32[]{:S(2)}) copy-start(f32[16,4,128]{2,1,0:T(4,128)} %param.10) | copy-start | bytes 98308
  29.1 6.7 %copy-start.18 = (f32[16,4,128]{2,1,0:T(4,128)S(1)}, f32[16,4,128]{2,1,0:T(4,128)}, u32[]{:S(2)}) copy-start(f32[16,4,128]{2,1,0:T(4,128)} %param.11) | copy-start | bytes 98308
  29.1 11.1 %copy-start.24 = (f32[1,2,256,256]{3,2,1,0:T(8,128)S(1)}, f32[1,2,256,256]{3,2,1,0:T(8,128)}, u32[]{:S(2)}) copy-start(f32[1,2,256,256]{3,2,1,0:T(8,128)} %get-tuple-element.90) | copy-start | bytes 1572868
  35.6 24.0 %collective-permute-start.10 = (f32[1,2,256,256]{3,2,1,0:T(8,128)}, f32[1,2,256,256]{3,2,1,0:T(8,128)S(1)}, u32[]{:S(2)}, u32[]{:S(2)}) collective-permute-start(f32[1,2,256,256]{3,2,1,0:T(8,128)} %collective-permute-done.2.refs_0_), channel_id=1, source_target_pairs={{0,16},{4,20},{8,24},{12,28},{16,0},{20,4},{24,8},{28,12},{1,17},{... | collective-permute-start | bytes 1572872 | tf_op jit(solution)/shard_map/ppermute | solution.py:400
  35.8 13.0 %collective-permute-start.6 = (f32[2,256,256]{2,1,0:T(8,128)S(1)}, f32[2,256,256]{2,1,0:T(8,128)S(1)}, u32[]{:S(2)}, u32[]{:S(2)}) collective-permute-start(f32[2,256,256]{2,1,0:T(8,128)S(1)} %get-tuple-element.73.whole_source), channel_id=1, source_target_pairs={{0,1},{2,3},{1,0},{3,2},{4,5},{6,7},{5,4},{7,6},{8,9},{10,11},{9,8... | collective-permute-start | bytes 1572872 | tf_op jit(solution)/shard_map/ppermute | solution.py:478
  40.2 12.9 %collective-permute-start.9 = (f32[1,2,256,256]{3,2,1,0:T(8,128)S(1)}, f32[1,2,256,256]{3,2,1,0:T(8,128)}, u32[]{:S(2)}, u32[]{:S(2)}) collective-permute-start(f32[1,2,256,256]{3,2,1,0:T(8,128)S(1)} %copy-done.24), channel_id=1, source_target_pairs={{0,8},{4,12},{8,0},{12,4},{16,24},{20,28},{24,16},{28,20},{1,9},{5... | collective-permute-start | bytes 1572872 | tf_op jit(solution)/shard_map/ppermute | solution.py:404
  41.2 19.2 %collective-permute-start.11 = (f32[1,2,256,256]{3,2,1,0:T(8,128)S(1)}, f32[1,2,256,256]{3,2,1,0:T(8,128)S(1)}, u32[]{:S(2)}, u32[]{:S(2)}) collective-permute-start(f32[1,2,256,256]{3,2,1,0:T(8,128)S(1)} %collective-permute-done.7.refs_1_), channel_id=1, source_target_pairs={{0,16},{4,20},{8,24},{12,28},{16,0},{20,4},{24,8},{28,12},{1,17},{... | collective-permute-start | bytes 1572872 | tf_op jit(solution)/shard_map/ppermute | solution.py:400
  49.7 14.0 %collective-permute-start.8 = (f32[2,256,256]{2,1,0:T(8,128)S(1)}, f32[2,256,256]{2,1,0:T(8,128)S(1)}, u32[]{:S(2)}, u32[]{:S(2)}) collective-permute-start(f32[2,256,256]{2,1,0:T(8,128)S(1)} %shard_map.115.before), channel_id=1, source_target_pairs={{1,2},{2,1},{5,6},{6,5},{9,10},{10,9},{13,14},{14,13},{17,18},{18,... | collective-permute-start | bytes 1572872 | tf_op jit(solution)/shard_map/ppermute | solution.py:478
  53.1 23.6 %collective-permute-start.13 = (f32[1,2,256,256]{3,2,1,0:T(8,128)}, f32[1,2,256,256]{3,2,1,0:T(8,128)}, u32[]{:S(2)}, u32[]{:S(2)}) collective-permute-start(f32[1,2,256,256]{3,2,1,0:T(8,128)} %get-tuple-element.98), channel_id=1, source_target_pairs={{0,8},{4,12},{8,0},{12,4},{16,24},{20,28},{24,16},{28,20},{1,9},{5... | collective-permute-start | bytes 1572872 | tf_op jit(solution)/shard_map/ppermute | solution.py:404
  58.3 21.4 %collective-permute-start.14 = (f32[1,2,256,256]{3,2,1,0:T(8,128)}, f32[1,2,256,256]{3,2,1,0:T(8,128)}, u32[]{:S(2)}, u32[]{:S(2)}) collective-permute-start(f32[1,2,256,256]{3,2,1,0:T(8,128)} %collective-permute-done.9.refs_0_), channel_id=1, source_target_pairs={{0,16},{4,20},{8,24},{12,28},{16,0},{20,4},{24,8},{28,12},{1,17},{... | collective-permute-start | bytes 1572872 | tf_op jit(solution)/shard_map/ppermute | solution.py:400
  59.5 6.0 %copy-start.10 = (f32[1,2,256,256]{3,2,1,0:T(8,128)}, f32[1,2,256,256]{3,2,1,0:T(8,128)S(1)}, u32[]{:S(2)}) copy-start(f32[1,2,256,256]{3,2,1,0:T(8,128)S(1)} %collective-permute-done.10.refs_0_) | copy-start | bytes 1572868
  60.3 6.7 %copy-start.12 = (f32[1,2,256,256]{3,2,1,0:T(8,128)}, f32[1,2,256,256]{3,2,1,0:T(8,128)S(1)}, u32[]{:S(2)}) copy-start(f32[1,2,256,256]{3,2,1,0:T(8,128)S(1)} %collective-permute-done.11.refs_1_) | copy-start | bytes 1572868
  67.1 12.6 %collective-permute-start.12 = (f32[2,256,256]{2,1,0:T(8,128)}, f32[2,256,256]{2,1,0:T(8,128)}, u32[]{:S(2)}, u32[]{:S(2)}) collective-permute-start(f32[2,256,256]{2,1,0:T(8,128)} %get-tuple-element.96), channel_id=1, source_target_pairs={{0,1},{2,3},{1,0},{3,2},{4,5},{6,7},{5,4},{7,6},{8,9},{10,11},{9,8... | collective-permute-start | bytes 1572872 | tf_op jit(solution)/shard_map/ppermute | solution.py:512
  67.1 23.7 %collective-permute-start.16 = (f32[2,256,256]{2,1,0:T(8,128)}, f32[2,256,256]{2,1,0:T(8,128)S(1)}, u32[]{:S(2)}, u32[]{:S(2)}) collective-permute-start(f32[2,256,256]{2,1,0:T(8,128)} %copy-done.14), channel_id=1, source_target_pairs={{8,17},{9,18},{10,19},{12,21},{13,22},{14,23},{16,9},{17,10},{18,1... | collective-permute-start | bytes 1572872 | tf_op jit(solution)/shard_map/ppermute | solution.py:513
  76.8 23.8 %collective-permute-start.17 = (f32[1,2,256,256]{3,2,1,0:T(8,128)}, f32[1,2,256,256]{3,2,1,0:T(8,128)S(1)}, u32[]{:S(2)}, u32[]{:S(2)}) collective-permute-start(f32[1,2,256,256]{3,2,1,0:T(8,128)} %collective-permute-done.13.refs_1_), channel_id=1, source_target_pairs={{0,16},{4,20},{8,24},{12,28},{16,0},{20,4},{24,8},{28,12},{1,17},{... | collective-permute-start | bytes 1572872 | tf_op jit(solution)/shard_map/ppermute | solution.py:400
  80.8 27.0 %collective-permute-start.15 = (f32[2,256,256]{2,1,0:T(8,128)S(1)}, f32[2,256,256]{2,1,0:T(8,128)S(1)}, u32[]{:S(2)}, u32[]{:S(2)}) collective-permute-start(f32[2,256,256]{2,1,0:T(8,128)S(1)} %broadcast_select_fusion.carried), channel_id=1, source_target_pairs={{0,8},{4,12},{8,0},{12,4},{16,24},{20,28},{24,16},{28,20},{1,9},{5... | collective-permute-start | bytes 1572872 | tf_op jit(solution)/shard_map/ppermute | solution.py:521
  110.5 5.6 %collective-permute-start.18 = (f32[2,2,256,256]{3,2,1,0:T(8,128)S(1)}, f32[2,2,256,256]{3,2,1,0:T(8,128)S(1)}, u32[]{:S(2)}, u32[]{:S(2)}) collective-permute-start(f32[2,2,256,256]{3,2,1,0:T(8,128)S(1)} %get-tuple-element.123), channel_id=1, source_target_pairs={{0,4},{4,0},{8,12},{12,8},{16,20},{20,16},{24,28},{28,24},{1,5},{5... | collective-permute-start | bytes 3145736 | tf_op jit(solution)/shard_map/ppermute | solution.py:573
  116.2 2.7 %collective-permute-start.19 = (f32[2,2,256,256]{3,2,1,0:T(8,128)S(1)}, f32[2,2,256,256]{3,2,1,0:T(8,128)S(1)}, u32[]{:S(2)}, u32[]{:S(2)}) collective-permute-start(f32[2,2,256,256]{3,2,1,0:T(8,128)S(1)} %get-tuple-element.131), channel_id=1, source_target_pairs={{0,4},{4,0},{8,12},{12,8},{16,20},{20,16},{24,28},{28,24},{1,5},{5... | collective-permute-start | bytes 3145736 | tf_op jit(solution)/shard_map/ppermute | solution.py:573
  (13 other events, 24.3 us)

commit v16 on v9

--- a/solution.py
+++ b/solution.py
@@ -364,6 +364,11 @@
     wire_after = jnp.where(even, arrived, crossed)
 
     cells, rows, depth = charge.shape
+    own_ends = jnp.concatenate(
+        [array[:, end] for array in (potential_old, permittivity) for end in (0, rows - 1)]
+    )
+    beyond = [(e, e + 1) for e in range(1, energies - 1, 2)]
+    other_ends = lax.ppermute(own_ends, "energy", beyond + [(b, a) for a, b in beyond])
     far, near = pl.BlockSpec(memory_space=pl.ANY), pl.BlockSpec(memory_space=pltpu.VMEM)
     sums, ends, *cuts = call(
         functools.partial(gather_kernel, rows, energies),
@@ -389,7 +394,9 @@
         ],
     )
     cuts = [first_cut, *cuts]
-    sums, twin_ends, crossed, arrived = exchanged(sums, ends, free_first[0])
+    sums, twin_ends, crossed, (arrived, other_ends) = exchanged(
+        sums, ends, (free_first[0], other_ends)
+    )
 
     crossed, cuts[1] = lax.optimization_barrier((crossed, cuts[1]))
     sums, arrived = lax.optimization_barrier((sums, arrived))
@@ -478,6 +485,7 @@
         if hop == 2:
             sent_on(2)
             sent_after(3)
+            free_first[:3] = lax.optimization_barrier(free_first[:3])
             beside_first[0] = beside(0, free_first[:2])
             arrived, beside_first[0], free_first[2], *free_second[:2] = lax.optimization_barrier(
                 (arrived, beside_first[0], free_first[2], *free_second[:2])
@@ -525,12 +533,10 @@
         in_specs=[block, block, pl.BlockSpec(sums.shape, lambda s: (0, 0)), one_state],
         out_specs=(block, one_state),
     )
-    carried_second, greens, free_second[3], ends, field, perm = lax.optimization_barrier(
-        (carried_second, greens, free_second[3], ends, potential_old, permittivity)
-    )
-
-    beyond = [(e, e + 1) for e in range(1, energies - 1, 2)]
-    other_ends = lax.ppermute(ends, "energy", beyond + [(b, a) for a, b in beyond])
+    carried_second, greens, free_second[3], field, perm = lax.optimization_barrier(
+        (carried_second, greens, free_second[3], potential_old, permittivity)
+    )
+
     ends_before = jnp.where(odd == 1, twin_ends, other_ends).reshape(2, 2, cells, 1, depth)
     ends_after = jnp.where(odd == 1, other_ends, twin_ends).reshape(2, 2, cells, 1, depth)
     edge = jnp.zeros((2, cells, rows, 1), jnp.float32)

time: 117 us -> 113 us (0.966); the launches traced: 115 us -> 112 us
  waiting for transfers between devices: 31.9 us -> 39.6 us
  Pallas kernels: 41.5 us -> 36 us
  starting transfers between devices: 29.9 us -> 24.7 us
    ppermute x4, waiting for transfers between devices: 7.46 us -> 13.2 us  [sent_on(): free_second.append(lax.ppermute(given, 'energy', relay_pairs))]
    pallas_call x13, Pallas kernels: 41.5 us -> 36 us  [call(): pl.pallas_call(kernel, out_shape=out_shapes, cost_estimate=cost, compiler...]
    ppermute x3, starting transfers between devices: 4.13 us -> 1.35 us  [exchanged(): lax.ppermute(given, 'energy', [(e, e ^ mask) for e in range(peers)])]
    ppermute x1, waiting for transfers between devices: 3.26 us -> 5 us  [per_device(): lax.ppermute(onward, ('energy', 'slab'), both(second_pairs))]
    slice x0 -> x2, local copies, waits for them, and re-layouts: none -> 1.7 us  [per_device(): array[:, end]]
    unnamed x36 -> x28, local copies, waits for them, and re-layouts: 3.25 us -> 1.65 us
    ppermute x1, waiting for transfers between devices: 0.62 us -> 2.21 us  [per_device(): arrived = lax.ppermute(leaving, 'slab', swaps((peers - 2) % 2))]
    ppermute x2, starting transfers between devices: 0.98 us -> 2.47 us  [per_device(): outputs.append(here + lax.ppermute(there, 'energy', twin_pairs))]
  transfers between devices with their start and end apart: 21 -> 21, of which waited for: 13 -> 13; matrix products, arithmetic and copies ran while one was open for 3% -> 4% of each run, Pallas kernels for 34% -> 30%
where the time goes in v16:
time: 113 us; the launch traced here: 112 us
  waiting for transfers between devices  39.6 us (35%)
  Pallas kernels  36 us (32%)
  starting transfers between devices  24.7 us (22%)
  other arithmetic  6.17 us (5%)
  local copies, waits for them, and re-layouts  4.72 us (4%)
    pallas_call x13, Pallas kernels, call(): pl.pallas_call(kernel, out_shape=out_shapes, cost_estimate=cost, compiler...  36 us
    ppermute x4, waiting for transfers between devices, sent_on(): free_second.append(lax.ppermute(given, 'energy', relay_pairs))  13.2 us
    ppermute x2, waiting for transfers between devices, per_device(): arrived = lax.ppermute(leaving, 'slab', swaps((hop - 1) % 2))  9.28 us
    ppermute x1, waiting for transfers between devices, per_device(): lax.ppermute(onward, ('energy', 'slab'), both(second_pairs))  5 us
    ppermute x3, waiting for transfers between devices, exchanged(): lax.ppermute(given, 'energy', [(e, e ^ mask) for e in range(peers)])  4.55 us
    ppermute x1, starting transfers between devices, per_device(): crossed = lax.ppermute(jnp.where(even, lower, upper), 'slab', swaps(1))  4.32 us
    ppermute x1, starting transfers between devices, per_device(): lax.ppermute(onward, ('energy', 'slab'), both(second_pairs))  3.71 us
    ppermute x1, starting transfers between devices, per_device(): lax.ppermute(own_ends, 'energy', beyond + [(b, a) for a, b in beyond])  3.56 us
  transfers between devices with their start and end apart: 21, of which 13 were waited for; matrix products, arithmetic and copies ran while one was open for 4% of the time, Pallas kernels for 30%

profile of v16, /device:TPU:13, one launch (start us, length us, event | category | flops | bytes accessed | tf_op | source)
XLA Modules:
  0.0 112.4 jit_solution(6828969459662376872)
XLA Ops:
  0.6 1.2 %slice_bitcast_fusion = f32[1,2,256,256]{3,2,1,0:T(8,128)S(1)} fusion(f32[1,4,2,256,256]{4,3,2,1,0:T(8,128)} %param.14), kind=kLoop, calls=%fused_computation.2 | loop fusion | bytes 1048576 | tf_op jit(solution)/shard_map/slice | solution.py:346
  1.9 1.3 %collective-permute-start.2 = (f32[1,2,256,256]{3,2,1,0:T(8,128)S(1)}, f32[1,2,256,256]{3,2,1,0:T(8,128)S(1)}, u32[]{:S(2)}, u32[]{:S(2)}) collective-permute-start(f32[1,2,256,256]{3,2,1,0:T(8,128)S(1)} %slice_bitcast_fusion), channel_id=1, source_target_pairs={{0,8},{4,12},{8,0},{12,4},{16,24},{20,28},{24,16},{28,20},{1,9},{5... | collective-permute-start | bytes 1572872 | tf_op jit(solution)/shard_map/ppermute | solution.py:347
  4.2 4.3 %collective-permute-start = (f32[2,1,4,128]{3,2,0,1:T(4,128)S(1)}, f32[2,1,4,128]{3,2,0,1:T(4,128)S(1)}, u32[]{:S(2)}, u32[]{:S(2)}) collective-permute-start(f32[2,1,4,128]{3,2,0,1:T(4,128)S(1)} %get-tuple-element.141), channel_id=1, source_target_pairs={{1,2},{2,1},{5,6},{6,5},{9,10},{10,9},{13,14},{14,13},{17,18},{18,... | collective-permute-start | bytes 12296 | tf_op jit(solution)/shard_map/ppermute | solution.py:362
  10.2 3.6 %collective-permute-start.3 = (f32[64,128]{1,0:T(8,128)S(1)}, f32[64,128]{1,0:T(8,128)S(1)}, u32[]{:S(2)}, u32[]{:S(2)}) collective-permute-start(f32[64,128]{1,0:T(8,128)S(1)} %pad_maximum_fusion.2), channel_id=1, source_target_pairs={{4,8},{12,16},{20,24},{8,4},{16,12},{24,20},{5,9},{13,17},{21,25},... | collective-permute-start | bytes 98312 | tf_op jit(solution)/shard_map/ppermute | solution.py:371
  14.4 3.7 %shard_map.113 = (f32[40,128]{1,0:T(8,128)}, f32[64,128]{1,0:T(8,128)}, f32[1,2,256,256]{3,2,1,0:T(8,128)}, f32[1,2,256,256]{3,2,1,0:T(8,128)}, f32[1,2,256,256]{3,2,1,0:T(8,128)}) custom-call(s32[1]{0:T(128)} %bitcast.2.mine, f32[64,128]{1,0:T(8,128)} %bitcast.60, f32[64,128]{1,0:T(8,128)} %bitcast.58, f32[64,128]{1,0:T(8,128)} %bitcast.61, ...), custom_call_target="tpu_custom_call" | custom-call | flops 301989888 | bytes 3833860 | tf_op jit(solution)/shard_map/pallas_call | solution.py:67
  18.2 2.8 %collective-permute-done.4 = f32[40,128]{1,0:T(8,128)S(1)} collective-permute-done((f32[40,128]{1,0:T(8,128)}, f32[40,128]{1,0:T(8,128)S(1)}, u32[]{:S(2)}, u32[]{:S(2)}) %collective-permute-start.4) | collective-permute-done | bytes 20512 | tf_op jit(solution)/shard_map/ppermute | solution.py:302
  24.8 1.5 %collective-permute-start.8 = (f32[1,2,256,256]{3,2,1,0:T(8,128)}, f32[1,2,256,256]{3,2,1,0:T(8,128)S(1)}, u32[]{:S(2)}, u32[]{:S(2)}) collective-permute-start(f32[1,2,256,256]{3,2,1,0:T(8,128)} %get-tuple-element.81), channel_id=1, source_target_pairs={{0,8},{4,12},{8,0},{12,4},{16,24},{20,28},{24,16},{28,20},{1,9},{5... | collective-permute-start | bytes 1572872 | tf_op jit(solution)/shard_map/ppermute | solution.py:403
  27.1 1.6 %copy-done.1 = f32[4,2,256,256]{3,2,1,0:T(8,128)S(1)} copy-done((f32[4,2,256,256]{3,2,1,0:T(8,128)S(1)}, f32[4,2,256,256]{3,2,1,0:T(8,128)}, u32[]{:S(2)}) %copy-start.1) | copy-done | bytes 2097176
  28.7 6.3 %shard_map.114 = (f32[2,256,256]{2,1,0:T(8,128)S(1)}, f32[2,256,256]{2,1,0:T(8,128)S(1)}) custom-call(f32[4,2,256,256]{3,2,1,0:T(8,128)S(1)} %bitcast.55, f32[4,2,256,256]{3,2,1,0:T(8,128)S(1)} %copy-done.1, f32[40,128]{1,0:T(8,128)S(1)} %add.107.sums.refs_3_), custom_call_target="tpu_custom_call" | custom-call | flops 5133828096 | bytes 5263360 | tf_op jit(solution)/shard_map/pallas_call | solution.py:67
  35.5 2.5 %collective-permute-done.8.refs_1_ = f32[1,2,256,256]{3,2,1,0:T(8,128)S(1)} collective-permute-done((f32[1,2,256,256]{3,2,1,0:T(8,128)}, f32[1,2,256,256]{3,2,1,0:T(8,128)S(1)}, u32[]{:S(2)}, u32[]{:S(2)}) %collective-permute-start.8) | collective-permute-done | bytes 524320 | tf_op jit(solution)/shard_map/ppermute | solution.py:403
  38.1 1.5 %collective-permute-start.10 = (f32[1,2,256,256]{3,2,1,0:T(8,128)S(1)}, f32[1,2,256,256]{3,2,1,0:T(8,128)S(1)}, u32[]{:S(2)}, u32[]{:S(2)}) collective-permute-start(f32[1,2,256,256]{3,2,1,0:T(8,128)S(1)} %copy-done.13), channel_id=1, source_target_pairs={{0,8},{4,12},{8,0},{12,4},{16,24},{20,28},{24,16},{28,20},{1,9},{5... | collective-permute-start | bytes 1572872 | tf_op jit(solution)/shard_map/ppermute | solution.py:412
  40.1 6.9 %collective-permute-done.7.carried = f32[2,256,256]{2,1,0:T(8,128)S(1)} collective-permute-done((f32[2,256,256]{2,1,0:T(8,128)S(1)}, f32[2,256,256]{2,1,0:T(8,128)S(1)}, u32[]{:S(2)}, u32[]{:S(2)}) %collective-permute-start.7) | collective-permute-done | bytes 524320 | tf_op jit(solution)/shard_map/ppermute | solution.py:478
  47.9 2.1 %collective-permute-start.9 = (f32[2,256,256]{2,1,0:T(8,128)S(1)}, f32[2,256,256]{2,1,0:T(8,128)S(1)}, u32[]{:S(2)}, u32[]{:S(2)}) collective-permute-start(f32[2,256,256]{2,1,0:T(8,128)S(1)} %shard_map.115.before), channel_id=1, source_target_pairs={{1,2},{2,1},{5,6},{6,5},{9,10},{10,9},{13,14},{14,13},{17,18},{18,... | collective-permute-start | bytes 1572872 | tf_op jit(solution)/shard_map/ppermute | solution.py:478
  50.3 1.5 %collective-permute-start.14 = (f32[1,2,256,256]{3,2,1,0:T(8,128)S(1)}, f32[1,2,256,256]{3,2,1,0:T(8,128)S(1)}, u32[]{:S(2)}, u32[]{:S(2)}) collective-permute-start(f32[1,2,256,256]{3,2,1,0:T(8,128)S(1)} %copy-done.12), channel_id=1, source_target_pairs={{0,8},{4,12},{8,0},{12,4},{16,24},{20,28},{24,16},{28,20},{1,9},{5... | collective-permute-start | bytes 1572872 | tf_op jit(solution)/shard_map/ppermute | solution.py:412
  52.0 1.5 %shard_map.116 = (f32[2,2,256,256]{3,2,1,0:T(8,128)S(1)}, f32[2,2,256,256]{3,2,1,0:T(8,128)S(1)}) custom-call(f32[1,2,256,256]{3,2,1,0:T(8,128)S(1)} %collective-permute-done.2.refs_0_, f32[1,2,256,256]{3,2,1,0:T(8,128)S(1)} %collective-permute-done.8.refs_1_, f32[4,2,256,256]{3,2,1,0:T(8,128)S(1)} %copy-done.2, f32[40,128]{1,0:T(8,128)S(1)} %add.107.sums.refs_3_), custom_call_target="tpu_custom_call" | custom-call | flops 1207959552 | bytes 5263360 | tf_op jit(solution)/shard_map/pallas_call | solution.py:67
  53.6 4.8 %collective-permute-done.12.refs_1_ = f32[1,2,256,256]{3,2,1,0:T(8,128)S(1)} collective-permute-done((f32[1,2,256,256]{3,2,1,0:T(8,128)S(1)}, f32[1,2,256,256]{3,2,1,0:T(8,128)S(1)}, u32[]{:S(2)}, u32[]{:S(2)}) %collective-permute-start.12) | collective-permute-done | bytes 524320 | tf_op jit(solution)/shard_map/ppermute | solution.py:408
  58.4 2.4 %collective-permute-done.9.carried = f32[2,256,256]{2,1,0:T(8,128)S(1)} collective-permute-done((f32[2,256,256]{2,1,0:T(8,128)S(1)}, f32[2,256,256]{2,1,0:T(8,128)S(1)}, u32[]{:S(2)}, u32[]{:S(2)}) %collective-permute-start.9) | collective-permute-done | bytes 524320 | tf_op jit(solution)/shard_map/ppermute | solution.py:478
  61.8 3.7 %collective-permute-start.17 = (f32[2,256,256]{2,1,0:T(8,128)S(1)}, f32[2,256,256]{2,1,0:T(8,128)S(1)}, u32[]{:S(2)}, u32[]{:S(2)}) collective-permute-start(f32[2,256,256]{2,1,0:T(8,128)S(1)} %get-tuple-element.108), channel_id=1, source_target_pairs={{8,17},{9,18},{10,19},{12,21},{13,22},{14,23},{16,9},{17,10},{18,1... | collective-permute-start | bytes 1572872 | tf_op jit(solution)/shard_map/ppermute | solution.py:514
  65.5 1.5 %shard_map.119 = (f32[2,2,256,256]{3,2,1,0:T(8,128)S(1)}, f32[2,2,256,256]{3,2,1,0:T(8,128)S(1)}) custom-call(f32[1,2,256,256]{3,2,1,0:T(8,128)S(1)} %collective-permute-done.11.refs_0_, f32[1,2,256,256]{3,2,1,0:T(8,128)S(1)} %collective-permute-done.12.refs_1_, f32[4,2,256,256]{3,2,1,0:T(8,128)S(1)} %copy-done.2, f32[40,128]{1,0:T(8,128)S(1)} %add.107.sums.refs_3_), custom_call_target="tpu_custom_call" | custom-call | flops 1207959552 | bytes 5263360 | tf_op jit(solution)/shard_map/pallas_call | solution.py:67
  67.1 1.5 %shard_map.118 = (f32[2,2,256,256]{3,2,1,0:T(8,128)S(1)}, f32[2,2,256,256]{3,2,1,0:T(8,128)S(1)}) custom-call(f32[1,2,256,256]{3,2,1,0:T(8,128)S(1)} %collective-permute-done.10.refs_0_, f32[1,2,256,256]{3,2,1,0:T(8,128)S(1)} %collective-permute-done.14.refs_1_, f32[4,2,256,256]{3,2,1,0:T(8,128)S(1)} %copy-done.2, f32[40,128]{1,0:T(8,128)S(1)} %add.107.sums.refs_3_), custom_call_target="tpu_custom_call" | custom-call | flops 1207959552 | bytes 5263360 | tf_op jit(solution)/shard_map/pallas_call | solution.py:67
  69.6 2.2 %collective-permute-done.13 = f32[2,256,256]{2,1,0:T(8,128)S(1)} collective-permute-done((f32[2,256,256]{2,1,0:T(8,128)S(1)}, f32[2,256,256]{2,1,0:T(8,128)S(1)}, u32[]{:S(2)}, u32[]{:S(2)}) %collective-permute-start.13) | collective-permute-done | bytes 524320 | tf_op jit(solution)/shard_map/ppermute | solution.py:513
  72.3 7.5 %shard_map.120 = (f32[4,2,256,256]{3,2,1,0:T(8,128)S(1)}, f32[2,256,256]{2,1,0:T(8,128)}) custom-call(f32[4,2,256,256]{3,2,1,0:T(8,128)S(1)} %bitcast.56, f32[4,2,256,256]{3,2,1,0:T(8,128)S(1)} %copy-done.2, f32[40,128]{1,0:T(8,128)S(1)} %add.107.sums.refs_3_, f32[2,256,256]{2,1,0:T(8,128)S(1)} %broadcast_select_fusion.carried), custom_call_target="tpu_custom_call" | custom-call | flops 4831838208 | bytes 7360512 | tf_op jit(solution)/shard_map/pallas_call | solution.py:67
  79.8 5.0 %collective-permute-done.17.carried = f32[2,256,256]{2,1,0:T(8,128)S(1)} collective-permute-done((f32[2,256,256]{2,1,0:T(8,128)S(1)}, f32[2,256,256]{2,1,0:T(8,128)S(1)}, u32[]{:S(2)}, u32[]{:S(2)}) %collective-permute-start.17) | collective-permute-done | bytes 524320 | tf_op jit(solution)/shard_map/ppermute | solution.py:514
  84.8 7.4 %collective-permute-done.18.refs_1_ = f32[1,2,256,256]{3,2,1,0:T(8,128)S(1)} collective-permute-done((f32[1,2,256,256]{3,2,1,0:T(8,128)S(1)}, f32[1,2,256,256]{3,2,1,0:T(8,128)S(1)}, u32[]{:S(2)}, u32[]{:S(2)}) %collective-permute-start.18) | collective-permute-done | bytes 524320 | tf_op jit(solution)/shard_map/ppermute | solution.py:408
  92.4 1.5 %shard_map.122 = (f32[2,2,256,256]{3,2,1,0:T(8,128)S(1)}, f32[2,2,256,256]{3,2,1,0:T(8,128)S(1)}) custom-call(f32[1,2,256,256]{3,2,1,0:T(8,128)S(1)} %collective-permute-done.15.refs_0_, f32[1,2,256,256]{3,2,1,0:T(8,128)S(1)} %collective-permute-done.18.refs_1_, f32[4,2,256,256]{3,2,1,0:T(8,128)S(1)} %copy-done.2, f32[40,128]{1,0:T(8,128)S(1)} %add.107.sums.refs_3_), custom_call_target="tpu_custom_call" | custom-call | flops 1207959552 | bytes 5263360 | tf_op jit(solution)/shard_map/pallas_call | solution.py:67
  93.9 1.9 %shard_map.121 = (f32[2,2,256,256]{3,2,1,0:T(8,128)S(1)}, f32[2,256,256]{2,1,0:T(8,128)S(1)}) custom-call(f32[2,2,256,256]{3,2,1,0:T(8,128)S(1)} %get-tuple-element.106.link, f32[2,2,256,256]{3,2,1,0:T(8,128)S(1)} %get-tuple-element.107.source, f32[2,256,256]{2,1,0:T(8,128)S(1)} %collective-permute-done.17.carried), custom_call_target="tpu_custom_call" | custom-call | flops 1207959552 | bytes 4194304 | tf_op jit(solution)/shard_map/pallas_call | solution.py:67
  95.8 2.7 %shard_map.123 = (f32[2,2,256,256]{3,2,1,0:T(8,128)S(1)}, f32[2,256,256]{2,1,0:T(8,128)}) custom-call(f32[2,2,256,256]{3,2,1,0:T(8,128)S(1)} %get-tuple-element.114.link, f32[2,2,256,256]{3,2,1,0:T(8,128)S(1)} %get-tuple-element.115.source, f32[2,256,256]{2,1,0:T(8,128)S(1)} %get-tuple-element.116.carried), custom_call_target="tpu_custom_call" | custom-call | flops 1207959552 | bytes 4194304 | tf_op jit(solution)/shard_map/pallas_call | solution.py:67
  99.3 2.7 %shard_map.124 = (f32[2,2,256,256]{3,2,1,0:T(8,128)S(1)}, f32[2,2,256,256]{3,2,1,0:T(8,128)S(1)}, f32[2,256,256]{2,1,0:T(8,128)S(1)}) custom-call(s32[2]{0:T(128)S(1)} %pad_add_fusion.pick, f32[2,2,256,256]{3,2,1,0:T(8,128)S(1)} %get-tuple-element.122.link, f32[2,2,256,256]{3,2,1,0:T(8,128)S(1)} %get-tuple-element.123.source, ...), custom_call_target="tpu_custom_call" | custom-call | flops 1207959552 | bytes 9437192 | tf_op jit(solution)/shard_map/pallas_call | solution.py:67
  102.0 2.4 %collective-permute-start.19 = (f32[2,2,256,256]{3,2,1,0:T(8,128)S(1)}, f32[2,2,256,256]{3,2,1,0:T(8,128)S(1)}, u32[]{:S(2)}, u32[]{:S(2)}) collective-permute-start(f32[2,2,256,256]{3,2,1,0:T(8,128)S(1)} %get-tuple-element.129), channel_id=1, source_target_pairs={{0,4},{4,0},{8,12},{12,8},{16,20},{20,16},{24,28},{28,24},{1,5},{5... | collective-permute-start | bytes 3145736 | tf_op jit(solution)/shard_map/ppermute | solution.py:582
  104.4 3.4 %shard_map.125 = (f32[2,2,256,256]{3,2,1,0:T(8,128)S(1)}, f32[2,2,256,256]{3,2,1,0:T(8,128)S(1)}, f32[2,256,256]{2,1,0:T(8,128)}) custom-call(s32[2]{0:T(128)S(1)} %pad_add_fusion.pick, f32[2,2,256,256]{3,2,1,0:T(8,128)S(1)} %get-tuple-element.130.link, f32[2,2,256,256]{3,2,1,0:T(8,128)S(1)} %get-tuple-element.131.source, ...), custom_call_target="tpu_custom_call" | custom-call | flops 1207959552 | bytes 9437192 | tf_op jit(solution)/shard_map/pallas_call | solution.py:67
  108.1 2.6 %collective-permute-done.20 = f32[2,2,256,256]{3,2,1,0:T(8,128)S(1)} collective-permute-done((f32[2,2,256,256]{3,2,1,0:T(8,128)S(1)}, f32[2,2,256,256]{3,2,1,0:T(8,128)S(1)}, u32[]{:S(2)}, u32[]{:S(2)}) %collective-permute-start.20) | collective-permute-done | bytes 1048608 | tf_op jit(solution)/shard_map/ppermute | solution.py:582
  110.8 1.5 %maximum_bitcast_fusion = f32[1,4,2,256,256]{4,3,2,1,0:T(8,128)} fusion(f32[2,2,256,256]{3,2,1,0:T(8,128)S(1)} %add.131, f32[2,2,256,256]{3,2,1,0:T(8,128)S(1)} %add.130), kind=kLoop, calls=%fused_computation.1 | loop fusion | flops 524288 | bytes 4194304 | tf_op jit(solution)/shard_map/broadcast_in_dim | solution.py:583
  (78 shorter events, 14.3 us)
Async XLA Ops:
  0.6 26.4 %copy-start = (f32[1,4,2,256,256]{4,3,2,1,0:T(8,128)S(1)}, f32[1,4,2,256,256]{4,3,2,1,0:T(8,128)}, u32[]{:S(2)}) copy-start(f32[1,4,2,256,256]{4,3,2,1,0:T(8,128)} %param.14) | copy-start | bytes 6291460
  1.9 16.2 %collective-permute-start.2 = (f32[1,2,256,256]{3,2,1,0:T(8,128)S(1)}, f32[1,2,256,256]{3,2,1,0:T(8,128)S(1)}, u32[]{:S(2)}, u32[]{:S(2)}) collective-permute-start(f32[1,2,256,256]{3,2,1,0:T(8,128)S(1)} %slice_bitcast_fusion), channel_id=1, source_target_pairs={{0,8},{4,12},{8,0},{12,4},{16,24},{20,28},{24,16},{28,20},{1,9},{5... | collective-permute-start | bytes 1572872 | tf_op jit(solution)/shard_map/ppermute | solution.py:347
  4.0 9.9 %collective-permute-start.1 = (f32[2,1,4,128]{3,2,0,1:T(4,128)S(1)}, f32[2,1,4,128]{3,2,0,1:T(4,128)S(1)}, u32[]{:S(2)}, u32[]{:S(2)}) collective-permute-start(f32[2,1,4,128]{3,2,0,1:T(4,128)S(1)} %get-tuple-element.140), channel_id=1, source_target_pairs={{0,1},{2,3},{1,0},{3,2},{4,5},{6,7},{5,4},{7,6},{8,9},{10,11},{9,8... | collective-permute-start | bytes 12296 | tf_op jit(solution)/shard_map/ppermute | solution.py:361
  4.2 9.6 %collective-permute-start = (f32[2,1,4,128]{3,2,0,1:T(4,128)S(1)}, f32[2,1,4,128]{3,2,0,1:T(4,128)S(1)}, u32[]{:S(2)}, u32[]{:S(2)}) collective-permute-start(f32[2,1,4,128]{3,2,0,1:T(4,128)S(1)} %get-tuple-element.141), channel_id=1, source_target_pairs={{1,2},{2,1},{5,6},{6,5},{9,10},{10,9},{13,14},{14,13},{17,18},{18,... | collective-permute-start | bytes 12296 | tf_op jit(solution)/shard_map/ppermute | solution.py:362
  10.2 7.9 %collective-permute-start.3 = (f32[64,128]{1,0:T(8,128)S(1)}, f32[64,128]{1,0:T(8,128)S(1)}, u32[]{:S(2)}, u32[]{:S(2)}) collective-permute-start(f32[64,128]{1,0:T(8,128)S(1)} %pad_maximum_fusion.2), channel_id=1, source_target_pairs={{4,8},{12,16},{20,24},{8,4},{16,12},{24,20},{5,9},{13,17},{21,25},... | collective-permute-start | bytes 98312 | tf_op jit(solution)/shard_map/ppermute | solution.py:371
  18.1 2.9 %collective-permute-start.4 = (f32[40,128]{1,0:T(8,128)}, f32[40,128]{1,0:T(8,128)S(1)}, u32[]{:S(2)}, u32[]{:S(2)}) collective-permute-start(f32[40,128]{1,0:T(8,128)} %get-tuple-element.72), channel_id=1, source_target_pairs={{0,8},{4,12},{8,0},{12,4},{16,24},{20,28},{24,16},{28,20},{1,9},{5... | collective-permute-start | bytes 61448 | tf_op jit(solution)/shard_map/ppermute | solution.py:302
  22.5 1.9 %collective-permute-start.5 = (f32[104,128]{1,0:T(8,128)S(1)}, f32[104,128]{1,0:T(8,128)S(1)}, u32[]{:S(2)}, u32[]{:S(2)}) collective-permute-start(f32[104,128]{1,0:T(8,128)S(1)} %pad_maximum_fusion.1), channel_id=1, source_target_pairs={{0,4},{4,0},{8,12},{12,8},{16,20},{20,16},{24,28},{28,24},{1,5},{5... | collective-permute-start | bytes 159752 | tf_op jit(solution)/shard_map/ppermute | solution.py:302
  24.4 2.6 %collective-permute-start.6 = (f32[40,128]{1,0:T(8,128)S(1)}, f32[40,128]{1,0:T(8,128)S(1)}, u32[]{:S(2)}, u32[]{:S(2)}) collective-permute-start(f32[40,128]{1,0:T(8,128)S(1)} %slice_add_fusion), channel_id=1, source_target_pairs={{0,16},{4,20},{8,24},{12,28},{16,0},{20,4},{24,8},{28,12},{1,17},{... | collective-permute-start | bytes 61448 | tf_op jit(solution)/shard_map/ppermute | solution.py:302
  24.8 13.3 %collective-permute-start.8 = (f32[1,2,256,256]{3,2,1,0:T(8,128)}, f32[1,2,256,256]{3,2,1,0:T(8,128)S(1)}, u32[]{:S(2)}, u32[]{:S(2)}) collective-permute-start(f32[1,2,256,256]{3,2,1,0:T(8,128)} %get-tuple-element.81), channel_id=1, source_target_pairs={{0,8},{4,12},{8,0},{12,4},{16,24},{20,28},{24,16},{28,20},{1,9},{5... | collective-permute-start | bytes 1572872 | tf_op jit(solution)/shard_map/ppermute | solution.py:403
  28.7 6.5 %copy-start.10 = (s32[4]{0:T(128)S(1)}, s32[4]{0:T(128)}, u32[]{:S(2)}) copy-start(s32[4]{0:T(128)} %param.16) | copy-start | bytes 52
  28.7 6.5 %copy-start.11 = (s32[4]{0:T(128)S(1)}, s32[4]{0:T(128)}, u32[]{:S(2)}) copy-start(s32[4]{0:T(128)} %constant.57.clone) | copy-start | bytes 52
  28.7 9.4 %copy-start.13 = (f32[1,2,256,256]{3,2,1,0:T(8,128)S(1)}, f32[1,2,256,256]{3,2,1,0:T(8,128)}, u32[]{:S(2)}) copy-start(f32[1,2,256,256]{3,2,1,0:T(8,128)} %get-tuple-element.87) | copy-start | bytes 1572868
  28.7 10.9 %copy-start.5 = (f32[4,256,256]{2,1,0:T(8,128)S(1)}, f32[4,256,256]{2,1,0:T(8,128)}, u32[]{:S(2)}) copy-start(f32[4,256,256]{2,1,0:T(8,128)} %param.18) | copy-start | bytes 3145732
  35.0 12.0 %collective-permute-start.7 = (f32[2,256,256]{2,1,0:T(8,128)S(1)}, f32[2,256,256]{2,1,0:T(8,128)S(1)}, u32[]{:S(2)}, u32[]{:S(2)}) collective-permute-start(f32[2,256,256]{2,1,0:T(8,128)S(1)} %get-tuple-element.78.whole_source), channel_id=1, source_target_pairs={{0,1},{2,3},{1,0},{3,2},{4,5},{6,7},{5,4},{7,6},{8,9},{10,11},{9,8... | collective-permute-start | bytes 1572872 | tf_op jit(solution)/shard_map/ppermute | solution.py:478
  35.2 18.3 %collective-permute-start.11 = (f32[1,2,256,256]{3,2,1,0:T(8,128)S(1)}, f32[1,2,256,256]{3,2,1,0:T(8,128)S(1)}, u32[]{:S(2)}, u32[]{:S(2)}) collective-permute-start(f32[1,2,256,256]{3,2,1,0:T(8,128)S(1)} %collective-permute-done.2.refs_0_), channel_id=1, source_target_pairs={{0,16},{4,20},{8,24},{12,28},{16,0},{20,4},{24,8},{28,12},{1,17},{... | collective-permute-start | bytes 1572872 | tf_op jit(solution)/shard_map/ppermute | solution.py:408
  38.0 12.0 %copy-start.7 = (f32[1,1,8,128]{3,2,0,1:T(8,128)S(1)}, f32[1,1,8,128]{3,2,0,1:T(8,128)}, u32[]{:S(2)}) copy-start(f32[1,1,8,128]{3,2,0,1:T(8,128)} %get-tuple-element.176) | copy-start | bytes 12292
  38.0 12.0 %copy-start.8 = (f32[1,1,8,128]{3,2,0,1:T(8,128)S(1)}, f32[1,1,8,128]{3,2,0,1:T(8,128)}, u32[]{:S(2)}) copy-start(f32[1,1,8,128]{3,2,0,1:T(8,128)} %get-tuple-element.177) | copy-start | bytes 12292
  38.0 12.2 %copy-start.12 = (f32[1,2,256,256]{3,2,1,0:T(8,128)S(1)}, f32[1,2,256,256]{3,2,1,0:T(8,128)}, u32[]{:S(2)}) copy-start(f32[1,2,256,256]{3,2,1,0:T(8,128)} %get-tuple-element.98) | copy-start | bytes 1572868
  38.1 14.0 %copy-start.2 = (f32[4,2,256,256]{3,2,1,0:T(8,128)S(1)}, f32[4,2,256,256]{3,2,1,0:T(8,128)}, u32[]{:S(2)}) copy-start(f32[4,2,256,256]{3,2,1,0:T(8,128)} %refs_2_.7) | copy-start | bytes 6291460
  38.1 12.2 %collective-permute-start.10 = (f32[1,2,256,256]{3,2,1,0:T(8,128)S(1)}, f32[1,2,256,256]{3,2,1,0:T(8,128)S(1)}, u32[]{:S(2)}, u32[]{:S(2)}) collective-permute-start(f32[1,2,256,256]{3,2,1,0:T(8,128)S(1)} %copy-done.13), channel_id=1, source_target_pairs={{0,8},{4,12},{8,0},{12,4},{16,24},{20,28},{24,16},{28,20},{1,9},{5... | collective-permute-start | bytes 1572872 | tf_op jit(solution)/shard_map/ppermute | solution.py:412
  40.0 18.4 %collective-permute-start.12 = (f32[1,2,256,256]{3,2,1,0:T(8,128)S(1)}, f32[1,2,256,256]{3,2,1,0:T(8,128)S(1)}, u32[]{:S(2)}, u32[]{:S(2)}) collective-permute-start(f32[1,2,256,256]{3,2,1,0:T(8,128)S(1)} %collective-permute-done.8.refs_1_), channel_id=1, source_target_pairs={{0,16},{4,20},{8,24},{12,28},{16,0},{20,4},{24,8},{28,12},{1,17},{... | collective-permute-start | bytes 1572872 | tf_op jit(solution)/shard_map/ppermute | solution.py:408
  47.9 12.9 %collective-permute-start.9 = (f32[2,256,256]{2,1,0:T(8,128)S(1)}, f32[2,256,256]{2,1,0:T(8,128)S(1)}, u32[]{:S(2)}, u32[]{:S(2)}) collective-permute-start(f32[2,256,256]{2,1,0:T(8,128)S(1)} %shard_map.115.before), channel_id=1, source_target_pairs={{1,2},{2,1},{5,6},{6,5},{9,10},{10,9},{13,14},{14,13},{17,18},{18,... | collective-permute-start | bytes 1572872 | tf_op jit(solution)/shard_map/ppermute | solution.py:478
  50.3 16.7 %collective-permute-start.14 = (f32[1,2,256,256]{3,2,1,0:T(8,128)S(1)}, f32[1,2,256,256]{3,2,1,0:T(8,128)S(1)}, u32[]{:S(2)}, u32[]{:S(2)}) collective-permute-start(f32[1,2,256,256]{3,2,1,0:T(8,128)S(1)} %copy-done.12), channel_id=1, source_target_pairs={{0,8},{4,12},{8,0},{12,4},{16,24},{20,28},{24,16},{28,20},{1,9},{5... | collective-permute-start | bytes 1572872 | tf_op jit(solution)/shard_map/ppermute | solution.py:412
  51.7 17.9 %collective-permute-start.15 = (f32[1,2,256,256]{3,2,1,0:T(8,128)S(1)}, f32[1,2,256,256]{3,2,1,0:T(8,128)S(1)}, u32[]{:S(2)}, u32[]{:S(2)}) collective-permute-start(f32[1,2,256,256]{3,2,1,0:T(8,128)S(1)} %collective-permute-done.10.refs_0_), channel_id=1, source_target_pairs={{0,16},{4,20},{8,24},{12,28},{16,0},{20,4},{24,8},{28,12},{1,17},{... | collective-permute-start | bytes 1572872 | tf_op jit(solution)/shard_map/ppermute | solution.py:408
  61.7 10.1 %collective-permute-start.13 = (f32[2,256,256]{2,1,0:T(8,128)S(1)}, f32[2,256,256]{2,1,0:T(8,128)S(1)}, u32[]{:S(2)}, u32[]{:S(2)}) collective-permute-start(f32[2,256,256]{2,1,0:T(8,128)S(1)} %get-tuple-element.96), channel_id=1, source_target_pairs={{0,1},{2,3},{1,0},{3,2},{4,5},{6,7},{5,4},{7,6},{8,9},{10,11},{9,8... | collective-permute-start | bytes 1572872 | tf_op jit(solution)/shard_map/ppermute | solution.py:513
  61.8 23.0 %collective-permute-start.17 = (f32[2,256,256]{2,1,0:T(8,128)S(1)}, f32[2,256,256]{2,1,0:T(8,128)S(1)}, u32[]{:S(2)}, u32[]{:S(2)}) collective-permute-start(f32[2,256,256]{2,1,0:T(8,128)S(1)} %get-tuple-element.108), channel_id=1, source_target_pairs={{8,17},{9,18},{10,19},{12,21},{13,22},{14,23},{16,9},{17,10},{18,1... | collective-permute-start | bytes 1572872 | tf_op jit(solution)/shard_map/ppermute | solution.py:514
  67.0 25.2 %collective-permute-start.18 = (f32[1,2,256,256]{3,2,1,0:T(8,128)S(1)}, f32[1,2,256,256]{3,2,1,0:T(8,128)S(1)}, u32[]{:S(2)}, u32[]{:S(2)}) collective-permute-start(f32[1,2,256,256]{3,2,1,0:T(8,128)S(1)} %collective-permute-done.14.refs_1_), channel_id=1, source_target_pairs={{0,16},{4,20},{8,24},{12,28},{16,0},{20,4},{24,8},{28,12},{1,17},{... | collective-permute-start | bytes 1572872 | tf_op jit(solution)/shard_map/ppermute | solution.py:408
  71.9 20.3 %copy-start.3 = (f32[16,4,128]{2,1,0:T(4,128)S(1)}, f32[16,4,128]{2,1,0:T(4,128)}, u32[]{:S(2)}) copy-start(f32[16,4,128]{2,1,0:T(4,128)} %param.12) | copy-start | bytes 98308
  71.9 20.3 %copy-start.4 = (f32[16,4,128]{2,1,0:T(4,128)S(1)}, f32[16,4,128]{2,1,0:T(4,128)}, u32[]{:S(2)}) copy-start(f32[16,4,128]{2,1,0:T(4,128)} %param.10) | copy-start | bytes 98308
  72.0 27.4 %collective-permute-start.16 = (f32[2,256,256]{2,1,0:T(8,128)S(1)}, f32[2,256,256]{2,1,0:T(8,128)S(1)}, u32[]{:S(2)}, u32[]{:S(2)}) collective-permute-start(f32[2,256,256]{2,1,0:T(8,128)S(1)} %broadcast_select_fusion.carried), channel_id=1, source_target_pairs={{0,8},{4,12},{8,0},{12,4},{16,24},{20,28},{24,16},{28,20},{1,9},{5... | collective-permute-start | bytes 1572872 | tf_op jit(solution)/shard_map/ppermute | solution.py:522
  102.0 5.8 %collective-permute-start.19 = (f32[2,2,256,256]{3,2,1,0:T(8,128)S(1)}, f32[2,2,256,256]{3,2,1,0:T(8,128)S(1)}, u32[]{:S(2)}, u32[]{:S(2)}) collective-permute-start(f32[2,2,256,256]{3,2,1,0:T(8,128)S(1)} %get-tuple-element.129), channel_id=1, source_target_pairs={{0,4},{4,0},{8,12},{12,8},{16,20},{20,16},{24,28},{28,24},{1,5},{5... | collective-permute-start | bytes 3145736 | tf_op jit(solution)/shard_map/ppermute | solution.py:582
  108.0 2.7 %collective-permute-start.20 = (f32[2,2,256,256]{3,2,1,0:T(8,128)S(1)}, f32[2,2,256,256]{3,2,1,0:T(8,128)S(1)}, u32[]{:S(2)}, u32[]{:S(2)}) collective-permute-start(f32[2,2,256,256]{3,2,1,0:T(8,128)S(1)} %get-tuple-element.137), channel_id=1, source_target_pairs={{0,4},{4,0},{8,12},{12,8},{16,20},{20,16},{24,28},{28,24},{1,5},{5... | collective-permute-start | bytes 3145736 | tf_op jit(solution)/shard_map/ppermute | solution.py:582
  (3 other events, 10.8 us)

commit v17 on v16

--- a/solution.py
+++ b/solution.py
@@ -290,7 +290,7 @@
     )
 
 
-def exchanged(sums, ends, early):
+def exchanged(sums, ends, other_ends, early):
     peers = lax.axis_size("energy")
     assert peers >= 4 and peers & (peers - 1) == 0
     masks = [2, 1] + [1 << k for k in range(2, peers.bit_length() - 1)]
@@ -298,13 +298,15 @@
     first = None
     sums, early = lax.optimization_barrier((sums, early))
     for mask in masks:
+        if mask == 4:
+            sums, other_ends = lax.optimization_barrier((sums, other_ends))
         given = jnp.concatenate([sums, ends]) if mask == 1 else sums
         arrived = lax.ppermute(given, "energy", [(e, e ^ mask) for e in range(peers)])
         if mask == 1:
             twin_ends = arrived[rows:]
         sums = sums + arrived[:rows]
         first = sums if first is None else first
-    return sums, twin_ends, first, early
+    return sums, twin_ends, other_ends, first, early
 
 
 def per_device(
@@ -364,11 +366,6 @@
     wire_after = jnp.where(even, arrived, crossed)
 
     cells, rows, depth = charge.shape
-    own_ends = jnp.concatenate(
-        [array[:, end] for array in (potential_old, permittivity) for end in (0, rows - 1)]
-    )
-    beyond = [(e, e + 1) for e in range(1, energies - 1, 2)]
-    other_ends = lax.ppermute(own_ends, "energy", beyond + [(b, a) for a, b in beyond])
     far, near = pl.BlockSpec(memory_space=pl.ANY), pl.BlockSpec(memory_space=pltpu.VMEM)
     sums, ends, *cuts = call(
         functools.partial(gather_kernel, rows, energies),
@@ -394,8 +391,10 @@
         ],
     )
     cuts = [first_cut, *cuts]
-    sums, twin_ends, crossed, (arrived, other_ends) = exchanged(
-        sums, ends, (free_first[0], other_ends)
+    beyond = [(e, e + 1) for e in range(1, energies - 1, 2)]
+    other_ends = lax.ppermute(ends, "energy", beyond + [(b, a) for a, b in beyond])
+    sums, twin_ends, other_ends, crossed, arrived = exchanged(
+        sums, ends, other_ends, free_first[0]
     )
 
     crossed, cuts[1] = lax.optimization_barrier((crossed, cuts[1]))

time: 113 us -> 118 us (1.044)
  starting transfers between devices: 24.7 us -> 34.9 us
  waiting for transfers between devices: 39.6 us -> 36 us
  local copies, waits for them, and re-layouts: 4.72 us -> 3.02 us
    ppermute x4, waiting for transfers between devices: 13.2 us -> 6.17 us  [sent_on(): free_second.append(lax.ppermute(given, 'energy', relay_pairs))]
    ppermute x1, starting transfers between devices: 3.71 us -> 8.06 us  [per_device(): lax.ppermute(onward, ('energy', 'slab'), both(second_pairs))]
    ppermute x1, waiting for transfers between devices: 5 us -> 8.5 us  [per_device(): lax.ppermute(onward, ('energy', 'slab'), both(second_pairs))]
    ppermute x1, waiting for transfers between devices: 0.01 us -> 2.7 us  [per_device(): lax.ppermute(ends, 'energy', beyond + [(b, a) for a, b in beyond])]
    ppermute x3, starting transfers between devices: 1.35 us -> 3.92 us  [exchanged(): lax.ppermute(given, 'energy', [(e, e ^ mask) for e in range(peers)])]
    ppermute x3, waiting for transfers between devices: 4.55 us -> 2.15 us  [exchanged(): lax.ppermute(given, 'energy', [(e, e ^ mask) for e in range(peers)])]
    ppermute x1, waiting for transfers between devices: 2.21 us -> 0.01 us  [per_device(): arrived = lax.ppermute(leaving, 'slab', swaps((peers - 2) % 2))]
    slice x2 -> x0, local copies, waits for them, and re-layouts: 1.7 us -> none  [per_device(): array[:, end]]
  transfers between devices with their start and end apart: 21 -> 21, of which waited for: 13 -> 13; matrix products, arithmetic and copies ran while one was open for 4% -> 3% of each run, Pallas kernels for 30% -> 28%
where the time goes in v17:
time: 118 us; the launch traced here: 117 us
  waiting for transfers between devices  36 us (31%)
  Pallas kernels  36 us (31%)
  starting transfers between devices  34.9 us (30%)
  other arithmetic  6.16 us (5%)
  local copies, waits for them, and re-layouts  3.02 us (3%)
    pallas_call x13, Pallas kernels, call(): pl.pallas_call(kernel, out_shape=out_shapes, cost_estimate=cost, compiler...  36 us
    ppermute x1, waiting for transfers between devices, per_device(): lax.ppermute(onward, ('energy', 'slab'), both(second_pairs))  8.5 us
    ppermute x1, starting transfers between devices, per_device(): lax.ppermute(onward, ('energy', 'slab'), both(second_pairs))  8.06 us
    ppermute x2, waiting for transfers between devices, per_device(): arrived = lax.ppermute(leaving, 'slab', swaps((hop - 1) % 2))  7.61 us
    ppermute x4, waiting for transfers between devices, sent_on(): free_second.append(lax.ppermute(given, 'energy', relay_pairs))  6.17 us
    ppermute x1, starting transfers between devices, per_device(): crossed = lax.ppermute(jnp.where(even, lower, upper), 'slab', swaps(1))  4.32 us
    ppermute x3, starting transfers between devices, exchanged(): lax.ppermute(given, 'energy', [(e, e ^ mask) for e in range(peers)])  3.92 us
    ppermute x2, starting transfers between devices, sent_after(): free_first.append(lax.ppermute(cut, 'energy', first_pairs))  3.72 us
  transfers between devices with their start and end apart: 21, of which 13 were waited for; matrix products, arithmetic and copies ran while one was open for 3% of the time, Pallas kernels for 28%

profile of v17, /device:TPU:13, one launch (start us, length us, event | category | flops | bytes accessed | tf_op | source)
XLA Modules:
  0.0 117.2 jit_solution(8931927834423350834)
XLA Ops:
  1.9 1.3 %collective-permute-start.2 = (f32[1,2,256,256]{3,2,1,0:T(8,128)S(1)}, f32[1,2,256,256]{3,2,1,0:T(8,128)S(1)}, u32[]{:S(2)}, u32[]{:S(2)}) collective-permute-start(f32[1,2,256,256]{3,2,1,0:T(8,128)S(1)} %slice_bitcast_fusion), channel_id=1, source_target_pairs={{0,8},{4,12},{8,0},{12,4},{16,24},{20,28},{24,16},{28,20},{1,9},{5... | collective-permute-start | bytes 1572872 | tf_op jit(solution)/shard_map/ppermute | solution.py:349
  4.2 4.3 %collective-permute-start = (f32[2,1,4,128]{3,2,0,1:T(4,128)S(1)}, f32[2,1,4,128]{3,2,0,1:T(4,128)S(1)}, u32[]{:S(2)}, u32[]{:S(2)}) collective-permute-start(f32[2,1,4,128]{3,2,0,1:T(4,128)S(1)} %get-tuple-element.143), channel_id=1, source_target_pairs={{1,2},{2,1},{5,6},{6,5},{9,10},{10,9},{13,14},{14,13},{17,18},{18,... | collective-permute-start | bytes 12296 | tf_op jit(solution)/shard_map/ppermute | solution.py:364
  10.4 3.6 %shard_map.113 = (f32[40,128]{1,0:T(8,128)}, f32[64,128]{1,0:T(8,128)}, f32[1,2,256,256]{3,2,1,0:T(8,128)}, f32[1,2,256,256]{3,2,1,0:T(8,128)}, f32[1,2,256,256]{3,2,1,0:T(8,128)}) custom-call(s32[1]{0:T(128)} %bitcast.2.mine, f32[64,128]{1,0:T(8,128)} %bitcast.48, f32[64,128]{1,0:T(8,128)} %bitcast.46, f32[64,128]{1,0:T(8,128)} %bitcast.49, ...), custom_call_target="tpu_custom_call" | custom-call | flops 301989888 | bytes 3833860 | tf_op jit(solution)/shard_map/pallas_call | solution.py:67
  15.9 1.6 %collective-permute-done.3 = f32[40,128]{1,0:T(8,128)S(1)} collective-permute-done((f32[40,128]{1,0:T(8,128)}, f32[40,128]{1,0:T(8,128)S(1)}, u32[]{:S(2)}, u32[]{:S(2)}) %collective-permute-start.3) | collective-permute-done | bytes 20512 | tf_op jit(solution)/shard_map/ppermute | solution.py:304
  19.1 2.7 %collective-permute-start.4 = (f32[104,128]{1,0:T(8,128)S(1)}, f32[104,128]{1,0:T(8,128)S(1)}, u32[]{:S(2)}, u32[]{:S(2)}) collective-permute-start(f32[104,128]{1,0:T(8,128)S(1)} %pad_maximum_fusion.1), channel_id=1, source_target_pairs={{0,4},{4,0},{8,12},{12,8},{16,20},{20,16},{24,28},{28,24},{1,5},{5... | collective-permute-start | bytes 159752 | tf_op jit(solution)/shard_map/ppermute | solution.py:304
  21.8 3.0 %collective-permute-start.5 = (f32[64,128]{1,0:T(8,128)}, f32[64,128]{1,0:T(8,128)S(1)}, u32[]{:S(2)}, u32[]{:S(2)}) collective-permute-start(f32[64,128]{1,0:T(8,128)} %get-tuple-element.74), channel_id=1, source_target_pairs={{4,8},{12,16},{20,24},{8,4},{16,12},{24,20},{5,9},{13,17},{21,25},... | collective-permute-start | bytes 98312 | tf_op jit(solution)/shard_map/ppermute | solution.py:395
  24.8 2.7 %collective-permute-done.5 = f32[64,128]{1,0:T(8,128)S(1)} collective-permute-done((f32[64,128]{1,0:T(8,128)}, f32[64,128]{1,0:T(8,128)S(1)}, u32[]{:S(2)}, u32[]{:S(2)}) %collective-permute-start.5) | collective-permute-done | bytes 32800 | tf_op jit(solution)/shard_map/ppermute | solution.py:395
  27.6 2.0 %collective-permute-start.8 = (f32[1,2,256,256]{3,2,1,0:T(8,128)}, f32[1,2,256,256]{3,2,1,0:T(8,128)S(1)}, u32[]{:S(2)}, u32[]{:S(2)}) collective-permute-start(f32[1,2,256,256]{3,2,1,0:T(8,128)} %get-tuple-element.83), channel_id=1, source_target_pairs={{0,8},{4,12},{8,0},{12,4},{16,24},{20,28},{24,16},{28,20},{1,9},{5... | collective-permute-start | bytes 1572872 | tf_op jit(solution)/shard_map/ppermute | solution.py:402
  30.1 1.6 %copy-done.1 = f32[4,2,256,256]{3,2,1,0:T(8,128)S(1)} copy-done((f32[4,2,256,256]{3,2,1,0:T(8,128)S(1)}, f32[4,2,256,256]{3,2,1,0:T(8,128)}, u32[]{:S(2)}) %copy-start.1) | copy-done | bytes 2097176
  31.7 6.3 %shard_map.114 = (f32[2,256,256]{2,1,0:T(8,128)S(1)}, f32[2,256,256]{2,1,0:T(8,128)S(1)}) custom-call(f32[4,2,256,256]{3,2,1,0:T(8,128)S(1)} %bitcast.43, f32[4,2,256,256]{3,2,1,0:T(8,128)S(1)} %copy-done.1, f32[40,128]{1,0:T(8,128)S(1)} %add.107.sums.refs_3_), custom_call_target="tpu_custom_call" | custom-call | flops 5133828096 | bytes 5263360 | tf_op jit(solution)/shard_map/pallas_call | solution.py:67
  38.5 3.3 %collective-permute-done.8.refs_1_ = f32[1,2,256,256]{3,2,1,0:T(8,128)S(1)} collective-permute-done((f32[1,2,256,256]{3,2,1,0:T(8,128)}, f32[1,2,256,256]{3,2,1,0:T(8,128)S(1)}, u32[]{:S(2)}, u32[]{:S(2)}) %collective-permute-start.8) | collective-permute-done | bytes 524320 | tf_op jit(solution)/shard_map/ppermute | solution.py:402
  41.8 1.9 %collective-permute-start.10 = (f32[1,2,256,256]{3,2,1,0:T(8,128)S(1)}, f32[1,2,256,256]{3,2,1,0:T(8,128)S(1)}, u32[]{:S(2)}, u32[]{:S(2)}) collective-permute-start(f32[1,2,256,256]{3,2,1,0:T(8,128)S(1)} %copy-done.13), channel_id=1, source_target_pairs={{0,8},{4,12},{8,0},{12,4},{16,24},{20,28},{24,16},{28,20},{1,9},{5... | collective-permute-start | bytes 1572872 | tf_op jit(solution)/shard_map/ppermute | solution.py:411
  44.2 5.5 %collective-permute-done.7.carried = f32[2,256,256]{2,1,0:T(8,128)S(1)} collective-permute-done((f32[2,256,256]{2,1,0:T(8,128)S(1)}, f32[2,256,256]{2,1,0:T(8,128)S(1)}, u32[]{:S(2)}, u32[]{:S(2)}) %collective-permute-start.7) | collective-permute-done | bytes 524320 | tf_op jit(solution)/shard_map/ppermute | solution.py:477
  50.6 3.5 %collective-permute-start.9 = (f32[2,256,256]{2,1,0:T(8,128)S(1)}, f32[2,256,256]{2,1,0:T(8,128)S(1)}, u32[]{:S(2)}, u32[]{:S(2)}) collective-permute-start(f32[2,256,256]{2,1,0:T(8,128)S(1)} %shard_map.115.before), channel_id=1, source_target_pairs={{1,2},{2,1},{5,6},{6,5},{9,10},{10,9},{13,14},{14,13},{17,18},{18,... | collective-permute-start | bytes 1572872 | tf_op jit(solution)/shard_map/ppermute | solution.py:477
  55.2 1.8 %collective-permute-start.14 = (f32[1,2,256,256]{3,2,1,0:T(8,128)S(1)}, f32[1,2,256,256]{3,2,1,0:T(8,128)S(1)}, u32[]{:S(2)}, u32[]{:S(2)}) collective-permute-start(f32[1,2,256,256]{3,2,1,0:T(8,128)S(1)} %copy-done.12), channel_id=1, source_target_pairs={{0,8},{4,12},{8,0},{12,4},{16,24},{20,28},{24,16},{28,20},{1,9},{5... | collective-permute-start | bytes 1572872 | tf_op jit(solution)/shard_map/ppermute | solution.py:411
  57.9 1.5 %shard_map.116 = (f32[2,2,256,256]{3,2,1,0:T(8,128)S(1)}, f32[2,2,256,256]{3,2,1,0:T(8,128)S(1)}) custom-call(f32[1,2,256,256]{3,2,1,0:T(8,128)S(1)} %collective-permute-done.2.refs_0_, f32[1,2,256,256]{3,2,1,0:T(8,128)S(1)} %collective-permute-done.8.refs_1_, f32[4,2,256,256]{3,2,1,0:T(8,128)S(1)} %copy-done.2, f32[40,128]{1,0:T(8,128)S(1)} %add.107.sums.refs_3_), custom_call_target="tpu_custom_call" | custom-call | flops 1207959552 | bytes 5263360 | tf_op jit(solution)/shard_map/pallas_call | solution.py:67
  59.4 1.7 %collective-permute-done.12.refs_1_ = f32[1,2,256,256]{3,2,1,0:T(8,128)S(1)} collective-permute-done((f32[1,2,256,256]{3,2,1,0:T(8,128)S(1)}, f32[1,2,256,256]{3,2,1,0:T(8,128)S(1)}, u32[]{:S(2)}, u32[]{:S(2)}) %collective-permute-start.12) | collective-permute-done | bytes 524320 | tf_op jit(solution)/shard_map/ppermute | solution.py:407
  61.1 2.1 %collective-permute-done.9.carried = f32[2,256,256]{2,1,0:T(8,128)S(1)} collective-permute-done((f32[2,256,256]{2,1,0:T(8,128)S(1)}, f32[2,256,256]{2,1,0:T(8,128)S(1)}, u32[]{:S(2)}, u32[]{:S(2)}) %collective-permute-start.9) | collective-permute-done | bytes 524320 | tf_op jit(solution)/shard_map/ppermute | solution.py:477
  64.2 8.1 %collective-permute-start.17 = (f32[2,256,256]{2,1,0:T(8,128)S(1)}, f32[2,256,256]{2,1,0:T(8,128)S(1)}, u32[]{:S(2)}, u32[]{:S(2)}) collective-permute-start(f32[2,256,256]{2,1,0:T(8,128)S(1)} %get-tuple-element.110), channel_id=1, source_target_pairs={{8,17},{9,18},{10,19},{12,21},{13,22},{14,23},{16,9},{17,10},{18,1... | collective-permute-start | bytes 1572872 | tf_op jit(solution)/shard_map/ppermute | solution.py:513
  72.3 1.5 %shard_map.119 = (f32[2,2,256,256]{3,2,1,0:T(8,128)S(1)}, f32[2,2,256,256]{3,2,1,0:T(8,128)S(1)}) custom-call(f32[1,2,256,256]{3,2,1,0:T(8,128)S(1)} %collective-permute-done.11.refs_0_, f32[1,2,256,256]{3,2,1,0:T(8,128)S(1)} %collective-permute-done.12.refs_1_, f32[4,2,256,256]{3,2,1,0:T(8,128)S(1)} %copy-done.2, f32[40,128]{1,0:T(8,128)S(1)} %add.107.sums.refs_3_), custom_call_target="tpu_custom_call" | custom-call | flops 1207959552 | bytes 5263360 | tf_op jit(solution)/shard_map/pallas_call | solution.py:67
  73.8 1.5 %shard_map.118 = (f32[2,2,256,256]{3,2,1,0:T(8,128)S(1)}, f32[2,2,256,256]{3,2,1,0:T(8,128)S(1)}) custom-call(f32[1,2,256,256]{3,2,1,0:T(8,128)S(1)} %collective-permute-done.10.refs_0_, f32[1,2,256,256]{3,2,1,0:T(8,128)S(1)} %collective-permute-done.14.refs_1_, f32[4,2,256,256]{3,2,1,0:T(8,128)S(1)} %copy-done.2, f32[40,128]{1,0:T(8,128)S(1)} %add.107.sums.refs_3_), custom_call_target="tpu_custom_call" | custom-call | flops 1207959552 | bytes 5263360 | tf_op jit(solution)/shard_map/pallas_call | solution.py:67
  75.7 7.5 %shard_map.120 = (f32[4,2,256,256]{3,2,1,0:T(8,128)S(1)}, f32[2,256,256]{2,1,0:T(8,128)}) custom-call(f32[4,2,256,256]{3,2,1,0:T(8,128)S(1)} %bitcast.44, f32[4,2,256,256]{3,2,1,0:T(8,128)S(1)} %copy-done.2, f32[40,128]{1,0:T(8,128)S(1)} %add.107.sums.refs_3_, f32[2,256,256]{2,1,0:T(8,128)S(1)} %broadcast_select_fusion.carried), custom_call_target="tpu_custom_call" | custom-call | flops 4831838208 | bytes 7360512 | tf_op jit(solution)/shard_map/pallas_call | solution.py:67
  83.2 8.5 %collective-permute-done.17.carried = f32[2,256,256]{2,1,0:T(8,128)S(1)} collective-permute-done((f32[2,256,256]{2,1,0:T(8,128)S(1)}, f32[2,256,256]{2,1,0:T(8,128)S(1)}, u32[]{:S(2)}, u32[]{:S(2)}) %collective-permute-start.17) | collective-permute-done | bytes 524320 | tf_op jit(solution)/shard_map/ppermute | solution.py:513
  91.7 4.5 %collective-permute-done.18.refs_1_ = f32[1,2,256,256]{3,2,1,0:T(8,128)S(1)} collective-permute-done((f32[1,2,256,256]{3,2,1,0:T(8,128)S(1)}, f32[1,2,256,256]{3,2,1,0:T(8,128)S(1)}, u32[]{:S(2)}, u32[]{:S(2)}) %collective-permute-start.18) | collective-permute-done | bytes 524320 | tf_op jit(solution)/shard_map/ppermute | solution.py:407
  96.3 1.5 %shard_map.122 = (f32[2,2,256,256]{3,2,1,0:T(8,128)S(1)}, f32[2,2,256,256]{3,2,1,0:T(8,128)S(1)}) custom-call(f32[1,2,256,256]{3,2,1,0:T(8,128)S(1)} %collective-permute-done.15.refs_0_, f32[1,2,256,256]{3,2,1,0:T(8,128)S(1)} %collective-permute-done.18.refs_1_, f32[4,2,256,256]{3,2,1,0:T(8,128)S(1)} %copy-done.2, f32[40,128]{1,0:T(8,128)S(1)} %add.107.sums.refs_3_), custom_call_target="tpu_custom_call" | custom-call | flops 1207959552 | bytes 5263360 | tf_op jit(solution)/shard_map/pallas_call | solution.py:67
  97.9 1.9 %shard_map.121 = (f32[2,2,256,256]{3,2,1,0:T(8,128)S(1)}, f32[2,256,256]{2,1,0:T(8,128)S(1)}) custom-call(f32[2,2,256,256]{3,2,1,0:T(8,128)S(1)} %get-tuple-element.108.link, f32[2,2,256,256]{3,2,1,0:T(8,128)S(1)} %get-tuple-element.109.source, f32[2,256,256]{2,1,0:T(8,128)S(1)} %collective-permute-done.17.carried), custom_call_target="tpu_custom_call" | custom-call | flops 1207959552 | bytes 4194304 | tf_op jit(solution)/shard_map/pallas_call | solution.py:67
  99.8 2.7 %shard_map.123 = (f32[2,2,256,256]{3,2,1,0:T(8,128)S(1)}, f32[2,256,256]{2,1,0:T(8,128)}) custom-call(f32[2,2,256,256]{3,2,1,0:T(8,128)S(1)} %get-tuple-element.116.link, f32[2,2,256,256]{3,2,1,0:T(8,128)S(1)} %get-tuple-element.117.source, f32[2,256,256]{2,1,0:T(8,128)S(1)} %get-tuple-element.118.carried), custom_call_target="tpu_custom_call" | custom-call | flops 1207959552 | bytes 4194304 | tf_op jit(solution)/shard_map/pallas_call | solution.py:67
  103.3 2.7 %shard_map.124 = (f32[2,2,256,256]{3,2,1,0:T(8,128)S(1)}, f32[2,2,256,256]{3,2,1,0:T(8,128)S(1)}, f32[2,256,256]{2,1,0:T(8,128)S(1)}) custom-call(s32[2]{0:T(128)S(1)} %pad_add_fusion.pick, f32[2,2,256,256]{3,2,1,0:T(8,128)S(1)} %get-tuple-element.124.link, f32[2,2,256,256]{3,2,1,0:T(8,128)S(1)} %get-tuple-element.125.source, ...), custom_call_target="tpu_custom_call" | custom-call | flops 1207959552 | bytes 9437192 | tf_op jit(solution)/shard_map/pallas_call | solution.py:67
  106.0 3.3 %collective-permute-start.19 = (f32[2,2,256,256]{3,2,1,0:T(8,128)S(1)}, f32[2,2,256,256]{3,2,1,0:T(8,128)S(1)}, u32[]{:S(2)}, u32[]{:S(2)}) collective-permute-start(f32[2,2,256,256]{3,2,1,0:T(8,128)S(1)} %get-tuple-element.131), channel_id=1, source_target_pairs={{0,4},{4,0},{8,12},{12,8},{16,20},{20,16},{24,28},{28,24},{1,5},{5... | collective-permute-start | bytes 3145736 | tf_op jit(solution)/shard_map/ppermute | solution.py:581
  109.2 3.4 %shard_map.125 = (f32[2,2,256,256]{3,2,1,0:T(8,128)S(1)}, f32[2,2,256,256]{3,2,1,0:T(8,128)S(1)}, f32[2,256,256]{2,1,0:T(8,128)}) custom-call(s32[2]{0:T(128)S(1)} %pad_add_fusion.pick, f32[2,2,256,256]{3,2,1,0:T(8,128)S(1)} %get-tuple-element.132.link, f32[2,2,256,256]{3,2,1,0:T(8,128)S(1)} %get-tuple-element.133.source, ...), custom_call_target="tpu_custom_call" | custom-call | flops 1207959552 | bytes 9437192 | tf_op jit(solution)/shard_map/pallas_call | solution.py:67
  112.9 2.6 %collective-permute-done.20 = f32[2,2,256,256]{3,2,1,0:T(8,128)S(1)} collective-permute-done((f32[2,2,256,256]{3,2,1,0:T(8,128)S(1)}, f32[2,2,256,256]{3,2,1,0:T(8,128)S(1)}, u32[]{:S(2)}, u32[]{:S(2)}) %collective-permute-start.20) | collective-permute-done | bytes 1048608 | tf_op jit(solution)/shard_map/ppermute | solution.py:581
  115.7 1.5 %maximum_bitcast_fusion = f32[1,4,2,256,256]{4,3,2,1,0:T(8,128)} fusion(f32[2,2,256,256]{3,2,1,0:T(8,128)S(1)} %add.131, f32[2,2,256,256]{3,2,1,0:T(8,128)S(1)} %add.130), kind=kLoop, calls=%fused_computation.1 | loop fusion | flops 524288 | bytes 4194304 | tf_op jit(solution)/shard_map/broadcast_in_dim | solution.py:582
  (75 shorter events, 14.5 us)
Async XLA Ops:
  0.6 29.5 %copy-start = (f32[1,4,2,256,256]{4,3,2,1,0:T(8,128)S(1)}, f32[1,4,2,256,256]{4,3,2,1,0:T(8,128)}, u32[]{:S(2)}) copy-start(f32[1,4,2,256,256]{4,3,2,1,0:T(8,128)} %param.14) | copy-start | bytes 6291460
  1.9 12.9 %collective-permute-start.2 = (f32[1,2,256,256]{3,2,1,0:T(8,128)S(1)}, f32[1,2,256,256]{3,2,1,0:T(8,128)S(1)}, u32[]{:S(2)}, u32[]{:S(2)}) collective-permute-start(f32[1,2,256,256]{3,2,1,0:T(8,128)S(1)} %slice_bitcast_fusion), channel_id=1, source_target_pairs={{0,8},{4,12},{8,0},{12,4},{16,24},{20,28},{24,16},{28,20},{1,9},{5... | collective-permute-start | bytes 1572872 | tf_op jit(solution)/shard_map/ppermute | solution.py:349
  4.0 4.6 %collective-permute-start.1 = (f32[2,1,4,128]{3,2,0,1:T(4,128)S(1)}, f32[2,1,4,128]{3,2,0,1:T(4,128)S(1)}, u32[]{:S(2)}, u32[]{:S(2)}) collective-permute-start(f32[2,1,4,128]{3,2,0,1:T(4,128)S(1)} %get-tuple-element.142), channel_id=1, source_target_pairs={{0,1},{2,3},{1,0},{3,2},{4,5},{6,7},{5,4},{7,6},{8,9},{10,11},{9,8... | collective-permute-start | bytes 12296 | tf_op jit(solution)/shard_map/ppermute | solution.py:363
  4.2 5.6 %collective-permute-start = (f32[2,1,4,128]{3,2,0,1:T(4,128)S(1)}, f32[2,1,4,128]{3,2,0,1:T(4,128)S(1)}, u32[]{:S(2)}, u32[]{:S(2)}) collective-permute-start(f32[2,1,4,128]{3,2,0,1:T(4,128)S(1)} %get-tuple-element.143), channel_id=1, source_target_pairs={{1,2},{2,1},{5,6},{6,5},{9,10},{10,9},{13,14},{14,13},{17,18},{18,... | collective-permute-start | bytes 12296 | tf_op jit(solution)/shard_map/ppermute | solution.py:364
  14.7 2.8 %collective-permute-start.3 = (f32[40,128]{1,0:T(8,128)}, f32[40,128]{1,0:T(8,128)S(1)}, u32[]{:S(2)}, u32[]{:S(2)}) collective-permute-start(f32[40,128]{1,0:T(8,128)} %get-tuple-element.73), channel_id=1, source_target_pairs={{0,8},{4,12},{8,0},{12,4},{16,24},{20,28},{24,16},{28,20},{1,9},{5... | collective-permute-start | bytes 61448 | tf_op jit(solution)/shard_map/ppermute | solution.py:304
  19.1 5.7 %collective-permute-start.4 = (f32[104,128]{1,0:T(8,128)S(1)}, f32[104,128]{1,0:T(8,128)S(1)}, u32[]{:S(2)}, u32[]{:S(2)}) collective-permute-start(f32[104,128]{1,0:T(8,128)S(1)} %pad_maximum_fusion.1), channel_id=1, source_target_pairs={{0,4},{4,0},{8,12},{12,8},{16,20},{20,16},{24,28},{28,24},{1,5},{5... | collective-permute-start | bytes 159752 | tf_op jit(solution)/shard_map/ppermute | solution.py:304
  21.8 5.7 %collective-permute-start.5 = (f32[64,128]{1,0:T(8,128)}, f32[64,128]{1,0:T(8,128)S(1)}, u32[]{:S(2)}, u32[]{:S(2)}) collective-permute-start(f32[64,128]{1,0:T(8,128)} %get-tuple-element.74), channel_id=1, source_target_pairs={{4,8},{12,16},{20,24},{8,4},{16,12},{24,20},{5,9},{13,17},{21,25},... | collective-permute-start | bytes 98312 | tf_op jit(solution)/shard_map/ppermute | solution.py:395
  27.5 2.6 %collective-permute-start.6 = (f32[40,128]{1,0:T(8,128)S(1)}, f32[40,128]{1,0:T(8,128)S(1)}, u32[]{:S(2)}, u32[]{:S(2)}) collective-permute-start(f32[40,128]{1,0:T(8,128)S(1)} %slice_add_fusion), channel_id=1, source_target_pairs={{0,16},{4,20},{8,24},{12,28},{16,0},{20,4},{24,8},{28,12},{1,17},{... | collective-permute-start | bytes 61448 | tf_op jit(solution)/shard_map/ppermute | solution.py:304
  27.6 14.2 %collective-permute-start.8 = (f32[1,2,256,256]{3,2,1,0:T(8,128)}, f32[1,2,256,256]{3,2,1,0:T(8,128)S(1)}, u32[]{:S(2)}, u32[]{:S(2)}) collective-permute-start(f32[1,2,256,256]{3,2,1,0:T(8,128)} %get-tuple-element.83), channel_id=1, source_target_pairs={{0,8},{4,12},{8,0},{12,4},{16,24},{20,28},{24,16},{28,20},{1,9},{5... | collective-permute-start | bytes 1572872 | tf_op jit(solution)/shard_map/ppermute | solution.py:402
  31.7 6.6 %copy-start.10 = (s32[4]{0:T(128)S(1)}, s32[4]{0:T(128)}, u32[]{:S(2)}) copy-start(s32[4]{0:T(128)} %param.16) | copy-start | bytes 52
  31.7 6.6 %copy-start.11 = (s32[4]{0:T(128)S(1)}, s32[4]{0:T(128)}, u32[]{:S(2)}) copy-start(s32[4]{0:T(128)} %constant.57.clone) | copy-start | bytes 52
  31.7 10.0 %copy-start.13 = (f32[1,2,256,256]{3,2,1,0:T(8,128)S(1)}, f32[1,2,256,256]{3,2,1,0:T(8,128)}, u32[]{:S(2)}) copy-start(f32[1,2,256,256]{3,2,1,0:T(8,128)} %get-tuple-element.89) | copy-start | bytes 1572868
  31.7 12.0 %copy-start.5 = (f32[4,256,256]{2,1,0:T(8,128)S(1)}, f32[4,256,256]{2,1,0:T(8,128)}, u32[]{:S(2)}) copy-start(f32[4,256,256]{2,1,0:T(8,128)} %param.18) | copy-start | bytes 3145732
  38.1 11.6 %collective-permute-start.7 = (f32[2,256,256]{2,1,0:T(8,128)S(1)}, f32[2,256,256]{2,1,0:T(8,128)S(1)}, u32[]{:S(2)}, u32[]{:S(2)}) collective-permute-start(f32[2,256,256]{2,1,0:T(8,128)S(1)} %get-tuple-element.80.whole_source), channel_id=1, source_target_pairs={{0,1},{2,3},{1,0},{3,2},{4,5},{6,7},{5,4},{7,6},{8,9},{10,11},{9,8... | collective-permute-start | bytes 1572872 | tf_op jit(solution)/shard_map/ppermute | solution.py:477
  38.4 20.9 %collective-permute-start.11 = (f32[1,2,256,256]{3,2,1,0:T(8,128)S(1)}, f32[1,2,256,256]{3,2,1,0:T(8,128)S(1)}, u32[]{:S(2)}, u32[]{:S(2)}) collective-permute-start(f32[1,2,256,256]{3,2,1,0:T(8,128)S(1)} %collective-permute-done.2.refs_0_), channel_id=1, source_target_pairs={{0,16},{4,20},{8,24},{12,28},{16,0},{20,4},{24,8},{28,12},{1,17},{... | collective-permute-start | bytes 1572872 | tf_op jit(solution)/shard_map/ppermute | solution.py:407
  41.8 12.3 %copy-start.7 = (f32[1,1,8,128]{3,2,0,1:T(8,128)S(1)}, f32[1,1,8,128]{3,2,0,1:T(8,128)}, u32[]{:S(2)}) copy-start(f32[1,1,8,128]{3,2,0,1:T(8,128)} %get-tuple-element.174) | copy-start | bytes 12292
  41.8 12.3 %copy-start.8 = (f32[1,1,8,128]{3,2,0,1:T(8,128)S(1)}, f32[1,1,8,128]{3,2,0,1:T(8,128)}, u32[]{:S(2)}) copy-start(f32[1,1,8,128]{3,2,0,1:T(8,128)} %get-tuple-element.175) | copy-start | bytes 12292
  41.8 13.4 %copy-start.12 = (f32[1,2,256,256]{3,2,1,0:T(8,128)S(1)}, f32[1,2,256,256]{3,2,1,0:T(8,128)}, u32[]{:S(2)}) copy-start(f32[1,2,256,256]{3,2,1,0:T(8,128)} %get-tuple-element.100) | copy-start | bytes 1572868
  41.8 16.1 %copy-start.2 = (f32[4,2,256,256]{3,2,1,0:T(8,128)S(1)}, f32[4,2,256,256]{3,2,1,0:T(8,128)}, u32[]{:S(2)}) copy-start(f32[4,2,256,256]{3,2,1,0:T(8,128)} %refs_2_.7) | copy-start | bytes 6291460
  41.8 13.4 %collective-permute-start.10 = (f32[1,2,256,256]{3,2,1,0:T(8,128)S(1)}, f32[1,2,256,256]{3,2,1,0:T(8,128)S(1)}, u32[]{:S(2)}, u32[]{:S(2)}) collective-permute-start(f32[1,2,256,256]{3,2,1,0:T(8,128)S(1)} %copy-done.13), channel_id=1, source_target_pairs={{0,8},{4,12},{8,0},{12,4},{16,24},{20,28},{24,16},{28,20},{1,9},{5... | collective-permute-start | bytes 1572872 | tf_op jit(solution)/shard_map/ppermute | solution.py:411
  44.1 17.0 %collective-permute-start.12 = (f32[1,2,256,256]{3,2,1,0:T(8,128)S(1)}, f32[1,2,256,256]{3,2,1,0:T(8,128)S(1)}, u32[]{:S(2)}, u32[]{:S(2)}) collective-permute-start(f32[1,2,256,256]{3,2,1,0:T(8,128)S(1)} %collective-permute-done.8.refs_1_), channel_id=1, source_target_pairs={{0,16},{4,20},{8,24},{12,28},{16,0},{20,4},{24,8},{28,12},{1,17},{... | collective-permute-start | bytes 1572872 | tf_op jit(solution)/shard_map/ppermute | solution.py:407
  50.6 12.5 %collective-permute-start.9 = (f32[2,256,256]{2,1,0:T(8,128)S(1)}, f32[2,256,256]{2,1,0:T(8,128)S(1)}, u32[]{:S(2)}, u32[]{:S(2)}) collective-permute-start(f32[2,256,256]{2,1,0:T(8,128)S(1)} %shard_map.115.before), channel_id=1, source_target_pairs={{1,2},{2,1},{5,6},{6,5},{9,10},{10,9},{13,14},{14,13},{17,18},{18,... | collective-permute-start | bytes 1572872 | tf_op jit(solution)/shard_map/ppermute | solution.py:477
  55.2 18.6 %collective-permute-start.14 = (f32[1,2,256,256]{3,2,1,0:T(8,128)S(1)}, f32[1,2,256,256]{3,2,1,0:T(8,128)S(1)}, u32[]{:S(2)}, u32[]{:S(2)}) collective-permute-start(f32[1,2,256,256]{3,2,1,0:T(8,128)S(1)} %copy-done.12), channel_id=1, source_target_pairs={{0,8},{4,12},{8,0},{12,4},{16,24},{20,28},{24,16},{28,20},{1,9},{5... | collective-permute-start | bytes 1572872 | tf_op jit(solution)/shard_map/ppermute | solution.py:411
  57.0 18.4 %collective-permute-start.15 = (f32[1,2,256,256]{3,2,1,0:T(8,128)S(1)}, f32[1,2,256,256]{3,2,1,0:T(8,128)S(1)}, u32[]{:S(2)}, u32[]{:S(2)}) collective-permute-start(f32[1,2,256,256]{3,2,1,0:T(8,128)S(1)} %collective-permute-done.10.refs_0_), channel_id=1, source_target_pairs={{0,16},{4,20},{8,24},{12,28},{16,0},{20,4},{24,8},{28,12},{1,17},{... | collective-permute-start | bytes 1572872 | tf_op jit(solution)/shard_map/ppermute | solution.py:407
  64.1 11.3 %collective-permute-start.13 = (f32[2,256,256]{2,1,0:T(8,128)S(1)}, f32[2,256,256]{2,1,0:T(8,128)S(1)}, u32[]{:S(2)}, u32[]{:S(2)}) collective-permute-start(f32[2,256,256]{2,1,0:T(8,128)S(1)} %get-tuple-element.98), channel_id=1, source_target_pairs={{0,1},{2,3},{1,0},{3,2},{4,5},{6,7},{5,4},{7,6},{8,9},{10,11},{9,8... | collective-permute-start | bytes 1572872 | tf_op jit(solution)/shard_map/ppermute | solution.py:512
  64.2 27.5 %collective-permute-start.17 = (f32[2,256,256]{2,1,0:T(8,128)S(1)}, f32[2,256,256]{2,1,0:T(8,128)S(1)}, u32[]{:S(2)}, u32[]{:S(2)}) collective-permute-start(f32[2,256,256]{2,1,0:T(8,128)S(1)} %get-tuple-element.110), channel_id=1, source_target_pairs={{8,17},{9,18},{10,19},{12,21},{13,22},{14,23},{16,9},{17,10},{18,1... | collective-permute-start | bytes 1572872 | tf_op jit(solution)/shard_map/ppermute | solution.py:513
  73.7 22.4 %collective-permute-start.18 = (f32[1,2,256,256]{3,2,1,0:T(8,128)S(1)}, f32[1,2,256,256]{3,2,1,0:T(8,128)S(1)}, u32[]{:S(2)}, u32[]{:S(2)}) collective-permute-start(f32[1,2,256,256]{3,2,1,0:T(8,128)S(1)} %collective-permute-done.14.refs_1_), channel_id=1, source_target_pairs={{0,16},{4,20},{8,24},{12,28},{16,0},{20,4},{24,8},{28,12},{1,17},{... | collective-permute-start | bytes 1572872 | tf_op jit(solution)/shard_map/ppermute | solution.py:407
  75.5 20.7 %copy-start.3 = (f32[16,4,128]{2,1,0:T(4,128)S(1)}, f32[16,4,128]{2,1,0:T(4,128)}, u32[]{:S(2)}) copy-start(f32[16,4,128]{2,1,0:T(4,128)} %param.12) | copy-start | bytes 98308
  75.5 20.7 %copy-start.4 = (f32[16,4,128]{2,1,0:T(4,128)S(1)}, f32[16,4,128]{2,1,0:T(4,128)}, u32[]{:S(2)}) copy-start(f32[16,4,128]{2,1,0:T(4,128)} %param.10) | copy-start | bytes 98308
  75.5 27.8 %collective-permute-start.16 = (f32[2,256,256]{2,1,0:T(8,128)S(1)}, f32[2,256,256]{2,1,0:T(8,128)S(1)}, u32[]{:S(2)}, u32[]{:S(2)}) collective-permute-start(f32[2,256,256]{2,1,0:T(8,128)S(1)} %broadcast_select_fusion.carried), channel_id=1, source_target_pairs={{0,8},{4,12},{8,0},{12,4},{16,24},{20,28},{24,16},{28,20},{1,9},{5... | collective-permute-start | bytes 1572872 | tf_op jit(solution)/shard_map/ppermute | solution.py:521
  106.0 6.7 %collective-permute-start.19 = (f32[2,2,256,256]{3,2,1,0:T(8,128)S(1)}, f32[2,2,256,256]{3,2,1,0:T(8,128)S(1)}, u32[]{:S(2)}, u32[]{:S(2)}) collective-permute-start(f32[2,2,256,256]{3,2,1,0:T(8,128)S(1)} %get-tuple-element.131), channel_id=1, source_target_pairs={{0,4},{4,0},{8,12},{12,8},{16,20},{20,16},{24,28},{28,24},{1,5},{5... | collective-permute-start | bytes 3145736 | tf_op jit(solution)/shard_map/ppermute | solution.py:581
  112.8 2.7 %collective-permute-start.20 = (f32[2,2,256,256]{3,2,1,0:T(8,128)S(1)}, f32[2,2,256,256]{3,2,1,0:T(8,128)S(1)}, u32[]{:S(2)}, u32[]{:S(2)}) collective-permute-start(f32[2,2,256,256]{3,2,1,0:T(8,128)S(1)} %get-tuple-element.139), channel_id=1, source_target_pairs={{0,4},{4,0},{8,12},{12,8},{16,20},{20,16},{24,28},{28,24},{1,5},{5... | collective-permute-start | bytes 3145736 | tf_op jit(solution)/shard_map/ppermute | solution.py:581
  (3 other events, 11.0 us)

commit v18 on v16

--- a/solution.py
+++ b/solution.py
@@ -303,7 +303,7 @@
         if mask == 1:
             twin_ends = arrived[rows:]
         sums = sums + arrived[:rows]
-        first = sums if first is None else first
+        first = arrived if first is None else first
     return sums, twin_ends, first, early
 
 
@@ -364,11 +364,8 @@
     wire_after = jnp.where(even, arrived, crossed)
 
     cells, rows, depth = charge.shape
-    own_ends = jnp.concatenate(
-        [array[:, end] for array in (potential_old, permittivity) for end in (0, rows - 1)]
-    )
     beyond = [(e, e + 1) for e in range(1, energies - 1, 2)]
-    other_ends = lax.ppermute(own_ends, "energy", beyond + [(b, a) for a, b in beyond])
+    other_ends = lax.ppermute(stacked, "energy", beyond + [(b, a) for a, b in beyond])
     far, near = pl.BlockSpec(memory_space=pl.ANY), pl.BlockSpec(memory_space=pltpu.VMEM)
     sums, ends, *cuts = call(
         functools.partial(gather_kernel, rows, energies),
@@ -537,10 +534,11 @@
         (carried_second, greens, free_second[3], potential_old, permittivity)
     )
 
-    ends_before = jnp.where(odd == 1, twin_ends, other_ends).reshape(2, 2, cells, 1, depth)
-    ends_after = jnp.where(odd == 1, other_ends, twin_ends).reshape(2, 2, cells, 1, depth)
+    twin_ends = twin_ends.reshape(2, 2, cells, 1, depth)
+    ends_before = jnp.where(odd == 1, twin_ends[:, 1], other_ends[:, :, rows - 1 :])
+    ends_after = jnp.where(odd == 1, other_ends[:, :, :1], twin_ends[:, 0])
     edge = jnp.zeros((2, cells, rows, 1), jnp.float32)
-    halos = ((wire_before, wire_after), (ends_before[:, 1], ends_after[:, 0]), (edge, edge))
+    halos = ((wire_before, wire_after), (ends_before, ends_after), (edge, edge))
     potential_new = relaxed(field, perm, charge, halos)
 
     beside_second[1] = beside(1, free_second[2:])

time: 113 us -> 113 us (level)
  starting transfers between devices: 24.7 us -> 27.9 us
  waiting for transfers between devices: 39.6 us -> 37.3 us
  local copies, waits for them, and re-layouts: 4.72 us -> 3.07 us
    slice x4 -> x2, local copies, waits for them, and re-layouts: 1.71 us -> 0.01 us  [the longest x1 0.01 us: per_device(): twin_ends[:, 1]]
    ppermute x4, waiting for transfers between devices: 13.2 us -> 11.8 us  [sent_on(): free_second.append(lax.ppermute(given, 'energy', relay_pairs))]
  transfers between devices with their start and end apart: 21 -> 21, of which waited for: 13 -> 13; matrix products, arithmetic and copies ran while one was open for 4% -> 3% of each run, Pallas kernels for 30% -> 30%
where the time goes in v18:
time: 113 us; the launch traced here: 112 us
  waiting for transfers between devices  37.3 us (33%)
  Pallas kernels  36 us (32%)
  starting transfers between devices  27.9 us (25%)
  other arithmetic  6.2 us (5%)
  local copies, waits for them, and re-layouts  3.07 us (3%)
    pallas_call x13, Pallas kernels, call(): pl.pallas_call(kernel, out_shape=out_shapes, cost_estimate=cost, compiler...  36 us
    ppermute x4, waiting for transfers between devices, sent_on(): free_second.append(lax.ppermute(given, 'energy', relay_pairs))  11.8 us
    ppermute x2, waiting for transfers between devices, per_device(): arrived = lax.ppermute(leaving, 'slab', swaps((hop - 1) % 2))  8.88 us
    ppermute x3, waiting for transfers between devices, exchanged(): lax.ppermute(given, 'energy', [(e, e ^ mask) for e in range(peers)])  4.99 us
    ppermute x1, starting transfers between devices, per_device(): crossed = lax.ppermute(jnp.where(even, lower, upper), 'slab', swaps(1))  4.32 us
    ppermute x1, starting transfers between devices, per_device(): lax.ppermute(onward, ('energy', 'slab'), both(second_pairs))  4.26 us
    ppermute x1, waiting for transfers between devices, per_device(): lax.ppermute(onward, ('energy', 'slab'), both(second_pairs))  3.95 us
    ppermute x1, starting transfers between devices, per_device(): lax.ppermute(stacked, 'energy', beyond + [(b, a) for a, b in beyond])  3.56 us
  transfers between devices with their start and end apart: 21, of which 13 were waited for; matrix products, arithmetic and copies ran while one was open for 3% of the time, Pallas kernels for 30%

profile of v18, /device:TPU:13, one launch (start us, length us, event | category | flops | bytes accessed | tf_op | source)
XLA Modules:
  0.0 111.6 jit_solution(4068405334724276568)
XLA Ops:
  1.9 1.3 %collective-permute-start.2 = (f32[1,2,256,256]{3,2,1,0:T(8,128)S(1)}, f32[1,2,256,256]{3,2,1,0:T(8,128)S(1)}, u32[]{:S(2)}, u32[]{:S(2)}) collective-permute-start(f32[1,2,256,256]{3,2,1,0:T(8,128)S(1)} %slice_bitcast_fusion), channel_id=1, source_target_pairs={{0,8},{4,12},{8,0},{12,4},{16,24},{20,28},{24,16},{28,20},{1,9},{5... | collective-permute-start | bytes 1572872 | tf_op jit(solution)/shard_map/ppermute | solution.py:347
  4.2 4.3 %collective-permute-start = (f32[2,1,4,128]{3,2,0,1:T(4,128)S(1)}, f32[2,1,4,128]{3,2,0,1:T(4,128)S(1)}, u32[]{:S(2)}, u32[]{:S(2)}) collective-permute-start(f32[2,1,4,128]{3,2,0,1:T(4,128)S(1)} %get-tuple-element.141), channel_id=1, source_target_pairs={{1,2},{2,1},{5,6},{6,5},{9,10},{10,9},{13,14},{14,13},{17,18},{18,... | collective-permute-start | bytes 12296 | tf_op jit(solution)/shard_map/ppermute | solution.py:362
  8.5 3.6 %collective-permute-start.3 = (f32[2,16,4,128]{3,2,0,1:T(4,128)S(1)}, f32[2,16,4,128]{3,2,0,1:T(4,128)S(1)}, u32[]{:S(2)}, u32[]{:S(2)}) collective-permute-start(f32[2,16,4,128]{3,2,0,1:T(4,128)S(1)} %pad_maximum_fusion), channel_id=1, source_target_pairs={{4,8},{12,16},{20,24},{8,4},{16,12},{24,20},{5,9},{13,17},{21,25},... | collective-permute-start | bytes 196616 | tf_op jit(solution)/shard_map/ppermute | solution.py:368
  12.7 3.6 %shard_map.113 = (f32[40,128]{1,0:T(8,128)}, f32[64,128]{1,0:T(8,128)}, f32[1,2,256,256]{3,2,1,0:T(8,128)}, f32[1,2,256,256]{3,2,1,0:T(8,128)}, f32[1,2,256,256]{3,2,1,0:T(8,128)}) custom-call(s32[1]{0:T(128)} %bitcast.2.mine, f32[64,128]{1,0:T(8,128)} %bitcast.57, f32[64,128]{1,0:T(8,128)} %bitcast.55, f32[64,128]{1,0:T(8,128)} %bitcast.58, ...), custom_call_target="tpu_custom_call" | custom-call | flops 301989888 | bytes 3833860 | tf_op jit(solution)/shard_map/pallas_call | solution.py:67
  16.6 2.8 %collective-permute-done.4 = f32[40,128]{1,0:T(8,128)S(1)} collective-permute-done((f32[40,128]{1,0:T(8,128)}, f32[40,128]{1,0:T(8,128)S(1)}, u32[]{:S(2)}, u32[]{:S(2)}) %collective-permute-start.4) | collective-permute-done | bytes 20512 | tf_op jit(solution)/shard_map/ppermute | solution.py:302
  20.9 1.9 %collective-permute-start.5 = (f32[104,128]{1,0:T(8,128)S(1)}, f32[104,128]{1,0:T(8,128)S(1)}, u32[]{:S(2)}, u32[]{:S(2)}) collective-permute-start(f32[104,128]{1,0:T(8,128)S(1)} %pad_maximum_fusion.1), channel_id=1, source_target_pairs={{0,4},{4,0},{8,12},{12,8},{16,20},{20,16},{24,28},{28,24},{1,5},{5... | collective-permute-start | bytes 159752 | tf_op jit(solution)/shard_map/ppermute | solution.py:302
  23.8 1.3 %collective-permute-start.8 = (f32[1,2,256,256]{3,2,1,0:T(8,128)}, f32[1,2,256,256]{3,2,1,0:T(8,128)S(1)}, u32[]{:S(2)}, u32[]{:S(2)}) collective-permute-start(f32[1,2,256,256]{3,2,1,0:T(8,128)} %get-tuple-element.81), channel_id=1, source_target_pairs={{0,8},{4,12},{8,0},{12,4},{16,24},{20,28},{24,16},{28,20},{1,9},{5... | collective-permute-start | bytes 1572872 | tf_op jit(solution)/shard_map/ppermute | solution.py:400
  25.0 1.3 %collective-permute-done.6 = f32[40,128]{1,0:T(8,128)S(1)} collective-permute-done((f32[40,128]{1,0:T(8,128)S(1)}, f32[40,128]{1,0:T(8,128)S(1)}, u32[]{:S(2)}, u32[]{:S(2)}) %collective-permute-start.6) | collective-permute-done | bytes 20512 | tf_op jit(solution)/shard_map/ppermute | solution.py:302
  26.3 1.6 %copy-done.1 = f32[4,2,256,256]{3,2,1,0:T(8,128)S(1)} copy-done((f32[4,2,256,256]{3,2,1,0:T(8,128)S(1)}, f32[4,2,256,256]{3,2,1,0:T(8,128)}, u32[]{:S(2)}) %copy-start.1) | copy-done | bytes 2097176
  27.9 6.3 %shard_map.114 = (f32[2,256,256]{2,1,0:T(8,128)S(1)}, f32[2,256,256]{2,1,0:T(8,128)S(1)}) custom-call(f32[4,2,256,256]{3,2,1,0:T(8,128)S(1)} %bitcast.52, f32[4,2,256,256]{3,2,1,0:T(8,128)S(1)} %copy-done.1, f32[40,128]{1,0:T(8,128)S(1)} %add.107.sums.refs_3_), custom_call_target="tpu_custom_call" | custom-call | flops 5133828096 | bytes 5263360 | tf_op jit(solution)/shard_map/pallas_call | solution.py:67
  34.5 2.6 %collective-permute-done.8.refs_1_ = f32[1,2,256,256]{3,2,1,0:T(8,128)S(1)} collective-permute-done((f32[1,2,256,256]{3,2,1,0:T(8,128)}, f32[1,2,256,256]{3,2,1,0:T(8,128)S(1)}, u32[]{:S(2)}, u32[]{:S(2)}) %collective-permute-start.8) | collective-permute-done | bytes 524320 | tf_op jit(solution)/shard_map/ppermute | solution.py:400
  39.7 6.5 %collective-permute-done.7.carried = f32[2,256,256]{2,1,0:T(8,128)S(1)} collective-permute-done((f32[2,256,256]{2,1,0:T(8,128)S(1)}, f32[2,256,256]{2,1,0:T(8,128)S(1)}, u32[]{:S(2)}, u32[]{:S(2)}) %collective-permute-start.7) | collective-permute-done | bytes 524320 | tf_op jit(solution)/shard_map/ppermute | solution.py:475
  47.1 2.8 %collective-permute-start.9 = (f32[2,256,256]{2,1,0:T(8,128)S(1)}, f32[2,256,256]{2,1,0:T(8,128)S(1)}, u32[]{:S(2)}, u32[]{:S(2)}) collective-permute-start(f32[2,256,256]{2,1,0:T(8,128)S(1)} %shard_map.115.before), channel_id=1, source_target_pairs={{1,2},{2,1},{5,6},{6,5},{9,10},{10,9},{13,14},{14,13},{17,18},{18,... | collective-permute-start | bytes 1572872 | tf_op jit(solution)/shard_map/ppermute | solution.py:475
  50.0 1.6 %collective-permute-start.14 = (f32[1,2,256,256]{3,2,1,0:T(8,128)S(1)}, f32[1,2,256,256]{3,2,1,0:T(8,128)S(1)}, u32[]{:S(2)}, u32[]{:S(2)}) collective-permute-start(f32[1,2,256,256]{3,2,1,0:T(8,128)S(1)} %copy-done.12), channel_id=1, source_target_pairs={{0,8},{4,12},{8,0},{12,4},{16,24},{20,28},{24,16},{28,20},{1,9},{5... | collective-permute-start | bytes 1572872 | tf_op jit(solution)/shard_map/ppermute | solution.py:409
  52.2 1.5 %shard_map.116 = (f32[2,2,256,256]{3,2,1,0:T(8,128)S(1)}, f32[2,2,256,256]{3,2,1,0:T(8,128)S(1)}) custom-call(f32[1,2,256,256]{3,2,1,0:T(8,128)S(1)} %collective-permute-done.2.refs_0_, f32[1,2,256,256]{3,2,1,0:T(8,128)S(1)} %collective-permute-done.8.refs_1_, f32[4,2,256,256]{3,2,1,0:T(8,128)S(1)} %copy-done.2, f32[40,128]{1,0:T(8,128)S(1)} %add.107.sums.refs_3_), custom_call_target="tpu_custom_call" | custom-call | flops 1207959552 | bytes 5263360 | tf_op jit(solution)/shard_map/pallas_call | solution.py:67
  53.7 3.9 %collective-permute-done.12.refs_1_ = f32[1,2,256,256]{3,2,1,0:T(8,128)S(1)} collective-permute-done((f32[1,2,256,256]{3,2,1,0:T(8,128)S(1)}, f32[1,2,256,256]{3,2,1,0:T(8,128)S(1)}, u32[]{:S(2)}, u32[]{:S(2)}) %collective-permute-start.12) | collective-permute-done | bytes 524320 | tf_op jit(solution)/shard_map/ppermute | solution.py:405
  57.6 2.4 %collective-permute-done.9.carried = f32[2,256,256]{2,1,0:T(8,128)S(1)} collective-permute-done((f32[2,256,256]{2,1,0:T(8,128)S(1)}, f32[2,256,256]{2,1,0:T(8,128)S(1)}, u32[]{:S(2)}, u32[]{:S(2)}) %collective-permute-start.9) | collective-permute-done | bytes 524320 | tf_op jit(solution)/shard_map/ppermute | solution.py:475
  61.1 4.3 %collective-permute-start.17 = (f32[2,256,256]{2,1,0:T(8,128)S(1)}, f32[2,256,256]{2,1,0:T(8,128)S(1)}, u32[]{:S(2)}, u32[]{:S(2)}) collective-permute-start(f32[2,256,256]{2,1,0:T(8,128)S(1)} %get-tuple-element.108), channel_id=1, source_target_pairs={{8,17},{9,18},{10,19},{12,21},{13,22},{14,23},{16,9},{17,10},{18,1... | collective-permute-start | bytes 1572872 | tf_op jit(solution)/shard_map/ppermute | solution.py:511
  65.4 1.5 %shard_map.119 = (f32[2,2,256,256]{3,2,1,0:T(8,128)S(1)}, f32[2,2,256,256]{3,2,1,0:T(8,128)S(1)}) custom-call(f32[1,2,256,256]{3,2,1,0:T(8,128)S(1)} %collective-permute-done.11.refs_0_, f32[1,2,256,256]{3,2,1,0:T(8,128)S(1)} %collective-permute-done.12.refs_1_, f32[4,2,256,256]{3,2,1,0:T(8,128)S(1)} %copy-done.2, f32[40,128]{1,0:T(8,128)S(1)} %add.107.sums.refs_3_), custom_call_target="tpu_custom_call" | custom-call | flops 1207959552 | bytes 5263360 | tf_op jit(solution)/shard_map/pallas_call | solution.py:67
  66.9 1.5 %shard_map.118 = (f32[2,2,256,256]{3,2,1,0:T(8,128)S(1)}, f32[2,2,256,256]{3,2,1,0:T(8,128)S(1)}) custom-call(f32[1,2,256,256]{3,2,1,0:T(8,128)S(1)} %collective-permute-done.10.refs_0_, f32[1,2,256,256]{3,2,1,0:T(8,128)S(1)} %collective-permute-done.14.refs_1_, f32[4,2,256,256]{3,2,1,0:T(8,128)S(1)} %copy-done.2, f32[40,128]{1,0:T(8,128)S(1)} %add.107.sums.refs_3_), custom_call_target="tpu_custom_call" | custom-call | flops 1207959552 | bytes 5263360 | tf_op jit(solution)/shard_map/pallas_call | solution.py:67
  68.9 2.2 %collective-permute-done.13 = f32[2,256,256]{2,1,0:T(8,128)S(1)} collective-permute-done((f32[2,256,256]{2,1,0:T(8,128)S(1)}, f32[2,256,256]{2,1,0:T(8,128)S(1)}, u32[]{:S(2)}, u32[]{:S(2)}) %collective-permute-start.13) | collective-permute-done | bytes 524320 | tf_op jit(solution)/shard_map/ppermute | solution.py:510
  72.2 7.5 %shard_map.120 = (f32[4,2,256,256]{3,2,1,0:T(8,128)S(1)}, f32[2,256,256]{2,1,0:T(8,128)}) custom-call(f32[4,2,256,256]{3,2,1,0:T(8,128)S(1)} %bitcast.53, f32[4,2,256,256]{3,2,1,0:T(8,128)S(1)} %copy-done.2, f32[40,128]{1,0:T(8,128)S(1)} %add.107.sums.refs_3_, f32[2,256,256]{2,1,0:T(8,128)S(1)} %broadcast_select_fusion.carried), custom_call_target="tpu_custom_call" | custom-call | flops 4831838208 | bytes 7360512 | tf_op jit(solution)/shard_map/pallas_call | solution.py:67
  79.6 4.0 %collective-permute-done.17.carried = f32[2,256,256]{2,1,0:T(8,128)S(1)} collective-permute-done((f32[2,256,256]{2,1,0:T(8,128)S(1)}, f32[2,256,256]{2,1,0:T(8,128)S(1)}, u32[]{:S(2)}, u32[]{:S(2)}) %collective-permute-start.17) | collective-permute-done | bytes 524320 | tf_op jit(solution)/shard_map/ppermute | solution.py:511
  83.6 7.5 %collective-permute-done.18.refs_1_ = f32[1,2,256,256]{3,2,1,0:T(8,128)S(1)} collective-permute-done((f32[1,2,256,256]{3,2,1,0:T(8,128)S(1)}, f32[1,2,256,256]{3,2,1,0:T(8,128)S(1)}, u32[]{:S(2)}, u32[]{:S(2)}) %collective-permute-start.18) | collective-permute-done | bytes 524320 | tf_op jit(solution)/shard_map/ppermute | solution.py:405
  91.2 1.5 %shard_map.122 = (f32[2,2,256,256]{3,2,1,0:T(8,128)S(1)}, f32[2,2,256,256]{3,2,1,0:T(8,128)S(1)}) custom-call(f32[1,2,256,256]{3,2,1,0:T(8,128)S(1)} %collective-permute-done.15.refs_0_, f32[1,2,256,256]{3,2,1,0:T(8,128)S(1)} %collective-permute-done.18.refs_1_, f32[4,2,256,256]{3,2,1,0:T(8,128)S(1)} %copy-done.2, f32[40,128]{1,0:T(8,128)S(1)} %add.107.sums.refs_3_), custom_call_target="tpu_custom_call" | custom-call | flops 1207959552 | bytes 5263360 | tf_op jit(solution)/shard_map/pallas_call | solution.py:67
  92.8 1.9 %shard_map.121 = (f32[2,2,256,256]{3,2,1,0:T(8,128)S(1)}, f32[2,256,256]{2,1,0:T(8,128)S(1)}) custom-call(f32[2,2,256,256]{3,2,1,0:T(8,128)S(1)} %get-tuple-element.106.link, f32[2,2,256,256]{3,2,1,0:T(8,128)S(1)} %get-tuple-element.107.source, f32[2,256,256]{2,1,0:T(8,128)S(1)} %collective-permute-done.17.carried), custom_call_target="tpu_custom_call" | custom-call | flops 1207959552 | bytes 4194304 | tf_op jit(solution)/shard_map/pallas_call | solution.py:67
  94.7 2.7 %shard_map.123 = (f32[2,2,256,256]{3,2,1,0:T(8,128)S(1)}, f32[2,256,256]{2,1,0:T(8,128)}) custom-call(f32[2,2,256,256]{3,2,1,0:T(8,128)S(1)} %get-tuple-element.114.link, f32[2,2,256,256]{3,2,1,0:T(8,128)S(1)} %get-tuple-element.115.source, f32[2,256,256]{2,1,0:T(8,128)S(1)} %get-tuple-element.116.carried), custom_call_target="tpu_custom_call" | custom-call | flops 1207959552 | bytes 4194304 | tf_op jit(solution)/shard_map/pallas_call | solution.py:67
  98.2 2.7 %shard_map.124 = (f32[2,2,256,256]{3,2,1,0:T(8,128)S(1)}, f32[2,2,256,256]{3,2,1,0:T(8,128)S(1)}, f32[2,256,256]{2,1,0:T(8,128)S(1)}) custom-call(s32[2]{0:T(128)S(1)} %pad_add_fusion.pick, f32[2,2,256,256]{3,2,1,0:T(8,128)S(1)} %get-tuple-element.122.link, f32[2,2,256,256]{3,2,1,0:T(8,128)S(1)} %get-tuple-element.123.source, ...), custom_call_target="tpu_custom_call" | custom-call | flops 1207959552 | bytes 9437192 | tf_op jit(solution)/shard_map/pallas_call | solution.py:67
  100.9 2.7 %collective-permute-start.19 = (f32[2,2,256,256]{3,2,1,0:T(8,128)S(1)}, f32[2,2,256,256]{3,2,1,0:T(8,128)S(1)}, u32[]{:S(2)}, u32[]{:S(2)}) collective-permute-start(f32[2,2,256,256]{3,2,1,0:T(8,128)S(1)} %get-tuple-element.129), channel_id=1, source_target_pairs={{0,4},{4,0},{8,12},{12,8},{16,20},{20,16},{24,28},{28,24},{1,5},{5... | collective-permute-start | bytes 3145736 | tf_op jit(solution)/shard_map/ppermute | solution.py:580
  103.6 3.4 %shard_map.125 = (f32[2,2,256,256]{3,2,1,0:T(8,128)S(1)}, f32[2,2,256,256]{3,2,1,0:T(8,128)S(1)}, f32[2,256,256]{2,1,0:T(8,128)}) custom-call(s32[2]{0:T(128)S(1)} %pad_add_fusion.pick, f32[2,2,256,256]{3,2,1,0:T(8,128)S(1)} %get-tuple-element.130.link, f32[2,2,256,256]{3,2,1,0:T(8,128)S(1)} %get-tuple-element.131.source, ...), custom_call_target="tpu_custom_call" | custom-call | flops 1207959552 | bytes 9437192 | tf_op jit(solution)/shard_map/pallas_call | solution.py:67
  107.3 2.6 %collective-permute-done.20 = f32[2,2,256,256]{3,2,1,0:T(8,128)S(1)} collective-permute-done((f32[2,2,256,256]{3,2,1,0:T(8,128)S(1)}, f32[2,2,256,256]{3,2,1,0:T(8,128)S(1)}, u32[]{:S(2)}, u32[]{:S(2)}) %collective-permute-start.20) | collective-permute-done | bytes 1048608 | tf_op jit(solution)/shard_map/ppermute | solution.py:580
  110.1 1.5 %maximum_bitcast_fusion = f32[1,4,2,256,256]{4,3,2,1,0:T(8,128)} fusion(f32[2,2,256,256]{3,2,1,0:T(8,128)S(1)} %add.131, f32[2,2,256,256]{3,2,1,0:T(8,128)S(1)} %add.130), kind=kLoop, calls=%fused_computation.1 | loop fusion | flops 524288 | bytes 4194304 | tf_op jit(solution)/shard_map/broadcast_in_dim | solution.py:581
  (78 shorter events, 13.8 us)
Async XLA Ops:
  0.6 25.7 %copy-start = (f32[1,4,2,256,256]{4,3,2,1,0:T(8,128)S(1)}, f32[1,4,2,256,256]{4,3,2,1,0:T(8,128)}, u32[]{:S(2)}) copy-start(f32[1,4,2,256,256]{4,3,2,1,0:T(8,128)} %param.14) | copy-start | bytes 6291460
  1.9 14.7 %collective-permute-start.2 = (f32[1,2,256,256]{3,2,1,0:T(8,128)S(1)}, f32[1,2,256,256]{3,2,1,0:T(8,128)S(1)}, u32[]{:S(2)}, u32[]{:S(2)}) collective-permute-start(f32[1,2,256,256]{3,2,1,0:T(8,128)S(1)} %slice_bitcast_fusion), channel_id=1, source_target_pairs={{0,8},{4,12},{8,0},{12,4},{16,24},{20,28},{24,16},{28,20},{1,9},{5... | collective-permute-start | bytes 1572872 | tf_op jit(solution)/shard_map/ppermute | solution.py:347
  4.0 8.1 %collective-permute-start.1 = (f32[2,1,4,128]{3,2,0,1:T(4,128)S(1)}, f32[2,1,4,128]{3,2,0,1:T(4,128)S(1)}, u32[]{:S(2)}, u32[]{:S(2)}) collective-permute-start(f32[2,1,4,128]{3,2,0,1:T(4,128)S(1)} %get-tuple-element.140), channel_id=1, source_target_pairs={{0,1},{2,3},{1,0},{3,2},{4,5},{6,7},{5,4},{7,6},{8,9},{10,11},{9,8... | collective-permute-start | bytes 12296 | tf_op jit(solution)/shard_map/ppermute | solution.py:361
  4.2 7.9 %collective-permute-start = (f32[2,1,4,128]{3,2,0,1:T(4,128)S(1)}, f32[2,1,4,128]{3,2,0,1:T(4,128)S(1)}, u32[]{:S(2)}, u32[]{:S(2)}) collective-permute-start(f32[2,1,4,128]{3,2,0,1:T(4,128)S(1)} %get-tuple-element.141), channel_id=1, source_target_pairs={{1,2},{2,1},{5,6},{6,5},{9,10},{10,9},{13,14},{14,13},{17,18},{18,... | collective-permute-start | bytes 12296 | tf_op jit(solution)/shard_map/ppermute | solution.py:362
  8.5 8.1 %collective-permute-start.3 = (f32[2,16,4,128]{3,2,0,1:T(4,128)S(1)}, f32[2,16,4,128]{3,2,0,1:T(4,128)S(1)}, u32[]{:S(2)}, u32[]{:S(2)}) collective-permute-start(f32[2,16,4,128]{3,2,0,1:T(4,128)S(1)} %pad_maximum_fusion), channel_id=1, source_target_pairs={{4,8},{12,16},{20,24},{8,4},{16,12},{24,20},{5,9},{13,17},{21,25},... | collective-permute-start | bytes 196616 | tf_op jit(solution)/shard_map/ppermute | solution.py:368
  16.6 2.8 %collective-permute-start.4 = (f32[40,128]{1,0:T(8,128)}, f32[40,128]{1,0:T(8,128)S(1)}, u32[]{:S(2)}, u32[]{:S(2)}) collective-permute-start(f32[40,128]{1,0:T(8,128)} %get-tuple-element.72), channel_id=1, source_target_pairs={{0,8},{4,12},{8,0},{12,4},{16,24},{20,28},{24,16},{28,20},{1,9},{5... | collective-permute-start | bytes 61448 | tf_op jit(solution)/shard_map/ppermute | solution.py:302
  20.9 2.7 %collective-permute-start.5 = (f32[104,128]{1,0:T(8,128)S(1)}, f32[104,128]{1,0:T(8,128)S(1)}, u32[]{:S(2)}, u32[]{:S(2)}) collective-permute-start(f32[104,128]{1,0:T(8,128)S(1)} %pad_maximum_fusion.1), channel_id=1, source_target_pairs={{0,4},{4,0},{8,12},{12,8},{16,20},{20,16},{24,28},{28,24},{1,5},{5... | collective-permute-start | bytes 159752 | tf_op jit(solution)/shard_map/ppermute | solution.py:302
  23.7 2.6 %collective-permute-start.6 = (f32[40,128]{1,0:T(8,128)S(1)}, f32[40,128]{1,0:T(8,128)S(1)}, u32[]{:S(2)}, u32[]{:S(2)}) collective-permute-start(f32[40,128]{1,0:T(8,128)S(1)} %slice_add_fusion), channel_id=1, source_target_pairs={{0,16},{4,20},{8,24},{12,28},{16,0},{20,4},{24,8},{28,12},{1,17},{... | collective-permute-start | bytes 61448 | tf_op jit(solution)/shard_map/ppermute | solution.py:302
  23.8 13.4 %collective-permute-start.8 = (f32[1,2,256,256]{3,2,1,0:T(8,128)}, f32[1,2,256,256]{3,2,1,0:T(8,128)S(1)}, u32[]{:S(2)}, u32[]{:S(2)}) collective-permute-start(f32[1,2,256,256]{3,2,1,0:T(8,128)} %get-tuple-element.81), channel_id=1, source_target_pairs={{0,8},{4,12},{8,0},{12,4},{16,24},{20,28},{24,16},{28,20},{1,9},{5... | collective-permute-start | bytes 1572872 | tf_op jit(solution)/shard_map/ppermute | solution.py:400
  27.9 6.5 %copy-start.10 = (s32[4]{0:T(128)S(1)}, s32[4]{0:T(128)}, u32[]{:S(2)}) copy-start(s32[4]{0:T(128)} %param.16) | copy-start | bytes 52
  27.9 6.5 %copy-start.11 = (s32[4]{0:T(128)S(1)}, s32[4]{0:T(128)}, u32[]{:S(2)}) copy-start(s32[4]{0:T(128)} %constant.57.clone) | copy-start | bytes 52
  27.9 9.2 %copy-start.13 = (f32[1,2,256,256]{3,2,1,0:T(8,128)S(1)}, f32[1,2,256,256]{3,2,1,0:T(8,128)}, u32[]{:S(2)}) copy-start(f32[1,2,256,256]{3,2,1,0:T(8,128)} %get-tuple-element.87) | copy-start | bytes 1572868
  27.9 10.5 %copy-start.5 = (f32[4,256,256]{2,1,0:T(8,128)S(1)}, f32[4,256,256]{2,1,0:T(8,128)}, u32[]{:S(2)}) copy-start(f32[4,256,256]{2,1,0:T(8,128)} %param.18) | copy-start | bytes 3145732
  34.2 12.0 %collective-permute-start.7 = (f32[2,256,256]{2,1,0:T(8,128)S(1)}, f32[2,256,256]{2,1,0:T(8,128)S(1)}, u32[]{:S(2)}, u32[]{:S(2)}) collective-permute-start(f32[2,256,256]{2,1,0:T(8,128)S(1)} %get-tuple-element.78.whole_source), channel_id=1, source_target_pairs={{0,1},{2,3},{1,0},{3,2},{4,5},{6,7},{5,4},{7,6},{8,9},{10,11},{9,8... | collective-permute-start | bytes 1572872 | tf_op jit(solution)/shard_map/ppermute | solution.py:475
  34.5 19.2 %collective-permute-start.11 = (f32[1,2,256,256]{3,2,1,0:T(8,128)S(1)}, f32[1,2,256,256]{3,2,1,0:T(8,128)S(1)}, u32[]{:S(2)}, u32[]{:S(2)}) collective-permute-start(f32[1,2,256,256]{3,2,1,0:T(8,128)S(1)} %collective-permute-done.2.refs_0_), channel_id=1, source_target_pairs={{0,16},{4,20},{8,24},{12,28},{16,0},{20,4},{24,8},{28,12},{1,17},{... | collective-permute-start | bytes 1572872 | tf_op jit(solution)/shard_map/ppermute | solution.py:405
  37.1 12.8 %copy-start.7 = (f32[1,1,8,128]{3,2,0,1:T(8,128)S(1)}, f32[1,1,8,128]{3,2,0,1:T(8,128)}, u32[]{:S(2)}) copy-start(f32[1,1,8,128]{3,2,0,1:T(8,128)} %get-tuple-element.176) | copy-start | bytes 12292
  37.1 12.8 %copy-start.8 = (f32[1,1,8,128]{3,2,0,1:T(8,128)S(1)}, f32[1,1,8,128]{3,2,0,1:T(8,128)}, u32[]{:S(2)}) copy-start(f32[1,1,8,128]{3,2,0,1:T(8,128)} %get-tuple-element.177) | copy-start | bytes 12292
  37.1 12.9 %copy-start.12 = (f32[1,2,256,256]{3,2,1,0:T(8,128)S(1)}, f32[1,2,256,256]{3,2,1,0:T(8,128)}, u32[]{:S(2)}) copy-start(f32[1,2,256,256]{3,2,1,0:T(8,128)} %get-tuple-element.98) | copy-start | bytes 1572868
  37.1 15.0 %copy-start.2 = (f32[4,2,256,256]{3,2,1,0:T(8,128)S(1)}, f32[4,2,256,256]{3,2,1,0:T(8,128)}, u32[]{:S(2)}) copy-start(f32[4,2,256,256]{3,2,1,0:T(8,128)} %refs_2_.7) | copy-start | bytes 6291460
  37.1 12.9 %collective-permute-start.10 = (f32[1,2,256,256]{3,2,1,0:T(8,128)S(1)}, f32[1,2,256,256]{3,2,1,0:T(8,128)S(1)}, u32[]{:S(2)}, u32[]{:S(2)}) collective-permute-start(f32[1,2,256,256]{3,2,1,0:T(8,128)S(1)} %copy-done.13), channel_id=1, source_target_pairs={{0,8},{4,12},{8,0},{12,4},{16,24},{20,28},{24,16},{28,20},{1,9},{5... | collective-permute-start | bytes 1572872 | tf_op jit(solution)/shard_map/ppermute | solution.py:409
  38.8 18.9 %collective-permute-start.12 = (f32[1,2,256,256]{3,2,1,0:T(8,128)S(1)}, f32[1,2,256,256]{3,2,1,0:T(8,128)S(1)}, u32[]{:S(2)}, u32[]{:S(2)}) collective-permute-start(f32[1,2,256,256]{3,2,1,0:T(8,128)S(1)} %collective-permute-done.8.refs_1_), channel_id=1, source_target_pairs={{0,16},{4,20},{8,24},{12,28},{16,0},{20,4},{24,8},{28,12},{1,17},{... | collective-permute-start | bytes 1572872 | tf_op jit(solution)/shard_map/ppermute | solution.py:405
  47.1 12.9 %collective-permute-start.9 = (f32[2,256,256]{2,1,0:T(8,128)S(1)}, f32[2,256,256]{2,1,0:T(8,128)S(1)}, u32[]{:S(2)}, u32[]{:S(2)}) collective-permute-start(f32[2,256,256]{2,1,0:T(8,128)S(1)} %shard_map.115.before), channel_id=1, source_target_pairs={{1,2},{2,1},{5,6},{6,5},{9,10},{10,9},{13,14},{14,13},{17,18},{18,... | collective-permute-start | bytes 1572872 | tf_op jit(solution)/shard_map/ppermute | solution.py:475
  50.0 16.8 %collective-permute-start.14 = (f32[1,2,256,256]{3,2,1,0:T(8,128)S(1)}, f32[1,2,256,256]{3,2,1,0:T(8,128)S(1)}, u32[]{:S(2)}, u32[]{:S(2)}) collective-permute-start(f32[1,2,256,256]{3,2,1,0:T(8,128)S(1)} %copy-done.12), channel_id=1, source_target_pairs={{0,8},{4,12},{8,0},{12,4},{16,24},{20,28},{24,16},{28,20},{1,9},{5... | collective-permute-start | bytes 1572872 | tf_op jit(solution)/shard_map/ppermute | solution.py:409
  51.6 17.3 %collective-permute-start.15 = (f32[1,2,256,256]{3,2,1,0:T(8,128)S(1)}, f32[1,2,256,256]{3,2,1,0:T(8,128)S(1)}, u32[]{:S(2)}, u32[]{:S(2)}) collective-permute-start(f32[1,2,256,256]{3,2,1,0:T(8,128)S(1)} %collective-permute-done.10.refs_0_), channel_id=1, source_target_pairs={{0,16},{4,20},{8,24},{12,28},{16,0},{20,4},{24,8},{28,12},{1,17},{... | collective-permute-start | bytes 1572872 | tf_op jit(solution)/shard_map/ppermute | solution.py:405
  61.0 10.1 %collective-permute-start.13 = (f32[2,256,256]{2,1,0:T(8,128)S(1)}, f32[2,256,256]{2,1,0:T(8,128)S(1)}, u32[]{:S(2)}, u32[]{:S(2)}) collective-permute-start(f32[2,256,256]{2,1,0:T(8,128)S(1)} %get-tuple-element.96), channel_id=1, source_target_pairs={{0,1},{2,3},{1,0},{3,2},{4,5},{6,7},{5,4},{7,6},{8,9},{10,11},{9,8... | collective-permute-start | bytes 1572872 | tf_op jit(solution)/shard_map/ppermute | solution.py:510
  61.1 22.5 %collective-permute-start.17 = (f32[2,256,256]{2,1,0:T(8,128)S(1)}, f32[2,256,256]{2,1,0:T(8,128)S(1)}, u32[]{:S(2)}, u32[]{:S(2)}) collective-permute-start(f32[2,256,256]{2,1,0:T(8,128)S(1)} %get-tuple-element.108), channel_id=1, source_target_pairs={{8,17},{9,18},{10,19},{12,21},{13,22},{14,23},{16,9},{17,10},{18,1... | collective-permute-start | bytes 1572872 | tf_op jit(solution)/shard_map/ppermute | solution.py:511
  66.9 24.2 %collective-permute-start.18 = (f32[1,2,256,256]{3,2,1,0:T(8,128)S(1)}, f32[1,2,256,256]{3,2,1,0:T(8,128)S(1)}, u32[]{:S(2)}, u32[]{:S(2)}) collective-permute-start(f32[1,2,256,256]{3,2,1,0:T(8,128)S(1)} %collective-permute-done.14.refs_1_), channel_id=1, source_target_pairs={{0,16},{4,20},{8,24},{12,28},{16,0},{20,4},{24,8},{28,12},{1,17},{... | collective-permute-start | bytes 1572872 | tf_op jit(solution)/shard_map/ppermute | solution.py:405
  71.2 19.9 %copy-start.3 = (f32[16,4,128]{2,1,0:T(4,128)S(1)}, f32[16,4,128]{2,1,0:T(4,128)}, u32[]{:S(2)}) copy-start(f32[16,4,128]{2,1,0:T(4,128)} %param.12) | copy-start | bytes 98308
  71.2 19.9 %copy-start.4 = (f32[16,4,128]{2,1,0:T(4,128)S(1)}, f32[16,4,128]{2,1,0:T(4,128)}, u32[]{:S(2)}) copy-start(f32[16,4,128]{2,1,0:T(4,128)} %param.10) | copy-start | bytes 98308
  71.2 27.0 %collective-permute-start.16 = (f32[2,256,256]{2,1,0:T(8,128)S(1)}, f32[2,256,256]{2,1,0:T(8,128)S(1)}, u32[]{:S(2)}, u32[]{:S(2)}) collective-permute-start(f32[2,256,256]{2,1,0:T(8,128)S(1)} %broadcast_select_fusion.carried), channel_id=1, source_target_pairs={{0,8},{4,12},{8,0},{12,4},{16,24},{20,28},{24,16},{28,20},{1,9},{5... | collective-permute-start | bytes 1572872 | tf_op jit(solution)/shard_map/ppermute | solution.py:519
  100.9 6.2 %collective-permute-start.19 = (f32[2,2,256,256]{3,2,1,0:T(8,128)S(1)}, f32[2,2,256,256]{3,2,1,0:T(8,128)S(1)}, u32[]{:S(2)}, u32[]{:S(2)}) collective-permute-start(f32[2,2,256,256]{3,2,1,0:T(8,128)S(1)} %get-tuple-element.129), channel_id=1, source_target_pairs={{0,4},{4,0},{8,12},{12,8},{16,20},{20,16},{24,28},{28,24},{1,5},{5... | collective-permute-start | bytes 3145736 | tf_op jit(solution)/shard_map/ppermute | solution.py:580
  107.2 2.7 %collective-permute-start.20 = (f32[2,2,256,256]{3,2,1,0:T(8,128)S(1)}, f32[2,2,256,256]{3,2,1,0:T(8,128)S(1)}, u32[]{:S(2)}, u32[]{:S(2)}) collective-permute-start(f32[2,2,256,256]{3,2,1,0:T(8,128)S(1)} %get-tuple-element.137), channel_id=1, source_target_pairs={{0,4},{4,0},{8,12},{12,8},{16,20},{20,16},{24,28},{28,24},{1,5},{5... | collective-permute-start | bytes 3145736 | tf_op jit(solution)/shard_map/ppermute | solution.py:580
  (3 other events, 10.8 us)

commit v19 on v18

--- a/solution.py
+++ b/solution.py
@@ -508,10 +508,11 @@
         return [(a * peers + i, b * peers + j) for a, b in pairs for i, j in wire_up]
 
     arrived = lax.ppermute(leaving, "slab", swaps((peers - 2) % 2))
-    carried_second = lax.ppermute(onward, ("energy", "slab"), both(second_pairs))
     sent_on(3)
     beside_second[0] = beside(0, free_second[:2])
     beside_first[1] = beside(1, free_first[2:])
+    onward, beside_first[1] = lax.optimization_barrier((onward, beside_first[1]))
+    carried_second = lax.ppermute(onward, ("energy", "slab"), both(second_pairs))
     arrived, beside_first[1], beside_second[0], free_second[2] = lax.optimization_barrier(
         (arrived, beside_first[1], beside_second[0], free_second[2])
     )

time: 113 us -> 113 us (level)
    ppermute x1, waiting for transfers between devices: 3.95 us -> 0.01 us  [per_device(): lax.ppermute(onward, ('energy', 'slab'), both(second_pairs))]
    ppermute x4, waiting for transfers between devices: 11.8 us -> 15.6 us  [sent_on(): free_second.append(lax.ppermute(given, 'energy', relay_pairs))]
  transfers between devices with their start and end apart: 21 -> 21, of which waited for: 13 -> 12; matrix products, arithmetic and copies ran while one was open for 3% -> 3% of each run, Pallas kernels for 30% -> 30%
where the time goes in v19:
time: 113 us; the launch traced here: 112 us
  waiting for transfers between devices  37.2 us (33%)
  Pallas kernels  35.9 us (32%)
  starting transfers between devices  28.6 us (25%)
  other arithmetic  6.18 us (5%)
  local copies, waits for them, and re-layouts  3.07 us (3%)
    pallas_call x13, Pallas kernels, call(): pl.pallas_call(kernel, out_shape=out_shapes, cost_estimate=cost, compiler...  35.9 us
    ppermute x4, waiting for transfers between devices, sent_on(): free_second.append(lax.ppermute(given, 'energy', relay_pairs))  15.6 us
    ppermute x2, waiting for transfers between devices, per_device(): arrived = lax.ppermute(leaving, 'slab', swaps((hop - 1) % 2))  8.73 us
    ppermute x3, waiting for transfers between devices, exchanged(): lax.ppermute(given, 'energy', [(e, e ^ mask) for e in range(peers)])  4.99 us
    ppermute x1, starting transfers between devices, per_device(): lax.ppermute(onward, ('energy', 'slab'), both(second_pairs))  4.49 us
    ppermute x1, starting transfers between devices, per_device(): crossed = lax.ppermute(jnp.where(even, lower, upper), 'slab', swaps(1))  4.32 us
    ppermute x1, starting transfers between devices, per_device(): lax.ppermute(stacked, 'energy', beyond + [(b, a) for a, b in beyond])  3.56 us
    ppermute x2, starting transfers between devices, per_device(): outputs.append(here + lax.ppermute(there, 'energy', twin_pairs))  3.26 us
  transfers between devices with their start and end apart: 21, of which 12 were waited for; matrix products, arithmetic and copies ran while one was open for 3% of the time, Pallas kernels for 30%

profile of v19, /device:TPU:13, one launch (start us, length us, event | category | flops | bytes accessed | tf_op | source)
XLA Modules:
  0.0 111.9 jit_solution(8722317544357209168)
XLA Ops:
  1.9 1.3 %collective-permute-start.2 = (f32[1,2,256,256]{3,2,1,0:T(8,128)S(1)}, f32[1,2,256,256]{3,2,1,0:T(8,128)S(1)}, u32[]{:S(2)}, u32[]{:S(2)}) collective-permute-start(f32[1,2,256,256]{3,2,1,0:T(8,128)S(1)} %slice_bitcast_fusion), channel_id=1, source_target_pairs={{0,8},{4,12},{8,0},{12,4},{16,24},{20,28},{24,16},{28,20},{1,9},{5... | collective-permute-start | bytes 1572872 | tf_op jit(solution)/shard_map/ppermute | solution.py:347
  4.2 4.3 %collective-permute-start = (f32[2,1,4,128]{3,2,0,1:T(4,128)S(1)}, f32[2,1,4,128]{3,2,0,1:T(4,128)S(1)}, u32[]{:S(2)}, u32[]{:S(2)}) collective-permute-start(f32[2,1,4,128]{3,2,0,1:T(4,128)S(1)} %get-tuple-element.147), channel_id=1, source_target_pairs={{1,2},{2,1},{5,6},{6,5},{9,10},{10,9},{13,14},{14,13},{17,18},{18,... | collective-permute-start | bytes 12296 | tf_op jit(solution)/shard_map/ppermute | solution.py:362
  8.5 3.6 %collective-permute-start.3 = (f32[2,16,4,128]{3,2,0,1:T(4,128)S(1)}, f32[2,16,4,128]{3,2,0,1:T(4,128)S(1)}, u32[]{:S(2)}, u32[]{:S(2)}) collective-permute-start(f32[2,16,4,128]{3,2,0,1:T(4,128)S(1)} %pad_maximum_fusion), channel_id=1, source_target_pairs={{4,8},{12,16},{20,24},{8,4},{16,12},{24,20},{5,9},{13,17},{21,25},... | collective-permute-start | bytes 196616 | tf_op jit(solution)/shard_map/ppermute | solution.py:368
  12.7 3.6 %shard_map.113 = (f32[40,128]{1,0:T(8,128)}, f32[64,128]{1,0:T(8,128)}, f32[1,2,256,256]{3,2,1,0:T(8,128)}, f32[1,2,256,256]{3,2,1,0:T(8,128)}, f32[1,2,256,256]{3,2,1,0:T(8,128)}) custom-call(s32[1]{0:T(128)} %bitcast.2.mine, f32[64,128]{1,0:T(8,128)} %bitcast.57, f32[64,128]{1,0:T(8,128)} %bitcast.55, f32[64,128]{1,0:T(8,128)} %bitcast.58, ...), custom_call_target="tpu_custom_call" | custom-call | flops 301989888 | bytes 3833860 | tf_op jit(solution)/shard_map/pallas_call | solution.py:67
  16.6 2.8 %collective-permute-done.4 = f32[40,128]{1,0:T(8,128)S(1)} collective-permute-done((f32[40,128]{1,0:T(8,128)}, f32[40,128]{1,0:T(8,128)S(1)}, u32[]{:S(2)}, u32[]{:S(2)}) %collective-permute-start.4) | collective-permute-done | bytes 20512 | tf_op jit(solution)/shard_map/ppermute | solution.py:302
  20.9 1.9 %collective-permute-start.5 = (f32[104,128]{1,0:T(8,128)S(1)}, f32[104,128]{1,0:T(8,128)S(1)}, u32[]{:S(2)}, u32[]{:S(2)}) collective-permute-start(f32[104,128]{1,0:T(8,128)S(1)} %pad_maximum_fusion.1), channel_id=1, source_target_pairs={{0,4},{4,0},{8,12},{12,8},{16,20},{20,16},{24,28},{28,24},{1,5},{5... | collective-permute-start | bytes 159752 | tf_op jit(solution)/shard_map/ppermute | solution.py:302
  23.8 1.3 %collective-permute-start.8 = (f32[1,2,256,256]{3,2,1,0:T(8,128)}, f32[1,2,256,256]{3,2,1,0:T(8,128)S(1)}, u32[]{:S(2)}, u32[]{:S(2)}) collective-permute-start(f32[1,2,256,256]{3,2,1,0:T(8,128)} %get-tuple-element.84), channel_id=1, source_target_pairs={{0,8},{4,12},{8,0},{12,4},{16,24},{20,28},{24,16},{28,20},{1,9},{5... | collective-permute-start | bytes 1572872 | tf_op jit(solution)/shard_map/ppermute | solution.py:400
  25.0 1.3 %collective-permute-done.6 = f32[40,128]{1,0:T(8,128)S(1)} collective-permute-done((f32[40,128]{1,0:T(8,128)S(1)}, f32[40,128]{1,0:T(8,128)S(1)}, u32[]{:S(2)}, u32[]{:S(2)}) %collective-permute-start.6) | collective-permute-done | bytes 20512 | tf_op jit(solution)/shard_map/ppermute | solution.py:302
  26.3 1.6 %copy-done.1 = f32[4,2,256,256]{3,2,1,0:T(8,128)S(1)} copy-done((f32[4,2,256,256]{3,2,1,0:T(8,128)S(1)}, f32[4,2,256,256]{3,2,1,0:T(8,128)}, u32[]{:S(2)}) %copy-start.1) | copy-done | bytes 2097176
  27.9 6.2 %shard_map.114 = (f32[2,256,256]{2,1,0:T(8,128)S(1)}, f32[2,256,256]{2,1,0:T(8,128)S(1)}) custom-call(f32[4,2,256,256]{3,2,1,0:T(8,128)S(1)} %bitcast.52, f32[4,2,256,256]{3,2,1,0:T(8,128)S(1)} %copy-done.1, f32[40,128]{1,0:T(8,128)S(1)} %add.107.sums.refs_3_), custom_call_target="tpu_custom_call" | custom-call | flops 5133828096 | bytes 5263360 | tf_op jit(solution)/shard_map/pallas_call | solution.py:67
  34.4 2.8 %collective-permute-done.8.refs_1_ = f32[1,2,256,256]{3,2,1,0:T(8,128)S(1)} collective-permute-done((f32[1,2,256,256]{3,2,1,0:T(8,128)}, f32[1,2,256,256]{3,2,1,0:T(8,128)S(1)}, u32[]{:S(2)}, u32[]{:S(2)}) %collective-permute-start.8) | collective-permute-done | bytes 524320 | tf_op jit(solution)/shard_map/ppermute | solution.py:400
  37.1 1.2 %collective-permute-start.10 = (f32[1,2,256,256]{3,2,1,0:T(8,128)S(1)}, f32[1,2,256,256]{3,2,1,0:T(8,128)S(1)}, u32[]{:S(2)}, u32[]{:S(2)}) collective-permute-start(f32[1,2,256,256]{3,2,1,0:T(8,128)S(1)} %copy-done.13), channel_id=1, source_target_pairs={{0,8},{4,12},{8,0},{12,4},{16,24},{20,28},{24,16},{28,20},{1,9},{5... | collective-permute-start | bytes 1572872 | tf_op jit(solution)/shard_map/ppermute | solution.py:409
  39.7 6.4 %collective-permute-done.7.carried = f32[2,256,256]{2,1,0:T(8,128)S(1)} collective-permute-done((f32[2,256,256]{2,1,0:T(8,128)S(1)}, f32[2,256,256]{2,1,0:T(8,128)S(1)}, u32[]{:S(2)}, u32[]{:S(2)}) %collective-permute-start.7) | collective-permute-done | bytes 524320 | tf_op jit(solution)/shard_map/ppermute | solution.py:475
  47.0 2.8 %collective-permute-start.9 = (f32[2,256,256]{2,1,0:T(8,128)S(1)}, f32[2,256,256]{2,1,0:T(8,128)S(1)}, u32[]{:S(2)}, u32[]{:S(2)}) collective-permute-start(f32[2,256,256]{2,1,0:T(8,128)S(1)} %shard_map.115.before), channel_id=1, source_target_pairs={{1,2},{2,1},{5,6},{6,5},{9,10},{10,9},{13,14},{14,13},{17,18},{18,... | collective-permute-start | bytes 1572872 | tf_op jit(solution)/shard_map/ppermute | solution.py:475
  49.9 1.6 %collective-permute-start.14 = (f32[1,2,256,256]{3,2,1,0:T(8,128)S(1)}, f32[1,2,256,256]{3,2,1,0:T(8,128)S(1)}, u32[]{:S(2)}, u32[]{:S(2)}) collective-permute-start(f32[1,2,256,256]{3,2,1,0:T(8,128)S(1)} %copy-done.12), channel_id=1, source_target_pairs={{0,8},{4,12},{8,0},{12,4},{16,24},{20,28},{24,16},{28,20},{1,9},{5... | collective-permute-start | bytes 1572872 | tf_op jit(solution)/shard_map/ppermute | solution.py:409
  52.0 1.5 %shard_map.116 = (f32[2,2,256,256]{3,2,1,0:T(8,128)S(1)}, f32[2,2,256,256]{3,2,1,0:T(8,128)S(1)}) custom-call(f32[1,2,256,256]{3,2,1,0:T(8,128)S(1)} %collective-permute-done.2.refs_0_, f32[1,2,256,256]{3,2,1,0:T(8,128)S(1)} %collective-permute-done.8.refs_1_, f32[4,2,256,256]{3,2,1,0:T(8,128)S(1)} %copy-done.2, f32[40,128]{1,0:T(8,128)S(1)} %add.107.sums.refs_3_), custom_call_target="tpu_custom_call" | custom-call | flops 1207959552 | bytes 5263360 | tf_op jit(solution)/shard_map/pallas_call | solution.py:67
  53.6 3.9 %collective-permute-done.12.refs_1_ = f32[1,2,256,256]{3,2,1,0:T(8,128)S(1)} collective-permute-done((f32[1,2,256,256]{3,2,1,0:T(8,128)S(1)}, f32[1,2,256,256]{3,2,1,0:T(8,128)S(1)}, u32[]{:S(2)}, u32[]{:S(2)}) %collective-permute-start.12) | collective-permute-done | bytes 524320 | tf_op jit(solution)/shard_map/ppermute | solution.py:405
  57.5 2.4 %collective-permute-done.9.carried = f32[2,256,256]{2,1,0:T(8,128)S(1)} collective-permute-done((f32[2,256,256]{2,1,0:T(8,128)S(1)}, f32[2,256,256]{2,1,0:T(8,128)S(1)}, u32[]{:S(2)}, u32[]{:S(2)}) %collective-permute-start.9) | collective-permute-done | bytes 524320 | tf_op jit(solution)/shard_map/ppermute | solution.py:475
  61.0 1.5 %shard_map.119 = (f32[2,2,256,256]{3,2,1,0:T(8,128)S(1)}, f32[2,2,256,256]{3,2,1,0:T(8,128)S(1)}) custom-call(f32[1,2,256,256]{3,2,1,0:T(8,128)S(1)} %collective-permute-done.11.refs_0_, f32[1,2,256,256]{3,2,1,0:T(8,128)S(1)} %collective-permute-done.12.refs_1_, f32[4,2,256,256]{3,2,1,0:T(8,128)S(1)} %copy-done.2, f32[40,128]{1,0:T(8,128)S(1)} %add.107.sums.refs_3_), custom_call_target="tpu_custom_call" | custom-call | flops 1207959552 | bytes 5263360 | tf_op jit(solution)/shard_map/pallas_call | solution.py:67
  62.5 1.5 %shard_map.118 = (f32[2,2,256,256]{3,2,1,0:T(8,128)S(1)}, f32[2,2,256,256]{3,2,1,0:T(8,128)S(1)}) custom-call(f32[1,2,256,256]{3,2,1,0:T(8,128)S(1)} %collective-permute-done.10.refs_0_, f32[1,2,256,256]{3,2,1,0:T(8,128)S(1)} %collective-permute-done.14.refs_1_, f32[4,2,256,256]{3,2,1,0:T(8,128)S(1)} %copy-done.2, f32[40,128]{1,0:T(8,128)S(1)} %add.107.sums.refs_3_), custom_call_target="tpu_custom_call" | custom-call | flops 1207959552 | bytes 5263360 | tf_op jit(solution)/shard_map/pallas_call | solution.py:67
  64.0 4.5 %collective-permute-start.17 = (f32[2,256,256]{2,1,0:T(8,128)S(1)}, f32[2,256,256]{2,1,0:T(8,128)S(1)}, u32[]{:S(2)}, u32[]{:S(2)}) collective-permute-start(f32[2,256,256]{2,1,0:T(8,128)S(1)} %get-tuple-element.114), channel_id=1, source_target_pairs={{8,17},{9,18},{10,19},{12,21},{13,22},{14,23},{16,9},{17,10},{18,1... | collective-permute-start | bytes 1572872 | tf_op jit(solution)/shard_map/ppermute | solution.py:515
  68.7 2.2 %collective-permute-done.13 = f32[2,256,256]{2,1,0:T(8,128)S(1)} collective-permute-done((f32[2,256,256]{2,1,0:T(8,128)S(1)}, f32[2,256,256]{2,1,0:T(8,128)S(1)}, u32[]{:S(2)}, u32[]{:S(2)}) %collective-permute-start.13) | collective-permute-done | bytes 524320 | tf_op jit(solution)/shard_map/ppermute | solution.py:510
  72.0 7.5 %shard_map.120 = (f32[4,2,256,256]{3,2,1,0:T(8,128)S(1)}, f32[2,256,256]{2,1,0:T(8,128)}) custom-call(f32[4,2,256,256]{3,2,1,0:T(8,128)S(1)} %bitcast.53, f32[4,2,256,256]{3,2,1,0:T(8,128)S(1)} %copy-done.2, f32[40,128]{1,0:T(8,128)S(1)} %add.107.sums.refs_3_, f32[2,256,256]{2,1,0:T(8,128)S(1)} %broadcast_select_fusion.carried), custom_call_target="tpu_custom_call" | custom-call | flops 4831838208 | bytes 7360512 | tf_op jit(solution)/shard_map/pallas_call | solution.py:67
  79.5 11.5 %collective-permute-done.18.refs_1_ = f32[1,2,256,256]{3,2,1,0:T(8,128)S(1)} collective-permute-done((f32[1,2,256,256]{3,2,1,0:T(8,128)S(1)}, f32[1,2,256,256]{3,2,1,0:T(8,128)S(1)}, u32[]{:S(2)}, u32[]{:S(2)}) %collective-permute-start.18) | collective-permute-done | bytes 524320 | tf_op jit(solution)/shard_map/ppermute | solution.py:405
  91.1 1.6 %shard_map.122 = (f32[2,2,256,256]{3,2,1,0:T(8,128)S(1)}, f32[2,2,256,256]{3,2,1,0:T(8,128)S(1)}) custom-call(f32[1,2,256,256]{3,2,1,0:T(8,128)S(1)} %collective-permute-done.15.refs_0_, f32[1,2,256,256]{3,2,1,0:T(8,128)S(1)} %collective-permute-done.18.refs_1_, f32[4,2,256,256]{3,2,1,0:T(8,128)S(1)} %copy-done.2, f32[40,128]{1,0:T(8,128)S(1)} %add.107.sums.refs_3_), custom_call_target="tpu_custom_call" | custom-call | flops 1207959552 | bytes 5263360 | tf_op jit(solution)/shard_map/pallas_call | solution.py:67
  92.7 1.9 %shard_map.121 = (f32[2,2,256,256]{3,2,1,0:T(8,128)S(1)}, f32[2,256,256]{2,1,0:T(8,128)S(1)}) custom-call(f32[2,2,256,256]{3,2,1,0:T(8,128)S(1)} %get-tuple-element.112.link, f32[2,2,256,256]{3,2,1,0:T(8,128)S(1)} %get-tuple-element.113.source, f32[2,256,256]{2,1,0:T(8,128)S(1)} %collective-permute-done.17.carried), custom_call_target="tpu_custom_call" | custom-call | flops 1207959552 | bytes 4194304 | tf_op jit(solution)/shard_map/pallas_call | solution.py:67
  94.6 2.7 %shard_map.123 = (f32[2,2,256,256]{3,2,1,0:T(8,128)S(1)}, f32[2,256,256]{2,1,0:T(8,128)}) custom-call(f32[2,2,256,256]{3,2,1,0:T(8,128)S(1)} %get-tuple-element.120.link, f32[2,2,256,256]{3,2,1,0:T(8,128)S(1)} %get-tuple-element.121.source, f32[2,256,256]{2,1,0:T(8,128)S(1)} %get-tuple-element.122.carried), custom_call_target="tpu_custom_call" | custom-call | flops 1207959552 | bytes 4194304 | tf_op jit(solution)/shard_map/pallas_call | solution.py:67
  98.1 2.7 %shard_map.124 = (f32[2,2,256,256]{3,2,1,0:T(8,128)S(1)}, f32[2,2,256,256]{3,2,1,0:T(8,128)S(1)}, f32[2,256,256]{2,1,0:T(8,128)S(1)}) custom-call(s32[2]{0:T(128)S(1)} %pad_add_fusion.pick, f32[2,2,256,256]{3,2,1,0:T(8,128)S(1)} %get-tuple-element.128.link, f32[2,2,256,256]{3,2,1,0:T(8,128)S(1)} %get-tuple-element.129.source, ...), custom_call_target="tpu_custom_call" | custom-call | flops 1207959552 | bytes 9437192 | tf_op jit(solution)/shard_map/pallas_call | solution.py:67
  100.8 3.2 %collective-permute-start.19 = (f32[2,2,256,256]{3,2,1,0:T(8,128)S(1)}, f32[2,2,256,256]{3,2,1,0:T(8,128)S(1)}, u32[]{:S(2)}, u32[]{:S(2)}) collective-permute-start(f32[2,2,256,256]{3,2,1,0:T(8,128)S(1)} %get-tuple-element.135), channel_id=1, source_target_pairs={{0,4},{4,0},{8,12},{12,8},{16,20},{20,16},{24,28},{28,24},{1,5},{5... | collective-permute-start | bytes 3145736 | tf_op jit(solution)/shard_map/ppermute | solution.py:581
  104.0 3.4 %shard_map.125 = (f32[2,2,256,256]{3,2,1,0:T(8,128)S(1)}, f32[2,2,256,256]{3,2,1,0:T(8,128)S(1)}, f32[2,256,256]{2,1,0:T(8,128)}) custom-call(s32[2]{0:T(128)S(1)} %pad_add_fusion.pick, f32[2,2,256,256]{3,2,1,0:T(8,128)S(1)} %get-tuple-element.136.link, f32[2,2,256,256]{3,2,1,0:T(8,128)S(1)} %get-tuple-element.137.source, ...), custom_call_target="tpu_custom_call" | custom-call | flops 1207959552 | bytes 9437192 | tf_op jit(solution)/shard_map/pallas_call | solution.py:67
  107.7 2.6 %collective-permute-done.20 = f32[2,2,256,256]{3,2,1,0:T(8,128)S(1)} collective-permute-done((f32[2,2,256,256]{3,2,1,0:T(8,128)S(1)}, f32[2,2,256,256]{3,2,1,0:T(8,128)S(1)}, u32[]{:S(2)}, u32[]{:S(2)}) %collective-permute-start.20) | collective-permute-done | bytes 1048608 | tf_op jit(solution)/shard_map/ppermute | solution.py:581
  110.4 1.5 %maximum_bitcast_fusion = f32[1,4,2,256,256]{4,3,2,1,0:T(8,128)} fusion(f32[2,2,256,256]{3,2,1,0:T(8,128)S(1)} %add.131, f32[2,2,256,256]{3,2,1,0:T(8,128)S(1)} %add.130), kind=kLoop, calls=%fused_computation.1 | loop fusion | flops 524288 | bytes 4194304 | tf_op jit(solution)/shard_map/broadcast_in_dim | solution.py:582
  (78 shorter events, 12.3 us)
Async XLA Ops:
  0.6 25.7 %copy-start = (f32[1,4,2,256,256]{4,3,2,1,0:T(8,128)S(1)}, f32[1,4,2,256,256]{4,3,2,1,0:T(8,128)}, u32[]{:S(2)}) copy-start(f32[1,4,2,256,256]{4,3,2,1,0:T(8,128)} %param.14) | copy-start | bytes 6291460
  1.9 14.7 %collective-permute-start.2 = (f32[1,2,256,256]{3,2,1,0:T(8,128)S(1)}, f32[1,2,256,256]{3,2,1,0:T(8,128)S(1)}, u32[]{:S(2)}, u32[]{:S(2)}) collective-permute-start(f32[1,2,256,256]{3,2,1,0:T(8,128)S(1)} %slice_bitcast_fusion), channel_id=1, source_target_pairs={{0,8},{4,12},{8,0},{12,4},{16,24},{20,28},{24,16},{28,20},{1,9},{5... | collective-permute-start | bytes 1572872 | tf_op jit(solution)/shard_map/ppermute | solution.py:347
  4.0 8.1 %collective-permute-start.1 = (f32[2,1,4,128]{3,2,0,1:T(4,128)S(1)}, f32[2,1,4,128]{3,2,0,1:T(4,128)S(1)}, u32[]{:S(2)}, u32[]{:S(2)}) collective-permute-start(f32[2,1,4,128]{3,2,0,1:T(4,128)S(1)} %get-tuple-element.146), channel_id=1, source_target_pairs={{0,1},{2,3},{1,0},{3,2},{4,5},{6,7},{5,4},{7,6},{8,9},{10,11},{9,8... | collective-permute-start | bytes 12296 | tf_op jit(solution)/shard_map/ppermute | solution.py:361
  4.2 7.9 %collective-permute-start = (f32[2,1,4,128]{3,2,0,1:T(4,128)S(1)}, f32[2,1,4,128]{3,2,0,1:T(4,128)S(1)}, u32[]{:S(2)}, u32[]{:S(2)}) collective-permute-start(f32[2,1,4,128]{3,2,0,1:T(4,128)S(1)} %get-tuple-element.147), channel_id=1, source_target_pairs={{1,2},{2,1},{5,6},{6,5},{9,10},{10,9},{13,14},{14,13},{17,18},{18,... | collective-permute-start | bytes 12296 | tf_op jit(solution)/shard_map/ppermute | solution.py:362
  8.5 8.1 %collective-permute-start.3 = (f32[2,16,4,128]{3,2,0,1:T(4,128)S(1)}, f32[2,16,4,128]{3,2,0,1:T(4,128)S(1)}, u32[]{:S(2)}, u32[]{:S(2)}) collective-permute-start(f32[2,16,4,128]{3,2,0,1:T(4,128)S(1)} %pad_maximum_fusion), channel_id=1, source_target_pairs={{4,8},{12,16},{20,24},{8,4},{16,12},{24,20},{5,9},{13,17},{21,25},... | collective-permute-start | bytes 196616 | tf_op jit(solution)/shard_map/ppermute | solution.py:368
  16.6 2.8 %collective-permute-start.4 = (f32[40,128]{1,0:T(8,128)}, f32[40,128]{1,0:T(8,128)S(1)}, u32[]{:S(2)}, u32[]{:S(2)}) collective-permute-start(f32[40,128]{1,0:T(8,128)} %get-tuple-element.75), channel_id=1, source_target_pairs={{0,8},{4,12},{8,0},{12,4},{16,24},{20,28},{24,16},{28,20},{1,9},{5... | collective-permute-start | bytes 61448 | tf_op jit(solution)/shard_map/ppermute | solution.py:302
  20.9 2.7 %collective-permute-start.5 = (f32[104,128]{1,0:T(8,128)S(1)}, f32[104,128]{1,0:T(8,128)S(1)}, u32[]{:S(2)}, u32[]{:S(2)}) collective-permute-start(f32[104,128]{1,0:T(8,128)S(1)} %pad_maximum_fusion.1), channel_id=1, source_target_pairs={{0,4},{4,0},{8,12},{12,8},{16,20},{20,16},{24,28},{28,24},{1,5},{5... | collective-permute-start | bytes 159752 | tf_op jit(solution)/shard_map/ppermute | solution.py:302
  23.7 2.6 %collective-permute-start.6 = (f32[40,128]{1,0:T(8,128)S(1)}, f32[40,128]{1,0:T(8,128)S(1)}, u32[]{:S(2)}, u32[]{:S(2)}) collective-permute-start(f32[40,128]{1,0:T(8,128)S(1)} %slice_add_fusion), channel_id=1, source_target_pairs={{0,16},{4,20},{8,24},{12,28},{16,0},{20,4},{24,8},{28,12},{1,17},{... | collective-permute-start | bytes 61448 | tf_op jit(solution)/shard_map/ppermute | solution.py:302
  23.8 13.4 %collective-permute-start.8 = (f32[1,2,256,256]{3,2,1,0:T(8,128)}, f32[1,2,256,256]{3,2,1,0:T(8,128)S(1)}, u32[]{:S(2)}, u32[]{:S(2)}) collective-permute-start(f32[1,2,256,256]{3,2,1,0:T(8,128)} %get-tuple-element.84), channel_id=1, source_target_pairs={{0,8},{4,12},{8,0},{12,4},{16,24},{20,28},{24,16},{28,20},{1,9},{5... | collective-permute-start | bytes 1572872 | tf_op jit(solution)/shard_map/ppermute | solution.py:400
  27.9 6.4 %copy-start.10 = (s32[4]{0:T(128)S(1)}, s32[4]{0:T(128)}, u32[]{:S(2)}) copy-start(s32[4]{0:T(128)} %param.16) | copy-start | bytes 52
  27.9 6.4 %copy-start.11 = (s32[4]{0:T(128)S(1)}, s32[4]{0:T(128)}, u32[]{:S(2)}) copy-start(s32[4]{0:T(128)} %constant.57.clone) | copy-start | bytes 52
  27.9 9.2 %copy-start.13 = (f32[1,2,256,256]{3,2,1,0:T(8,128)S(1)}, f32[1,2,256,256]{3,2,1,0:T(8,128)}, u32[]{:S(2)}) copy-start(f32[1,2,256,256]{3,2,1,0:T(8,128)} %get-tuple-element.90) | copy-start | bytes 1572868
  27.9 10.5 %copy-start.5 = (f32[4,256,256]{2,1,0:T(8,128)S(1)}, f32[4,256,256]{2,1,0:T(8,128)}, u32[]{:S(2)}) copy-start(f32[4,256,256]{2,1,0:T(8,128)} %param.18) | copy-start | bytes 3145732
  34.1 12.0 %collective-permute-start.7 = (f32[2,256,256]{2,1,0:T(8,128)S(1)}, f32[2,256,256]{2,1,0:T(8,128)S(1)}, u32[]{:S(2)}, u32[]{:S(2)}) collective-permute-start(f32[2,256,256]{2,1,0:T(8,128)S(1)} %get-tuple-element.81.whole_source), channel_id=1, source_target_pairs={{0,1},{2,3},{1,0},{3,2},{4,5},{6,7},{5,4},{7,6},{8,9},{10,11},{9,8... | collective-permute-start | bytes 1572872 | tf_op jit(solution)/shard_map/ppermute | solution.py:475
  34.4 19.2 %collective-permute-start.11 = (f32[1,2,256,256]{3,2,1,0:T(8,128)S(1)}, f32[1,2,256,256]{3,2,1,0:T(8,128)S(1)}, u32[]{:S(2)}, u32[]{:S(2)}) collective-permute-start(f32[1,2,256,256]{3,2,1,0:T(8,128)S(1)} %collective-permute-done.2.refs_0_), channel_id=1, source_target_pairs={{0,16},{4,20},{8,24},{12,28},{16,0},{20,4},{24,8},{28,12},{1,17},{... | collective-permute-start | bytes 1572872 | tf_op jit(solution)/shard_map/ppermute | solution.py:405
  37.1 12.7 %copy-start.7 = (f32[1,1,8,128]{3,2,0,1:T(8,128)S(1)}, f32[1,1,8,128]{3,2,0,1:T(8,128)}, u32[]{:S(2)}) copy-start(f32[1,1,8,128]{3,2,0,1:T(8,128)} %get-tuple-element.182) | copy-start | bytes 12292
  37.1 12.7 %copy-start.8 = (f32[1,1,8,128]{3,2,0,1:T(8,128)S(1)}, f32[1,1,8,128]{3,2,0,1:T(8,128)}, u32[]{:S(2)}) copy-start(f32[1,1,8,128]{3,2,0,1:T(8,128)} %get-tuple-element.183) | copy-start | bytes 12292
  37.1 12.8 %copy-start.12 = (f32[1,2,256,256]{3,2,1,0:T(8,128)S(1)}, f32[1,2,256,256]{3,2,1,0:T(8,128)}, u32[]{:S(2)}) copy-start(f32[1,2,256,256]{3,2,1,0:T(8,128)} %get-tuple-element.102) | copy-start | bytes 1572868
  37.1 14.9 %copy-start.2 = (f32[4,2,256,256]{3,2,1,0:T(8,128)S(1)}, f32[4,2,256,256]{3,2,1,0:T(8,128)}, u32[]{:S(2)}) copy-start(f32[4,2,256,256]{3,2,1,0:T(8,128)} %refs_2_.7) | copy-start | bytes 6291460
  37.1 12.8 %collective-permute-start.10 = (f32[1,2,256,256]{3,2,1,0:T(8,128)S(1)}, f32[1,2,256,256]{3,2,1,0:T(8,128)S(1)}, u32[]{:S(2)}, u32[]{:S(2)}) collective-permute-start(f32[1,2,256,256]{3,2,1,0:T(8,128)S(1)} %copy-done.13), channel_id=1, source_target_pairs={{0,8},{4,12},{8,0},{12,4},{16,24},{20,28},{24,16},{28,20},{1,9},{5... | collective-permute-start | bytes 1572872 | tf_op jit(solution)/shard_map/ppermute | solution.py:409
  38.8 18.7 %collective-permute-start.12 = (f32[1,2,256,256]{3,2,1,0:T(8,128)S(1)}, f32[1,2,256,256]{3,2,1,0:T(8,128)S(1)}, u32[]{:S(2)}, u32[]{:S(2)}) collective-permute-start(f32[1,2,256,256]{3,2,1,0:T(8,128)S(1)} %collective-permute-done.8.refs_1_), channel_id=1, source_target_pairs={{0,16},{4,20},{8,24},{12,28},{16,0},{20,4},{24,8},{28,12},{1,17},{... | collective-permute-start | bytes 1572872 | tf_op jit(solution)/shard_map/ppermute | solution.py:405
  47.0 12.9 %collective-permute-start.9 = (f32[2,256,256]{2,1,0:T(8,128)S(1)}, f32[2,256,256]{2,1,0:T(8,128)S(1)}, u32[]{:S(2)}, u32[]{:S(2)}) collective-permute-start(f32[2,256,256]{2,1,0:T(8,128)S(1)} %shard_map.115.before), channel_id=1, source_target_pairs={{1,2},{2,1},{5,6},{6,5},{9,10},{10,9},{13,14},{14,13},{17,18},{18,... | collective-permute-start | bytes 1572872 | tf_op jit(solution)/shard_map/ppermute | solution.py:475
  49.9 12.5 %collective-permute-start.14 = (f32[1,2,256,256]{3,2,1,0:T(8,128)S(1)}, f32[1,2,256,256]{3,2,1,0:T(8,128)S(1)}, u32[]{:S(2)}, u32[]{:S(2)}) collective-permute-start(f32[1,2,256,256]{3,2,1,0:T(8,128)S(1)} %copy-done.12), channel_id=1, source_target_pairs={{0,8},{4,12},{8,0},{12,4},{16,24},{20,28},{24,16},{28,20},{1,9},{5... | collective-permute-start | bytes 1572872 | tf_op jit(solution)/shard_map/ppermute | solution.py:409
  51.5 17.3 %collective-permute-start.15 = (f32[1,2,256,256]{3,2,1,0:T(8,128)S(1)}, f32[1,2,256,256]{3,2,1,0:T(8,128)S(1)}, u32[]{:S(2)}, u32[]{:S(2)}) collective-permute-start(f32[1,2,256,256]{3,2,1,0:T(8,128)S(1)} %collective-permute-done.10.refs_0_), channel_id=1, source_target_pairs={{0,16},{4,20},{8,24},{12,28},{16,0},{20,4},{24,8},{28,12},{1,17},{... | collective-permute-start | bytes 1572872 | tf_op jit(solution)/shard_map/ppermute | solution.py:405
  60.8 10.1 %collective-permute-start.13 = (f32[2,256,256]{2,1,0:T(8,128)S(1)}, f32[2,256,256]{2,1,0:T(8,128)S(1)}, u32[]{:S(2)}, u32[]{:S(2)}) collective-permute-start(f32[2,256,256]{2,1,0:T(8,128)S(1)} %get-tuple-element.99), channel_id=1, source_target_pairs={{0,1},{2,3},{1,0},{3,2},{4,5},{6,7},{5,4},{7,6},{8,9},{10,11},{9,8... | collective-permute-start | bytes 1572872 | tf_op jit(solution)/shard_map/ppermute | solution.py:510
  64.0 27.0 %collective-permute-start.17 = (f32[2,256,256]{2,1,0:T(8,128)S(1)}, f32[2,256,256]{2,1,0:T(8,128)S(1)}, u32[]{:S(2)}, u32[]{:S(2)}) collective-permute-start(f32[2,256,256]{2,1,0:T(8,128)S(1)} %get-tuple-element.114), channel_id=1, source_target_pairs={{8,17},{9,18},{10,19},{12,21},{13,22},{14,23},{16,9},{17,10},{18,1... | collective-permute-start | bytes 1572872 | tf_op jit(solution)/shard_map/ppermute | solution.py:515
  68.5 22.5 %collective-permute-start.18 = (f32[1,2,256,256]{3,2,1,0:T(8,128)S(1)}, f32[1,2,256,256]{3,2,1,0:T(8,128)S(1)}, u32[]{:S(2)}, u32[]{:S(2)}) collective-permute-start(f32[1,2,256,256]{3,2,1,0:T(8,128)S(1)} %collective-permute-done.14.refs_1_), channel_id=1, source_target_pairs={{0,16},{4,20},{8,24},{12,28},{16,0},{20,4},{24,8},{28,12},{1,17},{... | collective-permute-start | bytes 1572872 | tf_op jit(solution)/shard_map/ppermute | solution.py:405
  71.0 20.0 %copy-start.3 = (f32[16,4,128]{2,1,0:T(4,128)S(1)}, f32[16,4,128]{2,1,0:T(4,128)}, u32[]{:S(2)}) copy-start(f32[16,4,128]{2,1,0:T(4,128)} %param.12) | copy-start | bytes 98308
  71.0 20.0 %copy-start.4 = (f32[16,4,128]{2,1,0:T(4,128)S(1)}, f32[16,4,128]{2,1,0:T(4,128)}, u32[]{:S(2)}) copy-start(f32[16,4,128]{2,1,0:T(4,128)} %param.10) | copy-start | bytes 98308
  71.0 27.1 %collective-permute-start.16 = (f32[2,256,256]{2,1,0:T(8,128)S(1)}, f32[2,256,256]{2,1,0:T(8,128)S(1)}, u32[]{:S(2)}, u32[]{:S(2)}) collective-permute-start(f32[2,256,256]{2,1,0:T(8,128)S(1)} %broadcast_select_fusion.carried), channel_id=1, source_target_pairs={{0,8},{4,12},{8,0},{12,4},{16,24},{20,28},{24,16},{28,20},{1,9},{5... | collective-permute-start | bytes 1572872 | tf_op jit(solution)/shard_map/ppermute | solution.py:520
  100.8 6.6 %collective-permute-start.19 = (f32[2,2,256,256]{3,2,1,0:T(8,128)S(1)}, f32[2,2,256,256]{3,2,1,0:T(8,128)S(1)}, u32[]{:S(2)}, u32[]{:S(2)}) collective-permute-start(f32[2,2,256,256]{3,2,1,0:T(8,128)S(1)} %get-tuple-element.135), channel_id=1, source_target_pairs={{0,4},{4,0},{8,12},{12,8},{16,20},{20,16},{24,28},{28,24},{1,5},{5... | collective-permute-start | bytes 3145736 | tf_op jit(solution)/shard_map/ppermute | solution.py:581
  107.6 2.7 %collective-permute-start.20 = (f32[2,2,256,256]{3,2,1,0:T(8,128)S(1)}, f32[2,2,256,256]{3,2,1,0:T(8,128)S(1)}, u32[]{:S(2)}, u32[]{:S(2)}) collective-permute-start(f32[2,2,256,256]{3,2,1,0:T(8,128)S(1)} %get-tuple-element.143), channel_id=1, source_target_pairs={{0,4},{4,0},{8,12},{12,8},{16,20},{20,16},{24,28},{28,24},{1,5},{5... | collective-permute-start | bytes 3145736 | tf_op jit(solution)/shard_map/ppermute | solution.py:581
  (3 other events, 10.7 us)

commit v20 on v19

--- a/solution.py
+++ b/solution.py
@@ -297,14 +297,16 @@
     rows, twin_ends = sums.shape[0], None
     first = None
     sums, early = lax.optimization_barrier((sums, early))
+    payload = jnp.concatenate([sums, ends])
     for mask in masks:
-        given = jnp.concatenate([sums, ends]) if mask == 1 else sums
+        given = payload if mask == 1 else payload[:rows]
         arrived = lax.ppermute(given, "energy", [(e, e ^ mask) for e in range(peers)])
         if mask == 1:
             twin_ends = arrived[rows:]
-        sums = sums + arrived[:rows]
+        added_rows = ((0, payload.shape[0] - rows), (0, 0))
+        payload = payload + jnp.pad(arrived[:rows], added_rows)
         first = arrived if first is None else first
-    return sums, twin_ends, first, early
+    return payload[:rows], twin_ends, first, early
 
 
 def per_device(

time: 113 us -> 113 us (level)
  no operation moved by 1% of the time
where the time goes in v20:
time: 113 us; the launch traced here: 111 us
  waiting for transfers between devices  37.2 us (33%)
  Pallas kernels  35.9 us (32%)
  starting transfers between devices  28.6 us (25%)
  other arithmetic  5.54 us (5%)
  local copies, waits for them, and re-layouts  3.08 us (3%)
    pallas_call x13, Pallas kernels, call(): pl.pallas_call(kernel, out_shape=out_shapes, cost_estimate=cost, compiler...  35.9 us
    ppermute x4, waiting for transfers between devices, sent_on(): free_second.append(lax.ppermute(given, 'energy', relay_pairs))  15.6 us
    ppermute x2, waiting for transfers between devices, per_device(): arrived = lax.ppermute(leaving, 'slab', swaps((hop - 1) % 2))  8.74 us
    ppermute x3, waiting for transfers between devices, exchanged(): lax.ppermute(given, 'energy', [(e, e ^ mask) for e in range(peers)])  4.99 us
    ppermute x1, starting transfers between devices, per_device(): lax.ppermute(onward, ('energy', 'slab'), both(second_pairs))  4.52 us
    ppermute x1, starting transfers between devices, per_device(): crossed = lax.ppermute(jnp.where(even, lower, upper), 'slab', swaps(1))  4.32 us
    ppermute x1, starting transfers between devices, per_device(): lax.ppermute(stacked, 'energy', beyond + [(b, a) for a, b in beyond])  3.56 us
    ppermute x2, starting transfers between devices, per_device(): outputs.append(here + lax.ppermute(there, 'energy', twin_pairs))  3.21 us
  transfers between devices with their start and end apart: 21, of which 12 were waited for; matrix products, arithmetic and copies ran while one was open for 3% of the time, Pallas kernels for 30%

profile of v20, /device:TPU:13, one launch (start us, length us, event | category | flops | bytes accessed | tf_op | source)
XLA Modules:
  0.0 111.4 jit_solution(16598991751196188584)
XLA Ops:
  0.7 1.2 %slice_bitcast_fusion = f32[1,2,256,256]{3,2,1,0:T(8,128)S(1)} fusion(f32[1,4,2,256,256]{4,3,2,1,0:T(8,128)} %param.14), kind=kLoop, calls=%fused_computation.2 | loop fusion | bytes 1048576 | tf_op jit(solution)/shard_map/slice | solution.py:348
  1.9 1.3 %collective-permute-start.2 = (f32[1,2,256,256]{3,2,1,0:T(8,128)S(1)}, f32[1,2,256,256]{3,2,1,0:T(8,128)S(1)}, u32[]{:S(2)}, u32[]{:S(2)}) collective-permute-start(f32[1,2,256,256]{3,2,1,0:T(8,128)S(1)} %slice_bitcast_fusion), channel_id=1, source_target_pairs={{0,8},{4,12},{8,0},{12,4},{16,24},{20,28},{24,16},{28,20},{1,9},{5... | collective-permute-start | bytes 1572872 | tf_op jit(solution)/shard_map/ppermute | solution.py:349
  4.2 4.3 %collective-permute-start = (f32[2,1,4,128]{3,2,0,1:T(4,128)S(1)}, f32[2,1,4,128]{3,2,0,1:T(4,128)S(1)}, u32[]{:S(2)}, u32[]{:S(2)}) collective-permute-start(f32[2,1,4,128]{3,2,0,1:T(4,128)S(1)} %get-tuple-element.147), channel_id=1, source_target_pairs={{1,2},{2,1},{5,6},{6,5},{9,10},{10,9},{13,14},{14,13},{17,18},{18,... | collective-permute-start | bytes 12296 | tf_op jit(solution)/shard_map/ppermute | solution.py:364
  8.5 3.6 %collective-permute-start.3 = (f32[2,16,4,128]{3,2,0,1:T(4,128)S(1)}, f32[2,16,4,128]{3,2,0,1:T(4,128)S(1)}, u32[]{:S(2)}, u32[]{:S(2)}) collective-permute-start(f32[2,16,4,128]{3,2,0,1:T(4,128)S(1)} %pad_maximum_fusion), channel_id=1, source_target_pairs={{4,8},{12,16},{20,24},{8,4},{16,12},{24,20},{5,9},{13,17},{21,25},... | collective-permute-start | bytes 196616 | tf_op jit(solution)/shard_map/ppermute | solution.py:370
  12.7 3.7 %shard_map.113 = (f32[40,128]{1,0:T(8,128)}, f32[64,128]{1,0:T(8,128)}, f32[1,2,256,256]{3,2,1,0:T(8,128)}, f32[1,2,256,256]{3,2,1,0:T(8,128)}, f32[1,2,256,256]{3,2,1,0:T(8,128)}) custom-call(s32[1]{0:T(128)} %bitcast.2.mine, f32[64,128]{1,0:T(8,128)} %bitcast.57, f32[64,128]{1,0:T(8,128)} %bitcast.55, f32[64,128]{1,0:T(8,128)} %bitcast.58, ...), custom_call_target="tpu_custom_call" | custom-call | flops 301989888 | bytes 3833860 | tf_op jit(solution)/shard_map/pallas_call | solution.py:67
  16.6 2.8 %collective-permute-done.4 = f32[40,128]{1,0:T(8,128)S(1)} collective-permute-done((f32[40,128]{1,0:T(8,128)}, f32[40,128]{1,0:T(8,128)S(1)}, u32[]{:S(2)}, u32[]{:S(2)}) %collective-permute-start.4) | collective-permute-done | bytes 20512 | tf_op jit(solution)/shard_map/ppermute | solution.py:303
  20.2 1.9 %collective-permute-start.5 = (f32[104,128]{1,0:T(8,128)S(1)}, f32[104,128]{1,0:T(8,128)S(1)}, u32[]{:S(2)}, u32[]{:S(2)}) collective-permute-start(f32[104,128]{1,0:T(8,128)S(1)} %maximum_add_fusion), channel_id=1, source_target_pairs={{0,4},{4,0},{8,12},{12,8},{16,20},{20,16},{24,28},{28,24},{1,5},{5... | collective-permute-start | bytes 159752 | tf_op jit(solution)/shard_map/ppermute | solution.py:303
  23.2 1.3 %collective-permute-start.8 = (f32[1,2,256,256]{3,2,1,0:T(8,128)}, f32[1,2,256,256]{3,2,1,0:T(8,128)S(1)}, u32[]{:S(2)}, u32[]{:S(2)}) collective-permute-start(f32[1,2,256,256]{3,2,1,0:T(8,128)} %get-tuple-element.84), channel_id=1, source_target_pairs={{0,8},{4,12},{8,0},{12,4},{16,24},{20,28},{24,16},{28,20},{1,9},{5... | collective-permute-start | bytes 1572872 | tf_op jit(solution)/shard_map/ppermute | solution.py:402
  24.5 1.3 %collective-permute-done.6 = f32[40,128]{1,0:T(8,128)S(1)} collective-permute-done((f32[40,128]{1,0:T(8,128)S(1)}, f32[40,128]{1,0:T(8,128)S(1)}, u32[]{:S(2)}, u32[]{:S(2)}) %collective-permute-start.6) | collective-permute-done | bytes 20512 | tf_op jit(solution)/shard_map/ppermute | solution.py:303
  25.8 1.6 %copy-done.1 = f32[4,2,256,256]{3,2,1,0:T(8,128)S(1)} copy-done((f32[4,2,256,256]{3,2,1,0:T(8,128)S(1)}, f32[4,2,256,256]{3,2,1,0:T(8,128)}, u32[]{:S(2)}) %copy-start.1) | copy-done | bytes 2097176
  27.4 6.2 %shard_map.114 = (f32[2,256,256]{2,1,0:T(8,128)S(1)}, f32[2,256,256]{2,1,0:T(8,128)S(1)}) custom-call(f32[4,2,256,256]{3,2,1,0:T(8,128)S(1)} %bitcast.52, f32[4,2,256,256]{3,2,1,0:T(8,128)S(1)} %copy-done.1, f32[40,128]{1,0:T(8,128)S(1)} %pad_add_fusion.sums.refs_3_), custom_call_target="tpu_custom_call" | custom-call | flops 5133828096 | bytes 5263360 | tf_op jit(solution)/shard_map/pallas_call | solution.py:67
  33.8 2.8 %collective-permute-done.8.refs_1_ = f32[1,2,256,256]{3,2,1,0:T(8,128)S(1)} collective-permute-done((f32[1,2,256,256]{3,2,1,0:T(8,128)}, f32[1,2,256,256]{3,2,1,0:T(8,128)S(1)}, u32[]{:S(2)}, u32[]{:S(2)}) %collective-permute-start.8) | collective-permute-done | bytes 524320 | tf_op jit(solution)/shard_map/ppermute | solution.py:402
  39.2 6.4 %collective-permute-done.7.carried = f32[2,256,256]{2,1,0:T(8,128)S(1)} collective-permute-done((f32[2,256,256]{2,1,0:T(8,128)S(1)}, f32[2,256,256]{2,1,0:T(8,128)S(1)}, u32[]{:S(2)}, u32[]{:S(2)}) %collective-permute-start.7) | collective-permute-done | bytes 524320 | tf_op jit(solution)/shard_map/ppermute | solution.py:477
  46.5 2.8 %collective-permute-start.9 = (f32[2,256,256]{2,1,0:T(8,128)S(1)}, f32[2,256,256]{2,1,0:T(8,128)S(1)}, u32[]{:S(2)}, u32[]{:S(2)}) collective-permute-start(f32[2,256,256]{2,1,0:T(8,128)S(1)} %shard_map.115.before), channel_id=1, source_target_pairs={{1,2},{2,1},{5,6},{6,5},{9,10},{10,9},{13,14},{14,13},{17,18},{18,... | collective-permute-start | bytes 1572872 | tf_op jit(solution)/shard_map/ppermute | solution.py:477
  49.3 1.6 %collective-permute-start.14 = (f32[1,2,256,256]{3,2,1,0:T(8,128)S(1)}, f32[1,2,256,256]{3,2,1,0:T(8,128)S(1)}, u32[]{:S(2)}, u32[]{:S(2)}) collective-permute-start(f32[1,2,256,256]{3,2,1,0:T(8,128)S(1)} %copy-done.13), channel_id=1, source_target_pairs={{0,8},{4,12},{8,0},{12,4},{16,24},{20,28},{24,16},{28,20},{1,9},{5... | collective-permute-start | bytes 1572872 | tf_op jit(solution)/shard_map/ppermute | solution.py:411
  51.5 1.5 %shard_map.116 = (f32[2,2,256,256]{3,2,1,0:T(8,128)S(1)}, f32[2,2,256,256]{3,2,1,0:T(8,128)S(1)}) custom-call(f32[1,2,256,256]{3,2,1,0:T(8,128)S(1)} %collective-permute-done.2.refs_0_, f32[1,2,256,256]{3,2,1,0:T(8,128)S(1)} %collective-permute-done.8.refs_1_, f32[4,2,256,256]{3,2,1,0:T(8,128)S(1)} %copy-done.2, f32[40,128]{1,0:T(8,128)S(1)} %pad_add_fusion.sums.refs_3_), custom_call_target="tpu_custom_call" | custom-call | flops 1207959552 | bytes 5263360 | tf_op jit(solution)/shard_map/pallas_call | solution.py:67
  53.0 3.9 %collective-permute-done.12.refs_1_ = f32[1,2,256,256]{3,2,1,0:T(8,128)S(1)} collective-permute-done((f32[1,2,256,256]{3,2,1,0:T(8,128)S(1)}, f32[1,2,256,256]{3,2,1,0:T(8,128)S(1)}, u32[]{:S(2)}, u32[]{:S(2)}) %collective-permute-start.12) | collective-permute-done | bytes 524320 | tf_op jit(solution)/shard_map/ppermute | solution.py:407
  57.0 2.4 %collective-permute-done.9.carried = f32[2,256,256]{2,1,0:T(8,128)S(1)} collective-permute-done((f32[2,256,256]{2,1,0:T(8,128)S(1)}, f32[2,256,256]{2,1,0:T(8,128)S(1)}, u32[]{:S(2)}, u32[]{:S(2)}) %collective-permute-start.9) | collective-permute-done | bytes 524320 | tf_op jit(solution)/shard_map/ppermute | solution.py:477
  60.4 1.5 %shard_map.119 = (f32[2,2,256,256]{3,2,1,0:T(8,128)S(1)}, f32[2,2,256,256]{3,2,1,0:T(8,128)S(1)}) custom-call(f32[1,2,256,256]{3,2,1,0:T(8,128)S(1)} %collective-permute-done.11.refs_0_, f32[1,2,256,256]{3,2,1,0:T(8,128)S(1)} %collective-permute-done.12.refs_1_, f32[4,2,256,256]{3,2,1,0:T(8,128)S(1)} %copy-done.2, f32[40,128]{1,0:T(8,128)S(1)} %pad_add_fusion.sums.refs_3_), custom_call_target="tpu_custom_call" | custom-call | flops 1207959552 | bytes 5263360 | tf_op jit(solution)/shard_map/pallas_call | solution.py:67
  61.9 1.5 %shard_map.118 = (f32[2,2,256,256]{3,2,1,0:T(8,128)S(1)}, f32[2,2,256,256]{3,2,1,0:T(8,128)S(1)}) custom-call(f32[1,2,256,256]{3,2,1,0:T(8,128)S(1)} %collective-permute-done.10.refs_0_, f32[1,2,256,256]{3,2,1,0:T(8,128)S(1)} %collective-permute-done.14.refs_1_, f32[4,2,256,256]{3,2,1,0:T(8,128)S(1)} %copy-done.2, f32[40,128]{1,0:T(8,128)S(1)} %pad_add_fusion.sums.refs_3_), custom_call_target="tpu_custom_call" | custom-call | flops 1207959552 | bytes 5263360 | tf_op jit(solution)/shard_map/pallas_call | solution.py:67
  63.4 4.5 %collective-permute-start.17 = (f32[2,256,256]{2,1,0:T(8,128)S(1)}, f32[2,256,256]{2,1,0:T(8,128)S(1)}, u32[]{:S(2)}, u32[]{:S(2)}) collective-permute-start(f32[2,256,256]{2,1,0:T(8,128)S(1)} %get-tuple-element.114), channel_id=1, source_target_pairs={{8,17},{9,18},{10,19},{12,21},{13,22},{14,23},{16,9},{17,10},{18,1... | collective-permute-start | bytes 1572872 | tf_op jit(solution)/shard_map/ppermute | solution.py:517
  68.2 2.2 %collective-permute-done.13 = f32[2,256,256]{2,1,0:T(8,128)S(1)} collective-permute-done((f32[2,256,256]{2,1,0:T(8,128)S(1)}, f32[2,256,256]{2,1,0:T(8,128)S(1)}, u32[]{:S(2)}, u32[]{:S(2)}) %collective-permute-start.13) | collective-permute-done | bytes 524320 | tf_op jit(solution)/shard_map/ppermute | solution.py:512
  71.5 7.5 %shard_map.120 = (f32[4,2,256,256]{3,2,1,0:T(8,128)S(1)}, f32[2,256,256]{2,1,0:T(8,128)}) custom-call(f32[4,2,256,256]{3,2,1,0:T(8,128)S(1)} %bitcast.53, f32[4,2,256,256]{3,2,1,0:T(8,128)S(1)} %copy-done.2, f32[40,128]{1,0:T(8,128)S(1)} %pad_add_fusion.sums.refs_3_, f32[2,256,256]{2,1,0:T(8,128)S(1)} %broadcast_select_fusion.carried), custom_call_target="tpu_custom_call" | custom-call | flops 4831838208 | bytes 7360512 | tf_op jit(solution)/shard_map/pallas_call | solution.py:67
  79.0 11.5 %collective-permute-done.18.refs_1_ = f32[1,2,256,256]{3,2,1,0:T(8,128)S(1)} collective-permute-done((f32[1,2,256,256]{3,2,1,0:T(8,128)S(1)}, f32[1,2,256,256]{3,2,1,0:T(8,128)S(1)}, u32[]{:S(2)}, u32[]{:S(2)}) %collective-permute-start.18) | collective-permute-done | bytes 524320 | tf_op jit(solution)/shard_map/ppermute | solution.py:407
  90.7 1.5 %shard_map.122 = (f32[2,2,256,256]{3,2,1,0:T(8,128)S(1)}, f32[2,2,256,256]{3,2,1,0:T(8,128)S(1)}) custom-call(f32[1,2,256,256]{3,2,1,0:T(8,128)S(1)} %collective-permute-done.15.refs_0_, f32[1,2,256,256]{3,2,1,0:T(8,128)S(1)} %collective-permute-done.18.refs_1_, f32[4,2,256,256]{3,2,1,0:T(8,128)S(1)} %copy-done.2, f32[40,128]{1,0:T(8,128)S(1)} %pad_add_fusion.sums.refs_3_), custom_call_target="tpu_custom_call" | custom-call | flops 1207959552 | bytes 5263360 | tf_op jit(solution)/shard_map/pallas_call | solution.py:67
  92.2 1.9 %shard_map.121 = (f32[2,2,256,256]{3,2,1,0:T(8,128)S(1)}, f32[2,256,256]{2,1,0:T(8,128)S(1)}) custom-call(f32[2,2,256,256]{3,2,1,0:T(8,128)S(1)} %get-tuple-element.112.link, f32[2,2,256,256]{3,2,1,0:T(8,128)S(1)} %get-tuple-element.113.source, f32[2,256,256]{2,1,0:T(8,128)S(1)} %collective-permute-done.17.carried), custom_call_target="tpu_custom_call" | custom-call | flops 1207959552 | bytes 4194304 | tf_op jit(solution)/shard_map/pallas_call | solution.py:67
  94.2 2.7 %shard_map.123 = (f32[2,2,256,256]{3,2,1,0:T(8,128)S(1)}, f32[2,256,256]{2,1,0:T(8,128)}) custom-call(f32[2,2,256,256]{3,2,1,0:T(8,128)S(1)} %get-tuple-element.120.link, f32[2,2,256,256]{3,2,1,0:T(8,128)S(1)} %get-tuple-element.121.source, f32[2,256,256]{2,1,0:T(8,128)S(1)} %get-tuple-element.122.carried), custom_call_target="tpu_custom_call" | custom-call | flops 1207959552 | bytes 4194304 | tf_op jit(solution)/shard_map/pallas_call | solution.py:67
  97.7 2.7 %shard_map.124 = (f32[2,2,256,256]{3,2,1,0:T(8,128)S(1)}, f32[2,2,256,256]{3,2,1,0:T(8,128)S(1)}, f32[2,256,256]{2,1,0:T(8,128)S(1)}) custom-call(s32[2]{0:T(128)S(1)} %pad_add_fusion.1.pick, f32[2,2,256,256]{3,2,1,0:T(8,128)S(1)} %get-tuple-element.128.link, f32[2,2,256,256]{3,2,1,0:T(8,128)S(1)} %get-tuple-element.129.source, ...), custom_call_target="tpu_custom_call" | custom-call | flops 1207959552 | bytes 9437192 | tf_op jit(solution)/shard_map/pallas_call | solution.py:67
  100.3 3.1 %collective-permute-start.19 = (f32[2,2,256,256]{3,2,1,0:T(8,128)S(1)}, f32[2,2,256,256]{3,2,1,0:T(8,128)S(1)}, u32[]{:S(2)}, u32[]{:S(2)}) collective-permute-start(f32[2,2,256,256]{3,2,1,0:T(8,128)S(1)} %get-tuple-element.135), channel_id=1, source_target_pairs={{0,4},{4,0},{8,12},{12,8},{16,20},{20,16},{24,28},{28,24},{1,5},{5... | collective-permute-start | bytes 3145736 | tf_op jit(solution)/shard_map/ppermute | solution.py:583
  103.5 3.4 %shard_map.125 = (f32[2,2,256,256]{3,2,1,0:T(8,128)S(1)}, f32[2,2,256,256]{3,2,1,0:T(8,128)S(1)}, f32[2,256,256]{2,1,0:T(8,128)}) custom-call(s32[2]{0:T(128)S(1)} %pad_add_fusion.1.pick, f32[2,2,256,256]{3,2,1,0:T(8,128)S(1)} %get-tuple-element.136.link, f32[2,2,256,256]{3,2,1,0:T(8,128)S(1)} %get-tuple-element.137.source, ...), custom_call_target="tpu_custom_call" | custom-call | flops 1207959552 | bytes 9437192 | tf_op jit(solution)/shard_map/pallas_call | solution.py:67
  107.1 2.6 %collective-permute-done.20 = f32[2,2,256,256]{3,2,1,0:T(8,128)S(1)} collective-permute-done((f32[2,2,256,256]{3,2,1,0:T(8,128)S(1)}, f32[2,2,256,256]{3,2,1,0:T(8,128)S(1)}, u32[]{:S(2)}, u32[]{:S(2)}) %collective-permute-start.20) | collective-permute-done | bytes 1048608 | tf_op jit(solution)/shard_map/ppermute | solution.py:583
  109.9 1.5 %maximum_bitcast_fusion = f32[1,4,2,256,256]{4,3,2,1,0:T(8,128)} fusion(f32[2,2,256,256]{3,2,1,0:T(8,128)S(1)} %add.135, f32[2,2,256,256]{3,2,1,0:T(8,128)S(1)} %add.134), kind=kLoop, calls=%fused_computation.1 | loop fusion | flops 524288 | bytes 4194304 | tf_op jit(solution)/shard_map/broadcast_in_dim | solution.py:584
  (80 shorter events, 11.8 us)
Async XLA Ops:
  0.6 22.3 %copy-start.9 = (pred[104]{0:T(512)(128)(4,1)S(1)}, pred[104]{0:T(512)(128)(4,1)}, u32[]{:S(2)}) copy-start(pred[104]{0:T(512)(128)(4,1)} %constant.56.clone.1) | copy-start | bytes 316
  0.6 25.1 %copy-start = (f32[1,4,2,256,256]{4,3,2,1,0:T(8,128)S(1)}, f32[1,4,2,256,256]{4,3,2,1,0:T(8,128)}, u32[]{:S(2)}) copy-start(f32[1,4,2,256,256]{4,3,2,1,0:T(8,128)} %param.14) | copy-start | bytes 6291460
  1.9 14.7 %collective-permute-start.2 = (f32[1,2,256,256]{3,2,1,0:T(8,128)S(1)}, f32[1,2,256,256]{3,2,1,0:T(8,128)S(1)}, u32[]{:S(2)}, u32[]{:S(2)}) collective-permute-start(f32[1,2,256,256]{3,2,1,0:T(8,128)S(1)} %slice_bitcast_fusion), channel_id=1, source_target_pairs={{0,8},{4,12},{8,0},{12,4},{16,24},{20,28},{24,16},{28,20},{1,9},{5... | collective-permute-start | bytes 1572872 | tf_op jit(solution)/shard_map/ppermute | solution.py:349
  4.0 8.1 %collective-permute-start.1 = (f32[2,1,4,128]{3,2,0,1:T(4,128)S(1)}, f32[2,1,4,128]{3,2,0,1:T(4,128)S(1)}, u32[]{:S(2)}, u32[]{:S(2)}) collective-permute-start(f32[2,1,4,128]{3,2,0,1:T(4,128)S(1)} %get-tuple-element.146), channel_id=1, source_target_pairs={{0,1},{2,3},{1,0},{3,2},{4,5},{6,7},{5,4},{7,6},{8,9},{10,11},{9,8... | collective-permute-start | bytes 12296 | tf_op jit(solution)/shard_map/ppermute | solution.py:363
  4.2 7.9 %collective-permute-start = (f32[2,1,4,128]{3,2,0,1:T(4,128)S(1)}, f32[2,1,4,128]{3,2,0,1:T(4,128)S(1)}, u32[]{:S(2)}, u32[]{:S(2)}) collective-permute-start(f32[2,1,4,128]{3,2,0,1:T(4,128)S(1)} %get-tuple-element.147), channel_id=1, source_target_pairs={{1,2},{2,1},{5,6},{6,5},{9,10},{10,9},{13,14},{14,13},{17,18},{18,... | collective-permute-start | bytes 12296 | tf_op jit(solution)/shard_map/ppermute | solution.py:364
  8.5 8.1 %collective-permute-start.3 = (f32[2,16,4,128]{3,2,0,1:T(4,128)S(1)}, f32[2,16,4,128]{3,2,0,1:T(4,128)S(1)}, u32[]{:S(2)}, u32[]{:S(2)}) collective-permute-start(f32[2,16,4,128]{3,2,0,1:T(4,128)S(1)} %pad_maximum_fusion), channel_id=1, source_target_pairs={{4,8},{12,16},{20,24},{8,4},{16,12},{24,20},{5,9},{13,17},{21,25},... | collective-permute-start | bytes 196616 | tf_op jit(solution)/shard_map/ppermute | solution.py:370
  16.6 2.8 %collective-permute-start.4 = (f32[40,128]{1,0:T(8,128)}, f32[40,128]{1,0:T(8,128)S(1)}, u32[]{:S(2)}, u32[]{:S(2)}) collective-permute-start(f32[40,128]{1,0:T(8,128)} %get-tuple-element.75), channel_id=1, source_target_pairs={{0,8},{4,12},{8,0},{12,4},{16,24},{20,28},{24,16},{28,20},{1,9},{5... | collective-permute-start | bytes 61448 | tf_op jit(solution)/shard_map/ppermute | solution.py:303
  20.2 2.7 %collective-permute-start.5 = (f32[104,128]{1,0:T(8,128)S(1)}, f32[104,128]{1,0:T(8,128)S(1)}, u32[]{:S(2)}, u32[]{:S(2)}) collective-permute-start(f32[104,128]{1,0:T(8,128)S(1)} %maximum_add_fusion), channel_id=1, source_target_pairs={{0,4},{4,0},{8,12},{12,8},{16,20},{20,16},{24,28},{28,24},{1,5},{5... | collective-permute-start | bytes 159752 | tf_op jit(solution)/shard_map/ppermute | solution.py:303
  23.1 2.7 %collective-permute-start.6 = (f32[40,128]{1,0:T(8,128)S(1)}, f32[40,128]{1,0:T(8,128)S(1)}, u32[]{:S(2)}, u32[]{:S(2)}) collective-permute-start(f32[40,128]{1,0:T(8,128)S(1)} %slice.127), channel_id=1, source_target_pairs={{0,16},{4,20},{8,24},{12,28},{16,0},{20,4},{24,8},{28,12},{1,17},{... | collective-permute-start | bytes 61448 | tf_op jit(solution)/shard_map/ppermute | solution.py:303
  23.2 13.4 %collective-permute-start.8 = (f32[1,2,256,256]{3,2,1,0:T(8,128)}, f32[1,2,256,256]{3,2,1,0:T(8,128)S(1)}, u32[]{:S(2)}, u32[]{:S(2)}) collective-permute-start(f32[1,2,256,256]{3,2,1,0:T(8,128)} %get-tuple-element.84), channel_id=1, source_target_pairs={{0,8},{4,12},{8,0},{12,4},{16,24},{20,28},{24,16},{28,20},{1,9},{5... | collective-permute-start | bytes 1572872 | tf_op jit(solution)/shard_map/ppermute | solution.py:402
  27.4 6.4 %copy-start.12 = (s32[4]{0:T(128)S(1)}, s32[4]{0:T(128)}, u32[]{:S(2)}) copy-start(s32[4]{0:T(128)} %constant.60.clone) | copy-start | bytes 52
  27.4 9.2 %copy-start.14 = (f32[1,2,256,256]{3,2,1,0:T(8,128)S(1)}, f32[1,2,256,256]{3,2,1,0:T(8,128)}, u32[]{:S(2)}) copy-start(f32[1,2,256,256]{3,2,1,0:T(8,128)} %get-tuple-element.90) | copy-start | bytes 1572868
  27.4 10.5 %copy-start.5 = (f32[4,256,256]{2,1,0:T(8,128)S(1)}, f32[4,256,256]{2,1,0:T(8,128)}, u32[]{:S(2)}) copy-start(f32[4,256,256]{2,1,0:T(8,128)} %param.18) | copy-start | bytes 3145732
  33.6 12.0 %collective-permute-start.7 = (f32[2,256,256]{2,1,0:T(8,128)S(1)}, f32[2,256,256]{2,1,0:T(8,128)S(1)}, u32[]{:S(2)}, u32[]{:S(2)}) collective-permute-start(f32[2,256,256]{2,1,0:T(8,128)S(1)} %get-tuple-element.81.whole_source), channel_id=1, source_target_pairs={{0,1},{2,3},{1,0},{3,2},{4,5},{6,7},{5,4},{7,6},{8,9},{10,11},{9,8... | collective-permute-start | bytes 1572872 | tf_op jit(solution)/shard_map/ppermute | solution.py:477
  33.8 19.2 %collective-permute-start.11 = (f32[1,2,256,256]{3,2,1,0:T(8,128)S(1)}, f32[1,2,256,256]{3,2,1,0:T(8,128)S(1)}, u32[]{:S(2)}, u32[]{:S(2)}) collective-permute-start(f32[1,2,256,256]{3,2,1,0:T(8,128)S(1)} %collective-permute-done.2.refs_0_), channel_id=1, source_target_pairs={{0,16},{4,20},{8,24},{12,28},{16,0},{20,4},{24,8},{28,12},{1,17},{... | collective-permute-start | bytes 1572872 | tf_op jit(solution)/shard_map/ppermute | solution.py:407
  36.6 12.6 %copy-start.7 = (f32[1,1,8,128]{3,2,0,1:T(8,128)S(1)}, f32[1,1,8,128]{3,2,0,1:T(8,128)}, u32[]{:S(2)}) copy-start(f32[1,1,8,128]{3,2,0,1:T(8,128)} %get-tuple-element.182) | copy-start | bytes 12292
  36.6 12.6 %copy-start.8 = (f32[1,1,8,128]{3,2,0,1:T(8,128)S(1)}, f32[1,1,8,128]{3,2,0,1:T(8,128)}, u32[]{:S(2)}) copy-start(f32[1,1,8,128]{3,2,0,1:T(8,128)} %get-tuple-element.183) | copy-start | bytes 12292
  36.6 12.7 %copy-start.13 = (f32[1,2,256,256]{3,2,1,0:T(8,128)S(1)}, f32[1,2,256,256]{3,2,1,0:T(8,128)}, u32[]{:S(2)}) copy-start(f32[1,2,256,256]{3,2,1,0:T(8,128)} %get-tuple-element.102) | copy-start | bytes 1572868
  36.6 14.9 %copy-start.2 = (f32[4,2,256,256]{3,2,1,0:T(8,128)S(1)}, f32[4,2,256,256]{3,2,1,0:T(8,128)}, u32[]{:S(2)}) copy-start(f32[4,2,256,256]{3,2,1,0:T(8,128)} %refs_2_.7) | copy-start | bytes 6291460
  36.6 12.7 %collective-permute-start.10 = (f32[1,2,256,256]{3,2,1,0:T(8,128)S(1)}, f32[1,2,256,256]{3,2,1,0:T(8,128)S(1)}, u32[]{:S(2)}, u32[]{:S(2)}) collective-permute-start(f32[1,2,256,256]{3,2,1,0:T(8,128)S(1)} %copy-done.14), channel_id=1, source_target_pairs={{0,8},{4,12},{8,0},{12,4},{16,24},{20,28},{24,16},{28,20},{1,9},{5... | collective-permute-start | bytes 1572872 | tf_op jit(solution)/shard_map/ppermute | solution.py:411
  38.2 18.7 %collective-permute-start.12 = (f32[1,2,256,256]{3,2,1,0:T(8,128)S(1)}, f32[1,2,256,256]{3,2,1,0:T(8,128)S(1)}, u32[]{:S(2)}, u32[]{:S(2)}) collective-permute-start(f32[1,2,256,256]{3,2,1,0:T(8,128)S(1)} %collective-permute-done.8.refs_1_), channel_id=1, source_target_pairs={{0,16},{4,20},{8,24},{12,28},{16,0},{20,4},{24,8},{28,12},{1,17},{... | collective-permute-start | bytes 1572872 | tf_op jit(solution)/shard_map/ppermute | solution.py:407
  46.5 12.9 %collective-permute-start.9 = (f32[2,256,256]{2,1,0:T(8,128)S(1)}, f32[2,256,256]{2,1,0:T(8,128)S(1)}, u32[]{:S(2)}, u32[]{:S(2)}) collective-permute-start(f32[2,256,256]{2,1,0:T(8,128)S(1)} %shard_map.115.before), channel_id=1, source_target_pairs={{1,2},{2,1},{5,6},{6,5},{9,10},{10,9},{13,14},{14,13},{17,18},{18,... | collective-permute-start | bytes 1572872 | tf_op jit(solution)/shard_map/ppermute | solution.py:477
  49.3 12.6 %collective-permute-start.14 = (f32[1,2,256,256]{3,2,1,0:T(8,128)S(1)}, f32[1,2,256,256]{3,2,1,0:T(8,128)S(1)}, u32[]{:S(2)}, u32[]{:S(2)}) collective-permute-start(f32[1,2,256,256]{3,2,1,0:T(8,128)S(1)} %copy-done.13), channel_id=1, source_target_pairs={{0,8},{4,12},{8,0},{12,4},{16,24},{20,28},{24,16},{28,20},{1,9},{5... | collective-permute-start | bytes 1572872 | tf_op jit(solution)/shard_map/ppermute | solution.py:411
  50.9 17.3 %collective-permute-start.15 = (f32[1,2,256,256]{3,2,1,0:T(8,128)S(1)}, f32[1,2,256,256]{3,2,1,0:T(8,128)S(1)}, u32[]{:S(2)}, u32[]{:S(2)}) collective-permute-start(f32[1,2,256,256]{3,2,1,0:T(8,128)S(1)} %collective-permute-done.10.refs_0_), channel_id=1, source_target_pairs={{0,16},{4,20},{8,24},{12,28},{16,0},{20,4},{24,8},{28,12},{1,17},{... | collective-permute-start | bytes 1572872 | tf_op jit(solution)/shard_map/ppermute | solution.py:407
  60.3 10.1 %collective-permute-start.13 = (f32[2,256,256]{2,1,0:T(8,128)S(1)}, f32[2,256,256]{2,1,0:T(8,128)S(1)}, u32[]{:S(2)}, u32[]{:S(2)}) collective-permute-start(f32[2,256,256]{2,1,0:T(8,128)S(1)} %get-tuple-element.99), channel_id=1, source_target_pairs={{0,1},{2,3},{1,0},{3,2},{4,5},{6,7},{5,4},{7,6},{8,9},{10,11},{9,8... | collective-permute-start | bytes 1572872 | tf_op jit(solution)/shard_map/ppermute | solution.py:512
  63.4 27.1 %collective-permute-start.17 = (f32[2,256,256]{2,1,0:T(8,128)S(1)}, f32[2,256,256]{2,1,0:T(8,128)S(1)}, u32[]{:S(2)}, u32[]{:S(2)}) collective-permute-start(f32[2,256,256]{2,1,0:T(8,128)S(1)} %get-tuple-element.114), channel_id=1, source_target_pairs={{8,17},{9,18},{10,19},{12,21},{13,22},{14,23},{16,9},{17,10},{18,1... | collective-permute-start | bytes 1572872 | tf_op jit(solution)/shard_map/ppermute | solution.py:517
  67.9 22.6 %collective-permute-start.18 = (f32[1,2,256,256]{3,2,1,0:T(8,128)S(1)}, f32[1,2,256,256]{3,2,1,0:T(8,128)S(1)}, u32[]{:S(2)}, u32[]{:S(2)}) collective-permute-start(f32[1,2,256,256]{3,2,1,0:T(8,128)S(1)} %collective-permute-done.14.refs_1_), channel_id=1, source_target_pairs={{0,16},{4,20},{8,24},{12,28},{16,0},{20,4},{24,8},{28,12},{1,17},{... | collective-permute-start | bytes 1572872 | tf_op jit(solution)/shard_map/ppermute | solution.py:407
  70.5 20.1 %copy-start.3 = (f32[16,4,128]{2,1,0:T(4,128)S(1)}, f32[16,4,128]{2,1,0:T(4,128)}, u32[]{:S(2)}) copy-start(f32[16,4,128]{2,1,0:T(4,128)} %param.12) | copy-start | bytes 98308
  70.5 20.1 %copy-start.4 = (f32[16,4,128]{2,1,0:T(4,128)S(1)}, f32[16,4,128]{2,1,0:T(4,128)}, u32[]{:S(2)}) copy-start(f32[16,4,128]{2,1,0:T(4,128)} %param.10) | copy-start | bytes 98308
  70.5 27.2 %collective-permute-start.16 = (f32[2,256,256]{2,1,0:T(8,128)S(1)}, f32[2,256,256]{2,1,0:T(8,128)S(1)}, u32[]{:S(2)}, u32[]{:S(2)}) collective-permute-start(f32[2,256,256]{2,1,0:T(8,128)S(1)} %broadcast_select_fusion.carried), channel_id=1, source_target_pairs={{0,8},{4,12},{8,0},{12,4},{16,24},{20,28},{24,16},{28,20},{1,9},{5... | collective-permute-start | bytes 1572872 | tf_op jit(solution)/shard_map/ppermute | solution.py:522
  100.3 6.6 %collective-permute-start.19 = (f32[2,2,256,256]{3,2,1,0:T(8,128)S(1)}, f32[2,2,256,256]{3,2,1,0:T(8,128)S(1)}, u32[]{:S(2)}, u32[]{:S(2)}) collective-permute-start(f32[2,2,256,256]{3,2,1,0:T(8,128)S(1)} %get-tuple-element.135), channel_id=1, source_target_pairs={{0,4},{4,0},{8,12},{12,8},{16,20},{20,16},{24,28},{28,24},{1,5},{5... | collective-permute-start | bytes 3145736 | tf_op jit(solution)/shard_map/ppermute | solution.py:583
  107.0 2.7 %collective-permute-start.20 = (f32[2,2,256,256]{3,2,1,0:T(8,128)S(1)}, f32[2,2,256,256]{3,2,1,0:T(8,128)S(1)}, u32[]{:S(2)}, u32[]{:S(2)}) collective-permute-start(f32[2,2,256,256]{3,2,1,0:T(8,128)S(1)} %get-tuple-element.143), channel_id=1, source_target_pairs={{0,4},{4,0},{8,12},{12,8},{16,20},{20,16},{24,28},{28,24},{1,5},{5... | collective-permute-start | bytes 3145736 | tf_op jit(solution)/shard_map/ppermute | solution.py:583
  (4 other events, 17.0 us)
